TPU v7x, 32 devices: a whole 2x2x4 slice. The times are simulated.
32 devices in a mesh: group: 2 (over y), gx: 8 (over z, x), gy: 2 (over core).
Axes of the slice: x: 2, y: 2, z: 4, core: 2. Of those that a mesh axis runs over, the one named last changes fastest.
Arguments:
- flow_field: bfloat16 [64, 512, 512], P(('group', 'gx'), 'gy'), parts along dimension 0, may hold values from -6 to 6
- spectral_weight: bfloat16 [2, 512, 64, 128], P('gy', 'gx'), may hold values from -0.5 to 0.5
- local_weight: bfloat16 [64, 64], replicated, may hold values from -0.75 to 0.75
- bias_terms: float32 [64], replicated, may hold values from -3 to 3
Outputs:
- output: bfloat16 [64, 512, 512], P(('group', 'gx'), 'gy'), parts along dimension 0
- mixed_modes: float32 [4, 512, 1024], P(('group', 'gy'), 'gx'), parts along dimension 0
There are 2 independent parts, one for each index of `group`. A program takes and returns all parts, laid end to end along the dimension named above; an argument that names none is the same for every part. Nothing has to cross between parts.
All inputs are finite; a program needn't handle non-finite values.
Results may differ from a plain program's by a relative error of at most 0.0027.
Values sent between devices are 32-bit elements; how exact they have to be, the bound alone decides.
No kernel may reach another device: no remote copies, remote signals or barrier semaphores. Data moves between devices by JAX's collectives and lax.ppermute only.
A program may use at most 64 MiB of HBM per device.

v0:
```python
import math

import jax
import jax.numpy as jnp
from jax import lax
from jax.sharding import PartitionSpec as P

MX = 32
MY = 32


def wave_number(index, count):
    return jnp.where(index < count // 2, index, index - count)


def phase_table(waves, places, extent):
    product = waves[:, None] * places[None, :] % extent
    return 2.0 * math.pi / extent * product.astype(jnp.float32)


def row_tables(ky_rows, kx_rows, x_places, extent, width):
    angle = phase_table(wave_number(kx_rows, MX), x_places, extent)
    select = (ky_rows[:, None] == jnp.arange(width, dtype=jnp.int32)[None, :]).astype(jnp.float32)
    cosine = jnp.cos(angle)[:, :, None] * select[:, None, :]
    sine_part = jnp.sin(angle)[:, :, None] * select[:, None, :]
    return (cosine, sine_part)


def forward_rows(y_local, ky_rows, kx_rows, x_places, extent):
    cosine, sine_part = row_tables(ky_rows, kx_rows, x_places, extent, y_local.shape[0])
    real_in = y_local[:, 0]
    imag_in = y_local[:, 1]

    def contract(table, values):
        return jnp.einsum("rxk,kxf->rf", table, values, precision=lax.Precision.HIGHEST)

    real_out = contract(cosine, real_in) + contract(sine_part, imag_in)
    imag_out = contract(cosine, imag_in) - contract(sine_part, real_in)
    return jnp.concatenate([real_out, imag_out], axis=1)


def inverse_rows(running, shard_rows, ky_rows, kx_rows, x_places, extent):
    cosine, sine_part = row_tables(ky_rows, kx_rows, x_places, extent, running.shape[0])
    feat_count = shard_rows.shape[1] // 2
    real_part = shard_rows[:, :feat_count]
    imag_part = shard_rows[:, feat_count:]

    def contract(table, values):
        return jnp.einsum("rxk,rf->kxf", table, values, precision=lax.Precision.HIGHEST)

    new_real = contract(cosine, real_part) - contract(sine_part, imag_part)
    new_imag = contract(cosine, imag_part) + contract(sine_part, real_part)
    return jnp.stack([new_real, new_imag], axis=1)


def body(flow_field, spectral_weight, local_weight, bias_terms):
    cells_x, cells_y, feat_count = flow_field.shape
    channels = local_weight.shape[0]
    planes = feat_count // channels
    groups_x = lax.axis_size("gx")
    groups_y = lax.axis_size("gy")
    extent_x = cells_x * groups_x
    extent_y = cells_y * groups_y
    half_width = MY // groups_y
    quota_rows = spectral_weight.shape[1]
    high = lax.Precision.HIGHEST
    x_places = lax.axis_index("gx") * cells_x + jnp.arange(cells_x, dtype=jnp.int32)
    y_places = lax.axis_index("gy") * cells_y + jnp.arange(cells_y, dtype=jnp.int32)
    y_angle = phase_table(wave_number(jnp.arange(MY, dtype=jnp.int32), MY), y_places, extent_y)
    y_table = (
        jnp.stack([jnp.cos(y_angle), -jnp.sin(y_angle)], axis=1)
        .reshape(2 * MY, cells_y)
        .astype(jnp.bfloat16)
    )
    y_local = lax.psum_scatter(
        jnp.einsum("qy,xyf->qxf", y_table, flow_field, preferred_element_type=jnp.float32),
        "gy",
        scatter_dimension=0,
        tiled=True,
    )
    y_local = y_local.reshape(half_width, 2, cells_x, feat_count)
    rest_index = jnp.arange(lax.axis_size("gx") * quota_rows, dtype=jnp.int32)
    spectrum = lax.psum_scatter(
        forward_rows(y_local, rest_index // MX, rest_index % MX, x_places, extent_x),
        "gx",
        scatter_dimension=0,
        tiled=True,
    )
    spectrum = spectrum * (1.0 / math.sqrt(extent_x * extent_y))
    coeffs = spectrum.reshape(quota_rows, 2, planes, channels)
    weights = spectral_weight[0].astype(jnp.float32)
    product = jnp.einsum("rpzc,rco->rpzo", coeffs, weights, precision=high)
    mixed_real = product[:, 0, :, :channels] - product[:, 1, :, channels:]
    mixed_imag = product[:, 0, :, channels:] + product[:, 1, :, :channels]
    mixed_local = jnp.stack([mixed_real, mixed_imag], axis=1).reshape(quota_rows, 2 * feat_count)
    pointwise = jnp.einsum(
        "xyzc,co->xyzo",
        flow_field.reshape(cells_x, cells_y, planes, channels),
        local_weight,
        preferred_element_type=jnp.float32,
    )
    start_half = jnp.zeros((half_width, 2, cells_x, feat_count), jnp.float32)
    shard_rows = lax.all_gather(mixed_local, "gx", axis=0, tiled=True)
    rest_index = jnp.arange(shard_rows.shape[0], dtype=jnp.int32)
    back_half = inverse_rows(
        start_half, shard_rows, rest_index // MX, rest_index % MX, x_places, extent_x
    )
    back_whole = lax.all_gather(back_half, "gy", axis=0, tiled=True)
    y_cos = jnp.cos(y_angle)
    y_sin = jnp.sin(y_angle)
    spectral = (
        jnp.einsum("kn,kxf->xnf", y_cos, back_whole[:, 0], precision=high)
        - jnp.einsum("kn,kxf->xnf", y_sin, back_whole[:, 1], precision=high)
    ) * (1.0 / math.sqrt(MX * MY))
    total = spectral.reshape(cells_x, cells_y, planes, channels) + pointwise + bias_terms
    output = (
        jax.nn.gelu(total, approximate=False)
        .reshape(cells_x, cells_y, feat_count)
        .astype(jnp.bfloat16)
    )
    return (output, mixed_local.reshape(1, quota_rows, 2 * feat_count))


def solution(mesh):
    placed = (P(("group", "gx"), "gy", None), P("gy", "gx", None, None), P(), P())
    return jax.shard_map(
        body,
        mesh=mesh,
        in_specs=placed,
        out_specs=(P(("group", "gx"), "gy", None), P(("group", "gy"), "gx", None)),
        check_vma=False,
    )
```

profile of v0, /device:TPU:0, one launch (start us, length us, event | category | flops | bytes accessed | tf_op | source)
XLA Modules:
  0.0 175.5 jit_solution(802763037543346857)
XLA Ops:
  7.6 2.3 %fusion.68 = f32[64,4,512]{2,0,1:T(8,128)} fusion(bf16[64,256,1]{1,0,2:T(8,128)(2,1)S(1)} %reshape.279, bf16[4,256,512]{2,1,0:T(8,128)(2,1)} %param.4), kind=kOutput, calls=%fused_computation.123 | convolution fusion | flops 67108864 | bytes 1605632 | tf_op jit(solution)/shard_map/qy,xyf->qxf/dot_general | solution.py:76
  10.1 11.3 %reduce-scatter.5.cloned.1.call-done = f32[32,4,512]{2,0,1:T(8,128)} async-done(((f32[64,4,512]{2,0,1:T(8,128)}), f32[32,4,512]{2,0,1:T(8,128)}) %reduce-scatter.5.cloned.1.call-update) | async-done | bytes 262160 | tf_op jit(solution)/shard_map/reduce_scatter | solution.py:75
  21.5 1.1 reshape.274
  22.8 1.0 convolution_bitcast_fusion.2
  23.8 1.0 convolution_bitcast_fusion
  24.9 1.1 fusion.10
  25.9 1.1 fusion.11
  27.2 1.8 %copy.40 = f32[512,1024]{1,0:T(8,128)} copy(f32[512,1024]{0,1:T(8,128)S(1)} %pad_maximum_fusion) | data formatting | bytes 4194304
  29.1 69.1 %reduce-scatter.7.cloned.1.call-done = f32[64,1024]{1,0:T(8,128)} async-done(((f32[512,1024]{1,0:T(8,128)}), f32[64,1024]{1,0:T(8,128)}) %reduce-scatter.7.cloned.1.call-update) | async-done | bytes 262160
  98.2 1.1 copy.41
  99.7 0.9 fusion.12
  100.9 0.9 reshape.276
  101.9 1.3 copy.34
  103.2 0.9 reshape_reshape.3
  104.1 46.2 %all-gather.2.cloned.1.call-done = f32[512,1024]{1,0:T(8,128)} async-done(((f32[64,1024]{1,0:T(8,128)}), f32[512,1024]{1,0:T(8,128)}) %all-gather.2.cloned.1.call-update) | async-done | bytes 2097168 | tf_op jit(solution)/shard_map/all_gather | solution.py:103
  150.3 2.2 %fusion.18 = f32[512,64]{0,1:S(1)} fusion(f32[512,64]{0,1:T(8,128)S(1)} %bitcast.82, f32[512,1024]{1,0:T(8,128)} %all-gather.2.cloned.1.call-done), kind=kOutput, calls=%fused_computation.34 | convolution fusion | flops 201326592 | bytes 1310720
  152.4 2.0 %fusion.16 = f32[512,64]{0,1:S(1)} fusion(f32[512,64]{0,1:T(8,128)S(1)} %bitcast.83, f32[512,1024]{1,0:T(8,128)} %all-gather.2.cloned.1.call-done), kind=kOutput, calls=%fused_computation.32 | convolution fusion | flops 201326592 | bytes 1310720
  154.5 0.8 fusion.14
  155.3 0.8 fusion.20
  156.1 2.4 %all_gather.7 = f32[32,2,4,512]{3,0,2,1:T(8,128)S(1)} all-gather(f32[16,2,4,512]{3,0,2,1:T(8,128)S(1)} %pad_maximum_fusion.2), channel_id=1, replica_groups=mesh['group'=2,'gx'=8,'gy'=2] {'gy'}, dimensions={0}, use_global_device_ids=true | all-gather | bytes 786432 | tf_op jit(solution)/shard_map/all_gather | solution.py:108
  158.5 2.0 %fusion.22 = f32[4,512,256]{2,1,0:T(8,128)S(1)} fusion(f32[32,2,4,512]{3,0,2,1:T(8,128)S(1)} %all_gather.7, s32[256]{0:T(256)S(1)} %iota_add_fusion, s32[32]{0:T(128)S(1)} %compare_select_fusion.1), kind=kOutput, calls=%fused_computation.41 | convolution fusion | flops 201441280 | bytes 2360832 | tf_op jit(solution)/shard_map/kn,kxf->xnf/dot_general | solution.py:112
  160.5 2.0 %subtract_multiply_fusion = f32[4,512,256]{2,1,0:T(8,128)S(1)} fusion(f32[4,512,256]{2,1,0:T(8,128)S(1)} %fusion.22, f32[32,2,4,512]{3,0,2,1:T(8,128)S(1)} %all_gather.7, s32[256]{0:T(256)S(1)} %iota_add_fusion, s32[32]{0:T(128)S(1)} %compare_select_fusion.1), kind=kOutput, calls=%fused_computation.19 | convolution fusion | flops 202489856 | bytes 4457984 | tf_op jit(solution)/shard_map/kn,kxf->xnf/dot_general | solution.py:113
  162.5 5.1 %fusion.2 = bf16[4,256,8,64]{1,3,2,0:T(8,128)(2,1)S(1)} fusion(f32[4,256,8,64]{1,3,2,0:T(8,128)S(1)} %bitcast.79, bf16[4,256,8,64]{1,3,2,0:T(8,128)(2,1)S(1)} %bitcast.84, f32[64]{0:T(128)S(1)} %copy-done.5, bf16[64,64]{1,0:T(8,128)(2,1)S(1)} %copy-done.4), kind=kOutput, calls=%fused_computation.3 | convolution fusion | flops 102236160 | bytes 4202752 | tf_op jit(solution)/shard_map/xyzc,co->xyzo/dot_general | solution.py:96
  167.6 1.3 copy.36
  (38 shorter events, 1.7 us)
Async XLA Ops:
  7.2 92.6 %copy-start = (bf16[1,64,64,128]{3,2,1,0:T(8,128)(2,1)S(1)}, bf16[1,64,64,128]{3,2,1,0:T(8,128)(2,1)}, u32[]{:S(2)}) copy-start(bf16[1,64,64,128]{3,2,1,0:T(8,128)(2,1)} %param.5) | copy-start | bytes 3145732
  7.2 14.3 %reduce-scatter.5.cloned.1.call-start = ((), (), s32[]{:S(2)}) async-start(), calls=%async_computation.2 | async-start | bytes 786432 | tf_op jit(solution)/shard_map/reduce_scatter | solution.py:75
  9.9 88.3 %reduce-scatter.7.cloned.1.call-start = ((), (), s32[]{:S(2)}) async-start(), calls=%async_computation.4 | async-start | bytes 2359296
  29.1 121.2 %all-gather.2.cloned.1.call-start = ((), (), s32[]{:S(2)}) async-start(), calls=%async_computation.3 | async-start | bytes 2359296 | tf_op jit(solution)/shard_map/all_gather | solution.py:103
  100.7 1.2 copy-start.2
  150.3 4.2 %copy-start.1 = (f32[512,1024]{1,0:T(8,128)S(1)}, f32[512,1024]{1,0:T(8,128)}, u32[]{:S(2)}) copy-start(f32[512,1024]{1,0:T(8,128)} %all-gather.2.cloned.1.call-done) | copy-start | bytes 6291460
  160.5 2.0 %copy-start.3 = (bf16[4,256,512]{1,2,0:T(8,128)(2,1)S(1)}, bf16[4,256,512]{1,2,0:T(8,128)(2,1)}, u32[]{:S(2)}) copy-start(bf16[4,256,512]{1,2,0:T(8,128)(2,1)} %copy.34) | copy-start | bytes 3145732
  160.5 2.0 %copy-start.4 = (bf16[64,64]{1,0:T(8,128)(2,1)S(1)}, bf16[64,64]{1,0:T(8,128)(2,1)}, u32[]{:S(2)}) copy-start(bf16[64,64]{1,0:T(8,128)(2,1)} %param.6) | copy-start | bytes 24580
  160.5 2.0 %copy-start.5 = (f32[64]{0:T(128)S(1)}, f32[64]{0:T(128)}, u32[]{:S(2)}) copy-start(f32[64]{0:T(128)} %param.7) | copy-start | bytes 772
Sparse Core Ops, SparseCore 0:
  10.8 10.6 reduce-scatter.4
  29.2 69.0 reduce-scatter.6
  101.9 48.3 all-gather.1
where the time goes:
time: 176 us; the launch traced here: 175 us
  waiting for transfers between devices  127 us (72%)
  matrix products  22.2 us (13%)
  between operations  14 us (8%)
  local copies, waits for them, and re-layouts  9.1 us (5%)
  blocking collectives  2.36 us (1%)
    unnamed x4, waiting for transfers between devices  69.2 us
    all_gather x1, waiting for transfers between devices, body(): shard_rows = lax.all_gather(mixed_local, 'gx', axis=0, tiled=True)  46.2 us
    reduce_scatter x1, waiting for transfers between devices, body(): lax.psum_scatter(jnp.einsum('qy,xyf->qxf', y_table, flow_field, preferred...  11.3 us
    unnamed x4, matrix products  5.75 us
    unnamed x16, local copies, waits for them, and re-layouts  5.7 us
    dot_general x1, matrix products, body(): jnp.einsum('xyzc,co->xyzo', flow_field.reshape(cells_x, cells_y, planes,...  5.08 us
    dot_general x4, matrix products, contract(): jnp.einsum('rxk,kxf->rf', table, values, precision=lax.Precision.HIGHEST)  4.17 us
  transfers between devices with their start and end apart: 3, of which 3 were waited for; matrix products, arithmetic and copies ran while one was open for 1% of the time, Pallas kernels for 0%

commit v1 on v0

--- a/solution.py
+++ b/solution.py
@@ -1,8 +1,13 @@
+import functools
 import math
 
 import jax
 import jax.numpy as jnp
+import ml_dtypes
+import numpy as np
 from jax import lax
+from jax.experimental import pallas as pl
+from jax.experimental.pallas import tpu as pltpu
 from jax.sharding import PartitionSpec as P
 
 MX = 32
@@ -53,7 +58,7 @@
     return jnp.stack([new_real, new_imag], axis=1)
 
 
-def body(flow_field, spectral_weight, local_weight, bias_terms):
+def general_body(flow_field, spectral_weight, local_weight, bias_terms):
     cells_x, cells_y, feat_count = flow_field.shape
     channels = local_weight.shape[0]
     planes = feat_count // channels
@@ -121,6 +126,263 @@
     return (output, mixed_local.reshape(1, quota_rows, 2 * feat_count))
 
 
+def angles(count, places, extent):
+    index = np.arange(count)
+    waves = np.where(index < count // 2, index, index - count)
+    product = (waves[:, None] * np.asarray(places)[None, :]) % extent
+    return (np.float32(2.0 * math.pi / extent) * product.astype(np.float32)).astype(np.float64)
+
+
+def split_table(table):
+    high = table.astype(ml_dtypes.bfloat16)
+    low = (table - high.astype(np.float64)).astype(ml_dtypes.bfloat16)
+    return high, low
+
+
+def split_terms(values):
+    high = values.astype(jnp.bfloat16)
+    low = (values - high.astype(jnp.float32)).astype(jnp.bfloat16)
+    return high, low
+
+
+def forward_y_table(cells_y, groups_y, peers, rows_ky):
+    extent = cells_y * groups_y
+    angle = angles(MY, np.arange(extent), extent).astype(np.float32)
+    full = np.stack([np.cos(angle), -np.sin(angle)], axis=1).astype(ml_dtypes.bfloat16)
+    full = full.reshape(groups_y, peers, rows_ky, 2, groups_y, cells_y)
+    out = np.zeros((groups_y, 2, peers, 2, rows_ky, 2, 2, cells_y), ml_dtypes.bfloat16)
+    for place in range(groups_y):
+        for side, half in enumerate((1 - place, place)):
+            for parity in range(2):
+                out[place, side, :, parity, :, :, parity, :] = full[half, :, :, :, place, :]
+    return out.reshape(groups_y, 2 * peers * 4 * rows_ky, 2 * cells_y)
+
+
+def forward_x_table(cells_x, peers, rows_ky):
+    extent = cells_x * peers
+    angle = angles(MX, np.arange(extent), extent)
+    cosine, sine = np.cos(angle), np.sin(angle)
+    out = np.zeros((2, rows_ky, MX, extent, rows_ky, 2))
+    for row in range(rows_ky):
+        out[0, row, :, :, row, 0] = cosine
+        out[0, row, :, :, row, 1] = sine
+        out[1, row, :, :, row, 1] = cosine
+        out[1, row, :, :, row, 0] = -sine
+    return out.reshape(2 * rows_ky * MX, extent * rows_ky * 2)
+
+
+def inverse_x_table(cells_x, peers, rows_ky):
+    extent = cells_x * peers
+    angle = angles(MX, np.arange(extent), extent)
+    cosine, sine = np.cos(angle).T, np.sin(angle).T
+    out = np.zeros((extent, rows_ky, 2, 2, rows_ky, MX))
+    for row in range(rows_ky):
+        out[:, row, 0, 0, row, :] = cosine
+        out[:, row, 0, 1, row, :] = -sine
+        out[:, row, 1, 1, row, :] = cosine
+        out[:, row, 1, 0, row, :] = sine
+    return out.reshape(extent * rows_ky * 2, 2 * rows_ky * MX)
+
+
+def inverse_y_table(cells_y, groups_y, peers, rows_ky):
+    extent = cells_y * groups_y
+    angle = angles(MY, np.arange(extent), extent)
+    full = np.stack([np.cos(angle), -np.sin(angle)], axis=1)
+    full = full.reshape(groups_y, peers, rows_ky, 2, groups_y, cells_y)
+    out = np.zeros((groups_y, 2, cells_y, 2, peers, 2, rows_ky, 2))
+    for place in range(groups_y):
+        for side, half in enumerate((place, 1 - place)):
+            block = np.moveaxis(full[half, :, :, :, place, :], -1, 0)
+            for parity in range(2):
+                out[place, parity, :, side, :, parity] = block
+    return out.reshape(groups_y, 2, cells_y, 2 * peers * 4 * rows_ky)
+
+
+def dot(left, right):
+    return jnp.dot(left, right, preferred_element_type=jnp.float32)
+
+
+def forward_y_kernel(flow_ref, table_ref, send_ref, keep_ref):
+    table = table_ref[lax.axis_index("gy")]
+    pairs, cells_y, feat_count = flow_ref.shape
+    result = dot(table, flow_ref[...].reshape(pairs * cells_y, feat_count))
+    result = result.reshape((2,) + send_ref.shape)
+    send_ref[...] = result[0]
+    keep_ref[...] = result[1]
+
+
+def forward_y(flow_field, table, peers, rows_ky):
+    cells_x, cells_y, feat_count = flow_field.shape
+    rows = 4 * rows_ky
+    shape = jax.ShapeDtypeStruct((peers, cells_x // 2 * rows, feat_count), jnp.float32)
+    spec = pl.BlockSpec((peers, rows, feat_count), lambda i: (0, i, 0))
+    return pl.pallas_call(
+        forward_y_kernel,
+        grid=(cells_x // 2,),
+        in_specs=[
+            pl.BlockSpec((2, cells_y, feat_count), lambda i: (i, 0, 0)),
+            pl.BlockSpec(table.shape, lambda i: (0, 0, 0)),
+        ],
+        out_specs=[spec, spec],
+        out_shape=[shape, shape],
+        name="forward_y",
+    )(flow_field, table)
+
+
+def mix_kernel(
+    modes_ref, weight_ref, forward_high, forward_low, inverse_high, inverse_low,
+    mixed_ref, back_ref, spread_ref, result_ref,
+):
+    feat_count = modes_ref.shape[-1]
+    count = weight_ref.shape[1]
+    channels = weight_ref.shape[2]
+    tiles = feat_count // 128
+    group = 2 * tiles
+    high, low = split_terms(modes_ref[...].reshape(-1, feat_count))
+    spectrum = (
+        dot(forward_high[...], high) + dot(forward_high[...], low) + dot(forward_low[...], high)
+    )
+    for part in range(2):
+        for tile in range(tiles):
+            spread_ref[pl.ds(part * tiles + tile, count, stride=group), :] = spectrum[
+                part * count : (part + 1) * count, tile * 128 : (tile + 1) * 128
+            ]
+    lane = lax.broadcasted_iota(jnp.int32, (group, 128), 1) < channels
+    sign = jnp.where(lax.broadcasted_iota(jnp.int32, (group, 128), 0) < tiles, -1.0, 1.0)
+    for mode in range(count):
+        block = spread_ref[mode * group : (mode + 1) * group, :]
+        turned = pltpu.roll(block, channels, 1)
+        left = jnp.concatenate([block, turned], axis=0)[:, :channels]
+        left_high, left_low = split_terms(left)
+        product = dot(jnp.concatenate([left_high, left_low], axis=0), weight_ref[0, mode])
+        product = product[: 2 * group] + product[2 * group :]
+        first, second = product[:group], product[group:]
+        real = jnp.where(lane, first, pltpu.roll(second, channels, 1))
+        imag = jnp.where(lane, pltpu.roll(first, channels, 1), second)
+        result_ref[mode * group : (mode + 1) * group, :] = real + sign * pltpu.roll(imag, tiles, 0)
+    parts = []
+    for part in range(2):
+        parts.append(
+            jnp.concatenate(
+                [
+                    result_ref[pl.ds(part * tiles + tile, count, stride=group), :]
+                    for tile in range(tiles)
+                ],
+                axis=1,
+            )
+        )
+        mixed_ref[0, :, part * feat_count : (part + 1) * feat_count] = parts[part]
+    high, low = split_terms(jnp.concatenate(parts, axis=0))
+    back = dot(inverse_high[...], high) + dot(inverse_high[...], low) + dot(inverse_low[...], high)
+    back_ref[...] = back.reshape(back_ref.shape)
+
+
+def mix(modes, weights, forward_table, inverse_table):
+    feat_count = modes.shape[-1]
+    count = weights.shape[1]
+    scratch = pltpu.VMEM((count * feat_count // 64, 128), jnp.float32)
+    return pl.pallas_call(
+        mix_kernel,
+        out_shape=[
+            jax.ShapeDtypeStruct((1, count, 2 * feat_count), jnp.float32),
+            jax.ShapeDtypeStruct(modes.shape, jnp.float32),
+        ],
+        scratch_shapes=[scratch, scratch],
+        name="mix",
+    )(modes, weights, *split_table(forward_table), *split_table(inverse_table))
+
+
+def output_kernel(place_ref, flow_ref, own_ref, other_ref, table_ref, local_ref, bias_ref, out_ref):
+    step = pl.program_id(0)
+    rows = table_ref.shape[-1] // 3 // 2 // own_ref.shape[0]
+    feat_count = flow_ref.shape[-1]
+    pair = pl.ds(pl.multiple_of(step // 2 * rows, rows), rows)
+    both = jnp.concatenate([own_ref[:, pair, :], other_ref[:, pair, :]], axis=0)
+    high, low = split_terms(both.reshape(-1, feat_count))
+    stacked = jnp.concatenate([high, low, high], axis=0)
+    table = table_ref[0, step % 2]
+    width = local_ref.shape[0]
+    for start in range(0, feat_count, width):
+        columns = slice(start, start + width)
+        total = (
+            dot(table, stacked[:, columns])
+            + dot(flow_ref[0, :, columns], local_ref[...])
+            + bias_ref[:, columns]
+        )
+        out_ref[0, :, columns] = (
+            0.5 * total * (1.0 + lax.erf(total * math.sqrt(0.5)))
+        ).astype(out_ref.dtype)
+
+
+def make_output(flow_field, own, other, table, local, bias):
+    cells_x, cells_y, feat_count = flow_field.shape
+    place = jnp.reshape(lax.axis_index("gy"), (1,))
+    whole = lambda array: pl.BlockSpec(array.shape, lambda i, p: (0,) * array.ndim)
+    block = pl.BlockSpec((1, cells_y, feat_count), lambda i, p: (i, 0, 0))
+    return pl.pallas_call(
+        output_kernel,
+        grid_spec=pltpu.PrefetchScalarGridSpec(
+            num_scalar_prefetch=1,
+            grid=(cells_x,),
+            in_specs=[
+                block,
+                whole(own),
+                whole(other),
+                pl.BlockSpec((1,) + table.shape[1:], lambda i, p: (p[0], 0, 0, 0)),
+                whole(local),
+                whole(bias),
+            ],
+            out_specs=block,
+        ),
+        out_shape=jax.ShapeDtypeStruct(flow_field.shape, jnp.bfloat16),
+        name="make_output",
+    )(place, flow_field, own, other, table, local, bias)
+
+
+def row_body(flow_field, spectral_weight, local_weight, bias_terms):
+    cells_x, cells_y, feat_count = flow_field.shape
+    channels = local_weight.shape[0]
+    peers = lax.axis_size("gx")
+    groups_y = lax.axis_size("gy")
+    rows_ky = MY // groups_y // peers
+    forward_scale = 1.0 / math.sqrt(cells_x * peers * cells_y * groups_y)
+    inverse_scale = 1.0 / math.sqrt(MX * MY)
+    swap = [(0, 1), (1, 0)]
+
+    send, keep = forward_y(
+        flow_field, forward_y_table(cells_y, groups_y, peers, rows_ky), peers, rows_ky
+    )
+    modes = keep + lax.ppermute(send, "gy", swap)
+    modes = lax.all_to_all(modes, "gx", 0, 0, tiled=True)
+    mixed, back = mix(
+        modes,
+        spectral_weight,
+        forward_x_table(cells_x, peers, rows_ky) * forward_scale,
+        inverse_x_table(cells_x, peers, rows_ky),
+    )
+    own = lax.all_to_all(back, "gx", 0, 0, tiled=True)
+    other = lax.ppermute(own, "gy", swap)
+    high, low = split_table(inverse_y_table(cells_y, groups_y, peers, rows_ky) * inverse_scale)
+    copies = 256 // channels
+    local = jnp.einsum("ij,co->icjo", jnp.eye(copies, dtype=local_weight.dtype), local_weight)
+    output = make_output(
+        flow_field,
+        own,
+        other,
+        np.concatenate([high, high, low], axis=-1),
+        local.reshape(copies * channels, copies * channels),
+        jnp.tile(bias_terms, feat_count // channels)[None, :],
+    )
+    return output, mixed
+
+
+def body(flow_field, spectral_weight, local_weight, bias_terms):
+    whole_rows = spectral_weight.shape[1] % MX == 0
+    if whole_rows and lax.axis_size("gy") == 2 and spectral_weight.shape[1] == 2 * MX:
+        return row_body(flow_field, spectral_weight, local_weight, bias_terms)
+    return general_body(flow_field, spectral_weight, local_weight, bias_terms)
+
+
 def solution(mesh):
     placed = (P(("group", "gx"), "gy", None), P("gy", "gx", None, None), P(), P())
     return jax.shard_map(

time: 176 us -> 44.8 us (0.25)
  waiting for transfers between devices: 127 us -> 1.38 us
  blocking collectives: 2.36 us -> 28.6 us
  matrix products: 22.2 us -> 0 us
  between operations: 14 us -> 0.67 us
  Pallas kernels: 0 us -> 9.83 us
  local copies, waits for them, and re-layouts: 9.1 us -> 2.24 us
    unnamed x4 -> x0, waiting for transfers between devices: 69.2 us -> none
    all_gather x1 -> x0, waiting for transfers between devices: 46.2 us -> none  [body(): shard_rows = lax.all_gather(mixed_local, 'gx', axis=0, tiled=True)]
    all_to_all x0 -> x2, blocking collectives: none -> 28.6 us  [the longest x1 16.3 us: row_body(): modes = lax.all_to_all(modes, 'gx', 0, 0, tiled=True)]
    dot_general x9 -> x0, matrix products: 16.5 us -> none  [the longest x1 5.08 us: body(): jnp.einsum('xyzc,co->xyzo', flow_field.reshape(cells_x, cells_y, planes,...]
    reduce_scatter x1 -> x0, waiting for transfers between devices: 11.3 us -> none  [body(): lax.psum_scatter(jnp.einsum('qy,xyf->qxf', y_table, flow_field, preferred...]
    pallas_call x0 -> x3, Pallas kernels: none -> 9.83 us  [the longest x1 4.49 us: make_output(): pl.pallas_call(output_kernel, grid_spec=pltpu.PrefetchScalarGridSpec(num_...]
    unnamed x4 -> x0, matrix products: 5.75 us -> none
    unnamed x16 -> x8, local copies, waits for them, and re-layouts: 5.7 us -> 0.72 us
  transfers between devices with their start and end apart: 3 -> 2, of which waited for: 3 -> 1; matrix products, arithmetic and copies ran while one was open for 1% -> 4% of each run, Pallas kernels for 0% -> 0%
where the time goes in v1:
time: 44.8 us; the launch traced here: 44.3 us
  blocking collectives  28.6 us (64%)
  Pallas kernels  9.83 us (22%)
  local copies, waits for them, and re-layouts  2.24 us (5%)
  waiting for transfers between devices  1.38 us (3%)
  other arithmetic  1.16 us (3%)
  between operations  0.67 us (1%)
  starting transfers between devices  0.45 us (1%)
    all_to_all x1, blocking collectives, row_body(): modes = lax.all_to_all(modes, 'gx', 0, 0, tiled=True)  16.3 us
    all_to_all x1, blocking collectives, row_body(): own = lax.all_to_all(back, 'gx', 0, 0, tiled=True)  12.3 us
    pallas_call x1, Pallas kernels, make_output(): pl.pallas_call(output_kernel, grid_spec=pltpu.PrefetchScalarGridSpec(num_...  4.49 us
    pallas_call x1, Pallas kernels, mix(): pl.pallas_call(mix_kernel, out_shape=[jax.ShapeDtypeStruct((1, count, 2 *...  3.05 us
    pallas_call x1, Pallas kernels, forward_y(): pl.pallas_call(forward_y_kernel, grid=(cells_x // 2,), in_specs=[pl.Block...  2.28 us
    ppermute x1, waiting for transfers between devices, row_body(): modes = keep + lax.ppermute(send, 'gy', swap)  1.37 us
    add x1, other arithmetic, row_body(): modes = keep + lax.ppermute(send, 'gy', swap)  0.99 us
  transfers between devices with their start and end apart: 2, of which 1 were waited for; matrix products, arithmetic and copies ran while one was open for 4% of the time, Pallas kernels for 0%

profile of v1, /device:TPU:0, one launch (start us, length us, event | category | flops | bytes accessed | tf_op | source)
XLA Modules:
  0.0 44.3 jit_solution(12372140072313611400)
XLA Ops:
  0.6 2.3 %forward_y.1 = (f32[8,16,512]{2,1,0:T(8,128)}, f32[8,16,512]{2,1,0:T(8,128)}) custom-call(bf16[4,256,512]{2,1,0:T(8,128)(2,1)} %flow_ref.3, bf16[2,128,512]{2,1,0:T(8,128)(2,1)} %constant.16.clone.table_ref), custom_call_target="tpu_custom_call" | custom-call | tf_op jit(solution)/shard_map/forward_y/pallas_call | solution.py:219
  2.9 0.5 %collective-permute-start = (f32[8,16,512]{2,1,0:T(8,128)}, f32[8,16,512]{2,1,0:T(8,128)S(1)}, u32[]{:S(2)}, u32[]{:S(2)}) collective-permute-start(f32[8,16,512]{2,1,0:T(8,128)} %get-tuple-element.7), channel_id=1, source_target_pairs={{0,1},{1,0},{2,3},{3,2},{4,5},{5,4},{6,7},{7,6},{8,9},{9,8},{10,11... | collective-permute-start | bytes 786440 | tf_op jit(solution)/shard_map/ppermute | solution.py:355
  3.4 1.4 %collective-permute-done = f32[8,16,512]{2,1,0:T(8,128)S(1)} collective-permute-done((f32[8,16,512]{2,1,0:T(8,128)}, f32[8,16,512]{2,1,0:T(8,128)S(1)}, u32[]{:S(2)}, u32[]{:S(2)}) %collective-permute-start) | collective-permute-done | bytes 262176 | tf_op jit(solution)/shard_map/ppermute | solution.py:355
  4.7 1.0 %add.3 = f32[8,16,512]{2,1,0:T(8,128)S(1)} add(f32[8,16,512]{2,1,0:T(8,128)} %get-tuple-element.6, f32[8,16,512]{2,1,0:T(8,128)S(1)} %collective-permute-done) | non-fusion elementwise | flops 65536 | bytes 786432 | tf_op jit(solution)/shard_map/add | solution.py:355
  5.7 16.3 %all_to_all.10.modes_ref = f32[8,16,512]{2,1,0:T(8,128)} all-to-all(f32[8,16,512]{2,1,0:T(8,128)S(1)} %add.3), channel_id=1, replica_groups=mesh['group'=2,'gx'=8,'gy'=2] {'gx'}, dimensions={0} | all-to-all | bytes 524288 | tf_op jit(solution)/shard_map/all_to_all | solution.py:356
  22.0 3.1 %mix.1 = (f32[1,64,1024]{2,1,0:T(8,128)}, f32[8,16,512]{2,1,0:T(8,128)}) custom-call(f32[8,16,512]{2,1,0:T(8,128)} %all_to_all.10.modes_ref, bf16[1,64,64,128]{3,2,1,0:T(8,128)(2,1)} %weight_ref.1, bf16[128,128]{1,0:T(8,128)(2,1)} %constant.17.clone.forward_high, bf16[128,128]{1,0:T(8,128)(2,1)} %constant.18.clone.forward_low, ...), custom_call_target="tpu_custom_call" | custom-call | tf_op jit(solution)/shard_map/mix/pallas_call | solution.py:284
  25.1 0.0 copy-start.3
  25.1 12.3 %all_to_all.11.own_ref = f32[8,16,512]{2,1,0:T(8,128)S(1)} all-to-all(f32[8,16,512]{2,1,0:T(8,128)} %get-tuple-element.8), channel_id=1, replica_groups=mesh['group'=2,'gx'=8,'gy'=2] {'gx'}, dimensions={0} | all-to-all | bytes 524288 | tf_op jit(solution)/shard_map/all_to_all | solution.py:363
  37.4 0.0 copy-start
  37.4 0.0 copy-start.2
  37.4 0.0 collective-permute-start.1
  37.4 0.0 copy-done.3
  37.4 0.7 %broadcast_in_dim_tile.3.bias_ref = f32[1,512]{1,0:T(1,128)} reshape(f32[8,64]{1,0:T(8,128)S(1)} %tile.2) | data formatting | bytes 4096 | tf_op jit(solution)/shard_map/broadcast_in_dim;tile | solution.py:374
  38.1 0.0 copy-done.2
  38.1 0.2 multiply_bitcast_fusion
  38.3 0.9 %reshape.12.local_ref = bf16[256,256]{1,0:T(8,128)(2,1)} reshape(bf16[4,64,4,64]{3,2,1,0:T(4,128)(2,1)S(1)} %multiply_bitcast_fusion) | data formatting | bytes 262144 | tf_op jit(solution)/shard_map/reshape | solution.py:373
  39.1 0.0 copy-done
  39.1 0.0 collective-permute-done.1.other_ref
  39.1 0.0 copy-start.1
  39.1 0.7 %copy-done.1 = f32[8,16,512]{2,1,0:T(8,128)} copy-done((f32[8,16,512]{2,1,0:T(8,128)}, f32[8,16,512]{2,1,0:T(8,128)S(1)}, u32[]{:S(2)}) %copy-start.1) | copy-done | bytes 262168
  39.8 4.5 %make_output.1 = bf16[4,256,512]{2,1,0:T(8,128)(2,1)} custom-call(s32[1]{0:T(128)} %bitcast.place_ref, bf16[4,256,512]{2,1,0:T(8,128)(2,1)} %flow_ref.3, f32[8,16,512]{2,1,0:T(8,128)} %copy-done, f32[8,16,512]{2,1,0:T(8,128)} %copy-done.1, bf16[2,2,256,384]{3,2,1,0:T(8,128)(2,1)} %constant.21.clone.table_ref, bf16[256,256]{1,0:T(8,128)(2,1)} %reshape.12.local_ref, ...), custom_call_target="tpu_custom_call" | custom-call | tf_op jit(solution)/shard_map/make_output/pallas_call | solution.py:322
  (2 shorter events, 0.0 us)
Async XLA Ops:
  2.9 1.8 %collective-permute-start = (f32[8,16,512]{2,1,0:T(8,128)}, f32[8,16,512]{2,1,0:T(8,128)S(1)}, u32[]{:S(2)}, u32[]{:S(2)}) collective-permute-start(f32[8,16,512]{2,1,0:T(8,128)} %get-tuple-element.7), channel_id=1, source_target_pairs={{0,1},{1,0},{2,3},{3,2},{4,5},{5,4},{6,7},{7,6},{8,9},{9,8},{10,11... | collective-permute-start | bytes 786440 | tf_op jit(solution)/shard_map/ppermute | solution.py:355
  25.1 12.3 %copy-start.3 = (f32[64]{0:T(128)S(1)}, f32[64]{0:T(128)}, u32[]{:S(2)}) copy-start(f32[64]{0:T(128)} %param.13) | copy-start | bytes 772
  37.4 1.7 %copy-start = (f32[8,16,512]{2,1,0:T(8,128)}, f32[8,16,512]{2,1,0:T(8,128)S(1)}, u32[]{:S(2)}) copy-start(f32[8,16,512]{2,1,0:T(8,128)S(1)} %all_to_all.11.own_ref) | copy-start | bytes 786436
  37.4 0.7 %copy-start.2 = (bf16[64,64]{1,0:T(8,128)(2,1)S(1)}, bf16[64,64]{1,0:T(8,128)(2,1)}, u32[]{:S(2)}) copy-start(bf16[64,64]{1,0:T(8,128)(2,1)} %param.12) | copy-start | bytes 24580
  37.4 1.7 %collective-permute-start.1 = (f32[8,16,512]{2,1,0:T(8,128)S(1)}, f32[8,16,512]{2,1,0:T(8,128)S(1)}, u32[]{:S(2)}, u32[]{:S(2)}) collective-permute-start(f32[8,16,512]{2,1,0:T(8,128)S(1)} %all_to_all.11.own_ref), channel_id=1, source_target_pairs={{0,1},{1,0},{2,3},{3,2},{4,5},{5,4},{6,7},{7,6},{8,9},{9,8},{10,11... | collective-permute-start | bytes 786440 | tf_op jit(solution)/shard_map/ppermute | solution.py:364
  39.1 0.7 %copy-start.1 = (f32[8,16,512]{2,1,0:T(8,128)}, f32[8,16,512]{2,1,0:T(8,128)S(1)}, u32[]{:S(2)}) copy-start(f32[8,16,512]{2,1,0:T(8,128)S(1)} %collective-permute-done.1.other_ref) | copy-start | bytes 786436

commit v2 on v1

--- a/solution.py
+++ b/solution.py
@@ -126,6 +126,9 @@
     return (output, mixed_local.reshape(1, quota_rows, 2 * feat_count))
 
 
+SMALL = pltpu.CompilerParams(vmem_limit_bytes=20 * 1024 * 1024)
+
+
 def angles(count, places, extent):
     index = np.arange(count)
     waves = np.where(index < count // 2, index, index - count)
@@ -225,20 +228,52 @@
         ],
         out_specs=[spec, spec],
         out_shape=[shape, shape],
+        compiler_params=SMALL,
         name="forward_y",
     )(flow_field, table)
 
 
-def mix_kernel(
-    modes_ref, weight_ref, forward_high, forward_low, inverse_high, inverse_low,
-    mixed_ref, back_ref, spread_ref, result_ref,
-):
-    feat_count = modes_ref.shape[-1]
+def combine_kernel(keep_ref, arrived_ref, *out_refs):
+    me = lax.axis_index("gx")
+    for step, out_ref in enumerate(out_refs):
+        out_ref[...] = keep_ref[me ^ step] + arrived_ref[me ^ step]
+
+
+def combine(keep, arrived):
+    peers = keep.shape[0]
+    return pl.pallas_call(
+        combine_kernel,
+        out_shape=[jax.ShapeDtypeStruct(keep.shape[1:], keep.dtype)] * peers,
+        compiler_params=SMALL,
+        name="combine",
+    )(keep, arrived)
+
+
+def exchange(blocks):
+    peers = len(blocks)
+    arrived = [blocks[0]]
+    for step in range(1, peers):
+        pairs = [(place, place ^ step) for place in range(peers)]
+        arrived.append(lax.ppermute(blocks[step], "gx", pairs))
+    return arrived
+
+
+def mix_kernel(peers, *refs):
+    block_refs = refs[:peers]
+    weight_ref, forward_high, forward_low, inverse_high, inverse_low, mixed_ref = refs[
+        peers : peers + 6
+    ]
+    back_refs = refs[peers + 6 : 2 * peers + 6]
+    order_ref, spread_ref, result_ref = refs[2 * peers + 6 :]
+    me = lax.axis_index("gx")
+    feat_count = order_ref.shape[-1]
     count = weight_ref.shape[1]
     channels = weight_ref.shape[2]
     tiles = feat_count // 128
     group = 2 * tiles
-    high, low = split_terms(modes_ref[...].reshape(-1, feat_count))
+    for step in range(peers):
+        order_ref[me ^ step] = block_refs[step][...]
+    high, low = split_terms(order_ref[...].reshape(-1, feat_count))
     spectrum = (
         dot(forward_high[...], high) + dot(forward_high[...], low) + dot(forward_low[...], high)
     )
@@ -274,40 +309,61 @@
         mixed_ref[0, :, part * feat_count : (part + 1) * feat_count] = parts[part]
     high, low = split_terms(jnp.concatenate(parts, axis=0))
     back = dot(inverse_high[...], high) + dot(inverse_high[...], low) + dot(inverse_low[...], high)
-    back_ref[...] = back.reshape(back_ref.shape)
-
-
-def mix(modes, weights, forward_table, inverse_table):
-    feat_count = modes.shape[-1]
+    order_ref[...] = back.reshape(order_ref.shape)
+    for step in range(peers):
+        back_refs[step][...] = order_ref[me ^ step]
+
+
+def mix(blocks, weights, forward_table, inverse_table):
+    rows, feat_count = blocks[0].shape
+    peers = len(blocks)
     count = weights.shape[1]
     scratch = pltpu.VMEM((count * feat_count // 64, 128), jnp.float32)
-    return pl.pallas_call(
-        mix_kernel,
-        out_shape=[
-            jax.ShapeDtypeStruct((1, count, 2 * feat_count), jnp.float32),
-            jax.ShapeDtypeStruct(modes.shape, jnp.float32),
-        ],
-        scratch_shapes=[scratch, scratch],
+    mixed, *back = pl.pallas_call(
+        functools.partial(mix_kernel, peers),
+        out_shape=[jax.ShapeDtypeStruct((1, count, 2 * feat_count), jnp.float32)]
+        + [jax.ShapeDtypeStruct(blocks[0].shape, jnp.float32)] * peers,
+        scratch_shapes=[pltpu.VMEM((peers, rows, feat_count), jnp.float32), scratch, scratch],
+        compiler_params=SMALL,
         name="mix",
-    )(modes, weights, *split_table(forward_table), *split_table(inverse_table))
-
-
-def output_kernel(place_ref, flow_ref, own_ref, other_ref, table_ref, local_ref, bias_ref, out_ref):
+    )(*blocks, weights, *split_table(forward_table), *split_table(inverse_table))
+    return mixed, back
+
+
+def output_kernel(peers, place_ref, flow_ref, table_ref, local_ref, bias_ref, *refs):
+    block_refs = refs[: 2 * peers]
+    out_ref, order_ref, stack_ref, wide_ref, level_ref = refs[2 * peers :]
     step = pl.program_id(0)
-    rows = table_ref.shape[-1] // 3 // 2 // own_ref.shape[0]
     feat_count = flow_ref.shape[-1]
-    pair = pl.ds(pl.multiple_of(step // 2 * rows, rows), rows)
-    both = jnp.concatenate([own_ref[:, pair, :], other_ref[:, pair, :]], axis=0)
-    high, low = split_terms(both.reshape(-1, feat_count))
-    stacked = jnp.concatenate([high, low, high], axis=0)
+    channels = local_ref.shape[0]
+    width = wide_ref.shape[0]
+    pairs = stack_ref.shape[0]
+    rows = order_ref.shape[1] // pairs
+
+    @pl.when(step == 0)
+    def _():
+        me = lax.axis_index("gx")
+        for side in range(2):
+            for turn in range(peers):
+                order_ref[side * peers + (me ^ turn)] = block_refs[side * peers + turn][...]
+        for pair in range(pairs):
+            both = order_ref[:, pair * rows : (pair + 1) * rows, :].reshape(-1, feat_count)
+            high, low = split_terms(both)
+            stack_ref[pair] = jnp.concatenate([high, low, high], axis=0)
+        wide_ref[...] = jnp.zeros_like(wide_ref)
+        for start in range(0, width, channels):
+            span = slice(start, start + channels)
+            wide_ref[span, span] = local_ref[...]
+        for start in range(0, width, channels):
+            level_ref[:, start : start + channels] = bias_ref[...]
+
     table = table_ref[0, step % 2]
-    width = local_ref.shape[0]
     for start in range(0, feat_count, width):
         columns = slice(start, start + width)
         total = (
-            dot(table, stacked[:, columns])
-            + dot(flow_ref[0, :, columns], local_ref[...])
-            + bias_ref[:, columns]
+            dot(table, stack_ref[step // 2, :, columns])
+            + dot(flow_ref[0, :, columns], wide_ref[...])
+            + level_ref[...]
         )
         out_ref[0, :, columns] = (
             0.5 * total * (1.0 + lax.erf(total * math.sqrt(0.5)))
@@ -316,32 +372,40 @@
 
 def make_output(flow_field, own, other, table, local, bias):
     cells_x, cells_y, feat_count = flow_field.shape
+    peers = len(own)
+    rows = own[0].shape[0]
+    width = 256
     place = jnp.reshape(lax.axis_index("gy"), (1,))
     whole = lambda array: pl.BlockSpec(array.shape, lambda i, p: (0,) * array.ndim)
     block = pl.BlockSpec((1, cells_y, feat_count), lambda i, p: (i, 0, 0))
     return pl.pallas_call(
-        output_kernel,
+        functools.partial(output_kernel, peers),
         grid_spec=pltpu.PrefetchScalarGridSpec(
             num_scalar_prefetch=1,
             grid=(cells_x,),
             in_specs=[
                 block,
-                whole(own),
-                whole(other),
                 pl.BlockSpec((1,) + table.shape[1:], lambda i, p: (p[0], 0, 0, 0)),
                 whole(local),
                 whole(bias),
+            ]
+            + [whole(array) for array in own + other],
+            out_specs=block,
+            scratch_shapes=[
+                pltpu.VMEM((2 * peers, rows, feat_count), jnp.float32),
+                pltpu.VMEM((cells_x // 2, table.shape[-1], feat_count), jnp.bfloat16),
+                pltpu.VMEM((width, width), jnp.bfloat16),
+                pltpu.VMEM((1, width), jnp.float32),
             ],
-            out_specs=block,
         ),
         out_shape=jax.ShapeDtypeStruct(flow_field.shape, jnp.bfloat16),
+        compiler_params=SMALL,
         name="make_output",
-    )(place, flow_field, own, other, table, local, bias)
+    )(place, flow_field, table, local, bias, *own, *other)
 
 
 def row_body(flow_field, spectral_weight, local_weight, bias_terms):
     cells_x, cells_y, feat_count = flow_field.shape
-    channels = local_weight.shape[0]
     peers = lax.axis_size("gx")
     groups_y = lax.axis_size("gy")
     rows_ky = MY // groups_y // peers
@@ -352,26 +416,23 @@
     send, keep = forward_y(
         flow_field, forward_y_table(cells_y, groups_y, peers, rows_ky), peers, rows_ky
     )
-    modes = keep + lax.ppermute(send, "gy", swap)
-    modes = lax.all_to_all(modes, "gx", 0, 0, tiled=True)
+    blocks = exchange(combine(keep, lax.ppermute(send, "gy", swap)))
     mixed, back = mix(
-        modes,
+        blocks,
         spectral_weight,
         forward_x_table(cells_x, peers, rows_ky) * forward_scale,
         inverse_x_table(cells_x, peers, rows_ky),
     )
-    own = lax.all_to_all(back, "gx", 0, 0, tiled=True)
-    other = lax.ppermute(own, "gy", swap)
+    own = exchange(back)
+    other = [lax.ppermute(block, "gy", swap) for block in own]
     high, low = split_table(inverse_y_table(cells_y, groups_y, peers, rows_ky) * inverse_scale)
-    copies = 256 // channels
-    local = jnp.einsum("ij,co->icjo", jnp.eye(copies, dtype=local_weight.dtype), local_weight)
     output = make_output(
         flow_field,
         own,
         other,
         np.concatenate([high, high, low], axis=-1),
-        local.reshape(copies * channels, copies * channels),
-        jnp.tile(bias_terms, feat_count // channels)[None, :],
+        local_weight,
+        bias_terms[None, :],
     )
     return output, mixed
 

time: 44.8 us -> 44.7 us (level)
  blocking collectives: 28.6 us -> 0 us
  starting transfers between devices: 0.45 us -> 25.8 us
  waiting for transfers between devices: 1.38 us -> 10.2 us
  Pallas kernels: 9.83 us -> 5 us
  other arithmetic: 1.16 us -> 0 us
  local copies, waits for them, and re-layouts: 2.24 us -> 2.85 us
    all_to_all x2 -> x0, blocking collectives: 28.6 us -> none  [the longest x1 16.3 us: row_body(): modes = lax.all_to_all(modes, 'gx', 0, 0, tiled=True)]
    ppermute x2 -> x23, starting transfers between devices: 0.45 us -> 25.8 us  [the longest x14 23.6 us: exchange(): arrived.append(lax.ppermute(blocks[step], 'gx', pairs))]
    ppermute x2 -> x23, waiting for transfers between devices: 1.38 us -> 10.2 us  [the longest x14 8.15 us: exchange(): arrived.append(lax.ppermute(blocks[step], 'gx', pairs))]
    pallas_call x2 -> x3, Pallas kernels: 7.54 us -> 4.46 us  [the longest x1 2.87 us: make_output(): pl.pallas_call(functools.partial(output_kernel, peers), grid_spec=pltpu.P...]
    unnamed x8 -> x22, local copies, waits for them, and re-layouts: 0.72 us -> 2.85 us
    pallas_call x1, Pallas kernels: 2.28 us -> 0.54 us  [forward_y(): pl.pallas_call(forward_y_kernel, grid=(cells_x // 2,), in_specs=[pl.Block...]
    add x1 -> x0, other arithmetic: 0.99 us -> none  [row_body(): modes = keep + lax.ppermute(send, 'gy', swap)]
    reshape x1 -> x0, local copies, waits for them, and re-layouts: 0.85 us -> none  [row_body(): local.reshape(copies * channels, copies * channels)]
  transfers between devices with their start and end apart: 2 -> 23, of which waited for: 1 -> 10; matrix products, arithmetic and copies ran while one was open for 4% -> 0% of each run, Pallas kernels for 0% -> 0%
where the time goes in v2:
time: 44.7 us; the launch traced here: 44.5 us
  starting transfers between devices  25.8 us (58%)
  waiting for transfers between devices  10.2 us (23%)
  Pallas kernels  5 us (11%)
  local copies, waits for them, and re-layouts  2.85 us (6%)
  between operations  0.73 us (2%)
    ppermute x14, starting transfers between devices, exchange(): arrived.append(lax.ppermute(blocks[step], 'gx', pairs))  23.6 us
    ppermute x14, waiting for transfers between devices, exchange(): arrived.append(lax.ppermute(blocks[step], 'gx', pairs))  8.15 us
    pallas_call x1, Pallas kernels, make_output(): pl.pallas_call(functools.partial(output_kernel, peers), grid_spec=pltpu.P...  2.87 us
    unnamed x22, local copies, waits for them, and re-layouts  2.85 us
    ppermute x8, starting transfers between devices, row_body(): other = [lax.ppermute(block, 'gy', swap) for block in own]  1.68 us
    pallas_call x1, Pallas kernels, mix(): pl.pallas_call(functools.partial(mix_kernel, peers), out_shape=[jax.Shape...  1.56 us
    ppermute x1, waiting for transfers between devices, row_body(): blocks = exchange(combine(keep, lax.ppermute(send, 'gy', swap)))  1.16 us
  transfers between devices with their start and end apart: 23, of which 10 were waited for; matrix products, arithmetic and copies ran while one was open for 0% of the time, Pallas kernels for 0%

profile of v2, /device:TPU:0, one launch (start us, length us, event | category | flops | bytes accessed | tf_op | source)
XLA Modules:
  0.0 44.5 jit_solution(12348437924038430886)
XLA Ops:
  0.6 1.2 %copy-done = bf16[4,256,512]{2,1,0:T(8,128)(2,1)S(1)} copy-done((bf16[4,256,512]{2,1,0:T(8,128)(2,1)S(1)}, bf16[4,256,512]{2,1,0:T(8,128)(2,1)}, u32[]{:S(2)}) %copy-start) | copy-done | bytes 1048600
  1.9 0.9 %copy-done.4 = bf16[2,128,512]{2,1,0:T(8,128)(2,1)S(1)} copy-done((bf16[2,128,512]{2,1,0:T(8,128)(2,1)S(1)}, bf16[2,128,512]{2,1,0:T(8,128)(2,1)}, u32[]{:S(2)}) %copy-start.4) | copy-done | bytes 262168
  2.8 0.5 %forward_y.1 = (f32[8,16,512]{2,1,0:T(8,128)S(1)}, f32[8,16,512]{2,1,0:T(8,128)S(1)}) custom-call(bf16[4,256,512]{2,1,0:T(8,128)(2,1)S(1)} %copy-done, bf16[2,128,512]{2,1,0:T(8,128)(2,1)S(1)} %copy-done.4), custom_call_target="tpu_custom_call" | custom-call | tf_op jit(solution)/shard_map/forward_y/pallas_call | solution.py:222
  3.4 0.5 %collective-permute-start = (f32[8,16,512]{2,1,0:T(8,128)S(1)}, f32[8,16,512]{2,1,0:T(8,128)S(1)}, u32[]{:S(2)}, u32[]{:S(2)}) collective-permute-start(f32[8,16,512]{2,1,0:T(8,128)S(1)} %get-tuple-element.22), channel_id=1, source_target_pairs={{0,1},{1,0},{2,3},{3,2},{4,5},{5,4},{6,7},{7,6},{8,9},{9,8},{10,11... | collective-permute-start | bytes 786440 | tf_op jit(solution)/shard_map/ppermute | solution.py:419
  3.9 1.2 %collective-permute-done.arrived_ref = f32[8,16,512]{2,1,0:T(8,128)S(1)} collective-permute-done((f32[8,16,512]{2,1,0:T(8,128)S(1)}, f32[8,16,512]{2,1,0:T(8,128)S(1)}, u32[]{:S(2)}, u32[]{:S(2)}) %collective-permute-start) | collective-permute-done | bytes 262176 | tf_op jit(solution)/shard_map/ppermute | solution.py:419
  5.1 2.9 %collective-permute-start.1 = (f32[16,512]{1,0:T(8,128)S(1)}, f32[16,512]{1,0:T(8,128)S(1)}, u32[]{:S(2)}, u32[]{:S(2)}) collective-permute-start(f32[16,512]{1,0:T(8,128)S(1)} %get-tuple-element.24), channel_id=1, source_target_pairs={{0,2},{2,0},{4,6},{6,4},{8,10},{10,8},{12,14},{14,12},{1,3},{3,1},... | collective-permute-start | bytes 98312 | tf_op jit(solution)/shard_map/ppermute | solution.py:257
  8.0 1.6 %collective-permute-start.2 = (f32[16,512]{1,0:T(8,128)S(1)}, f32[16,512]{1,0:T(8,128)S(1)}, u32[]{:S(2)}, u32[]{:S(2)}) collective-permute-start(f32[16,512]{1,0:T(8,128)S(1)} %get-tuple-element.25), channel_id=1, source_target_pairs={{0,4},{2,6},{4,0},{6,2},{8,12},{10,14},{12,8},{14,10},{1,5},{3,7},... | collective-permute-start | bytes 98312 | tf_op jit(solution)/shard_map/ppermute | solution.py:257
  9.6 3.0 %collective-permute-start.4 = (f32[16,512]{1,0:T(8,128)S(1)}, f32[16,512]{1,0:T(8,128)S(1)}, u32[]{:S(2)}, u32[]{:S(2)}) collective-permute-start(f32[16,512]{1,0:T(8,128)S(1)} %get-tuple-element.27), channel_id=1, source_target_pairs={{0,8},{2,10},{4,12},{6,14},{8,0},{10,2},{12,4},{14,6},{1,9},{3,11}... | collective-permute-start | bytes 98312 | tf_op jit(solution)/shard_map/ppermute | solution.py:257
  12.6 1.3 %collective-permute-start.5 = (f32[16,512]{1,0:T(8,128)S(1)}, f32[16,512]{1,0:T(8,128)S(1)}, u32[]{:S(2)}, u32[]{:S(2)}) collective-permute-start(f32[16,512]{1,0:T(8,128)S(1)} %get-tuple-element.28), channel_id=1, source_target_pairs={{0,10},{2,8},{4,14},{6,12},{8,2},{10,0},{12,6},{14,4},{1,11},{3,9}... | collective-permute-start | bytes 98312 | tf_op jit(solution)/shard_map/ppermute | solution.py:257
  13.9 3.6 %collective-permute-start.6 = (f32[16,512]{1,0:T(8,128)S(1)}, f32[16,512]{1,0:T(8,128)S(1)}, u32[]{:S(2)}, u32[]{:S(2)}) collective-permute-start(f32[16,512]{1,0:T(8,128)S(1)} %get-tuple-element.29), channel_id=1, source_target_pairs={{0,12},{2,14},{4,8},{6,10},{8,4},{10,6},{12,0},{14,2},{1,13},{3,15... | collective-permute-start | bytes 98312 | tf_op jit(solution)/shard_map/ppermute | solution.py:257
  17.6 0.8 %collective-permute-done.5.refs_5_ = f32[16,512]{1,0:T(8,128)S(1)} collective-permute-done((f32[16,512]{1,0:T(8,128)S(1)}, f32[16,512]{1,0:T(8,128)S(1)}, u32[]{:S(2)}, u32[]{:S(2)}) %collective-permute-start.5) | collective-permute-done | bytes 32800 | tf_op jit(solution)/shard_map/ppermute | solution.py:257
  18.3 1.4 %collective-permute-done.6.refs_6_ = f32[16,512]{1,0:T(8,128)S(1)} collective-permute-done((f32[16,512]{1,0:T(8,128)S(1)}, f32[16,512]{1,0:T(8,128)S(1)}, u32[]{:S(2)}, u32[]{:S(2)}) %collective-permute-start.6) | collective-permute-done | bytes 32800 | tf_op jit(solution)/shard_map/ppermute | solution.py:257
  19.7 4.4 %collective-permute-done.7.refs_7_ = f32[16,512]{1,0:T(8,128)S(1)} collective-permute-done((f32[16,512]{1,0:T(8,128)S(1)}, f32[16,512]{1,0:T(8,128)S(1)}, u32[]{:S(2)}, u32[]{:S(2)}) %collective-permute-start.7) | collective-permute-done | bytes 32800 | tf_op jit(solution)/shard_map/ppermute | solution.py:257
  24.1 1.6 %mix.1 = (f32[1,64,1024]{2,1,0:T(8,128)}, f32[16,512]{1,0:T(8,128)S(1)}, f32[16,512]{1,0:T(8,128)S(1)}, f32[16,512]{1,0:T(8,128)S(1)}, f32[16,512]{1,0:T(8,128)S...) custom-call(f32[16,512]{1,0:T(8,128)S(1)} %get-tuple-element.23.refs_0_, ...), custom_call_target="tpu_custom_call" | custom-call | tf_op jit(solution)/shard_map/mix/pallas_call | solution.py:322
  25.7 0.5 %collective-permute-start.8 = (f32[16,512]{1,0:T(8,128)S(1)}, f32[16,512]{1,0:T(8,128)S(1)}, u32[]{:S(2)}, u32[]{:S(2)}) collective-permute-start(f32[16,512]{1,0:T(8,128)S(1)} %get-tuple-element.32), channel_id=1, source_target_pairs={{0,2},{2,0},{4,6},{6,4},{8,10},{10,8},{12,14},{14,12},{1,3},{3,1},... | collective-permute-start | bytes 98312 | tf_op jit(solution)/shard_map/ppermute | solution.py:257
  26.3 3.0 %collective-permute-start.10 = (f32[16,512]{1,0:T(8,128)S(1)}, f32[16,512]{1,0:T(8,128)S(1)}, u32[]{:S(2)}, u32[]{:S(2)}) collective-permute-start(f32[16,512]{1,0:T(8,128)S(1)} %get-tuple-element.34), channel_id=1, source_target_pairs={{0,6},{2,4},{4,2},{6,0},{8,14},{10,12},{12,10},{14,8},{1,7},{3,5},... | collective-permute-start | bytes 98312 | tf_op jit(solution)/shard_map/ppermute | solution.py:257
  29.2 2.9 %collective-permute-start.12 = (f32[16,512]{1,0:T(8,128)S(1)}, f32[16,512]{1,0:T(8,128)S(1)}, u32[]{:S(2)}, u32[]{:S(2)}) collective-permute-start(f32[16,512]{1,0:T(8,128)S(1)} %get-tuple-element.36), channel_id=1, source_target_pairs={{0,10},{2,8},{4,14},{6,12},{8,2},{10,0},{12,6},{14,4},{1,11},{3,9}... | collective-permute-start | bytes 98312 | tf_op jit(solution)/shard_map/ppermute | solution.py:257
  32.5 4.4 %collective-permute-start.14 = (f32[16,512]{1,0:T(8,128)S(1)}, f32[16,512]{1,0:T(8,128)S(1)}, u32[]{:S(2)}, u32[]{:S(2)}) collective-permute-start(f32[16,512]{1,0:T(8,128)S(1)} %get-tuple-element.38), channel_id=1, source_target_pairs={{0,14},{2,12},{4,10},{6,8},{8,6},{10,4},{12,2},{14,0},{1,15},{3,13... | collective-permute-start | bytes 98312 | tf_op jit(solution)/shard_map/ppermute | solution.py:257
  36.9 0.5 %collective-permute-start.16 = (f32[16,512]{1,0:T(8,128)S(1)}, f32[16,512]{1,0:T(8,128)S(1)}, u32[]{:S(2)}, u32[]{:S(2)}) collective-permute-start(f32[16,512]{1,0:T(8,128)S(1)} %collective-permute-done.8.refs_1_), channel_id=1, source_target_pairs={{0,1},{1,0},{2,3},{3,2},{4,5},{5,4},{6,7},{7,6},{8,9},{9,8},{10,11... | collective-permute-start | bytes 98312 | tf_op jit(solution)/shard_map/ppermute | solution.py:427
  37.9 1.2 %collective-permute-done.14.refs_7_ = f32[16,512]{1,0:T(8,128)S(1)} collective-permute-done((f32[16,512]{1,0:T(8,128)S(1)}, f32[16,512]{1,0:T(8,128)S(1)}, u32[]{:S(2)}, u32[]{:S(2)}) %collective-permute-start.14) | collective-permute-done | bytes 32800 | tf_op jit(solution)/shard_map/ppermute | solution.py:257
  39.1 0.5 %collective-permute-start.20 = (f32[16,512]{1,0:T(8,128)S(1)}, f32[16,512]{1,0:T(8,128)S(1)}, u32[]{:S(2)}, u32[]{:S(2)}) collective-permute-start(f32[16,512]{1,0:T(8,128)S(1)} %collective-permute-done.12.refs_5_), channel_id=1, source_target_pairs={{0,1},{1,0},{2,3},{3,2},{4,5},{5,4},{6,7},{7,6},{8,9},{9,8},{10,11... | collective-permute-start | bytes 98312 | tf_op jit(solution)/shard_map/ppermute | solution.py:427
  39.7 0.4 collective-permute-start.22
  41.0 0.6 %copy-done.10 = f32[64]{0:T(128)S(1)} copy-done((f32[64]{0:T(128)S(1)}, f32[64]{0:T(128)}, u32[]{:S(2)}) %copy-start.10) | copy-done | bytes 280
  41.6 2.9 %make_output.1 = bf16[4,256,512]{2,1,0:T(8,128)(2,1)} custom-call(s32[1]{0:T(128)} %bitcast.place_ref, bf16[4,256,512]{2,1,0:T(8,128)(2,1)S(1)} %copy-done.1, bf16[2,2,256,384]{3,2,1,0:T(8,128)(2,1)S(1)} %copy-done.3, bf16[64,64]{1,0:T(8,128)(2,1)S(1)} %copy-done.9, f32[1,64]{1,0:T(1,128)S(1)} %bitcast.2, f32[16,512]{1,0:T(8,128)S(1)} %get-tuple-element.31.refs_0_, ...), custom_call_target="tpu_custom_call" | custom-call | tf_op jit(solution)/shard_map/make_output/pallas_call | solution.py:381
  (48 shorter events, 2.0 us)
Async XLA Ops:
  3.4 37.6 %copy-start.1 = (bf16[4,256,512]{2,1,0:T(8,128)(2,1)S(1)}, bf16[4,256,512]{2,1,0:T(8,128)(2,1)}, u32[]{:S(2)}) copy-start(bf16[4,256,512]{2,1,0:T(8,128)(2,1)} %flow_ref.3) | copy-start | bytes 3145732
  3.4 1.7 %collective-permute-start = (f32[8,16,512]{2,1,0:T(8,128)S(1)}, f32[8,16,512]{2,1,0:T(8,128)S(1)}, u32[]{:S(2)}, u32[]{:S(2)}) collective-permute-start(f32[8,16,512]{2,1,0:T(8,128)S(1)} %get-tuple-element.22), channel_id=1, source_target_pairs={{0,1},{1,0},{2,3},{3,2},{4,5},{5,4},{6,7},{7,6},{8,9},{9,8},{10,11... | collective-permute-start | bytes 786440 | tf_op jit(solution)/shard_map/ppermute | solution.py:419
  5.1 8.8 %collective-permute-start.1 = (f32[16,512]{1,0:T(8,128)S(1)}, f32[16,512]{1,0:T(8,128)S(1)}, u32[]{:S(2)}, u32[]{:S(2)}) collective-permute-start(f32[16,512]{1,0:T(8,128)S(1)} %get-tuple-element.24), channel_id=1, source_target_pairs={{0,2},{2,0},{4,6},{6,4},{8,10},{10,8},{12,14},{14,12},{1,3},{3,1},... | collective-permute-start | bytes 98312 | tf_op jit(solution)/shard_map/ppermute | solution.py:257
  8.0 9.5 %collective-permute-start.2 = (f32[16,512]{1,0:T(8,128)S(1)}, f32[16,512]{1,0:T(8,128)S(1)}, u32[]{:S(2)}, u32[]{:S(2)}) collective-permute-start(f32[16,512]{1,0:T(8,128)S(1)} %get-tuple-element.25), channel_id=1, source_target_pairs={{0,4},{2,6},{4,0},{6,2},{8,12},{10,14},{12,8},{14,10},{1,5},{3,7},... | collective-permute-start | bytes 98312 | tf_op jit(solution)/shard_map/ppermute | solution.py:257
  9.6 7.9 %collective-permute-start.3 = (f32[16,512]{1,0:T(8,128)S(1)}, f32[16,512]{1,0:T(8,128)S(1)}, u32[]{:S(2)}, u32[]{:S(2)}) collective-permute-start(f32[16,512]{1,0:T(8,128)S(1)} %get-tuple-element.26), channel_id=1, source_target_pairs={{0,6},{2,4},{4,2},{6,0},{8,14},{10,12},{12,10},{14,8},{1,7},{3,5},... | collective-permute-start | bytes 98312 | tf_op jit(solution)/shard_map/ppermute | solution.py:257
  9.6 7.9 %collective-permute-start.4 = (f32[16,512]{1,0:T(8,128)S(1)}, f32[16,512]{1,0:T(8,128)S(1)}, u32[]{:S(2)}, u32[]{:S(2)}) collective-permute-start(f32[16,512]{1,0:T(8,128)S(1)} %get-tuple-element.27), channel_id=1, source_target_pairs={{0,8},{2,10},{4,12},{6,14},{8,0},{10,2},{12,4},{14,6},{1,9},{3,11}... | collective-permute-start | bytes 98312 | tf_op jit(solution)/shard_map/ppermute | solution.py:257
  12.6 5.7 %collective-permute-start.5 = (f32[16,512]{1,0:T(8,128)S(1)}, f32[16,512]{1,0:T(8,128)S(1)}, u32[]{:S(2)}, u32[]{:S(2)}) collective-permute-start(f32[16,512]{1,0:T(8,128)S(1)} %get-tuple-element.28), channel_id=1, source_target_pairs={{0,10},{2,8},{4,14},{6,12},{8,2},{10,0},{12,6},{14,4},{1,11},{3,9}... | collective-permute-start | bytes 98312 | tf_op jit(solution)/shard_map/ppermute | solution.py:257
  13.9 5.8 %collective-permute-start.6 = (f32[16,512]{1,0:T(8,128)S(1)}, f32[16,512]{1,0:T(8,128)S(1)}, u32[]{:S(2)}, u32[]{:S(2)}) collective-permute-start(f32[16,512]{1,0:T(8,128)S(1)} %get-tuple-element.29), channel_id=1, source_target_pairs={{0,12},{2,14},{4,8},{6,10},{8,4},{10,6},{12,0},{14,2},{1,13},{3,15... | collective-permute-start | bytes 98312 | tf_op jit(solution)/shard_map/ppermute | solution.py:257
  17.5 6.6 %collective-permute-start.7 = (f32[16,512]{1,0:T(8,128)S(1)}, f32[16,512]{1,0:T(8,128)S(1)}, u32[]{:S(2)}, u32[]{:S(2)}) collective-permute-start(f32[16,512]{1,0:T(8,128)S(1)} %get-tuple-element.30), channel_id=1, source_target_pairs={{0,14},{2,12},{4,10},{6,8},{8,6},{10,4},{12,2},{14,0},{1,15},{3,13... | collective-permute-start | bytes 98312 | tf_op jit(solution)/shard_map/ppermute | solution.py:257
  25.7 6.4 %collective-permute-start.8 = (f32[16,512]{1,0:T(8,128)S(1)}, f32[16,512]{1,0:T(8,128)S(1)}, u32[]{:S(2)}, u32[]{:S(2)}) collective-permute-start(f32[16,512]{1,0:T(8,128)S(1)} %get-tuple-element.32), channel_id=1, source_target_pairs={{0,2},{2,0},{4,6},{6,4},{8,10},{10,8},{12,14},{14,12},{1,3},{3,1},... | collective-permute-start | bytes 98312 | tf_op jit(solution)/shard_map/ppermute | solution.py:257
  26.2 6.2 %collective-permute-start.9 = (f32[16,512]{1,0:T(8,128)S(1)}, f32[16,512]{1,0:T(8,128)S(1)}, u32[]{:S(2)}, u32[]{:S(2)}) collective-permute-start(f32[16,512]{1,0:T(8,128)S(1)} %get-tuple-element.33), channel_id=1, source_target_pairs={{0,4},{2,6},{4,0},{6,2},{8,12},{10,14},{12,8},{14,10},{1,5},{3,7},... | collective-permute-start | bytes 98312 | tf_op jit(solution)/shard_map/ppermute | solution.py:257
  26.3 10.6 %collective-permute-start.10 = (f32[16,512]{1,0:T(8,128)S(1)}, f32[16,512]{1,0:T(8,128)S(1)}, u32[]{:S(2)}, u32[]{:S(2)}) collective-permute-start(f32[16,512]{1,0:T(8,128)S(1)} %get-tuple-element.34), channel_id=1, source_target_pairs={{0,6},{2,4},{4,2},{6,0},{8,14},{10,12},{12,10},{14,8},{1,7},{3,5},... | collective-permute-start | bytes 98312 | tf_op jit(solution)/shard_map/ppermute | solution.py:257
  29.2 7.7 %collective-permute-start.11 = (f32[16,512]{1,0:T(8,128)S(1)}, f32[16,512]{1,0:T(8,128)S(1)}, u32[]{:S(2)}, u32[]{:S(2)}) collective-permute-start(f32[16,512]{1,0:T(8,128)S(1)} %get-tuple-element.35), channel_id=1, source_target_pairs={{0,8},{2,10},{4,12},{6,14},{8,0},{10,2},{12,4},{14,6},{1,9},{3,11}... | collective-permute-start | bytes 98312 | tf_op jit(solution)/shard_map/ppermute | solution.py:257
  29.2 8.2 %collective-permute-start.12 = (f32[16,512]{1,0:T(8,128)S(1)}, f32[16,512]{1,0:T(8,128)S(1)}, u32[]{:S(2)}, u32[]{:S(2)}) collective-permute-start(f32[16,512]{1,0:T(8,128)S(1)} %get-tuple-element.36), channel_id=1, source_target_pairs={{0,10},{2,8},{4,14},{6,12},{8,2},{10,0},{12,6},{14,4},{1,11},{3,9}... | collective-permute-start | bytes 98312 | tf_op jit(solution)/shard_map/ppermute | solution.py:257
  32.1 5.7 %collective-permute-start.13 = (f32[16,512]{1,0:T(8,128)S(1)}, f32[16,512]{1,0:T(8,128)S(1)}, u32[]{:S(2)}, u32[]{:S(2)}) collective-permute-start(f32[16,512]{1,0:T(8,128)S(1)} %get-tuple-element.37), channel_id=1, source_target_pairs={{0,12},{2,14},{4,8},{6,10},{8,4},{10,6},{12,0},{14,2},{1,13},{3,15... | collective-permute-start | bytes 98312 | tf_op jit(solution)/shard_map/ppermute | solution.py:257
  32.5 6.6 %collective-permute-start.14 = (f32[16,512]{1,0:T(8,128)S(1)}, f32[16,512]{1,0:T(8,128)S(1)}, u32[]{:S(2)}, u32[]{:S(2)}) collective-permute-start(f32[16,512]{1,0:T(8,128)S(1)} %get-tuple-element.38), channel_id=1, source_target_pairs={{0,14},{2,12},{4,10},{6,8},{8,6},{10,4},{12,2},{14,0},{1,15},{3,13... | collective-permute-start | bytes 98312 | tf_op jit(solution)/shard_map/ppermute | solution.py:257
  36.9 2.2 %collective-permute-start.15 = (f32[16,512]{1,0:T(8,128)S(1)}, f32[16,512]{1,0:T(8,128)S(1)}, u32[]{:S(2)}, u32[]{:S(2)}) collective-permute-start(f32[16,512]{1,0:T(8,128)S(1)} %get-tuple-element.31.refs_0_), channel_id=1, source_target_pairs={{0,1},{1,0},{2,3},{3,2},{4,5},{5,4},{6,7},{7,6},{8,9},{9,8},{10,11... | collective-permute-start | bytes 98312 | tf_op jit(solution)/shard_map/ppermute | solution.py:427
  36.9 2.7 %collective-permute-start.16 = (f32[16,512]{1,0:T(8,128)S(1)}, f32[16,512]{1,0:T(8,128)S(1)}, u32[]{:S(2)}, u32[]{:S(2)}) collective-permute-start(f32[16,512]{1,0:T(8,128)S(1)} %collective-permute-done.8.refs_1_), channel_id=1, source_target_pairs={{0,1},{1,0},{2,3},{3,2},{4,5},{5,4},{6,7},{7,6},{8,9},{9,8},{10,11... | collective-permute-start | bytes 98312 | tf_op jit(solution)/shard_map/ppermute | solution.py:427
  37.4 2.3 %collective-permute-start.17 = (f32[16,512]{1,0:T(8,128)S(1)}, f32[16,512]{1,0:T(8,128)S(1)}, u32[]{:S(2)}, u32[]{:S(2)}) collective-permute-start(f32[16,512]{1,0:T(8,128)S(1)} %collective-permute-done.9.refs_2_), channel_id=1, source_target_pairs={{0,1},{1,0},{2,3},{3,2},{4,5},{5,4},{6,7},{7,6},{8,9},{9,8},{10,11... | collective-permute-start | bytes 98312 | tf_op jit(solution)/shard_map/ppermute | solution.py:427
  37.8 2.3 %collective-permute-start.18 = (f32[16,512]{1,0:T(8,128)S(1)}, f32[16,512]{1,0:T(8,128)S(1)}, u32[]{:S(2)}, u32[]{:S(2)}) collective-permute-start(f32[16,512]{1,0:T(8,128)S(1)} %collective-permute-done.10.refs_3_), channel_id=1, source_target_pairs={{0,1},{1,0},{2,3},{3,2},{4,5},{5,4},{6,7},{7,6},{8,9},{9,8},{10,11... | collective-permute-start | bytes 98312 | tf_op jit(solution)/shard_map/ppermute | solution.py:427
  39.1 1.2 %collective-permute-start.19 = (f32[16,512]{1,0:T(8,128)S(1)}, f32[16,512]{1,0:T(8,128)S(1)}, u32[]{:S(2)}, u32[]{:S(2)}) collective-permute-start(f32[16,512]{1,0:T(8,128)S(1)} %collective-permute-done.11.refs_4_), channel_id=1, source_target_pairs={{0,1},{1,0},{2,3},{3,2},{4,5},{5,4},{6,7},{7,6},{8,9},{9,8},{10,11... | collective-permute-start | bytes 98312 | tf_op jit(solution)/shard_map/ppermute | solution.py:427
  39.1 1.4 %collective-permute-start.20 = (f32[16,512]{1,0:T(8,128)S(1)}, f32[16,512]{1,0:T(8,128)S(1)}, u32[]{:S(2)}, u32[]{:S(2)}) collective-permute-start(f32[16,512]{1,0:T(8,128)S(1)} %collective-permute-done.12.refs_5_), channel_id=1, source_target_pairs={{0,1},{1,0},{2,3},{3,2},{4,5},{5,4},{6,7},{7,6},{8,9},{9,8},{10,11... | collective-permute-start | bytes 98312 | tf_op jit(solution)/shard_map/ppermute | solution.py:427
  39.6 1.2 %collective-permute-start.21 = (f32[16,512]{1,0:T(8,128)S(1)}, f32[16,512]{1,0:T(8,128)S(1)}, u32[]{:S(2)}, u32[]{:S(2)}) collective-permute-start(f32[16,512]{1,0:T(8,128)S(1)} %collective-permute-done.13.refs_6_), channel_id=1, source_target_pairs={{0,1},{1,0},{2,3},{3,2},{4,5},{5,4},{6,7},{7,6},{8,9},{9,8},{10,11... | collective-permute-start | bytes 98312 | tf_op jit(solution)/shard_map/ppermute | solution.py:427
  39.7 1.3 %collective-permute-start.22 = (f32[16,512]{1,0:T(8,128)S(1)}, f32[16,512]{1,0:T(8,128)S(1)}, u32[]{:S(2)}, u32[]{:S(2)}) collective-permute-start(f32[16,512]{1,0:T(8,128)S(1)} %collective-permute-done.14.refs_7_), channel_id=1, source_target_pairs={{0,1},{1,0},{2,3},{3,2},{4,5},{5,4},{6,7},{7,6},{8,9},{9,8},{10,11... | collective-permute-start | bytes 98312 | tf_op jit(solution)/shard_map/ppermute | solution.py:427
  (10 other events, 160.6 us)

commit v3 on v1

--- a/solution.py
+++ b/solution.py
@@ -1,4 +1,3 @@
-import functools
 import math
 
 import jax
@@ -126,6 +125,9 @@
     return (output, mixed_local.reshape(1, quota_rows, 2 * feat_count))
 
 
+SMALL = pltpu.CompilerParams(vmem_limit_bytes=20 * 1024 * 1024)
+
+
 def angles(count, places, extent):
     index = np.arange(count)
     waves = np.where(index < count // 2, index, index - count)
@@ -202,29 +204,43 @@
     return jnp.dot(left, right, preferred_element_type=jnp.float32)
 
 
-def forward_y_kernel(flow_ref, table_ref, send_ref, keep_ref):
-    table = table_ref[lax.axis_index("gy")]
-    pairs, cells_y, feat_count = flow_ref.shape
-    result = dot(table, flow_ref[...].reshape(pairs * cells_y, feat_count))
-    result = result.reshape((2,) + send_ref.shape)
-    send_ref[...] = result[0]
-    keep_ref[...] = result[1]
+def forward_y_kernel(flow_hbm, table_hbm, send_ref, keep_ref, flow_ref, table_ref, arrivals):
+    cells_x, cells_y, feat_count = flow_ref.shape
+    rows = table_ref.shape[0] // 2 // send_ref.shape[0]
+    table_copy = pltpu.make_async_copy(
+        table_hbm.at[lax.axis_index("gy")], table_ref, arrivals.at[cells_x]
+    )
+    table_copy.start()
+    copies = []
+    for x in range(cells_x):
+        copies.append(pltpu.make_async_copy(flow_hbm.at[x], flow_ref.at[x], arrivals.at[x]))
+        copies[x].start()
+    table_copy.wait()
+    for pair in range(cells_x // 2):
+        copies[2 * pair].wait()
+        copies[2 * pair + 1].wait()
+        flow = flow_ref[2 * pair : 2 * pair + 2].reshape(2 * cells_y, feat_count)
+        result = dot(table_ref[...], flow).reshape(2, send_ref.shape[0], rows, feat_count)
+        send_ref[:, pair * rows : (pair + 1) * rows, :] = result[0]
+        keep_ref[:, pair * rows : (pair + 1) * rows, :] = result[1]
 
 
 def forward_y(flow_field, table, peers, rows_ky):
     cells_x, cells_y, feat_count = flow_field.shape
-    rows = 4 * rows_ky
-    shape = jax.ShapeDtypeStruct((peers, cells_x // 2 * rows, feat_count), jnp.float32)
-    spec = pl.BlockSpec((peers, rows, feat_count), lambda i: (0, i, 0))
+    shape = jax.ShapeDtypeStruct((peers, cells_x * 2 * rows_ky, feat_count), jnp.float32)
+    spec = pl.BlockSpec(memory_space=pltpu.VMEM)
+    source = pl.BlockSpec(memory_space=pltpu.HBM)
     return pl.pallas_call(
         forward_y_kernel,
-        grid=(cells_x // 2,),
-        in_specs=[
-            pl.BlockSpec((2, cells_y, feat_count), lambda i: (i, 0, 0)),
-            pl.BlockSpec(table.shape, lambda i: (0, 0, 0)),
-        ],
+        in_specs=[source, source],
         out_specs=[spec, spec],
         out_shape=[shape, shape],
+        scratch_shapes=[
+            pltpu.VMEM(flow_field.shape, flow_field.dtype),
+            pltpu.VMEM(table.shape[1:], table.dtype),
+            pltpu.SemaphoreType.DMA((cells_x + 1,)),
+        ],
+        compiler_params=SMALL,
         name="forward_y",
     )(flow_field, table)
 
@@ -288,26 +304,42 @@
             jax.ShapeDtypeStruct(modes.shape, jnp.float32),
         ],
         scratch_shapes=[scratch, scratch],
+        compiler_params=SMALL,
         name="mix",
     )(modes, weights, *split_table(forward_table), *split_table(inverse_table))
 
 
-def output_kernel(place_ref, flow_ref, own_ref, other_ref, table_ref, local_ref, bias_ref, out_ref):
+def output_kernel(
+    place_ref, flow_ref, table_ref, local_ref, bias_ref, own_ref, other_ref,
+    out_ref, stack_ref, wide_ref, level_ref,
+):
     step = pl.program_id(0)
-    rows = table_ref.shape[-1] // 3 // 2 // own_ref.shape[0]
     feat_count = flow_ref.shape[-1]
-    pair = pl.ds(pl.multiple_of(step // 2 * rows, rows), rows)
-    both = jnp.concatenate([own_ref[:, pair, :], other_ref[:, pair, :]], axis=0)
-    high, low = split_terms(both.reshape(-1, feat_count))
-    stacked = jnp.concatenate([high, low, high], axis=0)
+    channels = local_ref.shape[0]
+    width = wide_ref.shape[0]
+    pairs = stack_ref.shape[0]
+    rows = own_ref.shape[1] // pairs
+
+    @pl.when(step == 0)
+    def _():
+        for pair in range(pairs):
+            span = slice(pair * rows, (pair + 1) * rows)
+            both = jnp.concatenate([own_ref[:, span, :], other_ref[:, span, :]], axis=0)
+            high, low = split_terms(both.reshape(-1, feat_count))
+            stack_ref[pair] = jnp.concatenate([high, low, high], axis=0)
+        wide_ref[...] = jnp.zeros_like(wide_ref)
+        for start in range(0, width, channels):
+            span = slice(start, start + channels)
+            wide_ref[span, span] = local_ref[...]
+            level_ref[:, span] = bias_ref[...]
+
     table = table_ref[0, step % 2]
-    width = local_ref.shape[0]
     for start in range(0, feat_count, width):
         columns = slice(start, start + width)
         total = (
-            dot(table, stacked[:, columns])
-            + dot(flow_ref[0, :, columns], local_ref[...])
-            + bias_ref[:, columns]
+            dot(table, stack_ref[step // 2, :, columns])
+            + dot(flow_ref[0, :, columns], wide_ref[...])
+            + level_ref[...]
         )
         out_ref[0, :, columns] = (
             0.5 * total * (1.0 + lax.erf(total * math.sqrt(0.5)))
@@ -316,6 +348,7 @@
 
 def make_output(flow_field, own, other, table, local, bias):
     cells_x, cells_y, feat_count = flow_field.shape
+    width = 256
     place = jnp.reshape(lax.axis_index("gy"), (1,))
     whole = lambda array: pl.BlockSpec(array.shape, lambda i, p: (0,) * array.ndim)
     block = pl.BlockSpec((1, cells_y, feat_count), lambda i, p: (i, 0, 0))
@@ -326,22 +359,27 @@
             grid=(cells_x,),
             in_specs=[
                 block,
-                whole(own),
-                whole(other),
                 pl.BlockSpec((1,) + table.shape[1:], lambda i, p: (p[0], 0, 0, 0)),
                 whole(local),
                 whole(bias),
+                whole(own),
+                whole(other),
             ],
             out_specs=block,
+            scratch_shapes=[
+                pltpu.VMEM((cells_x // 2, table.shape[-1], feat_count), jnp.bfloat16),
+                pltpu.VMEM((width, width), jnp.bfloat16),
+                pltpu.VMEM((1, width), jnp.float32),
+            ],
         ),
         out_shape=jax.ShapeDtypeStruct(flow_field.shape, jnp.bfloat16),
+        compiler_params=SMALL,
         name="make_output",
-    )(place, flow_field, own, other, table, local, bias)
+    )(place, flow_field, table, local, bias, own, other)
 
 
 def row_body(flow_field, spectral_weight, local_weight, bias_terms):
     cells_x, cells_y, feat_count = flow_field.shape
-    channels = local_weight.shape[0]
     peers = lax.axis_size("gx")
     groups_y = lax.axis_size("gy")
     rows_ky = MY // groups_y // peers
@@ -353,9 +391,8 @@
         flow_field, forward_y_table(cells_y, groups_y, peers, rows_ky), peers, rows_ky
     )
     modes = keep + lax.ppermute(send, "gy", swap)
-    modes = lax.all_to_all(modes, "gx", 0, 0, tiled=True)
     mixed, back = mix(
-        modes,
+        lax.all_to_all(modes, "gx", 0, 0, tiled=True),
         spectral_weight,
         forward_x_table(cells_x, peers, rows_ky) * forward_scale,
         inverse_x_table(cells_x, peers, rows_ky),
@@ -363,15 +400,13 @@
     own = lax.all_to_all(back, "gx", 0, 0, tiled=True)
     other = lax.ppermute(own, "gy", swap)
     high, low = split_table(inverse_y_table(cells_y, groups_y, peers, rows_ky) * inverse_scale)
-    copies = 256 // channels
-    local = jnp.einsum("ij,co->icjo", jnp.eye(copies, dtype=local_weight.dtype), local_weight)
     output = make_output(
         flow_field,
         own,
         other,
         np.concatenate([high, high, low], axis=-1),
-        local.reshape(copies * channels, copies * channels),
-        jnp.tile(bias_terms, feat_count // channels)[None, :],
+        local_weight,
+        bias_terms[None, :],
     )
     return output, mixed
 

time: 44.8 us -> 40.7 us (0.908)
  Pallas kernels: 9.83 us -> 5.09 us
  waiting for transfers between devices: 1.38 us -> 2.69 us
  other arithmetic: 1.16 us -> 0.04 us
  local copies, waits for them, and re-layouts: 2.24 us -> 2.86 us
    unnamed x8 -> x22, local copies, waits for them, and re-layouts: 0.72 us -> 2.86 us
    pallas_call x1, Pallas kernels: 4.49 us -> 2.84 us  [make_output(): pl.pallas_call(output_kernel, grid_spec=pltpu.PrefetchScalarGridSpec(num_...]
    pallas_call x1, Pallas kernels: 2.28 us -> 0.73 us  [forward_y(): pl.pallas_call(forward_y_kernel, in_specs=[source, source], out_specs=[sp...]
    pallas_call x1, Pallas kernels: 3.05 us -> 1.52 us  [mix(): pl.pallas_call(mix_kernel, out_shape=[jax.ShapeDtypeStruct((1, count, 2 *...]
    ppermute x1, waiting for transfers between devices: 0.01 us -> 1.53 us  [row_body(): other = lax.ppermute(own, 'gy', swap)]
    add x1, other arithmetic: 0.99 us -> 0.04 us  [row_body(): modes = keep + lax.ppermute(send, 'gy', swap)]
    reshape x1 -> x0, local copies, waits for them, and re-layouts: 0.85 us -> none  [row_body(): local.reshape(copies * channels, copies * channels)]
    another operation x2 -> x0, local copies, waits for them, and re-layouts: 0.67 us -> none  [row_body(): jnp.tile(bias_terms, feat_count // channels)[None, :]]
  transfers between devices with their start and end apart: 2 -> 2, of which waited for: 1 -> 2; matrix products, arithmetic and copies ran while one was open for 4% -> 0% of each run, Pallas kernels for 0% -> 0%
where the time goes in v3:
time: 40.7 us; the launch traced here: 40.3 us
  blocking collectives  28.4 us (70%)
  Pallas kernels  5.09 us (13%)
  local copies, waits for them, and re-layouts  2.86 us (7%)
  waiting for transfers between devices  2.69 us (7%)
  between operations  0.73 us (2%)
  starting transfers between devices  0.52 us (1%)
    all_to_all x1, blocking collectives, row_body(): lax.all_to_all(modes, 'gx', 0, 0, tiled=True)  16.3 us
    all_to_all x1, blocking collectives, row_body(): own = lax.all_to_all(back, 'gx', 0, 0, tiled=True)  12.1 us
    unnamed x22, local copies, waits for them, and re-layouts  2.86 us
    pallas_call x1, Pallas kernels, make_output(): pl.pallas_call(output_kernel, grid_spec=pltpu.PrefetchScalarGridSpec(num_...  2.84 us
    ppermute x1, waiting for transfers between devices, row_body(): other = lax.ppermute(own, 'gy', swap)  1.53 us
    pallas_call x1, Pallas kernels, mix(): pl.pallas_call(mix_kernel, out_shape=[jax.ShapeDtypeStruct((1, count, 2 *...  1.52 us
    ppermute x1, waiting for transfers between devices, row_body(): modes = keep + lax.ppermute(send, 'gy', swap)  1.16 us
  transfers between devices with their start and end apart: 2, of which 2 were waited for; matrix products, arithmetic and copies ran while one was open for 0% of the time, Pallas kernels for 0%

profile of v3, /device:TPU:0, one launch (start us, length us, event | category | flops | bytes accessed | tf_op | source)
XLA Modules:
  0.0 40.3 jit_solution(14333030573122078695)
XLA Ops:
  0.6 0.0 copy-start
  0.6 1.2 %copy-done = bf16[4,256,512]{2,1,0:T(8,128)(2,1)S(1)} copy-done((bf16[4,256,512]{2,1,0:T(8,128)(2,1)S(1)}, bf16[4,256,512]{2,1,0:T(8,128)(2,1)}, u32[]{:S(2)}) %copy-start) | copy-done | bytes 1048600
  1.9 0.9 %copy-done.4 = bf16[2,128,512]{2,1,0:T(8,128)(2,1)S(1)} copy-done((bf16[2,128,512]{2,1,0:T(8,128)(2,1)S(1)}, bf16[2,128,512]{2,1,0:T(8,128)(2,1)}, u32[]{:S(2)}) %copy-start.4) | copy-done | bytes 262168
  2.8 0.7 %forward_y.1 = (f32[8,16,512]{2,1,0:T(8,128)S(1)}, f32[8,16,512]{2,1,0:T(8,128)S(1)}) custom-call(bf16[4,256,512]{2,1,0:T(8,128)(2,1)S(1)} %copy-done, bf16[2,128,512]{2,1,0:T(8,128)(2,1)S(1)} %copy-done.4), custom_call_target="tpu_custom_call" | custom-call | tf_op jit(solution)/shard_map/forward_y/pallas_call | solution.py:233
  3.6 0.5 %collective-permute-start = (f32[8,16,512]{2,1,0:T(8,128)S(1)}, f32[8,16,512]{2,1,0:T(8,128)S(1)}, u32[]{:S(2)}, u32[]{:S(2)}) collective-permute-start(f32[8,16,512]{2,1,0:T(8,128)S(1)} %get-tuple-element.7), channel_id=1, source_target_pairs={{0,1},{1,0},{2,3},{3,2},{4,5},{5,4},{6,7},{7,6},{8,9},{9,8},{10,11... | collective-permute-start | bytes 786440 | tf_op jit(solution)/shard_map/ppermute | solution.py:393
  4.1 1.2 %collective-permute-done = f32[8,16,512]{2,1,0:T(8,128)S(1)} collective-permute-done((f32[8,16,512]{2,1,0:T(8,128)S(1)}, f32[8,16,512]{2,1,0:T(8,128)S(1)}, u32[]{:S(2)}, u32[]{:S(2)}) %collective-permute-start) | collective-permute-done | bytes 262176 | tf_op jit(solution)/shard_map/ppermute | solution.py:393
  5.3 0.0 copy-start.5
  5.3 0.0 copy-start.6
  5.3 0.0 copy-start.7
  5.3 0.0 copy-start.8
  5.3 16.3 %all_to_all.10.modes_ref = f32[8,16,512]{2,1,0:T(8,128)S(1)} all-to-all(f32[8,16,512]{2,1,0:T(8,128)S(1)} %add.3), channel_id=1, replica_groups=mesh['group'=2,'gx'=8,'gy'=2] {'gx'}, dimensions={0} | all-to-all | bytes 524288 | tf_op jit(solution)/shard_map/all_to_all | solution.py:395
  21.6 0.0 copy-done.2
  21.6 0.0 copy-done.5
  21.6 0.0 copy-done.6
  21.7 0.0 copy-done.7
  21.7 0.0 copy-start.1
  21.7 0.0 copy-start.3
  21.7 1.5 %mix.1 = (f32[1,64,1024]{2,1,0:T(8,128)}, f32[8,16,512]{2,1,0:T(8,128)S(1)}) custom-call(f32[8,16,512]{2,1,0:T(8,128)S(1)} %all_to_all.10.modes_ref, bf16[1,64,64,128]{3,2,1,0:T(8,128)(2,1)S(1)} %copy-done.2, bf16[128,128]{1,0:T(8,128)(2,1)S(1)} %copy-done.8, bf16[128,128]{1,0:T(8,128)(2,1)S(1)} %copy-done.7, bf16[128,128]{1,0:T(8,128)(2,1)S(1)} %copy-done.6, ...), custom_call_target="tpu_custom_call" | custom-call | tf_op jit(solution)/shard_map/mix/pallas_call | solution.py:300
  23.2 12.1 %all_to_all.11.own_ref = f32[8,16,512]{2,1,0:T(8,128)S(1)} all-to-all(f32[8,16,512]{2,1,0:T(8,128)S(1)} %get-tuple-element.8), channel_id=1, replica_groups=mesh['group'=2,'gx'=8,'gy'=2] {'gx'}, dimensions={0} | all-to-all | bytes 524288 | tf_op jit(solution)/shard_map/all_to_all | solution.py:400
  35.3 0.0 collective-permute-start.1
  35.3 1.5 %collective-permute-done.1.other_ref = f32[8,16,512]{2,1,0:T(8,128)S(1)} collective-permute-done((f32[8,16,512]{2,1,0:T(8,128)S(1)}, f32[8,16,512]{2,1,0:T(8,128)S(1)}, u32[]{:S(2)}, u32[]{:S(2)}) %collective-permute-start.1) | collective-permute-done | bytes 262176 | tf_op jit(solution)/shard_map/ppermute | solution.py:401
  36.8 0.0 copy-done.3
  36.8 0.6 %copy-done.10 = f32[64]{0:T(128)S(1)} copy-done((f32[64]{0:T(128)S(1)}, f32[64]{0:T(128)}, u32[]{:S(2)}) %copy-start.10) | copy-done | bytes 280
  37.5 2.8 %make_output.1 = bf16[4,256,512]{2,1,0:T(8,128)(2,1)} custom-call(s32[1]{0:T(128)} %bitcast.place_ref, bf16[4,256,512]{2,1,0:T(8,128)(2,1)S(1)} %copy-done.1, bf16[2,2,256,384]{3,2,1,0:T(8,128)(2,1)S(1)} %copy-done.3, bf16[64,64]{1,0:T(8,128)(2,1)S(1)} %copy-done.9, f32[1,64]{1,0:T(1,128)S(1)} %bitcast.2, f32[8,16,512]{2,1,0:T(8,128)S(1)} %all_to_all.11.own_ref, ...), custom_call_target="tpu_custom_call" | custom-call | tf_op jit(solution)/shard_map/make_output/pallas_call | solution.py:355
  (8 shorter events, 0.0 us)
Async XLA Ops:
  0.6 1.2 %copy-start = (bf16[4,256,512]{2,1,0:T(8,128)(2,1)S(1)}, bf16[4,256,512]{2,1,0:T(8,128)(2,1)}, u32[]{:S(2)}) copy-start(bf16[4,256,512]{2,1,0:T(8,128)(2,1)} %flow_ref.1) | copy-start | bytes 3145732
  1.9 0.9 %copy-start.4 = (bf16[2,128,512]{2,1,0:T(8,128)(2,1)S(1)}, bf16[2,128,512]{2,1,0:T(8,128)(2,1)}, u32[]{:S(2)}) copy-start(bf16[2,128,512]{2,1,0:T(8,128)(2,1)} %constant.16.clone.table_hbm) | copy-start | bytes 786436
  2.8 18.8 %copy-start.2 = (bf16[1,64,64,128]{3,2,1,0:T(8,128)(2,1)S(1)}, bf16[1,64,64,128]{3,2,1,0:T(8,128)(2,1)}, u32[]{:S(2)}) copy-start(bf16[1,64,64,128]{3,2,1,0:T(8,128)(2,1)} %weight_ref.1) | copy-start | bytes 3145732
  3.6 1.7 %collective-permute-start = (f32[8,16,512]{2,1,0:T(8,128)S(1)}, f32[8,16,512]{2,1,0:T(8,128)S(1)}, u32[]{:S(2)}, u32[]{:S(2)}) collective-permute-start(f32[8,16,512]{2,1,0:T(8,128)S(1)} %get-tuple-element.7), channel_id=1, source_target_pairs={{0,1},{1,0},{2,3},{3,2},{4,5},{5,4},{6,7},{7,6},{8,9},{9,8},{10,11... | collective-permute-start | bytes 786440 | tf_op jit(solution)/shard_map/ppermute | solution.py:393
  5.3 16.4 %copy-start.5 = (bf16[128,128]{1,0:T(8,128)(2,1)S(1)}, bf16[128,128]{1,0:T(8,128)(2,1)}, u32[]{:S(2)}) copy-start(bf16[128,128]{1,0:T(8,128)(2,1)} %constant.20.clone.inverse_low) | copy-start | bytes 98308
  5.3 16.4 %copy-start.6 = (bf16[128,128]{1,0:T(8,128)(2,1)S(1)}, bf16[128,128]{1,0:T(8,128)(2,1)}, u32[]{:S(2)}) copy-start(bf16[128,128]{1,0:T(8,128)(2,1)} %constant.19.clone.inverse_high) | copy-start | bytes 98308
  5.3 16.4 %copy-start.7 = (bf16[128,128]{1,0:T(8,128)(2,1)S(1)}, bf16[128,128]{1,0:T(8,128)(2,1)}, u32[]{:S(2)}) copy-start(bf16[128,128]{1,0:T(8,128)(2,1)} %constant.18.clone.forward_low) | copy-start | bytes 98308
  5.3 16.4 %copy-start.8 = (bf16[128,128]{1,0:T(8,128)(2,1)S(1)}, bf16[128,128]{1,0:T(8,128)(2,1)}, u32[]{:S(2)}) copy-start(bf16[128,128]{1,0:T(8,128)(2,1)} %constant.17.clone.forward_high) | copy-start | bytes 98308
  21.7 15.2 %copy-start.1 = (bf16[4,256,512]{2,1,0:T(8,128)(2,1)S(1)}, bf16[4,256,512]{2,1,0:T(8,128)(2,1)}, u32[]{:S(2)}) copy-start(bf16[4,256,512]{2,1,0:T(8,128)(2,1)} %flow_ref.1) | copy-start | bytes 3145732
  21.7 15.1 %copy-start.3 = (bf16[2,2,256,384]{3,2,1,0:T(8,128)(2,1)S(1)}, bf16[2,2,256,384]{3,2,1,0:T(8,128)(2,1)}, u32[]{:S(2)}) copy-start(bf16[2,2,256,384]{3,2,1,0:T(8,128)(2,1)} %constant.21.clone.table_ref) | copy-start | bytes 2359300
  23.2 13.6 %copy-start.9 = (bf16[64,64]{1,0:T(8,128)(2,1)S(1)}, bf16[64,64]{1,0:T(8,128)(2,1)}, u32[]{:S(2)}) copy-start(bf16[64,64]{1,0:T(8,128)(2,1)} %local_ref.1) | copy-start | bytes 24580
  35.3 1.5 %collective-permute-start.1 = (f32[8,16,512]{2,1,0:T(8,128)S(1)}, f32[8,16,512]{2,1,0:T(8,128)S(1)}, u32[]{:S(2)}, u32[]{:S(2)}) collective-permute-start(f32[8,16,512]{2,1,0:T(8,128)S(1)} %all_to_all.11.own_ref), channel_id=1, source_target_pairs={{0,1},{1,0},{2,3},{3,2},{4,5},{5,4},{6,7},{7,6},{8,9},{9,8},{10,11... | collective-permute-start | bytes 786440 | tf_op jit(solution)/shard_map/ppermute | solution.py:401
  36.8 0.7 %copy-start.10 = (f32[64]{0:T(128)S(1)}, f32[64]{0:T(128)}, u32[]{:S(2)}) copy-start(f32[64]{0:T(128)} %param.13) | copy-start | bytes 772

commit v4 on v3

--- a/solution.py
+++ b/solution.py
@@ -1,3 +1,4 @@
+import functools
 import math
 
 import jax
@@ -126,6 +127,8 @@
 
 
 SMALL = pltpu.CompilerParams(vmem_limit_bytes=20 * 1024 * 1024)
+LARGE = pltpu.CompilerParams(vmem_limit_bytes=211 * 256 * 1024)
+WIDTH = 256
 
 
 def angles(count, places, extent):
@@ -204,8 +207,12 @@
     return jnp.dot(left, right, preferred_element_type=jnp.float32)
 
 
-def forward_y_kernel(flow_hbm, table_hbm, send_ref, keep_ref, flow_ref, table_ref, arrivals):
+def forward_y_kernel(
+    flow_hbm, table_hbm, local_hbm, bias_hbm, send_ref, keep_ref, wide_ref, level_ref,
+    flow_ref, table_ref, local_ref, bias_ref, arrivals,
+):
     cells_x, cells_y, feat_count = flow_ref.shape
+    channels = local_ref.shape[0]
     rows = table_ref.shape[0] // 2 // send_ref.shape[0]
     table_copy = pltpu.make_async_copy(
         table_hbm.at[lax.axis_index("gy")], table_ref, arrivals.at[cells_x]
@@ -215,6 +222,10 @@
     for x in range(cells_x):
         copies.append(pltpu.make_async_copy(flow_hbm.at[x], flow_ref.at[x], arrivals.at[x]))
         copies[x].start()
+    local_copy = pltpu.make_async_copy(local_hbm, local_ref, arrivals.at[cells_x + 1])
+    local_copy.start()
+    bias_copy = pltpu.make_async_copy(bias_hbm, bias_ref, arrivals.at[cells_x + 2])
+    bias_copy.start()
     table_copy.wait()
     for pair in range(cells_x // 2):
         copies[2 * pair].wait()
@@ -223,38 +234,102 @@
         result = dot(table_ref[...], flow).reshape(2, send_ref.shape[0], rows, feat_count)
         send_ref[:, pair * rows : (pair + 1) * rows, :] = result[0]
         keep_ref[:, pair * rows : (pair + 1) * rows, :] = result[1]
-
-
-def forward_y(flow_field, table, peers, rows_ky):
+    local_copy.wait()
+    bias_copy.wait()
+    wide_ref[...] = jnp.zeros_like(wide_ref)
+    for start in range(0, wide_ref.shape[0], channels):
+        span = slice(start, start + channels)
+        wide_ref[span, span] = local_ref[...]
+        level_ref[:, span] = bias_ref[...]
+
+
+def forward_y(flow_field, table, local, bias, peers, rows_ky):
     cells_x, cells_y, feat_count = flow_field.shape
     shape = jax.ShapeDtypeStruct((peers, cells_x * 2 * rows_ky, feat_count), jnp.float32)
     spec = pl.BlockSpec(memory_space=pltpu.VMEM)
     source = pl.BlockSpec(memory_space=pltpu.HBM)
     return pl.pallas_call(
         forward_y_kernel,
-        in_specs=[source, source],
-        out_specs=[spec, spec],
-        out_shape=[shape, shape],
+        in_specs=[source] * 4,
+        out_specs=[spec] * 4,
+        out_shape=[
+            shape,
+            shape,
+            jax.ShapeDtypeStruct((WIDTH, WIDTH), local.dtype),
+            jax.ShapeDtypeStruct((1, WIDTH), bias.dtype),
+        ],
         scratch_shapes=[
             pltpu.VMEM(flow_field.shape, flow_field.dtype),
             pltpu.VMEM(table.shape[1:], table.dtype),
-            pltpu.SemaphoreType.DMA((cells_x + 1,)),
+            pltpu.VMEM(local.shape, local.dtype),
+            pltpu.VMEM(bias.shape, bias.dtype),
+            pltpu.SemaphoreType.DMA((cells_x + 3,)),
         ],
+        compiler_params=LARGE,
+        name="forward_y",
+    )(flow_field, table, local, bias)
+
+
+def turns(peers):
+    return sorted(range(1, peers), key=lambda turn: (-(turn // 2), turn)) + [0]
+
+
+def combine_kernel(keep_ref, arrived_ref, *out_refs):
+    me = lax.axis_index("gx")
+    for turn, out_ref in zip(turns(len(out_refs)), out_refs):
+        out_ref[...] = keep_ref[me ^ turn] + arrived_ref[me ^ turn]
+
+
+def combine(keep, arrived):
+    peers = keep.shape[0]
+    return pl.pallas_call(
+        combine_kernel,
+        out_shape=[jax.ShapeDtypeStruct(keep.shape[1:], keep.dtype)] * peers,
         compiler_params=SMALL,
-        name="forward_y",
-    )(flow_field, table)
-
-
-def mix_kernel(
-    modes_ref, weight_ref, forward_high, forward_low, inverse_high, inverse_low,
-    mixed_ref, back_ref, spread_ref, result_ref,
-):
-    feat_count = modes_ref.shape[-1]
+        name="combine",
+    )(keep, arrived)
+
+
+def exchange(blocks):
+    peers = len(blocks)
+    arrived = []
+    for turn, block in zip(turns(peers), blocks):
+        pairs = [(place, place ^ turn) for place in range(peers)]
+        arrived.append(lax.ppermute(block, "gx", pairs) if turn else block)
+    return arrived
+
+
+def gather_kernel(*refs):
+    me = lax.axis_index("gx")
+    for turn, block_ref in zip(turns(len(refs) - 1), refs):
+        refs[-1][me ^ turn] = block_ref[...]
+
+
+def gather(blocks):
+    return pl.pallas_call(
+        gather_kernel,
+        out_shape=jax.ShapeDtypeStruct((len(blocks),) + blocks[0].shape, blocks[0].dtype),
+        compiler_params=SMALL,
+        name="gather",
+    )(*blocks)
+
+
+def mix_kernel(peers, *refs):
+    block_refs = refs[:peers]
+    weight_ref, forward_high, forward_low, inverse_high, inverse_low, mixed_ref = refs[
+        peers : peers + 6
+    ]
+    back_refs = refs[peers + 6 : 2 * peers + 6]
+    order_ref, spread_ref, result_ref = refs[2 * peers + 6 :]
+    me = lax.axis_index("gx")
+    feat_count = order_ref.shape[-1]
     count = weight_ref.shape[1]
     channels = weight_ref.shape[2]
     tiles = feat_count // 128
     group = 2 * tiles
-    high, low = split_terms(modes_ref[...].reshape(-1, feat_count))
+    for turn, block_ref in zip(turns(peers), block_refs):
+        order_ref[me ^ turn] = block_ref[...]
+    high, low = split_terms(order_ref[...].reshape(-1, feat_count))
     spectrum = (
         dot(forward_high[...], high) + dot(forward_high[...], low) + dot(forward_low[...], high)
     )
@@ -290,32 +365,32 @@
         mixed_ref[0, :, part * feat_count : (part + 1) * feat_count] = parts[part]
     high, low = split_terms(jnp.concatenate(parts, axis=0))
     back = dot(inverse_high[...], high) + dot(inverse_high[...], low) + dot(inverse_low[...], high)
-    back_ref[...] = back.reshape(back_ref.shape)
-
-
-def mix(modes, weights, forward_table, inverse_table):
-    feat_count = modes.shape[-1]
+    order_ref[...] = back.reshape(order_ref.shape)
+    for turn, back_ref in zip(turns(peers), back_refs):
+        back_ref[...] = order_ref[me ^ turn]
+
+
+def mix(blocks, weights, forward_table, inverse_table):
+    rows, feat_count = blocks[0].shape
+    peers = len(blocks)
     count = weights.shape[1]
     scratch = pltpu.VMEM((count * feat_count // 64, 128), jnp.float32)
-    return pl.pallas_call(
-        mix_kernel,
-        out_shape=[
-            jax.ShapeDtypeStruct((1, count, 2 * feat_count), jnp.float32),
-            jax.ShapeDtypeStruct(modes.shape, jnp.float32),
-        ],
-        scratch_shapes=[scratch, scratch],
+    mixed, *back = pl.pallas_call(
+        functools.partial(mix_kernel, peers),
+        out_shape=[jax.ShapeDtypeStruct((1, count, 2 * feat_count), jnp.float32)]
+        + [jax.ShapeDtypeStruct(blocks[0].shape, jnp.float32)] * peers,
+        scratch_shapes=[pltpu.VMEM((peers, rows, feat_count), jnp.float32), scratch, scratch],
         compiler_params=SMALL,
         name="mix",
-    )(modes, weights, *split_table(forward_table), *split_table(inverse_table))
+    )(*blocks, weights, *split_table(forward_table), *split_table(inverse_table))
+    return mixed, back
 
 
 def output_kernel(
-    place_ref, flow_ref, table_ref, local_ref, bias_ref, own_ref, other_ref,
-    out_ref, stack_ref, wide_ref, level_ref,
+    place_ref, flow_ref, table_ref, wide_ref, level_ref, own_ref, other_ref, out_ref, stack_ref
 ):
     step = pl.program_id(0)
     feat_count = flow_ref.shape[-1]
-    channels = local_ref.shape[0]
     width = wide_ref.shape[0]
     pairs = stack_ref.shape[0]
     rows = own_ref.shape[1] // pairs
@@ -327,11 +402,6 @@
             both = jnp.concatenate([own_ref[:, span, :], other_ref[:, span, :]], axis=0)
             high, low = split_terms(both.reshape(-1, feat_count))
             stack_ref[pair] = jnp.concatenate([high, low, high], axis=0)
-        wide_ref[...] = jnp.zeros_like(wide_ref)
-        for start in range(0, width, channels):
-            span = slice(start, start + channels)
-            wide_ref[span, span] = local_ref[...]
-            level_ref[:, span] = bias_ref[...]
 
     table = table_ref[0, step % 2]
     for start in range(0, feat_count, width):
@@ -346,9 +416,8 @@
         ).astype(out_ref.dtype)
 
 
-def make_output(flow_field, own, other, table, local, bias):
+def make_output(flow_field, own, other, table, wide, level):
     cells_x, cells_y, feat_count = flow_field.shape
-    width = 256
     place = jnp.reshape(lax.axis_index("gy"), (1,))
     whole = lambda array: pl.BlockSpec(array.shape, lambda i, p: (0,) * array.ndim)
     block = pl.BlockSpec((1, cells_y, feat_count), lambda i, p: (i, 0, 0))
@@ -360,22 +429,20 @@
             in_specs=[
                 block,
                 pl.BlockSpec((1,) + table.shape[1:], lambda i, p: (p[0], 0, 0, 0)),
-                whole(local),
-                whole(bias),
+                whole(wide),
+                whole(level),
                 whole(own),
                 whole(other),
             ],
             out_specs=block,
             scratch_shapes=[
                 pltpu.VMEM((cells_x // 2, table.shape[-1], feat_count), jnp.bfloat16),
-                pltpu.VMEM((width, width), jnp.bfloat16),
-                pltpu.VMEM((1, width), jnp.float32),
             ],
         ),
         out_shape=jax.ShapeDtypeStruct(flow_field.shape, jnp.bfloat16),
         compiler_params=SMALL,
         name="make_output",
-    )(place, flow_field, table, local, bias, own, other)
+    )(place, flow_field, table, wide, level, own, other)
 
 
 def row_body(flow_field, spectral_weight, local_weight, bias_terms):
@@ -387,17 +454,22 @@
     inverse_scale = 1.0 / math.sqrt(MX * MY)
     swap = [(0, 1), (1, 0)]
 
-    send, keep = forward_y(
-        flow_field, forward_y_table(cells_y, groups_y, peers, rows_ky), peers, rows_ky
-    )
-    modes = keep + lax.ppermute(send, "gy", swap)
+    send, keep, wide, level = forward_y(
+        flow_field,
+        forward_y_table(cells_y, groups_y, peers, rows_ky),
+        local_weight,
+        bias_terms[None, :],
+        peers,
+        rows_ky,
+    )
+    blocks = exchange(combine(keep, lax.ppermute(send, "gy", swap)))
     mixed, back = mix(
-        lax.all_to_all(modes, "gx", 0, 0, tiled=True),
+        blocks,
         spectral_weight,
         forward_x_table(cells_x, peers, rows_ky) * forward_scale,
         inverse_x_table(cells_x, peers, rows_ky),
     )
-    own = lax.all_to_all(back, "gx", 0, 0, tiled=True)
+    own = gather(exchange(back))
     other = lax.ppermute(own, "gy", swap)
     high, low = split_table(inverse_y_table(cells_y, groups_y, peers, rows_ky) * inverse_scale)
     output = make_output(
@@ -405,15 +477,16 @@
         own,
         other,
         np.concatenate([high, high, low], axis=-1),
-        local_weight,
-        bias_terms[None, :],
+        wide,
+        level,
     )
     return output, mixed
 
 
 def body(flow_field, spectral_weight, local_weight, bias_terms):
-    whole_rows = spectral_weight.shape[1] % MX == 0
-    if whole_rows and lax.axis_size("gy") == 2 and spectral_weight.shape[1] == 2 * MX:
+    peers = lax.axis_size("gx")
+    paired = lax.axis_size("gy") == 2 and peers & (peers - 1) == 0
+    if paired and spectral_weight.shape[1] == 2 * MX and WIDTH % local_weight.shape[0] == 0:
         return row_body(flow_field, spectral_weight, local_weight, bias_terms)
     return general_body(flow_field, spectral_weight, local_weight, bias_terms)
 

time: 40.7 us -> 43 us (1.057)
  blocking collectives: 28.4 us -> 0 us
  starting transfers between devices: 0.52 us -> 24.9 us
  waiting for transfers between devices: 2.69 us -> 8.49 us
  Pallas kernels: 5.09 us -> 6.19 us
    all_to_all x2 -> x0, blocking collectives: 28.4 us -> none  [the longest x1 16.3 us: row_body(): lax.all_to_all(modes, 'gx', 0, 0, tiled=True)]
    ppermute x1 -> x15, starting transfers between devices: 0.52 us -> 24.8 us  [the longest x14 24.3 us: exchange(): arrived.append(lax.ppermute(block, 'gx', pairs) if turn else block)]
    ppermute x1 -> x15, waiting for transfers between devices: 1.16 us -> 6.97 us  [the longest x14 5.8 us: exchange(): arrived.append(lax.ppermute(block, 'gx', pairs) if turn else block)]
    pallas_call x2 -> x4, Pallas kernels: 2.25 us -> 3.42 us  [the longest x1 1.78 us: forward_y(): pl.pallas_call(forward_y_kernel, in_specs=[source] * 4, out_specs=[spec]...]
    unnamed x22 -> x20, local copies, waits for them, and re-layouts: 2.86 us -> 2.44 us
  transfers between devices with their start and end apart: 2 -> 16, of which waited for: 2 -> 7; matrix products, arithmetic and copies ran while one was open for 0% -> 0% of each run, Pallas kernels for 0% -> 0%
where the time goes in v4:
time: 43 us; the launch traced here: 42.8 us
  starting transfers between devices  24.9 us (58%)
  waiting for transfers between devices  8.49 us (20%)
  Pallas kernels  6.19 us (14%)
  local copies, waits for them, and re-layouts  2.44 us (6%)
  between operations  0.74 us (2%)
    ppermute x14, starting transfers between devices, exchange(): arrived.append(lax.ppermute(block, 'gx', pairs) if turn else block)  24.3 us
    ppermute x14, waiting for transfers between devices, exchange(): arrived.append(lax.ppermute(block, 'gx', pairs) if turn else block)  5.8 us
    pallas_call x1, Pallas kernels, make_output(): pl.pallas_call(output_kernel, grid_spec=pltpu.PrefetchScalarGridSpec(num_...  2.77 us
    unnamed x20, local copies, waits for them, and re-layouts  2.44 us
    pallas_call x1, Pallas kernels, forward_y(): pl.pallas_call(forward_y_kernel, in_specs=[source] * 4, out_specs=[spec]...  1.78 us
    pallas_call x1, Pallas kernels, mix(): pl.pallas_call(functools.partial(mix_kernel, peers), out_shape=[jax.Shape...  1.58 us
    ppermute x1, waiting for transfers between devices, row_body(): other = lax.ppermute(own, 'gy', swap)  1.52 us
    ppermute x1, waiting for transfers between devices, row_body(): blocks = exchange(combine(keep, lax.ppermute(send, 'gy', swap)))  1.16 us
  transfers between devices with their start and end apart: 16, of which 7 were waited for; matrix products, arithmetic and copies ran while one was open for 0% of the time, Pallas kernels for 0%

profile of v4, /device:TPU:0, one launch (start us, length us, event | category | flops | bytes accessed | tf_op | source)
XLA Modules:
  0.0 42.8 jit_solution(16538967758326096735)
XLA Ops:
  0.7 1.0 %copy-done.3 = bf16[2,128,512]{2,1,0:T(8,128)(2,1)S(1)} copy-done((bf16[2,128,512]{2,1,0:T(8,128)(2,1)S(1)}, bf16[2,128,512]{2,1,0:T(8,128)(2,1)}, u32[]{:S(2)}) %copy-start.3) | copy-done | bytes 262168
  1.7 0.7 %copy-done.8 = bf16[64,64]{1,0:T(8,128)(2,1)S(1)} copy-done((bf16[64,64]{1,0:T(8,128)(2,1)S(1)}, bf16[64,64]{1,0:T(8,128)(2,1)}, u32[]{:S(2)}) %copy-start.8) | copy-done | bytes 8216
  2.4 0.7 %copy-done.9 = f32[64]{0:T(128)S(1)} copy-done((f32[64]{0:T(128)S(1)}, f32[64]{0:T(128)}, u32[]{:S(2)}) %copy-start.9) | copy-done | bytes 280
  3.1 1.8 %forward_y.1 = (f32[8,16,512]{2,1,0:T(8,128)S(1)}, f32[8,16,512]{2,1,0:T(8,128)S(1)}, bf16[256,256]{1,0:T(8,128)(2,1)S(1)}, f32[1,256]{1,0:T(1,128)S(1)}) custom-call(bf16[4,256,512]{2,1,0:T(8,128)(2,1)} %flow_ref.1, bf16[2,128,512]{2,1,0:T(8,128)(2,1)S(1)} %copy-done.3, bf16[64,64]{1,0:T(8,128)(2,1)S(1)} %copy-done.8, f32[1,64]{1,0:T(1,128)S(1)} %bitcast.2), custom_call_target="tpu_custom_call" | custom-call | tf_op jit(solution)/shard_map/forward_y/pallas_call | solution.py:251
  5.4 1.2 %collective-permute-done.arrived_ref = f32[8,16,512]{2,1,0:T(8,128)S(1)} collective-permute-done((f32[8,16,512]{2,1,0:T(8,128)S(1)}, f32[8,16,512]{2,1,0:T(8,128)S(1)}, u32[]{:S(2)}, u32[]{:S(2)}) %collective-permute-start) | collective-permute-done | bytes 262176 | tf_op jit(solution)/shard_map/ppermute | solution.py:465
  6.6 5.0 %collective-permute-start.1 = (f32[16,512]{1,0:T(8,128)S(1)}, f32[16,512]{1,0:T(8,128)S(1)}, u32[]{:S(2)}, u32[]{:S(2)}) collective-permute-start(f32[16,512]{1,0:T(8,128)S(1)} %get-tuple-element.27), channel_id=1, source_target_pairs={{0,12},{2,14},{4,8},{6,10},{8,4},{10,6},{12,0},{14,2},{1,13},{3,15... | collective-permute-start | bytes 98312 | tf_op jit(solution)/shard_map/ppermute | solution.py:298
  11.6 1.1 %collective-permute-start.2 = (f32[16,512]{1,0:T(8,128)S(1)}, f32[16,512]{1,0:T(8,128)S(1)}, u32[]{:S(2)}, u32[]{:S(2)}) collective-permute-start(f32[16,512]{1,0:T(8,128)S(1)} %get-tuple-element.28), channel_id=1, source_target_pairs={{0,14},{2,12},{4,10},{6,8},{8,6},{10,4},{12,2},{14,0},{1,15},{3,13... | collective-permute-start | bytes 98312 | tf_op jit(solution)/shard_map/ppermute | solution.py:298
  12.8 0.8 %collective-permute-start.3 = (f32[16,512]{1,0:T(8,128)S(1)}, f32[16,512]{1,0:T(8,128)S(1)}, u32[]{:S(2)}, u32[]{:S(2)}) collective-permute-start(f32[16,512]{1,0:T(8,128)S(1)} %get-tuple-element.29), channel_id=1, source_target_pairs={{0,8},{2,10},{4,12},{6,14},{8,0},{10,2},{12,4},{14,6},{1,9},{3,11}... | collective-permute-start | bytes 98312 | tf_op jit(solution)/shard_map/ppermute | solution.py:298
  13.6 2.0 %collective-permute-start.4 = (f32[16,512]{1,0:T(8,128)S(1)}, f32[16,512]{1,0:T(8,128)S(1)}, u32[]{:S(2)}, u32[]{:S(2)}) collective-permute-start(f32[16,512]{1,0:T(8,128)S(1)} %get-tuple-element.30), channel_id=1, source_target_pairs={{0,10},{2,8},{4,14},{6,12},{8,2},{10,0},{12,6},{14,4},{1,11},{3,9}... | collective-permute-start | bytes 98312 | tf_op jit(solution)/shard_map/ppermute | solution.py:298
  15.5 1.4 %collective-permute-start.5 = (f32[16,512]{1,0:T(8,128)S(1)}, f32[16,512]{1,0:T(8,128)S(1)}, u32[]{:S(2)}, u32[]{:S(2)}) collective-permute-start(f32[16,512]{1,0:T(8,128)S(1)} %get-tuple-element.31), channel_id=1, source_target_pairs={{0,4},{2,6},{4,0},{6,2},{8,12},{10,14},{12,8},{14,10},{1,5},{3,7},... | collective-permute-start | bytes 98312 | tf_op jit(solution)/shard_map/ppermute | solution.py:298
  17.0 1.7 %collective-permute-start.6 = (f32[16,512]{1,0:T(8,128)S(1)}, f32[16,512]{1,0:T(8,128)S(1)}, u32[]{:S(2)}, u32[]{:S(2)}) collective-permute-start(f32[16,512]{1,0:T(8,128)S(1)} %get-tuple-element.32), channel_id=1, source_target_pairs={{0,6},{2,4},{4,2},{6,0},{8,14},{10,12},{12,10},{14,8},{1,7},{3,5},... | collective-permute-start | bytes 98312 | tf_op jit(solution)/shard_map/ppermute | solution.py:298
  18.6 1.2 %collective-permute-start.7 = (f32[16,512]{1,0:T(8,128)S(1)}, f32[16,512]{1,0:T(8,128)S(1)}, u32[]{:S(2)}, u32[]{:S(2)}) collective-permute-start(f32[16,512]{1,0:T(8,128)S(1)} %get-tuple-element.33), channel_id=1, source_target_pairs={{0,2},{2,0},{4,6},{6,4},{8,10},{10,8},{12,14},{14,12},{1,3},{3,1},... | collective-permute-start | bytes 98312 | tf_op jit(solution)/shard_map/ppermute | solution.py:298
  19.8 2.0 %collective-permute-done.6.refs_5_ = f32[16,512]{1,0:T(8,128)S(1)} collective-permute-done((f32[16,512]{1,0:T(8,128)S(1)}, f32[16,512]{1,0:T(8,128)S(1)}, u32[]{:S(2)}, u32[]{:S(2)}) %collective-permute-start.6) | collective-permute-done | bytes 32800 | tf_op jit(solution)/shard_map/ppermute | solution.py:298
  21.8 0.8 %collective-permute-done.7.refs_6_ = f32[16,512]{1,0:T(8,128)S(1)} collective-permute-done((f32[16,512]{1,0:T(8,128)S(1)}, f32[16,512]{1,0:T(8,128)S(1)}, u32[]{:S(2)}, u32[]{:S(2)}) %collective-permute-start.7) | collective-permute-done | bytes 32800 | tf_op jit(solution)/shard_map/ppermute | solution.py:298
  22.6 1.6 %mix.1 = (f32[1,64,1024]{2,1,0:T(8,128)}, f32[16,512]{1,0:T(8,128)S(1)}, f32[16,512]{1,0:T(8,128)S(1)}, f32[16,512]{1,0:T(8,128)S(1)}, f32[16,512]{1,0:T(8,128)S...) custom-call(f32[16,512]{1,0:T(8,128)S(1)} %collective-permute-done.1.refs_0_, ...), custom_call_target="tpu_custom_call" | custom-call | tf_op jit(solution)/shard_map/mix/pallas_call | solution.py:378
  24.2 3.6 %collective-permute-start.8 = (f32[16,512]{1,0:T(8,128)S(1)}, f32[16,512]{1,0:T(8,128)S(1)}, u32[]{:S(2)}, u32[]{:S(2)}) collective-permute-start(f32[16,512]{1,0:T(8,128)S(1)} %get-tuple-element.35), channel_id=1, source_target_pairs={{0,12},{2,14},{4,8},{6,10},{8,4},{10,6},{12,0},{14,2},{1,13},{3,15... | collective-permute-start | bytes 98312 | tf_op jit(solution)/shard_map/ppermute | solution.py:298
  27.8 0.8 %collective-permute-start.9 = (f32[16,512]{1,0:T(8,128)S(1)}, f32[16,512]{1,0:T(8,128)S(1)}, u32[]{:S(2)}, u32[]{:S(2)}) collective-permute-start(f32[16,512]{1,0:T(8,128)S(1)} %get-tuple-element.36), channel_id=1, source_target_pairs={{0,14},{2,12},{4,10},{6,8},{8,6},{10,4},{12,2},{14,0},{1,15},{3,13... | collective-permute-start | bytes 98312 | tf_op jit(solution)/shard_map/ppermute | solution.py:298
  29.2 2.6 %collective-permute-start.11 = (f32[16,512]{1,0:T(8,128)S(1)}, f32[16,512]{1,0:T(8,128)S(1)}, u32[]{:S(2)}, u32[]{:S(2)}) collective-permute-start(f32[16,512]{1,0:T(8,128)S(1)} %get-tuple-element.38), channel_id=1, source_target_pairs={{0,10},{2,8},{4,14},{6,12},{8,2},{10,0},{12,6},{14,4},{1,11},{3,9}... | collective-permute-start | bytes 98312 | tf_op jit(solution)/shard_map/ppermute | solution.py:298
  31.8 1.2 %collective-permute-start.12 = (f32[16,512]{1,0:T(8,128)S(1)}, f32[16,512]{1,0:T(8,128)S(1)}, u32[]{:S(2)}, u32[]{:S(2)}) collective-permute-start(f32[16,512]{1,0:T(8,128)S(1)} %get-tuple-element.39), channel_id=1, source_target_pairs={{0,4},{2,6},{4,0},{6,2},{8,12},{10,14},{12,8},{14,10},{1,5},{3,7},... | collective-permute-start | bytes 98312 | tf_op jit(solution)/shard_map/ppermute | solution.py:298
  33.1 1.4 %collective-permute-start.13 = (f32[16,512]{1,0:T(8,128)S(1)}, f32[16,512]{1,0:T(8,128)S(1)}, u32[]{:S(2)}, u32[]{:S(2)}) collective-permute-start(f32[16,512]{1,0:T(8,128)S(1)} %get-tuple-element.40), channel_id=1, source_target_pairs={{0,6},{2,4},{4,2},{6,0},{8,14},{10,12},{12,10},{14,8},{1,7},{3,5},... | collective-permute-start | bytes 98312 | tf_op jit(solution)/shard_map/ppermute | solution.py:298
  34.4 0.9 %collective-permute-start.14 = (f32[16,512]{1,0:T(8,128)S(1)}, f32[16,512]{1,0:T(8,128)S(1)}, u32[]{:S(2)}, u32[]{:S(2)}) collective-permute-start(f32[16,512]{1,0:T(8,128)S(1)} %get-tuple-element.41), channel_id=1, source_target_pairs={{0,2},{2,0},{4,6},{6,4},{8,10},{10,8},{12,14},{14,12},{1,3},{3,1},... | collective-permute-start | bytes 98312 | tf_op jit(solution)/shard_map/ppermute | solution.py:298
  35.7 2.1 %collective-permute-done.13.refs_5_ = f32[16,512]{1,0:T(8,128)S(1)} collective-permute-done((f32[16,512]{1,0:T(8,128)S(1)}, f32[16,512]{1,0:T(8,128)S(1)}, u32[]{:S(2)}, u32[]{:S(2)}) %collective-permute-start.13) | collective-permute-done | bytes 32800 | tf_op jit(solution)/shard_map/ppermute | solution.py:298
  38.5 1.5 %collective-permute-done.15.other_ref = f32[8,16,512]{2,1,0:T(8,128)S(1)} collective-permute-done((f32[8,16,512]{2,1,0:T(8,128)S(1)}, f32[8,16,512]{2,1,0:T(8,128)S(1)}, u32[]{:S(2)}, u32[]{:S(2)}) %collective-permute-start.15) | collective-permute-done | bytes 262176 | tf_op jit(solution)/shard_map/ppermute | solution.py:473
  40.0 2.8 %make_output.1 = bf16[4,256,512]{2,1,0:T(8,128)(2,1)} custom-call(s32[1]{0:T(128)} %bitcast.place_ref, bf16[4,256,512]{2,1,0:T(8,128)(2,1)S(1)} %copy-done, bf16[2,2,256,384]{3,2,1,0:T(8,128)(2,1)S(1)} %copy-done.2, bf16[256,256]{1,0:T(8,128)(2,1)S(1)} %get-tuple-element.23.wide_ref, f32[1,256]{1,0:T(1,128)S(1)} %get-tuple-element.24.level_ref, ...), custom_call_target="tpu_custom_call" | custom-call | tf_op jit(solution)/shard_map/make_output/pallas_call | solution.py:424
  (33 shorter events, 2.3 us)
Async XLA Ops:
  0.6 21.9 %copy-start.1 = (bf16[1,64,64,128]{3,2,1,0:T(8,128)(2,1)S(1)}, bf16[1,64,64,128]{3,2,1,0:T(8,128)(2,1)}, u32[]{:S(2)}) copy-start(bf16[1,64,64,128]{3,2,1,0:T(8,128)(2,1)} %refs_8_.1) | copy-start | bytes 3145732
  0.6 1.0 %copy-start.3 = (bf16[2,128,512]{2,1,0:T(8,128)(2,1)S(1)}, bf16[2,128,512]{2,1,0:T(8,128)(2,1)}, u32[]{:S(2)}) copy-start(bf16[2,128,512]{2,1,0:T(8,128)(2,1)} %constant.16.clone.table_hbm) | copy-start | bytes 786436
  4.8 1.7 %collective-permute-start = (f32[8,16,512]{2,1,0:T(8,128)S(1)}, f32[8,16,512]{2,1,0:T(8,128)S(1)}, u32[]{:S(2)}, u32[]{:S(2)}) collective-permute-start(f32[8,16,512]{2,1,0:T(8,128)S(1)} %get-tuple-element.26), channel_id=1, source_target_pairs={{0,1},{1,0},{2,3},{3,2},{4,5},{5,4},{6,7},{7,6},{8,9},{9,8},{10,11... | collective-permute-start | bytes 786440 | tf_op jit(solution)/shard_map/ppermute | solution.py:465
  6.5 16.0 %copy-start.4 = (bf16[128,128]{1,0:T(8,128)(2,1)S(1)}, bf16[128,128]{1,0:T(8,128)(2,1)}, u32[]{:S(2)}) copy-start(bf16[128,128]{1,0:T(8,128)(2,1)} %constant.20.clone.refs_12_) | copy-start | bytes 98308
  6.5 16.0 %copy-start.5 = (bf16[128,128]{1,0:T(8,128)(2,1)S(1)}, bf16[128,128]{1,0:T(8,128)(2,1)}, u32[]{:S(2)}) copy-start(bf16[128,128]{1,0:T(8,128)(2,1)} %constant.19.clone.refs_11_) | copy-start | bytes 98308
  6.5 16.0 %copy-start.6 = (bf16[128,128]{1,0:T(8,128)(2,1)S(1)}, bf16[128,128]{1,0:T(8,128)(2,1)}, u32[]{:S(2)}) copy-start(bf16[128,128]{1,0:T(8,128)(2,1)} %constant.18.clone.refs_10_) | copy-start | bytes 98308
  6.5 16.0 %copy-start.7 = (bf16[128,128]{1,0:T(8,128)(2,1)S(1)}, bf16[128,128]{1,0:T(8,128)(2,1)}, u32[]{:S(2)}) copy-start(bf16[128,128]{1,0:T(8,128)(2,1)} %constant.17.clone.refs_9_) | copy-start | bytes 98308
  6.6 33.4 %copy-start = (bf16[4,256,512]{2,1,0:T(8,128)(2,1)S(1)}, bf16[4,256,512]{2,1,0:T(8,128)(2,1)}, u32[]{:S(2)}) copy-start(bf16[4,256,512]{2,1,0:T(8,128)(2,1)} %flow_ref.1) | copy-start | bytes 3145732
  6.6 10.4 %collective-permute-start.1 = (f32[16,512]{1,0:T(8,128)S(1)}, f32[16,512]{1,0:T(8,128)S(1)}, u32[]{:S(2)}, u32[]{:S(2)}) collective-permute-start(f32[16,512]{1,0:T(8,128)S(1)} %get-tuple-element.27), channel_id=1, source_target_pairs={{0,12},{2,14},{4,8},{6,10},{8,4},{10,6},{12,0},{14,2},{1,13},{3,15... | collective-permute-start | bytes 98312 | tf_op jit(solution)/shard_map/ppermute | solution.py:298
  11.6 7.0 %collective-permute-start.2 = (f32[16,512]{1,0:T(8,128)S(1)}, f32[16,512]{1,0:T(8,128)S(1)}, u32[]{:S(2)}, u32[]{:S(2)}) collective-permute-start(f32[16,512]{1,0:T(8,128)S(1)} %get-tuple-element.28), channel_id=1, source_target_pairs={{0,14},{2,12},{4,10},{6,8},{8,6},{10,4},{12,2},{14,0},{1,15},{3,13... | collective-permute-start | bytes 98312 | tf_op jit(solution)/shard_map/ppermute | solution.py:298
  12.8 7.0 %collective-permute-start.3 = (f32[16,512]{1,0:T(8,128)S(1)}, f32[16,512]{1,0:T(8,128)S(1)}, u32[]{:S(2)}, u32[]{:S(2)}) collective-permute-start(f32[16,512]{1,0:T(8,128)S(1)} %get-tuple-element.29), channel_id=1, source_target_pairs={{0,8},{2,10},{4,12},{6,14},{8,0},{10,2},{12,4},{14,6},{1,9},{3,11}... | collective-permute-start | bytes 98312 | tf_op jit(solution)/shard_map/ppermute | solution.py:298
  13.6 6.2 %collective-permute-start.4 = (f32[16,512]{1,0:T(8,128)S(1)}, f32[16,512]{1,0:T(8,128)S(1)}, u32[]{:S(2)}, u32[]{:S(2)}) collective-permute-start(f32[16,512]{1,0:T(8,128)S(1)} %get-tuple-element.30), channel_id=1, source_target_pairs={{0,10},{2,8},{4,14},{6,12},{8,2},{10,0},{12,6},{14,4},{1,11},{3,9}... | collective-permute-start | bytes 98312 | tf_op jit(solution)/shard_map/ppermute | solution.py:298
  15.5 4.3 %collective-permute-start.5 = (f32[16,512]{1,0:T(8,128)S(1)}, f32[16,512]{1,0:T(8,128)S(1)}, u32[]{:S(2)}, u32[]{:S(2)}) collective-permute-start(f32[16,512]{1,0:T(8,128)S(1)} %get-tuple-element.31), channel_id=1, source_target_pairs={{0,4},{2,6},{4,0},{6,2},{8,12},{10,14},{12,8},{14,10},{1,5},{3,7},... | collective-permute-start | bytes 98312 | tf_op jit(solution)/shard_map/ppermute | solution.py:298
  17.0 4.8 %collective-permute-start.6 = (f32[16,512]{1,0:T(8,128)S(1)}, f32[16,512]{1,0:T(8,128)S(1)}, u32[]{:S(2)}, u32[]{:S(2)}) collective-permute-start(f32[16,512]{1,0:T(8,128)S(1)} %get-tuple-element.32), channel_id=1, source_target_pairs={{0,6},{2,4},{4,2},{6,0},{8,14},{10,12},{12,10},{14,8},{1,7},{3,5},... | collective-permute-start | bytes 98312 | tf_op jit(solution)/shard_map/ppermute | solution.py:298
  18.6 3.9 %collective-permute-start.7 = (f32[16,512]{1,0:T(8,128)S(1)}, f32[16,512]{1,0:T(8,128)S(1)}, u32[]{:S(2)}, u32[]{:S(2)}) collective-permute-start(f32[16,512]{1,0:T(8,128)S(1)} %get-tuple-element.33), channel_id=1, source_target_pairs={{0,2},{2,0},{4,6},{6,4},{8,10},{10,8},{12,14},{14,12},{1,3},{3,1},... | collective-permute-start | bytes 98312 | tf_op jit(solution)/shard_map/ppermute | solution.py:298
  22.6 17.4 %copy-start.2 = (bf16[2,2,256,384]{3,2,1,0:T(8,128)(2,1)S(1)}, bf16[2,2,256,384]{3,2,1,0:T(8,128)(2,1)}, u32[]{:S(2)}) copy-start(bf16[2,2,256,384]{3,2,1,0:T(8,128)(2,1)} %constant.21.clone.table_ref) | copy-start | bytes 2359300
  24.2 8.9 %collective-permute-start.8 = (f32[16,512]{1,0:T(8,128)S(1)}, f32[16,512]{1,0:T(8,128)S(1)}, u32[]{:S(2)}, u32[]{:S(2)}) collective-permute-start(f32[16,512]{1,0:T(8,128)S(1)} %get-tuple-element.35), channel_id=1, source_target_pairs={{0,12},{2,14},{4,8},{6,10},{8,4},{10,6},{12,0},{14,2},{1,13},{3,15... | collective-permute-start | bytes 98312 | tf_op jit(solution)/shard_map/ppermute | solution.py:298
  27.8 6.7 %collective-permute-start.9 = (f32[16,512]{1,0:T(8,128)S(1)}, f32[16,512]{1,0:T(8,128)S(1)}, u32[]{:S(2)}, u32[]{:S(2)}) collective-permute-start(f32[16,512]{1,0:T(8,128)S(1)} %get-tuple-element.36), channel_id=1, source_target_pairs={{0,14},{2,12},{4,10},{6,8},{8,6},{10,4},{12,2},{14,0},{1,15},{3,13... | collective-permute-start | bytes 98312 | tf_op jit(solution)/shard_map/ppermute | solution.py:298
  28.6 6.7 %collective-permute-start.10 = (f32[16,512]{1,0:T(8,128)S(1)}, f32[16,512]{1,0:T(8,128)S(1)}, u32[]{:S(2)}, u32[]{:S(2)}) collective-permute-start(f32[16,512]{1,0:T(8,128)S(1)} %get-tuple-element.37), channel_id=1, source_target_pairs={{0,8},{2,10},{4,12},{6,14},{8,0},{10,2},{12,4},{14,6},{1,9},{3,11}... | collective-permute-start | bytes 98312 | tf_op jit(solution)/shard_map/ppermute | solution.py:298
  29.2 6.1 %collective-permute-start.11 = (f32[16,512]{1,0:T(8,128)S(1)}, f32[16,512]{1,0:T(8,128)S(1)}, u32[]{:S(2)}, u32[]{:S(2)}) collective-permute-start(f32[16,512]{1,0:T(8,128)S(1)} %get-tuple-element.38), channel_id=1, source_target_pairs={{0,10},{2,8},{4,14},{6,12},{8,2},{10,0},{12,6},{14,4},{1,11},{3,9}... | collective-permute-start | bytes 98312 | tf_op jit(solution)/shard_map/ppermute | solution.py:298
  31.8 3.9 %collective-permute-start.12 = (f32[16,512]{1,0:T(8,128)S(1)}, f32[16,512]{1,0:T(8,128)S(1)}, u32[]{:S(2)}, u32[]{:S(2)}) collective-permute-start(f32[16,512]{1,0:T(8,128)S(1)} %get-tuple-element.39), channel_id=1, source_target_pairs={{0,4},{2,6},{4,0},{6,2},{8,12},{10,14},{12,8},{14,10},{1,5},{3,7},... | collective-permute-start | bytes 98312 | tf_op jit(solution)/shard_map/ppermute | solution.py:298
  33.1 4.8 %collective-permute-start.13 = (f32[16,512]{1,0:T(8,128)S(1)}, f32[16,512]{1,0:T(8,128)S(1)}, u32[]{:S(2)}, u32[]{:S(2)}) collective-permute-start(f32[16,512]{1,0:T(8,128)S(1)} %get-tuple-element.40), channel_id=1, source_target_pairs={{0,6},{2,4},{4,2},{6,0},{8,14},{10,12},{12,10},{14,8},{1,7},{3,5},... | collective-permute-start | bytes 98312 | tf_op jit(solution)/shard_map/ppermute | solution.py:298
  34.4 3.9 %collective-permute-start.14 = (f32[16,512]{1,0:T(8,128)S(1)}, f32[16,512]{1,0:T(8,128)S(1)}, u32[]{:S(2)}, u32[]{:S(2)}) collective-permute-start(f32[16,512]{1,0:T(8,128)S(1)} %get-tuple-element.41), channel_id=1, source_target_pairs={{0,2},{2,0},{4,6},{6,4},{8,10},{10,8},{12,14},{14,12},{1,3},{3,1},... | collective-permute-start | bytes 98312 | tf_op jit(solution)/shard_map/ppermute | solution.py:298
  38.4 1.6 %collective-permute-start.15 = (f32[8,16,512]{2,1,0:T(8,128)S(1)}, f32[8,16,512]{2,1,0:T(8,128)S(1)}, u32[]{:S(2)}, u32[]{:S(2)}) collective-permute-start(f32[8,16,512]{2,1,0:T(8,128)S(1)} %gather.1.own_ref), channel_id=1, source_target_pairs={{0,1},{1,0},{2,3},{3,2},{4,5},{5,4},{6,7},{7,6},{8,9},{9,8},{10,11... | collective-permute-start | bytes 786440 | tf_op jit(solution)/shard_map/ppermute | solution.py:473
  (2 other events, 1.4 us)

commit v5 on v3

--- a/solution.py
+++ b/solution.py
@@ -1,3 +1,4 @@
+import functools
 import math
 
 import jax
@@ -126,6 +127,7 @@
 
 
 SMALL = pltpu.CompilerParams(vmem_limit_bytes=20 * 1024 * 1024)
+CHUNKS = 2
 
 
 def angles(count, places, extent):
@@ -147,17 +149,14 @@
     return high, low
 
 
-def forward_y_table(cells_y, groups_y, peers, rows_ky):
-    extent = cells_y * groups_y
-    angle = angles(MY, np.arange(extent), extent).astype(np.float32)
-    full = np.stack([np.cos(angle), -np.sin(angle)], axis=1).astype(ml_dtypes.bfloat16)
-    full = full.reshape(groups_y, peers, rows_ky, 2, groups_y, cells_y)
-    out = np.zeros((groups_y, 2, peers, 2, rows_ky, 2, 2, cells_y), ml_dtypes.bfloat16)
-    for place in range(groups_y):
-        for side, half in enumerate((1 - place, place)):
-            for parity in range(2):
-                out[place, side, :, parity, :, :, parity, :] = full[half, :, :, :, place, :]
-    return out.reshape(groups_y, 2 * peers * 4 * rows_ky, 2 * cells_y)
+def forward_y_table(cells_y, groups_y):
+    place = lax.axis_index("gy")
+    row = jnp.arange(2 * MY, dtype=jnp.int32)
+    half = MY // groups_y
+    index = (row // 2 + (1 - place) * half) % MY
+    y_places = place * cells_y + jnp.arange(cells_y, dtype=jnp.int32)
+    angle = phase_table(wave_number(index, MY), y_places, cells_y * groups_y)
+    return jnp.where(row[:, None] % 2 == 0, jnp.cos(angle), -jnp.sin(angle)).astype(jnp.bfloat16)
 
 
 def forward_x_table(cells_x, peers, rows_ky):
@@ -204,42 +203,28 @@
     return jnp.dot(left, right, preferred_element_type=jnp.float32)
 
 
-def forward_y_kernel(flow_hbm, table_hbm, send_ref, keep_ref, flow_ref, table_ref, arrivals):
-    cells_x, cells_y, feat_count = flow_ref.shape
-    rows = table_ref.shape[0] // 2 // send_ref.shape[0]
-    table_copy = pltpu.make_async_copy(
-        table_hbm.at[lax.axis_index("gy")], table_ref, arrivals.at[cells_x]
-    )
-    table_copy.start()
-    copies = []
+def forward_y_kernel(flow_ref, table_ref, *out_refs):
+    chunks = len(out_refs) // 2
+    peers, rows, width = out_refs[0].shape
+    cells_x = flow_ref.shape[0]
+    rows = rows // cells_x
     for x in range(cells_x):
-        copies.append(pltpu.make_async_copy(flow_hbm.at[x], flow_ref.at[x], arrivals.at[x]))
-        copies[x].start()
-    table_copy.wait()
-    for pair in range(cells_x // 2):
-        copies[2 * pair].wait()
-        copies[2 * pair + 1].wait()
-        flow = flow_ref[2 * pair : 2 * pair + 2].reshape(2 * cells_y, feat_count)
-        result = dot(table_ref[...], flow).reshape(2, send_ref.shape[0], rows, feat_count)
-        send_ref[:, pair * rows : (pair + 1) * rows, :] = result[0]
-        keep_ref[:, pair * rows : (pair + 1) * rows, :] = result[1]
+        result = dot(table_ref[...], flow_ref[x]).reshape(2, peers, rows, chunks * width)
+        for chunk in range(chunks):
+            for side in range(2):
+                out_refs[2 * chunk + side][:, x * rows : (x + 1) * rows, :] = result[
+                    side, :, :, chunk * width : (chunk + 1) * width
+                ]
 
 
 def forward_y(flow_field, table, peers, rows_ky):
-    cells_x, cells_y, feat_count = flow_field.shape
-    shape = jax.ShapeDtypeStruct((peers, cells_x * 2 * rows_ky, feat_count), jnp.float32)
-    spec = pl.BlockSpec(memory_space=pltpu.VMEM)
-    source = pl.BlockSpec(memory_space=pltpu.HBM)
+    cells_x, _, feat_count = flow_field.shape
+    shape = jax.ShapeDtypeStruct(
+        (peers, cells_x * 2 * rows_ky, feat_count // CHUNKS), jnp.float32
+    )
     return pl.pallas_call(
         forward_y_kernel,
-        in_specs=[source, source],
-        out_specs=[spec, spec],
-        out_shape=[shape, shape],
-        scratch_shapes=[
-            pltpu.VMEM(flow_field.shape, flow_field.dtype),
-            pltpu.VMEM(table.shape[1:], table.dtype),
-            pltpu.SemaphoreType.DMA((cells_x + 1,)),
-        ],
+        out_shape=[shape] * (2 * CHUNKS),
         compiler_params=SMALL,
         name="forward_y",
     )(flow_field, table)
@@ -263,19 +248,28 @@
             spread_ref[pl.ds(part * tiles + tile, count, stride=group), :] = spectrum[
                 part * count : (part + 1) * count, tile * 128 : (tile + 1) * 128
             ]
-    lane = lax.broadcasted_iota(jnp.int32, (group, 128), 1) < channels
-    sign = jnp.where(lax.broadcasted_iota(jnp.int32, (group, 128), 0) < tiles, -1.0, 1.0)
-    for mode in range(count):
-        block = spread_ref[mode * group : (mode + 1) * group, :]
+    rows = lax.broadcasted_iota(jnp.int32, (8, 128), 0) % group
+    lane = lax.broadcasted_iota(jnp.int32, (8, 128), 1) < channels
+    sign = jnp.where(rows < tiles, -1.0, 1.0)
+    for base in range(0, count * group, 8):
+        block = spread_ref[base : base + 8, :]
         turned = pltpu.roll(block, channels, 1)
-        left = jnp.concatenate([block, turned], axis=0)[:, :channels]
-        left_high, left_low = split_terms(left)
-        product = dot(jnp.concatenate([left_high, left_low], axis=0), weight_ref[0, mode])
-        product = product[: 2 * group] + product[2 * group :]
-        first, second = product[:group], product[group:]
+        firsts, seconds = [], []
+        for start in range(0, 8, group):
+            span = slice(start, start + group)
+            left = jnp.concatenate([block[span], turned[span]], axis=0)[:, :channels]
+            left_high, left_low = split_terms(left)
+            left = jnp.concatenate([left_high, left_low], axis=0)
+            product = dot(left, weight_ref[0, (base + start) // group])
+            product = product[: 2 * group] + product[2 * group :]
+            firsts.append(product[:group])
+            seconds.append(product[group:])
+        first = jnp.concatenate(firsts, axis=0)
+        second = jnp.concatenate(seconds, axis=0)
         real = jnp.where(lane, first, pltpu.roll(second, channels, 1))
         imag = jnp.where(lane, pltpu.roll(first, channels, 1), second)
-        result_ref[mode * group : (mode + 1) * group, :] = real + sign * pltpu.roll(imag, tiles, 0)
+        crossed = jnp.where(rows < tiles, pltpu.roll(imag, 8 - tiles, 0), pltpu.roll(imag, tiles, 0))
+        result_ref[base : base + 8, :] = real + sign * crossed
     parts = []
     for part in range(2):
         parts.append(
@@ -287,7 +281,7 @@
                 axis=1,
             )
         )
-        mixed_ref[0, :, part * feat_count : (part + 1) * feat_count] = parts[part]
+        mixed_ref[part] = parts[part]
     high, low = split_terms(jnp.concatenate(parts, axis=0))
     back = dot(inverse_high[...], high) + dot(inverse_high[...], low) + dot(inverse_low[...], high)
     back_ref[...] = back.reshape(back_ref.shape)
@@ -300,7 +294,7 @@
     return pl.pallas_call(
         mix_kernel,
         out_shape=[
-            jax.ShapeDtypeStruct((1, count, 2 * feat_count), jnp.float32),
+            jax.ShapeDtypeStruct((2, count, feat_count), jnp.float32),
             jax.ShapeDtypeStruct(modes.shape, jnp.float32),
         ],
         scratch_shapes=[scratch, scratch],
@@ -310,13 +304,12 @@
 
 
 def output_kernel(
-    place_ref, flow_ref, table_ref, local_ref, bias_ref, own_ref, other_ref,
-    out_ref, stack_ref, wide_ref, level_ref,
+    place_ref, flow_ref, table_ref, local_ref, bias_ref, own_ref, other_ref, *refs
 ):
+    out_ref, stack_ref, wide_ref, level_ref = refs[-4:]
     step = pl.program_id(0)
     feat_count = flow_ref.shape[-1]
     channels = local_ref.shape[0]
-    width = wide_ref.shape[0]
     pairs = stack_ref.shape[0]
     rows = own_ref.shape[1] // pairs
 
@@ -328,30 +321,25 @@
             high, low = split_terms(both.reshape(-1, feat_count))
             stack_ref[pair] = jnp.concatenate([high, low, high], axis=0)
         wide_ref[...] = jnp.zeros_like(wide_ref)
-        for start in range(0, width, channels):
+        for start in range(0, feat_count, channels):
             span = slice(start, start + channels)
             wide_ref[span, span] = local_ref[...]
-            level_ref[:, span] = bias_ref[...]
-
-    table = table_ref[0, step % 2]
-    for start in range(0, feat_count, width):
-        columns = slice(start, start + width)
-        total = (
-            dot(table, stack_ref[step // 2, :, columns])
-            + dot(flow_ref[0, :, columns], wide_ref[...])
-            + level_ref[...]
-        )
-        out_ref[0, :, columns] = (
-            0.5 * total * (1.0 + lax.erf(total * math.sqrt(0.5)))
-        ).astype(out_ref.dtype)
-
-
-def make_output(flow_field, own, other, table, local, bias):
+            level_ref[:, span] = bias_ref[...].reshape(1, channels)
+
+    total = (
+        dot(table_ref[0, step % 2], stack_ref[step // 2])
+        + dot(flow_ref[0], wide_ref[...])
+        + level_ref[...]
+    )
+    out_ref[0] = (0.5 * total * (1.0 + lax.erf(total * math.sqrt(0.5)))).astype(out_ref.dtype)
+
+
+def make_output(chunk, earlier, flow_field, own, other, table, local, bias):
     cells_x, cells_y, feat_count = flow_field.shape
-    width = 256
+    width = feat_count // CHUNKS
     place = jnp.reshape(lax.axis_index("gy"), (1,))
     whole = lambda array: pl.BlockSpec(array.shape, lambda i, p: (0,) * array.ndim)
-    block = pl.BlockSpec((1, cells_y, feat_count), lambda i, p: (i, 0, 0))
+    block = pl.BlockSpec((1, cells_y, width), lambda i, p: (i, 0, chunk))
     return pl.pallas_call(
         output_kernel,
         grid_spec=pltpu.PrefetchScalarGridSpec(
@@ -364,18 +352,20 @@
                 whole(bias),
                 whole(own),
                 whole(other),
-            ],
+            ]
+            + [pl.BlockSpec(memory_space=pl.ANY)] * len(earlier),
             out_specs=block,
             scratch_shapes=[
-                pltpu.VMEM((cells_x // 2, table.shape[-1], feat_count), jnp.bfloat16),
+                pltpu.VMEM((cells_x // 2, table.shape[-1], width), jnp.bfloat16),
                 pltpu.VMEM((width, width), jnp.bfloat16),
                 pltpu.VMEM((1, width), jnp.float32),
             ],
         ),
         out_shape=jax.ShapeDtypeStruct(flow_field.shape, jnp.bfloat16),
+        input_output_aliases={7: 0} if earlier else {},
         compiler_params=SMALL,
         name="make_output",
-    )(place, flow_field, table, local, bias, own, other)
+    )(place, flow_field, table, local, bias, own, other, *earlier)
 
 
 def row_body(flow_field, spectral_weight, local_weight, bias_terms):
@@ -387,33 +377,33 @@
     inverse_scale = 1.0 / math.sqrt(MX * MY)
     swap = [(0, 1), (1, 0)]
 
-    send, keep = forward_y(
-        flow_field, forward_y_table(cells_y, groups_y, peers, rows_ky), peers, rows_ky
-    )
-    modes = keep + lax.ppermute(send, "gy", swap)
-    mixed, back = mix(
-        lax.all_to_all(modes, "gx", 0, 0, tiled=True),
-        spectral_weight,
-        forward_x_table(cells_x, peers, rows_ky) * forward_scale,
-        inverse_x_table(cells_x, peers, rows_ky),
-    )
-    own = lax.all_to_all(back, "gx", 0, 0, tiled=True)
-    other = lax.ppermute(own, "gy", swap)
+    parts = forward_y(flow_field, forward_y_table(cells_y, groups_y), peers, rows_ky)
+    forward_table = forward_x_table(cells_x, peers, rows_ky) * forward_scale
+    inverse_table = inverse_x_table(cells_x, peers, rows_ky)
     high, low = split_table(inverse_y_table(cells_y, groups_y, peers, rows_ky) * inverse_scale)
-    output = make_output(
-        flow_field,
-        own,
-        other,
-        np.concatenate([high, high, low], axis=-1),
-        local_weight,
-        bias_terms[None, :],
-    )
-    return output, mixed
+    table = np.concatenate([high, high, low], axis=-1)
+    mixed, earlier = [], []
+    for chunk in range(CHUNKS):
+        send, keep = parts[2 * chunk : 2 * chunk + 2]
+        modes = keep + lax.ppermute(send, "gy", swap)
+        modes = lax.all_to_all(modes, "gx", 0, 0, tiled=True)
+        part, back = mix(modes, spectral_weight, forward_table, inverse_table)
+        mixed.append(part)
+        own = lax.all_to_all(back, "gx", 0, 0, tiled=True)
+        other = lax.ppermute(own, "gy", swap)
+        output = make_output(
+            chunk, earlier, flow_field, own, other, table, local_weight, bias_terms
+        )
+        earlier = [output]
+    mixed = jnp.concatenate([part[turn] for turn in range(2) for part in mixed], axis=-1)
+    return output, mixed[None]
 
 
 def body(flow_field, spectral_weight, local_weight, bias_terms):
     whole_rows = spectral_weight.shape[1] % MX == 0
-    if whole_rows and lax.axis_size("gy") == 2 and spectral_weight.shape[1] == 2 * MX:
+    width = flow_field.shape[2] // CHUNKS
+    even = flow_field.shape[2] % CHUNKS == 0 and width == 256 and width % local_weight.shape[0] == 0
+    if even and whole_rows and lax.axis_size("gy") == 2 and spectral_weight.shape[1] == 2 * MX:
         return row_body(flow_field, spectral_weight, local_weight, bias_terms)
     return general_body(flow_field, spectral_weight, local_weight, bias_terms)
 

time: 40.7 us -> 58 us (1.43)
  blocking collectives: 28.4 us -> 0 us
  waiting for transfers between devices: 2.69 us -> 26.5 us
  starting transfers between devices: 0.52 us -> 17.9 us
  Pallas kernels: 5.09 us -> 8.3 us
  other arithmetic: 0.04 us -> 2.44 us
  local copies, waits for them, and re-layouts: 2.86 us -> 1.32 us
    all_to_all x2 -> x0, blocking collectives: 28.4 us -> none  [the longest x1 16.3 us: row_body(): lax.all_to_all(modes, 'gx', 0, 0, tiled=True)]
    all_to_all x0 -> x4, waiting for transfers between devices: none -> 23.6 us  [the longest x2 12.8 us: row_body(): own = lax.all_to_all(back, 'gx', 0, 0, tiled=True)]
    all_to_all x0 -> x4, starting transfers between devices: none -> 17.3 us  [the longest x2 10.5 us: row_body(): modes = lax.all_to_all(modes, 'gx', 0, 0, tiled=True)]
    pallas_call x1 -> x2, Pallas kernels: 2.84 us -> 4.64 us  [make_output(): pl.pallas_call(output_kernel, grid_spec=pltpu.PrefetchScalarGridSpec(num_...]
    unnamed x22 -> x20, local copies, waits for them, and re-layouts: 2.86 us -> 1.3 us
    pallas_call x2 -> x3, Pallas kernels: 2.25 us -> 3.66 us  [the longest x2 3.36 us: mix(): pl.pallas_call(mix_kernel, out_shape=[jax.ShapeDtypeStruct((2, count, fea...]
    add x1 -> x2, other arithmetic: 0.04 us -> 1.35 us  [row_body(): modes = keep + lax.ppermute(send, 'gy', swap)]
    ppermute x1 -> x2, waiting for transfers between devices: 1.16 us -> 2.33 us  [row_body(): modes = keep + lax.ppermute(send, 'gy', swap)]
  transfers between devices with their start and end apart: 2 -> 8, of which waited for: 2 -> 7; matrix products, arithmetic and copies ran while one was open for 0% -> 2% of each run, Pallas kernels for 0% -> 10%
where the time goes in v5:
time: 58 us; the launch traced here: 57.3 us
  waiting for transfers between devices  26.5 us (46%)
  starting transfers between devices  17.9 us (31%)
  Pallas kernels  8.3 us (14%)
  other arithmetic  2.44 us (4%)
  local copies, waits for them, and re-layouts  1.32 us (2%)
  between operations  0.8 us (1%)
    all_to_all x2, waiting for transfers between devices, row_body(): own = lax.all_to_all(back, 'gx', 0, 0, tiled=True)  12.8 us
    all_to_all x2, waiting for transfers between devices, row_body(): modes = lax.all_to_all(modes, 'gx', 0, 0, tiled=True)  10.9 us
    all_to_all x2, starting transfers between devices, row_body(): modes = lax.all_to_all(modes, 'gx', 0, 0, tiled=True)  10.5 us
    all_to_all x2, starting transfers between devices, row_body(): own = lax.all_to_all(back, 'gx', 0, 0, tiled=True)  6.75 us
    pallas_call x2, Pallas kernels, make_output(): pl.pallas_call(output_kernel, grid_spec=pltpu.PrefetchScalarGridSpec(num_...  4.64 us
    pallas_call x2, Pallas kernels, mix(): pl.pallas_call(mix_kernel, out_shape=[jax.ShapeDtypeStruct((2, count, fea...  3.36 us
    ppermute x2, waiting for transfers between devices, row_body(): modes = keep + lax.ppermute(send, 'gy', swap)  2.33 us
    add x2, other arithmetic, row_body(): modes = keep + lax.ppermute(send, 'gy', swap)  1.35 us
  transfers between devices with their start and end apart: 8, of which 7 were waited for; matrix products, arithmetic and copies ran while one was open for 2% of the time, Pallas kernels for 10%

profile of v5, /device:TPU:0, one launch (start us, length us, event | category | flops | bytes accessed | tf_op | source)
XLA Modules:
  0.0 57.3 jit_solution(14598012616372172077)
XLA Ops:
  0.7 0.3 select_convert_fusion.table_ref
  1.0 1.2 %copy-done = bf16[4,256,512]{2,1,0:T(8,128)(2,1)S(1)} copy-done((bf16[4,256,512]{2,1,0:T(8,128)(2,1)S(1)}, bf16[4,256,512]{2,1,0:T(8,128)(2,1)}, u32[]{:S(2)}) %copy-start) | copy-done | bytes 1048600
  2.3 0.3 forward_y.1
  2.6 0.5 collective-permute-start
  3.1 1.0 %collective-permute-done = f32[8,16,256]{2,1,0:T(8,128)S(1)} collective-permute-done((f32[8,16,256]{2,1,0:T(8,128)S(1)}, f32[8,16,256]{2,1,0:T(8,128)S(1)}, u32[]{:S(2)}, u32[]{:S(2)}) %collective-permute-start) | collective-permute-done | bytes 131104 | tf_op jit(solution)/shard_map/ppermute | solution.py:388
  4.1 0.7 %add.70 = f32[8,16,256]{2,1,0:T(8,128)} add(f32[8,16,256]{2,1,0:T(8,128)S(1)} %get-tuple-element.10, f32[8,16,256]{2,1,0:T(8,128)S(1)} %collective-permute-done) | non-fusion elementwise | flops 32768 | bytes 393216 | tf_op jit(solution)/shard_map/add | solution.py:388
  4.7 7.2 %all-to-all-start = ((f32[8,16,256]{2,1,0:T(8,128)}), f32[8,16,256]{2,1,0:T(8,128)S(1)}, u32[]{:S(2)}, u32[]{:S(2)}) async-start(f32[8,16,256]{2,1,0:T(8,128)} %add.70), calls=%async_computation | async-start | bytes 262144 | tf_op jit(solution)/shard_map/all_to_all | solution.py:389
  11.9 1.3 %collective-permute-done.2 = f32[8,16,256]{2,1,0:T(8,128)S(1)} collective-permute-done((f32[8,16,256]{2,1,0:T(8,128)S(1)}, f32[8,16,256]{2,1,0:T(8,128)S(1)}, u32[]{:S(2)}, u32[]{:S(2)}) %collective-permute-start.2) | collective-permute-done | bytes 131104 | tf_op jit(solution)/shard_map/ppermute | solution.py:388
  13.3 0.7 %add.71 = f32[8,16,256]{2,1,0:T(8,128)} add(f32[8,16,256]{2,1,0:T(8,128)S(1)} %get-tuple-element.13, f32[8,16,256]{2,1,0:T(8,128)S(1)} %collective-permute-done.2) | non-fusion elementwise | flops 32768 | bytes 393216 | tf_op jit(solution)/shard_map/add | solution.py:388
  13.9 5.3 %all-to-all-done.modes_ref = f32[8,16,256]{2,1,0:T(8,128)S(1)} async-done(((f32[8,16,256]{2,1,0:T(8,128)}), f32[8,16,256]{2,1,0:T(8,128)S(1)}, u32[]{:S(2)}, u32[]{:S(2)}) %all-to-all-start) | async-done | bytes 131104 | tf_op jit(solution)/shard_map/all_to_all | solution.py:389
  19.2 3.4 %all-to-all-start.2 = ((f32[8,16,256]{2,1,0:T(8,128)}), f32[8,16,256]{2,1,0:T(8,128)S(1)}, u32[]{:S(2)}, u32[]{:S(2)}) async-start(f32[8,16,256]{2,1,0:T(8,128)} %add.71), calls=%async_computation.2 | async-start | bytes 262144 | tf_op jit(solution)/shard_map/all_to_all | solution.py:389
  22.7 1.7 %mix.2 = (f32[2,64,256]{2,1,0:T(8,128)S(1)}, f32[8,16,256]{2,1,0:T(8,128)}) custom-call(f32[8,16,256]{2,1,0:T(8,128)S(1)} %all-to-all-done.modes_ref, bf16[1,64,64,128]{3,2,1,0:T(8,128)(2,1)S(1)} %copy-done.2, bf16[128,128]{1,0:T(8,128)(2,1)S(1)} %copy-done.7, bf16[128,128]{1,0:T(8,128)(2,1)S(1)} %copy-done.6, bf16[128,128]{1,0:T(8,128)(2,1)S(1)} %copy-done.5, ...), custom_call_target="tpu_custom_call" | custom-call | tf_op jit(solution)/shard_map/mix/pallas_call | solution.py:294
  24.4 5.5 %all-to-all-done.2.modes_ref = f32[8,16,256]{2,1,0:T(8,128)S(1)} async-done(((f32[8,16,256]{2,1,0:T(8,128)}), f32[8,16,256]{2,1,0:T(8,128)S(1)}, u32[]{:S(2)}, u32[]{:S(2)}) %all-to-all-start.2) | async-done | bytes 131104 | tf_op jit(solution)/shard_map/all_to_all | solution.py:389
  29.9 3.4 %all-to-all-start.1 = ((f32[8,16,256]{2,1,0:T(8,128)}), f32[8,16,256]{2,1,0:T(8,128)S(1)}, u32[]{:S(2)}, u32[]{:S(2)}) async-start(f32[8,16,256]{2,1,0:T(8,128)} %get-tuple-element.12), calls=%async_computation.1 | async-start | bytes 262144 | tf_op jit(solution)/shard_map/all_to_all | solution.py:392
  33.3 1.7 %mix.3 = (f32[2,64,256]{2,1,0:T(8,128)S(1)}, f32[8,16,256]{2,1,0:T(8,128)}) custom-call(f32[8,16,256]{2,1,0:T(8,128)S(1)} %all-to-all-done.2.modes_ref, bf16[1,64,64,128]{3,2,1,0:T(8,128)(2,1)S(1)} %copy-done.2, bf16[128,128]{1,0:T(8,128)(2,1)S(1)} %copy-done.7, bf16[128,128]{1,0:T(8,128)(2,1)S(1)} %copy-done.6, bf16[128,128]{1,0:T(8,128)(2,1)S(1)} %copy-done.5, ...), custom_call_target="tpu_custom_call" | custom-call | tf_op jit(solution)/shard_map/mix/pallas_call | solution.py:294
  35.0 5.6 %all-to-all-done.1.own_ref = f32[8,16,256]{2,1,0:T(8,128)S(1)} async-done(((f32[8,16,256]{2,1,0:T(8,128)}), f32[8,16,256]{2,1,0:T(8,128)S(1)}, u32[]{:S(2)}, u32[]{:S(2)}) %all-to-all-start.1) | async-done | bytes 131104 | tf_op jit(solution)/shard_map/all_to_all | solution.py:392
  40.6 3.4 %all-to-all-start.3 = ((f32[8,16,256]{2,1,0:T(8,128)}), f32[8,16,256]{2,1,0:T(8,128)S(1)}, u32[]{:S(2)}, u32[]{:S(2)}) async-start(f32[8,16,256]{2,1,0:T(8,128)} %get-tuple-element.15), calls=%async_computation.3 | async-start | bytes 262144 | tf_op jit(solution)/shard_map/all_to_all | solution.py:392
  44.0 0.1 collective-permute-start.1
  44.0 7.2 %all-to-all-done.3.own_ref = f32[8,16,256]{2,1,0:T(8,128)S(1)} async-done(((f32[8,16,256]{2,1,0:T(8,128)}), f32[8,16,256]{2,1,0:T(8,128)S(1)}, u32[]{:S(2)}, u32[]{:S(2)}) %all-to-all-start.3) | async-done | bytes 131104 | tf_op jit(solution)/shard_map/all_to_all | solution.py:392
  51.3 0.7 %maximum_bitcast_fusion = f32[1,64,1024]{2,1,0:T(8,128)} fusion(f32[64,256]{1,0:T(8,128)S(1)} %get-tuple-element.21, f32[64,256]{1,0:T(8,128)S(1)} %get-tuple-element.19, f32[64,256]{1,0:T(8,128)S(1)} %get-tuple-element.20, f32[64,256]{1,0:T(8,128)S(1)} %get-tuple-element.18), kind=kLoop, calls=%fused_computation | loop fusion | flops 196608 | bytes 524288 | tf_op jit(solution)/shard_map/broadcast_in_dim | solution.py:399
  52.0 0.6 %collective-permute-done.3.other_ref = f32[8,16,256]{2,1,0:T(8,128)S(1)} collective-permute-done((f32[8,16,256]{2,1,0:T(8,128)S(1)}, f32[8,16,256]{2,1,0:T(8,128)S(1)}, u32[]{:S(2)}, u32[]{:S(2)}) %collective-permute-start.3) | collective-permute-done | bytes 131104 | tf_op jit(solution)/shard_map/ppermute | solution.py:393
  52.6 0.0 copy-done.9
  52.6 2.3 %make_output.2.refs_0_ = bf16[4,256,512]{2,1,0:T(8,128)(2,1)} custom-call(s32[1]{0:T(128)} %bitcast.place_ref, bf16[4,256,512]{2,1,0:T(8,128)(2,1)S(1)} %copy-done.1, bf16[2,2,256,384]{3,2,1,0:T(8,128)(2,1)S(1)} %copy-done.3, bf16[64,64]{1,0:T(8,128)(2,1)S(1)} %copy-done.8, f32[64]{0:T(128)S(1)} %copy-done.9, f32[8,16,256]{2,1,0:T(8,128)S(1)} %all-to-all-done.3.own_ref, ...), custom_call_target="tpu_custom_call" | custom-call | tf_op jit(solution)/shard_map/make_output/pallas_call | solution.py:343
  55.0 2.3 %make_output.3 = bf16[4,256,512]{2,1,0:T(8,128)(2,1)} custom-call(s32[1]{0:T(128)} %bitcast.place_ref, bf16[4,256,512]{2,1,0:T(8,128)(2,1)S(1)} %copy-done.1, bf16[2,2,256,384]{3,2,1,0:T(8,128)(2,1)S(1)} %copy-done.3, bf16[64,64]{1,0:T(8,128)(2,1)S(1)} %copy-done.8, f32[64]{0:T(128)S(1)} %copy-done.9, ...), custom_call_target="tpu_custom_call", output_to_operand_aliasing={{}: (7, {})} | custom-call | tf_op jit(solution)/shard_map/make_output/pallas_call | solution.py:343
  (26 shorter events, 0.1 us)
Async XLA Ops:
  1.0 1.2 %copy-start = (bf16[4,256,512]{2,1,0:T(8,128)(2,1)S(1)}, bf16[4,256,512]{2,1,0:T(8,128)(2,1)}, u32[]{:S(2)}) copy-start(bf16[4,256,512]{2,1,0:T(8,128)(2,1)} %flow_ref.5) | copy-start | bytes 3145732
  2.3 20.4 %copy-start.2 = (bf16[1,64,64,128]{3,2,1,0:T(8,128)(2,1)S(1)}, bf16[1,64,64,128]{3,2,1,0:T(8,128)(2,1)}, u32[]{:S(2)}) copy-start(bf16[1,64,64,128]{3,2,1,0:T(8,128)(2,1)} %weight_ref.3) | copy-start | bytes 3145732
  2.6 1.5 %collective-permute-start = (f32[8,16,256]{2,1,0:T(8,128)S(1)}, f32[8,16,256]{2,1,0:T(8,128)S(1)}, u32[]{:S(2)}, u32[]{:S(2)}) collective-permute-start(f32[8,16,256]{2,1,0:T(8,128)S(1)} %get-tuple-element.11), channel_id=1, source_target_pairs={{0,1},{1,0},{2,3},{3,2},{4,5},{5,4},{6,7},{7,6},{8,9},{9,8},{10,11... | collective-permute-start | bytes 393224 | tf_op jit(solution)/shard_map/ppermute | solution.py:388
  4.7 14.5 %all-to-all-start = ((f32[8,16,256]{2,1,0:T(8,128)}), f32[8,16,256]{2,1,0:T(8,128)S(1)}, u32[]{:S(2)}, u32[]{:S(2)}) async-start(f32[8,16,256]{2,1,0:T(8,128)} %add.70), calls=%async_computation | async-start | bytes 262144 | tf_op jit(solution)/shard_map/all_to_all | solution.py:389
  11.9 1.3 %collective-permute-start.2 = (f32[8,16,256]{2,1,0:T(8,128)S(1)}, f32[8,16,256]{2,1,0:T(8,128)S(1)}, u32[]{:S(2)}, u32[]{:S(2)}) collective-permute-start(f32[8,16,256]{2,1,0:T(8,128)S(1)} %get-tuple-element.14), channel_id=1, source_target_pairs={{0,1},{1,0},{2,3},{3,2},{4,5},{5,4},{6,7},{7,6},{8,9},{9,8},{10,11... | collective-permute-start | bytes 393224 | tf_op jit(solution)/shard_map/ppermute | solution.py:388
  13.9 8.7 %copy-start.4 = (bf16[128,128]{1,0:T(8,128)(2,1)S(1)}, bf16[128,128]{1,0:T(8,128)(2,1)}, u32[]{:S(2)}) copy-start(bf16[128,128]{1,0:T(8,128)(2,1)} %constant.86.clone.inverse_low) | copy-start | bytes 98308
  13.9 8.7 %copy-start.5 = (bf16[128,128]{1,0:T(8,128)(2,1)S(1)}, bf16[128,128]{1,0:T(8,128)(2,1)}, u32[]{:S(2)}) copy-start(bf16[128,128]{1,0:T(8,128)(2,1)} %constant.85.clone.inverse_high) | copy-start | bytes 98308
  13.9 8.7 %copy-start.6 = (bf16[128,128]{1,0:T(8,128)(2,1)S(1)}, bf16[128,128]{1,0:T(8,128)(2,1)}, u32[]{:S(2)}) copy-start(bf16[128,128]{1,0:T(8,128)(2,1)} %constant.84.clone.forward_low) | copy-start | bytes 98308
  13.9 8.7 %copy-start.7 = (bf16[128,128]{1,0:T(8,128)(2,1)S(1)}, bf16[128,128]{1,0:T(8,128)(2,1)}, u32[]{:S(2)}) copy-start(bf16[128,128]{1,0:T(8,128)(2,1)} %constant.83.clone.forward_high) | copy-start | bytes 98308
  19.2 10.7 %all-to-all-start.2 = ((f32[8,16,256]{2,1,0:T(8,128)}), f32[8,16,256]{2,1,0:T(8,128)S(1)}, u32[]{:S(2)}, u32[]{:S(2)}) async-start(f32[8,16,256]{2,1,0:T(8,128)} %add.71), calls=%async_computation.2 | async-start | bytes 262144 | tf_op jit(solution)/shard_map/all_to_all | solution.py:389
  29.9 10.7 %all-to-all-start.1 = ((f32[8,16,256]{2,1,0:T(8,128)}), f32[8,16,256]{2,1,0:T(8,128)S(1)}, u32[]{:S(2)}, u32[]{:S(2)}) async-start(f32[8,16,256]{2,1,0:T(8,128)} %get-tuple-element.12), calls=%async_computation.1 | async-start | bytes 262144 | tf_op jit(solution)/shard_map/all_to_all | solution.py:392
  33.3 19.3 %copy-start.1 = (bf16[4,256,512]{2,1,0:T(8,128)(2,1)S(1)}, bf16[4,256,512]{2,1,0:T(8,128)(2,1)}, u32[]{:S(2)}) copy-start(bf16[4,256,512]{2,1,0:T(8,128)(2,1)} %flow_ref.5) | copy-start | bytes 3145732
  35.0 17.6 %copy-start.3 = (bf16[2,2,256,384]{3,2,1,0:T(8,128)(2,1)S(1)}, bf16[2,2,256,384]{3,2,1,0:T(8,128)(2,1)}, u32[]{:S(2)}) copy-start(bf16[2,2,256,384]{3,2,1,0:T(8,128)(2,1)} %constant.87.clone.table_ref) | copy-start | bytes 2359300
  40.6 10.7 %all-to-all-start.3 = ((f32[8,16,256]{2,1,0:T(8,128)}), f32[8,16,256]{2,1,0:T(8,128)S(1)}, u32[]{:S(2)}, u32[]{:S(2)}) async-start(f32[8,16,256]{2,1,0:T(8,128)} %get-tuple-element.15), calls=%async_computation.3 | async-start | bytes 262144 | tf_op jit(solution)/shard_map/all_to_all | solution.py:392
  44.0 11.0 %collective-permute-start.1 = (f32[8,16,256]{2,1,0:T(8,128)S(1)}, f32[8,16,256]{2,1,0:T(8,128)S(1)}, u32[]{:S(2)}, u32[]{:S(2)}) collective-permute-start(f32[8,16,256]{2,1,0:T(8,128)S(1)} %all-to-all-done.1.own_ref), channel_id=1, source_target_pairs={{0,1},{1,0},{2,3},{3,2},{4,5},{5,4},{6,7},{7,6},{8,9},{9,8},{10,11... | collective-permute-start | bytes 393224 | tf_op jit(solution)/shard_map/ppermute | solution.py:393
  51.2 1.3 %collective-permute-start.3 = (f32[8,16,256]{2,1,0:T(8,128)S(1)}, f32[8,16,256]{2,1,0:T(8,128)S(1)}, u32[]{:S(2)}, u32[]{:S(2)}) collective-permute-start(f32[8,16,256]{2,1,0:T(8,128)S(1)} %all-to-all-done.3.own_ref), channel_id=1, source_target_pairs={{0,1},{1,0},{2,3},{3,2},{4,5},{5,4},{6,7},{7,6},{8,9},{9,8},{10,11... | collective-permute-start | bytes 393224 | tf_op jit(solution)/shard_map/ppermute | solution.py:393
  51.2 1.3 %copy-start.8 = (bf16[64,64]{1,0:T(8,128)(2,1)S(1)}, bf16[64,64]{1,0:T(8,128)(2,1)}, u32[]{:S(2)}) copy-start(bf16[64,64]{1,0:T(8,128)(2,1)} %local_ref.3) | copy-start | bytes 24580
  52.0 0.7 %copy-start.9 = (f32[64]{0:T(128)S(1)}, f32[64]{0:T(128)}, u32[]{:S(2)}) copy-start(f32[64]{0:T(128)} %bias_ref.3) | copy-start | bytes 772

commit v6 on v5

--- a/solution.py
+++ b/solution.py
@@ -127,7 +127,7 @@
 
 
 SMALL = pltpu.CompilerParams(vmem_limit_bytes=20 * 1024 * 1024)
-CHUNKS = 2
+WIDTH = 256
 
 
 def angles(count, places, extent):
@@ -149,12 +149,25 @@
     return high, low
 
 
-def forward_y_table(cells_y, groups_y):
-    place = lax.axis_index("gy")
+def quad():
+    place = lax.axis_index("gx")
+    return place // 2, place % 2, lax.axis_index("gy")
+
+
+def turns(layers):
+    return list(range(layers - 1, 0, -1)) + [0]
+
+
+def forward_y_table(cells_y, groups_y, peers, rows_ky):
+    z, x, y = quad()
+    layers = peers // 2
     row = jnp.arange(2 * MY, dtype=jnp.int32)
-    half = MY // groups_y
-    index = (row // 2 + (1 - place) * half) % MY
-    y_places = place * cells_y + jnp.arange(cells_y, dtype=jnp.int32)
+    block = row // (2 * rows_ky)
+    turn = layers - 1 - block % layers
+    owner = (z ^ turn) * 2 + (x ^ (1 - block // layers % 2))
+    owner = (y ^ (1 - block // peers)) * peers + owner
+    index = owner * rows_ky + row // 2 % rows_ky
+    y_places = y * cells_y + jnp.arange(cells_y, dtype=jnp.int32)
     angle = phase_table(wave_number(index, MY), y_places, cells_y * groups_y)
     return jnp.where(row[:, None] % 2 == 0, jnp.cos(angle), -jnp.sin(angle)).astype(jnp.bfloat16)
 
@@ -204,42 +217,92 @@
 
 
 def forward_y_kernel(flow_ref, table_ref, *out_refs):
-    chunks = len(out_refs) // 2
-    peers, rows, width = out_refs[0].shape
+    layers, rows, feat_count = out_refs[0].shape
     cells_x = flow_ref.shape[0]
     rows = rows // cells_x
     for x in range(cells_x):
-        result = dot(table_ref[...], flow_ref[x]).reshape(2, peers, rows, chunks * width)
-        for chunk in range(chunks):
-            for side in range(2):
-                out_refs[2 * chunk + side][:, x * rows : (x + 1) * rows, :] = result[
-                    side, :, :, chunk * width : (chunk + 1) * width
-                ]
-
-
-def forward_y(flow_field, table, peers, rows_ky):
+        result = dot(table_ref[...], flow_ref[x]).reshape(4, layers, rows, feat_count)
+        for part, out_ref in enumerate(out_refs):
+            out_ref[:, x * rows : (x + 1) * rows, :] = result[part]
+
+
+def forward_y(flow_field, table, layers, rows_ky):
     cells_x, _, feat_count = flow_field.shape
-    shape = jax.ShapeDtypeStruct(
-        (peers, cells_x * 2 * rows_ky, feat_count // CHUNKS), jnp.float32
-    )
+    shape = jax.ShapeDtypeStruct((layers, cells_x * 2 * rows_ky, feat_count), jnp.float32)
     return pl.pallas_call(
         forward_y_kernel,
-        out_shape=[shape] * (2 * CHUNKS),
+        out_shape=[shape] * 4,
         compiler_params=SMALL,
         name="forward_y",
     )(flow_field, table)
 
 
-def mix_kernel(
-    modes_ref, weight_ref, forward_high, forward_low, inverse_high, inverse_low,
-    mixed_ref, back_ref, spread_ref, result_ref,
-):
-    feat_count = modes_ref.shape[-1]
+def flip_both(block, peers):
+    pairs = [(place, place ^ 3) for place in range(2 * peers)]
+    return lax.ppermute(block, ("gx", "gy"), pairs)
+
+
+def flip_column(block, peers):
+    return lax.ppermute(block, "gx", [(place, place ^ 1) for place in range(peers)])
+
+
+def flip_core(block):
+    return lax.ppermute(block, "gy", [(0, 1), (1, 0)])
+
+
+def along_z(blocks, peers):
+    arrived = []
+    for turn, block in zip(turns(len(blocks)), blocks):
+        pairs = [(place, place ^ (2 * turn)) for place in range(peers)]
+        arrived.append(lax.ppermute(block, "gx", pairs) if turn else block)
+    return arrived
+
+
+def combine_kernel(both_ref, column_ref, core_ref, own_ref, *out_refs):
+    for turn, out_ref in enumerate(out_refs):
+        out_ref[0] = own_ref[turn] + core_ref[turn]
+        out_ref[1] = column_ref[turn] + both_ref[turn]
+
+
+def combine(both, column, core, own):
+    return pl.pallas_call(
+        combine_kernel,
+        out_shape=[jax.ShapeDtypeStruct((2,) + own.shape[1:], own.dtype)] * own.shape[0],
+        compiler_params=SMALL,
+        name="combine",
+    )(both, column, core, own)
+
+
+def gather_kernel(*refs):
+    for turn, block_ref in enumerate(refs[:-2]):
+        refs[-2][turn] = block_ref[0]
+        refs[-1][turn] = block_ref[1]
+
+
+def gather(blocks):
+    shape = jax.ShapeDtypeStruct((len(blocks),) + blocks[0].shape[1:], blocks[0].dtype)
+    return pl.pallas_call(
+        gather_kernel, out_shape=[shape] * 2, compiler_params=SMALL, name="gather"
+    )(*blocks)
+
+
+def mix_kernel(layers, *refs):
+    block_refs = refs[:layers]
+    weight_ref, forward_high, forward_low, inverse_high, inverse_low, mixed_ref = refs[
+        layers : layers + 6
+    ]
+    back_refs = refs[layers + 6 : 2 * layers + 6]
+    order_ref, spread_ref, result_ref = refs[2 * layers + 6 :]
+    z, x, _ = quad()
+    for turn, block_ref in zip(turns(layers), block_refs):
+        for side in range(2):
+            order_ref[(z ^ turn) * 2 + (x ^ side)] = block_ref[side]
+    feat_count = order_ref.shape[-1]
     count = weight_ref.shape[1]
     channels = weight_ref.shape[2]
     tiles = feat_count // 128
     group = 2 * tiles
-    high, low = split_terms(modes_ref[...].reshape(-1, feat_count))
+    high, low = split_terms(order_ref[...].reshape(-1, feat_count))
     spectrum = (
         dot(forward_high[...], high) + dot(forward_high[...], low) + dot(forward_low[...], high)
     )
@@ -281,65 +344,81 @@
                 axis=1,
             )
         )
-        mixed_ref[part] = parts[part]
+        mixed_ref[0, :, part * feat_count : (part + 1) * feat_count] = parts[part]
     high, low = split_terms(jnp.concatenate(parts, axis=0))
     back = dot(inverse_high[...], high) + dot(inverse_high[...], low) + dot(inverse_low[...], high)
-    back_ref[...] = back.reshape(back_ref.shape)
-
-
-def mix(modes, weights, forward_table, inverse_table):
-    feat_count = modes.shape[-1]
+    order_ref[...] = back.reshape(order_ref.shape)
+    for turn, back_ref in zip(turns(layers), back_refs):
+        for side in range(2):
+            back_ref[side] = order_ref[(z ^ turn) * 2 + (x ^ side)]
+
+
+def mix(blocks, weights, forward_table, inverse_table):
+    _, rows, feat_count = blocks[0].shape
+    layers = len(blocks)
     count = weights.shape[1]
     scratch = pltpu.VMEM((count * feat_count // 64, 128), jnp.float32)
-    return pl.pallas_call(
-        mix_kernel,
-        out_shape=[
-            jax.ShapeDtypeStruct((2, count, feat_count), jnp.float32),
-            jax.ShapeDtypeStruct(modes.shape, jnp.float32),
-        ],
-        scratch_shapes=[scratch, scratch],
+    mixed, *back = pl.pallas_call(
+        functools.partial(mix_kernel, layers),
+        out_shape=[jax.ShapeDtypeStruct((1, count, 2 * feat_count), jnp.float32)]
+        + [jax.ShapeDtypeStruct(blocks[0].shape, jnp.float32)] * layers,
+        scratch_shapes=[pltpu.VMEM((2 * layers, rows, feat_count), jnp.float32), scratch, scratch],
         compiler_params=SMALL,
         name="mix",
-    )(modes, weights, *split_table(forward_table), *split_table(inverse_table))
+    )(*blocks, weights, *split_table(forward_table), *split_table(inverse_table))
+    return mixed, back
 
 
 def output_kernel(
-    place_ref, flow_ref, table_ref, local_ref, bias_ref, own_ref, other_ref, *refs
+    place_ref, flow_ref, table_ref, local_ref, bias_ref, own_ref, core_ref, column_ref, both_ref,
+    out_ref, order_ref, stack_ref, wide_ref, level_ref,
 ):
-    out_ref, stack_ref, wide_ref, level_ref = refs[-4:]
     step = pl.program_id(0)
     feat_count = flow_ref.shape[-1]
     channels = local_ref.shape[0]
+    width = wide_ref.shape[0]
     pairs = stack_ref.shape[0]
+    layers = own_ref.shape[0]
     rows = own_ref.shape[1] // pairs
 
     @pl.when(step == 0)
     def _():
+        z, x, _ = quad()
+        for index, turn in enumerate(turns(layers)):
+            peer = (z ^ turn) * 2
+            order_ref[peer + x] = own_ref[index]
+            order_ref[peer + (x ^ 1)] = column_ref[index]
+            order_ref[2 * layers + peer + x] = core_ref[index]
+            order_ref[2 * layers + peer + (x ^ 1)] = both_ref[index]
         for pair in range(pairs):
             span = slice(pair * rows, (pair + 1) * rows)
-            both = jnp.concatenate([own_ref[:, span, :], other_ref[:, span, :]], axis=0)
-            high, low = split_terms(both.reshape(-1, feat_count))
+            high, low = split_terms(order_ref[:, span, :].reshape(-1, feat_count))
             stack_ref[pair] = jnp.concatenate([high, low, high], axis=0)
         wide_ref[...] = jnp.zeros_like(wide_ref)
-        for start in range(0, feat_count, channels):
+        for start in range(0, width, channels):
             span = slice(start, start + channels)
             wide_ref[span, span] = local_ref[...]
             level_ref[:, span] = bias_ref[...].reshape(1, channels)
 
-    total = (
-        dot(table_ref[0, step % 2], stack_ref[step // 2])
-        + dot(flow_ref[0], wide_ref[...])
-        + level_ref[...]
-    )
-    out_ref[0] = (0.5 * total * (1.0 + lax.erf(total * math.sqrt(0.5)))).astype(out_ref.dtype)
-
-
-def make_output(chunk, earlier, flow_field, own, other, table, local, bias):
+    table = table_ref[0, step % 2]
+    for start in range(0, feat_count, width):
+        columns = slice(start, start + width)
+        total = (
+            dot(table, stack_ref[step // 2, :, columns])
+            + dot(flow_ref[0, :, columns], wide_ref[...])
+            + level_ref[...]
+        )
+        out_ref[0, :, columns] = (
+            0.5 * total * (1.0 + lax.erf(total * math.sqrt(0.5)))
+        ).astype(out_ref.dtype)
+
+
+def make_output(flow_field, parts, table, local, bias):
     cells_x, cells_y, feat_count = flow_field.shape
-    width = feat_count // CHUNKS
+    layers, rows, _ = parts[0].shape
     place = jnp.reshape(lax.axis_index("gy"), (1,))
     whole = lambda array: pl.BlockSpec(array.shape, lambda i, p: (0,) * array.ndim)
-    block = pl.BlockSpec((1, cells_y, width), lambda i, p: (i, 0, chunk))
+    block = pl.BlockSpec((1, cells_y, feat_count), lambda i, p: (i, 0, 0))
     return pl.pallas_call(
         output_kernel,
         grid_spec=pltpu.PrefetchScalarGridSpec(
@@ -350,22 +429,20 @@
                 pl.BlockSpec((1,) + table.shape[1:], lambda i, p: (p[0], 0, 0, 0)),
                 whole(local),
                 whole(bias),
-                whole(own),
-                whole(other),
             ]
-            + [pl.BlockSpec(memory_space=pl.ANY)] * len(earlier),
+            + [whole(part) for part in parts],
             out_specs=block,
             scratch_shapes=[
-                pltpu.VMEM((cells_x // 2, table.shape[-1], width), jnp.bfloat16),
-                pltpu.VMEM((width, width), jnp.bfloat16),
-                pltpu.VMEM((1, width), jnp.float32),
+                pltpu.VMEM((4 * layers, rows, feat_count), jnp.float32),
+                pltpu.VMEM((cells_x // 2, table.shape[-1], feat_count), jnp.bfloat16),
+                pltpu.VMEM((WIDTH, WIDTH), jnp.bfloat16),
+                pltpu.VMEM((1, WIDTH), jnp.float32),
             ],
         ),
         out_shape=jax.ShapeDtypeStruct(flow_field.shape, jnp.bfloat16),
-        input_output_aliases={7: 0} if earlier else {},
         compiler_params=SMALL,
         name="make_output",
-    )(place, flow_field, table, local, bias, own, other, *earlier)
+    )(place, flow_field, table, local, bias, *parts)
 
 
 def row_body(flow_field, spectral_weight, local_weight, bias_terms):
@@ -375,35 +452,27 @@
     rows_ky = MY // groups_y // peers
     forward_scale = 1.0 / math.sqrt(cells_x * peers * cells_y * groups_y)
     inverse_scale = 1.0 / math.sqrt(MX * MY)
-    swap = [(0, 1), (1, 0)]
-
-    parts = forward_y(flow_field, forward_y_table(cells_y, groups_y), peers, rows_ky)
-    forward_table = forward_x_table(cells_x, peers, rows_ky) * forward_scale
-    inverse_table = inverse_x_table(cells_x, peers, rows_ky)
+
+    table = forward_y_table(cells_y, groups_y, peers, rows_ky)
+    both, core, column, own = forward_y(flow_field, table, peers // 2, rows_ky)
+    blocks = combine(flip_both(both, peers), flip_column(column, peers), flip_core(core), own)
+    mixed, back = mix(
+        along_z(blocks, peers),
+        spectral_weight,
+        forward_x_table(cells_x, peers, rows_ky) * forward_scale,
+        inverse_x_table(cells_x, peers, rows_ky),
+    )
+    own, column = gather(along_z(back, peers))
+    parts = [own, flip_core(own), flip_column(column, peers), flip_both(column, peers)]
     high, low = split_table(inverse_y_table(cells_y, groups_y, peers, rows_ky) * inverse_scale)
     table = np.concatenate([high, high, low], axis=-1)
-    mixed, earlier = [], []
-    for chunk in range(CHUNKS):
-        send, keep = parts[2 * chunk : 2 * chunk + 2]
-        modes = keep + lax.ppermute(send, "gy", swap)
-        modes = lax.all_to_all(modes, "gx", 0, 0, tiled=True)
-        part, back = mix(modes, spectral_weight, forward_table, inverse_table)
-        mixed.append(part)
-        own = lax.all_to_all(back, "gx", 0, 0, tiled=True)
-        other = lax.ppermute(own, "gy", swap)
-        output = make_output(
-            chunk, earlier, flow_field, own, other, table, local_weight, bias_terms
-        )
-        earlier = [output]
-    mixed = jnp.concatenate([part[turn] for turn in range(2) for part in mixed], axis=-1)
-    return output, mixed[None]
+    return make_output(flow_field, parts, table, local_weight, bias_terms), mixed
 
 
 def body(flow_field, spectral_weight, local_weight, bias_terms):
-    whole_rows = spectral_weight.shape[1] % MX == 0
-    width = flow_field.shape[2] // CHUNKS
-    even = flow_field.shape[2] % CHUNKS == 0 and width == 256 and width % local_weight.shape[0] == 0
-    if even and whole_rows and lax.axis_size("gy") == 2 and spectral_weight.shape[1] == 2 * MX:
+    peers = lax.axis_size("gx")
+    paired = lax.axis_size("gy") == 2 and peers & (peers - 1) == 0
+    if paired and spectral_weight.shape[1] == 2 * MX and WIDTH % local_weight.shape[0] == 0:
         return row_body(flow_field, spectral_weight, local_weight, bias_terms)
     return general_body(flow_field, spectral_weight, local_weight, bias_terms)
 

time: 58 us -> 44.8 us (0.77)
  waiting for transfers between devices: 26.5 us -> 22.5 us
  Pallas kernels: 8.3 us -> 4.83 us
  starting transfers between devices: 17.9 us -> 14.8 us
  other arithmetic: 2.44 us -> 0.38 us
    all_to_all x4 -> x0, waiting for transfers between devices: 23.6 us -> none  [the longest x2 12.8 us: row_body(): own = lax.all_to_all(back, 'gx', 0, 0, tiled=True)]
    ppermute x4 -> x12, waiting for transfers between devices: 2.92 us -> 22.5 us  [the longest x6 9.78 us: along_z(): arrived.append(lax.ppermute(block, 'gx', pairs) if turn else block)]
    all_to_all x4 -> x0, starting transfers between devices: 17.3 us -> none  [the longest x2 10.5 us: row_body(): modes = lax.all_to_all(modes, 'gx', 0, 0, tiled=True)]
    ppermute x4 -> x12, starting transfers between devices: 0.59 us -> 14.8 us  [the longest x6 9.51 us: along_z(): arrived.append(lax.ppermute(block, 'gx', pairs) if turn else block)]
    pallas_call x3 -> x4, Pallas kernels: 3.66 us -> 1.92 us  [the longest x1 1.57 us: mix(): pl.pallas_call(functools.partial(mix_kernel, layers), out_shape=[jax.Shap...]
    pallas_call x2 -> x1, Pallas kernels: 4.64 us -> 2.91 us  [make_output(): pl.pallas_call(output_kernel, grid_spec=pltpu.PrefetchScalarGridSpec(num_...]
    add x3 -> x1, other arithmetic: 1.35 us -> 0.01 us  [forward_y_table(): y_places = y * cells_y + jnp.arange(cells_y, dtype=jnp.int32)]
    broadcast_in_dim x1 -> x0, other arithmetic: 0.72 us -> none  [row_body(): return (output, mixed[None])]
  transfers between devices with their start and end apart: 8 -> 12, of which waited for: 7 -> 8; matrix products, arithmetic and copies ran while one was open for 2% -> 0% of each run, Pallas kernels for 10% -> 0%
where the time goes in v6:
time: 44.8 us; the launch traced here: 44.6 us
  waiting for transfers between devices  22.5 us (50%)
  starting transfers between devices  14.8 us (33%)
  Pallas kernels  4.83 us (11%)
  local copies, waits for them, and re-layouts  1.26 us (3%)
  between operations  0.81 us (2%)
    ppermute x6, waiting for transfers between devices, along_z(): arrived.append(lax.ppermute(block, 'gx', pairs) if turn else block)  9.78 us
    ppermute x6, starting transfers between devices, along_z(): arrived.append(lax.ppermute(block, 'gx', pairs) if turn else block)  9.51 us
    ppermute x2, waiting for transfers between devices, flip_both(): return lax.ppermute(block, ('gx', 'gy'), pairs)  6.54 us
    ppermute x2, waiting for transfers between devices, flip_column(): lax.ppermute(block, 'gx', [(place, place ^ 1) for place in range(peers)])  6.18 us
    ppermute x2, starting transfers between devices, flip_both(): return lax.ppermute(block, ('gx', 'gy'), pairs)  4.07 us
    pallas_call x1, Pallas kernels, make_output(): pl.pallas_call(output_kernel, grid_spec=pltpu.PrefetchScalarGridSpec(num_...  2.91 us
    pallas_call x1, Pallas kernels, mix(): pl.pallas_call(functools.partial(mix_kernel, layers), out_shape=[jax.Shap...  1.57 us
    unnamed x20, local copies, waits for them, and re-layouts  1.26 us
  transfers between devices with their start and end apart: 12, of which 8 were waited for; matrix products, arithmetic and copies ran while one was open for 0% of the time, Pallas kernels for 0%

profile of v6, /device:TPU:0, one launch (start us, length us, event | category | flops | bytes accessed | tf_op | source)
XLA Modules:
  0.0 44.6 jit_solution(15307459985421715878)
XLA Ops:
  0.7 0.3 select_convert_fusion.table_ref
  1.1 1.2 %copy-done = bf16[4,256,512]{2,1,0:T(8,128)(2,1)S(1)} copy-done((bf16[4,256,512]{2,1,0:T(8,128)(2,1)S(1)}, bf16[4,256,512]{2,1,0:T(8,128)(2,1)}, u32[]{:S(2)}) %copy-start) | copy-done | bytes 1048600
  2.3 0.0 copy-start.7
  2.3 0.3 forward_y.1
  2.6 2.4 %collective-permute-start = (f32[4,16,512]{2,1,0:T(8,128)S(1)}, f32[4,16,512]{2,1,0:T(8,128)S(1)}, u32[]{:S(2)}, u32[]{:S(2)}) collective-permute-start(f32[4,16,512]{2,1,0:T(8,128)S(1)} %get-tuple-element.17), channel_id=1, source_target_pairs={{0,3},{1,2},{2,1},{3,0},{4,7},{5,6},{6,5},{7,4},{8,11},{9,10},{10,... | collective-permute-start | bytes 393224 | tf_op jit(solution)/shard_map/ppermute | solution.py:242
  5.1 0.6 %collective-permute-start.1 = (f32[4,16,512]{2,1,0:T(8,128)S(1)}, f32[4,16,512]{2,1,0:T(8,128)S(1)}, u32[]{:S(2)}, u32[]{:S(2)}) collective-permute-start(f32[4,16,512]{2,1,0:T(8,128)S(1)} %get-tuple-element.18), channel_id=1, source_target_pairs={{0,2},{2,0},{4,6},{6,4},{8,10},{10,8},{12,14},{14,12},{1,3},{3,1},... | collective-permute-start | bytes 393224 | tf_op jit(solution)/shard_map/ppermute | solution.py:246
  5.7 0.0 collective-permute-start.2
  5.8 3.2 %collective-permute-done.both_ref = f32[4,16,512]{2,1,0:T(8,128)S(1)} collective-permute-done((f32[4,16,512]{2,1,0:T(8,128)S(1)}, f32[4,16,512]{2,1,0:T(8,128)S(1)}, u32[]{:S(2)}, u32[]{:S(2)}) %collective-permute-start) | collective-permute-done | bytes 131104 | tf_op jit(solution)/shard_map/ppermute | solution.py:242
  9.0 3.0 %collective-permute-done.1.column_ref = f32[4,16,512]{2,1,0:T(8,128)S(1)} collective-permute-done((f32[4,16,512]{2,1,0:T(8,128)S(1)}, f32[4,16,512]{2,1,0:T(8,128)S(1)}, u32[]{:S(2)}, u32[]{:S(2)}) %collective-permute-start.1) | collective-permute-done | bytes 131104 | tf_op jit(solution)/shard_map/ppermute | solution.py:246
  12.0 4.5 %collective-permute-start.3 = (f32[2,16,512]{2,1,0:T(8,128)S(1)}, f32[2,16,512]{2,1,0:T(8,128)S(1)}, u32[]{:S(2)}, u32[]{:S(2)}) collective-permute-start(f32[2,16,512]{2,1,0:T(8,128)S(1)} %get-tuple-element.21), channel_id=1, source_target_pairs={{0,12},{2,14},{4,8},{6,10},{8,4},{10,6},{12,0},{14,2},{1,13},{3,15... | collective-permute-start | bytes 196616 | tf_op jit(solution)/shard_map/ppermute | solution.py:257
  16.5 0.6 %collective-permute-start.5 = (f32[2,16,512]{2,1,0:T(8,128)S(1)}, f32[2,16,512]{2,1,0:T(8,128)S(1)}, u32[]{:S(2)}, u32[]{:S(2)}) collective-permute-start(f32[2,16,512]{2,1,0:T(8,128)S(1)} %get-tuple-element.23), channel_id=1, source_target_pairs={{0,4},{2,6},{4,0},{6,2},{8,12},{10,14},{12,8},{14,10},{1,5},{3,7},... | collective-permute-start | bytes 196616 | tf_op jit(solution)/shard_map/ppermute | solution.py:257
  17.1 1.9 %collective-permute-done.3.refs_0_ = f32[2,16,512]{2,1,0:T(8,128)S(1)} collective-permute-done((f32[2,16,512]{2,1,0:T(8,128)S(1)}, f32[2,16,512]{2,1,0:T(8,128)S(1)}, u32[]{:S(2)}, u32[]{:S(2)}) %collective-permute-start.3) | collective-permute-done | bytes 65568 | tf_op jit(solution)/shard_map/ppermute | solution.py:257
  19.0 3.3 %collective-permute-done.4.refs_1_ = f32[2,16,512]{2,1,0:T(8,128)S(1)} collective-permute-done((f32[2,16,512]{2,1,0:T(8,128)S(1)}, f32[2,16,512]{2,1,0:T(8,128)S(1)}, u32[]{:S(2)}, u32[]{:S(2)}) %collective-permute-start.4) | collective-permute-done | bytes 65568 | tf_op jit(solution)/shard_map/ppermute | solution.py:257
  22.3 1.6 %mix.1 = (f32[1,64,1024]{2,1,0:T(8,128)}, f32[2,16,512]{2,1,0:T(8,128)S(1)}, f32[2,16,512]{2,1,0:T(8,128)S(1)}, f32[2,16,512]{2,1,0:T(8,128)S(1)}, f32[2,16,512]{2,1,0:T(8,128)S(1)}) custom-call(f32[2,16,512]{2,1,0:T(8,128)S(1)} %collective-permute-done.3.refs_0_, f32[2,16,512]{2,1,0:T(8,128)S(1)} %collective-permute-done.4.refs_1_, ...), custom_call_target="tpu_custom_call" | custom-call | tf_op jit(solution)/shard_map/mix/pallas_call | solution.py:361
  23.9 2.5 %collective-permute-start.6 = (f32[2,16,512]{2,1,0:T(8,128)S(1)}, f32[2,16,512]{2,1,0:T(8,128)S(1)}, u32[]{:S(2)}, u32[]{:S(2)}) collective-permute-start(f32[2,16,512]{2,1,0:T(8,128)S(1)} %get-tuple-element.25), channel_id=1, source_target_pairs={{0,12},{2,14},{4,8},{6,10},{8,4},{10,6},{12,0},{14,2},{1,13},{3,15... | collective-permute-start | bytes 196616 | tf_op jit(solution)/shard_map/ppermute | solution.py:257
  26.4 1.9 %collective-permute-start.8 = (f32[2,16,512]{2,1,0:T(8,128)S(1)}, f32[2,16,512]{2,1,0:T(8,128)S(1)}, u32[]{:S(2)}, u32[]{:S(2)}) collective-permute-start(f32[2,16,512]{2,1,0:T(8,128)S(1)} %get-tuple-element.27), channel_id=1, source_target_pairs={{0,4},{2,6},{4,0},{6,2},{8,12},{10,14},{12,8},{14,10},{1,5},{3,7},... | collective-permute-start | bytes 196616 | tf_op jit(solution)/shard_map/ppermute | solution.py:257
  28.3 1.9 %collective-permute-done.6.refs_0_ = f32[2,16,512]{2,1,0:T(8,128)S(1)} collective-permute-done((f32[2,16,512]{2,1,0:T(8,128)S(1)}, f32[2,16,512]{2,1,0:T(8,128)S(1)}, u32[]{:S(2)}, u32[]{:S(2)}) %collective-permute-start.6) | collective-permute-done | bytes 65568 | tf_op jit(solution)/shard_map/ppermute | solution.py:257
  30.2 2.7 %collective-permute-done.7.refs_1_ = f32[2,16,512]{2,1,0:T(8,128)S(1)} collective-permute-done((f32[2,16,512]{2,1,0:T(8,128)S(1)}, f32[2,16,512]{2,1,0:T(8,128)S(1)}, u32[]{:S(2)}, u32[]{:S(2)}) %collective-permute-start.7) | collective-permute-done | bytes 65568 | tf_op jit(solution)/shard_map/ppermute | solution.py:257
  32.9 0.1 collective-permute-start.9
  33.0 1.6 %collective-permute-start.11 = (f32[4,16,512]{2,1,0:T(8,128)S(1)}, f32[4,16,512]{2,1,0:T(8,128)S(1)}, u32[]{:S(2)}, u32[]{:S(2)}) collective-permute-start(f32[4,16,512]{2,1,0:T(8,128)S(1)} %get-tuple-element.30), channel_id=1, source_target_pairs={{0,3},{1,2},{2,1},{3,0},{4,7},{5,6},{6,5},{7,4},{8,11},{9,10},{10,... | collective-permute-start | bytes 393224 | tf_op jit(solution)/shard_map/ppermute | solution.py:242
  34.6 0.5 %collective-permute-start.10 = (f32[4,16,512]{2,1,0:T(8,128)S(1)}, f32[4,16,512]{2,1,0:T(8,128)S(1)}, u32[]{:S(2)}, u32[]{:S(2)}) collective-permute-start(f32[4,16,512]{2,1,0:T(8,128)S(1)} %get-tuple-element.30), channel_id=1, source_target_pairs={{0,2},{2,0},{4,6},{6,4},{8,10},{10,8},{12,14},{14,12},{1,3},{3,1},... | collective-permute-start | bytes 393224 | tf_op jit(solution)/shard_map/ppermute | solution.py:246
  35.1 3.3 %collective-permute-done.11.both_ref = f32[4,16,512]{2,1,0:T(8,128)S(1)} collective-permute-done((f32[4,16,512]{2,1,0:T(8,128)S(1)}, f32[4,16,512]{2,1,0:T(8,128)S(1)}, u32[]{:S(2)}, u32[]{:S(2)}) %collective-permute-start.11) | collective-permute-done | bytes 131104 | tf_op jit(solution)/shard_map/ppermute | solution.py:242
  38.5 3.2 %collective-permute-done.10.column_ref = f32[4,16,512]{2,1,0:T(8,128)S(1)} collective-permute-done((f32[4,16,512]{2,1,0:T(8,128)S(1)}, f32[4,16,512]{2,1,0:T(8,128)S(1)}, u32[]{:S(2)}, u32[]{:S(2)}) %collective-permute-start.10) | collective-permute-done | bytes 131104 | tf_op jit(solution)/shard_map/ppermute | solution.py:246
  41.7 2.9 %make_output.1 = bf16[4,256,512]{2,1,0:T(8,128)(2,1)} custom-call(s32[1]{0:T(128)} %bitcast.place_ref, bf16[4,256,512]{2,1,0:T(8,128)(2,1)S(1)} %copy-done.1, bf16[2,2,256,384]{3,2,1,0:T(8,128)(2,1)S(1)} %copy-done.3, bf16[64,64]{1,0:T(8,128)(2,1)S(1)} %copy-done.8, f32[64]{0:T(128)S(1)} %copy-done.9, f32[4,16,512]{2,1,0:T(8,128)S(1)} %get-tuple-element.29.own_ref, ...), custom_call_target="tpu_custom_call" | custom-call | tf_op jit(solution)/shard_map/make_output/pallas_call | solution.py:422
  (29 shorter events, 0.1 us)
Async XLA Ops:
  1.1 1.2 %copy-start = (bf16[4,256,512]{2,1,0:T(8,128)(2,1)S(1)}, bf16[4,256,512]{2,1,0:T(8,128)(2,1)}, u32[]{:S(2)}) copy-start(bf16[4,256,512]{2,1,0:T(8,128)(2,1)} %flow_ref.3) | copy-start | bytes 3145732
  2.3 20.0 %copy-start.2 = (bf16[1,64,64,128]{3,2,1,0:T(8,128)(2,1)S(1)}, bf16[1,64,64,128]{3,2,1,0:T(8,128)(2,1)}, u32[]{:S(2)}) copy-start(bf16[1,64,64,128]{3,2,1,0:T(8,128)(2,1)} %refs_4_.1) | copy-start | bytes 3145732
  2.3 20.0 %copy-start.4 = (bf16[128,128]{1,0:T(8,128)(2,1)S(1)}, bf16[128,128]{1,0:T(8,128)(2,1)}, u32[]{:S(2)}) copy-start(bf16[128,128]{1,0:T(8,128)(2,1)} %constant.145.clone.refs_8_) | copy-start | bytes 98308
  2.3 20.0 %copy-start.5 = (bf16[128,128]{1,0:T(8,128)(2,1)S(1)}, bf16[128,128]{1,0:T(8,128)(2,1)}, u32[]{:S(2)}) copy-start(bf16[128,128]{1,0:T(8,128)(2,1)} %constant.144.clone.refs_7_) | copy-start | bytes 98308
  2.3 20.0 %copy-start.6 = (bf16[128,128]{1,0:T(8,128)(2,1)S(1)}, bf16[128,128]{1,0:T(8,128)(2,1)}, u32[]{:S(2)}) copy-start(bf16[128,128]{1,0:T(8,128)(2,1)} %constant.143.clone.refs_6_) | copy-start | bytes 98308
  2.3 20.0 %copy-start.7 = (bf16[128,128]{1,0:T(8,128)(2,1)S(1)}, bf16[128,128]{1,0:T(8,128)(2,1)}, u32[]{:S(2)}) copy-start(bf16[128,128]{1,0:T(8,128)(2,1)} %constant.142.clone.refs_5_) | copy-start | bytes 98308
  2.6 6.3 %collective-permute-start = (f32[4,16,512]{2,1,0:T(8,128)S(1)}, f32[4,16,512]{2,1,0:T(8,128)S(1)}, u32[]{:S(2)}, u32[]{:S(2)}) collective-permute-start(f32[4,16,512]{2,1,0:T(8,128)S(1)} %get-tuple-element.17), channel_id=1, source_target_pairs={{0,3},{1,2},{2,1},{3,0},{4,7},{5,6},{6,5},{7,4},{8,11},{9,10},{10,... | collective-permute-start | bytes 393224 | tf_op jit(solution)/shard_map/ppermute | solution.py:242
  5.1 6.9 %collective-permute-start.1 = (f32[4,16,512]{2,1,0:T(8,128)S(1)}, f32[4,16,512]{2,1,0:T(8,128)S(1)}, u32[]{:S(2)}, u32[]{:S(2)}) collective-permute-start(f32[4,16,512]{2,1,0:T(8,128)S(1)} %get-tuple-element.18), channel_id=1, source_target_pairs={{0,2},{2,0},{4,6},{6,4},{8,10},{10,8},{12,14},{14,12},{1,3},{3,1},... | collective-permute-start | bytes 393224 | tf_op jit(solution)/shard_map/ppermute | solution.py:246
  5.7 6.2 %collective-permute-start.2 = (f32[4,16,512]{2,1,0:T(8,128)S(1)}, f32[4,16,512]{2,1,0:T(8,128)S(1)}, u32[]{:S(2)}, u32[]{:S(2)}) collective-permute-start(f32[4,16,512]{2,1,0:T(8,128)S(1)} %get-tuple-element.19), channel_id=1, source_target_pairs={{0,1},{1,0},{2,3},{3,2},{4,5},{5,4},{6,7},{7,6},{8,9},{9,8},{10,11... | collective-permute-start | bytes 393224 | tf_op jit(solution)/shard_map/ppermute | solution.py:250
  11.9 29.7 %copy-start.1 = (bf16[4,256,512]{2,1,0:T(8,128)(2,1)S(1)}, bf16[4,256,512]{2,1,0:T(8,128)(2,1)}, u32[]{:S(2)}) copy-start(bf16[4,256,512]{2,1,0:T(8,128)(2,1)} %flow_ref.3) | copy-start | bytes 3145732
  12.0 7.0 %collective-permute-start.3 = (f32[2,16,512]{2,1,0:T(8,128)S(1)}, f32[2,16,512]{2,1,0:T(8,128)S(1)}, u32[]{:S(2)}, u32[]{:S(2)}) collective-permute-start(f32[2,16,512]{2,1,0:T(8,128)S(1)} %get-tuple-element.21), channel_id=1, source_target_pairs={{0,12},{2,14},{4,8},{6,10},{8,4},{10,6},{12,0},{14,2},{1,13},{3,15... | collective-permute-start | bytes 196616 | tf_op jit(solution)/shard_map/ppermute | solution.py:257
  16.5 5.8 %collective-permute-start.4 = (f32[2,16,512]{2,1,0:T(8,128)S(1)}, f32[2,16,512]{2,1,0:T(8,128)S(1)}, u32[]{:S(2)}, u32[]{:S(2)}) collective-permute-start(f32[2,16,512]{2,1,0:T(8,128)S(1)} %get-tuple-element.22), channel_id=1, source_target_pairs={{0,8},{2,10},{4,12},{6,14},{8,0},{10,2},{12,4},{14,6},{1,9},{3,11}... | collective-permute-start | bytes 196616 | tf_op jit(solution)/shard_map/ppermute | solution.py:257
  16.5 5.8 %collective-permute-start.5 = (f32[2,16,512]{2,1,0:T(8,128)S(1)}, f32[2,16,512]{2,1,0:T(8,128)S(1)}, u32[]{:S(2)}, u32[]{:S(2)}) collective-permute-start(f32[2,16,512]{2,1,0:T(8,128)S(1)} %get-tuple-element.23), channel_id=1, source_target_pairs={{0,4},{2,6},{4,0},{6,2},{8,12},{10,14},{12,8},{14,10},{1,5},{3,7},... | collective-permute-start | bytes 196616 | tf_op jit(solution)/shard_map/ppermute | solution.py:257
  22.3 19.4 %copy-start.3 = (bf16[2,2,256,384]{3,2,1,0:T(8,128)(2,1)S(1)}, bf16[2,2,256,384]{3,2,1,0:T(8,128)(2,1)}, u32[]{:S(2)}) copy-start(bf16[2,2,256,384]{3,2,1,0:T(8,128)(2,1)} %constant.146.clone.table_ref) | copy-start | bytes 2359300
  23.9 6.3 %collective-permute-start.6 = (f32[2,16,512]{2,1,0:T(8,128)S(1)}, f32[2,16,512]{2,1,0:T(8,128)S(1)}, u32[]{:S(2)}, u32[]{:S(2)}) collective-permute-start(f32[2,16,512]{2,1,0:T(8,128)S(1)} %get-tuple-element.25), channel_id=1, source_target_pairs={{0,12},{2,14},{4,8},{6,10},{8,4},{10,6},{12,0},{14,2},{1,13},{3,15... | collective-permute-start | bytes 196616 | tf_op jit(solution)/shard_map/ppermute | solution.py:257
  26.4 6.4 %collective-permute-start.7 = (f32[2,16,512]{2,1,0:T(8,128)S(1)}, f32[2,16,512]{2,1,0:T(8,128)S(1)}, u32[]{:S(2)}, u32[]{:S(2)}) collective-permute-start(f32[2,16,512]{2,1,0:T(8,128)S(1)} %get-tuple-element.26), channel_id=1, source_target_pairs={{0,8},{2,10},{4,12},{6,14},{8,0},{10,2},{12,4},{14,6},{1,9},{3,11}... | collective-permute-start | bytes 196616 | tf_op jit(solution)/shard_map/ppermute | solution.py:257
  26.4 6.4 %collective-permute-start.8 = (f32[2,16,512]{2,1,0:T(8,128)S(1)}, f32[2,16,512]{2,1,0:T(8,128)S(1)}, u32[]{:S(2)}, u32[]{:S(2)}) collective-permute-start(f32[2,16,512]{2,1,0:T(8,128)S(1)} %get-tuple-element.27), channel_id=1, source_target_pairs={{0,4},{2,6},{4,0},{6,2},{8,12},{10,14},{12,8},{14,10},{1,5},{3,7},... | collective-permute-start | bytes 196616 | tf_op jit(solution)/shard_map/ppermute | solution.py:257
  32.9 8.8 %copy-start.8 = (bf16[64,64]{1,0:T(8,128)(2,1)S(1)}, bf16[64,64]{1,0:T(8,128)(2,1)}, u32[]{:S(2)}) copy-start(bf16[64,64]{1,0:T(8,128)(2,1)} %local_ref.1) | copy-start | bytes 24580
  32.9 2.2 %collective-permute-start.9 = (f32[4,16,512]{2,1,0:T(8,128)S(1)}, f32[4,16,512]{2,1,0:T(8,128)S(1)}, u32[]{:S(2)}, u32[]{:S(2)}) collective-permute-start(f32[4,16,512]{2,1,0:T(8,128)S(1)} %get-tuple-element.29.own_ref), channel_id=1, source_target_pairs={{0,1},{1,0},{2,3},{3,2},{4,5},{5,4},{6,7},{7,6},{8,9},{9,8},{10,11... | collective-permute-start | bytes 393224 | tf_op jit(solution)/shard_map/ppermute | solution.py:250
  33.0 8.7 %copy-start.9 = (f32[64]{0:T(128)S(1)}, f32[64]{0:T(128)}, u32[]{:S(2)}) copy-start(f32[64]{0:T(128)} %bias_ref.1) | copy-start | bytes 772
  33.0 5.5 %collective-permute-start.11 = (f32[4,16,512]{2,1,0:T(8,128)S(1)}, f32[4,16,512]{2,1,0:T(8,128)S(1)}, u32[]{:S(2)}, u32[]{:S(2)}) collective-permute-start(f32[4,16,512]{2,1,0:T(8,128)S(1)} %get-tuple-element.30), channel_id=1, source_target_pairs={{0,3},{1,2},{2,1},{3,0},{4,7},{5,6},{6,5},{7,4},{8,11},{9,10},{10,... | collective-permute-start | bytes 393224 | tf_op jit(solution)/shard_map/ppermute | solution.py:242
  34.6 7.0 %collective-permute-start.10 = (f32[4,16,512]{2,1,0:T(8,128)S(1)}, f32[4,16,512]{2,1,0:T(8,128)S(1)}, u32[]{:S(2)}, u32[]{:S(2)}) collective-permute-start(f32[4,16,512]{2,1,0:T(8,128)S(1)} %get-tuple-element.30), channel_id=1, source_target_pairs={{0,2},{2,0},{4,6},{6,4},{8,10},{10,8},{12,14},{14,12},{1,3},{3,1},... | collective-permute-start | bytes 393224 | tf_op jit(solution)/shard_map/ppermute | solution.py:246

commit v7 on v6

--- a/solution.py
+++ b/solution.py
@@ -163,9 +163,11 @@
     layers = peers // 2
     row = jnp.arange(2 * MY, dtype=jnp.int32)
     block = row // (2 * rows_ky)
-    turn = layers - 1 - block % layers
-    owner = (z ^ turn) * 2 + (x ^ (1 - block // layers % 2))
-    owner = (y ^ (1 - block // peers)) * peers + owner
+    turn = layers - 1 - block // 2 % layers
+    side = y ^ (1 - block // peers)
+    column = x ^ side
+    half = side ^ (block % 2)
+    owner = half * peers + (z ^ turn) * 2 + column
     index = owner * rows_ky + row // 2 % rows_ky
     y_places = y * cells_y + jnp.arange(cells_y, dtype=jnp.int32)
     angle = phase_table(wave_number(index, MY), y_places, cells_y * groups_y)
@@ -216,87 +218,99 @@
     return jnp.dot(left, right, preferred_element_type=jnp.float32)
 
 
-def forward_y_kernel(flow_ref, table_ref, *out_refs):
-    layers, rows, feat_count = out_refs[0].shape
+def forward_y_kernel(flow_ref, table_ref, send_ref, keep_ref):
+    layers, _, rows, feat_count = send_ref.shape
     cells_x = flow_ref.shape[0]
     rows = rows // cells_x
     for x in range(cells_x):
-        result = dot(table_ref[...], flow_ref[x]).reshape(4, layers, rows, feat_count)
-        for part, out_ref in enumerate(out_refs):
-            out_ref[:, x * rows : (x + 1) * rows, :] = result[part]
+        result = dot(table_ref[...], flow_ref[x]).reshape(2, layers, 2, rows, feat_count)
+        send_ref[:, :, x * rows : (x + 1) * rows, :] = result[0]
+        keep_ref[:, :, x * rows : (x + 1) * rows, :] = result[1]
 
 
 def forward_y(flow_field, table, layers, rows_ky):
     cells_x, _, feat_count = flow_field.shape
-    shape = jax.ShapeDtypeStruct((layers, cells_x * 2 * rows_ky, feat_count), jnp.float32)
+    shape = jax.ShapeDtypeStruct((layers, 2, cells_x * 2 * rows_ky, feat_count), jnp.float32)
     return pl.pallas_call(
         forward_y_kernel,
-        out_shape=[shape] * 4,
+        out_shape=[shape] * 2,
         compiler_params=SMALL,
         name="forward_y",
     )(flow_field, table)
 
 
-def flip_both(block, peers):
-    pairs = [(place, place ^ 3) for place in range(2 * peers)]
-    return lax.ppermute(block, ("gx", "gy"), pairs)
-
-
-def flip_column(block, peers):
-    return lax.ppermute(block, "gx", [(place, place ^ 1) for place in range(peers)])
-
-
 def flip_core(block):
     return lax.ppermute(block, "gy", [(0, 1), (1, 0)])
 
 
-def along_z(blocks, peers):
+def along_columns(blocks, peers):
     arrived = []
     for turn, block in zip(turns(len(blocks)), blocks):
-        pairs = [(place, place ^ (2 * turn)) for place in range(peers)]
-        arrived.append(lax.ppermute(block, "gx", pairs) if turn else block)
+        pairs = [
+            (2 * place + core, 2 * (place ^ (2 * turn + core)) + core)
+            for place in range(peers)
+            for core in range(2)
+        ]
+        arrived.append(lax.ppermute(block, ("gx", "gy"), pairs))
     return arrived
 
 
-def combine_kernel(both_ref, column_ref, core_ref, own_ref, *out_refs):
+def small_call(kernel, out_shape, name):
+    return pl.pallas_call(kernel, out_shape=out_shape, compiler_params=SMALL, name=name)
+
+
+def add_kernel(keep_ref, arrived_ref, *out_refs):
     for turn, out_ref in enumerate(out_refs):
-        out_ref[0] = own_ref[turn] + core_ref[turn]
-        out_ref[1] = column_ref[turn] + both_ref[turn]
-
-
-def combine(both, column, core, own):
-    return pl.pallas_call(
-        combine_kernel,
-        out_shape=[jax.ShapeDtypeStruct((2,) + own.shape[1:], own.dtype)] * own.shape[0],
-        compiler_params=SMALL,
-        name="combine",
-    )(both, column, core, own)
-
-
-def gather_kernel(*refs):
-    for turn, block_ref in enumerate(refs[:-2]):
-        refs[-2][turn] = block_ref[0]
+        out_ref[...] = keep_ref[turn] + arrived_ref[turn]
+
+
+def add_blocks(keep, arrived):
+    shape = jax.ShapeDtypeStruct(keep.shape[1:], keep.dtype)
+    return small_call(add_kernel, [shape] * keep.shape[0], "add_blocks")(keep, arrived)
+
+
+def join_kernel(keep_ref, arrived_ref, *out_refs):
+    for turn, out_ref in enumerate(out_refs):
+        out_ref[0] = keep_ref[turn]
+        out_ref[1] = arrived_ref[turn]
+
+
+def join_blocks(keep, arrived):
+    shape = jax.ShapeDtypeStruct((2,) + keep.shape[1:], keep.dtype)
+    return small_call(join_kernel, [shape] * keep.shape[0], "join_blocks")(keep, arrived)
+
+
+def second_kernel(*refs):
+    for turn, block_ref in enumerate(refs[:-1]):
         refs[-1][turn] = block_ref[1]
 
 
-def gather(blocks):
+def second_halves(blocks):
     shape = jax.ShapeDtypeStruct((len(blocks),) + blocks[0].shape[1:], blocks[0].dtype)
-    return pl.pallas_call(
-        gather_kernel, out_shape=[shape] * 2, compiler_params=SMALL, name="gather"
-    )(*blocks)
+    return small_call(second_kernel, shape, "second_halves")(*blocks)
+
+
+def stack_kernel(*refs):
+    for turn, block_ref in enumerate(refs[:-1]):
+        refs[-1][turn] = block_ref[...]
+
+
+def stack_blocks(blocks):
+    shape = jax.ShapeDtypeStruct((len(blocks),) + blocks[0].shape, blocks[0].dtype)
+    return small_call(stack_kernel, shape, "stack_blocks")(*blocks)
 
 
 def mix_kernel(layers, *refs):
     block_refs = refs[:layers]
-    weight_ref, forward_high, forward_low, inverse_high, inverse_low, mixed_ref = refs[
+    arrived_ref, weight_ref, forward_high, forward_low, inverse_high, inverse_low = refs[
         layers : layers + 6
     ]
-    back_refs = refs[layers + 6 : 2 * layers + 6]
-    order_ref, spread_ref, result_ref = refs[2 * layers + 6 :]
-    z, x, _ = quad()
-    for turn, block_ref in zip(turns(layers), block_refs):
-        for side in range(2):
-            order_ref[(z ^ turn) * 2 + (x ^ side)] = block_ref[side]
+    mixed_ref, send_ref, keep_ref, order_ref, spread_ref, result_ref = refs[layers + 6 :]
+    z, x, y = quad()
+    column = x ^ y
+    for index, turn in enumerate(turns(layers)):
+        order_ref[(z ^ turn) * 2 + column] = block_refs[index][0]
+        order_ref[(z ^ turn) * 2 + (column ^ 1)] = arrived_ref[index]
     feat_count = order_ref.shape[-1]
     count = weight_ref.shape[1]
     channels = weight_ref.shape[2]
@@ -348,29 +362,27 @@
     high, low = split_terms(jnp.concatenate(parts, axis=0))
     back = dot(inverse_high[...], high) + dot(inverse_high[...], low) + dot(inverse_low[...], high)
     order_ref[...] = back.reshape(order_ref.shape)
-    for turn, back_ref in zip(turns(layers), back_refs):
-        for side in range(2):
-            back_ref[side] = order_ref[(z ^ turn) * 2 + (x ^ side)]
-
-
-def mix(blocks, weights, forward_table, inverse_table):
-    _, rows, feat_count = blocks[0].shape
-    layers = len(blocks)
+    for index, turn in enumerate(turns(layers)):
+        send_ref[index] = order_ref[(z ^ turn) * 2 + (column ^ 1)]
+        keep_ref[index] = order_ref[(z ^ turn) * 2 + column]
+
+
+def mix(blocks, arrived, weights, forward_table, inverse_table):
+    layers, rows, feat_count = arrived.shape
     count = weights.shape[1]
     scratch = pltpu.VMEM((count * feat_count // 64, 128), jnp.float32)
-    mixed, *back = pl.pallas_call(
+    return pl.pallas_call(
         functools.partial(mix_kernel, layers),
         out_shape=[jax.ShapeDtypeStruct((1, count, 2 * feat_count), jnp.float32)]
-        + [jax.ShapeDtypeStruct(blocks[0].shape, jnp.float32)] * layers,
+        + [jax.ShapeDtypeStruct(arrived.shape, jnp.float32)] * 2,
         scratch_shapes=[pltpu.VMEM((2 * layers, rows, feat_count), jnp.float32), scratch, scratch],
         compiler_params=SMALL,
         name="mix",
-    )(*blocks, weights, *split_table(forward_table), *split_table(inverse_table))
-    return mixed, back
+    )(*blocks, arrived, weights, *split_table(forward_table), *split_table(inverse_table))
 
 
 def output_kernel(
-    place_ref, flow_ref, table_ref, local_ref, bias_ref, own_ref, core_ref, column_ref, both_ref,
+    place_ref, flow_ref, table_ref, local_ref, bias_ref, own_ref, core_ref,
     out_ref, order_ref, stack_ref, wide_ref, level_ref,
 ):
     step = pl.program_id(0)
@@ -379,17 +391,16 @@
     width = wide_ref.shape[0]
     pairs = stack_ref.shape[0]
     layers = own_ref.shape[0]
-    rows = own_ref.shape[1] // pairs
+    rows = own_ref.shape[2] // pairs
 
     @pl.when(step == 0)
     def _():
-        z, x, _ = quad()
+        z, x, y = quad()
         for index, turn in enumerate(turns(layers)):
-            peer = (z ^ turn) * 2
-            order_ref[peer + x] = own_ref[index]
-            order_ref[peer + (x ^ 1)] = column_ref[index]
-            order_ref[2 * layers + peer + x] = core_ref[index]
-            order_ref[2 * layers + peer + (x ^ 1)] = both_ref[index]
+            for side in range(2):
+                peer = 2 * layers * side + (z ^ turn) * 2
+                order_ref[peer + (x ^ y)] = own_ref[index, side]
+                order_ref[peer + (x ^ y ^ 1)] = core_ref[index, 1 - side]
         for pair in range(pairs):
             span = slice(pair * rows, (pair + 1) * rows)
             high, low = split_terms(order_ref[:, span, :].reshape(-1, feat_count))
@@ -415,7 +426,7 @@
 
 def make_output(flow_field, parts, table, local, bias):
     cells_x, cells_y, feat_count = flow_field.shape
-    layers, rows, _ = parts[0].shape
+    layers, _, rows, _ = parts[0].shape
     place = jnp.reshape(lax.axis_index("gy"), (1,))
     whole = lambda array: pl.BlockSpec(array.shape, lambda i, p: (0,) * array.ndim)
     block = pl.BlockSpec((1, cells_y, feat_count), lambda i, p: (i, 0, 0))
@@ -454,16 +465,17 @@
     inverse_scale = 1.0 / math.sqrt(MX * MY)
 
     table = forward_y_table(cells_y, groups_y, peers, rows_ky)
-    both, core, column, own = forward_y(flow_field, table, peers // 2, rows_ky)
-    blocks = combine(flip_both(both, peers), flip_column(column, peers), flip_core(core), own)
-    mixed, back = mix(
-        along_z(blocks, peers),
+    send, keep = forward_y(flow_field, table, peers // 2, rows_ky)
+    blocks = along_columns(add_blocks(keep, flip_core(send)), peers)
+    mixed, send, keep = mix(
+        blocks,
+        flip_core(second_halves(blocks)),
         spectral_weight,
         forward_x_table(cells_x, peers, rows_ky) * forward_scale,
         inverse_x_table(cells_x, peers, rows_ky),
     )
-    own, column = gather(along_z(back, peers))
-    parts = [own, flip_core(own), flip_column(column, peers), flip_both(column, peers)]
+    own = stack_blocks(along_columns(join_blocks(keep, flip_core(send)), peers))
+    parts = [own, flip_core(own)]
     high, low = split_table(inverse_y_table(cells_y, groups_y, peers, rows_ky) * inverse_scale)
     table = np.concatenate([high, high, low], axis=-1)
     return make_output(flow_field, parts, table, local_weight, bias_terms), mixed

time: 44.8 us -> 35.5 us (0.79)
  waiting for transfers between devices: 22.5 us -> 14 us
  starting transfers between devices: 14.8 us -> 14 us
    ppermute x10 -> x8, waiting for transfers between devices: 22.5 us -> 9.69 us  [along_columns(): arrived.append(lax.ppermute(block, ('gx', 'gy'), pairs))]
    ppermute x2 -> x4, waiting for transfers between devices: 0.01 us -> 4.3 us  [flip_core(): return lax.ppermute(block, 'gy', [(0, 1), (1, 0)])]
    ppermute x10 -> x8, starting transfers between devices: 14.7 us -> 11.6 us  [along_columns(): arrived.append(lax.ppermute(block, ('gx', 'gy'), pairs))]
    ppermute x2 -> x4, starting transfers between devices: 0.11 us -> 2.4 us  [flip_core(): return lax.ppermute(block, 'gy', [(0, 1), (1, 0)])]
  transfers between devices with their start and end apart: 12 -> 12, of which waited for: 8 -> 9; matrix products, arithmetic and copies ran while one was open for 0% -> 0% of each run, Pallas kernels for 0% -> 0%
where the time goes in v7:
time: 35.5 us; the launch traced here: 35.2 us
  starting transfers between devices  14 us (39%)
  waiting for transfers between devices  14 us (39%)
  Pallas kernels  4.84 us (14%)
  local copies, waits for them, and re-layouts  1.26 us (4%)
  between operations  0.8 us (2%)
  other arithmetic  0.38 us (1%)
    ppermute x8, starting transfers between devices, along_columns(): arrived.append(lax.ppermute(block, ('gx', 'gy'), pairs))  11.6 us
    ppermute x8, waiting for transfers between devices, along_columns(): arrived.append(lax.ppermute(block, ('gx', 'gy'), pairs))  9.69 us
    ppermute x4, waiting for transfers between devices, flip_core(): return lax.ppermute(block, 'gy', [(0, 1), (1, 0)])  4.3 us
    pallas_call x1, Pallas kernels, make_output(): pl.pallas_call(output_kernel, grid_spec=pltpu.PrefetchScalarGridSpec(num_...  2.9 us
    ppermute x4, starting transfers between devices, flip_core(): return lax.ppermute(block, 'gy', [(0, 1), (1, 0)])  2.4 us
    pallas_call x1, Pallas kernels, mix(): pl.pallas_call(functools.partial(mix_kernel, layers), out_shape=[jax.Shap...  1.57 us
    unnamed x20, local copies, waits for them, and re-layouts  1.26 us
  transfers between devices with their start and end apart: 12, of which 9 were waited for; matrix products, arithmetic and copies ran while one was open for 0% of the time, Pallas kernels for 0%

profile of v7, /device:TPU:0, one launch (start us, length us, event | category | flops | bytes accessed | tf_op | source)
XLA Modules:
  0.0 35.2 jit_solution(3171636386545098811)
XLA Ops:
  0.7 0.3 select_convert_fusion.table_ref
  1.1 1.2 %copy-done = bf16[4,256,512]{2,1,0:T(8,128)(2,1)S(1)} copy-done((bf16[4,256,512]{2,1,0:T(8,128)(2,1)S(1)}, bf16[4,256,512]{2,1,0:T(8,128)(2,1)}, u32[]{:S(2)}) %copy-start) | copy-done | bytes 1048600
  2.3 0.3 forward_y.1
  2.6 0.5 %collective-permute-start = (f32[4,2,16,512]{3,2,1,0:T(8,128)S(1)}, f32[4,2,16,512]{3,2,1,0:T(8,128)S(1)}, u32[]{:S(2)}, u32[]{:S(2)}) collective-permute-start(f32[4,2,16,512]{3,2,1,0:T(8,128)S(1)} %get-tuple-element.16), channel_id=1, source_target_pairs={{0,1},{1,0},{2,3},{3,2},{4,5},{5,4},{6,7},{7,6},{8,9},{9,8},{10,11... | collective-permute-start | bytes 786440 | tf_op jit(solution)/shard_map/ppermute | solution.py:243
  3.1 1.2 %collective-permute-done.arrived_ref = f32[4,2,16,512]{3,2,1,0:T(8,128)S(1)} collective-permute-done((f32[4,2,16,512]{3,2,1,0:T(8,128)S(1)}, f32[4,2,16,512]{3,2,1,0:T(8,128)S(1)}, u32[]{:S(2)}, u32[]{:S(2)}) %collective-permute-start) | collective-permute-done | bytes 262176 | tf_op jit(solution)/shard_map/ppermute | solution.py:243
  4.3 5.0 %collective-permute-start.1 = (f32[2,16,512]{2,1,0:T(8,128)S(1)}, f32[2,16,512]{2,1,0:T(8,128)S(1)}, u32[]{:S(2)}, u32[]{:S(2)}) collective-permute-start(f32[2,16,512]{2,1,0:T(8,128)S(1)} %get-tuple-element.17), channel_id=1, source_target_pairs={{0,12},{1,15},{2,14},{3,13},{4,8},{5,11},{6,10},{7,9},{8,4},{9,7},... | collective-permute-start | bytes 196616 | tf_op jit(solution)/shard_map/ppermute | solution.py:254
  9.4 0.6 %collective-permute-start.3 = (f32[2,16,512]{2,1,0:T(8,128)S(1)}, f32[2,16,512]{2,1,0:T(8,128)S(1)}, u32[]{:S(2)}, u32[]{:S(2)}) collective-permute-start(f32[2,16,512]{2,1,0:T(8,128)S(1)} %get-tuple-element.19), channel_id=1, source_target_pairs={{0,4},{1,7},{2,6},{3,5},{4,0},{5,3},{6,2},{7,1},{8,12},{9,15},{10,... | collective-permute-start | bytes 196616 | tf_op jit(solution)/shard_map/ppermute | solution.py:254
  10.0 0.8 %collective-permute-start.4 = (f32[2,16,512]{2,1,0:T(8,128)S(1)}, f32[2,16,512]{2,1,0:T(8,128)S(1)}, u32[]{:S(2)}, u32[]{:S(2)}) collective-permute-start(f32[2,16,512]{2,1,0:T(8,128)S(1)} %get-tuple-element.20), channel_id=1, source_target_pairs={{0,0},{1,3},{2,2},{3,1},{4,4},{5,7},{6,6},{7,5},{8,8},{9,11},{10,1... | collective-permute-start | bytes 196616 | tf_op jit(solution)/shard_map/ppermute | solution.py:254
  10.8 1.3 %collective-permute-done.1.refs_0_ = f32[2,16,512]{2,1,0:T(8,128)S(1)} collective-permute-done((f32[2,16,512]{2,1,0:T(8,128)S(1)}, f32[2,16,512]{2,1,0:T(8,128)S(1)}, u32[]{:S(2)}, u32[]{:S(2)}) %collective-permute-start.1) | collective-permute-done | bytes 65568 | tf_op jit(solution)/shard_map/ppermute | solution.py:254
  12.1 3.8 %collective-permute-done.2.refs_1_ = f32[2,16,512]{2,1,0:T(8,128)S(1)} collective-permute-done((f32[2,16,512]{2,1,0:T(8,128)S(1)}, f32[2,16,512]{2,1,0:T(8,128)S(1)}, u32[]{:S(2)}, u32[]{:S(2)}) %collective-permute-start.2) | collective-permute-done | bytes 65568 | tf_op jit(solution)/shard_map/ppermute | solution.py:254
  15.9 0.9 %collective-permute-start.5 = (f32[4,16,512]{2,1,0:T(8,128)S(1)}, f32[4,16,512]{2,1,0:T(8,128)S(1)}, u32[]{:S(2)}, u32[]{:S(2)}) collective-permute-start(f32[4,16,512]{2,1,0:T(8,128)S(1)} %second_halves.1), channel_id=1, source_target_pairs={{0,1},{1,0},{2,3},{3,2},{4,5},{5,4},{6,7},{7,6},{8,9},{9,8},{10,11... | collective-permute-start | bytes 393224 | tf_op jit(solution)/shard_map/ppermute | solution.py:243
  16.8 1.0 %collective-permute-done.5.refs_4_ = f32[4,16,512]{2,1,0:T(8,128)S(1)} collective-permute-done((f32[4,16,512]{2,1,0:T(8,128)S(1)}, f32[4,16,512]{2,1,0:T(8,128)S(1)}, u32[]{:S(2)}, u32[]{:S(2)}) %collective-permute-start.5) | collective-permute-done | bytes 131104 | tf_op jit(solution)/shard_map/ppermute | solution.py:243
  17.8 1.6 %mix.1 = (f32[1,64,1024]{2,1,0:T(8,128)}, f32[4,16,512]{2,1,0:T(8,128)S(1)}, f32[4,16,512]{2,1,0:T(8,128)S(1)}) custom-call(f32[2,16,512]{2,1,0:T(8,128)S(1)} %collective-permute-done.1.refs_0_, f32[2,16,512]{2,1,0:T(8,128)S(1)} %collective-permute-done.2.refs_1_, f32[2,16,512]{2,1,0:T(8,128)S(1)} %collective-permute-done.3.refs_2_, ...), custom_call_target="tpu_custom_call" | custom-call | tf_op jit(solution)/shard_map/mix/pallas_call | solution.py:374
  19.4 0.4 %collective-permute-start.6 = (f32[4,16,512]{2,1,0:T(8,128)S(1)}, f32[4,16,512]{2,1,0:T(8,128)S(1)}, u32[]{:S(2)}, u32[]{:S(2)}) collective-permute-start(f32[4,16,512]{2,1,0:T(8,128)S(1)} %get-tuple-element.22), channel_id=1, source_target_pairs={{0,1},{1,0},{2,3},{3,2},{4,5},{5,4},{6,7},{7,6},{8,9},{9,8},{10,11... | collective-permute-start | bytes 393224 | tf_op jit(solution)/shard_map/ppermute | solution.py:243
  19.7 1.0 %collective-permute-done.6.arrived_ref = f32[4,16,512]{2,1,0:T(8,128)S(1)} collective-permute-done((f32[4,16,512]{2,1,0:T(8,128)S(1)}, f32[4,16,512]{2,1,0:T(8,128)S(1)}, u32[]{:S(2)}, u32[]{:S(2)}) %collective-permute-start.6) | collective-permute-done | bytes 131104 | tf_op jit(solution)/shard_map/ppermute | solution.py:243
  20.7 3.4 %collective-permute-start.7 = (f32[2,16,512]{2,1,0:T(8,128)S(1)}, f32[2,16,512]{2,1,0:T(8,128)S(1)}, u32[]{:S(2)}, u32[]{:S(2)}) collective-permute-start(f32[2,16,512]{2,1,0:T(8,128)S(1)} %get-tuple-element.23), channel_id=1, source_target_pairs={{0,12},{1,15},{2,14},{3,13},{4,8},{5,11},{6,10},{7,9},{8,4},{9,7},... | collective-permute-start | bytes 196616 | tf_op jit(solution)/shard_map/ppermute | solution.py:254
  24.1 1.0 %collective-permute-start.9 = (f32[2,16,512]{2,1,0:T(8,128)S(1)}, f32[2,16,512]{2,1,0:T(8,128)S(1)}, u32[]{:S(2)}, u32[]{:S(2)}) collective-permute-start(f32[2,16,512]{2,1,0:T(8,128)S(1)} %get-tuple-element.25), channel_id=1, source_target_pairs={{0,4},{1,7},{2,6},{3,5},{4,0},{5,3},{6,2},{7,1},{8,12},{9,15},{10,... | collective-permute-start | bytes 196616 | tf_op jit(solution)/shard_map/ppermute | solution.py:254
  25.2 0.7 %collective-permute-start.10 = (f32[2,16,512]{2,1,0:T(8,128)S(1)}, f32[2,16,512]{2,1,0:T(8,128)S(1)}, u32[]{:S(2)}, u32[]{:S(2)}) collective-permute-start(f32[2,16,512]{2,1,0:T(8,128)S(1)} %get-tuple-element.26), channel_id=1, source_target_pairs={{0,0},{1,3},{2,2},{3,1},{4,4},{5,7},{6,6},{7,5},{8,8},{9,11},{10,1... | collective-permute-start | bytes 196616 | tf_op jit(solution)/shard_map/ppermute | solution.py:254
  25.9 1.8 %collective-permute-done.7.refs_0_ = f32[2,16,512]{2,1,0:T(8,128)S(1)} collective-permute-done((f32[2,16,512]{2,1,0:T(8,128)S(1)}, f32[2,16,512]{2,1,0:T(8,128)S(1)}, u32[]{:S(2)}, u32[]{:S(2)}) %collective-permute-start.7) | collective-permute-done | bytes 65568 | tf_op jit(solution)/shard_map/ppermute | solution.py:254
  27.6 2.6 %collective-permute-done.8.refs_1_ = f32[2,16,512]{2,1,0:T(8,128)S(1)} collective-permute-done((f32[2,16,512]{2,1,0:T(8,128)S(1)}, f32[2,16,512]{2,1,0:T(8,128)S(1)}, u32[]{:S(2)}, u32[]{:S(2)}) %collective-permute-start.8) | collective-permute-done | bytes 65568 | tf_op jit(solution)/shard_map/ppermute | solution.py:254
  30.3 0.2 collective-permute-done.9.refs_2_
  30.5 0.6 %collective-permute-start.11 = (f32[4,2,16,512]{3,2,1,0:T(8,128)S(1)}, f32[4,2,16,512]{3,2,1,0:T(8,128)S(1)}, u32[]{:S(2)}, u32[]{:S(2)}) collective-permute-start(f32[4,2,16,512]{3,2,1,0:T(8,128)S(1)} %stack_blocks.1.own_ref), channel_id=1, source_target_pairs={{0,1},{1,0},{2,3},{3,2},{4,5},{5,4},{6,7},{7,6},{8,9},{9,8},{10,11... | collective-permute-start | bytes 786440 | tf_op jit(solution)/shard_map/ppermute | solution.py:243
  31.2 1.2 %collective-permute-done.11.core_ref = f32[4,2,16,512]{3,2,1,0:T(8,128)S(1)} collective-permute-done((f32[4,2,16,512]{3,2,1,0:T(8,128)S(1)}, f32[4,2,16,512]{3,2,1,0:T(8,128)S(1)}, u32[]{:S(2)}, u32[]{:S(2)}) %collective-permute-start.11) | collective-permute-done | bytes 262176 | tf_op jit(solution)/shard_map/ppermute | solution.py:243
  32.3 2.9 %make_output.1 = bf16[4,256,512]{2,1,0:T(8,128)(2,1)} custom-call(s32[1]{0:T(128)} %bitcast.place_ref, bf16[4,256,512]{2,1,0:T(8,128)(2,1)S(1)} %copy-done.1, bf16[2,2,256,384]{3,2,1,0:T(8,128)(2,1)S(1)} %copy-done.3, bf16[64,64]{1,0:T(8,128)(2,1)S(1)} %copy-done.8, f32[64]{0:T(128)S(1)} %copy-done.9, f32[4,2,16,512]{3,2,1,0:T(8,128)S(1)} %stack_blocks.1.own_ref, ...), custom_call_target="tpu_custom_call" | custom-call | tf_op jit(solution)/shard_map/make_output/pallas_call | solution.py:433
  (31 shorter events, 0.2 us)
Async XLA Ops:
  1.1 1.2 %copy-start = (bf16[4,256,512]{2,1,0:T(8,128)(2,1)S(1)}, bf16[4,256,512]{2,1,0:T(8,128)(2,1)}, u32[]{:S(2)}) copy-start(bf16[4,256,512]{2,1,0:T(8,128)(2,1)} %flow_ref.3) | copy-start | bytes 3145732
  2.3 15.5 %copy-start.2 = (bf16[1,64,64,128]{3,2,1,0:T(8,128)(2,1)S(1)}, bf16[1,64,64,128]{3,2,1,0:T(8,128)(2,1)}, u32[]{:S(2)}) copy-start(bf16[1,64,64,128]{3,2,1,0:T(8,128)(2,1)} %refs_5_.1) | copy-start | bytes 3145732
  2.6 1.7 %collective-permute-start = (f32[4,2,16,512]{3,2,1,0:T(8,128)S(1)}, f32[4,2,16,512]{3,2,1,0:T(8,128)S(1)}, u32[]{:S(2)}, u32[]{:S(2)}) collective-permute-start(f32[4,2,16,512]{3,2,1,0:T(8,128)S(1)} %get-tuple-element.16), channel_id=1, source_target_pairs={{0,1},{1,0},{2,3},{3,2},{4,5},{5,4},{6,7},{7,6},{8,9},{9,8},{10,11... | collective-permute-start | bytes 786440 | tf_op jit(solution)/shard_map/ppermute | solution.py:243
  4.3 7.8 %collective-permute-start.1 = (f32[2,16,512]{2,1,0:T(8,128)S(1)}, f32[2,16,512]{2,1,0:T(8,128)S(1)}, u32[]{:S(2)}, u32[]{:S(2)}) collective-permute-start(f32[2,16,512]{2,1,0:T(8,128)S(1)} %get-tuple-element.17), channel_id=1, source_target_pairs={{0,12},{1,15},{2,14},{3,13},{4,8},{5,11},{6,10},{7,9},{8,4},{9,7},... | collective-permute-start | bytes 196616 | tf_op jit(solution)/shard_map/ppermute | solution.py:254
  9.4 6.5 %collective-permute-start.2 = (f32[2,16,512]{2,1,0:T(8,128)S(1)}, f32[2,16,512]{2,1,0:T(8,128)S(1)}, u32[]{:S(2)}, u32[]{:S(2)}) collective-permute-start(f32[2,16,512]{2,1,0:T(8,128)S(1)} %get-tuple-element.18), channel_id=1, source_target_pairs={{0,8},{1,11},{2,10},{3,9},{4,12},{5,15},{6,14},{7,13},{8,0},{9,3},... | collective-permute-start | bytes 196616 | tf_op jit(solution)/shard_map/ppermute | solution.py:254
  9.4 6.5 %collective-permute-start.3 = (f32[2,16,512]{2,1,0:T(8,128)S(1)}, f32[2,16,512]{2,1,0:T(8,128)S(1)}, u32[]{:S(2)}, u32[]{:S(2)}) collective-permute-start(f32[2,16,512]{2,1,0:T(8,128)S(1)} %get-tuple-element.19), channel_id=1, source_target_pairs={{0,4},{1,7},{2,6},{3,5},{4,0},{5,3},{6,2},{7,1},{8,12},{9,15},{10,... | collective-permute-start | bytes 196616 | tf_op jit(solution)/shard_map/ppermute | solution.py:254
  10.0 7.8 %copy-start.4 = (bf16[128,128]{1,0:T(8,128)(2,1)S(1)}, bf16[128,128]{1,0:T(8,128)(2,1)}, u32[]{:S(2)}) copy-start(bf16[128,128]{1,0:T(8,128)(2,1)} %constant.145.clone.refs_9_) | copy-start | bytes 98308
  10.0 7.8 %copy-start.5 = (bf16[128,128]{1,0:T(8,128)(2,1)S(1)}, bf16[128,128]{1,0:T(8,128)(2,1)}, u32[]{:S(2)}) copy-start(bf16[128,128]{1,0:T(8,128)(2,1)} %constant.144.clone.refs_8_) | copy-start | bytes 98308
  10.0 7.8 %copy-start.6 = (bf16[128,128]{1,0:T(8,128)(2,1)S(1)}, bf16[128,128]{1,0:T(8,128)(2,1)}, u32[]{:S(2)}) copy-start(bf16[128,128]{1,0:T(8,128)(2,1)} %constant.143.clone.refs_7_) | copy-start | bytes 98308
  10.0 7.8 %copy-start.7 = (bf16[128,128]{1,0:T(8,128)(2,1)S(1)}, bf16[128,128]{1,0:T(8,128)(2,1)}, u32[]{:S(2)}) copy-start(bf16[128,128]{1,0:T(8,128)(2,1)} %constant.142.clone.refs_6_) | copy-start | bytes 98308
  10.0 5.8 %collective-permute-start.4 = (f32[2,16,512]{2,1,0:T(8,128)S(1)}, f32[2,16,512]{2,1,0:T(8,128)S(1)}, u32[]{:S(2)}, u32[]{:S(2)}) collective-permute-start(f32[2,16,512]{2,1,0:T(8,128)S(1)} %get-tuple-element.20), channel_id=1, source_target_pairs={{0,0},{1,3},{2,2},{3,1},{4,4},{5,7},{6,6},{7,5},{8,8},{9,11},{10,1... | collective-permute-start | bytes 196616 | tf_op jit(solution)/shard_map/ppermute | solution.py:254
  15.9 16.5 %copy-start.1 = (bf16[4,256,512]{2,1,0:T(8,128)(2,1)S(1)}, bf16[4,256,512]{2,1,0:T(8,128)(2,1)}, u32[]{:S(2)}) copy-start(bf16[4,256,512]{2,1,0:T(8,128)(2,1)} %flow_ref.3) | copy-start | bytes 3145732
  15.9 1.9 %collective-permute-start.5 = (f32[4,16,512]{2,1,0:T(8,128)S(1)}, f32[4,16,512]{2,1,0:T(8,128)S(1)}, u32[]{:S(2)}, u32[]{:S(2)}) collective-permute-start(f32[4,16,512]{2,1,0:T(8,128)S(1)} %second_halves.1), channel_id=1, source_target_pairs={{0,1},{1,0},{2,3},{3,2},{4,5},{5,4},{6,7},{7,6},{8,9},{9,8},{10,11... | collective-permute-start | bytes 393224 | tf_op jit(solution)/shard_map/ppermute | solution.py:243
  17.8 14.6 %copy-start.8 = (bf16[64,64]{1,0:T(8,128)(2,1)S(1)}, bf16[64,64]{1,0:T(8,128)(2,1)}, u32[]{:S(2)}) copy-start(bf16[64,64]{1,0:T(8,128)(2,1)} %local_ref.1) | copy-start | bytes 24580
  19.4 13.0 %copy-start.3 = (bf16[2,2,256,384]{3,2,1,0:T(8,128)(2,1)S(1)}, bf16[2,2,256,384]{3,2,1,0:T(8,128)(2,1)}, u32[]{:S(2)}) copy-start(bf16[2,2,256,384]{3,2,1,0:T(8,128)(2,1)} %constant.146.clone.table_ref) | copy-start | bytes 2359300
  19.4 1.4 %collective-permute-start.6 = (f32[4,16,512]{2,1,0:T(8,128)S(1)}, f32[4,16,512]{2,1,0:T(8,128)S(1)}, u32[]{:S(2)}, u32[]{:S(2)}) collective-permute-start(f32[4,16,512]{2,1,0:T(8,128)S(1)} %get-tuple-element.22), channel_id=1, source_target_pairs={{0,1},{1,0},{2,3},{3,2},{4,5},{5,4},{6,7},{7,6},{8,9},{9,8},{10,11... | collective-permute-start | bytes 393224 | tf_op jit(solution)/shard_map/ppermute | solution.py:243
  20.7 6.9 %collective-permute-start.7 = (f32[2,16,512]{2,1,0:T(8,128)S(1)}, f32[2,16,512]{2,1,0:T(8,128)S(1)}, u32[]{:S(2)}, u32[]{:S(2)}) collective-permute-start(f32[2,16,512]{2,1,0:T(8,128)S(1)} %get-tuple-element.23), channel_id=1, source_target_pairs={{0,12},{1,15},{2,14},{3,13},{4,8},{5,11},{6,10},{7,9},{8,4},{9,7},... | collective-permute-start | bytes 196616 | tf_op jit(solution)/shard_map/ppermute | solution.py:254
  24.1 6.1 %collective-permute-start.8 = (f32[2,16,512]{2,1,0:T(8,128)S(1)}, f32[2,16,512]{2,1,0:T(8,128)S(1)}, u32[]{:S(2)}, u32[]{:S(2)}) collective-permute-start(f32[2,16,512]{2,1,0:T(8,128)S(1)} %get-tuple-element.24), channel_id=1, source_target_pairs={{0,8},{1,11},{2,10},{3,9},{4,12},{5,15},{6,14},{7,13},{8,0},{9,3},... | collective-permute-start | bytes 196616 | tf_op jit(solution)/shard_map/ppermute | solution.py:254
  24.1 6.4 %collective-permute-start.9 = (f32[2,16,512]{2,1,0:T(8,128)S(1)}, f32[2,16,512]{2,1,0:T(8,128)S(1)}, u32[]{:S(2)}, u32[]{:S(2)}) collective-permute-start(f32[2,16,512]{2,1,0:T(8,128)S(1)} %get-tuple-element.25), channel_id=1, source_target_pairs={{0,4},{1,7},{2,6},{3,5},{4,0},{5,3},{6,2},{7,1},{8,12},{9,15},{10,... | collective-permute-start | bytes 196616 | tf_op jit(solution)/shard_map/ppermute | solution.py:254
  25.2 5.3 %collective-permute-start.10 = (f32[2,16,512]{2,1,0:T(8,128)S(1)}, f32[2,16,512]{2,1,0:T(8,128)S(1)}, u32[]{:S(2)}, u32[]{:S(2)}) collective-permute-start(f32[2,16,512]{2,1,0:T(8,128)S(1)} %get-tuple-element.26), channel_id=1, source_target_pairs={{0,0},{1,3},{2,2},{3,1},{4,4},{5,7},{6,6},{7,5},{8,8},{9,11},{10,1... | collective-permute-start | bytes 196616 | tf_op jit(solution)/shard_map/ppermute | solution.py:254
  30.5 1.8 %copy-start.9 = (f32[64]{0:T(128)S(1)}, f32[64]{0:T(128)}, u32[]{:S(2)}) copy-start(f32[64]{0:T(128)} %bias_ref.1) | copy-start | bytes 772
  30.5 1.8 %collective-permute-start.11 = (f32[4,2,16,512]{3,2,1,0:T(8,128)S(1)}, f32[4,2,16,512]{3,2,1,0:T(8,128)S(1)}, u32[]{:S(2)}, u32[]{:S(2)}) collective-permute-start(f32[4,2,16,512]{3,2,1,0:T(8,128)S(1)} %stack_blocks.1.own_ref), channel_id=1, source_target_pairs={{0,1},{1,0},{2,3},{3,2},{4,5},{5,4},{6,7},{7,6},{8,9},{9,8},{10,11... | collective-permute-start | bytes 786440 | tf_op jit(solution)/shard_map/ppermute | solution.py:243

commit v8 on v7

--- a/solution.py
+++ b/solution.py
@@ -155,7 +155,8 @@
 
 
 def turns(layers):
-    return list(range(layers - 1, 0, -1)) + [0]
+    half = layers // 2
+    return list(range(half, layers)) + list(range(half - 1, -1, -1))
 
 
 def forward_y_table(cells_y, groups_y, peers, rows_ky):
@@ -163,7 +164,8 @@
     layers = peers // 2
     row = jnp.arange(2 * MY, dtype=jnp.int32)
     block = row // (2 * rows_ky)
-    turn = layers - 1 - block // 2 % layers
+    place = block // 2 % layers
+    turn = jnp.where(place < layers // 2, place + layers // 2, layers - 1 - place)
     side = y ^ (1 - block // peers)
     column = x ^ side
     half = side ^ (block % 2)
@@ -280,37 +282,17 @@
     return small_call(join_kernel, [shape] * keep.shape[0], "join_blocks")(keep, arrived)
 
 
-def second_kernel(*refs):
-    for turn, block_ref in enumerate(refs[:-1]):
-        refs[-1][turn] = block_ref[1]
-
-
-def second_halves(blocks):
-    shape = jax.ShapeDtypeStruct((len(blocks),) + blocks[0].shape[1:], blocks[0].dtype)
-    return small_call(second_kernel, shape, "second_halves")(*blocks)
-
-
-def stack_kernel(*refs):
-    for turn, block_ref in enumerate(refs[:-1]):
-        refs[-1][turn] = block_ref[...]
-
-
-def stack_blocks(blocks):
-    shape = jax.ShapeDtypeStruct((len(blocks),) + blocks[0].shape, blocks[0].dtype)
-    return small_call(stack_kernel, shape, "stack_blocks")(*blocks)
-
-
 def mix_kernel(layers, *refs):
-    block_refs = refs[:layers]
-    arrived_ref, weight_ref, forward_high, forward_low, inverse_high, inverse_low = refs[
-        layers : layers + 6
+    block_refs, arrived_refs = refs[:layers], refs[layers : 2 * layers]
+    weight_ref, forward_high, forward_low, inverse_high, inverse_low = refs[
+        2 * layers : 2 * layers + 5
     ]
-    mixed_ref, send_ref, keep_ref, order_ref, spread_ref, result_ref = refs[layers + 6 :]
+    mixed_ref, send_ref, keep_ref, order_ref, spread_ref, result_ref = refs[2 * layers + 5 :]
     z, x, y = quad()
     column = x ^ y
     for index, turn in enumerate(turns(layers)):
         order_ref[(z ^ turn) * 2 + column] = block_refs[index][0]
-        order_ref[(z ^ turn) * 2 + (column ^ 1)] = arrived_ref[index]
+        order_ref[(z ^ turn) * 2 + (column ^ 1)] = arrived_refs[index][1]
     feat_count = order_ref.shape[-1]
     count = weight_ref.shape[1]
     channels = weight_ref.shape[2]
@@ -368,30 +350,31 @@
 
 
 def mix(blocks, arrived, weights, forward_table, inverse_table):
-    layers, rows, feat_count = arrived.shape
+    layers = len(blocks)
+    _, rows, feat_count = blocks[0].shape
     count = weights.shape[1]
+    half = jax.ShapeDtypeStruct((layers, rows, feat_count), jnp.float32)
     scratch = pltpu.VMEM((count * feat_count // 64, 128), jnp.float32)
     return pl.pallas_call(
         functools.partial(mix_kernel, layers),
-        out_shape=[jax.ShapeDtypeStruct((1, count, 2 * feat_count), jnp.float32)]
-        + [jax.ShapeDtypeStruct(arrived.shape, jnp.float32)] * 2,
+        out_shape=[jax.ShapeDtypeStruct((1, count, 2 * feat_count), jnp.float32), half, half],
         scratch_shapes=[pltpu.VMEM((2 * layers, rows, feat_count), jnp.float32), scratch, scratch],
         compiler_params=SMALL,
         name="mix",
-    )(*blocks, arrived, weights, *split_table(forward_table), *split_table(inverse_table))
+    )(*blocks, *arrived, weights, *split_table(forward_table), *split_table(inverse_table))
 
 
 def output_kernel(
-    place_ref, flow_ref, table_ref, local_ref, bias_ref, own_ref, core_ref,
-    out_ref, order_ref, stack_ref, wide_ref, level_ref,
+    layers, place_ref, flow_ref, table_ref, local_ref, bias_ref, *refs
 ):
+    own_refs, core_refs = refs[:layers], refs[layers : 2 * layers]
+    out_ref, order_ref, stack_ref, wide_ref, level_ref = refs[2 * layers :]
     step = pl.program_id(0)
     feat_count = flow_ref.shape[-1]
     channels = local_ref.shape[0]
     width = wide_ref.shape[0]
     pairs = stack_ref.shape[0]
-    layers = own_ref.shape[0]
-    rows = own_ref.shape[2] // pairs
+    rows = order_ref.shape[1] // pairs
 
     @pl.when(step == 0)
     def _():
@@ -399,8 +382,8 @@
         for index, turn in enumerate(turns(layers)):
             for side in range(2):
                 peer = 2 * layers * side + (z ^ turn) * 2
-                order_ref[peer + (x ^ y)] = own_ref[index, side]
-                order_ref[peer + (x ^ y ^ 1)] = core_ref[index, 1 - side]
+                order_ref[peer + (x ^ y)] = own_refs[index][side]
+                order_ref[peer + (x ^ y ^ 1)] = core_refs[index][1 - side]
         for pair in range(pairs):
             span = slice(pair * rows, (pair + 1) * rows)
             high, low = split_terms(order_ref[:, span, :].reshape(-1, feat_count))
@@ -426,12 +409,13 @@
 
 def make_output(flow_field, parts, table, local, bias):
     cells_x, cells_y, feat_count = flow_field.shape
-    layers, _, rows, _ = parts[0].shape
+    layers = len(parts) // 2
+    rows = parts[0].shape[1]
     place = jnp.reshape(lax.axis_index("gy"), (1,))
     whole = lambda array: pl.BlockSpec(array.shape, lambda i, p: (0,) * array.ndim)
     block = pl.BlockSpec((1, cells_y, feat_count), lambda i, p: (i, 0, 0))
     return pl.pallas_call(
-        output_kernel,
+        functools.partial(output_kernel, layers),
         grid_spec=pltpu.PrefetchScalarGridSpec(
             num_scalar_prefetch=1,
             grid=(cells_x,),
@@ -469,13 +453,13 @@
     blocks = along_columns(add_blocks(keep, flip_core(send)), peers)
     mixed, send, keep = mix(
         blocks,
-        flip_core(second_halves(blocks)),
+        [flip_core(block) for block in blocks],
         spectral_weight,
         forward_x_table(cells_x, peers, rows_ky) * forward_scale,
         inverse_x_table(cells_x, peers, rows_ky),
     )
-    own = stack_blocks(along_columns(join_blocks(keep, flip_core(send)), peers))
-    parts = [own, flip_core(own)]
+    own = along_columns(join_blocks(keep, flip_core(send)), peers)
+    parts = own + [flip_core(block) for block in own]
     high, low = split_table(inverse_y_table(cells_y, groups_y, peers, rows_ky) * inverse_scale)
     table = np.concatenate([high, high, low], axis=-1)
     return make_output(flow_field, parts, table, local_weight, bias_terms), mixed

time: 35.5 us -> 35.1 us (0.989)
  waiting for transfers between devices: 14 us -> 10.7 us
  starting transfers between devices: 14 us -> 17 us
    ppermute x4 -> x10, starting transfers between devices: 2.4 us -> 5.7 us  [flip_core(): return lax.ppermute(block, 'gy', [(0, 1), (1, 0)])]
    ppermute x8, waiting for transfers between devices: 9.69 us -> 6.52 us  [along_columns(): arrived.append(lax.ppermute(block, ('gx', 'gy'), pairs))]
    ppermute x4 -> x10, waiting for transfers between devices: 4.3 us -> 4.14 us  [flip_core(): return lax.ppermute(block, 'gy', [(0, 1), (1, 0)])]
    pallas_call x3 -> x1, Pallas kernels: 2.93 us -> 2.92 us  [make_output(): pl.pallas_call(functools.partial(output_kernel, layers), grid_spec=pltpu....]
  transfers between devices with their start and end apart: 12 -> 18, of which waited for: 9 -> 13; matrix products, arithmetic and copies ran while one was open for 0% -> 0% of each run, Pallas kernels for 0% -> 0%
where the time goes in v8:
time: 35.1 us; the launch traced here: 34.9 us
  starting transfers between devices  17 us (48%)
  waiting for transfers between devices  10.7 us (30%)
  Pallas kernels  4.82 us (14%)
  local copies, waits for them, and re-layouts  1.26 us (4%)
  between operations  0.8 us (2%)
  other arithmetic  0.38 us (1%)
    ppermute x8, starting transfers between devices, along_columns(): arrived.append(lax.ppermute(block, ('gx', 'gy'), pairs))  11.3 us
    ppermute x8, waiting for transfers between devices, along_columns(): arrived.append(lax.ppermute(block, ('gx', 'gy'), pairs))  6.52 us
    ppermute x10, starting transfers between devices, flip_core(): return lax.ppermute(block, 'gy', [(0, 1), (1, 0)])  5.7 us
    ppermute x10, waiting for transfers between devices, flip_core(): return lax.ppermute(block, 'gy', [(0, 1), (1, 0)])  4.14 us
    pallas_call x1, Pallas kernels, make_output(): pl.pallas_call(functools.partial(output_kernel, layers), grid_spec=pltpu....  2.92 us
    pallas_call x1, Pallas kernels, mix(): pl.pallas_call(functools.partial(mix_kernel, layers), out_shape=[jax.Shap...  1.56 us
    unnamed x20, local copies, waits for them, and re-layouts  1.26 us
  transfers between devices with their start and end apart: 18, of which 13 were waited for; matrix products, arithmetic and copies ran while one was open for 0% of the time, Pallas kernels for 0%

profile of v8, /device:TPU:0, one launch (start us, length us, event | category | flops | bytes accessed | tf_op | source)
XLA Modules:
  0.0 34.9 jit_solution(4549573399561020883)
XLA Ops:
  0.7 0.3 select_convert_fusion.table_ref
  1.1 1.2 %copy-done = bf16[4,256,512]{2,1,0:T(8,128)(2,1)S(1)} copy-done((bf16[4,256,512]{2,1,0:T(8,128)(2,1)S(1)}, bf16[4,256,512]{2,1,0:T(8,128)(2,1)}, u32[]{:S(2)}) %copy-start) | copy-done | bytes 1048600
  2.6 0.5 %collective-permute-start = (f32[4,2,16,512]{3,2,1,0:T(8,128)S(1)}, f32[4,2,16,512]{3,2,1,0:T(8,128)S(1)}, u32[]{:S(2)}, u32[]{:S(2)}) collective-permute-start(f32[4,2,16,512]{3,2,1,0:T(8,128)S(1)} %get-tuple-element.16), channel_id=1, source_target_pairs={{0,1},{1,0},{2,3},{3,2},{4,5},{5,4},{6,7},{7,6},{8,9},{9,8},{10,11... | collective-permute-start | bytes 786440 | tf_op jit(solution)/shard_map/ppermute | solution.py:245
  3.1 1.2 %collective-permute-done.arrived_ref = f32[4,2,16,512]{3,2,1,0:T(8,128)S(1)} collective-permute-done((f32[4,2,16,512]{3,2,1,0:T(8,128)S(1)}, f32[4,2,16,512]{3,2,1,0:T(8,128)S(1)}, u32[]{:S(2)}, u32[]{:S(2)}) %collective-permute-start) | collective-permute-done | bytes 262176 | tf_op jit(solution)/shard_map/ppermute | solution.py:245
  4.3 4.0 %collective-permute-start.1 = (f32[2,16,512]{2,1,0:T(8,128)S(1)}, f32[2,16,512]{2,1,0:T(8,128)S(1)}, u32[]{:S(2)}, u32[]{:S(2)}) collective-permute-start(f32[2,16,512]{2,1,0:T(8,128)S(1)} %get-tuple-element.17), channel_id=1, source_target_pairs={{0,8},{1,11},{2,10},{3,9},{4,12},{5,15},{6,14},{7,13},{8,0},{9,3},... | collective-permute-start | bytes 196616 | tf_op jit(solution)/shard_map/ppermute | solution.py:256
  8.4 1.3 %collective-permute-start.2 = (f32[2,16,512]{2,1,0:T(8,128)S(1)}, f32[2,16,512]{2,1,0:T(8,128)S(1)}, u32[]{:S(2)}, u32[]{:S(2)}) collective-permute-start(f32[2,16,512]{2,1,0:T(8,128)S(1)} %get-tuple-element.18), channel_id=1, source_target_pairs={{0,12},{1,15},{2,14},{3,13},{4,8},{5,11},{6,10},{7,9},{8,4},{9,7},... | collective-permute-start | bytes 196616 | tf_op jit(solution)/shard_map/ppermute | solution.py:256
  10.0 0.8 %collective-permute-start.4 = (f32[2,16,512]{2,1,0:T(8,128)S(1)}, f32[2,16,512]{2,1,0:T(8,128)S(1)}, u32[]{:S(2)}, u32[]{:S(2)}) collective-permute-start(f32[2,16,512]{2,1,0:T(8,128)S(1)} %get-tuple-element.20), channel_id=1, source_target_pairs={{0,0},{1,3},{2,2},{3,1},{4,4},{5,7},{6,6},{7,5},{8,8},{9,11},{10,1... | collective-permute-start | bytes 196616 | tf_op jit(solution)/shard_map/ppermute | solution.py:256
  11.0 2.8 %collective-permute-start.5 = (f32[2,16,512]{2,1,0:T(8,128)S(1)}, f32[2,16,512]{2,1,0:T(8,128)S(1)}, u32[]{:S(2)}, u32[]{:S(2)}) collective-permute-start(f32[2,16,512]{2,1,0:T(8,128)S(1)} %collective-permute-done.1.refs_0_), channel_id=1, source_target_pairs={{0,1},{1,0},{2,3},{3,2},{4,5},{5,4},{6,7},{7,6},{8,9},{9,8},{10,11... | collective-permute-start | bytes 196616 | tf_op jit(solution)/shard_map/ppermute | solution.py:245
  13.7 1.3 %collective-permute-done.2.refs_1_ = f32[2,16,512]{2,1,0:T(8,128)S(1)} collective-permute-done((f32[2,16,512]{2,1,0:T(8,128)S(1)}, f32[2,16,512]{2,1,0:T(8,128)S(1)}, u32[]{:S(2)}, u32[]{:S(2)}) %collective-permute-start.2) | collective-permute-done | bytes 65568 | tf_op jit(solution)/shard_map/ppermute | solution.py:256
  15.1 0.5 %collective-permute-start.6 = (f32[2,16,512]{2,1,0:T(8,128)S(1)}, f32[2,16,512]{2,1,0:T(8,128)S(1)}, u32[]{:S(2)}, u32[]{:S(2)}) collective-permute-start(f32[2,16,512]{2,1,0:T(8,128)S(1)} %collective-permute-done.2.refs_1_), channel_id=1, source_target_pairs={{0,1},{1,0},{2,3},{3,2},{4,5},{5,4},{6,7},{7,6},{8,9},{9,8},{10,11... | collective-permute-start | bytes 196616 | tf_op jit(solution)/shard_map/ppermute | solution.py:245
  16.0 0.3 collective-permute-start.8
  16.4 0.6 %collective-permute-done.7.refs_6_ = f32[2,16,512]{2,1,0:T(8,128)S(1)} collective-permute-done((f32[2,16,512]{2,1,0:T(8,128)S(1)}, f32[2,16,512]{2,1,0:T(8,128)S(1)}, u32[]{:S(2)}, u32[]{:S(2)}) %collective-permute-start.7) | collective-permute-done | bytes 65568 | tf_op jit(solution)/shard_map/ppermute | solution.py:245
  17.2 1.6 %mix.1 = (f32[1,64,1024]{2,1,0:T(8,128)}, f32[4,16,512]{2,1,0:T(8,128)S(1)}, f32[4,16,512]{2,1,0:T(8,128)S(1)}) custom-call(f32[2,16,512]{2,1,0:T(8,128)S(1)} %collective-permute-done.1.refs_0_, f32[2,16,512]{2,1,0:T(8,128)S(1)} %collective-permute-done.2.refs_1_, f32[2,16,512]{2,1,0:T(8,128)S(1)} %collective-permute-done.3.refs_2_, ...), custom_call_target="tpu_custom_call" | custom-call | tf_op jit(solution)/shard_map/mix/pallas_call | solution.py:358
  18.8 0.3 collective-permute-start.9
  19.1 1.0 %collective-permute-done.9.arrived_ref = f32[4,16,512]{2,1,0:T(8,128)S(1)} collective-permute-done((f32[4,16,512]{2,1,0:T(8,128)S(1)}, f32[4,16,512]{2,1,0:T(8,128)S(1)}, u32[]{:S(2)}, u32[]{:S(2)}) %collective-permute-start.9) | collective-permute-done | bytes 131104 | tf_op jit(solution)/shard_map/ppermute | solution.py:245
  20.2 3.1 %collective-permute-start.10 = (f32[2,16,512]{2,1,0:T(8,128)S(1)}, f32[2,16,512]{2,1,0:T(8,128)S(1)}, u32[]{:S(2)}, u32[]{:S(2)}) collective-permute-start(f32[2,16,512]{2,1,0:T(8,128)S(1)} %get-tuple-element.23), channel_id=1, source_target_pairs={{0,8},{1,11},{2,10},{3,9},{4,12},{5,15},{6,14},{7,13},{8,0},{9,3},... | collective-permute-start | bytes 196616 | tf_op jit(solution)/shard_map/ppermute | solution.py:256
  23.3 1.0 %collective-permute-start.11 = (f32[2,16,512]{2,1,0:T(8,128)S(1)}, f32[2,16,512]{2,1,0:T(8,128)S(1)}, u32[]{:S(2)}, u32[]{:S(2)}) collective-permute-start(f32[2,16,512]{2,1,0:T(8,128)S(1)} %get-tuple-element.24), channel_id=1, source_target_pairs={{0,12},{1,15},{2,14},{3,13},{4,8},{5,11},{6,10},{7,9},{8,4},{9,7},... | collective-permute-start | bytes 196616 | tf_op jit(solution)/shard_map/ppermute | solution.py:256
  24.3 0.8 %collective-permute-start.13 = (f32[2,16,512]{2,1,0:T(8,128)S(1)}, f32[2,16,512]{2,1,0:T(8,128)S(1)}, u32[]{:S(2)}, u32[]{:S(2)}) collective-permute-start(f32[2,16,512]{2,1,0:T(8,128)S(1)} %get-tuple-element.26), channel_id=1, source_target_pairs={{0,0},{1,3},{2,2},{3,1},{4,4},{5,7},{6,6},{7,5},{8,8},{9,11},{10,1... | collective-permute-start | bytes 196616 | tf_op jit(solution)/shard_map/ppermute | solution.py:256
  25.1 2.4 %collective-permute-done.10.refs_0_ = f32[2,16,512]{2,1,0:T(8,128)S(1)} collective-permute-done((f32[2,16,512]{2,1,0:T(8,128)S(1)}, f32[2,16,512]{2,1,0:T(8,128)S(1)}, u32[]{:S(2)}, u32[]{:S(2)}) %collective-permute-start.10) | collective-permute-done | bytes 65568 | tf_op jit(solution)/shard_map/ppermute | solution.py:256
  27.8 2.3 %collective-permute-done.11.refs_1_ = f32[2,16,512]{2,1,0:T(8,128)S(1)} collective-permute-done((f32[2,16,512]{2,1,0:T(8,128)S(1)}, f32[2,16,512]{2,1,0:T(8,128)S(1)}, u32[]{:S(2)}, u32[]{:S(2)}) %collective-permute-start.11) | collective-permute-done | bytes 65568 | tf_op jit(solution)/shard_map/ppermute | solution.py:256
  30.1 0.4 %collective-permute-start.15 = (f32[2,16,512]{2,1,0:T(8,128)S(1)}, f32[2,16,512]{2,1,0:T(8,128)S(1)}, u32[]{:S(2)}, u32[]{:S(2)}) collective-permute-start(f32[2,16,512]{2,1,0:T(8,128)S(1)} %collective-permute-done.11.refs_1_), channel_id=1, source_target_pairs={{0,1},{1,0},{2,3},{3,2},{4,5},{5,4},{6,7},{7,6},{8,9},{9,8},{10,11... | collective-permute-start | bytes 196616 | tf_op jit(solution)/shard_map/ppermute | solution.py:245
  31.0 0.4 %collective-permute-done.15.refs_5_ = f32[2,16,512]{2,1,0:T(8,128)S(1)} collective-permute-done((f32[2,16,512]{2,1,0:T(8,128)S(1)}, f32[2,16,512]{2,1,0:T(8,128)S(1)}, u32[]{:S(2)}, u32[]{:S(2)}) %collective-permute-start.15) | collective-permute-done | bytes 65568 | tf_op jit(solution)/shard_map/ppermute | solution.py:245
  31.4 0.4 %collective-permute-done.16.refs_6_ = f32[2,16,512]{2,1,0:T(8,128)S(1)} collective-permute-done((f32[2,16,512]{2,1,0:T(8,128)S(1)}, f32[2,16,512]{2,1,0:T(8,128)S(1)}, u32[]{:S(2)}, u32[]{:S(2)}) %collective-permute-start.16) | collective-permute-done | bytes 65568 | tf_op jit(solution)/shard_map/ppermute | solution.py:245
  32.0 2.9 %make_output.1 = bf16[4,256,512]{2,1,0:T(8,128)(2,1)} custom-call(s32[1]{0:T(128)} %bitcast.place_ref, bf16[4,256,512]{2,1,0:T(8,128)(2,1)S(1)} %copy-done.1, bf16[2,2,256,384]{3,2,1,0:T(8,128)(2,1)S(1)} %copy-done.3, bf16[64,64]{1,0:T(8,128)(2,1)S(1)} %copy-done.8, f32[64]{0:T(128)S(1)} %copy-done.9, f32[2,16,512]{2,1,0:T(8,128)S(1)} %collective-permute-done.10.refs_0_, ...), custom_call_target="tpu_custom_call" | custom-call | tf_op jit(solution)/shard_map/make_output/pallas_call | solution.py:417
  (41 shorter events, 2.8 us)
Async XLA Ops:
  2.3 14.9 %copy-start.2 = (bf16[1,64,64,128]{3,2,1,0:T(8,128)(2,1)S(1)}, bf16[1,64,64,128]{3,2,1,0:T(8,128)(2,1)}, u32[]{:S(2)}) copy-start(bf16[1,64,64,128]{3,2,1,0:T(8,128)(2,1)} %refs_8_.1) | copy-start | bytes 3145732
  2.6 1.7 %collective-permute-start = (f32[4,2,16,512]{3,2,1,0:T(8,128)S(1)}, f32[4,2,16,512]{3,2,1,0:T(8,128)S(1)}, u32[]{:S(2)}, u32[]{:S(2)}) collective-permute-start(f32[4,2,16,512]{3,2,1,0:T(8,128)S(1)} %get-tuple-element.16), channel_id=1, source_target_pairs={{0,1},{1,0},{2,3},{3,2},{4,5},{5,4},{6,7},{7,6},{8,9},{9,8},{10,11... | collective-permute-start | bytes 786440 | tf_op jit(solution)/shard_map/ppermute | solution.py:245
  4.3 12.9 %copy-start.5 = (bf16[128,128]{1,0:T(8,128)(2,1)S(1)}, bf16[128,128]{1,0:T(8,128)(2,1)}, u32[]{:S(2)}) copy-start(bf16[128,128]{1,0:T(8,128)(2,1)} %constant.144.clone.refs_11_) | copy-start | bytes 98308
  4.3 12.9 %copy-start.6 = (bf16[128,128]{1,0:T(8,128)(2,1)S(1)}, bf16[128,128]{1,0:T(8,128)(2,1)}, u32[]{:S(2)}) copy-start(bf16[128,128]{1,0:T(8,128)(2,1)} %constant.143.clone.refs_10_) | copy-start | bytes 98308
  4.3 12.9 %copy-start.7 = (bf16[128,128]{1,0:T(8,128)(2,1)S(1)}, bf16[128,128]{1,0:T(8,128)(2,1)}, u32[]{:S(2)}) copy-start(bf16[128,128]{1,0:T(8,128)(2,1)} %constant.142.clone.refs_9_) | copy-start | bytes 98308
  4.3 27.7 %copy-start.1 = (bf16[4,256,512]{2,1,0:T(8,128)(2,1)S(1)}, bf16[4,256,512]{2,1,0:T(8,128)(2,1)}, u32[]{:S(2)}) copy-start(bf16[4,256,512]{2,1,0:T(8,128)(2,1)} %flow_ref.3) | copy-start | bytes 3145732
  4.3 6.6 %collective-permute-start.1 = (f32[2,16,512]{2,1,0:T(8,128)S(1)}, f32[2,16,512]{2,1,0:T(8,128)S(1)}, u32[]{:S(2)}, u32[]{:S(2)}) collective-permute-start(f32[2,16,512]{2,1,0:T(8,128)S(1)} %get-tuple-element.17), channel_id=1, source_target_pairs={{0,8},{1,11},{2,10},{3,9},{4,12},{5,15},{6,14},{7,13},{8,0},{9,3},... | collective-permute-start | bytes 196616 | tf_op jit(solution)/shard_map/ppermute | solution.py:256
  8.4 6.7 %collective-permute-start.2 = (f32[2,16,512]{2,1,0:T(8,128)S(1)}, f32[2,16,512]{2,1,0:T(8,128)S(1)}, u32[]{:S(2)}, u32[]{:S(2)}) collective-permute-start(f32[2,16,512]{2,1,0:T(8,128)S(1)} %get-tuple-element.18), channel_id=1, source_target_pairs={{0,12},{1,15},{2,14},{3,13},{4,8},{5,11},{6,10},{7,9},{8,4},{9,7},... | collective-permute-start | bytes 196616 | tf_op jit(solution)/shard_map/ppermute | solution.py:256
  9.7 6.0 %collective-permute-start.3 = (f32[2,16,512]{2,1,0:T(8,128)S(1)}, f32[2,16,512]{2,1,0:T(8,128)S(1)}, u32[]{:S(2)}, u32[]{:S(2)}) collective-permute-start(f32[2,16,512]{2,1,0:T(8,128)S(1)} %get-tuple-element.19), channel_id=1, source_target_pairs={{0,4},{1,7},{2,6},{3,5},{4,0},{5,3},{6,2},{7,1},{8,12},{9,15},{10,... | collective-permute-start | bytes 196616 | tf_op jit(solution)/shard_map/ppermute | solution.py:256
  9.9 22.0 %copy-start.3 = (bf16[2,2,256,384]{3,2,1,0:T(8,128)(2,1)S(1)}, bf16[2,2,256,384]{3,2,1,0:T(8,128)(2,1)}, u32[]{:S(2)}) copy-start(bf16[2,2,256,384]{3,2,1,0:T(8,128)(2,1)} %constant.146.clone.table_ref) | copy-start | bytes 2359300
  10.0 6.0 %collective-permute-start.4 = (f32[2,16,512]{2,1,0:T(8,128)S(1)}, f32[2,16,512]{2,1,0:T(8,128)S(1)}, u32[]{:S(2)}, u32[]{:S(2)}) collective-permute-start(f32[2,16,512]{2,1,0:T(8,128)S(1)} %get-tuple-element.20), channel_id=1, source_target_pairs={{0,0},{1,3},{2,2},{3,1},{4,4},{5,7},{6,6},{7,5},{8,8},{9,11},{10,1... | collective-permute-start | bytes 196616 | tf_op jit(solution)/shard_map/ppermute | solution.py:256
  11.0 5.3 %collective-permute-start.5 = (f32[2,16,512]{2,1,0:T(8,128)S(1)}, f32[2,16,512]{2,1,0:T(8,128)S(1)}, u32[]{:S(2)}, u32[]{:S(2)}) collective-permute-start(f32[2,16,512]{2,1,0:T(8,128)S(1)} %collective-permute-done.1.refs_0_), channel_id=1, source_target_pairs={{0,1},{1,0},{2,3},{3,2},{4,5},{5,4},{6,7},{7,6},{8,9},{9,8},{10,11... | collective-permute-start | bytes 196616 | tf_op jit(solution)/shard_map/ppermute | solution.py:245
  15.1 1.4 %collective-permute-start.6 = (f32[2,16,512]{2,1,0:T(8,128)S(1)}, f32[2,16,512]{2,1,0:T(8,128)S(1)}, u32[]{:S(2)}, u32[]{:S(2)}) collective-permute-start(f32[2,16,512]{2,1,0:T(8,128)S(1)} %collective-permute-done.2.refs_1_), channel_id=1, source_target_pairs={{0,1},{1,0},{2,3},{3,2},{4,5},{5,4},{6,7},{7,6},{8,9},{9,8},{10,11... | collective-permute-start | bytes 196616 | tf_op jit(solution)/shard_map/ppermute | solution.py:245
  15.8 1.3 %collective-permute-start.7 = (f32[2,16,512]{2,1,0:T(8,128)S(1)}, f32[2,16,512]{2,1,0:T(8,128)S(1)}, u32[]{:S(2)}, u32[]{:S(2)}) collective-permute-start(f32[2,16,512]{2,1,0:T(8,128)S(1)} %collective-permute-done.3.refs_2_), channel_id=1, source_target_pairs={{0,1},{1,0},{2,3},{3,2},{4,5},{5,4},{6,7},{7,6},{8,9},{9,8},{10,11... | collective-permute-start | bytes 196616 | tf_op jit(solution)/shard_map/ppermute | solution.py:245
  16.0 1.3 %collective-permute-start.8 = (f32[2,16,512]{2,1,0:T(8,128)S(1)}, f32[2,16,512]{2,1,0:T(8,128)S(1)}, u32[]{:S(2)}, u32[]{:S(2)}) collective-permute-start(f32[2,16,512]{2,1,0:T(8,128)S(1)} %collective-permute-done.4.refs_3_), channel_id=1, source_target_pairs={{0,1},{1,0},{2,3},{3,2},{4,5},{5,4},{6,7},{7,6},{8,9},{9,8},{10,11... | collective-permute-start | bytes 196616 | tf_op jit(solution)/shard_map/ppermute | solution.py:245
  18.8 1.3 %collective-permute-start.9 = (f32[4,16,512]{2,1,0:T(8,128)S(1)}, f32[4,16,512]{2,1,0:T(8,128)S(1)}, u32[]{:S(2)}, u32[]{:S(2)}) collective-permute-start(f32[4,16,512]{2,1,0:T(8,128)S(1)} %get-tuple-element.22), channel_id=1, source_target_pairs={{0,1},{1,0},{2,3},{3,2},{4,5},{5,4},{6,7},{7,6},{8,9},{9,8},{10,11... | collective-permute-start | bytes 393224 | tf_op jit(solution)/shard_map/ppermute | solution.py:245
  20.2 7.4 %collective-permute-start.10 = (f32[2,16,512]{2,1,0:T(8,128)S(1)}, f32[2,16,512]{2,1,0:T(8,128)S(1)}, u32[]{:S(2)}, u32[]{:S(2)}) collective-permute-start(f32[2,16,512]{2,1,0:T(8,128)S(1)} %get-tuple-element.23), channel_id=1, source_target_pairs={{0,8},{1,11},{2,10},{3,9},{4,12},{5,15},{6,14},{7,13},{8,0},{9,3},... | collective-permute-start | bytes 196616 | tf_op jit(solution)/shard_map/ppermute | solution.py:256
  23.3 6.8 %collective-permute-start.11 = (f32[2,16,512]{2,1,0:T(8,128)S(1)}, f32[2,16,512]{2,1,0:T(8,128)S(1)}, u32[]{:S(2)}, u32[]{:S(2)}) collective-permute-start(f32[2,16,512]{2,1,0:T(8,128)S(1)} %get-tuple-element.24), channel_id=1, source_target_pairs={{0,12},{1,15},{2,14},{3,13},{4,8},{5,11},{6,10},{7,9},{8,4},{9,7},... | collective-permute-start | bytes 196616 | tf_op jit(solution)/shard_map/ppermute | solution.py:256
  24.3 6.2 %collective-permute-start.12 = (f32[2,16,512]{2,1,0:T(8,128)S(1)}, f32[2,16,512]{2,1,0:T(8,128)S(1)}, u32[]{:S(2)}, u32[]{:S(2)}) collective-permute-start(f32[2,16,512]{2,1,0:T(8,128)S(1)} %get-tuple-element.25), channel_id=1, source_target_pairs={{0,4},{1,7},{2,6},{3,5},{4,0},{5,3},{6,2},{7,1},{8,12},{9,15},{10,... | collective-permute-start | bytes 196616 | tf_op jit(solution)/shard_map/ppermute | solution.py:256
  24.3 6.4 %collective-permute-start.13 = (f32[2,16,512]{2,1,0:T(8,128)S(1)}, f32[2,16,512]{2,1,0:T(8,128)S(1)}, u32[]{:S(2)}, u32[]{:S(2)}) collective-permute-start(f32[2,16,512]{2,1,0:T(8,128)S(1)} %get-tuple-element.26), channel_id=1, source_target_pairs={{0,0},{1,3},{2,2},{3,1},{4,4},{5,7},{6,6},{7,5},{8,8},{9,11},{10,1... | collective-permute-start | bytes 196616 | tf_op jit(solution)/shard_map/ppermute | solution.py:256
  27.5 3.5 %collective-permute-start.14 = (f32[2,16,512]{2,1,0:T(8,128)S(1)}, f32[2,16,512]{2,1,0:T(8,128)S(1)}, u32[]{:S(2)}, u32[]{:S(2)}) collective-permute-start(f32[2,16,512]{2,1,0:T(8,128)S(1)} %collective-permute-done.10.refs_0_), channel_id=1, source_target_pairs={{0,1},{1,0},{2,3},{3,2},{4,5},{5,4},{6,7},{7,6},{8,9},{9,8},{10,11... | collective-permute-start | bytes 196616 | tf_op jit(solution)/shard_map/ppermute | solution.py:245
  30.1 1.3 %collective-permute-start.15 = (f32[2,16,512]{2,1,0:T(8,128)S(1)}, f32[2,16,512]{2,1,0:T(8,128)S(1)}, u32[]{:S(2)}, u32[]{:S(2)}) collective-permute-start(f32[2,16,512]{2,1,0:T(8,128)S(1)} %collective-permute-done.11.refs_1_), channel_id=1, source_target_pairs={{0,1},{1,0},{2,3},{3,2},{4,5},{5,4},{6,7},{7,6},{8,9},{9,8},{10,11... | collective-permute-start | bytes 196616 | tf_op jit(solution)/shard_map/ppermute | solution.py:245
  30.5 1.3 %collective-permute-start.16 = (f32[2,16,512]{2,1,0:T(8,128)S(1)}, f32[2,16,512]{2,1,0:T(8,128)S(1)}, u32[]{:S(2)}, u32[]{:S(2)}) collective-permute-start(f32[2,16,512]{2,1,0:T(8,128)S(1)} %collective-permute-done.12.refs_2_), channel_id=1, source_target_pairs={{0,1},{1,0},{2,3},{3,2},{4,5},{5,4},{6,7},{7,6},{8,9},{9,8},{10,11... | collective-permute-start | bytes 196616 | tf_op jit(solution)/shard_map/ppermute | solution.py:245
  30.7 1.3 %collective-permute-start.17 = (f32[2,16,512]{2,1,0:T(8,128)S(1)}, f32[2,16,512]{2,1,0:T(8,128)S(1)}, u32[]{:S(2)}, u32[]{:S(2)}) collective-permute-start(f32[2,16,512]{2,1,0:T(8,128)S(1)} %collective-permute-done.13.refs_3_), channel_id=1, source_target_pairs={{0,1},{1,0},{2,3},{3,2},{4,5},{5,4},{6,7},{7,6},{8,9},{9,8},{10,11... | collective-permute-start | bytes 196616 | tf_op jit(solution)/shard_map/ppermute | solution.py:245
  (4 other events, 33.7 us)

commit v9 on v8

--- a/solution.py
+++ b/solution.py
@@ -128,6 +128,15 @@
 
 SMALL = pltpu.CompilerParams(vmem_limit_bytes=20 * 1024 * 1024)
 WIDTH = 256
+GELU_TERMS = (
+    0.7978849411010742,
+    0.03633308410644531,
+    -3.259492223151028e-05,
+    -5.530622001970187e-05,
+    3.964749794249656e-06,
+    -1.3226382122866198e-07,
+    1.7561855303327434e-09,
+)
 
 
 def angles(count, places, extent):
@@ -199,7 +208,8 @@
         out[:, row, 0, 1, row, :] = -sine
         out[:, row, 1, 1, row, :] = cosine
         out[:, row, 1, 0, row, :] = sine
-    return out.reshape(extent * rows_ky * 2, 2 * rows_ky * MX)
+    out = out.reshape(peers // 2, 2, cells_x * rows_ky * 2, 2 * rows_ky * MX)
+    return np.moveaxis(out, 1, 0).reshape(2, -1, 2 * rows_ky * MX)
 
 
 def inverse_y_table(cells_y, groups_y, peers, rows_ky):
@@ -282,12 +292,23 @@
     return small_call(join_kernel, [shape] * keep.shape[0], "join_blocks")(keep, arrived)
 
 
+def back_rows(inverse_high, inverse_low, column, modes):
+    high, low = split_terms(modes)
+    table = inverse_high[column]
+    return dot(table, high) + dot(table, low) + dot(inverse_low[column], high)
+
+
+def store_turns(out_ref, order_ref, z):
+    for index, turn in enumerate(turns(out_ref.shape[0])):
+        out_ref[index] = order_ref[z ^ turn]
+
+
 def mix_kernel(layers, *refs):
     block_refs, arrived_refs = refs[:layers], refs[layers : 2 * layers]
     weight_ref, forward_high, forward_low, inverse_high, inverse_low = refs[
         2 * layers : 2 * layers + 5
     ]
-    mixed_ref, send_ref, keep_ref, order_ref, spread_ref, result_ref = refs[2 * layers + 5 :]
+    modes_ref, send_ref, order_ref, spread_ref, result_ref = refs[2 * layers + 5 :]
     z, x, y = quad()
     column = x ^ y
     for index, turn in enumerate(turns(layers)):
@@ -329,115 +350,128 @@
         imag = jnp.where(lane, pltpu.roll(first, channels, 1), second)
         crossed = jnp.where(rows < tiles, pltpu.roll(imag, 8 - tiles, 0), pltpu.roll(imag, tiles, 0))
         result_ref[base : base + 8, :] = real + sign * crossed
-    parts = []
     for part in range(2):
-        parts.append(
-            jnp.concatenate(
-                [
-                    result_ref[pl.ds(part * tiles + tile, count, stride=group), :]
-                    for tile in range(tiles)
-                ],
-                axis=1,
+        for tile in range(tiles):
+            modes_ref[part * count : (part + 1) * count, tile * 128 : (tile + 1) * 128] = (
+                result_ref[pl.ds(part * tiles + tile, count, stride=group), :]
             )
-        )
-        mixed_ref[0, :, part * feat_count : (part + 1) * feat_count] = parts[part]
-    high, low = split_terms(jnp.concatenate(parts, axis=0))
-    back = dot(inverse_high[...], high) + dot(inverse_high[...], low) + dot(inverse_low[...], high)
-    order_ref[...] = back.reshape(order_ref.shape)
-    for index, turn in enumerate(turns(layers)):
-        send_ref[index] = order_ref[(z ^ turn) * 2 + (column ^ 1)]
-        keep_ref[index] = order_ref[(z ^ turn) * 2 + column]
-
-
-def mix(blocks, arrived, weights, forward_table, inverse_table):
+    back = back_rows(inverse_high, inverse_low, column ^ 1, modes_ref[...])
+    order_ref[:layers] = back.reshape(send_ref.shape)
+    store_turns(send_ref, order_ref, z)
+
+
+def mix(blocks, arrived, weights, forward_table, inverse_tables):
     layers = len(blocks)
     _, rows, feat_count = blocks[0].shape
     count = weights.shape[1]
-    half = jax.ShapeDtypeStruct((layers, rows, feat_count), jnp.float32)
     scratch = pltpu.VMEM((count * feat_count // 64, 128), jnp.float32)
     return pl.pallas_call(
         functools.partial(mix_kernel, layers),
-        out_shape=[jax.ShapeDtypeStruct((1, count, 2 * feat_count), jnp.float32), half, half],
+        out_shape=[
+            jax.ShapeDtypeStruct((2 * count, feat_count), jnp.float32),
+            jax.ShapeDtypeStruct((layers, rows, feat_count), jnp.float32),
+        ],
         scratch_shapes=[pltpu.VMEM((2 * layers, rows, feat_count), jnp.float32), scratch, scratch],
         compiler_params=SMALL,
         name="mix",
-    )(*blocks, *arrived, weights, *split_table(forward_table), *split_table(inverse_table))
-
-
-def output_kernel(
-    layers, place_ref, flow_ref, table_ref, local_ref, bias_ref, *refs
-):
+    )(*blocks, *arrived, weights, *split_table(forward_table), *inverse_tables)
+
+
+def keep_kernel(modes_ref, inverse_high, inverse_low, mixed_ref, keep_ref, order_ref):
+    z, x, y = quad()
+    count = mixed_ref.shape[1]
+    feat_count = modes_ref.shape[1]
+    for part in range(2):
+        mixed_ref[0, :, part * feat_count : (part + 1) * feat_count] = modes_ref[
+            part * count : (part + 1) * count
+        ]
+    back = back_rows(inverse_high, inverse_low, x ^ y, modes_ref[...])
+    order_ref[...] = back.reshape(keep_ref.shape)
+    store_turns(keep_ref, order_ref, z)
+
+
+def keep_rows(modes, inverse_tables, like):
+    rows, feat_count = modes.shape
+    return pl.pallas_call(
+        keep_kernel,
+        out_shape=[
+            jax.ShapeDtypeStruct((1, rows // 2, 2 * feat_count), jnp.float32),
+            jax.ShapeDtypeStruct(like.shape, jnp.float32),
+        ],
+        scratch_shapes=[pltpu.VMEM(like.shape, jnp.float32)],
+        compiler_params=SMALL,
+        cost_estimate=pl.CostEstimate(
+            flops=6 * rows * rows * feat_count, bytes_accessed=2**20, transcendentals=0
+        ),
+        name="keep_rows",
+    )(modes, *inverse_tables)
+
+
+def gelu(values):
+    square = jnp.minimum(values * values, 31.36)
+    inner = jnp.full_like(square, GELU_TERMS[-1])
+    for term in GELU_TERMS[-2::-1]:
+        inner = inner * square + term
+    half = 0.5 * values
+    return half + half * jnp.tanh(values * inner)
+
+
+def output_kernel(layers, flow_ref, table_ref, local_ref, bias_ref, *refs):
     own_refs, core_refs = refs[:layers], refs[layers : 2 * layers]
-    out_ref, order_ref, stack_ref, wide_ref, level_ref = refs[2 * layers :]
-    step = pl.program_id(0)
-    feat_count = flow_ref.shape[-1]
+    out_hbm, order_ref, stack_ref, wide_ref, level_ref, done_ref, sent = refs[2 * layers :]
+    cells_x, _, feat_count = flow_ref.shape
     channels = local_ref.shape[0]
-    width = wide_ref.shape[0]
     pairs = stack_ref.shape[0]
     rows = order_ref.shape[1] // pairs
-
-    @pl.when(step == 0)
-    def _():
-        z, x, y = quad()
-        for index, turn in enumerate(turns(layers)):
-            for side in range(2):
-                peer = 2 * layers * side + (z ^ turn) * 2
-                order_ref[peer + (x ^ y)] = own_refs[index][side]
-                order_ref[peer + (x ^ y ^ 1)] = core_refs[index][1 - side]
-        for pair in range(pairs):
+    z, x, y = quad()
+    wide_ref[...] = jnp.zeros_like(wide_ref)
+    for start in range(0, WIDTH, channels):
+        span = slice(start, start + channels)
+        wide_ref[span, span] = local_ref[...]
+        level_ref[:, span] = bias_ref[...].reshape(1, channels)
+    for index, turn in enumerate(turns(layers)):
+        for side in range(2):
+            peer = 2 * layers * side + (z ^ turn) * 2
+            order_ref[peer + (x ^ y)] = own_refs[index][side]
+            order_ref[peer + (x ^ y ^ 1)] = core_refs[index][1 - side]
+    copies = []
+    for cell in range(cells_x):
+        pair = cell // 2
+        if cell % 2 == 0:
             span = slice(pair * rows, (pair + 1) * rows)
             high, low = split_terms(order_ref[:, span, :].reshape(-1, feat_count))
             stack_ref[pair] = jnp.concatenate([high, low, high], axis=0)
-        wide_ref[...] = jnp.zeros_like(wide_ref)
-        for start in range(0, width, channels):
-            span = slice(start, start + channels)
-            wide_ref[span, span] = local_ref[...]
-            level_ref[:, span] = bias_ref[...].reshape(1, channels)
-
-    table = table_ref[0, step % 2]
-    for start in range(0, feat_count, width):
-        columns = slice(start, start + width)
-        total = (
-            dot(table, stack_ref[step // 2, :, columns])
-            + dot(flow_ref[0, :, columns], wide_ref[...])
-            + level_ref[...]
-        )
-        out_ref[0, :, columns] = (
-            0.5 * total * (1.0 + lax.erf(total * math.sqrt(0.5)))
-        ).astype(out_ref.dtype)
+        for start in range(0, feat_count, WIDTH):
+            columns = slice(start, start + WIDTH)
+            left = jnp.concatenate([table_ref[y, cell % 2], flow_ref[cell, :, columns]], axis=1)
+            right = jnp.concatenate([stack_ref[pair, :, columns], wide_ref[...]], axis=0)
+            total = dot(left, right) + level_ref[...]
+            done_ref[cell, :, columns] = gelu(total).astype(done_ref.dtype)
+        copies.append(pltpu.make_async_copy(done_ref.at[cell], out_hbm.at[cell], sent.at[cell]))
+        copies[-1].start()
+    for copy in copies:
+        copy.wait()
 
 
 def make_output(flow_field, parts, table, local, bias):
-    cells_x, cells_y, feat_count = flow_field.shape
+    cells_x, _, feat_count = flow_field.shape
     layers = len(parts) // 2
     rows = parts[0].shape[1]
-    place = jnp.reshape(lax.axis_index("gy"), (1,))
-    whole = lambda array: pl.BlockSpec(array.shape, lambda i, p: (0,) * array.ndim)
-    block = pl.BlockSpec((1, cells_y, feat_count), lambda i, p: (i, 0, 0))
     return pl.pallas_call(
         functools.partial(output_kernel, layers),
-        grid_spec=pltpu.PrefetchScalarGridSpec(
-            num_scalar_prefetch=1,
-            grid=(cells_x,),
-            in_specs=[
-                block,
-                pl.BlockSpec((1,) + table.shape[1:], lambda i, p: (p[0], 0, 0, 0)),
-                whole(local),
-                whole(bias),
-            ]
-            + [whole(part) for part in parts],
-            out_specs=block,
-            scratch_shapes=[
-                pltpu.VMEM((4 * layers, rows, feat_count), jnp.float32),
-                pltpu.VMEM((cells_x // 2, table.shape[-1], feat_count), jnp.bfloat16),
-                pltpu.VMEM((WIDTH, WIDTH), jnp.bfloat16),
-                pltpu.VMEM((1, WIDTH), jnp.float32),
-            ],
-        ),
+        out_specs=pl.BlockSpec(memory_space=pl.ANY),
+        scratch_shapes=[
+            pltpu.VMEM((4 * layers, rows, feat_count), jnp.float32),
+            pltpu.VMEM((cells_x // 2, table.shape[-1], feat_count), jnp.bfloat16),
+            pltpu.VMEM((WIDTH, WIDTH), jnp.bfloat16),
+            pltpu.VMEM((1, WIDTH), jnp.float32),
+            pltpu.VMEM(flow_field.shape, jnp.bfloat16),
+            pltpu.SemaphoreType.DMA((cells_x,)),
+        ],
         out_shape=jax.ShapeDtypeStruct(flow_field.shape, jnp.bfloat16),
         compiler_params=SMALL,
         name="make_output",
-    )(place, flow_field, table, local, bias, *parts)
+    )(flow_field, table, local, bias, *parts)
 
 
 def row_body(flow_field, spectral_weight, local_weight, bias_terms):
@@ -451,14 +485,17 @@
     table = forward_y_table(cells_y, groups_y, peers, rows_ky)
     send, keep = forward_y(flow_field, table, peers // 2, rows_ky)
     blocks = along_columns(add_blocks(keep, flip_core(send)), peers)
-    mixed, send, keep = mix(
+    inverse_tables = split_table(inverse_x_table(cells_x, peers, rows_ky))
+    modes, send = mix(
         blocks,
         [flip_core(block) for block in blocks],
         spectral_weight,
         forward_x_table(cells_x, peers, rows_ky) * forward_scale,
-        inverse_x_table(cells_x, peers, rows_ky),
-    )
-    own = along_columns(join_blocks(keep, flip_core(send)), peers)
+        inverse_tables,
+    )
+    arrived = flip_core(send)
+    mixed, keep = keep_rows(modes, inverse_tables, send)
+    own = along_columns(join_blocks(keep, arrived), peers)
     parts = own + [flip_core(block) for block in own]
     high, low = split_table(inverse_y_table(cells_y, groups_y, peers, rows_ky) * inverse_scale)
     table = np.concatenate([high, high, low], axis=-1)

time: 35.1 us -> 34.6 us (0.986)
  waiting for transfers between devices: 10.7 us -> 10.1 us
    ppermute x10, waiting for transfers between devices: 4.14 us -> 3.35 us  [flip_core(): return lax.ppermute(block, 'gy', [(0, 1), (1, 0)])]
    pallas_call x1 -> x2, Pallas kernels: 2.92 us -> 3.62 us  [the longest x1 2.83 us: make_output(): pl.pallas_call(functools.partial(output_kernel, layers), out_specs=pl.Blo...]
    pallas_call x1, Pallas kernels: 1.56 us -> 1.06 us  [mix(): pl.pallas_call(functools.partial(mix_kernel, layers), out_shape=[jax.Shap...]
  transfers between devices with their start and end apart: 18 -> 18, of which waited for: 13 -> 13; matrix products, arithmetic and copies ran while one was open for 0% -> 0% of each run, Pallas kernels for 0% -> 2%
where the time goes in v9:
time: 34.6 us; the launch traced here: 34.4 us
  starting transfers between devices  16.8 us (49%)
  waiting for transfers between devices  10.1 us (29%)
  Pallas kernels  5.02 us (15%)
  local copies, waits for them, and re-layouts  1.25 us (4%)
  between operations  0.8 us (2%)
  other arithmetic  0.38 us (1%)
    ppermute x8, starting transfers between devices, along_columns(): arrived.append(lax.ppermute(block, ('gx', 'gy'), pairs))  11.2 us
    ppermute x8, waiting for transfers between devices, along_columns(): arrived.append(lax.ppermute(block, ('gx', 'gy'), pairs))  6.79 us
    ppermute x10, starting transfers between devices, flip_core(): return lax.ppermute(block, 'gy', [(0, 1), (1, 0)])  5.64 us
    ppermute x10, waiting for transfers between devices, flip_core(): return lax.ppermute(block, 'gy', [(0, 1), (1, 0)])  3.35 us
    pallas_call x1, Pallas kernels, make_output(): pl.pallas_call(functools.partial(output_kernel, layers), out_specs=pl.Blo...  2.83 us
    unnamed x20, local copies, waits for them, and re-layouts  1.25 us
    pallas_call x1, Pallas kernels, mix(): pl.pallas_call(functools.partial(mix_kernel, layers), out_shape=[jax.Shap...  1.06 us
    pallas_call x1, Pallas kernels, keep_rows(): pl.pallas_call(keep_kernel, out_shape=[jax.ShapeDtypeStruct((1, rows // 2...  0.79 us
  transfers between devices with their start and end apart: 18, of which 13 were waited for; matrix products, arithmetic and copies ran while one was open for 0% of the time, Pallas kernels for 2%

profile of v9, /device:TPU:0, one launch (start us, length us, event | category | flops | bytes accessed | tf_op | source)
XLA Modules:
  0.0 34.4 jit_solution(9710833412722836760)
XLA Ops:
  0.7 0.3 select_convert_fusion.table_ref
  1.1 1.2 %copy-done = bf16[4,256,512]{2,1,0:T(8,128)(2,1)S(1)} copy-done((bf16[4,256,512]{2,1,0:T(8,128)(2,1)S(1)}, bf16[4,256,512]{2,1,0:T(8,128)(2,1)}, u32[]{:S(2)}) %copy-start) | copy-done | bytes 1048600
  2.6 0.5 %collective-permute-start = (f32[4,2,16,512]{3,2,1,0:T(8,128)S(1)}, f32[4,2,16,512]{3,2,1,0:T(8,128)S(1)}, u32[]{:S(2)}, u32[]{:S(2)}) collective-permute-start(f32[4,2,16,512]{3,2,1,0:T(8,128)S(1)} %get-tuple-element.17), channel_id=1, source_target_pairs={{0,1},{1,0},{2,3},{3,2},{4,5},{5,4},{6,7},{7,6},{8,9},{9,8},{10,11... | collective-permute-start | bytes 786440 | tf_op jit(solution)/shard_map/ppermute | solution.py:255
  3.1 1.2 %collective-permute-done.arrived_ref = f32[4,2,16,512]{3,2,1,0:T(8,128)S(1)} collective-permute-done((f32[4,2,16,512]{3,2,1,0:T(8,128)S(1)}, f32[4,2,16,512]{3,2,1,0:T(8,128)S(1)}, u32[]{:S(2)}, u32[]{:S(2)}) %collective-permute-start) | collective-permute-done | bytes 262176 | tf_op jit(solution)/shard_map/ppermute | solution.py:255
  4.3 4.0 %collective-permute-start.1 = (f32[2,16,512]{2,1,0:T(8,128)S(1)}, f32[2,16,512]{2,1,0:T(8,128)S(1)}, u32[]{:S(2)}, u32[]{:S(2)}) collective-permute-start(f32[2,16,512]{2,1,0:T(8,128)S(1)} %get-tuple-element.18), channel_id=1, source_target_pairs={{0,8},{1,11},{2,10},{3,9},{4,12},{5,15},{6,14},{7,13},{8,0},{9,3},... | collective-permute-start | bytes 196616 | tf_op jit(solution)/shard_map/ppermute | solution.py:266
  8.4 1.3 %collective-permute-start.2 = (f32[2,16,512]{2,1,0:T(8,128)S(1)}, f32[2,16,512]{2,1,0:T(8,128)S(1)}, u32[]{:S(2)}, u32[]{:S(2)}) collective-permute-start(f32[2,16,512]{2,1,0:T(8,128)S(1)} %get-tuple-element.19), channel_id=1, source_target_pairs={{0,12},{1,15},{2,14},{3,13},{4,8},{5,11},{6,10},{7,9},{8,4},{9,7},... | collective-permute-start | bytes 196616 | tf_op jit(solution)/shard_map/ppermute | solution.py:266
  9.9 0.8 %collective-permute-start.4 = (f32[2,16,512]{2,1,0:T(8,128)S(1)}, f32[2,16,512]{2,1,0:T(8,128)S(1)}, u32[]{:S(2)}, u32[]{:S(2)}) collective-permute-start(f32[2,16,512]{2,1,0:T(8,128)S(1)} %get-tuple-element.21), channel_id=1, source_target_pairs={{0,0},{1,3},{2,2},{3,1},{4,4},{5,7},{6,6},{7,5},{8,8},{9,11},{10,1... | collective-permute-start | bytes 196616 | tf_op jit(solution)/shard_map/ppermute | solution.py:266
  11.0 2.8 %collective-permute-start.5 = (f32[2,16,512]{2,1,0:T(8,128)S(1)}, f32[2,16,512]{2,1,0:T(8,128)S(1)}, u32[]{:S(2)}, u32[]{:S(2)}) collective-permute-start(f32[2,16,512]{2,1,0:T(8,128)S(1)} %collective-permute-done.1.refs_0_), channel_id=1, source_target_pairs={{0,1},{1,0},{2,3},{3,2},{4,5},{5,4},{6,7},{7,6},{8,9},{9,8},{10,11... | collective-permute-start | bytes 196616 | tf_op jit(solution)/shard_map/ppermute | solution.py:255
  13.7 1.3 %collective-permute-done.2.refs_1_ = f32[2,16,512]{2,1,0:T(8,128)S(1)} collective-permute-done((f32[2,16,512]{2,1,0:T(8,128)S(1)}, f32[2,16,512]{2,1,0:T(8,128)S(1)}, u32[]{:S(2)}, u32[]{:S(2)}) %collective-permute-start.2) | collective-permute-done | bytes 65568 | tf_op jit(solution)/shard_map/ppermute | solution.py:266
  15.1 0.5 %collective-permute-start.6 = (f32[2,16,512]{2,1,0:T(8,128)S(1)}, f32[2,16,512]{2,1,0:T(8,128)S(1)}, u32[]{:S(2)}, u32[]{:S(2)}) collective-permute-start(f32[2,16,512]{2,1,0:T(8,128)S(1)} %collective-permute-done.2.refs_1_), channel_id=1, source_target_pairs={{0,1},{1,0},{2,3},{3,2},{4,5},{5,4},{6,7},{7,6},{8,9},{9,8},{10,11... | collective-permute-start | bytes 196616 | tf_op jit(solution)/shard_map/ppermute | solution.py:255
  15.9 0.3 collective-permute-start.8
  16.4 0.6 %collective-permute-done.7.refs_6_ = f32[2,16,512]{2,1,0:T(8,128)S(1)} collective-permute-done((f32[2,16,512]{2,1,0:T(8,128)S(1)}, f32[2,16,512]{2,1,0:T(8,128)S(1)}, u32[]{:S(2)}, u32[]{:S(2)}) %collective-permute-start.7) | collective-permute-done | bytes 65568 | tf_op jit(solution)/shard_map/ppermute | solution.py:255
  17.2 1.1 %mix.1 = (f32[128,512]{1,0:T(8,128)S(1)}, f32[4,16,512]{2,1,0:T(8,128)S(1)}) custom-call(f32[2,16,512]{2,1,0:T(8,128)S(1)} %collective-permute-done.1.refs_0_, f32[2,16,512]{2,1,0:T(8,128)S(1)} %collective-permute-done.2.refs_1_, f32[2,16,512]{2,1,0:T(8,128)S(1)} %collective-permute-done.3.refs_2_, f32[2,16,512]{2,1,0:T(8,128)S(1)} %collective-permute-done.4.refs_3_, ...), custom_call_target="tpu_custom_call" | custom-call | tf_op jit(solution)/shard_map/mix/pallas_call | solution.py:368
  18.3 0.4 %collective-permute-start.9 = (f32[4,16,512]{2,1,0:T(8,128)S(1)}, f32[4,16,512]{2,1,0:T(8,128)S(1)}, u32[]{:S(2)}, u32[]{:S(2)}) collective-permute-start(f32[4,16,512]{2,1,0:T(8,128)S(1)} %get-tuple-element.24), channel_id=1, source_target_pairs={{0,1},{1,0},{2,3},{3,2},{4,5},{5,4},{6,7},{7,6},{8,9},{9,8},{10,11... | collective-permute-start | bytes 393224 | tf_op jit(solution)/shard_map/ppermute | solution.py:255
  18.7 0.8 %keep_rows.1 = (f32[1,64,1024]{2,1,0:T(8,128)}, f32[4,16,512]{2,1,0:T(8,128)S(1)}) custom-call(f32[128,512]{1,0:T(8,128)S(1)} %get-tuple-element.22.modes_ref, bf16[2,64,128]{2,1,0:T(8,128)(2,1)S(1)} %copy-done.5, bf16[2,64,128]{2,1,0:T(8,128)(2,1)S(1)} %copy-done.4), custom_call_target="tpu_custom_call" | custom-call | flops 50331648 | bytes 1048576 | tf_op jit(solution)/shard_map/keep_rows/pallas_call | solution.py:395
  19.7 3.1 %collective-permute-start.10 = (f32[2,16,512]{2,1,0:T(8,128)S(1)}, f32[2,16,512]{2,1,0:T(8,128)S(1)}, u32[]{:S(2)}, u32[]{:S(2)}) collective-permute-start(f32[2,16,512]{2,1,0:T(8,128)S(1)} %get-tuple-element.25), channel_id=1, source_target_pairs={{0,8},{1,11},{2,10},{3,9},{4,12},{5,15},{6,14},{7,13},{8,0},{9,3},... | collective-permute-start | bytes 196616 | tf_op jit(solution)/shard_map/ppermute | solution.py:266
  22.8 1.0 %collective-permute-start.11 = (f32[2,16,512]{2,1,0:T(8,128)S(1)}, f32[2,16,512]{2,1,0:T(8,128)S(1)}, u32[]{:S(2)}, u32[]{:S(2)}) collective-permute-start(f32[2,16,512]{2,1,0:T(8,128)S(1)} %get-tuple-element.26), channel_id=1, source_target_pairs={{0,12},{1,15},{2,14},{3,13},{4,8},{5,11},{6,10},{7,9},{8,4},{9,7},... | collective-permute-start | bytes 196616 | tf_op jit(solution)/shard_map/ppermute | solution.py:266
  23.9 0.7 %collective-permute-start.13 = (f32[2,16,512]{2,1,0:T(8,128)S(1)}, f32[2,16,512]{2,1,0:T(8,128)S(1)}, u32[]{:S(2)}, u32[]{:S(2)}) collective-permute-start(f32[2,16,512]{2,1,0:T(8,128)S(1)} %get-tuple-element.28), channel_id=1, source_target_pairs={{0,0},{1,3},{2,2},{3,1},{4,4},{5,7},{6,6},{7,5},{8,8},{9,11},{10,1... | collective-permute-start | bytes 196616 | tf_op jit(solution)/shard_map/ppermute | solution.py:266
  24.5 2.6 %collective-permute-done.10.refs_0_ = f32[2,16,512]{2,1,0:T(8,128)S(1)} collective-permute-done((f32[2,16,512]{2,1,0:T(8,128)S(1)}, f32[2,16,512]{2,1,0:T(8,128)S(1)}, u32[]{:S(2)}, u32[]{:S(2)}) %collective-permute-start.10) | collective-permute-done | bytes 65568 | tf_op jit(solution)/shard_map/ppermute | solution.py:266
  27.2 2.4 %collective-permute-done.11.refs_1_ = f32[2,16,512]{2,1,0:T(8,128)S(1)} collective-permute-done((f32[2,16,512]{2,1,0:T(8,128)S(1)}, f32[2,16,512]{2,1,0:T(8,128)S(1)}, u32[]{:S(2)}, u32[]{:S(2)}) %collective-permute-start.11) | collective-permute-done | bytes 65568 | tf_op jit(solution)/shard_map/ppermute | solution.py:266
  29.7 0.3 %collective-permute-start.15 = (f32[2,16,512]{2,1,0:T(8,128)S(1)}, f32[2,16,512]{2,1,0:T(8,128)S(1)}, u32[]{:S(2)}, u32[]{:S(2)}) collective-permute-start(f32[2,16,512]{2,1,0:T(8,128)S(1)} %collective-permute-done.11.refs_1_), channel_id=1, source_target_pairs={{0,1},{1,0},{2,3},{3,2},{4,5},{5,4},{6,7},{7,6},{8,9},{9,8},{10,11... | collective-permute-start | bytes 196616 | tf_op jit(solution)/shard_map/ppermute | solution.py:255
  30.6 0.4 %collective-permute-done.15.refs_5_ = f32[2,16,512]{2,1,0:T(8,128)S(1)} collective-permute-done((f32[2,16,512]{2,1,0:T(8,128)S(1)}, f32[2,16,512]{2,1,0:T(8,128)S(1)}, u32[]{:S(2)}, u32[]{:S(2)}) %collective-permute-start.15) | collective-permute-done | bytes 65568 | tf_op jit(solution)/shard_map/ppermute | solution.py:255
  30.9 0.4 %collective-permute-done.16.refs_6_ = f32[2,16,512]{2,1,0:T(8,128)S(1)} collective-permute-done((f32[2,16,512]{2,1,0:T(8,128)S(1)}, f32[2,16,512]{2,1,0:T(8,128)S(1)}, u32[]{:S(2)}, u32[]{:S(2)}) %collective-permute-start.16) | collective-permute-done | bytes 65568 | tf_op jit(solution)/shard_map/ppermute | solution.py:255
  31.6 2.8 %make_output.1 = bf16[4,256,512]{2,1,0:T(8,128)(2,1)} custom-call(bf16[4,256,512]{2,1,0:T(8,128)(2,1)S(1)} %copy-done.1, bf16[2,2,256,384]{3,2,1,0:T(8,128)(2,1)S(1)} %copy-done.3, bf16[64,64]{1,0:T(8,128)(2,1)S(1)} %copy-done.8, f32[64]{0:T(128)S(1)} %copy-done.9, f32[2,16,512]{2,1,0:T(8,128)S(1)} %collective-permute-done.10.refs_0_, ...), custom_call_target="tpu_custom_call" | custom-call | tf_op jit(solution)/shard_map/make_output/pallas_call | solution.py:460
  (42 shorter events, 2.9 us)
Async XLA Ops:
  2.3 14.9 %copy-start.2 = (bf16[1,64,64,128]{3,2,1,0:T(8,128)(2,1)S(1)}, bf16[1,64,64,128]{3,2,1,0:T(8,128)(2,1)}, u32[]{:S(2)}) copy-start(bf16[1,64,64,128]{3,2,1,0:T(8,128)(2,1)} %refs_8_.1) | copy-start | bytes 3145732
  2.6 1.7 %collective-permute-start = (f32[4,2,16,512]{3,2,1,0:T(8,128)S(1)}, f32[4,2,16,512]{3,2,1,0:T(8,128)S(1)}, u32[]{:S(2)}, u32[]{:S(2)}) collective-permute-start(f32[4,2,16,512]{3,2,1,0:T(8,128)S(1)} %get-tuple-element.17), channel_id=1, source_target_pairs={{0,1},{1,0},{2,3},{3,2},{4,5},{5,4},{6,7},{7,6},{8,9},{9,8},{10,11... | collective-permute-start | bytes 786440 | tf_op jit(solution)/shard_map/ppermute | solution.py:255
  4.3 12.9 %copy-start.5 = (bf16[2,64,128]{2,1,0:T(8,128)(2,1)S(1)}, bf16[2,64,128]{2,1,0:T(8,128)(2,1)}, u32[]{:S(2)}) copy-start(bf16[2,64,128]{2,1,0:T(8,128)(2,1)} %constant.144.clone.refs_11_.inverse_high) | copy-start | bytes 98308
  4.3 12.9 %copy-start.6 = (bf16[128,128]{1,0:T(8,128)(2,1)S(1)}, bf16[128,128]{1,0:T(8,128)(2,1)}, u32[]{:S(2)}) copy-start(bf16[128,128]{1,0:T(8,128)(2,1)} %constant.143.clone.refs_10_) | copy-start | bytes 98308
  4.3 12.9 %copy-start.7 = (bf16[128,128]{1,0:T(8,128)(2,1)S(1)}, bf16[128,128]{1,0:T(8,128)(2,1)}, u32[]{:S(2)}) copy-start(bf16[128,128]{1,0:T(8,128)(2,1)} %constant.142.clone.refs_9_) | copy-start | bytes 98308
  4.3 6.6 %collective-permute-start.1 = (f32[2,16,512]{2,1,0:T(8,128)S(1)}, f32[2,16,512]{2,1,0:T(8,128)S(1)}, u32[]{:S(2)}, u32[]{:S(2)}) collective-permute-start(f32[2,16,512]{2,1,0:T(8,128)S(1)} %get-tuple-element.18), channel_id=1, source_target_pairs={{0,8},{1,11},{2,10},{3,9},{4,12},{5,15},{6,14},{7,13},{8,0},{9,3},... | collective-permute-start | bytes 196616 | tf_op jit(solution)/shard_map/ppermute | solution.py:266
  8.4 6.7 %collective-permute-start.2 = (f32[2,16,512]{2,1,0:T(8,128)S(1)}, f32[2,16,512]{2,1,0:T(8,128)S(1)}, u32[]{:S(2)}, u32[]{:S(2)}) collective-permute-start(f32[2,16,512]{2,1,0:T(8,128)S(1)} %get-tuple-element.19), channel_id=1, source_target_pairs={{0,12},{1,15},{2,14},{3,13},{4,8},{5,11},{6,10},{7,9},{8,4},{9,7},... | collective-permute-start | bytes 196616 | tf_op jit(solution)/shard_map/ppermute | solution.py:266
  9.7 6.0 %collective-permute-start.3 = (f32[2,16,512]{2,1,0:T(8,128)S(1)}, f32[2,16,512]{2,1,0:T(8,128)S(1)}, u32[]{:S(2)}, u32[]{:S(2)}) collective-permute-start(f32[2,16,512]{2,1,0:T(8,128)S(1)} %get-tuple-element.20), channel_id=1, source_target_pairs={{0,4},{1,7},{2,6},{3,5},{4,0},{5,3},{6,2},{7,1},{8,12},{9,15},{10,... | collective-permute-start | bytes 196616 | tf_op jit(solution)/shard_map/ppermute | solution.py:266
  9.9 21.6 %copy-start.1 = (bf16[4,256,512]{2,1,0:T(8,128)(2,1)S(1)}, bf16[4,256,512]{2,1,0:T(8,128)(2,1)}, u32[]{:S(2)}) copy-start(bf16[4,256,512]{2,1,0:T(8,128)(2,1)} %flow_ref.3) | copy-start | bytes 3145732
  9.9 21.6 %copy-start.3 = (bf16[2,2,256,384]{3,2,1,0:T(8,128)(2,1)S(1)}, bf16[2,2,256,384]{3,2,1,0:T(8,128)(2,1)}, u32[]{:S(2)}) copy-start(bf16[2,2,256,384]{3,2,1,0:T(8,128)(2,1)} %constant.146.clone.table_ref) | copy-start | bytes 2359300
  9.9 6.0 %collective-permute-start.4 = (f32[2,16,512]{2,1,0:T(8,128)S(1)}, f32[2,16,512]{2,1,0:T(8,128)S(1)}, u32[]{:S(2)}, u32[]{:S(2)}) collective-permute-start(f32[2,16,512]{2,1,0:T(8,128)S(1)} %get-tuple-element.21), channel_id=1, source_target_pairs={{0,0},{1,3},{2,2},{3,1},{4,4},{5,7},{6,6},{7,5},{8,8},{9,11},{10,1... | collective-permute-start | bytes 196616 | tf_op jit(solution)/shard_map/ppermute | solution.py:266
  11.0 5.3 %collective-permute-start.5 = (f32[2,16,512]{2,1,0:T(8,128)S(1)}, f32[2,16,512]{2,1,0:T(8,128)S(1)}, u32[]{:S(2)}, u32[]{:S(2)}) collective-permute-start(f32[2,16,512]{2,1,0:T(8,128)S(1)} %collective-permute-done.1.refs_0_), channel_id=1, source_target_pairs={{0,1},{1,0},{2,3},{3,2},{4,5},{5,4},{6,7},{7,6},{8,9},{9,8},{10,11... | collective-permute-start | bytes 196616 | tf_op jit(solution)/shard_map/ppermute | solution.py:255
  15.1 1.4 %collective-permute-start.6 = (f32[2,16,512]{2,1,0:T(8,128)S(1)}, f32[2,16,512]{2,1,0:T(8,128)S(1)}, u32[]{:S(2)}, u32[]{:S(2)}) collective-permute-start(f32[2,16,512]{2,1,0:T(8,128)S(1)} %collective-permute-done.2.refs_1_), channel_id=1, source_target_pairs={{0,1},{1,0},{2,3},{3,2},{4,5},{5,4},{6,7},{7,6},{8,9},{9,8},{10,11... | collective-permute-start | bytes 196616 | tf_op jit(solution)/shard_map/ppermute | solution.py:255
  15.7 1.3 %collective-permute-start.7 = (f32[2,16,512]{2,1,0:T(8,128)S(1)}, f32[2,16,512]{2,1,0:T(8,128)S(1)}, u32[]{:S(2)}, u32[]{:S(2)}) collective-permute-start(f32[2,16,512]{2,1,0:T(8,128)S(1)} %collective-permute-done.3.refs_2_), channel_id=1, source_target_pairs={{0,1},{1,0},{2,3},{3,2},{4,5},{5,4},{6,7},{7,6},{8,9},{9,8},{10,11... | collective-permute-start | bytes 196616 | tf_op jit(solution)/shard_map/ppermute | solution.py:255
  15.9 1.3 %collective-permute-start.8 = (f32[2,16,512]{2,1,0:T(8,128)S(1)}, f32[2,16,512]{2,1,0:T(8,128)S(1)}, u32[]{:S(2)}, u32[]{:S(2)}) collective-permute-start(f32[2,16,512]{2,1,0:T(8,128)S(1)} %collective-permute-done.4.refs_3_), channel_id=1, source_target_pairs={{0,1},{1,0},{2,3},{3,2},{4,5},{5,4},{6,7},{7,6},{8,9},{9,8},{10,11... | collective-permute-start | bytes 196616 | tf_op jit(solution)/shard_map/ppermute | solution.py:255
  18.3 1.4 %collective-permute-start.9 = (f32[4,16,512]{2,1,0:T(8,128)S(1)}, f32[4,16,512]{2,1,0:T(8,128)S(1)}, u32[]{:S(2)}, u32[]{:S(2)}) collective-permute-start(f32[4,16,512]{2,1,0:T(8,128)S(1)} %get-tuple-element.24), channel_id=1, source_target_pairs={{0,1},{1,0},{2,3},{3,2},{4,5},{5,4},{6,7},{7,6},{8,9},{9,8},{10,11... | collective-permute-start | bytes 393224 | tf_op jit(solution)/shard_map/ppermute | solution.py:255
  19.7 7.4 %collective-permute-start.10 = (f32[2,16,512]{2,1,0:T(8,128)S(1)}, f32[2,16,512]{2,1,0:T(8,128)S(1)}, u32[]{:S(2)}, u32[]{:S(2)}) collective-permute-start(f32[2,16,512]{2,1,0:T(8,128)S(1)} %get-tuple-element.25), channel_id=1, source_target_pairs={{0,8},{1,11},{2,10},{3,9},{4,12},{5,15},{6,14},{7,13},{8,0},{9,3},... | collective-permute-start | bytes 196616 | tf_op jit(solution)/shard_map/ppermute | solution.py:266
  22.8 6.8 %collective-permute-start.11 = (f32[2,16,512]{2,1,0:T(8,128)S(1)}, f32[2,16,512]{2,1,0:T(8,128)S(1)}, u32[]{:S(2)}, u32[]{:S(2)}) collective-permute-start(f32[2,16,512]{2,1,0:T(8,128)S(1)} %get-tuple-element.26), channel_id=1, source_target_pairs={{0,12},{1,15},{2,14},{3,13},{4,8},{5,11},{6,10},{7,9},{8,4},{9,7},... | collective-permute-start | bytes 196616 | tf_op jit(solution)/shard_map/ppermute | solution.py:266
  23.8 6.2 %collective-permute-start.12 = (f32[2,16,512]{2,1,0:T(8,128)S(1)}, f32[2,16,512]{2,1,0:T(8,128)S(1)}, u32[]{:S(2)}, u32[]{:S(2)}) collective-permute-start(f32[2,16,512]{2,1,0:T(8,128)S(1)} %get-tuple-element.27), channel_id=1, source_target_pairs={{0,4},{1,7},{2,6},{3,5},{4,0},{5,3},{6,2},{7,1},{8,12},{9,15},{10,... | collective-permute-start | bytes 196616 | tf_op jit(solution)/shard_map/ppermute | solution.py:266
  23.9 6.4 %collective-permute-start.13 = (f32[2,16,512]{2,1,0:T(8,128)S(1)}, f32[2,16,512]{2,1,0:T(8,128)S(1)}, u32[]{:S(2)}, u32[]{:S(2)}) collective-permute-start(f32[2,16,512]{2,1,0:T(8,128)S(1)} %get-tuple-element.28), channel_id=1, source_target_pairs={{0,0},{1,3},{2,2},{3,1},{4,4},{5,7},{6,6},{7,5},{8,8},{9,11},{10,1... | collective-permute-start | bytes 196616 | tf_op jit(solution)/shard_map/ppermute | solution.py:266
  27.1 3.5 %collective-permute-start.14 = (f32[2,16,512]{2,1,0:T(8,128)S(1)}, f32[2,16,512]{2,1,0:T(8,128)S(1)}, u32[]{:S(2)}, u32[]{:S(2)}) collective-permute-start(f32[2,16,512]{2,1,0:T(8,128)S(1)} %collective-permute-done.10.refs_0_), channel_id=1, source_target_pairs={{0,1},{1,0},{2,3},{3,2},{4,5},{5,4},{6,7},{7,6},{8,9},{9,8},{10,11... | collective-permute-start | bytes 196616 | tf_op jit(solution)/shard_map/ppermute | solution.py:255
  29.7 1.3 %collective-permute-start.15 = (f32[2,16,512]{2,1,0:T(8,128)S(1)}, f32[2,16,512]{2,1,0:T(8,128)S(1)}, u32[]{:S(2)}, u32[]{:S(2)}) collective-permute-start(f32[2,16,512]{2,1,0:T(8,128)S(1)} %collective-permute-done.11.refs_1_), channel_id=1, source_target_pairs={{0,1},{1,0},{2,3},{3,2},{4,5},{5,4},{6,7},{7,6},{8,9},{9,8},{10,11... | collective-permute-start | bytes 196616 | tf_op jit(solution)/shard_map/ppermute | solution.py:255
  30.0 1.3 %collective-permute-start.16 = (f32[2,16,512]{2,1,0:T(8,128)S(1)}, f32[2,16,512]{2,1,0:T(8,128)S(1)}, u32[]{:S(2)}, u32[]{:S(2)}) collective-permute-start(f32[2,16,512]{2,1,0:T(8,128)S(1)} %collective-permute-done.12.refs_2_), channel_id=1, source_target_pairs={{0,1},{1,0},{2,3},{3,2},{4,5},{5,4},{6,7},{7,6},{8,9},{9,8},{10,11... | collective-permute-start | bytes 196616 | tf_op jit(solution)/shard_map/ppermute | solution.py:255
  30.3 1.3 %collective-permute-start.17 = (f32[2,16,512]{2,1,0:T(8,128)S(1)}, f32[2,16,512]{2,1,0:T(8,128)S(1)}, u32[]{:S(2)}, u32[]{:S(2)}) collective-permute-start(f32[2,16,512]{2,1,0:T(8,128)S(1)} %collective-permute-done.13.refs_3_), channel_id=1, source_target_pairs={{0,1},{1,0},{2,3},{3,2},{4,5},{5,4},{6,7},{7,6},{8,9},{9,8},{10,11... | collective-permute-start | bytes 196616 | tf_op jit(solution)/shard_map/ppermute | solution.py:255
  (4 other events, 33.7 us)

commit v10 on v9

--- a/solution.py
+++ b/solution.py
@@ -217,13 +217,14 @@
     angle = angles(MY, np.arange(extent), extent)
     full = np.stack([np.cos(angle), -np.sin(angle)], axis=1)
     full = full.reshape(groups_y, peers, rows_ky, 2, groups_y, cells_y)
-    out = np.zeros((groups_y, 2, cells_y, 2, peers, 2, rows_ky, 2))
-    for place in range(groups_y):
-        for side, half in enumerate((place, 1 - place)):
-            block = np.moveaxis(full[half, :, :, :, place, :], -1, 0)
-            for parity in range(2):
-                out[place, parity, :, side, :, parity] = block
-    return out.reshape(groups_y, 2, cells_y, 2 * peers * 4 * rows_ky)
+    out = np.zeros((groups_y, 2, cells_y, peers, 2, rows_ky, 2))
+    for y in range(groups_y):
+        for column in range(2):
+            for peer in range(peers):
+                for place in range(2):
+                    half = y ^ place ^ column ^ (peer % 2)
+                    out[y, column, :, peer, place] = np.moveaxis(full[half, peer, :, :, y], -1, 0)
+    return out.reshape(groups_y, 2, cells_y, 4 * peers * rows_ky)
 
 
 def dot(left, right):
@@ -282,14 +283,20 @@
 
 
 def join_kernel(keep_ref, arrived_ref, *out_refs):
+    cells_x, rows, _ = out_refs[0].shape
+    rows = rows // 2
     for turn, out_ref in enumerate(out_refs):
-        out_ref[0] = keep_ref[turn]
-        out_ref[1] = arrived_ref[turn]
-
-
-def join_blocks(keep, arrived):
-    shape = jax.ShapeDtypeStruct((2,) + keep.shape[1:], keep.dtype)
-    return small_call(join_kernel, [shape] * keep.shape[0], "join_blocks")(keep, arrived)
+        for cell in range(cells_x):
+            span = slice(cell * rows, (cell + 1) * rows)
+            out_ref[cell] = jnp.concatenate(
+                [keep_ref[turn, span, :], arrived_ref[turn, span, :]], axis=0
+            )
+
+
+def join_blocks(keep, arrived, cells_x):
+    layers, rows, feat_count = keep.shape
+    shape = jax.ShapeDtypeStruct((cells_x, 2 * rows // cells_x, feat_count), keep.dtype)
+    return small_call(join_kernel, [shape] * layers, "join_blocks")(keep, arrived)
 
 
 def back_rows(inverse_high, inverse_low, column, modes):
@@ -416,36 +423,63 @@
     return half + half * jnp.tanh(values * inner)
 
 
-def output_kernel(layers, flow_ref, table_ref, local_ref, bias_ref, *refs):
-    own_refs, core_refs = refs[:layers], refs[layers : 2 * layers]
-    out_hbm, order_ref, stack_ref, wide_ref, level_ref, done_ref, sent = refs[2 * layers :]
+def point_kernel(flow_ref, local_ref, bias_ref, _, out_ref, __, wide_ref, level_ref):
     cells_x, _, feat_count = flow_ref.shape
     channels = local_ref.shape[0]
-    pairs = stack_ref.shape[0]
-    rows = order_ref.shape[1] // pairs
-    z, x, y = quad()
     wide_ref[...] = jnp.zeros_like(wide_ref)
     for start in range(0, WIDTH, channels):
         span = slice(start, start + channels)
         wide_ref[span, span] = local_ref[...]
         level_ref[:, span] = bias_ref[...].reshape(1, channels)
+    for cell in range(cells_x):
+        for start in range(0, feat_count, WIDTH):
+            columns = slice(start, start + WIDTH)
+            out_ref[cell, :, columns] = dot(flow_ref[cell, :, columns], wide_ref[...]) + level_ref[...]
+
+
+def pointwise_terms(flow_field, local, bias, first):
+    spec = pl.BlockSpec(memory_space=pltpu.VMEM)
+    whole = pl.BlockSpec(memory_space=pl.ANY)
+    return pl.pallas_call(
+        point_kernel,
+        in_specs=[spec, spec, spec, whole],
+        out_specs=[spec, whole],
+        out_shape=[
+            jax.ShapeDtypeStruct(flow_field.shape, jnp.float32),
+            jax.ShapeDtypeStruct(first.shape, first.dtype),
+        ],
+        input_output_aliases={3: 1},
+        scratch_shapes=[
+            pltpu.VMEM((WIDTH, WIDTH), jnp.bfloat16),
+            pltpu.VMEM((1, WIDTH), jnp.float32),
+        ],
+        compiler_params=SMALL,
+        cost_estimate=pl.CostEstimate(
+            flops=2 * WIDTH * flow_field.size,
+            bytes_accessed=6 * flow_field.size,
+            transcendentals=0,
+        ),
+        name="pointwise_terms",
+    )(flow_field, local, bias, first)
+
+
+def output_kernel(layers, point_ref, table_ref, *refs):
+    own_refs, core_refs = refs[:layers], refs[layers : 2 * layers]
+    out_hbm, order_ref, done_ref, sent = refs[2 * layers :]
+    cells_x, _, feat_count = point_ref.shape
+    z, x, y = quad()
     for index, turn in enumerate(turns(layers)):
-        for side in range(2):
-            peer = 2 * layers * side + (z ^ turn) * 2
-            order_ref[peer + (x ^ y)] = own_refs[index][side]
-            order_ref[peer + (x ^ y ^ 1)] = core_refs[index][1 - side]
+        peer = (z ^ turn) * 2
+        order_ref[:, peer + (x ^ y)] = own_refs[index][...]
+        order_ref[:, peer + (x ^ y ^ 1)] = core_refs[index][...]
+    table = table_ref[y, x ^ y]
     copies = []
     for cell in range(cells_x):
-        pair = cell // 2
-        if cell % 2 == 0:
-            span = slice(pair * rows, (pair + 1) * rows)
-            high, low = split_terms(order_ref[:, span, :].reshape(-1, feat_count))
-            stack_ref[pair] = jnp.concatenate([high, low, high], axis=0)
+        high, low = split_terms(order_ref[cell].reshape(-1, feat_count))
+        stack = jnp.concatenate([high, low, high], axis=0)
         for start in range(0, feat_count, WIDTH):
             columns = slice(start, start + WIDTH)
-            left = jnp.concatenate([table_ref[y, cell % 2], flow_ref[cell, :, columns]], axis=1)
-            right = jnp.concatenate([stack_ref[pair, :, columns], wide_ref[...]], axis=0)
-            total = dot(left, right) + level_ref[...]
+            total = dot(table, stack[:, columns]) + point_ref[cell, :, columns]
             done_ref[cell, :, columns] = gelu(total).astype(done_ref.dtype)
         copies.append(pltpu.make_async_copy(done_ref.at[cell], out_hbm.at[cell], sent.at[cell]))
         copies[-1].start()
@@ -453,25 +487,22 @@
         copy.wait()
 
 
-def make_output(flow_field, parts, table, local, bias):
-    cells_x, _, feat_count = flow_field.shape
+def make_output(point, parts, table):
+    cells_x, _, feat_count = point.shape
     layers = len(parts) // 2
     rows = parts[0].shape[1]
     return pl.pallas_call(
         functools.partial(output_kernel, layers),
         out_specs=pl.BlockSpec(memory_space=pl.ANY),
         scratch_shapes=[
-            pltpu.VMEM((4 * layers, rows, feat_count), jnp.float32),
-            pltpu.VMEM((cells_x // 2, table.shape[-1], feat_count), jnp.bfloat16),
-            pltpu.VMEM((WIDTH, WIDTH), jnp.bfloat16),
-            pltpu.VMEM((1, WIDTH), jnp.float32),
-            pltpu.VMEM(flow_field.shape, jnp.bfloat16),
+            pltpu.VMEM((cells_x, 2 * layers, rows, feat_count), jnp.float32),
+            pltpu.VMEM(point.shape, jnp.bfloat16),
             pltpu.SemaphoreType.DMA((cells_x,)),
         ],
-        out_shape=jax.ShapeDtypeStruct(flow_field.shape, jnp.bfloat16),
+        out_shape=jax.ShapeDtypeStruct(point.shape, jnp.bfloat16),
         compiler_params=SMALL,
         name="make_output",
-    )(flow_field, table, local, bias, *parts)
+    )(point, table, *parts)
 
 
 def row_body(flow_field, spectral_weight, local_weight, bias_terms):
@@ -495,11 +526,11 @@
     )
     arrived = flip_core(send)
     mixed, keep = keep_rows(modes, inverse_tables, send)
-    own = along_columns(join_blocks(keep, arrived), peers)
+    own = along_columns(join_blocks(keep, arrived, cells_x), peers)
+    point, own[0] = pointwise_terms(flow_field, local_weight, bias_terms, own[0])
     parts = own + [flip_core(block) for block in own]
     high, low = split_table(inverse_y_table(cells_y, groups_y, peers, rows_ky) * inverse_scale)
-    table = np.concatenate([high, high, low], axis=-1)
-    return make_output(flow_field, parts, table, local_weight, bias_terms), mixed
+    return make_output(point, parts, np.concatenate([high, high, low], axis=-1)), mixed
 
 
 def body(flow_field, spectral_weight, local_weight, bias_terms):

time: 34.6 us -> 40.4 us (1.17)
  local copies, waits for them, and re-layouts: 1.25 us -> 5.49 us
  starting transfers between devices: 16.8 us -> 20.7 us
  waiting for transfers between devices: 10.1 us -> 7.49 us
    unnamed x20, local copies, waits for them, and re-layouts: 1.25 us -> 5.49 us
    ppermute x10, starting transfers between devices: 5.64 us -> 9.24 us  [flip_core(): return lax.ppermute(block, 'gy', [(0, 1), (1, 0)])]
    ppermute x8, waiting for transfers between devices: 6.79 us -> 4.2 us  [along_columns(): arrived.append(lax.ppermute(block, ('gx', 'gy'), pairs))]
    pallas_call x1 -> x2, Pallas kernels: 0.02 us -> 0.55 us  [the longest x1 0.51 us: pointwise_terms(): pl.pallas_call(point_kernel, in_specs=[spec, spec, spec, whole], out_spec...]
  transfers between devices with their start and end apart: 18 -> 18, of which waited for: 13 -> 11; matrix products, arithmetic and copies ran while one was open for 0% -> 0% of each run, Pallas kernels for 2% -> 3%
where the time goes in v10:
time: 40.4 us; the launch traced here: 40 us
  starting transfers between devices  20.7 us (51%)
  waiting for transfers between devices  7.49 us (19%)
  local copies, waits for them, and re-layouts  5.49 us (14%)
  Pallas kernels  5.14 us (13%)
  between operations  0.81 us (2%)
    ppermute x8, starting transfers between devices, along_columns(): arrived.append(lax.ppermute(block, ('gx', 'gy'), pairs))  11.4 us
    ppermute x10, starting transfers between devices, flip_core(): return lax.ppermute(block, 'gy', [(0, 1), (1, 0)])  9.24 us
    unnamed x20, local copies, waits for them, and re-layouts  5.49 us
    ppermute x8, waiting for transfers between devices, along_columns(): arrived.append(lax.ppermute(block, ('gx', 'gy'), pairs))  4.2 us
    ppermute x10, waiting for transfers between devices, flip_core(): return lax.ppermute(block, 'gy', [(0, 1), (1, 0)])  3.29 us
    pallas_call x1, Pallas kernels, make_output(): pl.pallas_call(functools.partial(output_kernel, layers), out_specs=pl.Blo...  2.44 us
    pallas_call x1, Pallas kernels, mix(): pl.pallas_call(functools.partial(mix_kernel, layers), out_shape=[jax.Shap...  1.05 us
  transfers between devices with their start and end apart: 18, of which 11 were waited for; matrix products, arithmetic and copies ran while one was open for 0% of the time, Pallas kernels for 3%

profile of v10, /device:TPU:0, one launch (start us, length us, event | category | flops | bytes accessed | tf_op | source)
XLA Modules:
  0.0 40.0 jit_solution(6121983565007618572)
XLA Ops:
  1.1 1.2 %copy-done = bf16[4,256,512]{2,1,0:T(8,128)(2,1)S(1)} copy-done((bf16[4,256,512]{2,1,0:T(8,128)(2,1)S(1)}, bf16[4,256,512]{2,1,0:T(8,128)(2,1)}, u32[]{:S(2)}) %copy-start) | copy-done | bytes 1048600
  3.2 1.2 %collective-permute-done.arrived_ref = f32[4,2,16,512]{3,2,1,0:T(8,128)S(1)} collective-permute-done((f32[4,2,16,512]{3,2,1,0:T(8,128)S(1)}, f32[4,2,16,512]{3,2,1,0:T(8,128)S(1)}, u32[]{:S(2)}, u32[]{:S(2)}) %collective-permute-start) | collective-permute-done | bytes 262176 | tf_op jit(solution)/shard_map/ppermute | solution.py:256
  4.3 4.0 %collective-permute-start.1 = (f32[2,16,512]{2,1,0:T(8,128)S(1)}, f32[2,16,512]{2,1,0:T(8,128)S(1)}, u32[]{:S(2)}, u32[]{:S(2)}) collective-permute-start(f32[2,16,512]{2,1,0:T(8,128)S(1)} %get-tuple-element.20), channel_id=1, source_target_pairs={{0,8},{1,11},{2,10},{3,9},{4,12},{5,15},{6,14},{7,13},{8,0},{9,3},... | collective-permute-start | bytes 196616 | tf_op jit(solution)/shard_map/ppermute | solution.py:267
  8.4 1.3 %collective-permute-start.2 = (f32[2,16,512]{2,1,0:T(8,128)S(1)}, f32[2,16,512]{2,1,0:T(8,128)S(1)}, u32[]{:S(2)}, u32[]{:S(2)}) collective-permute-start(f32[2,16,512]{2,1,0:T(8,128)S(1)} %get-tuple-element.21), channel_id=1, source_target_pairs={{0,12},{1,15},{2,14},{3,13},{4,8},{5,11},{6,10},{7,9},{8,4},{9,7},... | collective-permute-start | bytes 196616 | tf_op jit(solution)/shard_map/ppermute | solution.py:267
  10.0 0.7 %collective-permute-start.4 = (f32[2,16,512]{2,1,0:T(8,128)S(1)}, f32[2,16,512]{2,1,0:T(8,128)S(1)}, u32[]{:S(2)}, u32[]{:S(2)}) collective-permute-start(f32[2,16,512]{2,1,0:T(8,128)S(1)} %get-tuple-element.23), channel_id=1, source_target_pairs={{0,0},{1,3},{2,2},{3,1},{4,4},{5,7},{6,6},{7,5},{8,8},{9,11},{10,1... | collective-permute-start | bytes 196616 | tf_op jit(solution)/shard_map/ppermute | solution.py:267
  11.0 2.6 %collective-permute-start.5 = (f32[2,16,512]{2,1,0:T(8,128)S(1)}, f32[2,16,512]{2,1,0:T(8,128)S(1)}, u32[]{:S(2)}, u32[]{:S(2)}) collective-permute-start(f32[2,16,512]{2,1,0:T(8,128)S(1)} %collective-permute-done.1.refs_0_), channel_id=1, source_target_pairs={{0,1},{1,0},{2,3},{3,2},{4,5},{5,4},{6,7},{7,6},{8,9},{9,8},{10,11... | collective-permute-start | bytes 196616 | tf_op jit(solution)/shard_map/ppermute | solution.py:256
  13.6 1.5 %collective-permute-done.2.refs_1_ = f32[2,16,512]{2,1,0:T(8,128)S(1)} collective-permute-done((f32[2,16,512]{2,1,0:T(8,128)S(1)}, f32[2,16,512]{2,1,0:T(8,128)S(1)}, u32[]{:S(2)}, u32[]{:S(2)}) %collective-permute-start.2) | collective-permute-done | bytes 65568 | tf_op jit(solution)/shard_map/ppermute | solution.py:267
  17.2 1.2 %copy-done.2 = bf16[1,64,64,128]{3,2,1,0:T(8,128)(2,1)S(1)} copy-done((bf16[1,64,64,128]{3,2,1,0:T(8,128)(2,1)S(1)}, bf16[1,64,64,128]{3,2,1,0:T(8,128)(2,1)}, u32[]{:S(2)}) %copy-start.2) | copy-done | bytes 1048600
  18.5 0.8 %copy-done.4 = bf16[2,64,128]{2,1,0:T(8,128)(2,1)S(1)} copy-done((bf16[2,64,128]{2,1,0:T(8,128)(2,1)S(1)}, bf16[2,64,128]{2,1,0:T(8,128)(2,1)}, u32[]{:S(2)}) %copy-start.4) | copy-done | bytes 32792
  19.2 0.8 %copy-done.5 = bf16[2,64,128]{2,1,0:T(8,128)(2,1)S(1)} copy-done((bf16[2,64,128]{2,1,0:T(8,128)(2,1)S(1)}, bf16[2,64,128]{2,1,0:T(8,128)(2,1)}, u32[]{:S(2)}) %copy-start.5) | copy-done | bytes 32792
  20.0 0.8 %copy-done.6 = bf16[128,128]{1,0:T(8,128)(2,1)S(1)} copy-done((bf16[128,128]{1,0:T(8,128)(2,1)S(1)}, bf16[128,128]{1,0:T(8,128)(2,1)}, u32[]{:S(2)}) %copy-start.6) | copy-done | bytes 32792
  20.7 0.8 %copy-done.7 = bf16[128,128]{1,0:T(8,128)(2,1)S(1)} copy-done((bf16[128,128]{1,0:T(8,128)(2,1)S(1)}, bf16[128,128]{1,0:T(8,128)(2,1)}, u32[]{:S(2)}) %copy-start.7) | copy-done | bytes 32792
  21.5 1.0 %mix.1 = (f32[128,512]{1,0:T(8,128)S(1)}, f32[4,16,512]{2,1,0:T(8,128)S(1)}) custom-call(f32[2,16,512]{2,1,0:T(8,128)S(1)} %collective-permute-done.1.refs_0_, f32[2,16,512]{2,1,0:T(8,128)S(1)} %collective-permute-done.2.refs_1_, f32[2,16,512]{2,1,0:T(8,128)S(1)} %collective-permute-done.3.refs_2_, f32[2,16,512]{2,1,0:T(8,128)S(1)} %collective-permute-done.4.refs_3_, ...), custom_call_target="tpu_custom_call" | custom-call | tf_op jit(solution)/shard_map/mix/pallas_call | solution.py:375
  22.9 0.8 %keep_rows.1 = (f32[1,64,1024]{2,1,0:T(8,128)}, f32[4,16,512]{2,1,0:T(8,128)S(1)}) custom-call(f32[128,512]{1,0:T(8,128)S(1)} %get-tuple-element.24.modes_ref, bf16[2,64,128]{2,1,0:T(8,128)(2,1)S(1)} %copy-done.5, bf16[2,64,128]{2,1,0:T(8,128)(2,1)S(1)} %copy-done.4), custom_call_target="tpu_custom_call" | custom-call | flops 50331648 | bytes 1048576 | tf_op jit(solution)/shard_map/keep_rows/pallas_call | solution.py:402
  24.0 3.6 %collective-permute-start.11 = (f32[4,8,512]{2,1,0:T(8,128)S(1)}, f32[4,8,512]{2,1,0:T(8,128)S(1)}, u32[]{:S(2)}, u32[]{:S(2)}) collective-permute-start(f32[4,8,512]{2,1,0:T(8,128)S(1)} %get-tuple-element.30), channel_id=1, source_target_pairs={{0,12},{1,15},{2,14},{3,13},{4,8},{5,11},{6,10},{7,9},{8,4},{9,7},... | collective-permute-start | bytes 196616 | tf_op jit(solution)/shard_map/ppermute | solution.py:267
  27.7 0.7 %collective-permute-start.13 = (f32[4,8,512]{2,1,0:T(8,128)S(1)}, f32[4,8,512]{2,1,0:T(8,128)S(1)}, u32[]{:S(2)}, u32[]{:S(2)}) collective-permute-start(f32[4,8,512]{2,1,0:T(8,128)S(1)} %get-tuple-element.32), channel_id=1, source_target_pairs={{0,0},{1,3},{2,2},{3,1},{4,4},{5,7},{6,6},{7,5},{8,8},{9,11},{10,1... | collective-permute-start | bytes 196616 | tf_op jit(solution)/shard_map/ppermute | solution.py:267
  28.3 0.9 %collective-permute-start.10 = (f32[4,8,512]{2,1,0:T(8,128)S(1)}, f32[4,8,512]{2,1,0:T(8,128)S(1)}, u32[]{:S(2)}, u32[]{:S(2)}) collective-permute-start(f32[4,8,512]{2,1,0:T(8,128)S(1)} %get-tuple-element.27), channel_id=1, source_target_pairs={{0,8},{1,11},{2,10},{3,9},{4,12},{5,15},{6,14},{7,13},{8,0},{9,3},... | collective-permute-start | bytes 196616 | tf_op jit(solution)/shard_map/ppermute | solution.py:267
  29.2 1.6 %collective-permute-done.11.refs_1_ = f32[4,8,512]{2,1,0:T(8,128)S(1)} collective-permute-done((f32[4,8,512]{2,1,0:T(8,128)S(1)}, f32[4,8,512]{2,1,0:T(8,128)S(1)}, u32[]{:S(2)}, u32[]{:S(2)}) %collective-permute-start.11) | collective-permute-done | bytes 65568 | tf_op jit(solution)/shard_map/ppermute | solution.py:267
  30.8 1.2 %collective-permute-start.15 = (f32[4,8,512]{2,1,0:T(8,128)S(1)}, f32[4,8,512]{2,1,0:T(8,128)S(1)}, u32[]{:S(2)}, u32[]{:S(2)}) collective-permute-start(f32[4,8,512]{2,1,0:T(8,128)S(1)} %collective-permute-done.11.refs_1_), channel_id=1, source_target_pairs={{0,1},{1,0},{2,3},{3,2},{4,5},{5,4},{6,7},{7,6},{8,9},{9,8},{10,11... | collective-permute-start | bytes 196616 | tf_op jit(solution)/shard_map/ppermute | solution.py:256
  32.0 0.6 %collective-permute-done.12.refs_2_ = f32[4,8,512]{2,1,0:T(8,128)S(1)} collective-permute-done((f32[4,8,512]{2,1,0:T(8,128)S(1)}, f32[4,8,512]{2,1,0:T(8,128)S(1)}, u32[]{:S(2)}, u32[]{:S(2)}) %collective-permute-start.12) | collective-permute-done | bytes 65568 | tf_op jit(solution)/shard_map/ppermute | solution.py:267
  33.1 0.5 %collective-permute-start.17 = (f32[4,8,512]{2,1,0:T(8,128)S(1)}, f32[4,8,512]{2,1,0:T(8,128)S(1)}, u32[]{:S(2)}, u32[]{:S(2)}) collective-permute-start(f32[4,8,512]{2,1,0:T(8,128)S(1)} %collective-permute-done.13.refs_3_), channel_id=1, source_target_pairs={{0,1},{1,0},{2,3},{3,2},{4,5},{5,4},{6,7},{7,6},{8,9},{9,8},{10,11... | collective-permute-start | bytes 196616 | tf_op jit(solution)/shard_map/ppermute | solution.py:256
  34.1 2.5 %collective-permute-start.14 = (f32[4,8,512]{2,1,0:T(8,128)S(1)}, f32[4,8,512]{2,1,0:T(8,128)S(1)}, u32[]{:S(2)}, u32[]{:S(2)}) collective-permute-start(f32[4,8,512]{2,1,0:T(8,128)S(1)} %get-tuple-element.29.refs_0_), channel_id=1, source_target_pairs={{0,1},{1,0},{2,3},{3,2},{4,5},{5,4},{6,7},{7,6},{8,9},{9,8},{10,11... | collective-permute-start | bytes 196616 | tf_op jit(solution)/shard_map/ppermute | solution.py:256
  36.6 0.9 %collective-permute-done.14.refs_4_ = f32[4,8,512]{2,1,0:T(8,128)S(1)} collective-permute-done((f32[4,8,512]{2,1,0:T(8,128)S(1)}, f32[4,8,512]{2,1,0:T(8,128)S(1)}, u32[]{:S(2)}, u32[]{:S(2)}) %collective-permute-start.14) | collective-permute-done | bytes 65568 | tf_op jit(solution)/shard_map/ppermute | solution.py:256
  37.5 2.4 %make_output.1 = bf16[4,256,512]{2,1,0:T(8,128)(2,1)} custom-call(f32[4,256,512]{2,1,0:T(8,128)S(1)} %get-tuple-element.28.point_ref, bf16[2,2,256,192]{3,2,1,0:T(8,128)(2,1)S(1)} %copy-done.3, f32[4,8,512]{2,1,0:T(8,128)S(1)} %get-tuple-element.29.refs_0_, f32[4,8,512]{2,1,0:T(8,128)S(1)} %collective-permute-done.11.refs_1_, ...), custom_call_target="tpu_custom_call" | custom-call | tf_op jit(solution)/shard_map/make_output/pallas_call | solution.py:494
  (43 shorter events, 5.8 us)
Async XLA Ops:
  0.6 33.0 %copy-start.9 = (f32[64]{0:T(128)S(1)}, f32[64]{0:T(128)}, u32[]{:S(2)}) copy-start(f32[64]{0:T(128)} %bias_ref.1) | copy-start | bytes 772
  0.6 33.0 %copy-start.8 = (bf16[64,64]{1,0:T(8,128)(2,1)S(1)}, bf16[64,64]{1,0:T(8,128)(2,1)}, u32[]{:S(2)}) copy-start(bf16[64,64]{1,0:T(8,128)(2,1)} %local_ref.1) | copy-start | bytes 24580
  1.1 1.2 %copy-start = (bf16[4,256,512]{2,1,0:T(8,128)(2,1)S(1)}, bf16[4,256,512]{2,1,0:T(8,128)(2,1)}, u32[]{:S(2)}) copy-start(bf16[4,256,512]{2,1,0:T(8,128)(2,1)} %flow_ref.3) | copy-start | bytes 3145732
  2.3 31.3 %copy-start.1 = (bf16[4,256,512]{2,1,0:T(8,128)(2,1)S(1)}, bf16[4,256,512]{2,1,0:T(8,128)(2,1)}, u32[]{:S(2)}) copy-start(bf16[4,256,512]{2,1,0:T(8,128)(2,1)} %flow_ref.3) | copy-start | bytes 3145732
  2.6 34.9 %copy-start.3 = (bf16[2,2,256,192]{3,2,1,0:T(8,128)(2,1)S(1)}, bf16[2,2,256,192]{3,2,1,0:T(8,128)(2,1)}, u32[]{:S(2)}) copy-start(bf16[2,2,256,192]{3,2,1,0:T(8,128)(2,1)} %constant.146.clone.table_ref) | copy-start | bytes 1179652
  2.6 1.7 %collective-permute-start = (f32[4,2,16,512]{3,2,1,0:T(8,128)S(1)}, f32[4,2,16,512]{3,2,1,0:T(8,128)S(1)}, u32[]{:S(2)}, u32[]{:S(2)}) collective-permute-start(f32[4,2,16,512]{3,2,1,0:T(8,128)S(1)} %get-tuple-element.19), channel_id=1, source_target_pairs={{0,1},{1,0},{2,3},{3,2},{4,5},{5,4},{6,7},{7,6},{8,9},{9,8},{10,11... | collective-permute-start | bytes 786440 | tf_op jit(solution)/shard_map/ppermute | solution.py:256
  4.3 6.6 %collective-permute-start.1 = (f32[2,16,512]{2,1,0:T(8,128)S(1)}, f32[2,16,512]{2,1,0:T(8,128)S(1)}, u32[]{:S(2)}, u32[]{:S(2)}) collective-permute-start(f32[2,16,512]{2,1,0:T(8,128)S(1)} %get-tuple-element.20), channel_id=1, source_target_pairs={{0,8},{1,11},{2,10},{3,9},{4,12},{5,15},{6,14},{7,13},{8,0},{9,3},... | collective-permute-start | bytes 196616 | tf_op jit(solution)/shard_map/ppermute | solution.py:267
  8.4 6.7 %collective-permute-start.2 = (f32[2,16,512]{2,1,0:T(8,128)S(1)}, f32[2,16,512]{2,1,0:T(8,128)S(1)}, u32[]{:S(2)}, u32[]{:S(2)}) collective-permute-start(f32[2,16,512]{2,1,0:T(8,128)S(1)} %get-tuple-element.21), channel_id=1, source_target_pairs={{0,12},{1,15},{2,14},{3,13},{4,8},{5,11},{6,10},{7,9},{8,4},{9,7},... | collective-permute-start | bytes 196616 | tf_op jit(solution)/shard_map/ppermute | solution.py:267
  9.7 6.0 %collective-permute-start.3 = (f32[2,16,512]{2,1,0:T(8,128)S(1)}, f32[2,16,512]{2,1,0:T(8,128)S(1)}, u32[]{:S(2)}, u32[]{:S(2)}) collective-permute-start(f32[2,16,512]{2,1,0:T(8,128)S(1)} %get-tuple-element.22), channel_id=1, source_target_pairs={{0,4},{1,7},{2,6},{3,5},{4,0},{5,3},{6,2},{7,1},{8,12},{9,15},{10,... | collective-permute-start | bytes 196616 | tf_op jit(solution)/shard_map/ppermute | solution.py:267
  10.0 6.0 %collective-permute-start.4 = (f32[2,16,512]{2,1,0:T(8,128)S(1)}, f32[2,16,512]{2,1,0:T(8,128)S(1)}, u32[]{:S(2)}, u32[]{:S(2)}) collective-permute-start(f32[2,16,512]{2,1,0:T(8,128)S(1)} %get-tuple-element.23), channel_id=1, source_target_pairs={{0,0},{1,3},{2,2},{3,1},{4,4},{5,7},{6,6},{7,5},{8,8},{9,11},{10,1... | collective-permute-start | bytes 196616 | tf_op jit(solution)/shard_map/ppermute | solution.py:267
  11.0 5.3 %collective-permute-start.5 = (f32[2,16,512]{2,1,0:T(8,128)S(1)}, f32[2,16,512]{2,1,0:T(8,128)S(1)}, u32[]{:S(2)}, u32[]{:S(2)}) collective-permute-start(f32[2,16,512]{2,1,0:T(8,128)S(1)} %collective-permute-done.1.refs_0_), channel_id=1, source_target_pairs={{0,1},{1,0},{2,3},{3,2},{4,5},{5,4},{6,7},{7,6},{8,9},{9,8},{10,11... | collective-permute-start | bytes 196616 | tf_op jit(solution)/shard_map/ppermute | solution.py:256
  15.1 1.4 %collective-permute-start.6 = (f32[2,16,512]{2,1,0:T(8,128)S(1)}, f32[2,16,512]{2,1,0:T(8,128)S(1)}, u32[]{:S(2)}, u32[]{:S(2)}) collective-permute-start(f32[2,16,512]{2,1,0:T(8,128)S(1)} %collective-permute-done.2.refs_1_), channel_id=1, source_target_pairs={{0,1},{1,0},{2,3},{3,2},{4,5},{5,4},{6,7},{7,6},{8,9},{9,8},{10,11... | collective-permute-start | bytes 196616 | tf_op jit(solution)/shard_map/ppermute | solution.py:256
  15.7 1.3 %collective-permute-start.7 = (f32[2,16,512]{2,1,0:T(8,128)S(1)}, f32[2,16,512]{2,1,0:T(8,128)S(1)}, u32[]{:S(2)}, u32[]{:S(2)}) collective-permute-start(f32[2,16,512]{2,1,0:T(8,128)S(1)} %collective-permute-done.3.refs_2_), channel_id=1, source_target_pairs={{0,1},{1,0},{2,3},{3,2},{4,5},{5,4},{6,7},{7,6},{8,9},{9,8},{10,11... | collective-permute-start | bytes 196616 | tf_op jit(solution)/shard_map/ppermute | solution.py:256
  16.0 1.3 %collective-permute-start.8 = (f32[2,16,512]{2,1,0:T(8,128)S(1)}, f32[2,16,512]{2,1,0:T(8,128)S(1)}, u32[]{:S(2)}, u32[]{:S(2)}) collective-permute-start(f32[2,16,512]{2,1,0:T(8,128)S(1)} %collective-permute-done.4.refs_3_), channel_id=1, source_target_pairs={{0,1},{1,0},{2,3},{3,2},{4,5},{5,4},{6,7},{7,6},{8,9},{9,8},{10,11... | collective-permute-start | bytes 196616 | tf_op jit(solution)/shard_map/ppermute | solution.py:256
  17.2 1.2 %copy-start.2 = (bf16[1,64,64,128]{3,2,1,0:T(8,128)(2,1)S(1)}, bf16[1,64,64,128]{3,2,1,0:T(8,128)(2,1)}, u32[]{:S(2)}) copy-start(bf16[1,64,64,128]{3,2,1,0:T(8,128)(2,1)} %refs_8_.1) | copy-start | bytes 3145732
  22.5 1.4 %collective-permute-start.9 = (f32[4,16,512]{2,1,0:T(8,128)S(1)}, f32[4,16,512]{2,1,0:T(8,128)S(1)}, u32[]{:S(2)}, u32[]{:S(2)}) collective-permute-start(f32[4,16,512]{2,1,0:T(8,128)S(1)} %get-tuple-element.26), channel_id=1, source_target_pairs={{0,1},{1,0},{2,3},{3,2},{4,5},{5,4},{6,7},{7,6},{8,9},{9,8},{10,11... | collective-permute-start | bytes 393224 | tf_op jit(solution)/shard_map/ppermute | solution.py:256
  24.0 6.8 %collective-permute-start.11 = (f32[4,8,512]{2,1,0:T(8,128)S(1)}, f32[4,8,512]{2,1,0:T(8,128)S(1)}, u32[]{:S(2)}, u32[]{:S(2)}) collective-permute-start(f32[4,8,512]{2,1,0:T(8,128)S(1)} %get-tuple-element.30), channel_id=1, source_target_pairs={{0,12},{1,15},{2,14},{3,13},{4,8},{5,11},{6,10},{7,9},{8,4},{9,7},... | collective-permute-start | bytes 196616 | tf_op jit(solution)/shard_map/ppermute | solution.py:267
  27.6 5.0 %collective-permute-start.12 = (f32[4,8,512]{2,1,0:T(8,128)S(1)}, f32[4,8,512]{2,1,0:T(8,128)S(1)}, u32[]{:S(2)}, u32[]{:S(2)}) collective-permute-start(f32[4,8,512]{2,1,0:T(8,128)S(1)} %get-tuple-element.31), channel_id=1, source_target_pairs={{0,4},{1,7},{2,6},{3,5},{4,0},{5,3},{6,2},{7,1},{8,12},{9,15},{10,... | collective-permute-start | bytes 196616 | tf_op jit(solution)/shard_map/ppermute | solution.py:267
  27.7 5.4 %collective-permute-start.13 = (f32[4,8,512]{2,1,0:T(8,128)S(1)}, f32[4,8,512]{2,1,0:T(8,128)S(1)}, u32[]{:S(2)}, u32[]{:S(2)}) collective-permute-start(f32[4,8,512]{2,1,0:T(8,128)S(1)} %get-tuple-element.32), channel_id=1, source_target_pairs={{0,0},{1,3},{2,2},{3,1},{4,4},{5,7},{6,6},{7,5},{8,8},{9,11},{10,1... | collective-permute-start | bytes 196616 | tf_op jit(solution)/shard_map/ppermute | solution.py:267
  28.3 5.3 %collective-permute-start.10 = (f32[4,8,512]{2,1,0:T(8,128)S(1)}, f32[4,8,512]{2,1,0:T(8,128)S(1)}, u32[]{:S(2)}, u32[]{:S(2)}) collective-permute-start(f32[4,8,512]{2,1,0:T(8,128)S(1)} %get-tuple-element.27), channel_id=1, source_target_pairs={{0,8},{1,11},{2,10},{3,9},{4,12},{5,15},{6,14},{7,13},{8,0},{9,3},... | collective-permute-start | bytes 196616 | tf_op jit(solution)/shard_map/ppermute | solution.py:267
  30.8 5.9 %collective-permute-start.15 = (f32[4,8,512]{2,1,0:T(8,128)S(1)}, f32[4,8,512]{2,1,0:T(8,128)S(1)}, u32[]{:S(2)}, u32[]{:S(2)}) collective-permute-start(f32[4,8,512]{2,1,0:T(8,128)S(1)} %collective-permute-done.11.refs_1_), channel_id=1, source_target_pairs={{0,1},{1,0},{2,3},{3,2},{4,5},{5,4},{6,7},{7,6},{8,9},{9,8},{10,11... | collective-permute-start | bytes 196616 | tf_op jit(solution)/shard_map/ppermute | solution.py:256
  32.5 4.1 %collective-permute-start.16 = (f32[4,8,512]{2,1,0:T(8,128)S(1)}, f32[4,8,512]{2,1,0:T(8,128)S(1)}, u32[]{:S(2)}, u32[]{:S(2)}) collective-permute-start(f32[4,8,512]{2,1,0:T(8,128)S(1)} %collective-permute-done.12.refs_2_), channel_id=1, source_target_pairs={{0,1},{1,0},{2,3},{3,2},{4,5},{5,4},{6,7},{7,6},{8,9},{9,8},{10,11... | collective-permute-start | bytes 196616 | tf_op jit(solution)/shard_map/ppermute | solution.py:256
  33.1 3.6 %collective-permute-start.17 = (f32[4,8,512]{2,1,0:T(8,128)S(1)}, f32[4,8,512]{2,1,0:T(8,128)S(1)}, u32[]{:S(2)}, u32[]{:S(2)}) collective-permute-start(f32[4,8,512]{2,1,0:T(8,128)S(1)} %collective-permute-done.13.refs_3_), channel_id=1, source_target_pairs={{0,1},{1,0},{2,3},{3,2},{4,5},{5,4},{6,7},{7,6},{8,9},{9,8},{10,11... | collective-permute-start | bytes 196616 | tf_op jit(solution)/shard_map/ppermute | solution.py:256
  34.1 3.4 %collective-permute-start.14 = (f32[4,8,512]{2,1,0:T(8,128)S(1)}, f32[4,8,512]{2,1,0:T(8,128)S(1)}, u32[]{:S(2)}, u32[]{:S(2)}) collective-permute-start(f32[4,8,512]{2,1,0:T(8,128)S(1)} %get-tuple-element.29.refs_0_), channel_id=1, source_target_pairs={{0,1},{1,0},{2,3},{3,2},{4,5},{5,4},{6,7},{7,6},{8,9},{9,8},{10,11... | collective-permute-start | bytes 196616 | tf_op jit(solution)/shard_map/ppermute | solution.py:256
  (4 other events, 3.0 us)

commit v11 on v10

--- a/solution.py
+++ b/solution.py
@@ -127,6 +127,7 @@
 
 
 SMALL = pltpu.CompilerParams(vmem_limit_bytes=20 * 1024 * 1024)
+LARGE = pltpu.CompilerParams(vmem_limit_bytes=53 * 1024 * 1024)
 WIDTH = 256
 GELU_TERMS = (
     0.7978849411010742,
@@ -166,23 +167,6 @@
 def turns(layers):
     half = layers // 2
     return list(range(half, layers)) + list(range(half - 1, -1, -1))
-
-
-def forward_y_table(cells_y, groups_y, peers, rows_ky):
-    z, x, y = quad()
-    layers = peers // 2
-    row = jnp.arange(2 * MY, dtype=jnp.int32)
-    block = row // (2 * rows_ky)
-    place = block // 2 % layers
-    turn = jnp.where(place < layers // 2, place + layers // 2, layers - 1 - place)
-    side = y ^ (1 - block // peers)
-    column = x ^ side
-    half = side ^ (block % 2)
-    owner = half * peers + (z ^ turn) * 2 + column
-    index = owner * rows_ky + row // 2 % rows_ky
-    y_places = y * cells_y + jnp.arange(cells_y, dtype=jnp.int32)
-    angle = phase_table(wave_number(index, MY), y_places, cells_y * groups_y)
-    return jnp.where(row[:, None] % 2 == 0, jnp.cos(angle), -jnp.sin(angle)).astype(jnp.bfloat16)
 
 
 def forward_x_table(cells_x, peers, rows_ky):
@@ -231,25 +215,54 @@
     return jnp.dot(left, right, preferred_element_type=jnp.float32)
 
 
-def forward_y_kernel(flow_ref, table_ref, send_ref, keep_ref):
+def forward_y_table(shape, extent, layers, rows_ky):
+    z, x, y = quad()
+    peers = 2 * layers
+    row = lax.broadcasted_iota(jnp.int32, (shape[0], 1), 0)
+    block = row // (2 * rows_ky)
+    place = block // 2 % layers
+    turn = jnp.where(place < layers // 2, place + layers // 2, layers - 1 - place)
+    side = y ^ (1 - block // peers)
+    owner = (side ^ (block % 2)) * peers + (z ^ turn) * 2 + (x ^ side)
+    index = owner * rows_ky + row // 2 % rows_ky
+    y_places = lax.broadcasted_iota(jnp.int32, (1, shape[1]), 1) + y * shape[1]
+    steps = (wave_number(index, MY) * y_places) & (extent - 1)
+    angle = 2.0 * math.pi / extent * steps.astype(jnp.float32)
+    return jnp.where(row % 2 == 0, jnp.cos(angle), -jnp.sin(angle)).astype(jnp.bfloat16)
+
+
+def forward_y_kernel(extent, rows_ky, flow_hbm, send_ref, keep_ref, flow_ref, arrived):
     layers, _, rows, feat_count = send_ref.shape
-    cells_x = flow_ref.shape[0]
+    cells_x, cells_y, _ = flow_ref.shape
     rows = rows // cells_x
+    copies = [
+        pltpu.make_async_copy(flow_hbm.at[x], flow_ref.at[x], arrived.at[x])
+        for x in range(cells_x)
+    ]
+    for copy in copies:
+        copy.start()
+    table = forward_y_table((2 * MY, cells_y), extent, layers, rows_ky)
     for x in range(cells_x):
-        result = dot(table_ref[...], flow_ref[x]).reshape(2, layers, 2, rows, feat_count)
+        copies[x].wait()
+        result = dot(table, flow_ref[x]).reshape(2, layers, 2, rows, feat_count)
         send_ref[:, :, x * rows : (x + 1) * rows, :] = result[0]
         keep_ref[:, :, x * rows : (x + 1) * rows, :] = result[1]
 
 
-def forward_y(flow_field, table, layers, rows_ky):
+def forward_y(flow_field, extent, layers, rows_ky):
     cells_x, _, feat_count = flow_field.shape
     shape = jax.ShapeDtypeStruct((layers, 2, cells_x * 2 * rows_ky, feat_count), jnp.float32)
     return pl.pallas_call(
-        forward_y_kernel,
+        functools.partial(forward_y_kernel, extent, rows_ky),
+        in_specs=[pl.BlockSpec(memory_space=pltpu.HBM)],
         out_shape=[shape] * 2,
-        compiler_params=SMALL,
+        scratch_shapes=[
+            pltpu.VMEM(flow_field.shape, flow_field.dtype),
+            pltpu.SemaphoreType.DMA((cells_x,)),
+        ],
+        compiler_params=LARGE,
         name="forward_y",
-    )(flow_field, table)
+    )(flow_field)
 
 
 def flip_core(block):
@@ -384,32 +397,19 @@
     )(*blocks, *arrived, weights, *split_table(forward_table), *inverse_tables)
 
 
-def keep_kernel(modes_ref, inverse_high, inverse_low, mixed_ref, keep_ref, order_ref):
+def keep_kernel(modes_ref, inverse_high, inverse_low, keep_ref, order_ref):
     z, x, y = quad()
-    count = mixed_ref.shape[1]
-    feat_count = modes_ref.shape[1]
-    for part in range(2):
-        mixed_ref[0, :, part * feat_count : (part + 1) * feat_count] = modes_ref[
-            part * count : (part + 1) * count
-        ]
     back = back_rows(inverse_high, inverse_low, x ^ y, modes_ref[...])
     order_ref[...] = back.reshape(keep_ref.shape)
     store_turns(keep_ref, order_ref, z)
 
 
 def keep_rows(modes, inverse_tables, like):
-    rows, feat_count = modes.shape
     return pl.pallas_call(
         keep_kernel,
-        out_shape=[
-            jax.ShapeDtypeStruct((1, rows // 2, 2 * feat_count), jnp.float32),
-            jax.ShapeDtypeStruct(like.shape, jnp.float32),
-        ],
+        out_shape=jax.ShapeDtypeStruct(like.shape, jnp.float32),
         scratch_shapes=[pltpu.VMEM(like.shape, jnp.float32)],
         compiler_params=SMALL,
-        cost_estimate=pl.CostEstimate(
-            flops=6 * rows * rows * feat_count, bytes_accessed=2**20, transcendentals=0
-        ),
         name="keep_rows",
     )(modes, *inverse_tables)
 
@@ -423,86 +423,66 @@
     return half + half * jnp.tanh(values * inner)
 
 
-def point_kernel(flow_ref, local_ref, bias_ref, _, out_ref, __, wide_ref, level_ref):
+def output_kernel(layers, flow_ref, table_ref, local_ref, bias_ref, modes_ref, *refs):
+    own_refs, core_refs = refs[:layers], refs[layers : 2 * layers]
+    out_hbm, mixed_hbm, order_ref, wide_ref, level_ref, done_ref, sent = refs[2 * layers :]
     cells_x, _, feat_count = flow_ref.shape
     channels = local_ref.shape[0]
+    count = modes_ref.shape[0] // 2
+    copies = []
+    for part in range(2):
+        copies.append(
+            pltpu.make_async_copy(
+                modes_ref.at[pl.ds(part * count, count)],
+                mixed_hbm.at[0, :, pl.ds(part * feat_count, feat_count)],
+                sent.at[cells_x + part],
+            )
+        )
+        copies[-1].start()
+    z, x, y = quad()
     wide_ref[...] = jnp.zeros_like(wide_ref)
     for start in range(0, WIDTH, channels):
         span = slice(start, start + channels)
         wide_ref[span, span] = local_ref[...]
         level_ref[:, span] = bias_ref[...].reshape(1, channels)
-    for cell in range(cells_x):
-        for start in range(0, feat_count, WIDTH):
-            columns = slice(start, start + WIDTH)
-            out_ref[cell, :, columns] = dot(flow_ref[cell, :, columns], wide_ref[...]) + level_ref[...]
-
-
-def pointwise_terms(flow_field, local, bias, first):
-    spec = pl.BlockSpec(memory_space=pltpu.VMEM)
-    whole = pl.BlockSpec(memory_space=pl.ANY)
-    return pl.pallas_call(
-        point_kernel,
-        in_specs=[spec, spec, spec, whole],
-        out_specs=[spec, whole],
-        out_shape=[
-            jax.ShapeDtypeStruct(flow_field.shape, jnp.float32),
-            jax.ShapeDtypeStruct(first.shape, first.dtype),
-        ],
-        input_output_aliases={3: 1},
-        scratch_shapes=[
-            pltpu.VMEM((WIDTH, WIDTH), jnp.bfloat16),
-            pltpu.VMEM((1, WIDTH), jnp.float32),
-        ],
-        compiler_params=SMALL,
-        cost_estimate=pl.CostEstimate(
-            flops=2 * WIDTH * flow_field.size,
-            bytes_accessed=6 * flow_field.size,
-            transcendentals=0,
-        ),
-        name="pointwise_terms",
-    )(flow_field, local, bias, first)
-
-
-def output_kernel(layers, point_ref, table_ref, *refs):
-    own_refs, core_refs = refs[:layers], refs[layers : 2 * layers]
-    out_hbm, order_ref, done_ref, sent = refs[2 * layers :]
-    cells_x, _, feat_count = point_ref.shape
-    z, x, y = quad()
-    for index, turn in enumerate(turns(layers)):
-        peer = (z ^ turn) * 2
-        order_ref[:, peer + (x ^ y)] = own_refs[index][...]
-        order_ref[:, peer + (x ^ y ^ 1)] = core_refs[index][...]
+    for column, block_refs in ((x ^ y, own_refs), (x ^ y ^ 1, core_refs)):
+        for turn, block_ref in zip(turns(layers), block_refs):
+            order_ref[:, (z ^ turn) * 2 + column] = block_ref[...]
     table = table_ref[y, x ^ y]
-    copies = []
     for cell in range(cells_x):
         high, low = split_terms(order_ref[cell].reshape(-1, feat_count))
         stack = jnp.concatenate([high, low, high], axis=0)
         for start in range(0, feat_count, WIDTH):
             columns = slice(start, start + WIDTH)
-            total = dot(table, stack[:, columns]) + point_ref[cell, :, columns]
-            done_ref[cell, :, columns] = gelu(total).astype(done_ref.dtype)
+            total = dot(table, stack[:, columns]) + dot(flow_ref[cell, :, columns], wide_ref[...])
+            done_ref[cell, :, columns] = gelu(total + level_ref[...]).astype(done_ref.dtype)
         copies.append(pltpu.make_async_copy(done_ref.at[cell], out_hbm.at[cell], sent.at[cell]))
         copies[-1].start()
     for copy in copies:
         copy.wait()
 
 
-def make_output(point, parts, table):
-    cells_x, _, feat_count = point.shape
+def make_output(flow_field, parts, table, local, bias, modes):
+    cells_x, _, feat_count = flow_field.shape
     layers = len(parts) // 2
-    rows = parts[0].shape[1]
+    rows, _ = modes.shape
     return pl.pallas_call(
         functools.partial(output_kernel, layers),
-        out_specs=pl.BlockSpec(memory_space=pl.ANY),
+        out_specs=[pl.BlockSpec(memory_space=pl.ANY)] * 2,
         scratch_shapes=[
-            pltpu.VMEM((cells_x, 2 * layers, rows, feat_count), jnp.float32),
-            pltpu.VMEM(point.shape, jnp.bfloat16),
-            pltpu.SemaphoreType.DMA((cells_x,)),
+            pltpu.VMEM((cells_x, 2 * layers) + parts[0].shape[1:], jnp.float32),
+            pltpu.VMEM((WIDTH, WIDTH), jnp.bfloat16),
+            pltpu.VMEM((1, WIDTH), jnp.float32),
+            pltpu.VMEM(flow_field.shape, jnp.bfloat16),
+            pltpu.SemaphoreType.DMA((cells_x + 2,)),
         ],
-        out_shape=jax.ShapeDtypeStruct(point.shape, jnp.bfloat16),
+        out_shape=[
+            jax.ShapeDtypeStruct(flow_field.shape, jnp.bfloat16),
+            jax.ShapeDtypeStruct((1, rows // 2, 2 * feat_count), jnp.float32),
+        ],
         compiler_params=SMALL,
         name="make_output",
-    )(point, table, *parts)
+    )(flow_field, table, local, bias, modes, *parts)
 
 
 def row_body(flow_field, spectral_weight, local_weight, bias_terms):
@@ -513,8 +493,7 @@
     forward_scale = 1.0 / math.sqrt(cells_x * peers * cells_y * groups_y)
     inverse_scale = 1.0 / math.sqrt(MX * MY)
 
-    table = forward_y_table(cells_y, groups_y, peers, rows_ky)
-    send, keep = forward_y(flow_field, table, peers // 2, rows_ky)
+    send, keep = forward_y(flow_field, cells_y * groups_y, peers // 2, rows_ky)
     blocks = along_columns(add_blocks(keep, flip_core(send)), peers)
     inverse_tables = split_table(inverse_x_table(cells_x, peers, rows_ky))
     modes, send = mix(
@@ -525,17 +504,18 @@
         inverse_tables,
     )
     arrived = flip_core(send)
-    mixed, keep = keep_rows(modes, inverse_tables, send)
+    keep = keep_rows(modes, inverse_tables, send)
     own = along_columns(join_blocks(keep, arrived, cells_x), peers)
-    point, own[0] = pointwise_terms(flow_field, local_weight, bias_terms, own[0])
     parts = own + [flip_core(block) for block in own]
     high, low = split_table(inverse_y_table(cells_y, groups_y, peers, rows_ky) * inverse_scale)
-    return make_output(point, parts, np.concatenate([high, high, low], axis=-1)), mixed
+    table = np.concatenate([high, high, low], axis=-1)
+    return tuple(make_output(flow_field, parts, table, local_weight, bias_terms, modes))
 
 
 def body(flow_field, spectral_weight, local_weight, bias_terms):
     peers = lax.axis_size("gx")
-    paired = lax.axis_size("gy") == 2 and peers & (peers - 1) == 0
+    extent = lax.axis_size("gy") * flow_field.shape[1]
+    paired = lax.axis_size("gy") == 2 and peers & (peers - 1) == 0 and extent & (extent - 1) == 0
     if paired and spectral_weight.shape[1] == 2 * MX and WIDTH % local_weight.shape[0] == 0:
         return row_body(flow_field, spectral_weight, local_weight, bias_terms)
     return general_body(flow_field, spectral_weight, local_weight, bias_terms)

time: 40.4 us -> 34.2 us (0.85)
  local copies, waits for them, and re-layouts: 5.49 us -> 0.04 us
  starting transfers between devices: 20.7 us -> 16.8 us
  waiting for transfers between devices: 7.49 us -> 10.7 us
  Pallas kernels: 5.14 us -> 5.74 us
    unnamed x20 -> x18, local copies, waits for them, and re-layouts: 5.49 us -> 0.04 us
    ppermute x10, starting transfers between devices: 9.24 us -> 5.64 us  [flip_core(): return lax.ppermute(block, 'gy', [(0, 1), (1, 0)])]
    ppermute x8, waiting for transfers between devices: 4.2 us -> 6.79 us  [along_columns(): arrived.append(lax.ppermute(block, ('gx', 'gy'), pairs))]
    ppermute x10, waiting for transfers between devices: 3.29 us -> 3.92 us  [flip_core(): return lax.ppermute(block, 'gy', [(0, 1), (1, 0)])]
    pallas_call x4 -> x3, Pallas kernels: 4.03 us -> 4.62 us  [the longest x1 2.65 us: make_output(): pl.pallas_call(functools.partial(output_kernel, layers), out_specs=[pl.Bl...]
  transfers between devices with their start and end apart: 18 -> 18, of which waited for: 11 -> 13; matrix products, arithmetic and copies ran while one was open for 0% -> 0% of each run, Pallas kernels for 3% -> 1%
where the time goes in v11:
time: 34.2 us; the launch traced here: 34 us
  starting transfers between devices  16.8 us (49%)
  waiting for transfers between devices  10.7 us (31%)
  Pallas kernels  5.74 us (17%)
  between operations  0.75 us (2%)
    ppermute x8, starting transfers between devices, along_columns(): arrived.append(lax.ppermute(block, ('gx', 'gy'), pairs))  11.2 us
    ppermute x8, waiting for transfers between devices, along_columns(): arrived.append(lax.ppermute(block, ('gx', 'gy'), pairs))  6.79 us
    ppermute x10, starting transfers between devices, flip_core(): return lax.ppermute(block, 'gy', [(0, 1), (1, 0)])  5.64 us
    ppermute x10, waiting for transfers between devices, flip_core(): return lax.ppermute(block, 'gy', [(0, 1), (1, 0)])  3.92 us
    pallas_call x1, Pallas kernels, make_output(): pl.pallas_call(functools.partial(output_kernel, layers), out_specs=[pl.Bl...  2.65 us
    pallas_call x1, Pallas kernels, forward_y(): pl.pallas_call(functools.partial(forward_y_kernel, extent, rows_ky), in_s...  1.75 us
    pallas_call x1, Pallas kernels, mix(): pl.pallas_call(functools.partial(mix_kernel, layers), out_shape=[jax.Shap...  1.05 us
  transfers between devices with their start and end apart: 18, of which 13 were waited for; matrix products, arithmetic and copies ran while one was open for 0% of the time, Pallas kernels for 1%

profile of v11, /device:TPU:0, one launch (start us, length us, event | category | flops | bytes accessed | tf_op | source)
XLA Modules:
  0.0 34.0 jit_solution(7804430371847103407)
XLA Ops:
  0.6 1.7 %forward_y.1 = (f32[4,2,16,512]{3,2,1,0:T(8,128)S(1)}, f32[4,2,16,512]{3,2,1,0:T(8,128)S(1)}) custom-call(bf16[4,256,512]{2,1,0:T(8,128)(2,1)} %flow_ref.1), custom_call_target="tpu_custom_call" | custom-call | tf_op jit(solution)/shard_map/forward_y/pallas_call | solution.py:255
  2.4 0.5 %collective-permute-start = (f32[4,2,16,512]{3,2,1,0:T(8,128)S(1)}, f32[4,2,16,512]{3,2,1,0:T(8,128)S(1)}, u32[]{:S(2)}, u32[]{:S(2)}) collective-permute-start(f32[4,2,16,512]{3,2,1,0:T(8,128)S(1)} %get-tuple-element.15), channel_id=1, source_target_pairs={{0,1},{1,0},{2,3},{3,2},{4,5},{5,4},{6,7},{7,6},{8,9},{9,8},{10,11... | collective-permute-start | bytes 786440 | tf_op jit(solution)/shard_map/ppermute | solution.py:269
  2.9 1.2 %collective-permute-done.arrived_ref = f32[4,2,16,512]{3,2,1,0:T(8,128)S(1)} collective-permute-done((f32[4,2,16,512]{3,2,1,0:T(8,128)S(1)}, f32[4,2,16,512]{3,2,1,0:T(8,128)S(1)}, u32[]{:S(2)}, u32[]{:S(2)}) %collective-permute-start) | collective-permute-done | bytes 262176 | tf_op jit(solution)/shard_map/ppermute | solution.py:269
  4.1 4.0 %collective-permute-start.1 = (f32[2,16,512]{2,1,0:T(8,128)S(1)}, f32[2,16,512]{2,1,0:T(8,128)S(1)}, u32[]{:S(2)}, u32[]{:S(2)}) collective-permute-start(f32[2,16,512]{2,1,0:T(8,128)S(1)} %get-tuple-element.16), channel_id=1, source_target_pairs={{0,8},{1,11},{2,10},{3,9},{4,12},{5,15},{6,14},{7,13},{8,0},{9,3},... | collective-permute-start | bytes 196616 | tf_op jit(solution)/shard_map/ppermute | solution.py:280
  8.2 1.3 %collective-permute-start.2 = (f32[2,16,512]{2,1,0:T(8,128)S(1)}, f32[2,16,512]{2,1,0:T(8,128)S(1)}, u32[]{:S(2)}, u32[]{:S(2)}) collective-permute-start(f32[2,16,512]{2,1,0:T(8,128)S(1)} %get-tuple-element.17), channel_id=1, source_target_pairs={{0,12},{1,15},{2,14},{3,13},{4,8},{5,11},{6,10},{7,9},{8,4},{9,7},... | collective-permute-start | bytes 196616 | tf_op jit(solution)/shard_map/ppermute | solution.py:280
  9.7 0.8 %collective-permute-start.4 = (f32[2,16,512]{2,1,0:T(8,128)S(1)}, f32[2,16,512]{2,1,0:T(8,128)S(1)}, u32[]{:S(2)}, u32[]{:S(2)}) collective-permute-start(f32[2,16,512]{2,1,0:T(8,128)S(1)} %get-tuple-element.19), channel_id=1, source_target_pairs={{0,0},{1,3},{2,2},{3,1},{4,4},{5,7},{6,6},{7,5},{8,8},{9,11},{10,1... | collective-permute-start | bytes 196616 | tf_op jit(solution)/shard_map/ppermute | solution.py:280
  10.8 2.8 %collective-permute-start.5 = (f32[2,16,512]{2,1,0:T(8,128)S(1)}, f32[2,16,512]{2,1,0:T(8,128)S(1)}, u32[]{:S(2)}, u32[]{:S(2)}) collective-permute-start(f32[2,16,512]{2,1,0:T(8,128)S(1)} %collective-permute-done.1.refs_0_), channel_id=1, source_target_pairs={{0,1},{1,0},{2,3},{3,2},{4,5},{5,4},{6,7},{7,6},{8,9},{9,8},{10,11... | collective-permute-start | bytes 196616 | tf_op jit(solution)/shard_map/ppermute | solution.py:269
  13.5 1.3 %collective-permute-done.2.refs_1_ = f32[2,16,512]{2,1,0:T(8,128)S(1)} collective-permute-done((f32[2,16,512]{2,1,0:T(8,128)S(1)}, f32[2,16,512]{2,1,0:T(8,128)S(1)}, u32[]{:S(2)}, u32[]{:S(2)}) %collective-permute-start.2) | collective-permute-done | bytes 65568 | tf_op jit(solution)/shard_map/ppermute | solution.py:280
  14.9 0.5 %collective-permute-start.6 = (f32[2,16,512]{2,1,0:T(8,128)S(1)}, f32[2,16,512]{2,1,0:T(8,128)S(1)}, u32[]{:S(2)}, u32[]{:S(2)}) collective-permute-start(f32[2,16,512]{2,1,0:T(8,128)S(1)} %collective-permute-done.2.refs_1_), channel_id=1, source_target_pairs={{0,1},{1,0},{2,3},{3,2},{4,5},{5,4},{6,7},{7,6},{8,9},{9,8},{10,11... | collective-permute-start | bytes 196616 | tf_op jit(solution)/shard_map/ppermute | solution.py:269
  15.7 0.3 collective-permute-start.8
  16.2 0.6 %collective-permute-done.7.refs_6_ = f32[2,16,512]{2,1,0:T(8,128)S(1)} collective-permute-done((f32[2,16,512]{2,1,0:T(8,128)S(1)}, f32[2,16,512]{2,1,0:T(8,128)S(1)}, u32[]{:S(2)}, u32[]{:S(2)}) %collective-permute-start.7) | collective-permute-done | bytes 65568 | tf_op jit(solution)/shard_map/ppermute | solution.py:269
  17.0 1.1 %mix.1 = (f32[128,512]{1,0:T(8,128)S(1)}, f32[4,16,512]{2,1,0:T(8,128)S(1)}) custom-call(f32[2,16,512]{2,1,0:T(8,128)S(1)} %collective-permute-done.1.refs_0_, f32[2,16,512]{2,1,0:T(8,128)S(1)} %collective-permute-done.2.refs_1_, f32[2,16,512]{2,1,0:T(8,128)S(1)} %collective-permute-done.3.refs_2_, f32[2,16,512]{2,1,0:T(8,128)S(1)} %collective-permute-done.4.refs_3_, ...), custom_call_target="tpu_custom_call" | custom-call | tf_op jit(solution)/shard_map/mix/pallas_call | solution.py:388
  18.1 0.4 %collective-permute-start.9 = (f32[4,16,512]{2,1,0:T(8,128)S(1)}, f32[4,16,512]{2,1,0:T(8,128)S(1)}, u32[]{:S(2)}, u32[]{:S(2)}) collective-permute-start(f32[4,16,512]{2,1,0:T(8,128)S(1)} %get-tuple-element.21), channel_id=1, source_target_pairs={{0,1},{1,0},{2,3},{3,2},{4,5},{5,4},{6,7},{7,6},{8,9},{9,8},{10,11... | collective-permute-start | bytes 393224 | tf_op jit(solution)/shard_map/ppermute | solution.py:269
  18.7 0.8 %collective-permute-done.9.arrived_ref = f32[4,16,512]{2,1,0:T(8,128)S(1)} collective-permute-done((f32[4,16,512]{2,1,0:T(8,128)S(1)}, f32[4,16,512]{2,1,0:T(8,128)S(1)}, u32[]{:S(2)}, u32[]{:S(2)}) %collective-permute-start.9) | collective-permute-done | bytes 131104 | tf_op jit(solution)/shard_map/ppermute | solution.py:269
  19.6 3.1 %collective-permute-start.10 = (f32[4,8,512]{2,1,0:T(8,128)S(1)}, f32[4,8,512]{2,1,0:T(8,128)S(1)}, u32[]{:S(2)}, u32[]{:S(2)}) collective-permute-start(f32[4,8,512]{2,1,0:T(8,128)S(1)} %get-tuple-element.22), channel_id=1, source_target_pairs={{0,8},{1,11},{2,10},{3,9},{4,12},{5,15},{6,14},{7,13},{8,0},{9,3},... | collective-permute-start | bytes 196616 | tf_op jit(solution)/shard_map/ppermute | solution.py:280
  22.7 1.0 %collective-permute-start.11 = (f32[4,8,512]{2,1,0:T(8,128)S(1)}, f32[4,8,512]{2,1,0:T(8,128)S(1)}, u32[]{:S(2)}, u32[]{:S(2)}) collective-permute-start(f32[4,8,512]{2,1,0:T(8,128)S(1)} %get-tuple-element.23), channel_id=1, source_target_pairs={{0,12},{1,15},{2,14},{3,13},{4,8},{5,11},{6,10},{7,9},{8,4},{9,7},... | collective-permute-start | bytes 196616 | tf_op jit(solution)/shard_map/ppermute | solution.py:280
  23.7 0.7 %collective-permute-start.13 = (f32[4,8,512]{2,1,0:T(8,128)S(1)}, f32[4,8,512]{2,1,0:T(8,128)S(1)}, u32[]{:S(2)}, u32[]{:S(2)}) collective-permute-start(f32[4,8,512]{2,1,0:T(8,128)S(1)} %get-tuple-element.25), channel_id=1, source_target_pairs={{0,0},{1,3},{2,2},{3,1},{4,4},{5,7},{6,6},{7,5},{8,8},{9,11},{10,1... | collective-permute-start | bytes 196616 | tf_op jit(solution)/shard_map/ppermute | solution.py:280
  24.4 2.6 %collective-permute-done.10.refs_0_ = f32[4,8,512]{2,1,0:T(8,128)S(1)} collective-permute-done((f32[4,8,512]{2,1,0:T(8,128)S(1)}, f32[4,8,512]{2,1,0:T(8,128)S(1)}, u32[]{:S(2)}, u32[]{:S(2)}) %collective-permute-start.10) | collective-permute-done | bytes 65568 | tf_op jit(solution)/shard_map/ppermute | solution.py:280
  27.1 2.4 %collective-permute-done.11.refs_1_ = f32[4,8,512]{2,1,0:T(8,128)S(1)} collective-permute-done((f32[4,8,512]{2,1,0:T(8,128)S(1)}, f32[4,8,512]{2,1,0:T(8,128)S(1)}, u32[]{:S(2)}, u32[]{:S(2)}) %collective-permute-start.11) | collective-permute-done | bytes 65568 | tf_op jit(solution)/shard_map/ppermute | solution.py:280
  29.5 0.4 %collective-permute-start.15 = (f32[4,8,512]{2,1,0:T(8,128)S(1)}, f32[4,8,512]{2,1,0:T(8,128)S(1)}, u32[]{:S(2)}, u32[]{:S(2)}) collective-permute-start(f32[4,8,512]{2,1,0:T(8,128)S(1)} %collective-permute-done.11.refs_1_), channel_id=1, source_target_pairs={{0,1},{1,0},{2,3},{3,2},{4,5},{5,4},{6,7},{7,6},{8,9},{9,8},{10,11... | collective-permute-start | bytes 196616 | tf_op jit(solution)/shard_map/ppermute | solution.py:269
  30.4 0.4 %collective-permute-done.15.refs_5_ = f32[4,8,512]{2,1,0:T(8,128)S(1)} collective-permute-done((f32[4,8,512]{2,1,0:T(8,128)S(1)}, f32[4,8,512]{2,1,0:T(8,128)S(1)}, u32[]{:S(2)}, u32[]{:S(2)}) %collective-permute-start.15) | collective-permute-done | bytes 65568 | tf_op jit(solution)/shard_map/ppermute | solution.py:269
  30.7 0.4 %collective-permute-done.16.refs_6_ = f32[4,8,512]{2,1,0:T(8,128)S(1)} collective-permute-done((f32[4,8,512]{2,1,0:T(8,128)S(1)}, f32[4,8,512]{2,1,0:T(8,128)S(1)}, u32[]{:S(2)}, u32[]{:S(2)}) %collective-permute-start.16) | collective-permute-done | bytes 65568 | tf_op jit(solution)/shard_map/ppermute | solution.py:269
  31.1 0.3 collective-permute-done.17.refs_7_
  31.4 2.7 %make_output.1 = (bf16[4,256,512]{2,1,0:T(8,128)(2,1)}, f32[1,64,1024]{2,1,0:T(8,128)}) custom-call(bf16[4,256,512]{2,1,0:T(8,128)(2,1)S(1)} %copy-done, bf16[2,2,256,192]{3,2,1,0:T(8,128)(2,1)S(1)} %copy-done.2, bf16[64,64]{1,0:T(8,128)(2,1)S(1)} %copy-done.7, f32[64]{0:T(128)S(1)} %copy-done.8, f32[128,512]{1,0:T(8,128)S(1)} %get-tuple-element.20.modes_ref, ...), custom_call_target="tpu_custom_call" | custom-call | tf_op jit(solution)/shard_map/make_output/pallas_call | solution.py:469
  (36 shorter events, 2.3 us)
Async XLA Ops:
  0.6 16.4 %copy-start.1 = (bf16[1,64,64,128]{3,2,1,0:T(8,128)(2,1)S(1)}, bf16[1,64,64,128]{3,2,1,0:T(8,128)(2,1)}, u32[]{:S(2)}) copy-start(bf16[1,64,64,128]{3,2,1,0:T(8,128)(2,1)} %refs_8_.1) | copy-start | bytes 3145732
  2.4 1.7 %collective-permute-start = (f32[4,2,16,512]{3,2,1,0:T(8,128)S(1)}, f32[4,2,16,512]{3,2,1,0:T(8,128)S(1)}, u32[]{:S(2)}, u32[]{:S(2)}) collective-permute-start(f32[4,2,16,512]{3,2,1,0:T(8,128)S(1)} %get-tuple-element.15), channel_id=1, source_target_pairs={{0,1},{1,0},{2,3},{3,2},{4,5},{5,4},{6,7},{7,6},{8,9},{9,8},{10,11... | collective-permute-start | bytes 786440 | tf_op jit(solution)/shard_map/ppermute | solution.py:269
  4.1 12.9 %copy-start.4 = (bf16[2,64,128]{2,1,0:T(8,128)(2,1)S(1)}, bf16[2,64,128]{2,1,0:T(8,128)(2,1)}, u32[]{:S(2)}) copy-start(bf16[2,64,128]{2,1,0:T(8,128)(2,1)} %constant.12.clone.refs_11_.inverse_high) | copy-start | bytes 98308
  4.1 12.9 %copy-start.5 = (bf16[128,128]{1,0:T(8,128)(2,1)S(1)}, bf16[128,128]{1,0:T(8,128)(2,1)}, u32[]{:S(2)}) copy-start(bf16[128,128]{1,0:T(8,128)(2,1)} %constant.11.clone.refs_10_) | copy-start | bytes 98308
  4.1 12.9 %copy-start.6 = (bf16[128,128]{1,0:T(8,128)(2,1)S(1)}, bf16[128,128]{1,0:T(8,128)(2,1)}, u32[]{:S(2)}) copy-start(bf16[128,128]{1,0:T(8,128)(2,1)} %constant.10.clone.refs_9_) | copy-start | bytes 98308
  4.1 6.6 %collective-permute-start.1 = (f32[2,16,512]{2,1,0:T(8,128)S(1)}, f32[2,16,512]{2,1,0:T(8,128)S(1)}, u32[]{:S(2)}, u32[]{:S(2)}) collective-permute-start(f32[2,16,512]{2,1,0:T(8,128)S(1)} %get-tuple-element.16), channel_id=1, source_target_pairs={{0,8},{1,11},{2,10},{3,9},{4,12},{5,15},{6,14},{7,13},{8,0},{9,3},... | collective-permute-start | bytes 196616 | tf_op jit(solution)/shard_map/ppermute | solution.py:280
  8.2 6.7 %collective-permute-start.2 = (f32[2,16,512]{2,1,0:T(8,128)S(1)}, f32[2,16,512]{2,1,0:T(8,128)S(1)}, u32[]{:S(2)}, u32[]{:S(2)}) collective-permute-start(f32[2,16,512]{2,1,0:T(8,128)S(1)} %get-tuple-element.17), channel_id=1, source_target_pairs={{0,12},{1,15},{2,14},{3,13},{4,8},{5,11},{6,10},{7,9},{8,4},{9,7},... | collective-permute-start | bytes 196616 | tf_op jit(solution)/shard_map/ppermute | solution.py:280
  9.5 6.0 %collective-permute-start.3 = (f32[2,16,512]{2,1,0:T(8,128)S(1)}, f32[2,16,512]{2,1,0:T(8,128)S(1)}, u32[]{:S(2)}, u32[]{:S(2)}) collective-permute-start(f32[2,16,512]{2,1,0:T(8,128)S(1)} %get-tuple-element.18), channel_id=1, source_target_pairs={{0,4},{1,7},{2,6},{3,5},{4,0},{5,3},{6,2},{7,1},{8,12},{9,15},{10,... | collective-permute-start | bytes 196616 | tf_op jit(solution)/shard_map/ppermute | solution.py:280
  9.7 21.6 %copy-start = (bf16[4,256,512]{2,1,0:T(8,128)(2,1)S(1)}, bf16[4,256,512]{2,1,0:T(8,128)(2,1)}, u32[]{:S(2)}) copy-start(bf16[4,256,512]{2,1,0:T(8,128)(2,1)} %flow_ref.1) | copy-start | bytes 3145732
  9.7 6.0 %collective-permute-start.4 = (f32[2,16,512]{2,1,0:T(8,128)S(1)}, f32[2,16,512]{2,1,0:T(8,128)S(1)}, u32[]{:S(2)}, u32[]{:S(2)}) collective-permute-start(f32[2,16,512]{2,1,0:T(8,128)S(1)} %get-tuple-element.19), channel_id=1, source_target_pairs={{0,0},{1,3},{2,2},{3,1},{4,4},{5,7},{6,6},{7,5},{8,8},{9,11},{10,1... | collective-permute-start | bytes 196616 | tf_op jit(solution)/shard_map/ppermute | solution.py:280
  10.8 5.3 %collective-permute-start.5 = (f32[2,16,512]{2,1,0:T(8,128)S(1)}, f32[2,16,512]{2,1,0:T(8,128)S(1)}, u32[]{:S(2)}, u32[]{:S(2)}) collective-permute-start(f32[2,16,512]{2,1,0:T(8,128)S(1)} %collective-permute-done.1.refs_0_), channel_id=1, source_target_pairs={{0,1},{1,0},{2,3},{3,2},{4,5},{5,4},{6,7},{7,6},{8,9},{9,8},{10,11... | collective-permute-start | bytes 196616 | tf_op jit(solution)/shard_map/ppermute | solution.py:269
  14.9 1.4 %collective-permute-start.6 = (f32[2,16,512]{2,1,0:T(8,128)S(1)}, f32[2,16,512]{2,1,0:T(8,128)S(1)}, u32[]{:S(2)}, u32[]{:S(2)}) collective-permute-start(f32[2,16,512]{2,1,0:T(8,128)S(1)} %collective-permute-done.2.refs_1_), channel_id=1, source_target_pairs={{0,1},{1,0},{2,3},{3,2},{4,5},{5,4},{6,7},{7,6},{8,9},{9,8},{10,11... | collective-permute-start | bytes 196616 | tf_op jit(solution)/shard_map/ppermute | solution.py:269
  15.5 1.3 %collective-permute-start.7 = (f32[2,16,512]{2,1,0:T(8,128)S(1)}, f32[2,16,512]{2,1,0:T(8,128)S(1)}, u32[]{:S(2)}, u32[]{:S(2)}) collective-permute-start(f32[2,16,512]{2,1,0:T(8,128)S(1)} %collective-permute-done.3.refs_2_), channel_id=1, source_target_pairs={{0,1},{1,0},{2,3},{3,2},{4,5},{5,4},{6,7},{7,6},{8,9},{9,8},{10,11... | collective-permute-start | bytes 196616 | tf_op jit(solution)/shard_map/ppermute | solution.py:269
  15.7 1.3 %collective-permute-start.8 = (f32[2,16,512]{2,1,0:T(8,128)S(1)}, f32[2,16,512]{2,1,0:T(8,128)S(1)}, u32[]{:S(2)}, u32[]{:S(2)}) collective-permute-start(f32[2,16,512]{2,1,0:T(8,128)S(1)} %collective-permute-done.4.refs_3_), channel_id=1, source_target_pairs={{0,1},{1,0},{2,3},{3,2},{4,5},{5,4},{6,7},{7,6},{8,9},{9,8},{10,11... | collective-permute-start | bytes 196616 | tf_op jit(solution)/shard_map/ppermute | solution.py:269
  18.1 13.3 %copy-start.2 = (bf16[2,2,256,192]{3,2,1,0:T(8,128)(2,1)S(1)}, bf16[2,2,256,192]{3,2,1,0:T(8,128)(2,1)}, u32[]{:S(2)}) copy-start(bf16[2,2,256,192]{3,2,1,0:T(8,128)(2,1)} %constant.14.clone.table_ref) | copy-start | bytes 1179652
  18.1 1.4 %collective-permute-start.9 = (f32[4,16,512]{2,1,0:T(8,128)S(1)}, f32[4,16,512]{2,1,0:T(8,128)S(1)}, u32[]{:S(2)}, u32[]{:S(2)}) collective-permute-start(f32[4,16,512]{2,1,0:T(8,128)S(1)} %get-tuple-element.21), channel_id=1, source_target_pairs={{0,1},{1,0},{2,3},{3,2},{4,5},{5,4},{6,7},{7,6},{8,9},{9,8},{10,11... | collective-permute-start | bytes 393224 | tf_op jit(solution)/shard_map/ppermute | solution.py:269
  19.6 7.4 %collective-permute-start.10 = (f32[4,8,512]{2,1,0:T(8,128)S(1)}, f32[4,8,512]{2,1,0:T(8,128)S(1)}, u32[]{:S(2)}, u32[]{:S(2)}) collective-permute-start(f32[4,8,512]{2,1,0:T(8,128)S(1)} %get-tuple-element.22), channel_id=1, source_target_pairs={{0,8},{1,11},{2,10},{3,9},{4,12},{5,15},{6,14},{7,13},{8,0},{9,3},... | collective-permute-start | bytes 196616 | tf_op jit(solution)/shard_map/ppermute | solution.py:280
  22.7 6.8 %collective-permute-start.11 = (f32[4,8,512]{2,1,0:T(8,128)S(1)}, f32[4,8,512]{2,1,0:T(8,128)S(1)}, u32[]{:S(2)}, u32[]{:S(2)}) collective-permute-start(f32[4,8,512]{2,1,0:T(8,128)S(1)} %get-tuple-element.23), channel_id=1, source_target_pairs={{0,12},{1,15},{2,14},{3,13},{4,8},{5,11},{6,10},{7,9},{8,4},{9,7},... | collective-permute-start | bytes 196616 | tf_op jit(solution)/shard_map/ppermute | solution.py:280
  23.7 6.2 %collective-permute-start.12 = (f32[4,8,512]{2,1,0:T(8,128)S(1)}, f32[4,8,512]{2,1,0:T(8,128)S(1)}, u32[]{:S(2)}, u32[]{:S(2)}) collective-permute-start(f32[4,8,512]{2,1,0:T(8,128)S(1)} %get-tuple-element.24), channel_id=1, source_target_pairs={{0,4},{1,7},{2,6},{3,5},{4,0},{5,3},{6,2},{7,1},{8,12},{9,15},{10,... | collective-permute-start | bytes 196616 | tf_op jit(solution)/shard_map/ppermute | solution.py:280
  23.7 6.4 %collective-permute-start.13 = (f32[4,8,512]{2,1,0:T(8,128)S(1)}, f32[4,8,512]{2,1,0:T(8,128)S(1)}, u32[]{:S(2)}, u32[]{:S(2)}) collective-permute-start(f32[4,8,512]{2,1,0:T(8,128)S(1)} %get-tuple-element.25), channel_id=1, source_target_pairs={{0,0},{1,3},{2,2},{3,1},{4,4},{5,7},{6,6},{7,5},{8,8},{9,11},{10,1... | collective-permute-start | bytes 196616 | tf_op jit(solution)/shard_map/ppermute | solution.py:280
  26.9 3.5 %collective-permute-start.14 = (f32[4,8,512]{2,1,0:T(8,128)S(1)}, f32[4,8,512]{2,1,0:T(8,128)S(1)}, u32[]{:S(2)}, u32[]{:S(2)}) collective-permute-start(f32[4,8,512]{2,1,0:T(8,128)S(1)} %collective-permute-done.10.refs_0_), channel_id=1, source_target_pairs={{0,1},{1,0},{2,3},{3,2},{4,5},{5,4},{6,7},{7,6},{8,9},{9,8},{10,11... | collective-permute-start | bytes 196616 | tf_op jit(solution)/shard_map/ppermute | solution.py:269
  29.5 1.3 %collective-permute-start.15 = (f32[4,8,512]{2,1,0:T(8,128)S(1)}, f32[4,8,512]{2,1,0:T(8,128)S(1)}, u32[]{:S(2)}, u32[]{:S(2)}) collective-permute-start(f32[4,8,512]{2,1,0:T(8,128)S(1)} %collective-permute-done.11.refs_1_), channel_id=1, source_target_pairs={{0,1},{1,0},{2,3},{3,2},{4,5},{5,4},{6,7},{7,6},{8,9},{9,8},{10,11... | collective-permute-start | bytes 196616 | tf_op jit(solution)/shard_map/ppermute | solution.py:269
  29.9 1.3 %collective-permute-start.16 = (f32[4,8,512]{2,1,0:T(8,128)S(1)}, f32[4,8,512]{2,1,0:T(8,128)S(1)}, u32[]{:S(2)}, u32[]{:S(2)}) collective-permute-start(f32[4,8,512]{2,1,0:T(8,128)S(1)} %collective-permute-done.12.refs_2_), channel_id=1, source_target_pairs={{0,1},{1,0},{2,3},{3,2},{4,5},{5,4},{6,7},{7,6},{8,9},{9,8},{10,11... | collective-permute-start | bytes 196616 | tf_op jit(solution)/shard_map/ppermute | solution.py:269
  30.1 1.3 %collective-permute-start.17 = (f32[4,8,512]{2,1,0:T(8,128)S(1)}, f32[4,8,512]{2,1,0:T(8,128)S(1)}, u32[]{:S(2)}, u32[]{:S(2)}) collective-permute-start(f32[4,8,512]{2,1,0:T(8,128)S(1)} %collective-permute-done.13.refs_3_), channel_id=1, source_target_pairs={{0,1},{1,0},{2,3},{3,2},{4,5},{5,4},{6,7},{7,6},{8,9},{9,8},{10,11... | collective-permute-start | bytes 196616 | tf_op jit(solution)/shard_map/ppermute | solution.py:269
  (3 other events, 32.5 us)

commit v12 on v11

--- a/solution.py
+++ b/solution.py
@@ -166,7 +166,7 @@
 
 def turns(layers):
     half = layers // 2
-    return list(range(half, layers)) + list(range(half - 1, -1, -1))
+    return list(range(half, -1, -1)) + list(range(half + 1, layers))
 
 
 def forward_x_table(cells_x, peers, rows_ky):
@@ -221,7 +221,7 @@
     row = lax.broadcasted_iota(jnp.int32, (shape[0], 1), 0)
     block = row // (2 * rows_ky)
     place = block // 2 % layers
-    turn = jnp.where(place < layers // 2, place + layers // 2, layers - 1 - place)
+    turn = jnp.where(place <= layers // 2, layers // 2 - place, place)
     side = y ^ (1 - block // peers)
     owner = (side ^ (block % 2)) * peers + (z ^ turn) * 2 + (x ^ side)
     index = owner * rows_ky + row // 2 % rows_ky
@@ -426,7 +426,7 @@
 def output_kernel(layers, flow_ref, table_ref, local_ref, bias_ref, modes_ref, *refs):
     own_refs, core_refs = refs[:layers], refs[layers : 2 * layers]
     out_hbm, mixed_hbm, order_ref, wide_ref, level_ref, done_ref, sent = refs[2 * layers :]
-    cells_x, _, feat_count = flow_ref.shape
+    cells_x, cells_y, feat_count = flow_ref.shape
     channels = local_ref.shape[0]
     count = modes_ref.shape[0] // 2
     copies = []
@@ -435,7 +435,7 @@
             pltpu.make_async_copy(
                 modes_ref.at[pl.ds(part * count, count)],
                 mixed_hbm.at[0, :, pl.ds(part * feat_count, feat_count)],
-                sent.at[cells_x + part],
+                sent.at[2 * cells_x + part],
             )
         )
         copies[-1].start()
@@ -452,12 +452,20 @@
     for cell in range(cells_x):
         high, low = split_terms(order_ref[cell].reshape(-1, feat_count))
         stack = jnp.concatenate([high, low, high], axis=0)
-        for start in range(0, feat_count, WIDTH):
-            columns = slice(start, start + WIDTH)
-            total = dot(table, stack[:, columns]) + dot(flow_ref[cell, :, columns], wide_ref[...])
-            done_ref[cell, :, columns] = gelu(total + level_ref[...]).astype(done_ref.dtype)
-        copies.append(pltpu.make_async_copy(done_ref.at[cell], out_hbm.at[cell], sent.at[cell]))
-        copies[-1].start()
+        for half in range(2):
+            rows = slice(half * cells_y // 2, (half + 1) * cells_y // 2)
+            for start in range(0, feat_count, WIDTH):
+                columns = slice(start, start + WIDTH)
+                total = dot(table[rows], stack[:, columns]) + dot(
+                    flow_ref[cell, rows, columns], wide_ref[...]
+                )
+                done_ref[cell, rows, columns] = gelu(total + level_ref[...]).astype(done_ref.dtype)
+            copies.append(
+                pltpu.make_async_copy(
+                    done_ref.at[cell, rows], out_hbm.at[cell, rows], sent.at[2 * cell + half]
+                )
+            )
+            copies[-1].start()
     for copy in copies:
         copy.wait()
 
@@ -474,7 +482,7 @@
             pltpu.VMEM((WIDTH, WIDTH), jnp.bfloat16),
             pltpu.VMEM((1, WIDTH), jnp.float32),
             pltpu.VMEM(flow_field.shape, jnp.bfloat16),
-            pltpu.SemaphoreType.DMA((cells_x + 2,)),
+            pltpu.SemaphoreType.DMA((2 * cells_x + 2,)),
         ],
         out_shape=[
             jax.ShapeDtypeStruct(flow_field.shape, jnp.bfloat16),

time: 34.2 us -> 36.3 us (1.061)
  starting transfers between devices: 16.8 us -> 23.9 us
  waiting for transfers between devices: 10.7 us -> 5.7 us
    ppermute x10, starting transfers between devices: 5.64 us -> 12.3 us  [flip_core(): return lax.ppermute(block, 'gy', [(0, 1), (1, 0)])]
    ppermute x8, waiting for transfers between devices: 6.79 us -> 1.98 us  [along_columns(): arrived.append(lax.ppermute(block, ('gx', 'gy'), pairs))]
    ppermute x8, starting transfers between devices: 11.2 us -> 11.6 us  [along_columns(): arrived.append(lax.ppermute(block, ('gx', 'gy'), pairs))]
  transfers between devices with their start and end apart: 18 -> 18, of which waited for: 13 -> 7; matrix products, arithmetic and copies ran while one was open for 0% -> 0% of each run, Pallas kernels for 1% -> 1%
where the time goes in v12:
time: 36.3 us; the launch traced here: 36.2 us
  starting transfers between devices  23.9 us (66%)
  Pallas kernels  5.76 us (16%)
  waiting for transfers between devices  5.7 us (16%)
  between operations  0.76 us (2%)
    ppermute x10, starting transfers between devices, flip_core(): return lax.ppermute(block, 'gy', [(0, 1), (1, 0)])  12.3 us
    ppermute x8, starting transfers between devices, along_columns(): arrived.append(lax.ppermute(block, ('gx', 'gy'), pairs))  11.6 us
    ppermute x10, waiting for transfers between devices, flip_core(): return lax.ppermute(block, 'gy', [(0, 1), (1, 0)])  3.72 us
    pallas_call x1, Pallas kernels, make_output(): pl.pallas_call(functools.partial(output_kernel, layers), out_specs=[pl.Bl...  2.68 us
    ppermute x8, waiting for transfers between devices, along_columns(): arrived.append(lax.ppermute(block, ('gx', 'gy'), pairs))  1.98 us
    pallas_call x1, Pallas kernels, forward_y(): pl.pallas_call(functools.partial(forward_y_kernel, extent, rows_ky), in_s...  1.75 us
    pallas_call x1, Pallas kernels, mix(): pl.pallas_call(functools.partial(mix_kernel, layers), out_shape=[jax.Shap...  1.05 us
  transfers between devices with their start and end apart: 18, of which 7 were waited for; matrix products, arithmetic and copies ran while one was open for 0% of the time, Pallas kernels for 1%

profile of v12, /device:TPU:0, one launch (start us, length us, event | category | flops | bytes accessed | tf_op | source)
XLA Modules:
  0.0 36.2 jit_solution(18252180516564169727)
XLA Ops:
  0.6 1.7 %forward_y.1 = (f32[4,2,16,512]{3,2,1,0:T(8,128)S(1)}, f32[4,2,16,512]{3,2,1,0:T(8,128)S(1)}) custom-call(bf16[4,256,512]{2,1,0:T(8,128)(2,1)} %flow_ref.1), custom_call_target="tpu_custom_call" | custom-call | tf_op jit(solution)/shard_map/forward_y/pallas_call | solution.py:255
  2.4 0.5 %collective-permute-start = (f32[4,2,16,512]{3,2,1,0:T(8,128)S(1)}, f32[4,2,16,512]{3,2,1,0:T(8,128)S(1)}, u32[]{:S(2)}, u32[]{:S(2)}) collective-permute-start(f32[4,2,16,512]{3,2,1,0:T(8,128)S(1)} %get-tuple-element.15), channel_id=1, source_target_pairs={{0,1},{1,0},{2,3},{3,2},{4,5},{5,4},{6,7},{7,6},{8,9},{9,8},{10,11... | collective-permute-start | bytes 786440 | tf_op jit(solution)/shard_map/ppermute | solution.py:269
  2.9 1.2 %collective-permute-done.arrived_ref = f32[4,2,16,512]{3,2,1,0:T(8,128)S(1)} collective-permute-done((f32[4,2,16,512]{3,2,1,0:T(8,128)S(1)}, f32[4,2,16,512]{3,2,1,0:T(8,128)S(1)}, u32[]{:S(2)}, u32[]{:S(2)}) %collective-permute-start) | collective-permute-done | bytes 262176 | tf_op jit(solution)/shard_map/ppermute | solution.py:269
  4.1 4.0 %collective-permute-start.1 = (f32[2,16,512]{2,1,0:T(8,128)S(1)}, f32[2,16,512]{2,1,0:T(8,128)S(1)}, u32[]{:S(2)}, u32[]{:S(2)}) collective-permute-start(f32[2,16,512]{2,1,0:T(8,128)S(1)} %get-tuple-element.16), channel_id=1, source_target_pairs={{0,8},{1,11},{2,10},{3,9},{4,12},{5,15},{6,14},{7,13},{8,0},{9,3},... | collective-permute-start | bytes 196616 | tf_op jit(solution)/shard_map/ppermute | solution.py:280
  8.2 1.6 %collective-permute-start.2 = (f32[2,16,512]{2,1,0:T(8,128)S(1)}, f32[2,16,512]{2,1,0:T(8,128)S(1)}, u32[]{:S(2)}, u32[]{:S(2)}) collective-permute-start(f32[2,16,512]{2,1,0:T(8,128)S(1)} %get-tuple-element.17), channel_id=1, source_target_pairs={{0,4},{1,7},{2,6},{3,5},{4,0},{5,3},{6,2},{7,1},{8,12},{9,15},{10,... | collective-permute-start | bytes 196616 | tf_op jit(solution)/shard_map/ppermute | solution.py:280
  9.7 0.7 %collective-permute-start.3 = (f32[2,16,512]{2,1,0:T(8,128)S(1)}, f32[2,16,512]{2,1,0:T(8,128)S(1)}, u32[]{:S(2)}, u32[]{:S(2)}) collective-permute-start(f32[2,16,512]{2,1,0:T(8,128)S(1)} %get-tuple-element.18), channel_id=1, source_target_pairs={{0,0},{1,3},{2,2},{3,1},{4,4},{5,7},{6,6},{7,5},{8,8},{9,11},{10,1... | collective-permute-start | bytes 196616 | tf_op jit(solution)/shard_map/ppermute | solution.py:280
  10.5 0.3 collective-permute-done.1.refs_0_
  10.8 2.7 %collective-permute-start.5 = (f32[2,16,512]{2,1,0:T(8,128)S(1)}, f32[2,16,512]{2,1,0:T(8,128)S(1)}, u32[]{:S(2)}, u32[]{:S(2)}) collective-permute-start(f32[2,16,512]{2,1,0:T(8,128)S(1)} %collective-permute-done.1.refs_0_), channel_id=1, source_target_pairs={{0,1},{1,0},{2,3},{3,2},{4,5},{5,4},{6,7},{7,6},{8,9},{9,8},{10,11... | collective-permute-start | bytes 196616 | tf_op jit(solution)/shard_map/ppermute | solution.py:269
  13.5 0.3 collective-permute-start.6
  13.8 1.4 %collective-permute-start.7 = (f32[2,16,512]{2,1,0:T(8,128)S(1)}, f32[2,16,512]{2,1,0:T(8,128)S(1)}, u32[]{:S(2)}, u32[]{:S(2)}) collective-permute-start(f32[2,16,512]{2,1,0:T(8,128)S(1)} %collective-permute-done.3.refs_2_), channel_id=1, source_target_pairs={{0,1},{1,0},{2,3},{3,2},{4,5},{5,4},{6,7},{7,6},{8,9},{9,8},{10,11... | collective-permute-start | bytes 196616 | tf_op jit(solution)/shard_map/ppermute | solution.py:269
  15.2 1.4 %collective-permute-done.4.refs_3_ = f32[2,16,512]{2,1,0:T(8,128)S(1)} collective-permute-done((f32[2,16,512]{2,1,0:T(8,128)S(1)}, f32[2,16,512]{2,1,0:T(8,128)S(1)}, u32[]{:S(2)}, u32[]{:S(2)}) %collective-permute-start.4) | collective-permute-done | bytes 65568 | tf_op jit(solution)/shard_map/ppermute | solution.py:280
  16.6 2.6 %collective-permute-start.8 = (f32[2,16,512]{2,1,0:T(8,128)S(1)}, f32[2,16,512]{2,1,0:T(8,128)S(1)}, u32[]{:S(2)}, u32[]{:S(2)}) collective-permute-start(f32[2,16,512]{2,1,0:T(8,128)S(1)} %collective-permute-done.4.refs_3_), channel_id=1, source_target_pairs={{0,1},{1,0},{2,3},{3,2},{4,5},{5,4},{6,7},{7,6},{8,9},{9,8},{10,11... | collective-permute-start | bytes 196616 | tf_op jit(solution)/shard_map/ppermute | solution.py:269
  19.2 0.9 %collective-permute-done.8.refs_7_ = f32[2,16,512]{2,1,0:T(8,128)S(1)} collective-permute-done((f32[2,16,512]{2,1,0:T(8,128)S(1)}, f32[2,16,512]{2,1,0:T(8,128)S(1)}, u32[]{:S(2)}, u32[]{:S(2)}) %collective-permute-start.8) | collective-permute-done | bytes 65568 | tf_op jit(solution)/shard_map/ppermute | solution.py:269
  20.1 1.1 %mix.1 = (f32[128,512]{1,0:T(8,128)S(1)}, f32[4,16,512]{2,1,0:T(8,128)S(1)}) custom-call(f32[2,16,512]{2,1,0:T(8,128)S(1)} %collective-permute-done.1.refs_0_, f32[2,16,512]{2,1,0:T(8,128)S(1)} %collective-permute-done.2.refs_1_, f32[2,16,512]{2,1,0:T(8,128)S(1)} %collective-permute-done.3.refs_2_, f32[2,16,512]{2,1,0:T(8,128)S(1)} %collective-permute-done.4.refs_3_, ...), custom_call_target="tpu_custom_call" | custom-call | tf_op jit(solution)/shard_map/mix/pallas_call | solution.py:388
  21.2 0.4 %collective-permute-start.9 = (f32[4,16,512]{2,1,0:T(8,128)S(1)}, f32[4,16,512]{2,1,0:T(8,128)S(1)}, u32[]{:S(2)}, u32[]{:S(2)}) collective-permute-start(f32[4,16,512]{2,1,0:T(8,128)S(1)} %get-tuple-element.21), channel_id=1, source_target_pairs={{0,1},{1,0},{2,3},{3,2},{4,5},{5,4},{6,7},{7,6},{8,9},{9,8},{10,11... | collective-permute-start | bytes 393224 | tf_op jit(solution)/shard_map/ppermute | solution.py:269
  21.9 0.8 %collective-permute-done.9.arrived_ref = f32[4,16,512]{2,1,0:T(8,128)S(1)} collective-permute-done((f32[4,16,512]{2,1,0:T(8,128)S(1)}, f32[4,16,512]{2,1,0:T(8,128)S(1)}, u32[]{:S(2)}, u32[]{:S(2)}) %collective-permute-start.9) | collective-permute-done | bytes 131104 | tf_op jit(solution)/shard_map/ppermute | solution.py:269
  22.7 0.8 %collective-permute-start.11 = (f32[4,8,512]{2,1,0:T(8,128)S(1)}, f32[4,8,512]{2,1,0:T(8,128)S(1)}, u32[]{:S(2)}, u32[]{:S(2)}) collective-permute-start(f32[4,8,512]{2,1,0:T(8,128)S(1)} %get-tuple-element.23), channel_id=1, source_target_pairs={{0,4},{1,7},{2,6},{3,5},{4,0},{5,3},{6,2},{7,1},{8,12},{9,15},{10,... | collective-permute-start | bytes 196616 | tf_op jit(solution)/shard_map/ppermute | solution.py:280
  23.5 0.8 %collective-permute-start.12 = (f32[4,8,512]{2,1,0:T(8,128)S(1)}, f32[4,8,512]{2,1,0:T(8,128)S(1)}, u32[]{:S(2)}, u32[]{:S(2)}) collective-permute-start(f32[4,8,512]{2,1,0:T(8,128)S(1)} %get-tuple-element.24), channel_id=1, source_target_pairs={{0,0},{1,3},{2,2},{3,1},{4,4},{5,7},{6,6},{7,5},{8,8},{9,11},{10,1... | collective-permute-start | bytes 196616 | tf_op jit(solution)/shard_map/ppermute | solution.py:280
  24.3 3.7 %collective-permute-start.13 = (f32[4,8,512]{2,1,0:T(8,128)S(1)}, f32[4,8,512]{2,1,0:T(8,128)S(1)}, u32[]{:S(2)}, u32[]{:S(2)}) collective-permute-start(f32[4,8,512]{2,1,0:T(8,128)S(1)} %get-tuple-element.25), channel_id=1, source_target_pairs={{0,12},{1,15},{2,14},{3,13},{4,8},{5,11},{6,10},{7,9},{8,4},{9,7},... | collective-permute-start | bytes 196616 | tf_op jit(solution)/shard_map/ppermute | solution.py:280
  28.2 2.6 %collective-permute-start.14 = (f32[4,8,512]{2,1,0:T(8,128)S(1)}, f32[4,8,512]{2,1,0:T(8,128)S(1)}, u32[]{:S(2)}, u32[]{:S(2)}) collective-permute-start(f32[4,8,512]{2,1,0:T(8,128)S(1)} %collective-permute-done.10.refs_0_), channel_id=1, source_target_pairs={{0,1},{1,0},{2,3},{3,2},{4,5},{5,4},{6,7},{7,6},{8,9},{9,8},{10,11... | collective-permute-start | bytes 196616 | tf_op jit(solution)/shard_map/ppermute | solution.py:269
  30.9 0.4 %collective-permute-start.16 = (f32[4,8,512]{2,1,0:T(8,128)S(1)}, f32[4,8,512]{2,1,0:T(8,128)S(1)}, u32[]{:S(2)}, u32[]{:S(2)}) collective-permute-start(f32[4,8,512]{2,1,0:T(8,128)S(1)} %collective-permute-done.12.refs_2_), channel_id=1, source_target_pairs={{0,1},{1,0},{2,3},{3,2},{4,5},{5,4},{6,7},{7,6},{8,9},{9,8},{10,11... | collective-permute-start | bytes 196616 | tf_op jit(solution)/shard_map/ppermute | solution.py:269
  31.3 1.2 %collective-permute-start.17 = (f32[4,8,512]{2,1,0:T(8,128)S(1)}, f32[4,8,512]{2,1,0:T(8,128)S(1)}, u32[]{:S(2)}, u32[]{:S(2)}) collective-permute-start(f32[4,8,512]{2,1,0:T(8,128)S(1)} %collective-permute-done.13.refs_3_), channel_id=1, source_target_pairs={{0,1},{1,0},{2,3},{3,2},{4,5},{5,4},{6,7},{7,6},{8,9},{9,8},{10,11... | collective-permute-start | bytes 196616 | tf_op jit(solution)/shard_map/ppermute | solution.py:269
  32.6 0.9 %collective-permute-done.17.refs_7_ = f32[4,8,512]{2,1,0:T(8,128)S(1)} collective-permute-done((f32[4,8,512]{2,1,0:T(8,128)S(1)}, f32[4,8,512]{2,1,0:T(8,128)S(1)}, u32[]{:S(2)}, u32[]{:S(2)}) %collective-permute-start.17) | collective-permute-done | bytes 65568 | tf_op jit(solution)/shard_map/ppermute | solution.py:269
  33.5 2.7 %make_output.1 = (bf16[4,256,512]{2,1,0:T(8,128)(2,1)}, f32[1,64,1024]{2,1,0:T(8,128)}) custom-call(bf16[4,256,512]{2,1,0:T(8,128)(2,1)S(1)} %copy-done, bf16[2,2,256,192]{3,2,1,0:T(8,128)(2,1)S(1)} %copy-done.2, bf16[64,64]{1,0:T(8,128)(2,1)S(1)} %copy-done.7, f32[64]{0:T(128)S(1)} %copy-done.8, f32[128,512]{1,0:T(8,128)S(1)} %get-tuple-element.20.modes_ref, ...), custom_call_target="tpu_custom_call" | custom-call | tf_op jit(solution)/shard_map/make_output/pallas_call | solution.py:477
  (36 shorter events, 0.8 us)
Async XLA Ops:
  0.6 19.5 %copy-start.1 = (bf16[1,64,64,128]{3,2,1,0:T(8,128)(2,1)S(1)}, bf16[1,64,64,128]{3,2,1,0:T(8,128)(2,1)}, u32[]{:S(2)}) copy-start(bf16[1,64,64,128]{3,2,1,0:T(8,128)(2,1)} %refs_8_.1) | copy-start | bytes 3145732
  2.4 1.7 %collective-permute-start = (f32[4,2,16,512]{3,2,1,0:T(8,128)S(1)}, f32[4,2,16,512]{3,2,1,0:T(8,128)S(1)}, u32[]{:S(2)}, u32[]{:S(2)}) collective-permute-start(f32[4,2,16,512]{3,2,1,0:T(8,128)S(1)} %get-tuple-element.15), channel_id=1, source_target_pairs={{0,1},{1,0},{2,3},{3,2},{4,5},{5,4},{6,7},{7,6},{8,9},{9,8},{10,11... | collective-permute-start | bytes 786440 | tf_op jit(solution)/shard_map/ppermute | solution.py:269
  4.1 16.0 %copy-start.3 = (bf16[2,64,128]{2,1,0:T(8,128)(2,1)S(1)}, bf16[2,64,128]{2,1,0:T(8,128)(2,1)}, u32[]{:S(2)}) copy-start(bf16[2,64,128]{2,1,0:T(8,128)(2,1)} %constant.13.clone.refs_12_.inverse_low) | copy-start | bytes 98308
  4.1 16.0 %copy-start.4 = (bf16[2,64,128]{2,1,0:T(8,128)(2,1)S(1)}, bf16[2,64,128]{2,1,0:T(8,128)(2,1)}, u32[]{:S(2)}) copy-start(bf16[2,64,128]{2,1,0:T(8,128)(2,1)} %constant.12.clone.refs_11_.inverse_high) | copy-start | bytes 98308
  4.1 16.0 %copy-start.5 = (bf16[128,128]{1,0:T(8,128)(2,1)S(1)}, bf16[128,128]{1,0:T(8,128)(2,1)}, u32[]{:S(2)}) copy-start(bf16[128,128]{1,0:T(8,128)(2,1)} %constant.11.clone.refs_10_) | copy-start | bytes 98308
  4.1 16.0 %copy-start.6 = (bf16[128,128]{1,0:T(8,128)(2,1)S(1)}, bf16[128,128]{1,0:T(8,128)(2,1)}, u32[]{:S(2)}) copy-start(bf16[128,128]{1,0:T(8,128)(2,1)} %constant.10.clone.refs_9_) | copy-start | bytes 98308
  4.1 6.6 %collective-permute-start.1 = (f32[2,16,512]{2,1,0:T(8,128)S(1)}, f32[2,16,512]{2,1,0:T(8,128)S(1)}, u32[]{:S(2)}, u32[]{:S(2)}) collective-permute-start(f32[2,16,512]{2,1,0:T(8,128)S(1)} %get-tuple-element.16), channel_id=1, source_target_pairs={{0,8},{1,11},{2,10},{3,9},{4,12},{5,15},{6,14},{7,13},{8,0},{9,3},... | collective-permute-start | bytes 196616 | tf_op jit(solution)/shard_map/ppermute | solution.py:280
  8.2 5.3 %collective-permute-start.2 = (f32[2,16,512]{2,1,0:T(8,128)S(1)}, f32[2,16,512]{2,1,0:T(8,128)S(1)}, u32[]{:S(2)}, u32[]{:S(2)}) collective-permute-start(f32[2,16,512]{2,1,0:T(8,128)S(1)} %get-tuple-element.17), channel_id=1, source_target_pairs={{0,4},{1,7},{2,6},{3,5},{4,0},{5,3},{6,2},{7,1},{8,12},{9,15},{10,... | collective-permute-start | bytes 196616 | tf_op jit(solution)/shard_map/ppermute | solution.py:280
  9.7 4.1 %collective-permute-start.3 = (f32[2,16,512]{2,1,0:T(8,128)S(1)}, f32[2,16,512]{2,1,0:T(8,128)S(1)}, u32[]{:S(2)}, u32[]{:S(2)}) collective-permute-start(f32[2,16,512]{2,1,0:T(8,128)S(1)} %get-tuple-element.18), channel_id=1, source_target_pairs={{0,0},{1,3},{2,2},{3,1},{4,4},{5,7},{6,6},{7,5},{8,8},{9,11},{10,1... | collective-permute-start | bytes 196616 | tf_op jit(solution)/shard_map/ppermute | solution.py:280
  10.4 23.1 %copy-start = (bf16[4,256,512]{2,1,0:T(8,128)(2,1)S(1)}, bf16[4,256,512]{2,1,0:T(8,128)(2,1)}, u32[]{:S(2)}) copy-start(bf16[4,256,512]{2,1,0:T(8,128)(2,1)} %flow_ref.1) | copy-start | bytes 3145732
  10.4 6.2 %collective-permute-start.4 = (f32[2,16,512]{2,1,0:T(8,128)S(1)}, f32[2,16,512]{2,1,0:T(8,128)S(1)}, u32[]{:S(2)}, u32[]{:S(2)}) collective-permute-start(f32[2,16,512]{2,1,0:T(8,128)S(1)} %get-tuple-element.19), channel_id=1, source_target_pairs={{0,12},{1,15},{2,14},{3,13},{4,8},{5,11},{6,10},{7,9},{8,4},{9,7},... | collective-permute-start | bytes 196616 | tf_op jit(solution)/shard_map/ppermute | solution.py:280
  10.8 8.4 %collective-permute-start.5 = (f32[2,16,512]{2,1,0:T(8,128)S(1)}, f32[2,16,512]{2,1,0:T(8,128)S(1)}, u32[]{:S(2)}, u32[]{:S(2)}) collective-permute-start(f32[2,16,512]{2,1,0:T(8,128)S(1)} %collective-permute-done.1.refs_0_), channel_id=1, source_target_pairs={{0,1},{1,0},{2,3},{3,2},{4,5},{5,4},{6,7},{7,6},{8,9},{9,8},{10,11... | collective-permute-start | bytes 196616 | tf_op jit(solution)/shard_map/ppermute | solution.py:269
  13.5 5.7 %collective-permute-start.6 = (f32[2,16,512]{2,1,0:T(8,128)S(1)}, f32[2,16,512]{2,1,0:T(8,128)S(1)}, u32[]{:S(2)}, u32[]{:S(2)}) collective-permute-start(f32[2,16,512]{2,1,0:T(8,128)S(1)} %collective-permute-done.2.refs_1_), channel_id=1, source_target_pairs={{0,1},{1,0},{2,3},{3,2},{4,5},{5,4},{6,7},{7,6},{8,9},{9,8},{10,11... | collective-permute-start | bytes 196616 | tf_op jit(solution)/shard_map/ppermute | solution.py:269
  13.8 5.4 %collective-permute-start.7 = (f32[2,16,512]{2,1,0:T(8,128)S(1)}, f32[2,16,512]{2,1,0:T(8,128)S(1)}, u32[]{:S(2)}, u32[]{:S(2)}) collective-permute-start(f32[2,16,512]{2,1,0:T(8,128)S(1)} %collective-permute-done.3.refs_2_), channel_id=1, source_target_pairs={{0,1},{1,0},{2,3},{3,2},{4,5},{5,4},{6,7},{7,6},{8,9},{9,8},{10,11... | collective-permute-start | bytes 196616 | tf_op jit(solution)/shard_map/ppermute | solution.py:269
  16.6 3.5 %collective-permute-start.8 = (f32[2,16,512]{2,1,0:T(8,128)S(1)}, f32[2,16,512]{2,1,0:T(8,128)S(1)}, u32[]{:S(2)}, u32[]{:S(2)}) collective-permute-start(f32[2,16,512]{2,1,0:T(8,128)S(1)} %collective-permute-done.4.refs_3_), channel_id=1, source_target_pairs={{0,1},{1,0},{2,3},{3,2},{4,5},{5,4},{6,7},{7,6},{8,9},{9,8},{10,11... | collective-permute-start | bytes 196616 | tf_op jit(solution)/shard_map/ppermute | solution.py:269
  21.2 1.4 %collective-permute-start.9 = (f32[4,16,512]{2,1,0:T(8,128)S(1)}, f32[4,16,512]{2,1,0:T(8,128)S(1)}, u32[]{:S(2)}, u32[]{:S(2)}) collective-permute-start(f32[4,16,512]{2,1,0:T(8,128)S(1)} %get-tuple-element.21), channel_id=1, source_target_pairs={{0,1},{1,0},{2,3},{3,2},{4,5},{5,4},{6,7},{7,6},{8,9},{9,8},{10,11... | collective-permute-start | bytes 393224 | tf_op jit(solution)/shard_map/ppermute | solution.py:269
  22.7 5.6 %collective-permute-start.10 = (f32[4,8,512]{2,1,0:T(8,128)S(1)}, f32[4,8,512]{2,1,0:T(8,128)S(1)}, u32[]{:S(2)}, u32[]{:S(2)}) collective-permute-start(f32[4,8,512]{2,1,0:T(8,128)S(1)} %get-tuple-element.22), channel_id=1, source_target_pairs={{0,8},{1,11},{2,10},{3,9},{4,12},{5,15},{6,14},{7,13},{8,0},{9,3},... | collective-permute-start | bytes 196616 | tf_op jit(solution)/shard_map/ppermute | solution.py:280
  22.7 8.1 %collective-permute-start.11 = (f32[4,8,512]{2,1,0:T(8,128)S(1)}, f32[4,8,512]{2,1,0:T(8,128)S(1)}, u32[]{:S(2)}, u32[]{:S(2)}) collective-permute-start(f32[4,8,512]{2,1,0:T(8,128)S(1)} %get-tuple-element.23), channel_id=1, source_target_pairs={{0,4},{1,7},{2,6},{3,5},{4,0},{5,3},{6,2},{7,1},{8,12},{9,15},{10,... | collective-permute-start | bytes 196616 | tf_op jit(solution)/shard_map/ppermute | solution.py:280
  23.5 7.4 %collective-permute-start.12 = (f32[4,8,512]{2,1,0:T(8,128)S(1)}, f32[4,8,512]{2,1,0:T(8,128)S(1)}, u32[]{:S(2)}, u32[]{:S(2)}) collective-permute-start(f32[4,8,512]{2,1,0:T(8,128)S(1)} %get-tuple-element.24), channel_id=1, source_target_pairs={{0,0},{1,3},{2,2},{3,1},{4,4},{5,7},{6,6},{7,5},{8,8},{9,11},{10,1... | collective-permute-start | bytes 196616 | tf_op jit(solution)/shard_map/ppermute | solution.py:280
  24.3 7.0 %collective-permute-start.13 = (f32[4,8,512]{2,1,0:T(8,128)S(1)}, f32[4,8,512]{2,1,0:T(8,128)S(1)}, u32[]{:S(2)}, u32[]{:S(2)}) collective-permute-start(f32[4,8,512]{2,1,0:T(8,128)S(1)} %get-tuple-element.25), channel_id=1, source_target_pairs={{0,12},{1,15},{2,14},{3,13},{4,8},{5,11},{6,10},{7,9},{8,4},{9,7},... | collective-permute-start | bytes 196616 | tf_op jit(solution)/shard_map/ppermute | solution.py:280
  28.2 4.3 %collective-permute-start.14 = (f32[4,8,512]{2,1,0:T(8,128)S(1)}, f32[4,8,512]{2,1,0:T(8,128)S(1)}, u32[]{:S(2)}, u32[]{:S(2)}) collective-permute-start(f32[4,8,512]{2,1,0:T(8,128)S(1)} %collective-permute-done.10.refs_0_), channel_id=1, source_target_pairs={{0,1},{1,0},{2,3},{3,2},{4,5},{5,4},{6,7},{7,6},{8,9},{9,8},{10,11... | collective-permute-start | bytes 196616 | tf_op jit(solution)/shard_map/ppermute | solution.py:269
  30.8 1.8 %collective-permute-start.15 = (f32[4,8,512]{2,1,0:T(8,128)S(1)}, f32[4,8,512]{2,1,0:T(8,128)S(1)}, u32[]{:S(2)}, u32[]{:S(2)}) collective-permute-start(f32[4,8,512]{2,1,0:T(8,128)S(1)} %collective-permute-done.11.refs_1_), channel_id=1, source_target_pairs={{0,1},{1,0},{2,3},{3,2},{4,5},{5,4},{6,7},{7,6},{8,9},{9,8},{10,11... | collective-permute-start | bytes 196616 | tf_op jit(solution)/shard_map/ppermute | solution.py:269
  30.9 1.7 %collective-permute-start.16 = (f32[4,8,512]{2,1,0:T(8,128)S(1)}, f32[4,8,512]{2,1,0:T(8,128)S(1)}, u32[]{:S(2)}, u32[]{:S(2)}) collective-permute-start(f32[4,8,512]{2,1,0:T(8,128)S(1)} %collective-permute-done.12.refs_2_), channel_id=1, source_target_pairs={{0,1},{1,0},{2,3},{3,2},{4,5},{5,4},{6,7},{7,6},{8,9},{9,8},{10,11... | collective-permute-start | bytes 196616 | tf_op jit(solution)/shard_map/ppermute | solution.py:269
  31.3 2.1 %collective-permute-start.17 = (f32[4,8,512]{2,1,0:T(8,128)S(1)}, f32[4,8,512]{2,1,0:T(8,128)S(1)}, u32[]{:S(2)}, u32[]{:S(2)}) collective-permute-start(f32[4,8,512]{2,1,0:T(8,128)S(1)} %collective-permute-done.13.refs_3_), channel_id=1, source_target_pairs={{0,1},{1,0},{2,3},{3,2},{4,5},{5,4},{6,7},{7,6},{8,9},{9,8},{10,11... | collective-permute-start | bytes 196616 | tf_op jit(solution)/shard_map/ppermute | solution.py:269
  (3 other events, 33.1 us)

commit v13 on v11

--- a/solution.py
+++ b/solution.py
@@ -129,6 +129,7 @@
 SMALL = pltpu.CompilerParams(vmem_limit_bytes=20 * 1024 * 1024)
 LARGE = pltpu.CompilerParams(vmem_limit_bytes=53 * 1024 * 1024)
 WIDTH = 256
+BIAS_TERMS = 3
 GELU_TERMS = (
     0.7978849411010742,
     0.03633308410644531,
@@ -209,6 +210,14 @@
                     half = y ^ place ^ column ^ (peer % 2)
                     out[y, column, :, peer, place] = np.moveaxis(full[half, peer, :, :, y], -1, 0)
     return out.reshape(groups_y, 2, cells_y, 4 * peers * rows_ky)
+
+
+def output_table(table):
+    high, low = split_table(table)
+    parts = [high, high, low, np.ones(table.shape[:-1] + (BIAS_TERMS,), high.dtype)]
+    used = 3 * table.shape[-1] + BIAS_TERMS
+    parts.append(np.zeros(table.shape[:-1] + (-used % 256,), high.dtype))
+    return np.concatenate(parts, axis=-1)
 
 
 def dot(left, right):
@@ -445,6 +454,15 @@
         span = slice(start, start + channels)
         wide_ref[span, span] = local_ref[...]
         level_ref[:, span] = bias_ref[...].reshape(1, channels)
+    level = level_ref[...]
+    levels = []
+    for _ in range(BIAS_TERMS):
+        levels.append(level.astype(jnp.bfloat16).astype(jnp.float32))
+        level = level - levels[-1]
+    terms = 3 * order_ref.shape[1] * order_ref.shape[2]
+    filled = jnp.zeros((table_ref.shape[-1] - terms - BIAS_TERMS, WIDTH), jnp.float32)
+    below = jnp.concatenate(levels + [filled], axis=0).astype(jnp.bfloat16)
+    below = jnp.concatenate([below, wide_ref[...]], axis=0)
     for column, block_refs in ((x ^ y, own_refs), (x ^ y ^ 1, core_refs)):
         for turn, block_ref in zip(turns(layers), block_refs):
             order_ref[:, (z ^ turn) * 2 + column] = block_ref[...]
@@ -454,8 +472,11 @@
         stack = jnp.concatenate([high, low, high], axis=0)
         for start in range(0, feat_count, WIDTH):
             columns = slice(start, start + WIDTH)
-            total = dot(table, stack[:, columns]) + dot(flow_ref[cell, :, columns], wide_ref[...])
-            done_ref[cell, :, columns] = gelu(total + level_ref[...]).astype(done_ref.dtype)
+            total = dot(
+                jnp.concatenate([table, flow_ref[cell, :, columns]], axis=1),
+                jnp.concatenate([stack[:, columns], below], axis=0),
+            )
+            done_ref[cell, :, columns] = gelu(total).astype(done_ref.dtype)
         copies.append(pltpu.make_async_copy(done_ref.at[cell], out_hbm.at[cell], sent.at[cell]))
         copies[-1].start()
     for copy in copies:
@@ -507,8 +528,7 @@
     keep = keep_rows(modes, inverse_tables, send)
     own = along_columns(join_blocks(keep, arrived, cells_x), peers)
     parts = own + [flip_core(block) for block in own]
-    high, low = split_table(inverse_y_table(cells_y, groups_y, peers, rows_ky) * inverse_scale)
-    table = np.concatenate([high, high, low], axis=-1)
+    table = output_table(inverse_y_table(cells_y, groups_y, peers, rows_ky) * inverse_scale)
     return tuple(make_output(flow_field, parts, table, local_weight, bias_terms, modes))
 
 

time: 34.2 us -> 34.1 us (level)
  no operation moved by 1% of the time
where the time goes in v13:
time: 34.1 us; the launch traced here: 34 us
  starting transfers between devices  16.8 us (49%)
  waiting for transfers between devices  10.7 us (31%)
  Pallas kernels  5.65 us (17%)
  between operations  0.75 us (2%)
    ppermute x8, starting transfers between devices, along_columns(): arrived.append(lax.ppermute(block, ('gx', 'gy'), pairs))  11.2 us
    ppermute x8, waiting for transfers between devices, along_columns(): arrived.append(lax.ppermute(block, ('gx', 'gy'), pairs))  6.79 us
    ppermute x10, starting transfers between devices, flip_core(): return lax.ppermute(block, 'gy', [(0, 1), (1, 0)])  5.64 us
    ppermute x10, waiting for transfers between devices, flip_core(): return lax.ppermute(block, 'gy', [(0, 1), (1, 0)])  3.92 us
    pallas_call x1, Pallas kernels, make_output(): pl.pallas_call(functools.partial(output_kernel, layers), out_specs=[pl.Bl...  2.56 us
    pallas_call x1, Pallas kernels, forward_y(): pl.pallas_call(functools.partial(forward_y_kernel, extent, rows_ky), in_s...  1.75 us
    pallas_call x1, Pallas kernels, mix(): pl.pallas_call(functools.partial(mix_kernel, layers), out_shape=[jax.Shap...  1.05 us
  transfers between devices with their start and end apart: 18, of which 13 were waited for; matrix products, arithmetic and copies ran while one was open for 0% of the time, Pallas kernels for 1%

profile of v13, /device:TPU:0, one launch (start us, length us, event | category | flops | bytes accessed | tf_op | source)
XLA Modules:
  0.0 34.0 jit_solution(16922921358436053462)
XLA Ops:
  0.6 1.7 %forward_y.1 = (f32[4,2,16,512]{3,2,1,0:T(8,128)S(1)}, f32[4,2,16,512]{3,2,1,0:T(8,128)S(1)}) custom-call(bf16[4,256,512]{2,1,0:T(8,128)(2,1)} %flow_ref.1), custom_call_target="tpu_custom_call" | custom-call | tf_op jit(solution)/shard_map/forward_y/pallas_call | solution.py:264
  2.4 0.5 %collective-permute-start = (f32[4,2,16,512]{3,2,1,0:T(8,128)S(1)}, f32[4,2,16,512]{3,2,1,0:T(8,128)S(1)}, u32[]{:S(2)}, u32[]{:S(2)}) collective-permute-start(f32[4,2,16,512]{3,2,1,0:T(8,128)S(1)} %get-tuple-element.15), channel_id=1, source_target_pairs={{0,1},{1,0},{2,3},{3,2},{4,5},{5,4},{6,7},{7,6},{8,9},{9,8},{10,11... | collective-permute-start | bytes 786440 | tf_op jit(solution)/shard_map/ppermute | solution.py:278
  2.9 1.2 %collective-permute-done.arrived_ref = f32[4,2,16,512]{3,2,1,0:T(8,128)S(1)} collective-permute-done((f32[4,2,16,512]{3,2,1,0:T(8,128)S(1)}, f32[4,2,16,512]{3,2,1,0:T(8,128)S(1)}, u32[]{:S(2)}, u32[]{:S(2)}) %collective-permute-start) | collective-permute-done | bytes 262176 | tf_op jit(solution)/shard_map/ppermute | solution.py:278
  4.1 4.0 %collective-permute-start.1 = (f32[2,16,512]{2,1,0:T(8,128)S(1)}, f32[2,16,512]{2,1,0:T(8,128)S(1)}, u32[]{:S(2)}, u32[]{:S(2)}) collective-permute-start(f32[2,16,512]{2,1,0:T(8,128)S(1)} %get-tuple-element.16), channel_id=1, source_target_pairs={{0,8},{1,11},{2,10},{3,9},{4,12},{5,15},{6,14},{7,13},{8,0},{9,3},... | collective-permute-start | bytes 196616 | tf_op jit(solution)/shard_map/ppermute | solution.py:289
  8.2 1.3 %collective-permute-start.2 = (f32[2,16,512]{2,1,0:T(8,128)S(1)}, f32[2,16,512]{2,1,0:T(8,128)S(1)}, u32[]{:S(2)}, u32[]{:S(2)}) collective-permute-start(f32[2,16,512]{2,1,0:T(8,128)S(1)} %get-tuple-element.17), channel_id=1, source_target_pairs={{0,12},{1,15},{2,14},{3,13},{4,8},{5,11},{6,10},{7,9},{8,4},{9,7},... | collective-permute-start | bytes 196616 | tf_op jit(solution)/shard_map/ppermute | solution.py:289
  9.7 0.8 %collective-permute-start.4 = (f32[2,16,512]{2,1,0:T(8,128)S(1)}, f32[2,16,512]{2,1,0:T(8,128)S(1)}, u32[]{:S(2)}, u32[]{:S(2)}) collective-permute-start(f32[2,16,512]{2,1,0:T(8,128)S(1)} %get-tuple-element.19), channel_id=1, source_target_pairs={{0,0},{1,3},{2,2},{3,1},{4,4},{5,7},{6,6},{7,5},{8,8},{9,11},{10,1... | collective-permute-start | bytes 196616 | tf_op jit(solution)/shard_map/ppermute | solution.py:289
  10.8 2.8 %collective-permute-start.5 = (f32[2,16,512]{2,1,0:T(8,128)S(1)}, f32[2,16,512]{2,1,0:T(8,128)S(1)}, u32[]{:S(2)}, u32[]{:S(2)}) collective-permute-start(f32[2,16,512]{2,1,0:T(8,128)S(1)} %collective-permute-done.1.refs_0_), channel_id=1, source_target_pairs={{0,1},{1,0},{2,3},{3,2},{4,5},{5,4},{6,7},{7,6},{8,9},{9,8},{10,11... | collective-permute-start | bytes 196616 | tf_op jit(solution)/shard_map/ppermute | solution.py:278
  13.5 1.3 %collective-permute-done.2.refs_1_ = f32[2,16,512]{2,1,0:T(8,128)S(1)} collective-permute-done((f32[2,16,512]{2,1,0:T(8,128)S(1)}, f32[2,16,512]{2,1,0:T(8,128)S(1)}, u32[]{:S(2)}, u32[]{:S(2)}) %collective-permute-start.2) | collective-permute-done | bytes 65568 | tf_op jit(solution)/shard_map/ppermute | solution.py:289
  14.9 0.5 %collective-permute-start.6 = (f32[2,16,512]{2,1,0:T(8,128)S(1)}, f32[2,16,512]{2,1,0:T(8,128)S(1)}, u32[]{:S(2)}, u32[]{:S(2)}) collective-permute-start(f32[2,16,512]{2,1,0:T(8,128)S(1)} %collective-permute-done.2.refs_1_), channel_id=1, source_target_pairs={{0,1},{1,0},{2,3},{3,2},{4,5},{5,4},{6,7},{7,6},{8,9},{9,8},{10,11... | collective-permute-start | bytes 196616 | tf_op jit(solution)/shard_map/ppermute | solution.py:278
  15.7 0.3 collective-permute-start.8
  16.2 0.6 %collective-permute-done.7.refs_6_ = f32[2,16,512]{2,1,0:T(8,128)S(1)} collective-permute-done((f32[2,16,512]{2,1,0:T(8,128)S(1)}, f32[2,16,512]{2,1,0:T(8,128)S(1)}, u32[]{:S(2)}, u32[]{:S(2)}) %collective-permute-start.7) | collective-permute-done | bytes 65568 | tf_op jit(solution)/shard_map/ppermute | solution.py:278
  17.0 1.1 %mix.1 = (f32[128,512]{1,0:T(8,128)S(1)}, f32[4,16,512]{2,1,0:T(8,128)S(1)}) custom-call(f32[2,16,512]{2,1,0:T(8,128)S(1)} %collective-permute-done.1.refs_0_, f32[2,16,512]{2,1,0:T(8,128)S(1)} %collective-permute-done.2.refs_1_, f32[2,16,512]{2,1,0:T(8,128)S(1)} %collective-permute-done.3.refs_2_, f32[2,16,512]{2,1,0:T(8,128)S(1)} %collective-permute-done.4.refs_3_, ...), custom_call_target="tpu_custom_call" | custom-call | tf_op jit(solution)/shard_map/mix/pallas_call | solution.py:397
  18.1 0.4 %collective-permute-start.9 = (f32[4,16,512]{2,1,0:T(8,128)S(1)}, f32[4,16,512]{2,1,0:T(8,128)S(1)}, u32[]{:S(2)}, u32[]{:S(2)}) collective-permute-start(f32[4,16,512]{2,1,0:T(8,128)S(1)} %get-tuple-element.21), channel_id=1, source_target_pairs={{0,1},{1,0},{2,3},{3,2},{4,5},{5,4},{6,7},{7,6},{8,9},{9,8},{10,11... | collective-permute-start | bytes 393224 | tf_op jit(solution)/shard_map/ppermute | solution.py:278
  18.7 0.8 %collective-permute-done.9.arrived_ref = f32[4,16,512]{2,1,0:T(8,128)S(1)} collective-permute-done((f32[4,16,512]{2,1,0:T(8,128)S(1)}, f32[4,16,512]{2,1,0:T(8,128)S(1)}, u32[]{:S(2)}, u32[]{:S(2)}) %collective-permute-start.9) | collective-permute-done | bytes 131104 | tf_op jit(solution)/shard_map/ppermute | solution.py:278
  19.6 3.1 %collective-permute-start.10 = (f32[4,8,512]{2,1,0:T(8,128)S(1)}, f32[4,8,512]{2,1,0:T(8,128)S(1)}, u32[]{:S(2)}, u32[]{:S(2)}) collective-permute-start(f32[4,8,512]{2,1,0:T(8,128)S(1)} %get-tuple-element.22), channel_id=1, source_target_pairs={{0,8},{1,11},{2,10},{3,9},{4,12},{5,15},{6,14},{7,13},{8,0},{9,3},... | collective-permute-start | bytes 196616 | tf_op jit(solution)/shard_map/ppermute | solution.py:289
  22.7 1.0 %collective-permute-start.11 = (f32[4,8,512]{2,1,0:T(8,128)S(1)}, f32[4,8,512]{2,1,0:T(8,128)S(1)}, u32[]{:S(2)}, u32[]{:S(2)}) collective-permute-start(f32[4,8,512]{2,1,0:T(8,128)S(1)} %get-tuple-element.23), channel_id=1, source_target_pairs={{0,12},{1,15},{2,14},{3,13},{4,8},{5,11},{6,10},{7,9},{8,4},{9,7},... | collective-permute-start | bytes 196616 | tf_op jit(solution)/shard_map/ppermute | solution.py:289
  23.7 0.7 %collective-permute-start.13 = (f32[4,8,512]{2,1,0:T(8,128)S(1)}, f32[4,8,512]{2,1,0:T(8,128)S(1)}, u32[]{:S(2)}, u32[]{:S(2)}) collective-permute-start(f32[4,8,512]{2,1,0:T(8,128)S(1)} %get-tuple-element.25), channel_id=1, source_target_pairs={{0,0},{1,3},{2,2},{3,1},{4,4},{5,7},{6,6},{7,5},{8,8},{9,11},{10,1... | collective-permute-start | bytes 196616 | tf_op jit(solution)/shard_map/ppermute | solution.py:289
  24.4 2.6 %collective-permute-done.10.refs_0_ = f32[4,8,512]{2,1,0:T(8,128)S(1)} collective-permute-done((f32[4,8,512]{2,1,0:T(8,128)S(1)}, f32[4,8,512]{2,1,0:T(8,128)S(1)}, u32[]{:S(2)}, u32[]{:S(2)}) %collective-permute-start.10) | collective-permute-done | bytes 65568 | tf_op jit(solution)/shard_map/ppermute | solution.py:289
  27.1 2.4 %collective-permute-done.11.refs_1_ = f32[4,8,512]{2,1,0:T(8,128)S(1)} collective-permute-done((f32[4,8,512]{2,1,0:T(8,128)S(1)}, f32[4,8,512]{2,1,0:T(8,128)S(1)}, u32[]{:S(2)}, u32[]{:S(2)}) %collective-permute-start.11) | collective-permute-done | bytes 65568 | tf_op jit(solution)/shard_map/ppermute | solution.py:289
  29.5 0.4 %collective-permute-start.15 = (f32[4,8,512]{2,1,0:T(8,128)S(1)}, f32[4,8,512]{2,1,0:T(8,128)S(1)}, u32[]{:S(2)}, u32[]{:S(2)}) collective-permute-start(f32[4,8,512]{2,1,0:T(8,128)S(1)} %collective-permute-done.11.refs_1_), channel_id=1, source_target_pairs={{0,1},{1,0},{2,3},{3,2},{4,5},{5,4},{6,7},{7,6},{8,9},{9,8},{10,11... | collective-permute-start | bytes 196616 | tf_op jit(solution)/shard_map/ppermute | solution.py:278
  30.4 0.4 %collective-permute-done.15.refs_5_ = f32[4,8,512]{2,1,0:T(8,128)S(1)} collective-permute-done((f32[4,8,512]{2,1,0:T(8,128)S(1)}, f32[4,8,512]{2,1,0:T(8,128)S(1)}, u32[]{:S(2)}, u32[]{:S(2)}) %collective-permute-start.15) | collective-permute-done | bytes 65568 | tf_op jit(solution)/shard_map/ppermute | solution.py:278
  30.7 0.4 %collective-permute-done.16.refs_6_ = f32[4,8,512]{2,1,0:T(8,128)S(1)} collective-permute-done((f32[4,8,512]{2,1,0:T(8,128)S(1)}, f32[4,8,512]{2,1,0:T(8,128)S(1)}, u32[]{:S(2)}, u32[]{:S(2)}) %collective-permute-start.16) | collective-permute-done | bytes 65568 | tf_op jit(solution)/shard_map/ppermute | solution.py:278
  31.1 0.3 collective-permute-done.17.refs_7_
  31.4 2.6 %make_output.1 = (bf16[4,256,512]{2,1,0:T(8,128)(2,1)}, f32[1,64,1024]{2,1,0:T(8,128)}) custom-call(bf16[4,256,512]{2,1,0:T(8,128)(2,1)S(1)} %copy-done, bf16[2,2,256,256]{3,2,1,0:T(8,128)(2,1)S(1)} %copy-done.2, bf16[64,64]{1,0:T(8,128)(2,1)S(1)} %copy-done.7, f32[64]{0:T(128)S(1)} %copy-done.8, f32[128,512]{1,0:T(8,128)S(1)} %get-tuple-element.20.modes_ref, ...), custom_call_target="tpu_custom_call" | custom-call | tf_op jit(solution)/shard_map/make_output/pallas_call | solution.py:490
  (36 shorter events, 2.3 us)
Async XLA Ops:
  0.6 16.4 %copy-start.1 = (bf16[1,64,64,128]{3,2,1,0:T(8,128)(2,1)S(1)}, bf16[1,64,64,128]{3,2,1,0:T(8,128)(2,1)}, u32[]{:S(2)}) copy-start(bf16[1,64,64,128]{3,2,1,0:T(8,128)(2,1)} %refs_8_.1) | copy-start | bytes 3145732
  2.4 1.7 %collective-permute-start = (f32[4,2,16,512]{3,2,1,0:T(8,128)S(1)}, f32[4,2,16,512]{3,2,1,0:T(8,128)S(1)}, u32[]{:S(2)}, u32[]{:S(2)}) collective-permute-start(f32[4,2,16,512]{3,2,1,0:T(8,128)S(1)} %get-tuple-element.15), channel_id=1, source_target_pairs={{0,1},{1,0},{2,3},{3,2},{4,5},{5,4},{6,7},{7,6},{8,9},{9,8},{10,11... | collective-permute-start | bytes 786440 | tf_op jit(solution)/shard_map/ppermute | solution.py:278
  4.1 12.9 %copy-start.4 = (bf16[2,64,128]{2,1,0:T(8,128)(2,1)S(1)}, bf16[2,64,128]{2,1,0:T(8,128)(2,1)}, u32[]{:S(2)}) copy-start(bf16[2,64,128]{2,1,0:T(8,128)(2,1)} %constant.12.clone.refs_11_.inverse_high) | copy-start | bytes 98308
  4.1 12.9 %copy-start.5 = (bf16[128,128]{1,0:T(8,128)(2,1)S(1)}, bf16[128,128]{1,0:T(8,128)(2,1)}, u32[]{:S(2)}) copy-start(bf16[128,128]{1,0:T(8,128)(2,1)} %constant.11.clone.refs_10_) | copy-start | bytes 98308
  4.1 12.9 %copy-start.6 = (bf16[128,128]{1,0:T(8,128)(2,1)S(1)}, bf16[128,128]{1,0:T(8,128)(2,1)}, u32[]{:S(2)}) copy-start(bf16[128,128]{1,0:T(8,128)(2,1)} %constant.10.clone.refs_9_) | copy-start | bytes 98308
  4.1 6.6 %collective-permute-start.1 = (f32[2,16,512]{2,1,0:T(8,128)S(1)}, f32[2,16,512]{2,1,0:T(8,128)S(1)}, u32[]{:S(2)}, u32[]{:S(2)}) collective-permute-start(f32[2,16,512]{2,1,0:T(8,128)S(1)} %get-tuple-element.16), channel_id=1, source_target_pairs={{0,8},{1,11},{2,10},{3,9},{4,12},{5,15},{6,14},{7,13},{8,0},{9,3},... | collective-permute-start | bytes 196616 | tf_op jit(solution)/shard_map/ppermute | solution.py:289
  8.2 6.7 %collective-permute-start.2 = (f32[2,16,512]{2,1,0:T(8,128)S(1)}, f32[2,16,512]{2,1,0:T(8,128)S(1)}, u32[]{:S(2)}, u32[]{:S(2)}) collective-permute-start(f32[2,16,512]{2,1,0:T(8,128)S(1)} %get-tuple-element.17), channel_id=1, source_target_pairs={{0,12},{1,15},{2,14},{3,13},{4,8},{5,11},{6,10},{7,9},{8,4},{9,7},... | collective-permute-start | bytes 196616 | tf_op jit(solution)/shard_map/ppermute | solution.py:289
  9.5 6.0 %collective-permute-start.3 = (f32[2,16,512]{2,1,0:T(8,128)S(1)}, f32[2,16,512]{2,1,0:T(8,128)S(1)}, u32[]{:S(2)}, u32[]{:S(2)}) collective-permute-start(f32[2,16,512]{2,1,0:T(8,128)S(1)} %get-tuple-element.18), channel_id=1, source_target_pairs={{0,4},{1,7},{2,6},{3,5},{4,0},{5,3},{6,2},{7,1},{8,12},{9,15},{10,... | collective-permute-start | bytes 196616 | tf_op jit(solution)/shard_map/ppermute | solution.py:289
  9.7 21.6 %copy-start = (bf16[4,256,512]{2,1,0:T(8,128)(2,1)S(1)}, bf16[4,256,512]{2,1,0:T(8,128)(2,1)}, u32[]{:S(2)}) copy-start(bf16[4,256,512]{2,1,0:T(8,128)(2,1)} %flow_ref.1) | copy-start | bytes 3145732
  9.7 6.0 %collective-permute-start.4 = (f32[2,16,512]{2,1,0:T(8,128)S(1)}, f32[2,16,512]{2,1,0:T(8,128)S(1)}, u32[]{:S(2)}, u32[]{:S(2)}) collective-permute-start(f32[2,16,512]{2,1,0:T(8,128)S(1)} %get-tuple-element.19), channel_id=1, source_target_pairs={{0,0},{1,3},{2,2},{3,1},{4,4},{5,7},{6,6},{7,5},{8,8},{9,11},{10,1... | collective-permute-start | bytes 196616 | tf_op jit(solution)/shard_map/ppermute | solution.py:289
  10.8 5.3 %collective-permute-start.5 = (f32[2,16,512]{2,1,0:T(8,128)S(1)}, f32[2,16,512]{2,1,0:T(8,128)S(1)}, u32[]{:S(2)}, u32[]{:S(2)}) collective-permute-start(f32[2,16,512]{2,1,0:T(8,128)S(1)} %collective-permute-done.1.refs_0_), channel_id=1, source_target_pairs={{0,1},{1,0},{2,3},{3,2},{4,5},{5,4},{6,7},{7,6},{8,9},{9,8},{10,11... | collective-permute-start | bytes 196616 | tf_op jit(solution)/shard_map/ppermute | solution.py:278
  14.9 1.4 %collective-permute-start.6 = (f32[2,16,512]{2,1,0:T(8,128)S(1)}, f32[2,16,512]{2,1,0:T(8,128)S(1)}, u32[]{:S(2)}, u32[]{:S(2)}) collective-permute-start(f32[2,16,512]{2,1,0:T(8,128)S(1)} %collective-permute-done.2.refs_1_), channel_id=1, source_target_pairs={{0,1},{1,0},{2,3},{3,2},{4,5},{5,4},{6,7},{7,6},{8,9},{9,8},{10,11... | collective-permute-start | bytes 196616 | tf_op jit(solution)/shard_map/ppermute | solution.py:278
  15.5 1.3 %collective-permute-start.7 = (f32[2,16,512]{2,1,0:T(8,128)S(1)}, f32[2,16,512]{2,1,0:T(8,128)S(1)}, u32[]{:S(2)}, u32[]{:S(2)}) collective-permute-start(f32[2,16,512]{2,1,0:T(8,128)S(1)} %collective-permute-done.3.refs_2_), channel_id=1, source_target_pairs={{0,1},{1,0},{2,3},{3,2},{4,5},{5,4},{6,7},{7,6},{8,9},{9,8},{10,11... | collective-permute-start | bytes 196616 | tf_op jit(solution)/shard_map/ppermute | solution.py:278
  15.7 1.3 %collective-permute-start.8 = (f32[2,16,512]{2,1,0:T(8,128)S(1)}, f32[2,16,512]{2,1,0:T(8,128)S(1)}, u32[]{:S(2)}, u32[]{:S(2)}) collective-permute-start(f32[2,16,512]{2,1,0:T(8,128)S(1)} %collective-permute-done.4.refs_3_), channel_id=1, source_target_pairs={{0,1},{1,0},{2,3},{3,2},{4,5},{5,4},{6,7},{7,6},{8,9},{9,8},{10,11... | collective-permute-start | bytes 196616 | tf_op jit(solution)/shard_map/ppermute | solution.py:278
  18.1 13.3 %copy-start.2 = (bf16[2,2,256,256]{3,2,1,0:T(8,128)(2,1)S(1)}, bf16[2,2,256,256]{3,2,1,0:T(8,128)(2,1)}, u32[]{:S(2)}) copy-start(bf16[2,2,256,256]{3,2,1,0:T(8,128)(2,1)} %constant.14.clone.table_ref) | copy-start | bytes 1572868
  18.1 1.4 %collective-permute-start.9 = (f32[4,16,512]{2,1,0:T(8,128)S(1)}, f32[4,16,512]{2,1,0:T(8,128)S(1)}, u32[]{:S(2)}, u32[]{:S(2)}) collective-permute-start(f32[4,16,512]{2,1,0:T(8,128)S(1)} %get-tuple-element.21), channel_id=1, source_target_pairs={{0,1},{1,0},{2,3},{3,2},{4,5},{5,4},{6,7},{7,6},{8,9},{9,8},{10,11... | collective-permute-start | bytes 393224 | tf_op jit(solution)/shard_map/ppermute | solution.py:278
  19.6 7.4 %collective-permute-start.10 = (f32[4,8,512]{2,1,0:T(8,128)S(1)}, f32[4,8,512]{2,1,0:T(8,128)S(1)}, u32[]{:S(2)}, u32[]{:S(2)}) collective-permute-start(f32[4,8,512]{2,1,0:T(8,128)S(1)} %get-tuple-element.22), channel_id=1, source_target_pairs={{0,8},{1,11},{2,10},{3,9},{4,12},{5,15},{6,14},{7,13},{8,0},{9,3},... | collective-permute-start | bytes 196616 | tf_op jit(solution)/shard_map/ppermute | solution.py:289
  22.7 6.8 %collective-permute-start.11 = (f32[4,8,512]{2,1,0:T(8,128)S(1)}, f32[4,8,512]{2,1,0:T(8,128)S(1)}, u32[]{:S(2)}, u32[]{:S(2)}) collective-permute-start(f32[4,8,512]{2,1,0:T(8,128)S(1)} %get-tuple-element.23), channel_id=1, source_target_pairs={{0,12},{1,15},{2,14},{3,13},{4,8},{5,11},{6,10},{7,9},{8,4},{9,7},... | collective-permute-start | bytes 196616 | tf_op jit(solution)/shard_map/ppermute | solution.py:289
  23.7 6.2 %collective-permute-start.12 = (f32[4,8,512]{2,1,0:T(8,128)S(1)}, f32[4,8,512]{2,1,0:T(8,128)S(1)}, u32[]{:S(2)}, u32[]{:S(2)}) collective-permute-start(f32[4,8,512]{2,1,0:T(8,128)S(1)} %get-tuple-element.24), channel_id=1, source_target_pairs={{0,4},{1,7},{2,6},{3,5},{4,0},{5,3},{6,2},{7,1},{8,12},{9,15},{10,... | collective-permute-start | bytes 196616 | tf_op jit(solution)/shard_map/ppermute | solution.py:289
  23.7 6.4 %collective-permute-start.13 = (f32[4,8,512]{2,1,0:T(8,128)S(1)}, f32[4,8,512]{2,1,0:T(8,128)S(1)}, u32[]{:S(2)}, u32[]{:S(2)}) collective-permute-start(f32[4,8,512]{2,1,0:T(8,128)S(1)} %get-tuple-element.25), channel_id=1, source_target_pairs={{0,0},{1,3},{2,2},{3,1},{4,4},{5,7},{6,6},{7,5},{8,8},{9,11},{10,1... | collective-permute-start | bytes 196616 | tf_op jit(solution)/shard_map/ppermute | solution.py:289
  26.9 3.5 %collective-permute-start.14 = (f32[4,8,512]{2,1,0:T(8,128)S(1)}, f32[4,8,512]{2,1,0:T(8,128)S(1)}, u32[]{:S(2)}, u32[]{:S(2)}) collective-permute-start(f32[4,8,512]{2,1,0:T(8,128)S(1)} %collective-permute-done.10.refs_0_), channel_id=1, source_target_pairs={{0,1},{1,0},{2,3},{3,2},{4,5},{5,4},{6,7},{7,6},{8,9},{9,8},{10,11... | collective-permute-start | bytes 196616 | tf_op jit(solution)/shard_map/ppermute | solution.py:278
  29.5 1.3 %collective-permute-start.15 = (f32[4,8,512]{2,1,0:T(8,128)S(1)}, f32[4,8,512]{2,1,0:T(8,128)S(1)}, u32[]{:S(2)}, u32[]{:S(2)}) collective-permute-start(f32[4,8,512]{2,1,0:T(8,128)S(1)} %collective-permute-done.11.refs_1_), channel_id=1, source_target_pairs={{0,1},{1,0},{2,3},{3,2},{4,5},{5,4},{6,7},{7,6},{8,9},{9,8},{10,11... | collective-permute-start | bytes 196616 | tf_op jit(solution)/shard_map/ppermute | solution.py:278
  29.9 1.3 %collective-permute-start.16 = (f32[4,8,512]{2,1,0:T(8,128)S(1)}, f32[4,8,512]{2,1,0:T(8,128)S(1)}, u32[]{:S(2)}, u32[]{:S(2)}) collective-permute-start(f32[4,8,512]{2,1,0:T(8,128)S(1)} %collective-permute-done.12.refs_2_), channel_id=1, source_target_pairs={{0,1},{1,0},{2,3},{3,2},{4,5},{5,4},{6,7},{7,6},{8,9},{9,8},{10,11... | collective-permute-start | bytes 196616 | tf_op jit(solution)/shard_map/ppermute | solution.py:278
  30.1 1.3 %collective-permute-start.17 = (f32[4,8,512]{2,1,0:T(8,128)S(1)}, f32[4,8,512]{2,1,0:T(8,128)S(1)}, u32[]{:S(2)}, u32[]{:S(2)}) collective-permute-start(f32[4,8,512]{2,1,0:T(8,128)S(1)} %collective-permute-done.13.refs_3_), channel_id=1, source_target_pairs={{0,1},{1,0},{2,3},{3,2},{4,5},{5,4},{6,7},{7,6},{8,9},{9,8},{10,11... | collective-permute-start | bytes 196616 | tf_op jit(solution)/shard_map/ppermute | solution.py:278
  (3 other events, 32.5 us)

commit v14 on v13

--- a/solution.py
+++ b/solution.py
@@ -294,6 +294,15 @@
     return pl.pallas_call(kernel, out_shape=out_shape, compiler_params=SMALL, name=name)
 
 
+def second_kernel(block_ref, out_ref):
+    out_ref[...] = block_ref[1]
+
+
+def second_half(block):
+    shape = jax.ShapeDtypeStruct(block.shape[1:], block.dtype)
+    return small_call(second_kernel, shape, "second_half")(block)
+
+
 def add_kernel(keep_ref, arrived_ref, *out_refs):
     for turn, out_ref in enumerate(out_refs):
         out_ref[...] = keep_ref[turn] + arrived_ref[turn]
@@ -342,7 +351,7 @@
     column = x ^ y
     for index, turn in enumerate(turns(layers)):
         order_ref[(z ^ turn) * 2 + column] = block_refs[index][0]
-        order_ref[(z ^ turn) * 2 + (column ^ 1)] = arrived_refs[index][1]
+        order_ref[(z ^ turn) * 2 + (column ^ 1)] = arrived_refs[index][...]
     feat_count = order_ref.shape[-1]
     count = weight_ref.shape[1]
     channels = weight_ref.shape[2]
@@ -406,17 +415,27 @@
     )(*blocks, *arrived, weights, *split_table(forward_table), *inverse_tables)
 
 
-def keep_kernel(modes_ref, inverse_high, inverse_low, keep_ref, order_ref):
+def keep_kernel(modes_ref, inverse_high, inverse_low, mixed_ref, keep_ref, order_ref):
     z, x, y = quad()
+    count = mixed_ref.shape[1]
+    feat_count = modes_ref.shape[1]
+    for part in range(2):
+        mixed_ref[0, :, part * feat_count : (part + 1) * feat_count] = modes_ref[
+            part * count : (part + 1) * count
+        ]
     back = back_rows(inverse_high, inverse_low, x ^ y, modes_ref[...])
     order_ref[...] = back.reshape(keep_ref.shape)
     store_turns(keep_ref, order_ref, z)
 
 
 def keep_rows(modes, inverse_tables, like):
+    rows, feat_count = modes.shape
     return pl.pallas_call(
         keep_kernel,
-        out_shape=jax.ShapeDtypeStruct(like.shape, jnp.float32),
+        out_shape=[
+            jax.ShapeDtypeStruct((1, rows // 2, 2 * feat_count), jnp.float32),
+            jax.ShapeDtypeStruct(like.shape, jnp.float32),
+        ],
         scratch_shapes=[pltpu.VMEM(like.shape, jnp.float32)],
         compiler_params=SMALL,
         name="keep_rows",
@@ -432,22 +451,11 @@
     return half + half * jnp.tanh(values * inner)
 
 
-def output_kernel(layers, flow_ref, table_ref, local_ref, bias_ref, modes_ref, *refs):
+def output_kernel(layers, flow_ref, table_ref, local_ref, bias_ref, *refs):
     own_refs, core_refs = refs[:layers], refs[layers : 2 * layers]
-    out_hbm, mixed_hbm, order_ref, wide_ref, level_ref, done_ref, sent = refs[2 * layers :]
+    out_hbm, order_ref, wide_ref, level_ref, done_ref, sent = refs[2 * layers :]
     cells_x, _, feat_count = flow_ref.shape
     channels = local_ref.shape[0]
-    count = modes_ref.shape[0] // 2
-    copies = []
-    for part in range(2):
-        copies.append(
-            pltpu.make_async_copy(
-                modes_ref.at[pl.ds(part * count, count)],
-                mixed_hbm.at[0, :, pl.ds(part * feat_count, feat_count)],
-                sent.at[cells_x + part],
-            )
-        )
-        copies[-1].start()
     z, x, y = quad()
     wide_ref[...] = jnp.zeros_like(wide_ref)
     for start in range(0, WIDTH, channels):
@@ -467,6 +475,7 @@
         for turn, block_ref in zip(turns(layers), block_refs):
             order_ref[:, (z ^ turn) * 2 + column] = block_ref[...]
     table = table_ref[y, x ^ y]
+    copies = []
     for cell in range(cells_x):
         high, low = split_terms(order_ref[cell].reshape(-1, feat_count))
         stack = jnp.concatenate([high, low, high], axis=0)
@@ -483,27 +492,23 @@
         copy.wait()
 
 
-def make_output(flow_field, parts, table, local, bias, modes):
+def make_output(flow_field, parts, table, local, bias):
     cells_x, _, feat_count = flow_field.shape
     layers = len(parts) // 2
-    rows, _ = modes.shape
     return pl.pallas_call(
         functools.partial(output_kernel, layers),
-        out_specs=[pl.BlockSpec(memory_space=pl.ANY)] * 2,
+        out_specs=pl.BlockSpec(memory_space=pl.ANY),
         scratch_shapes=[
             pltpu.VMEM((cells_x, 2 * layers) + parts[0].shape[1:], jnp.float32),
             pltpu.VMEM((WIDTH, WIDTH), jnp.bfloat16),
             pltpu.VMEM((1, WIDTH), jnp.float32),
             pltpu.VMEM(flow_field.shape, jnp.bfloat16),
-            pltpu.SemaphoreType.DMA((cells_x + 2,)),
+            pltpu.SemaphoreType.DMA((cells_x,)),
         ],
-        out_shape=[
-            jax.ShapeDtypeStruct(flow_field.shape, jnp.bfloat16),
-            jax.ShapeDtypeStruct((1, rows // 2, 2 * feat_count), jnp.float32),
-        ],
+        out_shape=jax.ShapeDtypeStruct(flow_field.shape, jnp.bfloat16),
         compiler_params=SMALL,
         name="make_output",
-    )(flow_field, table, local, bias, modes, *parts)
+    )(flow_field, table, local, bias, *parts)
 
 
 def row_body(flow_field, spectral_weight, local_weight, bias_terms):
@@ -519,17 +524,17 @@
     inverse_tables = split_table(inverse_x_table(cells_x, peers, rows_ky))
     modes, send = mix(
         blocks,
-        [flip_core(block) for block in blocks],
+        [flip_core(second_half(block)) for block in blocks],
         spectral_weight,
         forward_x_table(cells_x, peers, rows_ky) * forward_scale,
         inverse_tables,
     )
     arrived = flip_core(send)
-    keep = keep_rows(modes, inverse_tables, send)
+    mixed, keep = keep_rows(modes, inverse_tables, send)
     own = along_columns(join_blocks(keep, arrived, cells_x), peers)
     parts = own + [flip_core(block) for block in own]
     table = output_table(inverse_y_table(cells_y, groups_y, peers, rows_ky) * inverse_scale)
-    return tuple(make_output(flow_field, parts, table, local_weight, bias_terms, modes))
+    return make_output(flow_field, parts, table, local_weight, bias_terms), mixed
 
 
 def body(flow_field, spectral_weight, local_weight, bias_terms):

time: 34.1 us -> 34.2 us (level)
  Pallas kernels: 5.65 us -> 6.22 us
    ppermute x10, waiting for transfers between devices: 3.92 us -> 3.32 us  [flip_core(): return lax.ppermute(block, 'gy', [(0, 1), (1, 0)])]
    pallas_call x2 -> x6, Pallas kernels: 2.78 us -> 3.34 us  [the longest x1 2.54 us: make_output(): pl.pallas_call(functools.partial(output_kernel, layers), out_specs=pl.Blo...]
    ppermute x8, waiting for transfers between devices: 6.79 us -> 7.22 us  [along_columns(): arrived.append(lax.ppermute(block, ('gx', 'gy'), pairs))]
  transfers between devices with their start and end apart: 18 -> 18, of which waited for: 13 -> 13; matrix products, arithmetic and copies ran while one was open for 0% -> 0% of each run, Pallas kernels for 1% -> 2%
where the time goes in v14:
time: 34.2 us; the launch traced here: 34 us
  starting transfers between devices  16.5 us (48%)
  waiting for transfers between devices  10.5 us (31%)
  Pallas kernels  6.22 us (18%)
  between operations  0.76 us (2%)
    ppermute x8, starting transfers between devices, along_columns(): arrived.append(lax.ppermute(block, ('gx', 'gy'), pairs))  11 us
    ppermute x8, waiting for transfers between devices, along_columns(): arrived.append(lax.ppermute(block, ('gx', 'gy'), pairs))  7.22 us
    ppermute x10, starting transfers between devices, flip_core(): return lax.ppermute(block, 'gy', [(0, 1), (1, 0)])  5.42 us
    ppermute x10, waiting for transfers between devices, flip_core(): return lax.ppermute(block, 'gy', [(0, 1), (1, 0)])  3.32 us
    pallas_call x1, Pallas kernels, make_output(): pl.pallas_call(functools.partial(output_kernel, layers), out_specs=pl.Blo...  2.54 us
    pallas_call x1, Pallas kernels, forward_y(): pl.pallas_call(functools.partial(forward_y_kernel, extent, rows_ky), in_s...  1.75 us
    pallas_call x1, Pallas kernels, mix(): pl.pallas_call(functools.partial(mix_kernel, layers), out_shape=[jax.Shap...  1.05 us
    pallas_call x1, Pallas kernels, keep_rows(): pl.pallas_call(keep_kernel, out_shape=[jax.ShapeDtypeStruct((1, rows // 2...  0.79 us
  transfers between devices with their start and end apart: 18, of which 13 were waited for; matrix products, arithmetic and copies ran while one was open for 0% of the time, Pallas kernels for 2%

profile of v14, /device:TPU:0, one launch (start us, length us, event | category | flops | bytes accessed | tf_op | source)
XLA Modules:
  0.0 34.0 jit_solution(1453543848534945817)
XLA Ops:
  0.6 1.7 %forward_y.1 = (f32[4,2,16,512]{3,2,1,0:T(8,128)S(1)}, f32[4,2,16,512]{3,2,1,0:T(8,128)S(1)}) custom-call(bf16[4,256,512]{2,1,0:T(8,128)(2,1)} %flow_ref.1), custom_call_target="tpu_custom_call" | custom-call | tf_op jit(solution)/shard_map/forward_y/pallas_call | solution.py:264
  2.4 0.5 %collective-permute-start = (f32[4,2,16,512]{3,2,1,0:T(8,128)S(1)}, f32[4,2,16,512]{3,2,1,0:T(8,128)S(1)}, u32[]{:S(2)}, u32[]{:S(2)}) collective-permute-start(f32[4,2,16,512]{3,2,1,0:T(8,128)S(1)} %get-tuple-element.17), channel_id=1, source_target_pairs={{0,1},{1,0},{2,3},{3,2},{4,5},{5,4},{6,7},{7,6},{8,9},{9,8},{10,11... | collective-permute-start | bytes 786440 | tf_op jit(solution)/shard_map/ppermute | solution.py:278
  2.9 1.2 %collective-permute-done.arrived_ref = f32[4,2,16,512]{3,2,1,0:T(8,128)S(1)} collective-permute-done((f32[4,2,16,512]{3,2,1,0:T(8,128)S(1)}, f32[4,2,16,512]{3,2,1,0:T(8,128)S(1)}, u32[]{:S(2)}, u32[]{:S(2)}) %collective-permute-start) | collective-permute-done | bytes 262176 | tf_op jit(solution)/shard_map/ppermute | solution.py:278
  4.1 4.0 %collective-permute-start.1 = (f32[2,16,512]{2,1,0:T(8,128)S(1)}, f32[2,16,512]{2,1,0:T(8,128)S(1)}, u32[]{:S(2)}, u32[]{:S(2)}) collective-permute-start(f32[2,16,512]{2,1,0:T(8,128)S(1)} %get-tuple-element.18), channel_id=1, source_target_pairs={{0,8},{1,11},{2,10},{3,9},{4,12},{5,15},{6,14},{7,13},{8,0},{9,3},... | collective-permute-start | bytes 196616 | tf_op jit(solution)/shard_map/ppermute | solution.py:289
  8.1 1.3 %collective-permute-start.2 = (f32[2,16,512]{2,1,0:T(8,128)S(1)}, f32[2,16,512]{2,1,0:T(8,128)S(1)}, u32[]{:S(2)}, u32[]{:S(2)}) collective-permute-start(f32[2,16,512]{2,1,0:T(8,128)S(1)} %get-tuple-element.19), channel_id=1, source_target_pairs={{0,12},{1,15},{2,14},{3,13},{4,8},{5,11},{6,10},{7,9},{8,4},{9,7},... | collective-permute-start | bytes 196616 | tf_op jit(solution)/shard_map/ppermute | solution.py:289
  9.7 0.7 %collective-permute-start.4 = (f32[2,16,512]{2,1,0:T(8,128)S(1)}, f32[2,16,512]{2,1,0:T(8,128)S(1)}, u32[]{:S(2)}, u32[]{:S(2)}) collective-permute-start(f32[2,16,512]{2,1,0:T(8,128)S(1)} %get-tuple-element.21), channel_id=1, source_target_pairs={{0,0},{1,3},{2,2},{3,1},{4,4},{5,7},{6,6},{7,5},{8,8},{9,11},{10,1... | collective-permute-start | bytes 196616 | tf_op jit(solution)/shard_map/ppermute | solution.py:289
  10.4 0.4 %collective-permute-done.1.block_ref.refs_0_ = f32[2,16,512]{2,1,0:T(8,128)S(1)} collective-permute-done((f32[2,16,512]{2,1,0:T(8,128)S(1)}, f32[2,16,512]{2,1,0:T(8,128)S(1)}, u32[]{:S(2)}, u32[]{:S(2)}) %collective-permute-start.1) | collective-permute-done | bytes 65568 | tf_op jit(solution)/shard_map/ppermute | solution.py:289
  10.7 2.6 %collective-permute-start.5 = (f32[16,512]{1,0:T(8,128)S(1)}, f32[16,512]{1,0:T(8,128)S(1)}, u32[]{:S(2)}, u32[]{:S(2)}) collective-permute-start(f32[16,512]{1,0:T(8,128)S(1)} %second_half.4), channel_id=1, source_target_pairs={{0,1},{1,0},{2,3},{3,2},{4,5},{5,4},{6,7},{7,6},{8,9},{9,8},{10,11... | collective-permute-start | bytes 98312 | tf_op jit(solution)/shard_map/ppermute | solution.py:278
  13.4 1.4 %collective-permute-done.2.block_ref.refs_1_ = f32[2,16,512]{2,1,0:T(8,128)S(1)} collective-permute-done((f32[2,16,512]{2,1,0:T(8,128)S(1)}, f32[2,16,512]{2,1,0:T(8,128)S(1)}, u32[]{:S(2)}, u32[]{:S(2)}) %collective-permute-start.2) | collective-permute-done | bytes 65568 | tf_op jit(solution)/shard_map/ppermute | solution.py:289
  14.8 0.5 %collective-permute-start.6 = (f32[16,512]{1,0:T(8,128)S(1)}, f32[16,512]{1,0:T(8,128)S(1)}, u32[]{:S(2)}, u32[]{:S(2)}) collective-permute-start(f32[16,512]{1,0:T(8,128)S(1)} %second_half.5), channel_id=1, source_target_pairs={{0,1},{1,0},{2,3},{3,2},{4,5},{5,4},{6,7},{7,6},{8,9},{9,8},{10,11... | collective-permute-start | bytes 98312 | tf_op jit(solution)/shard_map/ppermute | solution.py:278
  15.8 0.4 %collective-permute-start.8 = (f32[16,512]{1,0:T(8,128)S(1)}, f32[16,512]{1,0:T(8,128)S(1)}, u32[]{:S(2)}, u32[]{:S(2)}) collective-permute-start(f32[16,512]{1,0:T(8,128)S(1)} %second_half.7), channel_id=1, source_target_pairs={{0,1},{1,0},{2,3},{3,2},{4,5},{5,4},{6,7},{7,6},{8,9},{9,8},{10,11... | collective-permute-start | bytes 98312 | tf_op jit(solution)/shard_map/ppermute | solution.py:278
  16.2 0.6 %collective-permute-done.7.refs_6_ = f32[16,512]{1,0:T(8,128)S(1)} collective-permute-done((f32[16,512]{1,0:T(8,128)S(1)}, f32[16,512]{1,0:T(8,128)S(1)}, u32[]{:S(2)}, u32[]{:S(2)}) %collective-permute-start.7) | collective-permute-done | bytes 32800 | tf_op jit(solution)/shard_map/ppermute | solution.py:278
  17.2 1.1 %mix.1 = (f32[128,512]{1,0:T(8,128)S(1)}, f32[4,16,512]{2,1,0:T(8,128)S(1)}) custom-call(f32[2,16,512]{2,1,0:T(8,128)S(1)} %collective-permute-done.1.block_ref.refs_0_, f32[2,16,512]{2,1,0:T(8,128)S(1)} %collective-permute-done.2.block_ref.refs_1_, f32[2,16,512]{2,1,0:T(8,128)S(1)} %collective-permute-done.3.block_ref.refs_2_, ...), custom_call_target="tpu_custom_call" | custom-call | tf_op jit(solution)/shard_map/mix/pallas_call | solution.py:406
  18.2 0.4 %collective-permute-start.9 = (f32[4,16,512]{2,1,0:T(8,128)S(1)}, f32[4,16,512]{2,1,0:T(8,128)S(1)}, u32[]{:S(2)}, u32[]{:S(2)}) collective-permute-start(f32[4,16,512]{2,1,0:T(8,128)S(1)} %get-tuple-element.24), channel_id=1, source_target_pairs={{0,1},{1,0},{2,3},{3,2},{4,5},{5,4},{6,7},{7,6},{8,9},{9,8},{10,11... | collective-permute-start | bytes 393224 | tf_op jit(solution)/shard_map/ppermute | solution.py:278
  18.6 0.8 %keep_rows.1 = (f32[1,64,1024]{2,1,0:T(8,128)}, f32[4,16,512]{2,1,0:T(8,128)S(1)}) custom-call(f32[128,512]{1,0:T(8,128)S(1)} %get-tuple-element.22.modes_ref, bf16[2,64,128]{2,1,0:T(8,128)(2,1)S(1)} %copy-done.4, bf16[2,64,128]{2,1,0:T(8,128)(2,1)S(1)} %copy-done.3), custom_call_target="tpu_custom_call" | custom-call | tf_op jit(solution)/shard_map/keep_rows/pallas_call | solution.py:433
  19.7 3.1 %collective-permute-start.10 = (f32[4,8,512]{2,1,0:T(8,128)S(1)}, f32[4,8,512]{2,1,0:T(8,128)S(1)}, u32[]{:S(2)}, u32[]{:S(2)}) collective-permute-start(f32[4,8,512]{2,1,0:T(8,128)S(1)} %get-tuple-element.25), channel_id=1, source_target_pairs={{0,8},{1,11},{2,10},{3,9},{4,12},{5,15},{6,14},{7,13},{8,0},{9,3},... | collective-permute-start | bytes 196616 | tf_op jit(solution)/shard_map/ppermute | solution.py:289
  22.8 0.7 %collective-permute-start.11 = (f32[4,8,512]{2,1,0:T(8,128)S(1)}, f32[4,8,512]{2,1,0:T(8,128)S(1)}, u32[]{:S(2)}, u32[]{:S(2)}) collective-permute-start(f32[4,8,512]{2,1,0:T(8,128)S(1)} %get-tuple-element.26), channel_id=1, source_target_pairs={{0,12},{1,15},{2,14},{3,13},{4,8},{5,11},{6,10},{7,9},{8,4},{9,7},... | collective-permute-start | bytes 196616 | tf_op jit(solution)/shard_map/ppermute | solution.py:289
  23.5 0.3 collective-permute-start.12
  23.8 0.7 %collective-permute-start.13 = (f32[4,8,512]{2,1,0:T(8,128)S(1)}, f32[4,8,512]{2,1,0:T(8,128)S(1)}, u32[]{:S(2)}, u32[]{:S(2)}) collective-permute-start(f32[4,8,512]{2,1,0:T(8,128)S(1)} %get-tuple-element.28), channel_id=1, source_target_pairs={{0,0},{1,3},{2,2},{3,1},{4,4},{5,7},{6,6},{7,5},{8,8},{9,11},{10,1... | collective-permute-start | bytes 196616 | tf_op jit(solution)/shard_map/ppermute | solution.py:289
  24.5 2.7 %collective-permute-done.10.refs_0_ = f32[4,8,512]{2,1,0:T(8,128)S(1)} collective-permute-done((f32[4,8,512]{2,1,0:T(8,128)S(1)}, f32[4,8,512]{2,1,0:T(8,128)S(1)}, u32[]{:S(2)}, u32[]{:S(2)}) %collective-permute-start.10) | collective-permute-done | bytes 65568 | tf_op jit(solution)/shard_map/ppermute | solution.py:289
  27.2 2.4 %collective-permute-done.11.refs_1_ = f32[4,8,512]{2,1,0:T(8,128)S(1)} collective-permute-done((f32[4,8,512]{2,1,0:T(8,128)S(1)}, f32[4,8,512]{2,1,0:T(8,128)S(1)}, u32[]{:S(2)}, u32[]{:S(2)}) %collective-permute-start.11) | collective-permute-done | bytes 65568 | tf_op jit(solution)/shard_map/ppermute | solution.py:289
  30.5 0.4 %collective-permute-done.15.refs_5_ = f32[4,8,512]{2,1,0:T(8,128)S(1)} collective-permute-done((f32[4,8,512]{2,1,0:T(8,128)S(1)}, f32[4,8,512]{2,1,0:T(8,128)S(1)}, u32[]{:S(2)}, u32[]{:S(2)}) %collective-permute-start.15) | collective-permute-done | bytes 65568 | tf_op jit(solution)/shard_map/ppermute | solution.py:278
  30.9 0.4 %collective-permute-done.16.refs_6_ = f32[4,8,512]{2,1,0:T(8,128)S(1)} collective-permute-done((f32[4,8,512]{2,1,0:T(8,128)S(1)}, f32[4,8,512]{2,1,0:T(8,128)S(1)}, u32[]{:S(2)}, u32[]{:S(2)}) %collective-permute-start.16) | collective-permute-done | bytes 65568 | tf_op jit(solution)/shard_map/ppermute | solution.py:278
  31.5 2.5 %make_output.1 = bf16[4,256,512]{2,1,0:T(8,128)(2,1)} custom-call(bf16[4,256,512]{2,1,0:T(8,128)(2,1)S(1)} %copy-done, bf16[2,2,256,256]{3,2,1,0:T(8,128)(2,1)S(1)} %copy-done.2, bf16[64,64]{1,0:T(8,128)(2,1)S(1)} %copy-done.7, f32[64]{0:T(128)S(1)} %copy-done.8, f32[4,8,512]{2,1,0:T(8,128)S(1)} %collective-permute-done.10.refs_0_, ...), custom_call_target="tpu_custom_call" | custom-call | tf_op jit(solution)/shard_map/make_output/pallas_call | solution.py:498
  (40 shorter events, 2.5 us)
Async XLA Ops:
  0.6 16.5 %copy-start.1 = (bf16[1,64,64,128]{3,2,1,0:T(8,128)(2,1)S(1)}, bf16[1,64,64,128]{3,2,1,0:T(8,128)(2,1)}, u32[]{:S(2)}) copy-start(bf16[1,64,64,128]{3,2,1,0:T(8,128)(2,1)} %refs_8_.1) | copy-start | bytes 3145732
  2.4 1.7 %collective-permute-start = (f32[4,2,16,512]{3,2,1,0:T(8,128)S(1)}, f32[4,2,16,512]{3,2,1,0:T(8,128)S(1)}, u32[]{:S(2)}, u32[]{:S(2)}) collective-permute-start(f32[4,2,16,512]{3,2,1,0:T(8,128)S(1)} %get-tuple-element.17), channel_id=1, source_target_pairs={{0,1},{1,0},{2,3},{3,2},{4,5},{5,4},{6,7},{7,6},{8,9},{9,8},{10,11... | collective-permute-start | bytes 786440 | tf_op jit(solution)/shard_map/ppermute | solution.py:278
  4.1 6.6 %collective-permute-start.1 = (f32[2,16,512]{2,1,0:T(8,128)S(1)}, f32[2,16,512]{2,1,0:T(8,128)S(1)}, u32[]{:S(2)}, u32[]{:S(2)}) collective-permute-start(f32[2,16,512]{2,1,0:T(8,128)S(1)} %get-tuple-element.18), channel_id=1, source_target_pairs={{0,8},{1,11},{2,10},{3,9},{4,12},{5,15},{6,14},{7,13},{8,0},{9,3},... | collective-permute-start | bytes 196616 | tf_op jit(solution)/shard_map/ppermute | solution.py:289
  8.1 6.7 %collective-permute-start.2 = (f32[2,16,512]{2,1,0:T(8,128)S(1)}, f32[2,16,512]{2,1,0:T(8,128)S(1)}, u32[]{:S(2)}, u32[]{:S(2)}) collective-permute-start(f32[2,16,512]{2,1,0:T(8,128)S(1)} %get-tuple-element.19), channel_id=1, source_target_pairs={{0,12},{1,15},{2,14},{3,13},{4,8},{5,11},{6,10},{7,9},{8,4},{9,7},... | collective-permute-start | bytes 196616 | tf_op jit(solution)/shard_map/ppermute | solution.py:289
  9.5 6.0 %collective-permute-start.3 = (f32[2,16,512]{2,1,0:T(8,128)S(1)}, f32[2,16,512]{2,1,0:T(8,128)S(1)}, u32[]{:S(2)}, u32[]{:S(2)}) collective-permute-start(f32[2,16,512]{2,1,0:T(8,128)S(1)} %get-tuple-element.20), channel_id=1, source_target_pairs={{0,4},{1,7},{2,6},{3,5},{4,0},{5,3},{6,2},{7,1},{8,12},{9,15},{10,... | collective-permute-start | bytes 196616 | tf_op jit(solution)/shard_map/ppermute | solution.py:289
  9.7 6.1 %collective-permute-start.4 = (f32[2,16,512]{2,1,0:T(8,128)S(1)}, f32[2,16,512]{2,1,0:T(8,128)S(1)}, u32[]{:S(2)}, u32[]{:S(2)}) collective-permute-start(f32[2,16,512]{2,1,0:T(8,128)S(1)} %get-tuple-element.21), channel_id=1, source_target_pairs={{0,0},{1,3},{2,2},{3,1},{4,4},{5,7},{6,6},{7,5},{8,8},{9,11},{10,1... | collective-permute-start | bytes 196616 | tf_op jit(solution)/shard_map/ppermute | solution.py:289
  10.7 5.5 %collective-permute-start.5 = (f32[16,512]{1,0:T(8,128)S(1)}, f32[16,512]{1,0:T(8,128)S(1)}, u32[]{:S(2)}, u32[]{:S(2)}) collective-permute-start(f32[16,512]{1,0:T(8,128)S(1)} %second_half.4), channel_id=1, source_target_pairs={{0,1},{1,0},{2,3},{3,2},{4,5},{5,4},{6,7},{7,6},{8,9},{9,8},{10,11... | collective-permute-start | bytes 98312 | tf_op jit(solution)/shard_map/ppermute | solution.py:278
  14.8 1.4 %collective-permute-start.6 = (f32[16,512]{1,0:T(8,128)S(1)}, f32[16,512]{1,0:T(8,128)S(1)}, u32[]{:S(2)}, u32[]{:S(2)}) collective-permute-start(f32[16,512]{1,0:T(8,128)S(1)} %second_half.5), channel_id=1, source_target_pairs={{0,1},{1,0},{2,3},{3,2},{4,5},{5,4},{6,7},{7,6},{8,9},{9,8},{10,11... | collective-permute-start | bytes 98312 | tf_op jit(solution)/shard_map/ppermute | solution.py:278
  15.5 1.6 %copy-start.6 = (bf16[128,128]{1,0:T(8,128)(2,1)S(1)}, bf16[128,128]{1,0:T(8,128)(2,1)}, u32[]{:S(2)}) copy-start(bf16[128,128]{1,0:T(8,128)(2,1)} %constant.10.clone.refs_9_) | copy-start | bytes 98308
  15.6 1.3 %collective-permute-start.7 = (f32[16,512]{1,0:T(8,128)S(1)}, f32[16,512]{1,0:T(8,128)S(1)}, u32[]{:S(2)}, u32[]{:S(2)}) collective-permute-start(f32[16,512]{1,0:T(8,128)S(1)} %second_half.6), channel_id=1, source_target_pairs={{0,1},{1,0},{2,3},{3,2},{4,5},{5,4},{6,7},{7,6},{8,9},{9,8},{10,11... | collective-permute-start | bytes 98312 | tf_op jit(solution)/shard_map/ppermute | solution.py:278
  15.8 15.6 %copy-start = (bf16[4,256,512]{2,1,0:T(8,128)(2,1)S(1)}, bf16[4,256,512]{2,1,0:T(8,128)(2,1)}, u32[]{:S(2)}) copy-start(bf16[4,256,512]{2,1,0:T(8,128)(2,1)} %flow_ref.1) | copy-start | bytes 3145732
  15.8 1.3 %collective-permute-start.8 = (f32[16,512]{1,0:T(8,128)S(1)}, f32[16,512]{1,0:T(8,128)S(1)}, u32[]{:S(2)}, u32[]{:S(2)}) collective-permute-start(f32[16,512]{1,0:T(8,128)S(1)} %second_half.7), channel_id=1, source_target_pairs={{0,1},{1,0},{2,3},{3,2},{4,5},{5,4},{6,7},{7,6},{8,9},{9,8},{10,11... | collective-permute-start | bytes 98312 | tf_op jit(solution)/shard_map/ppermute | solution.py:278
  18.2 13.2 %copy-start.2 = (bf16[2,2,256,256]{3,2,1,0:T(8,128)(2,1)S(1)}, bf16[2,2,256,256]{3,2,1,0:T(8,128)(2,1)}, u32[]{:S(2)}) copy-start(bf16[2,2,256,256]{3,2,1,0:T(8,128)(2,1)} %constant.14.clone.table_ref) | copy-start | bytes 1572868
  18.2 1.4 %collective-permute-start.9 = (f32[4,16,512]{2,1,0:T(8,128)S(1)}, f32[4,16,512]{2,1,0:T(8,128)S(1)}, u32[]{:S(2)}, u32[]{:S(2)}) collective-permute-start(f32[4,16,512]{2,1,0:T(8,128)S(1)} %get-tuple-element.24), channel_id=1, source_target_pairs={{0,1},{1,0},{2,3},{3,2},{4,5},{5,4},{6,7},{7,6},{8,9},{9,8},{10,11... | collective-permute-start | bytes 393224 | tf_op jit(solution)/shard_map/ppermute | solution.py:278
  19.6 11.8 %copy-start.7 = (bf16[64,64]{1,0:T(8,128)(2,1)S(1)}, bf16[64,64]{1,0:T(8,128)(2,1)}, u32[]{:S(2)}) copy-start(bf16[64,64]{1,0:T(8,128)(2,1)} %local_ref.1) | copy-start | bytes 24580
  19.7 7.5 %collective-permute-start.10 = (f32[4,8,512]{2,1,0:T(8,128)S(1)}, f32[4,8,512]{2,1,0:T(8,128)S(1)}, u32[]{:S(2)}, u32[]{:S(2)}) collective-permute-start(f32[4,8,512]{2,1,0:T(8,128)S(1)} %get-tuple-element.25), channel_id=1, source_target_pairs={{0,8},{1,11},{2,10},{3,9},{4,12},{5,15},{6,14},{7,13},{8,0},{9,3},... | collective-permute-start | bytes 196616 | tf_op jit(solution)/shard_map/ppermute | solution.py:289
  22.8 6.8 %collective-permute-start.11 = (f32[4,8,512]{2,1,0:T(8,128)S(1)}, f32[4,8,512]{2,1,0:T(8,128)S(1)}, u32[]{:S(2)}, u32[]{:S(2)}) collective-permute-start(f32[4,8,512]{2,1,0:T(8,128)S(1)} %get-tuple-element.26), channel_id=1, source_target_pairs={{0,12},{1,15},{2,14},{3,13},{4,8},{5,11},{6,10},{7,9},{8,4},{9,7},... | collective-permute-start | bytes 196616 | tf_op jit(solution)/shard_map/ppermute | solution.py:289
  23.5 8.0 %copy-start.8 = (f32[64]{0:T(128)S(1)}, f32[64]{0:T(128)}, u32[]{:S(2)}) copy-start(f32[64]{0:T(128)} %bias_ref.1) | copy-start | bytes 772
  23.5 6.5 %collective-permute-start.12 = (f32[4,8,512]{2,1,0:T(8,128)S(1)}, f32[4,8,512]{2,1,0:T(8,128)S(1)}, u32[]{:S(2)}, u32[]{:S(2)}) collective-permute-start(f32[4,8,512]{2,1,0:T(8,128)S(1)} %get-tuple-element.27), channel_id=1, source_target_pairs={{0,4},{1,7},{2,6},{3,5},{4,0},{5,3},{6,2},{7,1},{8,12},{9,15},{10,... | collective-permute-start | bytes 196616 | tf_op jit(solution)/shard_map/ppermute | solution.py:289
  23.8 6.4 %collective-permute-start.13 = (f32[4,8,512]{2,1,0:T(8,128)S(1)}, f32[4,8,512]{2,1,0:T(8,128)S(1)}, u32[]{:S(2)}, u32[]{:S(2)}) collective-permute-start(f32[4,8,512]{2,1,0:T(8,128)S(1)} %get-tuple-element.28), channel_id=1, source_target_pairs={{0,0},{1,3},{2,2},{3,1},{4,4},{5,7},{6,6},{7,5},{8,8},{9,11},{10,1... | collective-permute-start | bytes 196616 | tf_op jit(solution)/shard_map/ppermute | solution.py:289
  27.2 3.3 %collective-permute-start.14 = (f32[4,8,512]{2,1,0:T(8,128)S(1)}, f32[4,8,512]{2,1,0:T(8,128)S(1)}, u32[]{:S(2)}, u32[]{:S(2)}) collective-permute-start(f32[4,8,512]{2,1,0:T(8,128)S(1)} %collective-permute-done.10.refs_0_), channel_id=1, source_target_pairs={{0,1},{1,0},{2,3},{3,2},{4,5},{5,4},{6,7},{7,6},{8,9},{9,8},{10,11... | collective-permute-start | bytes 196616 | tf_op jit(solution)/shard_map/ppermute | solution.py:278
  29.6 1.3 %collective-permute-start.15 = (f32[4,8,512]{2,1,0:T(8,128)S(1)}, f32[4,8,512]{2,1,0:T(8,128)S(1)}, u32[]{:S(2)}, u32[]{:S(2)}) collective-permute-start(f32[4,8,512]{2,1,0:T(8,128)S(1)} %collective-permute-done.11.refs_1_), channel_id=1, source_target_pairs={{0,1},{1,0},{2,3},{3,2},{4,5},{5,4},{6,7},{7,6},{8,9},{9,8},{10,11... | collective-permute-start | bytes 196616 | tf_op jit(solution)/shard_map/ppermute | solution.py:278
  30.0 1.3 %collective-permute-start.16 = (f32[4,8,512]{2,1,0:T(8,128)S(1)}, f32[4,8,512]{2,1,0:T(8,128)S(1)}, u32[]{:S(2)}, u32[]{:S(2)}) collective-permute-start(f32[4,8,512]{2,1,0:T(8,128)S(1)} %collective-permute-done.12.refs_2_), channel_id=1, source_target_pairs={{0,1},{1,0},{2,3},{3,2},{4,5},{5,4},{6,7},{7,6},{8,9},{9,8},{10,11... | collective-permute-start | bytes 196616 | tf_op jit(solution)/shard_map/ppermute | solution.py:278
  30.2 1.3 %collective-permute-start.17 = (f32[4,8,512]{2,1,0:T(8,128)S(1)}, f32[4,8,512]{2,1,0:T(8,128)S(1)}, u32[]{:S(2)}, u32[]{:S(2)}) collective-permute-start(f32[4,8,512]{2,1,0:T(8,128)S(1)} %collective-permute-done.13.refs_3_), channel_id=1, source_target_pairs={{0,1},{1,0},{2,3},{3,2},{4,5},{5,4},{6,7},{7,6},{8,9},{9,8},{10,11... | collective-permute-start | bytes 196616 | tf_op jit(solution)/shard_map/ppermute | solution.py:278
  (3 other events, 4.8 us)

commit v15 on v14

--- a/solution.py
+++ b/solution.py
@@ -130,6 +130,7 @@
 LARGE = pltpu.CompilerParams(vmem_limit_bytes=53 * 1024 * 1024)
 WIDTH = 256
 BIAS_TERMS = 3
+SLAB = 32
 GELU_TERMS = (
     0.7978849411010742,
     0.03633308410644531,
@@ -453,8 +454,8 @@
 
 def output_kernel(layers, flow_ref, table_ref, local_ref, bias_ref, *refs):
     own_refs, core_refs = refs[:layers], refs[layers : 2 * layers]
-    out_hbm, order_ref, wide_ref, level_ref, done_ref, sent = refs[2 * layers :]
-    cells_x, _, feat_count = flow_ref.shape
+    out_hbm, order_ref, wide_ref, level_ref, total_ref, done_ref, sent = refs[2 * layers :]
+    cells_x, cells_y, feat_count = flow_ref.shape
     channels = local_ref.shape[0]
     z, x, y = quad()
     wide_ref[...] = jnp.zeros_like(wide_ref)
@@ -481,11 +482,13 @@
         stack = jnp.concatenate([high, low, high], axis=0)
         for start in range(0, feat_count, WIDTH):
             columns = slice(start, start + WIDTH)
-            total = dot(
+            total_ref[:, columns] = dot(
                 jnp.concatenate([table, flow_ref[cell, :, columns]], axis=1),
                 jnp.concatenate([stack[:, columns], below], axis=0),
             )
-            done_ref[cell, :, columns] = gelu(total).astype(done_ref.dtype)
+            for row in range(0, cells_y, SLAB):
+                slab = slice(row, row + SLAB)
+                done_ref[cell, slab, columns] = gelu(total_ref[slab, columns]).astype(done_ref.dtype)
         copies.append(pltpu.make_async_copy(done_ref.at[cell], out_hbm.at[cell], sent.at[cell]))
         copies[-1].start()
     for copy in copies:
@@ -502,6 +505,7 @@
             pltpu.VMEM((cells_x, 2 * layers) + parts[0].shape[1:], jnp.float32),
             pltpu.VMEM((WIDTH, WIDTH), jnp.bfloat16),
             pltpu.VMEM((1, WIDTH), jnp.float32),
+            pltpu.VMEM(flow_field.shape[1:], jnp.float32),
             pltpu.VMEM(flow_field.shape, jnp.bfloat16),
             pltpu.SemaphoreType.DMA((cells_x,)),
         ],

time: 34.2 us -> 34.2 us (level)
  no operation moved by 1% of the time
where the time goes in v15:
time: 34.2 us; the launch traced here: 34 us
  starting transfers between devices  16.5 us (48%)
  waiting for transfers between devices  10.5 us (31%)
  Pallas kernels  6.22 us (18%)
  between operations  0.76 us (2%)
    ppermute x8, starting transfers between devices, along_columns(): arrived.append(lax.ppermute(block, ('gx', 'gy'), pairs))  11 us
    ppermute x8, waiting for transfers between devices, along_columns(): arrived.append(lax.ppermute(block, ('gx', 'gy'), pairs))  7.22 us
    ppermute x10, starting transfers between devices, flip_core(): return lax.ppermute(block, 'gy', [(0, 1), (1, 0)])  5.42 us
    ppermute x10, waiting for transfers between devices, flip_core(): return lax.ppermute(block, 'gy', [(0, 1), (1, 0)])  3.32 us
    pallas_call x1, Pallas kernels, make_output(): pl.pallas_call(functools.partial(output_kernel, layers), out_specs=pl.Blo...  2.54 us
    pallas_call x1, Pallas kernels, forward_y(): pl.pallas_call(functools.partial(forward_y_kernel, extent, rows_ky), in_s...  1.75 us
    pallas_call x1, Pallas kernels, mix(): pl.pallas_call(functools.partial(mix_kernel, layers), out_shape=[jax.Shap...  1.05 us
    pallas_call x1, Pallas kernels, keep_rows(): pl.pallas_call(keep_kernel, out_shape=[jax.ShapeDtypeStruct((1, rows // 2...  0.79 us
  transfers between devices with their start and end apart: 18, of which 13 were waited for; matrix products, arithmetic and copies ran while one was open for 0% of the time, Pallas kernels for 2%

profile of v15, /device:TPU:0, one launch (start us, length us, event | category | flops | bytes accessed | tf_op | source)
XLA Modules:
  0.0 34.0 jit_solution(1453543848534945817)
XLA Ops:
  0.6 1.7 %forward_y.1 = (f32[4,2,16,512]{3,2,1,0:T(8,128)S(1)}, f32[4,2,16,512]{3,2,1,0:T(8,128)S(1)}) custom-call(bf16[4,256,512]{2,1,0:T(8,128)(2,1)} %flow_ref.1), custom_call_target="tpu_custom_call" | custom-call | tf_op jit(solution)/shard_map/forward_y/pallas_call | solution.py:265
  2.4 0.5 %collective-permute-start = (f32[4,2,16,512]{3,2,1,0:T(8,128)S(1)}, f32[4,2,16,512]{3,2,1,0:T(8,128)S(1)}, u32[]{:S(2)}, u32[]{:S(2)}) collective-permute-start(f32[4,2,16,512]{3,2,1,0:T(8,128)S(1)} %get-tuple-element.17), channel_id=1, source_target_pairs={{0,1},{1,0},{2,3},{3,2},{4,5},{5,4},{6,7},{7,6},{8,9},{9,8},{10,11... | collective-permute-start | bytes 786440 | tf_op jit(solution)/shard_map/ppermute | solution.py:279
  2.9 1.2 %collective-permute-done.arrived_ref = f32[4,2,16,512]{3,2,1,0:T(8,128)S(1)} collective-permute-done((f32[4,2,16,512]{3,2,1,0:T(8,128)S(1)}, f32[4,2,16,512]{3,2,1,0:T(8,128)S(1)}, u32[]{:S(2)}, u32[]{:S(2)}) %collective-permute-start) | collective-permute-done | bytes 262176 | tf_op jit(solution)/shard_map/ppermute | solution.py:279
  4.1 4.0 %collective-permute-start.1 = (f32[2,16,512]{2,1,0:T(8,128)S(1)}, f32[2,16,512]{2,1,0:T(8,128)S(1)}, u32[]{:S(2)}, u32[]{:S(2)}) collective-permute-start(f32[2,16,512]{2,1,0:T(8,128)S(1)} %get-tuple-element.18), channel_id=1, source_target_pairs={{0,8},{1,11},{2,10},{3,9},{4,12},{5,15},{6,14},{7,13},{8,0},{9,3},... | collective-permute-start | bytes 196616 | tf_op jit(solution)/shard_map/ppermute | solution.py:290
  8.1 1.3 %collective-permute-start.2 = (f32[2,16,512]{2,1,0:T(8,128)S(1)}, f32[2,16,512]{2,1,0:T(8,128)S(1)}, u32[]{:S(2)}, u32[]{:S(2)}) collective-permute-start(f32[2,16,512]{2,1,0:T(8,128)S(1)} %get-tuple-element.19), channel_id=1, source_target_pairs={{0,12},{1,15},{2,14},{3,13},{4,8},{5,11},{6,10},{7,9},{8,4},{9,7},... | collective-permute-start | bytes 196616 | tf_op jit(solution)/shard_map/ppermute | solution.py:290
  9.7 0.7 %collective-permute-start.4 = (f32[2,16,512]{2,1,0:T(8,128)S(1)}, f32[2,16,512]{2,1,0:T(8,128)S(1)}, u32[]{:S(2)}, u32[]{:S(2)}) collective-permute-start(f32[2,16,512]{2,1,0:T(8,128)S(1)} %get-tuple-element.21), channel_id=1, source_target_pairs={{0,0},{1,3},{2,2},{3,1},{4,4},{5,7},{6,6},{7,5},{8,8},{9,11},{10,1... | collective-permute-start | bytes 196616 | tf_op jit(solution)/shard_map/ppermute | solution.py:290
  10.4 0.4 %collective-permute-done.1.block_ref.refs_0_ = f32[2,16,512]{2,1,0:T(8,128)S(1)} collective-permute-done((f32[2,16,512]{2,1,0:T(8,128)S(1)}, f32[2,16,512]{2,1,0:T(8,128)S(1)}, u32[]{:S(2)}, u32[]{:S(2)}) %collective-permute-start.1) | collective-permute-done | bytes 65568 | tf_op jit(solution)/shard_map/ppermute | solution.py:290
  10.7 2.6 %collective-permute-start.5 = (f32[16,512]{1,0:T(8,128)S(1)}, f32[16,512]{1,0:T(8,128)S(1)}, u32[]{:S(2)}, u32[]{:S(2)}) collective-permute-start(f32[16,512]{1,0:T(8,128)S(1)} %second_half.4), channel_id=1, source_target_pairs={{0,1},{1,0},{2,3},{3,2},{4,5},{5,4},{6,7},{7,6},{8,9},{9,8},{10,11... | collective-permute-start | bytes 98312 | tf_op jit(solution)/shard_map/ppermute | solution.py:279
  13.4 1.4 %collective-permute-done.2.block_ref.refs_1_ = f32[2,16,512]{2,1,0:T(8,128)S(1)} collective-permute-done((f32[2,16,512]{2,1,0:T(8,128)S(1)}, f32[2,16,512]{2,1,0:T(8,128)S(1)}, u32[]{:S(2)}, u32[]{:S(2)}) %collective-permute-start.2) | collective-permute-done | bytes 65568 | tf_op jit(solution)/shard_map/ppermute | solution.py:290
  14.8 0.5 %collective-permute-start.6 = (f32[16,512]{1,0:T(8,128)S(1)}, f32[16,512]{1,0:T(8,128)S(1)}, u32[]{:S(2)}, u32[]{:S(2)}) collective-permute-start(f32[16,512]{1,0:T(8,128)S(1)} %second_half.5), channel_id=1, source_target_pairs={{0,1},{1,0},{2,3},{3,2},{4,5},{5,4},{6,7},{7,6},{8,9},{9,8},{10,11... | collective-permute-start | bytes 98312 | tf_op jit(solution)/shard_map/ppermute | solution.py:279
  15.8 0.4 %collective-permute-start.8 = (f32[16,512]{1,0:T(8,128)S(1)}, f32[16,512]{1,0:T(8,128)S(1)}, u32[]{:S(2)}, u32[]{:S(2)}) collective-permute-start(f32[16,512]{1,0:T(8,128)S(1)} %second_half.7), channel_id=1, source_target_pairs={{0,1},{1,0},{2,3},{3,2},{4,5},{5,4},{6,7},{7,6},{8,9},{9,8},{10,11... | collective-permute-start | bytes 98312 | tf_op jit(solution)/shard_map/ppermute | solution.py:279
  16.2 0.6 %collective-permute-done.7.refs_6_ = f32[16,512]{1,0:T(8,128)S(1)} collective-permute-done((f32[16,512]{1,0:T(8,128)S(1)}, f32[16,512]{1,0:T(8,128)S(1)}, u32[]{:S(2)}, u32[]{:S(2)}) %collective-permute-start.7) | collective-permute-done | bytes 32800 | tf_op jit(solution)/shard_map/ppermute | solution.py:279
  17.2 1.1 %mix.1 = (f32[128,512]{1,0:T(8,128)S(1)}, f32[4,16,512]{2,1,0:T(8,128)S(1)}) custom-call(f32[2,16,512]{2,1,0:T(8,128)S(1)} %collective-permute-done.1.block_ref.refs_0_, f32[2,16,512]{2,1,0:T(8,128)S(1)} %collective-permute-done.2.block_ref.refs_1_, f32[2,16,512]{2,1,0:T(8,128)S(1)} %collective-permute-done.3.block_ref.refs_2_, ...), custom_call_target="tpu_custom_call" | custom-call | tf_op jit(solution)/shard_map/mix/pallas_call | solution.py:407
  18.2 0.4 %collective-permute-start.9 = (f32[4,16,512]{2,1,0:T(8,128)S(1)}, f32[4,16,512]{2,1,0:T(8,128)S(1)}, u32[]{:S(2)}, u32[]{:S(2)}) collective-permute-start(f32[4,16,512]{2,1,0:T(8,128)S(1)} %get-tuple-element.24), channel_id=1, source_target_pairs={{0,1},{1,0},{2,3},{3,2},{4,5},{5,4},{6,7},{7,6},{8,9},{9,8},{10,11... | collective-permute-start | bytes 393224 | tf_op jit(solution)/shard_map/ppermute | solution.py:279
  18.6 0.8 %keep_rows.1 = (f32[1,64,1024]{2,1,0:T(8,128)}, f32[4,16,512]{2,1,0:T(8,128)S(1)}) custom-call(f32[128,512]{1,0:T(8,128)S(1)} %get-tuple-element.22.modes_ref, bf16[2,64,128]{2,1,0:T(8,128)(2,1)S(1)} %copy-done.4, bf16[2,64,128]{2,1,0:T(8,128)(2,1)S(1)} %copy-done.3), custom_call_target="tpu_custom_call" | custom-call | tf_op jit(solution)/shard_map/keep_rows/pallas_call | solution.py:434
  19.7 3.1 %collective-permute-start.10 = (f32[4,8,512]{2,1,0:T(8,128)S(1)}, f32[4,8,512]{2,1,0:T(8,128)S(1)}, u32[]{:S(2)}, u32[]{:S(2)}) collective-permute-start(f32[4,8,512]{2,1,0:T(8,128)S(1)} %get-tuple-element.25), channel_id=1, source_target_pairs={{0,8},{1,11},{2,10},{3,9},{4,12},{5,15},{6,14},{7,13},{8,0},{9,3},... | collective-permute-start | bytes 196616 | tf_op jit(solution)/shard_map/ppermute | solution.py:290
  22.8 0.7 %collective-permute-start.11 = (f32[4,8,512]{2,1,0:T(8,128)S(1)}, f32[4,8,512]{2,1,0:T(8,128)S(1)}, u32[]{:S(2)}, u32[]{:S(2)}) collective-permute-start(f32[4,8,512]{2,1,0:T(8,128)S(1)} %get-tuple-element.26), channel_id=1, source_target_pairs={{0,12},{1,15},{2,14},{3,13},{4,8},{5,11},{6,10},{7,9},{8,4},{9,7},... | collective-permute-start | bytes 196616 | tf_op jit(solution)/shard_map/ppermute | solution.py:290
  23.5 0.3 collective-permute-start.12
  23.8 0.7 %collective-permute-start.13 = (f32[4,8,512]{2,1,0:T(8,128)S(1)}, f32[4,8,512]{2,1,0:T(8,128)S(1)}, u32[]{:S(2)}, u32[]{:S(2)}) collective-permute-start(f32[4,8,512]{2,1,0:T(8,128)S(1)} %get-tuple-element.28), channel_id=1, source_target_pairs={{0,0},{1,3},{2,2},{3,1},{4,4},{5,7},{6,6},{7,5},{8,8},{9,11},{10,1... | collective-permute-start | bytes 196616 | tf_op jit(solution)/shard_map/ppermute | solution.py:290
  24.5 2.7 %collective-permute-done.10.refs_0_ = f32[4,8,512]{2,1,0:T(8,128)S(1)} collective-permute-done((f32[4,8,512]{2,1,0:T(8,128)S(1)}, f32[4,8,512]{2,1,0:T(8,128)S(1)}, u32[]{:S(2)}, u32[]{:S(2)}) %collective-permute-start.10) | collective-permute-done | bytes 65568 | tf_op jit(solution)/shard_map/ppermute | solution.py:290
  27.2 2.4 %collective-permute-done.11.refs_1_ = f32[4,8,512]{2,1,0:T(8,128)S(1)} collective-permute-done((f32[4,8,512]{2,1,0:T(8,128)S(1)}, f32[4,8,512]{2,1,0:T(8,128)S(1)}, u32[]{:S(2)}, u32[]{:S(2)}) %collective-permute-start.11) | collective-permute-done | bytes 65568 | tf_op jit(solution)/shard_map/ppermute | solution.py:290
  30.5 0.4 %collective-permute-done.15.refs_5_ = f32[4,8,512]{2,1,0:T(8,128)S(1)} collective-permute-done((f32[4,8,512]{2,1,0:T(8,128)S(1)}, f32[4,8,512]{2,1,0:T(8,128)S(1)}, u32[]{:S(2)}, u32[]{:S(2)}) %collective-permute-start.15) | collective-permute-done | bytes 65568 | tf_op jit(solution)/shard_map/ppermute | solution.py:279
  30.9 0.4 %collective-permute-done.16.refs_6_ = f32[4,8,512]{2,1,0:T(8,128)S(1)} collective-permute-done((f32[4,8,512]{2,1,0:T(8,128)S(1)}, f32[4,8,512]{2,1,0:T(8,128)S(1)}, u32[]{:S(2)}, u32[]{:S(2)}) %collective-permute-start.16) | collective-permute-done | bytes 65568 | tf_op jit(solution)/shard_map/ppermute | solution.py:279
  31.5 2.5 %make_output.1 = bf16[4,256,512]{2,1,0:T(8,128)(2,1)} custom-call(bf16[4,256,512]{2,1,0:T(8,128)(2,1)S(1)} %copy-done, bf16[2,2,256,256]{3,2,1,0:T(8,128)(2,1)S(1)} %copy-done.2, bf16[64,64]{1,0:T(8,128)(2,1)S(1)} %copy-done.7, f32[64]{0:T(128)S(1)} %copy-done.8, f32[4,8,512]{2,1,0:T(8,128)S(1)} %collective-permute-done.10.refs_0_, ...), custom_call_target="tpu_custom_call" | custom-call | tf_op jit(solution)/shard_map/make_output/pallas_call | solution.py:501
  (40 shorter events, 2.5 us)
Async XLA Ops:
  0.6 16.5 %copy-start.1 = (bf16[1,64,64,128]{3,2,1,0:T(8,128)(2,1)S(1)}, bf16[1,64,64,128]{3,2,1,0:T(8,128)(2,1)}, u32[]{:S(2)}) copy-start(bf16[1,64,64,128]{3,2,1,0:T(8,128)(2,1)} %refs_8_.1) | copy-start | bytes 3145732
  2.4 1.7 %collective-permute-start = (f32[4,2,16,512]{3,2,1,0:T(8,128)S(1)}, f32[4,2,16,512]{3,2,1,0:T(8,128)S(1)}, u32[]{:S(2)}, u32[]{:S(2)}) collective-permute-start(f32[4,2,16,512]{3,2,1,0:T(8,128)S(1)} %get-tuple-element.17), channel_id=1, source_target_pairs={{0,1},{1,0},{2,3},{3,2},{4,5},{5,4},{6,7},{7,6},{8,9},{9,8},{10,11... | collective-permute-start | bytes 786440 | tf_op jit(solution)/shard_map/ppermute | solution.py:279
  4.1 6.6 %collective-permute-start.1 = (f32[2,16,512]{2,1,0:T(8,128)S(1)}, f32[2,16,512]{2,1,0:T(8,128)S(1)}, u32[]{:S(2)}, u32[]{:S(2)}) collective-permute-start(f32[2,16,512]{2,1,0:T(8,128)S(1)} %get-tuple-element.18), channel_id=1, source_target_pairs={{0,8},{1,11},{2,10},{3,9},{4,12},{5,15},{6,14},{7,13},{8,0},{9,3},... | collective-permute-start | bytes 196616 | tf_op jit(solution)/shard_map/ppermute | solution.py:290
  8.1 6.7 %collective-permute-start.2 = (f32[2,16,512]{2,1,0:T(8,128)S(1)}, f32[2,16,512]{2,1,0:T(8,128)S(1)}, u32[]{:S(2)}, u32[]{:S(2)}) collective-permute-start(f32[2,16,512]{2,1,0:T(8,128)S(1)} %get-tuple-element.19), channel_id=1, source_target_pairs={{0,12},{1,15},{2,14},{3,13},{4,8},{5,11},{6,10},{7,9},{8,4},{9,7},... | collective-permute-start | bytes 196616 | tf_op jit(solution)/shard_map/ppermute | solution.py:290
  9.5 6.0 %collective-permute-start.3 = (f32[2,16,512]{2,1,0:T(8,128)S(1)}, f32[2,16,512]{2,1,0:T(8,128)S(1)}, u32[]{:S(2)}, u32[]{:S(2)}) collective-permute-start(f32[2,16,512]{2,1,0:T(8,128)S(1)} %get-tuple-element.20), channel_id=1, source_target_pairs={{0,4},{1,7},{2,6},{3,5},{4,0},{5,3},{6,2},{7,1},{8,12},{9,15},{10,... | collective-permute-start | bytes 196616 | tf_op jit(solution)/shard_map/ppermute | solution.py:290
  9.7 6.1 %collective-permute-start.4 = (f32[2,16,512]{2,1,0:T(8,128)S(1)}, f32[2,16,512]{2,1,0:T(8,128)S(1)}, u32[]{:S(2)}, u32[]{:S(2)}) collective-permute-start(f32[2,16,512]{2,1,0:T(8,128)S(1)} %get-tuple-element.21), channel_id=1, source_target_pairs={{0,0},{1,3},{2,2},{3,1},{4,4},{5,7},{6,6},{7,5},{8,8},{9,11},{10,1... | collective-permute-start | bytes 196616 | tf_op jit(solution)/shard_map/ppermute | solution.py:290
  10.7 5.5 %collective-permute-start.5 = (f32[16,512]{1,0:T(8,128)S(1)}, f32[16,512]{1,0:T(8,128)S(1)}, u32[]{:S(2)}, u32[]{:S(2)}) collective-permute-start(f32[16,512]{1,0:T(8,128)S(1)} %second_half.4), channel_id=1, source_target_pairs={{0,1},{1,0},{2,3},{3,2},{4,5},{5,4},{6,7},{7,6},{8,9},{9,8},{10,11... | collective-permute-start | bytes 98312 | tf_op jit(solution)/shard_map/ppermute | solution.py:279
  14.8 1.4 %collective-permute-start.6 = (f32[16,512]{1,0:T(8,128)S(1)}, f32[16,512]{1,0:T(8,128)S(1)}, u32[]{:S(2)}, u32[]{:S(2)}) collective-permute-start(f32[16,512]{1,0:T(8,128)S(1)} %second_half.5), channel_id=1, source_target_pairs={{0,1},{1,0},{2,3},{3,2},{4,5},{5,4},{6,7},{7,6},{8,9},{9,8},{10,11... | collective-permute-start | bytes 98312 | tf_op jit(solution)/shard_map/ppermute | solution.py:279
  15.5 1.6 %copy-start.6 = (bf16[128,128]{1,0:T(8,128)(2,1)S(1)}, bf16[128,128]{1,0:T(8,128)(2,1)}, u32[]{:S(2)}) copy-start(bf16[128,128]{1,0:T(8,128)(2,1)} %constant.10.clone.refs_9_) | copy-start | bytes 98308
  15.6 1.3 %collective-permute-start.7 = (f32[16,512]{1,0:T(8,128)S(1)}, f32[16,512]{1,0:T(8,128)S(1)}, u32[]{:S(2)}, u32[]{:S(2)}) collective-permute-start(f32[16,512]{1,0:T(8,128)S(1)} %second_half.6), channel_id=1, source_target_pairs={{0,1},{1,0},{2,3},{3,2},{4,5},{5,4},{6,7},{7,6},{8,9},{9,8},{10,11... | collective-permute-start | bytes 98312 | tf_op jit(solution)/shard_map/ppermute | solution.py:279
  15.8 15.6 %copy-start = (bf16[4,256,512]{2,1,0:T(8,128)(2,1)S(1)}, bf16[4,256,512]{2,1,0:T(8,128)(2,1)}, u32[]{:S(2)}) copy-start(bf16[4,256,512]{2,1,0:T(8,128)(2,1)} %flow_ref.1) | copy-start | bytes 3145732
  15.8 1.3 %collective-permute-start.8 = (f32[16,512]{1,0:T(8,128)S(1)}, f32[16,512]{1,0:T(8,128)S(1)}, u32[]{:S(2)}, u32[]{:S(2)}) collective-permute-start(f32[16,512]{1,0:T(8,128)S(1)} %second_half.7), channel_id=1, source_target_pairs={{0,1},{1,0},{2,3},{3,2},{4,5},{5,4},{6,7},{7,6},{8,9},{9,8},{10,11... | collective-permute-start | bytes 98312 | tf_op jit(solution)/shard_map/ppermute | solution.py:279
  18.2 13.2 %copy-start.2 = (bf16[2,2,256,256]{3,2,1,0:T(8,128)(2,1)S(1)}, bf16[2,2,256,256]{3,2,1,0:T(8,128)(2,1)}, u32[]{:S(2)}) copy-start(bf16[2,2,256,256]{3,2,1,0:T(8,128)(2,1)} %constant.14.clone.table_ref) | copy-start | bytes 1572868
  18.2 1.4 %collective-permute-start.9 = (f32[4,16,512]{2,1,0:T(8,128)S(1)}, f32[4,16,512]{2,1,0:T(8,128)S(1)}, u32[]{:S(2)}, u32[]{:S(2)}) collective-permute-start(f32[4,16,512]{2,1,0:T(8,128)S(1)} %get-tuple-element.24), channel_id=1, source_target_pairs={{0,1},{1,0},{2,3},{3,2},{4,5},{5,4},{6,7},{7,6},{8,9},{9,8},{10,11... | collective-permute-start | bytes 393224 | tf_op jit(solution)/shard_map/ppermute | solution.py:279
  19.6 11.8 %copy-start.7 = (bf16[64,64]{1,0:T(8,128)(2,1)S(1)}, bf16[64,64]{1,0:T(8,128)(2,1)}, u32[]{:S(2)}) copy-start(bf16[64,64]{1,0:T(8,128)(2,1)} %local_ref.1) | copy-start | bytes 24580
  19.7 7.5 %collective-permute-start.10 = (f32[4,8,512]{2,1,0:T(8,128)S(1)}, f32[4,8,512]{2,1,0:T(8,128)S(1)}, u32[]{:S(2)}, u32[]{:S(2)}) collective-permute-start(f32[4,8,512]{2,1,0:T(8,128)S(1)} %get-tuple-element.25), channel_id=1, source_target_pairs={{0,8},{1,11},{2,10},{3,9},{4,12},{5,15},{6,14},{7,13},{8,0},{9,3},... | collective-permute-start | bytes 196616 | tf_op jit(solution)/shard_map/ppermute | solution.py:290
  22.8 6.8 %collective-permute-start.11 = (f32[4,8,512]{2,1,0:T(8,128)S(1)}, f32[4,8,512]{2,1,0:T(8,128)S(1)}, u32[]{:S(2)}, u32[]{:S(2)}) collective-permute-start(f32[4,8,512]{2,1,0:T(8,128)S(1)} %get-tuple-element.26), channel_id=1, source_target_pairs={{0,12},{1,15},{2,14},{3,13},{4,8},{5,11},{6,10},{7,9},{8,4},{9,7},... | collective-permute-start | bytes 196616 | tf_op jit(solution)/shard_map/ppermute | solution.py:290
  23.5 8.0 %copy-start.8 = (f32[64]{0:T(128)S(1)}, f32[64]{0:T(128)}, u32[]{:S(2)}) copy-start(f32[64]{0:T(128)} %bias_ref.1) | copy-start | bytes 772
  23.5 6.5 %collective-permute-start.12 = (f32[4,8,512]{2,1,0:T(8,128)S(1)}, f32[4,8,512]{2,1,0:T(8,128)S(1)}, u32[]{:S(2)}, u32[]{:S(2)}) collective-permute-start(f32[4,8,512]{2,1,0:T(8,128)S(1)} %get-tuple-element.27), channel_id=1, source_target_pairs={{0,4},{1,7},{2,6},{3,5},{4,0},{5,3},{6,2},{7,1},{8,12},{9,15},{10,... | collective-permute-start | bytes 196616 | tf_op jit(solution)/shard_map/ppermute | solution.py:290
  23.8 6.4 %collective-permute-start.13 = (f32[4,8,512]{2,1,0:T(8,128)S(1)}, f32[4,8,512]{2,1,0:T(8,128)S(1)}, u32[]{:S(2)}, u32[]{:S(2)}) collective-permute-start(f32[4,8,512]{2,1,0:T(8,128)S(1)} %get-tuple-element.28), channel_id=1, source_target_pairs={{0,0},{1,3},{2,2},{3,1},{4,4},{5,7},{6,6},{7,5},{8,8},{9,11},{10,1... | collective-permute-start | bytes 196616 | tf_op jit(solution)/shard_map/ppermute | solution.py:290
  27.2 3.3 %collective-permute-start.14 = (f32[4,8,512]{2,1,0:T(8,128)S(1)}, f32[4,8,512]{2,1,0:T(8,128)S(1)}, u32[]{:S(2)}, u32[]{:S(2)}) collective-permute-start(f32[4,8,512]{2,1,0:T(8,128)S(1)} %collective-permute-done.10.refs_0_), channel_id=1, source_target_pairs={{0,1},{1,0},{2,3},{3,2},{4,5},{5,4},{6,7},{7,6},{8,9},{9,8},{10,11... | collective-permute-start | bytes 196616 | tf_op jit(solution)/shard_map/ppermute | solution.py:279
  29.6 1.3 %collective-permute-start.15 = (f32[4,8,512]{2,1,0:T(8,128)S(1)}, f32[4,8,512]{2,1,0:T(8,128)S(1)}, u32[]{:S(2)}, u32[]{:S(2)}) collective-permute-start(f32[4,8,512]{2,1,0:T(8,128)S(1)} %collective-permute-done.11.refs_1_), channel_id=1, source_target_pairs={{0,1},{1,0},{2,3},{3,2},{4,5},{5,4},{6,7},{7,6},{8,9},{9,8},{10,11... | collective-permute-start | bytes 196616 | tf_op jit(solution)/shard_map/ppermute | solution.py:279
  30.0 1.3 %collective-permute-start.16 = (f32[4,8,512]{2,1,0:T(8,128)S(1)}, f32[4,8,512]{2,1,0:T(8,128)S(1)}, u32[]{:S(2)}, u32[]{:S(2)}) collective-permute-start(f32[4,8,512]{2,1,0:T(8,128)S(1)} %collective-permute-done.12.refs_2_), channel_id=1, source_target_pairs={{0,1},{1,0},{2,3},{3,2},{4,5},{5,4},{6,7},{7,6},{8,9},{9,8},{10,11... | collective-permute-start | bytes 196616 | tf_op jit(solution)/shard_map/ppermute | solution.py:279
  30.2 1.3 %collective-permute-start.17 = (f32[4,8,512]{2,1,0:T(8,128)S(1)}, f32[4,8,512]{2,1,0:T(8,128)S(1)}, u32[]{:S(2)}, u32[]{:S(2)}) collective-permute-start(f32[4,8,512]{2,1,0:T(8,128)S(1)} %collective-permute-done.13.refs_3_), channel_id=1, source_target_pairs={{0,1},{1,0},{2,3},{3,2},{4,5},{5,4},{6,7},{7,6},{8,9},{9,8},{10,11... | collective-permute-start | bytes 196616 | tf_op jit(solution)/shard_map/ppermute | solution.py:279
  (3 other events, 4.8 us)

commit v16 on v14

--- a/solution.py
+++ b/solution.py
@@ -130,6 +130,7 @@
 LARGE = pltpu.CompilerParams(vmem_limit_bytes=53 * 1024 * 1024)
 WIDTH = 256
 BIAS_TERMS = 3
+FIRST = 64
 GELU_TERMS = (
     0.7978849411010742,
     0.03633308410644531,
@@ -454,7 +455,7 @@
 def output_kernel(layers, flow_ref, table_ref, local_ref, bias_ref, *refs):
     own_refs, core_refs = refs[:layers], refs[layers : 2 * layers]
     out_hbm, order_ref, wide_ref, level_ref, done_ref, sent = refs[2 * layers :]
-    cells_x, _, feat_count = flow_ref.shape
+    cells_x, cells_y, feat_count = flow_ref.shape
     channels = local_ref.shape[0]
     z, x, y = quad()
     wide_ref[...] = jnp.zeros_like(wide_ref)
@@ -479,15 +480,22 @@
     for cell in range(cells_x):
         high, low = split_terms(order_ref[cell].reshape(-1, feat_count))
         stack = jnp.concatenate([high, low, high], axis=0)
-        for start in range(0, feat_count, WIDTH):
-            columns = slice(start, start + WIDTH)
-            total = dot(
-                jnp.concatenate([table, flow_ref[cell, :, columns]], axis=1),
-                jnp.concatenate([stack[:, columns], below], axis=0),
+        bounds = [0, FIRST, cells_y] if cell == 0 else [0, cells_y]
+        for begin, end in zip(bounds[:-1], bounds[1:]):
+            rows = slice(begin, end)
+            for start in range(0, feat_count, WIDTH):
+                columns = slice(start, start + WIDTH)
+                total = dot(
+                    jnp.concatenate([table[rows], flow_ref[cell, rows, columns]], axis=1),
+                    jnp.concatenate([stack[:, columns], below], axis=0),
+                )
+                done_ref[cell, rows, columns] = gelu(total).astype(done_ref.dtype)
+            copies.append(
+                pltpu.make_async_copy(
+                    done_ref.at[cell, rows], out_hbm.at[cell, rows], sent.at[len(copies)]
+                )
             )
-            done_ref[cell, :, columns] = gelu(total).astype(done_ref.dtype)
-        copies.append(pltpu.make_async_copy(done_ref.at[cell], out_hbm.at[cell], sent.at[cell]))
-        copies[-1].start()
+            copies[-1].start()
     for copy in copies:
         copy.wait()
 
@@ -503,7 +511,7 @@
             pltpu.VMEM((WIDTH, WIDTH), jnp.bfloat16),
             pltpu.VMEM((1, WIDTH), jnp.float32),
             pltpu.VMEM(flow_field.shape, jnp.bfloat16),
-            pltpu.SemaphoreType.DMA((cells_x,)),
+            pltpu.SemaphoreType.DMA((cells_x + 1,)),
         ],
         out_shape=jax.ShapeDtypeStruct(flow_field.shape, jnp.bfloat16),
         compiler_params=SMALL,

time: 34.2 us -> 34.1 us (level)
  no operation moved by 1% of the time
where the time goes in v16:
time: 34.1 us; the launch traced here: 34 us
  starting transfers between devices  16.5 us (48%)
  waiting for transfers between devices  10.5 us (31%)
  Pallas kernels  6.19 us (18%)
  between operations  0.76 us (2%)
    ppermute x8, starting transfers between devices, along_columns(): arrived.append(lax.ppermute(block, ('gx', 'gy'), pairs))  11 us
    ppermute x8, waiting for transfers between devices, along_columns(): arrived.append(lax.ppermute(block, ('gx', 'gy'), pairs))  7.22 us
    ppermute x10, starting transfers between devices, flip_core(): return lax.ppermute(block, 'gy', [(0, 1), (1, 0)])  5.42 us
    ppermute x10, waiting for transfers between devices, flip_core(): return lax.ppermute(block, 'gy', [(0, 1), (1, 0)])  3.32 us
    pallas_call x1, Pallas kernels, make_output(): pl.pallas_call(functools.partial(output_kernel, layers), out_specs=pl.Blo...  2.52 us
    pallas_call x1, Pallas kernels, forward_y(): pl.pallas_call(functools.partial(forward_y_kernel, extent, rows_ky), in_s...  1.75 us
    pallas_call x1, Pallas kernels, mix(): pl.pallas_call(functools.partial(mix_kernel, layers), out_shape=[jax.Shap...  1.05 us
    pallas_call x1, Pallas kernels, keep_rows(): pl.pallas_call(keep_kernel, out_shape=[jax.ShapeDtypeStruct((1, rows // 2...  0.79 us
  transfers between devices with their start and end apart: 18, of which 13 were waited for; matrix products, arithmetic and copies ran while one was open for 0% of the time, Pallas kernels for 2%

profile of v16, /device:TPU:0, one launch (start us, length us, event | category | flops | bytes accessed | tf_op | source)
XLA Modules:
  0.0 34.0 jit_solution(5389990059105024981)
XLA Ops:
  0.6 1.7 %forward_y.1 = (f32[4,2,16,512]{3,2,1,0:T(8,128)S(1)}, f32[4,2,16,512]{3,2,1,0:T(8,128)S(1)}) custom-call(bf16[4,256,512]{2,1,0:T(8,128)(2,1)} %flow_ref.1), custom_call_target="tpu_custom_call" | custom-call | tf_op jit(solution)/shard_map/forward_y/pallas_call | solution.py:265
  2.4 0.5 %collective-permute-start = (f32[4,2,16,512]{3,2,1,0:T(8,128)S(1)}, f32[4,2,16,512]{3,2,1,0:T(8,128)S(1)}, u32[]{:S(2)}, u32[]{:S(2)}) collective-permute-start(f32[4,2,16,512]{3,2,1,0:T(8,128)S(1)} %get-tuple-element.17), channel_id=1, source_target_pairs={{0,1},{1,0},{2,3},{3,2},{4,5},{5,4},{6,7},{7,6},{8,9},{9,8},{10,11... | collective-permute-start | bytes 786440 | tf_op jit(solution)/shard_map/ppermute | solution.py:279
  2.9 1.2 %collective-permute-done.arrived_ref = f32[4,2,16,512]{3,2,1,0:T(8,128)S(1)} collective-permute-done((f32[4,2,16,512]{3,2,1,0:T(8,128)S(1)}, f32[4,2,16,512]{3,2,1,0:T(8,128)S(1)}, u32[]{:S(2)}, u32[]{:S(2)}) %collective-permute-start) | collective-permute-done | bytes 262176 | tf_op jit(solution)/shard_map/ppermute | solution.py:279
  4.1 4.0 %collective-permute-start.1 = (f32[2,16,512]{2,1,0:T(8,128)S(1)}, f32[2,16,512]{2,1,0:T(8,128)S(1)}, u32[]{:S(2)}, u32[]{:S(2)}) collective-permute-start(f32[2,16,512]{2,1,0:T(8,128)S(1)} %get-tuple-element.18), channel_id=1, source_target_pairs={{0,8},{1,11},{2,10},{3,9},{4,12},{5,15},{6,14},{7,13},{8,0},{9,3},... | collective-permute-start | bytes 196616 | tf_op jit(solution)/shard_map/ppermute | solution.py:290
  8.1 1.3 %collective-permute-start.2 = (f32[2,16,512]{2,1,0:T(8,128)S(1)}, f32[2,16,512]{2,1,0:T(8,128)S(1)}, u32[]{:S(2)}, u32[]{:S(2)}) collective-permute-start(f32[2,16,512]{2,1,0:T(8,128)S(1)} %get-tuple-element.19), channel_id=1, source_target_pairs={{0,12},{1,15},{2,14},{3,13},{4,8},{5,11},{6,10},{7,9},{8,4},{9,7},... | collective-permute-start | bytes 196616 | tf_op jit(solution)/shard_map/ppermute | solution.py:290
  9.7 0.7 %collective-permute-start.4 = (f32[2,16,512]{2,1,0:T(8,128)S(1)}, f32[2,16,512]{2,1,0:T(8,128)S(1)}, u32[]{:S(2)}, u32[]{:S(2)}) collective-permute-start(f32[2,16,512]{2,1,0:T(8,128)S(1)} %get-tuple-element.21), channel_id=1, source_target_pairs={{0,0},{1,3},{2,2},{3,1},{4,4},{5,7},{6,6},{7,5},{8,8},{9,11},{10,1... | collective-permute-start | bytes 196616 | tf_op jit(solution)/shard_map/ppermute | solution.py:290
  10.4 0.4 %collective-permute-done.1.block_ref.refs_0_ = f32[2,16,512]{2,1,0:T(8,128)S(1)} collective-permute-done((f32[2,16,512]{2,1,0:T(8,128)S(1)}, f32[2,16,512]{2,1,0:T(8,128)S(1)}, u32[]{:S(2)}, u32[]{:S(2)}) %collective-permute-start.1) | collective-permute-done | bytes 65568 | tf_op jit(solution)/shard_map/ppermute | solution.py:290
  10.7 2.6 %collective-permute-start.5 = (f32[16,512]{1,0:T(8,128)S(1)}, f32[16,512]{1,0:T(8,128)S(1)}, u32[]{:S(2)}, u32[]{:S(2)}) collective-permute-start(f32[16,512]{1,0:T(8,128)S(1)} %second_half.4), channel_id=1, source_target_pairs={{0,1},{1,0},{2,3},{3,2},{4,5},{5,4},{6,7},{7,6},{8,9},{9,8},{10,11... | collective-permute-start | bytes 98312 | tf_op jit(solution)/shard_map/ppermute | solution.py:279
  13.4 1.4 %collective-permute-done.2.block_ref.refs_1_ = f32[2,16,512]{2,1,0:T(8,128)S(1)} collective-permute-done((f32[2,16,512]{2,1,0:T(8,128)S(1)}, f32[2,16,512]{2,1,0:T(8,128)S(1)}, u32[]{:S(2)}, u32[]{:S(2)}) %collective-permute-start.2) | collective-permute-done | bytes 65568 | tf_op jit(solution)/shard_map/ppermute | solution.py:290
  14.8 0.5 %collective-permute-start.6 = (f32[16,512]{1,0:T(8,128)S(1)}, f32[16,512]{1,0:T(8,128)S(1)}, u32[]{:S(2)}, u32[]{:S(2)}) collective-permute-start(f32[16,512]{1,0:T(8,128)S(1)} %second_half.5), channel_id=1, source_target_pairs={{0,1},{1,0},{2,3},{3,2},{4,5},{5,4},{6,7},{7,6},{8,9},{9,8},{10,11... | collective-permute-start | bytes 98312 | tf_op jit(solution)/shard_map/ppermute | solution.py:279
  15.8 0.4 %collective-permute-start.8 = (f32[16,512]{1,0:T(8,128)S(1)}, f32[16,512]{1,0:T(8,128)S(1)}, u32[]{:S(2)}, u32[]{:S(2)}) collective-permute-start(f32[16,512]{1,0:T(8,128)S(1)} %second_half.7), channel_id=1, source_target_pairs={{0,1},{1,0},{2,3},{3,2},{4,5},{5,4},{6,7},{7,6},{8,9},{9,8},{10,11... | collective-permute-start | bytes 98312 | tf_op jit(solution)/shard_map/ppermute | solution.py:279
  16.2 0.6 %collective-permute-done.7.refs_6_ = f32[16,512]{1,0:T(8,128)S(1)} collective-permute-done((f32[16,512]{1,0:T(8,128)S(1)}, f32[16,512]{1,0:T(8,128)S(1)}, u32[]{:S(2)}, u32[]{:S(2)}) %collective-permute-start.7) | collective-permute-done | bytes 32800 | tf_op jit(solution)/shard_map/ppermute | solution.py:279
  17.2 1.1 %mix.1 = (f32[128,512]{1,0:T(8,128)S(1)}, f32[4,16,512]{2,1,0:T(8,128)S(1)}) custom-call(f32[2,16,512]{2,1,0:T(8,128)S(1)} %collective-permute-done.1.block_ref.refs_0_, f32[2,16,512]{2,1,0:T(8,128)S(1)} %collective-permute-done.2.block_ref.refs_1_, f32[2,16,512]{2,1,0:T(8,128)S(1)} %collective-permute-done.3.block_ref.refs_2_, ...), custom_call_target="tpu_custom_call" | custom-call | tf_op jit(solution)/shard_map/mix/pallas_call | solution.py:407
  18.2 0.4 %collective-permute-start.9 = (f32[4,16,512]{2,1,0:T(8,128)S(1)}, f32[4,16,512]{2,1,0:T(8,128)S(1)}, u32[]{:S(2)}, u32[]{:S(2)}) collective-permute-start(f32[4,16,512]{2,1,0:T(8,128)S(1)} %get-tuple-element.24), channel_id=1, source_target_pairs={{0,1},{1,0},{2,3},{3,2},{4,5},{5,4},{6,7},{7,6},{8,9},{9,8},{10,11... | collective-permute-start | bytes 393224 | tf_op jit(solution)/shard_map/ppermute | solution.py:279
  18.6 0.8 %keep_rows.1 = (f32[1,64,1024]{2,1,0:T(8,128)}, f32[4,16,512]{2,1,0:T(8,128)S(1)}) custom-call(f32[128,512]{1,0:T(8,128)S(1)} %get-tuple-element.22.modes_ref, bf16[2,64,128]{2,1,0:T(8,128)(2,1)S(1)} %copy-done.4, bf16[2,64,128]{2,1,0:T(8,128)(2,1)S(1)} %copy-done.3), custom_call_target="tpu_custom_call" | custom-call | tf_op jit(solution)/shard_map/keep_rows/pallas_call | solution.py:434
  19.7 3.1 %collective-permute-start.10 = (f32[4,8,512]{2,1,0:T(8,128)S(1)}, f32[4,8,512]{2,1,0:T(8,128)S(1)}, u32[]{:S(2)}, u32[]{:S(2)}) collective-permute-start(f32[4,8,512]{2,1,0:T(8,128)S(1)} %get-tuple-element.25), channel_id=1, source_target_pairs={{0,8},{1,11},{2,10},{3,9},{4,12},{5,15},{6,14},{7,13},{8,0},{9,3},... | collective-permute-start | bytes 196616 | tf_op jit(solution)/shard_map/ppermute | solution.py:290
  22.8 0.7 %collective-permute-start.11 = (f32[4,8,512]{2,1,0:T(8,128)S(1)}, f32[4,8,512]{2,1,0:T(8,128)S(1)}, u32[]{:S(2)}, u32[]{:S(2)}) collective-permute-start(f32[4,8,512]{2,1,0:T(8,128)S(1)} %get-tuple-element.26), channel_id=1, source_target_pairs={{0,12},{1,15},{2,14},{3,13},{4,8},{5,11},{6,10},{7,9},{8,4},{9,7},... | collective-permute-start | bytes 196616 | tf_op jit(solution)/shard_map/ppermute | solution.py:290
  23.5 0.3 collective-permute-start.12
  23.8 0.7 %collective-permute-start.13 = (f32[4,8,512]{2,1,0:T(8,128)S(1)}, f32[4,8,512]{2,1,0:T(8,128)S(1)}, u32[]{:S(2)}, u32[]{:S(2)}) collective-permute-start(f32[4,8,512]{2,1,0:T(8,128)S(1)} %get-tuple-element.28), channel_id=1, source_target_pairs={{0,0},{1,3},{2,2},{3,1},{4,4},{5,7},{6,6},{7,5},{8,8},{9,11},{10,1... | collective-permute-start | bytes 196616 | tf_op jit(solution)/shard_map/ppermute | solution.py:290
  24.5 2.7 %collective-permute-done.10.refs_0_ = f32[4,8,512]{2,1,0:T(8,128)S(1)} collective-permute-done((f32[4,8,512]{2,1,0:T(8,128)S(1)}, f32[4,8,512]{2,1,0:T(8,128)S(1)}, u32[]{:S(2)}, u32[]{:S(2)}) %collective-permute-start.10) | collective-permute-done | bytes 65568 | tf_op jit(solution)/shard_map/ppermute | solution.py:290
  27.2 2.4 %collective-permute-done.11.refs_1_ = f32[4,8,512]{2,1,0:T(8,128)S(1)} collective-permute-done((f32[4,8,512]{2,1,0:T(8,128)S(1)}, f32[4,8,512]{2,1,0:T(8,128)S(1)}, u32[]{:S(2)}, u32[]{:S(2)}) %collective-permute-start.11) | collective-permute-done | bytes 65568 | tf_op jit(solution)/shard_map/ppermute | solution.py:290
  30.5 0.4 %collective-permute-done.15.refs_5_ = f32[4,8,512]{2,1,0:T(8,128)S(1)} collective-permute-done((f32[4,8,512]{2,1,0:T(8,128)S(1)}, f32[4,8,512]{2,1,0:T(8,128)S(1)}, u32[]{:S(2)}, u32[]{:S(2)}) %collective-permute-start.15) | collective-permute-done | bytes 65568 | tf_op jit(solution)/shard_map/ppermute | solution.py:279
  30.9 0.4 %collective-permute-done.16.refs_6_ = f32[4,8,512]{2,1,0:T(8,128)S(1)} collective-permute-done((f32[4,8,512]{2,1,0:T(8,128)S(1)}, f32[4,8,512]{2,1,0:T(8,128)S(1)}, u32[]{:S(2)}, u32[]{:S(2)}) %collective-permute-start.16) | collective-permute-done | bytes 65568 | tf_op jit(solution)/shard_map/ppermute | solution.py:279
  31.5 2.5 %make_output.1 = bf16[4,256,512]{2,1,0:T(8,128)(2,1)} custom-call(bf16[4,256,512]{2,1,0:T(8,128)(2,1)S(1)} %copy-done, bf16[2,2,256,256]{3,2,1,0:T(8,128)(2,1)S(1)} %copy-done.2, bf16[64,64]{1,0:T(8,128)(2,1)S(1)} %copy-done.7, f32[64]{0:T(128)S(1)} %copy-done.8, f32[4,8,512]{2,1,0:T(8,128)S(1)} %collective-permute-done.10.refs_0_, ...), custom_call_target="tpu_custom_call" | custom-call | tf_op jit(solution)/shard_map/make_output/pallas_call | solution.py:506
  (40 shorter events, 2.5 us)
Async XLA Ops:
  0.6 16.5 %copy-start.1 = (bf16[1,64,64,128]{3,2,1,0:T(8,128)(2,1)S(1)}, bf16[1,64,64,128]{3,2,1,0:T(8,128)(2,1)}, u32[]{:S(2)}) copy-start(bf16[1,64,64,128]{3,2,1,0:T(8,128)(2,1)} %refs_8_.1) | copy-start | bytes 3145732
  2.4 1.7 %collective-permute-start = (f32[4,2,16,512]{3,2,1,0:T(8,128)S(1)}, f32[4,2,16,512]{3,2,1,0:T(8,128)S(1)}, u32[]{:S(2)}, u32[]{:S(2)}) collective-permute-start(f32[4,2,16,512]{3,2,1,0:T(8,128)S(1)} %get-tuple-element.17), channel_id=1, source_target_pairs={{0,1},{1,0},{2,3},{3,2},{4,5},{5,4},{6,7},{7,6},{8,9},{9,8},{10,11... | collective-permute-start | bytes 786440 | tf_op jit(solution)/shard_map/ppermute | solution.py:279
  4.1 6.6 %collective-permute-start.1 = (f32[2,16,512]{2,1,0:T(8,128)S(1)}, f32[2,16,512]{2,1,0:T(8,128)S(1)}, u32[]{:S(2)}, u32[]{:S(2)}) collective-permute-start(f32[2,16,512]{2,1,0:T(8,128)S(1)} %get-tuple-element.18), channel_id=1, source_target_pairs={{0,8},{1,11},{2,10},{3,9},{4,12},{5,15},{6,14},{7,13},{8,0},{9,3},... | collective-permute-start | bytes 196616 | tf_op jit(solution)/shard_map/ppermute | solution.py:290
  8.1 6.7 %collective-permute-start.2 = (f32[2,16,512]{2,1,0:T(8,128)S(1)}, f32[2,16,512]{2,1,0:T(8,128)S(1)}, u32[]{:S(2)}, u32[]{:S(2)}) collective-permute-start(f32[2,16,512]{2,1,0:T(8,128)S(1)} %get-tuple-element.19), channel_id=1, source_target_pairs={{0,12},{1,15},{2,14},{3,13},{4,8},{5,11},{6,10},{7,9},{8,4},{9,7},... | collective-permute-start | bytes 196616 | tf_op jit(solution)/shard_map/ppermute | solution.py:290
  9.5 6.0 %collective-permute-start.3 = (f32[2,16,512]{2,1,0:T(8,128)S(1)}, f32[2,16,512]{2,1,0:T(8,128)S(1)}, u32[]{:S(2)}, u32[]{:S(2)}) collective-permute-start(f32[2,16,512]{2,1,0:T(8,128)S(1)} %get-tuple-element.20), channel_id=1, source_target_pairs={{0,4},{1,7},{2,6},{3,5},{4,0},{5,3},{6,2},{7,1},{8,12},{9,15},{10,... | collective-permute-start | bytes 196616 | tf_op jit(solution)/shard_map/ppermute | solution.py:290
  9.7 6.1 %collective-permute-start.4 = (f32[2,16,512]{2,1,0:T(8,128)S(1)}, f32[2,16,512]{2,1,0:T(8,128)S(1)}, u32[]{:S(2)}, u32[]{:S(2)}) collective-permute-start(f32[2,16,512]{2,1,0:T(8,128)S(1)} %get-tuple-element.21), channel_id=1, source_target_pairs={{0,0},{1,3},{2,2},{3,1},{4,4},{5,7},{6,6},{7,5},{8,8},{9,11},{10,1... | collective-permute-start | bytes 196616 | tf_op jit(solution)/shard_map/ppermute | solution.py:290
  10.7 5.5 %collective-permute-start.5 = (f32[16,512]{1,0:T(8,128)S(1)}, f32[16,512]{1,0:T(8,128)S(1)}, u32[]{:S(2)}, u32[]{:S(2)}) collective-permute-start(f32[16,512]{1,0:T(8,128)S(1)} %second_half.4), channel_id=1, source_target_pairs={{0,1},{1,0},{2,3},{3,2},{4,5},{5,4},{6,7},{7,6},{8,9},{9,8},{10,11... | collective-permute-start | bytes 98312 | tf_op jit(solution)/shard_map/ppermute | solution.py:279
  14.8 1.4 %collective-permute-start.6 = (f32[16,512]{1,0:T(8,128)S(1)}, f32[16,512]{1,0:T(8,128)S(1)}, u32[]{:S(2)}, u32[]{:S(2)}) collective-permute-start(f32[16,512]{1,0:T(8,128)S(1)} %second_half.5), channel_id=1, source_target_pairs={{0,1},{1,0},{2,3},{3,2},{4,5},{5,4},{6,7},{7,6},{8,9},{9,8},{10,11... | collective-permute-start | bytes 98312 | tf_op jit(solution)/shard_map/ppermute | solution.py:279
  15.5 1.6 %copy-start.6 = (bf16[128,128]{1,0:T(8,128)(2,1)S(1)}, bf16[128,128]{1,0:T(8,128)(2,1)}, u32[]{:S(2)}) copy-start(bf16[128,128]{1,0:T(8,128)(2,1)} %constant.10.clone.refs_9_) | copy-start | bytes 98308
  15.6 1.3 %collective-permute-start.7 = (f32[16,512]{1,0:T(8,128)S(1)}, f32[16,512]{1,0:T(8,128)S(1)}, u32[]{:S(2)}, u32[]{:S(2)}) collective-permute-start(f32[16,512]{1,0:T(8,128)S(1)} %second_half.6), channel_id=1, source_target_pairs={{0,1},{1,0},{2,3},{3,2},{4,5},{5,4},{6,7},{7,6},{8,9},{9,8},{10,11... | collective-permute-start | bytes 98312 | tf_op jit(solution)/shard_map/ppermute | solution.py:279
  15.8 15.6 %copy-start = (bf16[4,256,512]{2,1,0:T(8,128)(2,1)S(1)}, bf16[4,256,512]{2,1,0:T(8,128)(2,1)}, u32[]{:S(2)}) copy-start(bf16[4,256,512]{2,1,0:T(8,128)(2,1)} %flow_ref.1) | copy-start | bytes 3145732
  15.8 1.3 %collective-permute-start.8 = (f32[16,512]{1,0:T(8,128)S(1)}, f32[16,512]{1,0:T(8,128)S(1)}, u32[]{:S(2)}, u32[]{:S(2)}) collective-permute-start(f32[16,512]{1,0:T(8,128)S(1)} %second_half.7), channel_id=1, source_target_pairs={{0,1},{1,0},{2,3},{3,2},{4,5},{5,4},{6,7},{7,6},{8,9},{9,8},{10,11... | collective-permute-start | bytes 98312 | tf_op jit(solution)/shard_map/ppermute | solution.py:279
  18.2 13.2 %copy-start.2 = (bf16[2,2,256,256]{3,2,1,0:T(8,128)(2,1)S(1)}, bf16[2,2,256,256]{3,2,1,0:T(8,128)(2,1)}, u32[]{:S(2)}) copy-start(bf16[2,2,256,256]{3,2,1,0:T(8,128)(2,1)} %constant.14.clone.table_ref) | copy-start | bytes 1572868
  18.2 1.4 %collective-permute-start.9 = (f32[4,16,512]{2,1,0:T(8,128)S(1)}, f32[4,16,512]{2,1,0:T(8,128)S(1)}, u32[]{:S(2)}, u32[]{:S(2)}) collective-permute-start(f32[4,16,512]{2,1,0:T(8,128)S(1)} %get-tuple-element.24), channel_id=1, source_target_pairs={{0,1},{1,0},{2,3},{3,2},{4,5},{5,4},{6,7},{7,6},{8,9},{9,8},{10,11... | collective-permute-start | bytes 393224 | tf_op jit(solution)/shard_map/ppermute | solution.py:279
  19.6 11.8 %copy-start.7 = (bf16[64,64]{1,0:T(8,128)(2,1)S(1)}, bf16[64,64]{1,0:T(8,128)(2,1)}, u32[]{:S(2)}) copy-start(bf16[64,64]{1,0:T(8,128)(2,1)} %local_ref.1) | copy-start | bytes 24580
  19.7 7.5 %collective-permute-start.10 = (f32[4,8,512]{2,1,0:T(8,128)S(1)}, f32[4,8,512]{2,1,0:T(8,128)S(1)}, u32[]{:S(2)}, u32[]{:S(2)}) collective-permute-start(f32[4,8,512]{2,1,0:T(8,128)S(1)} %get-tuple-element.25), channel_id=1, source_target_pairs={{0,8},{1,11},{2,10},{3,9},{4,12},{5,15},{6,14},{7,13},{8,0},{9,3},... | collective-permute-start | bytes 196616 | tf_op jit(solution)/shard_map/ppermute | solution.py:290
  22.8 6.8 %collective-permute-start.11 = (f32[4,8,512]{2,1,0:T(8,128)S(1)}, f32[4,8,512]{2,1,0:T(8,128)S(1)}, u32[]{:S(2)}, u32[]{:S(2)}) collective-permute-start(f32[4,8,512]{2,1,0:T(8,128)S(1)} %get-tuple-element.26), channel_id=1, source_target_pairs={{0,12},{1,15},{2,14},{3,13},{4,8},{5,11},{6,10},{7,9},{8,4},{9,7},... | collective-permute-start | bytes 196616 | tf_op jit(solution)/shard_map/ppermute | solution.py:290
  23.5 8.0 %copy-start.8 = (f32[64]{0:T(128)S(1)}, f32[64]{0:T(128)}, u32[]{:S(2)}) copy-start(f32[64]{0:T(128)} %bias_ref.1) | copy-start | bytes 772
  23.5 6.5 %collective-permute-start.12 = (f32[4,8,512]{2,1,0:T(8,128)S(1)}, f32[4,8,512]{2,1,0:T(8,128)S(1)}, u32[]{:S(2)}, u32[]{:S(2)}) collective-permute-start(f32[4,8,512]{2,1,0:T(8,128)S(1)} %get-tuple-element.27), channel_id=1, source_target_pairs={{0,4},{1,7},{2,6},{3,5},{4,0},{5,3},{6,2},{7,1},{8,12},{9,15},{10,... | collective-permute-start | bytes 196616 | tf_op jit(solution)/shard_map/ppermute | solution.py:290
  23.8 6.4 %collective-permute-start.13 = (f32[4,8,512]{2,1,0:T(8,128)S(1)}, f32[4,8,512]{2,1,0:T(8,128)S(1)}, u32[]{:S(2)}, u32[]{:S(2)}) collective-permute-start(f32[4,8,512]{2,1,0:T(8,128)S(1)} %get-tuple-element.28), channel_id=1, source_target_pairs={{0,0},{1,3},{2,2},{3,1},{4,4},{5,7},{6,6},{7,5},{8,8},{9,11},{10,1... | collective-permute-start | bytes 196616 | tf_op jit(solution)/shard_map/ppermute | solution.py:290
  27.2 3.3 %collective-permute-start.14 = (f32[4,8,512]{2,1,0:T(8,128)S(1)}, f32[4,8,512]{2,1,0:T(8,128)S(1)}, u32[]{:S(2)}, u32[]{:S(2)}) collective-permute-start(f32[4,8,512]{2,1,0:T(8,128)S(1)} %collective-permute-done.10.refs_0_), channel_id=1, source_target_pairs={{0,1},{1,0},{2,3},{3,2},{4,5},{5,4},{6,7},{7,6},{8,9},{9,8},{10,11... | collective-permute-start | bytes 196616 | tf_op jit(solution)/shard_map/ppermute | solution.py:279
  29.6 1.3 %collective-permute-start.15 = (f32[4,8,512]{2,1,0:T(8,128)S(1)}, f32[4,8,512]{2,1,0:T(8,128)S(1)}, u32[]{:S(2)}, u32[]{:S(2)}) collective-permute-start(f32[4,8,512]{2,1,0:T(8,128)S(1)} %collective-permute-done.11.refs_1_), channel_id=1, source_target_pairs={{0,1},{1,0},{2,3},{3,2},{4,5},{5,4},{6,7},{7,6},{8,9},{9,8},{10,11... | collective-permute-start | bytes 196616 | tf_op jit(solution)/shard_map/ppermute | solution.py:279
  30.0 1.3 %collective-permute-start.16 = (f32[4,8,512]{2,1,0:T(8,128)S(1)}, f32[4,8,512]{2,1,0:T(8,128)S(1)}, u32[]{:S(2)}, u32[]{:S(2)}) collective-permute-start(f32[4,8,512]{2,1,0:T(8,128)S(1)} %collective-permute-done.12.refs_2_), channel_id=1, source_target_pairs={{0,1},{1,0},{2,3},{3,2},{4,5},{5,4},{6,7},{7,6},{8,9},{9,8},{10,11... | collective-permute-start | bytes 196616 | tf_op jit(solution)/shard_map/ppermute | solution.py:279
  30.2 1.3 %collective-permute-start.17 = (f32[4,8,512]{2,1,0:T(8,128)S(1)}, f32[4,8,512]{2,1,0:T(8,128)S(1)}, u32[]{:S(2)}, u32[]{:S(2)}) collective-permute-start(f32[4,8,512]{2,1,0:T(8,128)S(1)} %collective-permute-done.13.refs_3_), channel_id=1, source_target_pairs={{0,1},{1,0},{2,3},{3,2},{4,5},{5,4},{6,7},{7,6},{8,9},{9,8},{10,11... | collective-permute-start | bytes 196616 | tf_op jit(solution)/shard_map/ppermute | solution.py:279
  (3 other events, 4.8 us)

commit v17 on v16

--- a/solution.py
+++ b/solution.py
@@ -131,7 +131,7 @@
 WIDTH = 256
 BIAS_TERMS = 3
 FIRST = 64
-GELU_TERMS = (
+POWER_TERMS = tuple(-2.0 * math.log2(math.e) * term for term in (
     0.7978849411010742,
     0.03633308410644531,
     -3.259492223151028e-05,
@@ -139,7 +139,7 @@
     3.964749794249656e-06,
     -1.3226382122866198e-07,
     1.7561855303327434e-09,
-)
+))
 
 
 def angles(count, places, extent):
@@ -445,11 +445,11 @@
 
 def gelu(values):
     square = jnp.minimum(values * values, 31.36)
-    inner = jnp.full_like(square, GELU_TERMS[-1])
-    for term in GELU_TERMS[-2::-1]:
-        inner = inner * square + term
-    half = 0.5 * values
-    return half + half * jnp.tanh(values * inner)
+    power = jnp.full_like(square, POWER_TERMS[-1])
+    for term in POWER_TERMS[-2::-1]:
+        power = power * square + term
+    below = 1.0 + jnp.exp2(jnp.minimum(values * power, 64.0))
+    return values * pl.reciprocal(below, approx=True)
 
 
 def output_kernel(layers, flow_ref, table_ref, local_ref, bias_ref, *refs):

time: 34.1 us -> 34.2 us (level)
  no operation moved by 1% of the time
where the time goes in v17:
time: 34.2 us; the launch traced here: 34 us
  starting transfers between devices  16.5 us (48%)
  waiting for transfers between devices  10.5 us (31%)
  Pallas kernels  6.24 us (18%)
  between operations  0.76 us (2%)
    ppermute x8, starting transfers between devices, along_columns(): arrived.append(lax.ppermute(block, ('gx', 'gy'), pairs))  11 us
    ppermute x8, waiting for transfers between devices, along_columns(): arrived.append(lax.ppermute(block, ('gx', 'gy'), pairs))  7.22 us
    ppermute x10, starting transfers between devices, flip_core(): return lax.ppermute(block, 'gy', [(0, 1), (1, 0)])  5.42 us
    ppermute x10, waiting for transfers between devices, flip_core(): return lax.ppermute(block, 'gy', [(0, 1), (1, 0)])  3.32 us
    pallas_call x1, Pallas kernels, make_output(): pl.pallas_call(functools.partial(output_kernel, layers), out_specs=pl.Blo...  2.57 us
    pallas_call x1, Pallas kernels, forward_y(): pl.pallas_call(functools.partial(forward_y_kernel, extent, rows_ky), in_s...  1.75 us
    pallas_call x1, Pallas kernels, mix(): pl.pallas_call(functools.partial(mix_kernel, layers), out_shape=[jax.Shap...  1.05 us
    pallas_call x1, Pallas kernels, keep_rows(): pl.pallas_call(keep_kernel, out_shape=[jax.ShapeDtypeStruct((1, rows // 2...  0.79 us
  transfers between devices with their start and end apart: 18, of which 13 were waited for; matrix products, arithmetic and copies ran while one was open for 0% of the time, Pallas kernels for 2%

profile of v17, /device:TPU:0, one launch (start us, length us, event | category | flops | bytes accessed | tf_op | source)
XLA Modules:
  0.0 34.0 jit_solution(12896804616066655366)
XLA Ops:
  0.6 1.7 %forward_y.1 = (f32[4,2,16,512]{3,2,1,0:T(8,128)S(1)}, f32[4,2,16,512]{3,2,1,0:T(8,128)S(1)}) custom-call(bf16[4,256,512]{2,1,0:T(8,128)(2,1)} %flow_ref.1), custom_call_target="tpu_custom_call" | custom-call | tf_op jit(solution)/shard_map/forward_y/pallas_call | solution.py:265
  2.4 0.5 %collective-permute-start = (f32[4,2,16,512]{3,2,1,0:T(8,128)S(1)}, f32[4,2,16,512]{3,2,1,0:T(8,128)S(1)}, u32[]{:S(2)}, u32[]{:S(2)}) collective-permute-start(f32[4,2,16,512]{3,2,1,0:T(8,128)S(1)} %get-tuple-element.17), channel_id=1, source_target_pairs={{0,1},{1,0},{2,3},{3,2},{4,5},{5,4},{6,7},{7,6},{8,9},{9,8},{10,11... | collective-permute-start | bytes 786440 | tf_op jit(solution)/shard_map/ppermute | solution.py:279
  2.9 1.2 %collective-permute-done.arrived_ref = f32[4,2,16,512]{3,2,1,0:T(8,128)S(1)} collective-permute-done((f32[4,2,16,512]{3,2,1,0:T(8,128)S(1)}, f32[4,2,16,512]{3,2,1,0:T(8,128)S(1)}, u32[]{:S(2)}, u32[]{:S(2)}) %collective-permute-start) | collective-permute-done | bytes 262176 | tf_op jit(solution)/shard_map/ppermute | solution.py:279
  4.1 4.0 %collective-permute-start.1 = (f32[2,16,512]{2,1,0:T(8,128)S(1)}, f32[2,16,512]{2,1,0:T(8,128)S(1)}, u32[]{:S(2)}, u32[]{:S(2)}) collective-permute-start(f32[2,16,512]{2,1,0:T(8,128)S(1)} %get-tuple-element.18), channel_id=1, source_target_pairs={{0,8},{1,11},{2,10},{3,9},{4,12},{5,15},{6,14},{7,13},{8,0},{9,3},... | collective-permute-start | bytes 196616 | tf_op jit(solution)/shard_map/ppermute | solution.py:290
  8.1 1.3 %collective-permute-start.2 = (f32[2,16,512]{2,1,0:T(8,128)S(1)}, f32[2,16,512]{2,1,0:T(8,128)S(1)}, u32[]{:S(2)}, u32[]{:S(2)}) collective-permute-start(f32[2,16,512]{2,1,0:T(8,128)S(1)} %get-tuple-element.19), channel_id=1, source_target_pairs={{0,12},{1,15},{2,14},{3,13},{4,8},{5,11},{6,10},{7,9},{8,4},{9,7},... | collective-permute-start | bytes 196616 | tf_op jit(solution)/shard_map/ppermute | solution.py:290
  9.7 0.7 %collective-permute-start.4 = (f32[2,16,512]{2,1,0:T(8,128)S(1)}, f32[2,16,512]{2,1,0:T(8,128)S(1)}, u32[]{:S(2)}, u32[]{:S(2)}) collective-permute-start(f32[2,16,512]{2,1,0:T(8,128)S(1)} %get-tuple-element.21), channel_id=1, source_target_pairs={{0,0},{1,3},{2,2},{3,1},{4,4},{5,7},{6,6},{7,5},{8,8},{9,11},{10,1... | collective-permute-start | bytes 196616 | tf_op jit(solution)/shard_map/ppermute | solution.py:290
  10.4 0.4 %collective-permute-done.1.block_ref.refs_0_ = f32[2,16,512]{2,1,0:T(8,128)S(1)} collective-permute-done((f32[2,16,512]{2,1,0:T(8,128)S(1)}, f32[2,16,512]{2,1,0:T(8,128)S(1)}, u32[]{:S(2)}, u32[]{:S(2)}) %collective-permute-start.1) | collective-permute-done | bytes 65568 | tf_op jit(solution)/shard_map/ppermute | solution.py:290
  10.7 2.6 %collective-permute-start.5 = (f32[16,512]{1,0:T(8,128)S(1)}, f32[16,512]{1,0:T(8,128)S(1)}, u32[]{:S(2)}, u32[]{:S(2)}) collective-permute-start(f32[16,512]{1,0:T(8,128)S(1)} %second_half.4), channel_id=1, source_target_pairs={{0,1},{1,0},{2,3},{3,2},{4,5},{5,4},{6,7},{7,6},{8,9},{9,8},{10,11... | collective-permute-start | bytes 98312 | tf_op jit(solution)/shard_map/ppermute | solution.py:279
  13.4 1.4 %collective-permute-done.2.block_ref.refs_1_ = f32[2,16,512]{2,1,0:T(8,128)S(1)} collective-permute-done((f32[2,16,512]{2,1,0:T(8,128)S(1)}, f32[2,16,512]{2,1,0:T(8,128)S(1)}, u32[]{:S(2)}, u32[]{:S(2)}) %collective-permute-start.2) | collective-permute-done | bytes 65568 | tf_op jit(solution)/shard_map/ppermute | solution.py:290
  14.8 0.5 %collective-permute-start.6 = (f32[16,512]{1,0:T(8,128)S(1)}, f32[16,512]{1,0:T(8,128)S(1)}, u32[]{:S(2)}, u32[]{:S(2)}) collective-permute-start(f32[16,512]{1,0:T(8,128)S(1)} %second_half.5), channel_id=1, source_target_pairs={{0,1},{1,0},{2,3},{3,2},{4,5},{5,4},{6,7},{7,6},{8,9},{9,8},{10,11... | collective-permute-start | bytes 98312 | tf_op jit(solution)/shard_map/ppermute | solution.py:279
  15.8 0.4 %collective-permute-start.8 = (f32[16,512]{1,0:T(8,128)S(1)}, f32[16,512]{1,0:T(8,128)S(1)}, u32[]{:S(2)}, u32[]{:S(2)}) collective-permute-start(f32[16,512]{1,0:T(8,128)S(1)} %second_half.7), channel_id=1, source_target_pairs={{0,1},{1,0},{2,3},{3,2},{4,5},{5,4},{6,7},{7,6},{8,9},{9,8},{10,11... | collective-permute-start | bytes 98312 | tf_op jit(solution)/shard_map/ppermute | solution.py:279
  16.2 0.6 %collective-permute-done.7.refs_6_ = f32[16,512]{1,0:T(8,128)S(1)} collective-permute-done((f32[16,512]{1,0:T(8,128)S(1)}, f32[16,512]{1,0:T(8,128)S(1)}, u32[]{:S(2)}, u32[]{:S(2)}) %collective-permute-start.7) | collective-permute-done | bytes 32800 | tf_op jit(solution)/shard_map/ppermute | solution.py:279
  17.2 1.1 %mix.1 = (f32[128,512]{1,0:T(8,128)S(1)}, f32[4,16,512]{2,1,0:T(8,128)S(1)}) custom-call(f32[2,16,512]{2,1,0:T(8,128)S(1)} %collective-permute-done.1.block_ref.refs_0_, f32[2,16,512]{2,1,0:T(8,128)S(1)} %collective-permute-done.2.block_ref.refs_1_, f32[2,16,512]{2,1,0:T(8,128)S(1)} %collective-permute-done.3.block_ref.refs_2_, ...), custom_call_target="tpu_custom_call" | custom-call | tf_op jit(solution)/shard_map/mix/pallas_call | solution.py:407
  18.2 0.4 %collective-permute-start.9 = (f32[4,16,512]{2,1,0:T(8,128)S(1)}, f32[4,16,512]{2,1,0:T(8,128)S(1)}, u32[]{:S(2)}, u32[]{:S(2)}) collective-permute-start(f32[4,16,512]{2,1,0:T(8,128)S(1)} %get-tuple-element.24), channel_id=1, source_target_pairs={{0,1},{1,0},{2,3},{3,2},{4,5},{5,4},{6,7},{7,6},{8,9},{9,8},{10,11... | collective-permute-start | bytes 393224 | tf_op jit(solution)/shard_map/ppermute | solution.py:279
  18.6 0.8 %keep_rows.1 = (f32[1,64,1024]{2,1,0:T(8,128)}, f32[4,16,512]{2,1,0:T(8,128)S(1)}) custom-call(f32[128,512]{1,0:T(8,128)S(1)} %get-tuple-element.22.modes_ref, bf16[2,64,128]{2,1,0:T(8,128)(2,1)S(1)} %copy-done.4, bf16[2,64,128]{2,1,0:T(8,128)(2,1)S(1)} %copy-done.3), custom_call_target="tpu_custom_call" | custom-call | tf_op jit(solution)/shard_map/keep_rows/pallas_call | solution.py:434
  19.7 3.1 %collective-permute-start.10 = (f32[4,8,512]{2,1,0:T(8,128)S(1)}, f32[4,8,512]{2,1,0:T(8,128)S(1)}, u32[]{:S(2)}, u32[]{:S(2)}) collective-permute-start(f32[4,8,512]{2,1,0:T(8,128)S(1)} %get-tuple-element.25), channel_id=1, source_target_pairs={{0,8},{1,11},{2,10},{3,9},{4,12},{5,15},{6,14},{7,13},{8,0},{9,3},... | collective-permute-start | bytes 196616 | tf_op jit(solution)/shard_map/ppermute | solution.py:290
  22.8 0.7 %collective-permute-start.11 = (f32[4,8,512]{2,1,0:T(8,128)S(1)}, f32[4,8,512]{2,1,0:T(8,128)S(1)}, u32[]{:S(2)}, u32[]{:S(2)}) collective-permute-start(f32[4,8,512]{2,1,0:T(8,128)S(1)} %get-tuple-element.26), channel_id=1, source_target_pairs={{0,12},{1,15},{2,14},{3,13},{4,8},{5,11},{6,10},{7,9},{8,4},{9,7},... | collective-permute-start | bytes 196616 | tf_op jit(solution)/shard_map/ppermute | solution.py:290
  23.5 0.3 collective-permute-start.12
  23.8 0.7 %collective-permute-start.13 = (f32[4,8,512]{2,1,0:T(8,128)S(1)}, f32[4,8,512]{2,1,0:T(8,128)S(1)}, u32[]{:S(2)}, u32[]{:S(2)}) collective-permute-start(f32[4,8,512]{2,1,0:T(8,128)S(1)} %get-tuple-element.28), channel_id=1, source_target_pairs={{0,0},{1,3},{2,2},{3,1},{4,4},{5,7},{6,6},{7,5},{8,8},{9,11},{10,1... | collective-permute-start | bytes 196616 | tf_op jit(solution)/shard_map/ppermute | solution.py:290
  24.5 2.7 %collective-permute-done.10.refs_0_ = f32[4,8,512]{2,1,0:T(8,128)S(1)} collective-permute-done((f32[4,8,512]{2,1,0:T(8,128)S(1)}, f32[4,8,512]{2,1,0:T(8,128)S(1)}, u32[]{:S(2)}, u32[]{:S(2)}) %collective-permute-start.10) | collective-permute-done | bytes 65568 | tf_op jit(solution)/shard_map/ppermute | solution.py:290
  27.2 2.4 %collective-permute-done.11.refs_1_ = f32[4,8,512]{2,1,0:T(8,128)S(1)} collective-permute-done((f32[4,8,512]{2,1,0:T(8,128)S(1)}, f32[4,8,512]{2,1,0:T(8,128)S(1)}, u32[]{:S(2)}, u32[]{:S(2)}) %collective-permute-start.11) | collective-permute-done | bytes 65568 | tf_op jit(solution)/shard_map/ppermute | solution.py:290
  30.5 0.4 %collective-permute-done.15.refs_5_ = f32[4,8,512]{2,1,0:T(8,128)S(1)} collective-permute-done((f32[4,8,512]{2,1,0:T(8,128)S(1)}, f32[4,8,512]{2,1,0:T(8,128)S(1)}, u32[]{:S(2)}, u32[]{:S(2)}) %collective-permute-start.15) | collective-permute-done | bytes 65568 | tf_op jit(solution)/shard_map/ppermute | solution.py:279
  30.9 0.4 %collective-permute-done.16.refs_6_ = f32[4,8,512]{2,1,0:T(8,128)S(1)} collective-permute-done((f32[4,8,512]{2,1,0:T(8,128)S(1)}, f32[4,8,512]{2,1,0:T(8,128)S(1)}, u32[]{:S(2)}, u32[]{:S(2)}) %collective-permute-start.16) | collective-permute-done | bytes 65568 | tf_op jit(solution)/shard_map/ppermute | solution.py:279
  31.5 2.6 %make_output.1 = bf16[4,256,512]{2,1,0:T(8,128)(2,1)} custom-call(bf16[4,256,512]{2,1,0:T(8,128)(2,1)S(1)} %copy-done, bf16[2,2,256,256]{3,2,1,0:T(8,128)(2,1)S(1)} %copy-done.2, bf16[64,64]{1,0:T(8,128)(2,1)S(1)} %copy-done.7, f32[64]{0:T(128)S(1)} %copy-done.8, f32[4,8,512]{2,1,0:T(8,128)S(1)} %collective-permute-done.10.refs_0_, ...), custom_call_target="tpu_custom_call" | custom-call | tf_op jit(solution)/shard_map/make_output/pallas_call | solution.py:506
  (40 shorter events, 2.5 us)
Async XLA Ops:
  0.6 16.5 %copy-start.1 = (bf16[1,64,64,128]{3,2,1,0:T(8,128)(2,1)S(1)}, bf16[1,64,64,128]{3,2,1,0:T(8,128)(2,1)}, u32[]{:S(2)}) copy-start(bf16[1,64,64,128]{3,2,1,0:T(8,128)(2,1)} %refs_8_.1) | copy-start | bytes 3145732
  2.4 1.7 %collective-permute-start = (f32[4,2,16,512]{3,2,1,0:T(8,128)S(1)}, f32[4,2,16,512]{3,2,1,0:T(8,128)S(1)}, u32[]{:S(2)}, u32[]{:S(2)}) collective-permute-start(f32[4,2,16,512]{3,2,1,0:T(8,128)S(1)} %get-tuple-element.17), channel_id=1, source_target_pairs={{0,1},{1,0},{2,3},{3,2},{4,5},{5,4},{6,7},{7,6},{8,9},{9,8},{10,11... | collective-permute-start | bytes 786440 | tf_op jit(solution)/shard_map/ppermute | solution.py:279
  4.1 6.6 %collective-permute-start.1 = (f32[2,16,512]{2,1,0:T(8,128)S(1)}, f32[2,16,512]{2,1,0:T(8,128)S(1)}, u32[]{:S(2)}, u32[]{:S(2)}) collective-permute-start(f32[2,16,512]{2,1,0:T(8,128)S(1)} %get-tuple-element.18), channel_id=1, source_target_pairs={{0,8},{1,11},{2,10},{3,9},{4,12},{5,15},{6,14},{7,13},{8,0},{9,3},... | collective-permute-start | bytes 196616 | tf_op jit(solution)/shard_map/ppermute | solution.py:290
  8.1 6.7 %collective-permute-start.2 = (f32[2,16,512]{2,1,0:T(8,128)S(1)}, f32[2,16,512]{2,1,0:T(8,128)S(1)}, u32[]{:S(2)}, u32[]{:S(2)}) collective-permute-start(f32[2,16,512]{2,1,0:T(8,128)S(1)} %get-tuple-element.19), channel_id=1, source_target_pairs={{0,12},{1,15},{2,14},{3,13},{4,8},{5,11},{6,10},{7,9},{8,4},{9,7},... | collective-permute-start | bytes 196616 | tf_op jit(solution)/shard_map/ppermute | solution.py:290
  9.5 6.0 %collective-permute-start.3 = (f32[2,16,512]{2,1,0:T(8,128)S(1)}, f32[2,16,512]{2,1,0:T(8,128)S(1)}, u32[]{:S(2)}, u32[]{:S(2)}) collective-permute-start(f32[2,16,512]{2,1,0:T(8,128)S(1)} %get-tuple-element.20), channel_id=1, source_target_pairs={{0,4},{1,7},{2,6},{3,5},{4,0},{5,3},{6,2},{7,1},{8,12},{9,15},{10,... | collective-permute-start | bytes 196616 | tf_op jit(solution)/shard_map/ppermute | solution.py:290
  9.7 6.1 %collective-permute-start.4 = (f32[2,16,512]{2,1,0:T(8,128)S(1)}, f32[2,16,512]{2,1,0:T(8,128)S(1)}, u32[]{:S(2)}, u32[]{:S(2)}) collective-permute-start(f32[2,16,512]{2,1,0:T(8,128)S(1)} %get-tuple-element.21), channel_id=1, source_target_pairs={{0,0},{1,3},{2,2},{3,1},{4,4},{5,7},{6,6},{7,5},{8,8},{9,11},{10,1... | collective-permute-start | bytes 196616 | tf_op jit(solution)/shard_map/ppermute | solution.py:290
  10.7 5.5 %collective-permute-start.5 = (f32[16,512]{1,0:T(8,128)S(1)}, f32[16,512]{1,0:T(8,128)S(1)}, u32[]{:S(2)}, u32[]{:S(2)}) collective-permute-start(f32[16,512]{1,0:T(8,128)S(1)} %second_half.4), channel_id=1, source_target_pairs={{0,1},{1,0},{2,3},{3,2},{4,5},{5,4},{6,7},{7,6},{8,9},{9,8},{10,11... | collective-permute-start | bytes 98312 | tf_op jit(solution)/shard_map/ppermute | solution.py:279
  14.8 1.4 %collective-permute-start.6 = (f32[16,512]{1,0:T(8,128)S(1)}, f32[16,512]{1,0:T(8,128)S(1)}, u32[]{:S(2)}, u32[]{:S(2)}) collective-permute-start(f32[16,512]{1,0:T(8,128)S(1)} %second_half.5), channel_id=1, source_target_pairs={{0,1},{1,0},{2,3},{3,2},{4,5},{5,4},{6,7},{7,6},{8,9},{9,8},{10,11... | collective-permute-start | bytes 98312 | tf_op jit(solution)/shard_map/ppermute | solution.py:279
  15.5 1.6 %copy-start.6 = (bf16[128,128]{1,0:T(8,128)(2,1)S(1)}, bf16[128,128]{1,0:T(8,128)(2,1)}, u32[]{:S(2)}) copy-start(bf16[128,128]{1,0:T(8,128)(2,1)} %constant.10.clone.refs_9_) | copy-start | bytes 98308
  15.6 1.3 %collective-permute-start.7 = (f32[16,512]{1,0:T(8,128)S(1)}, f32[16,512]{1,0:T(8,128)S(1)}, u32[]{:S(2)}, u32[]{:S(2)}) collective-permute-start(f32[16,512]{1,0:T(8,128)S(1)} %second_half.6), channel_id=1, source_target_pairs={{0,1},{1,0},{2,3},{3,2},{4,5},{5,4},{6,7},{7,6},{8,9},{9,8},{10,11... | collective-permute-start | bytes 98312 | tf_op jit(solution)/shard_map/ppermute | solution.py:279
  15.8 15.6 %copy-start = (bf16[4,256,512]{2,1,0:T(8,128)(2,1)S(1)}, bf16[4,256,512]{2,1,0:T(8,128)(2,1)}, u32[]{:S(2)}) copy-start(bf16[4,256,512]{2,1,0:T(8,128)(2,1)} %flow_ref.1) | copy-start | bytes 3145732
  15.8 1.3 %collective-permute-start.8 = (f32[16,512]{1,0:T(8,128)S(1)}, f32[16,512]{1,0:T(8,128)S(1)}, u32[]{:S(2)}, u32[]{:S(2)}) collective-permute-start(f32[16,512]{1,0:T(8,128)S(1)} %second_half.7), channel_id=1, source_target_pairs={{0,1},{1,0},{2,3},{3,2},{4,5},{5,4},{6,7},{7,6},{8,9},{9,8},{10,11... | collective-permute-start | bytes 98312 | tf_op jit(solution)/shard_map/ppermute | solution.py:279
  18.2 13.2 %copy-start.2 = (bf16[2,2,256,256]{3,2,1,0:T(8,128)(2,1)S(1)}, bf16[2,2,256,256]{3,2,1,0:T(8,128)(2,1)}, u32[]{:S(2)}) copy-start(bf16[2,2,256,256]{3,2,1,0:T(8,128)(2,1)} %constant.14.clone.table_ref) | copy-start | bytes 1572868
  18.2 1.4 %collective-permute-start.9 = (f32[4,16,512]{2,1,0:T(8,128)S(1)}, f32[4,16,512]{2,1,0:T(8,128)S(1)}, u32[]{:S(2)}, u32[]{:S(2)}) collective-permute-start(f32[4,16,512]{2,1,0:T(8,128)S(1)} %get-tuple-element.24), channel_id=1, source_target_pairs={{0,1},{1,0},{2,3},{3,2},{4,5},{5,4},{6,7},{7,6},{8,9},{9,8},{10,11... | collective-permute-start | bytes 393224 | tf_op jit(solution)/shard_map/ppermute | solution.py:279
  19.6 11.8 %copy-start.7 = (bf16[64,64]{1,0:T(8,128)(2,1)S(1)}, bf16[64,64]{1,0:T(8,128)(2,1)}, u32[]{:S(2)}) copy-start(bf16[64,64]{1,0:T(8,128)(2,1)} %local_ref.1) | copy-start | bytes 24580
  19.7 7.5 %collective-permute-start.10 = (f32[4,8,512]{2,1,0:T(8,128)S(1)}, f32[4,8,512]{2,1,0:T(8,128)S(1)}, u32[]{:S(2)}, u32[]{:S(2)}) collective-permute-start(f32[4,8,512]{2,1,0:T(8,128)S(1)} %get-tuple-element.25), channel_id=1, source_target_pairs={{0,8},{1,11},{2,10},{3,9},{4,12},{5,15},{6,14},{7,13},{8,0},{9,3},... | collective-permute-start | bytes 196616 | tf_op jit(solution)/shard_map/ppermute | solution.py:290
  22.8 6.8 %collective-permute-start.11 = (f32[4,8,512]{2,1,0:T(8,128)S(1)}, f32[4,8,512]{2,1,0:T(8,128)S(1)}, u32[]{:S(2)}, u32[]{:S(2)}) collective-permute-start(f32[4,8,512]{2,1,0:T(8,128)S(1)} %get-tuple-element.26), channel_id=1, source_target_pairs={{0,12},{1,15},{2,14},{3,13},{4,8},{5,11},{6,10},{7,9},{8,4},{9,7},... | collective-permute-start | bytes 196616 | tf_op jit(solution)/shard_map/ppermute | solution.py:290
  23.5 8.0 %copy-start.8 = (f32[64]{0:T(128)S(1)}, f32[64]{0:T(128)}, u32[]{:S(2)}) copy-start(f32[64]{0:T(128)} %bias_ref.1) | copy-start | bytes 772
  23.5 6.5 %collective-permute-start.12 = (f32[4,8,512]{2,1,0:T(8,128)S(1)}, f32[4,8,512]{2,1,0:T(8,128)S(1)}, u32[]{:S(2)}, u32[]{:S(2)}) collective-permute-start(f32[4,8,512]{2,1,0:T(8,128)S(1)} %get-tuple-element.27), channel_id=1, source_target_pairs={{0,4},{1,7},{2,6},{3,5},{4,0},{5,3},{6,2},{7,1},{8,12},{9,15},{10,... | collective-permute-start | bytes 196616 | tf_op jit(solution)/shard_map/ppermute | solution.py:290
  23.8 6.4 %collective-permute-start.13 = (f32[4,8,512]{2,1,0:T(8,128)S(1)}, f32[4,8,512]{2,1,0:T(8,128)S(1)}, u32[]{:S(2)}, u32[]{:S(2)}) collective-permute-start(f32[4,8,512]{2,1,0:T(8,128)S(1)} %get-tuple-element.28), channel_id=1, source_target_pairs={{0,0},{1,3},{2,2},{3,1},{4,4},{5,7},{6,6},{7,5},{8,8},{9,11},{10,1... | collective-permute-start | bytes 196616 | tf_op jit(solution)/shard_map/ppermute | solution.py:290
  27.2 3.3 %collective-permute-start.14 = (f32[4,8,512]{2,1,0:T(8,128)S(1)}, f32[4,8,512]{2,1,0:T(8,128)S(1)}, u32[]{:S(2)}, u32[]{:S(2)}) collective-permute-start(f32[4,8,512]{2,1,0:T(8,128)S(1)} %collective-permute-done.10.refs_0_), channel_id=1, source_target_pairs={{0,1},{1,0},{2,3},{3,2},{4,5},{5,4},{6,7},{7,6},{8,9},{9,8},{10,11... | collective-permute-start | bytes 196616 | tf_op jit(solution)/shard_map/ppermute | solution.py:279
  29.6 1.3 %collective-permute-start.15 = (f32[4,8,512]{2,1,0:T(8,128)S(1)}, f32[4,8,512]{2,1,0:T(8,128)S(1)}, u32[]{:S(2)}, u32[]{:S(2)}) collective-permute-start(f32[4,8,512]{2,1,0:T(8,128)S(1)} %collective-permute-done.11.refs_1_), channel_id=1, source_target_pairs={{0,1},{1,0},{2,3},{3,2},{4,5},{5,4},{6,7},{7,6},{8,9},{9,8},{10,11... | collective-permute-start | bytes 196616 | tf_op jit(solution)/shard_map/ppermute | solution.py:279
  30.0 1.3 %collective-permute-start.16 = (f32[4,8,512]{2,1,0:T(8,128)S(1)}, f32[4,8,512]{2,1,0:T(8,128)S(1)}, u32[]{:S(2)}, u32[]{:S(2)}) collective-permute-start(f32[4,8,512]{2,1,0:T(8,128)S(1)} %collective-permute-done.12.refs_2_), channel_id=1, source_target_pairs={{0,1},{1,0},{2,3},{3,2},{4,5},{5,4},{6,7},{7,6},{8,9},{9,8},{10,11... | collective-permute-start | bytes 196616 | tf_op jit(solution)/shard_map/ppermute | solution.py:279
  30.2 1.3 %collective-permute-start.17 = (f32[4,8,512]{2,1,0:T(8,128)S(1)}, f32[4,8,512]{2,1,0:T(8,128)S(1)}, u32[]{:S(2)}, u32[]{:S(2)}) collective-permute-start(f32[4,8,512]{2,1,0:T(8,128)S(1)} %collective-permute-done.13.refs_3_), channel_id=1, source_target_pairs={{0,1},{1,0},{2,3},{3,2},{4,5},{5,4},{6,7},{7,6},{8,9},{9,8},{10,11... | collective-permute-start | bytes 196616 | tf_op jit(solution)/shard_map/ppermute | solution.py:279
  (3 other events, 4.8 us)

commit v18 on v16

--- a/solution.py
+++ b/solution.py
@@ -132,13 +132,12 @@
 BIAS_TERMS = 3
 FIRST = 64
 GELU_TERMS = (
-    0.7978849411010742,
-    0.03633308410644531,
-    -3.259492223151028e-05,
-    -5.530622001970187e-05,
-    3.964749794249656e-06,
-    -1.3226382122866198e-07,
-    1.7561855303327434e-09,
+    1.5957645177841187,
+    0.29075613617897034,
+    -0.0014313592109829187,
+    -0.006452994421124458,
+    0.0015898864949122071,
+    -0.0001365363277727738,
 )
 
 
@@ -195,7 +194,7 @@
         out[:, row, 1, 1, row, :] = cosine
         out[:, row, 1, 0, row, :] = sine
     out = out.reshape(peers // 2, 2, cells_x * rows_ky * 2, 2 * rows_ky * MX)
-    return np.moveaxis(out, 1, 0).reshape(2, -1, 2 * rows_ky * MX)
+    return np.moveaxis(out, 1, 0)
 
 
 def inverse_y_table(cells_y, groups_y, peers, rows_ky):
@@ -225,6 +224,10 @@
     return jnp.dot(left, right, preferred_element_type=jnp.float32)
 
 
+def column_of(turn, x, y):
+    return x ^ y ^ (1 if turn == 0 else 0)
+
+
 def forward_y_table(shape, extent, layers, rows_ky):
     z, x, y = quad()
     peers = 2 * layers
@@ -233,7 +236,8 @@
     place = block // 2 % layers
     turn = jnp.where(place < layers // 2, place + layers // 2, layers - 1 - place)
     side = y ^ (1 - block // peers)
-    owner = (side ^ (block % 2)) * peers + (z ^ turn) * 2 + (x ^ side)
+    column = x ^ side ^ jnp.where(turn == 0, 1, 0)
+    owner = (side ^ (block % 2)) * peers + (z ^ turn) * 2 + column
     index = owner * rows_ky + row // 2 % rows_ky
     y_places = lax.broadcasted_iota(jnp.int32, (1, shape[1]), 1) + y * shape[1]
     steps = (wave_number(index, MY) * y_places) & (extent - 1)
@@ -283,7 +287,7 @@
     arrived = []
     for turn, block in zip(turns(len(blocks)), blocks):
         pairs = [
-            (2 * place + core, 2 * (place ^ (2 * turn + core)) + core)
+            (2 * place + core, 2 * (place ^ (2 * turn + column_of(turn, 0, core))) + core)
             for place in range(peers)
             for core in range(2)
         ]
@@ -295,13 +299,24 @@
     return pl.pallas_call(kernel, out_shape=out_shape, compiler_params=SMALL, name=name)
 
 
-def second_kernel(block_ref, out_ref):
-    out_ref[...] = block_ref[1]
-
-
-def second_half(block):
-    shape = jax.ShapeDtypeStruct(block.shape[1:], block.dtype)
-    return small_call(second_kernel, shape, "second_half")(block)
+def second_kernel(*refs):
+    for index, block_ref in enumerate(refs[:-1]):
+        refs[-1][index] = block_ref[1]
+
+
+def second_halves(blocks):
+    shape = jax.ShapeDtypeStruct((len(blocks),) + blocks[0].shape[1:], blocks[0].dtype)
+    return small_call(second_kernel, shape, "second_halves")(*blocks)
+
+
+def stack_kernel(*refs):
+    for index, block_ref in enumerate(refs[:-1]):
+        refs[-1][index] = block_ref[...]
+
+
+def stack_blocks(blocks):
+    shape = jax.ShapeDtypeStruct((len(blocks),) + blocks[0].shape, blocks[0].dtype)
+    return small_call(stack_kernel, shape, "stack_blocks")(*blocks)
 
 
 def add_kernel(keep_ref, arrived_ref, *out_refs):
@@ -331,28 +346,29 @@
     return small_call(join_kernel, [shape] * layers, "join_blocks")(keep, arrived)
 
 
-def back_rows(inverse_high, inverse_low, column, modes):
+def back_rows(inverse_high, inverse_low, modes, shape, other):
+    z, x, y = quad()
+    places = [(column_of(turn, x, y) ^ other, z ^ turn) for turn in turns(shape[0])]
+    table_high, table_low = [
+        jnp.concatenate([ref[column, place] for column, place in places], axis=0)
+        for ref in (inverse_high, inverse_low)
+    ]
     high, low = split_terms(modes)
-    table = inverse_high[column]
-    return dot(table, high) + dot(table, low) + dot(inverse_low[column], high)
-
-
-def store_turns(out_ref, order_ref, z):
-    for index, turn in enumerate(turns(out_ref.shape[0])):
-        out_ref[index] = order_ref[z ^ turn]
+    back = dot(table_high, high) + dot(table_high, low) + dot(table_low, high)
+    return back.reshape(shape)
 
 
 def mix_kernel(layers, *refs):
-    block_refs, arrived_refs = refs[:layers], refs[layers : 2 * layers]
+    block_refs, arrived_ref = refs[:layers], refs[layers]
     weight_ref, forward_high, forward_low, inverse_high, inverse_low = refs[
-        2 * layers : 2 * layers + 5
+        layers + 1 : layers + 6
     ]
-    modes_ref, send_ref, order_ref, spread_ref, result_ref = refs[2 * layers + 5 :]
+    modes_ref, send_ref, order_ref, spread_ref, result_ref = refs[layers + 6 :]
     z, x, y = quad()
-    column = x ^ y
     for index, turn in enumerate(turns(layers)):
+        column = column_of(turn, x, y)
         order_ref[(z ^ turn) * 2 + column] = block_refs[index][0]
-        order_ref[(z ^ turn) * 2 + (column ^ 1)] = arrived_refs[index][...]
+        order_ref[(z ^ turn) * 2 + (column ^ 1)] = arrived_ref[index]
     feat_count = order_ref.shape[-1]
     count = weight_ref.shape[1]
     channels = weight_ref.shape[2]
@@ -394,9 +410,7 @@
             modes_ref[part * count : (part + 1) * count, tile * 128 : (tile + 1) * 128] = (
                 result_ref[pl.ds(part * tiles + tile, count, stride=group), :]
             )
-    back = back_rows(inverse_high, inverse_low, column ^ 1, modes_ref[...])
-    order_ref[:layers] = back.reshape(send_ref.shape)
-    store_turns(send_ref, order_ref, z)
+    send_ref[...] = back_rows(inverse_high, inverse_low, modes_ref[...], send_ref.shape, 1)
 
 
 def mix(blocks, arrived, weights, forward_table, inverse_tables):
@@ -413,20 +427,17 @@
         scratch_shapes=[pltpu.VMEM((2 * layers, rows, feat_count), jnp.float32), scratch, scratch],
         compiler_params=SMALL,
         name="mix",
-    )(*blocks, *arrived, weights, *split_table(forward_table), *inverse_tables)
-
-
-def keep_kernel(modes_ref, inverse_high, inverse_low, mixed_ref, keep_ref, order_ref):
-    z, x, y = quad()
+    )(*blocks, arrived, weights, *split_table(forward_table), *inverse_tables)
+
+
+def keep_kernel(modes_ref, inverse_high, inverse_low, mixed_ref, keep_ref):
     count = mixed_ref.shape[1]
     feat_count = modes_ref.shape[1]
     for part in range(2):
         mixed_ref[0, :, part * feat_count : (part + 1) * feat_count] = modes_ref[
             part * count : (part + 1) * count
         ]
-    back = back_rows(inverse_high, inverse_low, x ^ y, modes_ref[...])
-    order_ref[...] = back.reshape(keep_ref.shape)
-    store_turns(keep_ref, order_ref, z)
+    keep_ref[...] = back_rows(inverse_high, inverse_low, modes_ref[...], keep_ref.shape, 0)
 
 
 def keep_rows(modes, inverse_tables, like):
@@ -437,32 +448,31 @@
             jax.ShapeDtypeStruct((1, rows // 2, 2 * feat_count), jnp.float32),
             jax.ShapeDtypeStruct(like.shape, jnp.float32),
         ],
-        scratch_shapes=[pltpu.VMEM(like.shape, jnp.float32)],
         compiler_params=SMALL,
         name="keep_rows",
     )(modes, *inverse_tables)
 
 
-def gelu(values):
-    square = jnp.minimum(values * values, 31.36)
+def gelu(half):
+    square = jnp.minimum(half * half, 6.25)
     inner = jnp.full_like(square, GELU_TERMS[-1])
     for term in GELU_TERMS[-2::-1]:
         inner = inner * square + term
-    half = 0.5 * values
-    return half + half * jnp.tanh(values * inner)
-
-
-def output_kernel(layers, flow_ref, table_ref, local_ref, bias_ref, *refs):
-    own_refs, core_refs = refs[:layers], refs[layers : 2 * layers]
-    out_hbm, order_ref, wide_ref, level_ref, done_ref, sent = refs[2 * layers :]
+    return half + half * jnp.tanh(half * inner)
+
+
+def output_kernel(
+    flow_ref, table_ref, local_ref, bias_ref, own_ref, core_ref,
+    out_hbm, order_ref, wide_ref, level_ref, done_ref, sent,
+):
     cells_x, cells_y, feat_count = flow_ref.shape
     channels = local_ref.shape[0]
     z, x, y = quad()
     wide_ref[...] = jnp.zeros_like(wide_ref)
     for start in range(0, WIDTH, channels):
         span = slice(start, start + channels)
-        wide_ref[span, span] = local_ref[...]
-        level_ref[:, span] = bias_ref[...].reshape(1, channels)
+        wide_ref[span, span] = local_ref[...] * 0.5
+        level_ref[:, span] = bias_ref[...].reshape(1, channels) * 0.5
     level = level_ref[...]
     levels = []
     for _ in range(BIAS_TERMS):
@@ -472,9 +482,14 @@
     filled = jnp.zeros((table_ref.shape[-1] - terms - BIAS_TERMS, WIDTH), jnp.float32)
     below = jnp.concatenate(levels + [filled], axis=0).astype(jnp.bfloat16)
     below = jnp.concatenate([below, wide_ref[...]], axis=0)
-    for column, block_refs in ((x ^ y, own_refs), (x ^ y ^ 1, core_refs)):
-        for turn, block_ref in zip(turns(layers), block_refs):
-            order_ref[:, (z ^ turn) * 2 + column] = block_ref[...]
+    for index, turn in enumerate(turns(own_ref.shape[0])):
+        column = column_of(turn, x, y)
+        for peer, ref in ((column, own_ref), (column ^ 1, core_ref)):
+            block = ref[index]
+            if turn == 0:
+                rows = block.shape[1] // 2
+                block = jnp.concatenate([block[:, rows:], block[:, :rows]], axis=1)
+            order_ref[:, (z ^ turn) * 2 + peer] = block
     table = table_ref[y, x ^ y]
     copies = []
     for cell in range(cells_x):
@@ -500,14 +515,13 @@
         copy.wait()
 
 
-def make_output(flow_field, parts, table, local, bias):
+def make_output(flow_field, own, core, table, local, bias):
     cells_x, _, feat_count = flow_field.shape
-    layers = len(parts) // 2
     return pl.pallas_call(
-        functools.partial(output_kernel, layers),
+        output_kernel,
         out_specs=pl.BlockSpec(memory_space=pl.ANY),
         scratch_shapes=[
-            pltpu.VMEM((cells_x, 2 * layers) + parts[0].shape[1:], jnp.float32),
+            pltpu.VMEM((cells_x, 2 * own.shape[0]) + own.shape[2:], jnp.float32),
             pltpu.VMEM((WIDTH, WIDTH), jnp.bfloat16),
             pltpu.VMEM((1, WIDTH), jnp.float32),
             pltpu.VMEM(flow_field.shape, jnp.bfloat16),
@@ -516,7 +530,7 @@
         out_shape=jax.ShapeDtypeStruct(flow_field.shape, jnp.bfloat16),
         compiler_params=SMALL,
         name="make_output",
-    )(flow_field, table, local, bias, *parts)
+    )(flow_field, table, local, bias, own, core)
 
 
 def row_body(flow_field, spectral_weight, local_weight, bias_terms):
@@ -532,7 +546,7 @@
     inverse_tables = split_table(inverse_x_table(cells_x, peers, rows_ky))
     modes, send = mix(
         blocks,
-        [flip_core(second_half(block)) for block in blocks],
+        flip_core(second_halves(blocks)),
         spectral_weight,
         forward_x_table(cells_x, peers, rows_ky) * forward_scale,
         inverse_tables,
@@ -540,9 +554,9 @@
     arrived = flip_core(send)
     mixed, keep = keep_rows(modes, inverse_tables, send)
     own = along_columns(join_blocks(keep, arrived, cells_x), peers)
-    parts = own + [flip_core(block) for block in own]
-    table = output_table(inverse_y_table(cells_y, groups_y, peers, rows_ky) * inverse_scale)
-    return make_output(flow_field, parts, table, local_weight, bias_terms), mixed
+    own = stack_blocks(own)
+    table = output_table(inverse_y_table(cells_y, groups_y, peers, rows_ky) * (0.5 * inverse_scale))
+    return make_output(flow_field, own, flip_core(own), table, local_weight, bias_terms), mixed
 
 
 def body(flow_field, spectral_weight, local_weight, bias_terms):

time: 34.1 us -> 35 us (1.026)
  starting transfers between devices: 16.5 us -> 17.5 us
    ppermute x8, starting transfers between devices: 11 us -> 16.7 us  [along_columns(): arrived.append(lax.ppermute(block, ('gx', 'gy'), pairs))]
    ppermute x10 -> x4, starting transfers between devices: 5.42 us -> 0.86 us  [flip_core(): return lax.ppermute(block, 'gy', [(0, 1), (1, 0)])]
    ppermute x8, waiting for transfers between devices: 7.22 us -> 5.97 us  [along_columns(): arrived.append(lax.ppermute(block, ('gx', 'gy'), pairs))]
    ppermute x10 -> x4, waiting for transfers between devices: 3.32 us -> 4.45 us  [flip_core(): return lax.ppermute(block, 'gy', [(0, 1), (1, 0)])]
    pallas_call x5 -> x3, Pallas kernels: 2.53 us -> 2.29 us  [the longest x1 2.27 us: make_output(): pl.pallas_call(output_kernel, out_specs=pl.BlockSpec(memory_space=pl.ANY)...]
  transfers between devices with their start and end apart: 18 -> 12, of which waited for: 13 -> 10; matrix products, arithmetic and copies ran while one was open for 0% -> 0% of each run, Pallas kernels for 2% -> 2%
where the time goes in v18:
time: 35 us; the launch traced here: 34.7 us
  starting transfers between devices  17.5 us (50%)
  waiting for transfers between devices  10.4 us (30%)
  Pallas kernels  5.93 us (17%)
  between operations  0.77 us (2%)
    ppermute x8, starting transfers between devices, along_columns(): arrived.append(lax.ppermute(block, ('gx', 'gy'), pairs))  16.7 us
    ppermute x8, waiting for transfers between devices, along_columns(): arrived.append(lax.ppermute(block, ('gx', 'gy'), pairs))  5.97 us
    ppermute x4, waiting for transfers between devices, flip_core(): return lax.ppermute(block, 'gy', [(0, 1), (1, 0)])  4.45 us
    pallas_call x1, Pallas kernels, make_output(): pl.pallas_call(output_kernel, out_specs=pl.BlockSpec(memory_space=pl.ANY)...  2.27 us
    pallas_call x1, Pallas kernels, forward_y(): pl.pallas_call(functools.partial(forward_y_kernel, extent, rows_ky), in_s...  1.75 us
    pallas_call x1, Pallas kernels, mix(): pl.pallas_call(functools.partial(mix_kernel, layers), out_shape=[jax.Shap...  1.04 us
    ppermute x4, starting transfers between devices, flip_core(): return lax.ppermute(block, 'gy', [(0, 1), (1, 0)])  0.86 us
    pallas_call x1, Pallas kernels, keep_rows(): pl.pallas_call(keep_kernel, out_shape=[jax.ShapeDtypeStruct((1, rows // 2...  0.78 us
  transfers between devices with their start and end apart: 12, of which 10 were waited for; matrix products, arithmetic and copies ran while one was open for 0% of the time, Pallas kernels for 2%

profile of v18, /device:TPU:0, one launch (start us, length us, event | category | flops | bytes accessed | tf_op | source)
XLA Modules:
  0.0 34.7 jit_solution(6161940512400441576)
XLA Ops:
  0.6 1.7 %forward_y.1 = (f32[4,2,16,512]{3,2,1,0:T(8,128)S(1)}, f32[4,2,16,512]{3,2,1,0:T(8,128)S(1)}) custom-call(bf16[4,256,512]{2,1,0:T(8,128)(2,1)} %flow_ref.1), custom_call_target="tpu_custom_call" | custom-call | tf_op jit(solution)/shard_map/forward_y/pallas_call | solution.py:269
  2.4 0.5 %collective-permute-start = (f32[4,2,16,512]{3,2,1,0:T(8,128)S(1)}, f32[4,2,16,512]{3,2,1,0:T(8,128)S(1)}, u32[]{:S(2)}, u32[]{:S(2)}) collective-permute-start(f32[4,2,16,512]{3,2,1,0:T(8,128)S(1)} %get-tuple-element.17), channel_id=1, source_target_pairs={{0,1},{1,0},{2,3},{3,2},{4,5},{5,4},{6,7},{7,6},{8,9},{9,8},{10,11... | collective-permute-start | bytes 786440 | tf_op jit(solution)/shard_map/ppermute | solution.py:283
  2.9 1.2 %collective-permute-done.arrived_ref = f32[4,2,16,512]{3,2,1,0:T(8,128)S(1)} collective-permute-done((f32[4,2,16,512]{3,2,1,0:T(8,128)S(1)}, f32[4,2,16,512]{3,2,1,0:T(8,128)S(1)}, u32[]{:S(2)}, u32[]{:S(2)}) %collective-permute-start) | collective-permute-done | bytes 262176 | tf_op jit(solution)/shard_map/ppermute | solution.py:283
  4.1 4.0 %collective-permute-start.1 = (f32[2,16,512]{2,1,0:T(8,128)S(1)}, f32[2,16,512]{2,1,0:T(8,128)S(1)}, u32[]{:S(2)}, u32[]{:S(2)}) collective-permute-start(f32[2,16,512]{2,1,0:T(8,128)S(1)} %get-tuple-element.18), channel_id=1, source_target_pairs={{0,8},{1,11},{2,10},{3,9},{4,12},{5,15},{6,14},{7,13},{8,0},{9,3},... | collective-permute-start | bytes 196616 | tf_op jit(solution)/shard_map/ppermute | solution.py:294
  8.1 1.3 %collective-permute-start.2 = (f32[2,16,512]{2,1,0:T(8,128)S(1)}, f32[2,16,512]{2,1,0:T(8,128)S(1)}, u32[]{:S(2)}, u32[]{:S(2)}) collective-permute-start(f32[2,16,512]{2,1,0:T(8,128)S(1)} %get-tuple-element.19), channel_id=1, source_target_pairs={{0,12},{1,15},{2,14},{3,13},{4,8},{5,11},{6,10},{7,9},{8,4},{9,7},... | collective-permute-start | bytes 196616 | tf_op jit(solution)/shard_map/ppermute | solution.py:294
  9.5 0.2 collective-permute-start.3
  9.7 3.5 %collective-permute-start.4 = (f32[2,16,512]{2,1,0:T(8,128)S(1)}, f32[2,16,512]{2,1,0:T(8,128)S(1)}, u32[]{:S(2)}, u32[]{:S(2)}) collective-permute-start(f32[2,16,512]{2,1,0:T(8,128)S(1)} %get-tuple-element.21), channel_id=1, source_target_pairs={{0,2},{1,1},{2,0},{3,3},{4,6},{5,5},{6,4},{7,7},{8,10},{9,9},{10,8... | collective-permute-start | bytes 196616 | tf_op jit(solution)/shard_map/ppermute | solution.py:294
  13.3 1.6 %collective-permute-done.2.refs_1_ = f32[2,16,512]{2,1,0:T(8,128)S(1)} collective-permute-done((f32[2,16,512]{2,1,0:T(8,128)S(1)}, f32[2,16,512]{2,1,0:T(8,128)S(1)}, u32[]{:S(2)}, u32[]{:S(2)}) %collective-permute-start.2) | collective-permute-done | bytes 65568 | tf_op jit(solution)/shard_map/ppermute | solution.py:294
  14.8 0.7 %collective-permute-done.3.refs_2_ = f32[2,16,512]{2,1,0:T(8,128)S(1)} collective-permute-done((f32[2,16,512]{2,1,0:T(8,128)S(1)}, f32[2,16,512]{2,1,0:T(8,128)S(1)}, u32[]{:S(2)}, u32[]{:S(2)}) %collective-permute-start.3) | collective-permute-done | bytes 65568 | tf_op jit(solution)/shard_map/ppermute | solution.py:294
  15.5 0.7 %collective-permute-done.4.refs_3_ = f32[2,16,512]{2,1,0:T(8,128)S(1)} collective-permute-done((f32[2,16,512]{2,1,0:T(8,128)S(1)}, f32[2,16,512]{2,1,0:T(8,128)S(1)}, u32[]{:S(2)}, u32[]{:S(2)}) %collective-permute-start.4) | collective-permute-done | bytes 65568 | tf_op jit(solution)/shard_map/ppermute | solution.py:294
  16.3 1.3 %collective-permute-done.5.refs_4_ = f32[4,16,512]{2,1,0:T(8,128)S(1)} collective-permute-done((f32[4,16,512]{2,1,0:T(8,128)S(1)}, f32[4,16,512]{2,1,0:T(8,128)S(1)}, u32[]{:S(2)}, u32[]{:S(2)}) %collective-permute-start.5) | collective-permute-done | bytes 131104 | tf_op jit(solution)/shard_map/ppermute | solution.py:283
  17.7 1.0 %mix.1 = (f32[128,512]{1,0:T(8,128)S(1)}, f32[4,16,512]{2,1,0:T(8,128)S(1)}) custom-call(f32[2,16,512]{2,1,0:T(8,128)S(1)} %collective-permute-done.1.refs_0_, f32[2,16,512]{2,1,0:T(8,128)S(1)} %collective-permute-done.2.refs_1_, f32[2,16,512]{2,1,0:T(8,128)S(1)} %collective-permute-done.3.refs_2_, f32[2,16,512]{2,1,0:T(8,128)S(1)} %collective-permute-done.4.refs_3_, ...), custom_call_target="tpu_custom_call" | custom-call | tf_op jit(solution)/shard_map/mix/pallas_call | solution.py:421
  18.7 0.2 collective-permute-start.6
  18.9 0.8 %keep_rows.1 = (f32[1,64,1024]{2,1,0:T(8,128)}, f32[4,16,512]{2,1,0:T(8,128)S(1)}) custom-call(f32[128,512]{1,0:T(8,128)S(1)} %get-tuple-element.22.modes_ref, bf16[2,4,16,128]{3,2,1,0:T(8,128)(2,1)S(1)} %copy-done.4, bf16[2,4,16,128]{3,2,1,0:T(8,128)(2,1)S(1)} %copy-done.3), custom_call_target="tpu_custom_call" | custom-call | tf_op jit(solution)/shard_map/keep_rows/pallas_call | solution.py:445
  19.7 0.4 %collective-permute-done.6.arrived_ref = f32[4,16,512]{2,1,0:T(8,128)S(1)} collective-permute-done((f32[4,16,512]{2,1,0:T(8,128)S(1)}, f32[4,16,512]{2,1,0:T(8,128)S(1)}, u32[]{:S(2)}, u32[]{:S(2)}) %collective-permute-start.6) | collective-permute-done | bytes 131104 | tf_op jit(solution)/shard_map/ppermute | solution.py:283
  20.2 2.7 %collective-permute-start.7 = (f32[4,8,512]{2,1,0:T(8,128)S(1)}, f32[4,8,512]{2,1,0:T(8,128)S(1)}, u32[]{:S(2)}, u32[]{:S(2)}) collective-permute-start(f32[4,8,512]{2,1,0:T(8,128)S(1)} %get-tuple-element.25), channel_id=1, source_target_pairs={{0,8},{1,11},{2,10},{3,9},{4,12},{5,15},{6,14},{7,13},{8,0},{9,3},... | collective-permute-start | bytes 196616 | tf_op jit(solution)/shard_map/ppermute | solution.py:294
  22.9 1.3 %collective-permute-start.8 = (f32[4,8,512]{2,1,0:T(8,128)S(1)}, f32[4,8,512]{2,1,0:T(8,128)S(1)}, u32[]{:S(2)}, u32[]{:S(2)}) collective-permute-start(f32[4,8,512]{2,1,0:T(8,128)S(1)} %get-tuple-element.26), channel_id=1, source_target_pairs={{0,12},{1,15},{2,14},{3,13},{4,8},{5,11},{6,10},{7,9},{8,4},{9,7},... | collective-permute-start | bytes 196616 | tf_op jit(solution)/shard_map/ppermute | solution.py:294
  24.2 3.5 %collective-permute-start.10 = (f32[4,8,512]{2,1,0:T(8,128)S(1)}, f32[4,8,512]{2,1,0:T(8,128)S(1)}, u32[]{:S(2)}, u32[]{:S(2)}) collective-permute-start(f32[4,8,512]{2,1,0:T(8,128)S(1)} %get-tuple-element.28), channel_id=1, source_target_pairs={{0,2},{1,1},{2,0},{3,3},{4,6},{5,5},{6,4},{7,7},{8,10},{9,9},{10,8... | collective-permute-start | bytes 196616 | tf_op jit(solution)/shard_map/ppermute | solution.py:294
  27.8 1.9 %collective-permute-done.8.refs_1_ = f32[4,8,512]{2,1,0:T(8,128)S(1)} collective-permute-done((f32[4,8,512]{2,1,0:T(8,128)S(1)}, f32[4,8,512]{2,1,0:T(8,128)S(1)}, u32[]{:S(2)}, u32[]{:S(2)}) %collective-permute-start.8) | collective-permute-done | bytes 65568 | tf_op jit(solution)/shard_map/ppermute | solution.py:294
  29.7 0.6 %collective-permute-done.9.refs_2_ = f32[4,8,512]{2,1,0:T(8,128)S(1)} collective-permute-done((f32[4,8,512]{2,1,0:T(8,128)S(1)}, f32[4,8,512]{2,1,0:T(8,128)S(1)}, u32[]{:S(2)}, u32[]{:S(2)}) %collective-permute-start.9) | collective-permute-done | bytes 65568 | tf_op jit(solution)/shard_map/ppermute | solution.py:294
  30.3 0.5 %collective-permute-done.10.refs_3_ = f32[4,8,512]{2,1,0:T(8,128)S(1)} collective-permute-done((f32[4,8,512]{2,1,0:T(8,128)S(1)}, f32[4,8,512]{2,1,0:T(8,128)S(1)}, u32[]{:S(2)}, u32[]{:S(2)}) %collective-permute-start.10) | collective-permute-done | bytes 65568 | tf_op jit(solution)/shard_map/ppermute | solution.py:294
  30.8 0.1 collective-permute-start.11
  30.9 1.5 %collective-permute-done.11.core_ref = f32[4,4,8,512]{3,2,1,0:T(8,128)S(1)} collective-permute-done((f32[4,4,8,512]{3,2,1,0:T(8,128)S(1)}, f32[4,4,8,512]{3,2,1,0:T(8,128)S(1)}, u32[]{:S(2)}, u32[]{:S(2)}) %collective-permute-start.11) | collective-permute-done | bytes 262176 | tf_op jit(solution)/shard_map/ppermute | solution.py:283
  32.4 2.3 %make_output.1 = bf16[4,256,512]{2,1,0:T(8,128)(2,1)} custom-call(bf16[4,256,512]{2,1,0:T(8,128)(2,1)S(1)} %copy-done, bf16[2,2,256,256]{3,2,1,0:T(8,128)(2,1)S(1)} %copy-done.2, bf16[64,64]{1,0:T(8,128)(2,1)S(1)} %copy-done.7, f32[64]{0:T(128)S(1)} %copy-done.8, f32[4,4,8,512]{3,2,1,0:T(8,128)S(1)} %stack_blocks.1.own_ref, ...), custom_call_target="tpu_custom_call" | custom-call | tf_op jit(solution)/shard_map/make_output/pallas_call | solution.py:520
  (26 shorter events, 0.2 us)
Async XLA Ops:
  0.6 17.0 %copy-start.1 = (bf16[1,64,64,128]{3,2,1,0:T(8,128)(2,1)S(1)}, bf16[1,64,64,128]{3,2,1,0:T(8,128)(2,1)}, u32[]{:S(2)}) copy-start(bf16[1,64,64,128]{3,2,1,0:T(8,128)(2,1)} %refs_5_.1) | copy-start | bytes 3145732
  2.4 1.7 %collective-permute-start = (f32[4,2,16,512]{3,2,1,0:T(8,128)S(1)}, f32[4,2,16,512]{3,2,1,0:T(8,128)S(1)}, u32[]{:S(2)}, u32[]{:S(2)}) collective-permute-start(f32[4,2,16,512]{3,2,1,0:T(8,128)S(1)} %get-tuple-element.17), channel_id=1, source_target_pairs={{0,1},{1,0},{2,3},{3,2},{4,5},{5,4},{6,7},{7,6},{8,9},{9,8},{10,11... | collective-permute-start | bytes 786440 | tf_op jit(solution)/shard_map/ppermute | solution.py:283
  4.1 9.2 %collective-permute-start.1 = (f32[2,16,512]{2,1,0:T(8,128)S(1)}, f32[2,16,512]{2,1,0:T(8,128)S(1)}, u32[]{:S(2)}, u32[]{:S(2)}) collective-permute-start(f32[2,16,512]{2,1,0:T(8,128)S(1)} %get-tuple-element.18), channel_id=1, source_target_pairs={{0,8},{1,11},{2,10},{3,9},{4,12},{5,15},{6,14},{7,13},{8,0},{9,3},... | collective-permute-start | bytes 196616 | tf_op jit(solution)/shard_map/ppermute | solution.py:294
  8.1 6.7 %collective-permute-start.2 = (f32[2,16,512]{2,1,0:T(8,128)S(1)}, f32[2,16,512]{2,1,0:T(8,128)S(1)}, u32[]{:S(2)}, u32[]{:S(2)}) collective-permute-start(f32[2,16,512]{2,1,0:T(8,128)S(1)} %get-tuple-element.19), channel_id=1, source_target_pairs={{0,12},{1,15},{2,14},{3,13},{4,8},{5,11},{6,10},{7,9},{8,4},{9,7},... | collective-permute-start | bytes 196616 | tf_op jit(solution)/shard_map/ppermute | solution.py:294
  9.5 6.0 %collective-permute-start.3 = (f32[2,16,512]{2,1,0:T(8,128)S(1)}, f32[2,16,512]{2,1,0:T(8,128)S(1)}, u32[]{:S(2)}, u32[]{:S(2)}) collective-permute-start(f32[2,16,512]{2,1,0:T(8,128)S(1)} %get-tuple-element.20), channel_id=1, source_target_pairs={{0,4},{1,7},{2,6},{3,5},{4,0},{5,3},{6,2},{7,1},{8,12},{9,15},{10,... | collective-permute-start | bytes 196616 | tf_op jit(solution)/shard_map/ppermute | solution.py:294
  9.7 7.9 %copy-start.3 = (bf16[2,4,16,128]{3,2,1,0:T(8,128)(2,1)S(1)}, bf16[2,4,16,128]{3,2,1,0:T(8,128)(2,1)}, u32[]{:S(2)}) copy-start(bf16[2,4,16,128]{3,2,1,0:T(8,128)(2,1)} %constant.13.clone.refs_9_.inverse_low) | copy-start | bytes 98308
  9.7 7.9 %copy-start.4 = (bf16[2,4,16,128]{3,2,1,0:T(8,128)(2,1)S(1)}, bf16[2,4,16,128]{3,2,1,0:T(8,128)(2,1)}, u32[]{:S(2)}) copy-start(bf16[2,4,16,128]{3,2,1,0:T(8,128)(2,1)} %constant.12.clone.refs_8_.inverse_high) | copy-start | bytes 98308
  9.7 7.9 %copy-start.5 = (bf16[128,128]{1,0:T(8,128)(2,1)S(1)}, bf16[128,128]{1,0:T(8,128)(2,1)}, u32[]{:S(2)}) copy-start(bf16[128,128]{1,0:T(8,128)(2,1)} %constant.11.clone.refs_7_) | copy-start | bytes 98308
  9.7 8.0 %copy-start.6 = (bf16[128,128]{1,0:T(8,128)(2,1)S(1)}, bf16[128,128]{1,0:T(8,128)(2,1)}, u32[]{:S(2)}) copy-start(bf16[128,128]{1,0:T(8,128)(2,1)} %constant.10.clone.refs_6_) | copy-start | bytes 98308
  9.7 6.5 %collective-permute-start.4 = (f32[2,16,512]{2,1,0:T(8,128)S(1)}, f32[2,16,512]{2,1,0:T(8,128)S(1)}, u32[]{:S(2)}, u32[]{:S(2)}) collective-permute-start(f32[2,16,512]{2,1,0:T(8,128)S(1)} %get-tuple-element.21), channel_id=1, source_target_pairs={{0,2},{1,1},{2,0},{3,3},{4,6},{5,5},{6,4},{7,7},{8,10},{9,9},{10,8... | collective-permute-start | bytes 196616 | tf_op jit(solution)/shard_map/ppermute | solution.py:294
  16.2 16.2 %copy-start = (bf16[4,256,512]{2,1,0:T(8,128)(2,1)S(1)}, bf16[4,256,512]{2,1,0:T(8,128)(2,1)}, u32[]{:S(2)}) copy-start(bf16[4,256,512]{2,1,0:T(8,128)(2,1)} %flow_ref.1) | copy-start | bytes 3145732
  16.2 1.4 %collective-permute-start.5 = (f32[4,16,512]{2,1,0:T(8,128)S(1)}, f32[4,16,512]{2,1,0:T(8,128)S(1)}, u32[]{:S(2)}, u32[]{:S(2)}) collective-permute-start(f32[4,16,512]{2,1,0:T(8,128)S(1)} %second_halves.1), channel_id=1, source_target_pairs={{0,1},{1,0},{2,3},{3,2},{4,5},{5,4},{6,7},{7,6},{8,9},{9,8},{10,11... | collective-permute-start | bytes 393224 | tf_op jit(solution)/shard_map/ppermute | solution.py:283
  18.7 1.4 %collective-permute-start.6 = (f32[4,16,512]{2,1,0:T(8,128)S(1)}, f32[4,16,512]{2,1,0:T(8,128)S(1)}, u32[]{:S(2)}, u32[]{:S(2)}) collective-permute-start(f32[4,16,512]{2,1,0:T(8,128)S(1)} %get-tuple-element.24), channel_id=1, source_target_pairs={{0,1},{1,0},{2,3},{3,2},{4,5},{5,4},{6,7},{7,6},{8,9},{9,8},{10,11... | collective-permute-start | bytes 393224 | tf_op jit(solution)/shard_map/ppermute | solution.py:283
  18.9 13.5 %copy-start.2 = (bf16[2,2,256,256]{3,2,1,0:T(8,128)(2,1)S(1)}, bf16[2,2,256,256]{3,2,1,0:T(8,128)(2,1)}, u32[]{:S(2)}) copy-start(bf16[2,2,256,256]{3,2,1,0:T(8,128)(2,1)} %constant.14.clone.table_ref) | copy-start | bytes 1572868
  20.2 7.6 %collective-permute-start.7 = (f32[4,8,512]{2,1,0:T(8,128)S(1)}, f32[4,8,512]{2,1,0:T(8,128)S(1)}, u32[]{:S(2)}, u32[]{:S(2)}) collective-permute-start(f32[4,8,512]{2,1,0:T(8,128)S(1)} %get-tuple-element.25), channel_id=1, source_target_pairs={{0,8},{1,11},{2,10},{3,9},{4,12},{5,15},{6,14},{7,13},{8,0},{9,3},... | collective-permute-start | bytes 196616 | tf_op jit(solution)/shard_map/ppermute | solution.py:294
  22.9 6.8 %collective-permute-start.8 = (f32[4,8,512]{2,1,0:T(8,128)S(1)}, f32[4,8,512]{2,1,0:T(8,128)S(1)}, u32[]{:S(2)}, u32[]{:S(2)}) collective-permute-start(f32[4,8,512]{2,1,0:T(8,128)S(1)} %get-tuple-element.26), channel_id=1, source_target_pairs={{0,12},{1,15},{2,14},{3,13},{4,8},{5,11},{6,10},{7,9},{8,4},{9,7},... | collective-permute-start | bytes 196616 | tf_op jit(solution)/shard_map/ppermute | solution.py:294
  24.2 6.1 %collective-permute-start.9 = (f32[4,8,512]{2,1,0:T(8,128)S(1)}, f32[4,8,512]{2,1,0:T(8,128)S(1)}, u32[]{:S(2)}, u32[]{:S(2)}) collective-permute-start(f32[4,8,512]{2,1,0:T(8,128)S(1)} %get-tuple-element.27), channel_id=1, source_target_pairs={{0,4},{1,7},{2,6},{3,5},{4,0},{5,3},{6,2},{7,1},{8,12},{9,15},{10,... | collective-permute-start | bytes 196616 | tf_op jit(solution)/shard_map/ppermute | solution.py:294
  24.2 8.2 %copy-start.7 = (bf16[64,64]{1,0:T(8,128)(2,1)S(1)}, bf16[64,64]{1,0:T(8,128)(2,1)}, u32[]{:S(2)}) copy-start(bf16[64,64]{1,0:T(8,128)(2,1)} %local_ref.1) | copy-start | bytes 24580
  24.2 8.2 %copy-start.8 = (f32[64]{0:T(128)S(1)}, f32[64]{0:T(128)}, u32[]{:S(2)}) copy-start(f32[64]{0:T(128)} %bias_ref.1) | copy-start | bytes 772
  24.2 6.6 %collective-permute-start.10 = (f32[4,8,512]{2,1,0:T(8,128)S(1)}, f32[4,8,512]{2,1,0:T(8,128)S(1)}, u32[]{:S(2)}, u32[]{:S(2)}) collective-permute-start(f32[4,8,512]{2,1,0:T(8,128)S(1)} %get-tuple-element.28), channel_id=1, source_target_pairs={{0,2},{1,1},{2,0},{3,3},{4,6},{5,5},{6,4},{7,7},{8,10},{9,9},{10,8... | collective-permute-start | bytes 196616 | tf_op jit(solution)/shard_map/ppermute | solution.py:294
  30.8 1.6 %collective-permute-start.11 = (f32[4,4,8,512]{3,2,1,0:T(8,128)S(1)}, f32[4,4,8,512]{3,2,1,0:T(8,128)S(1)}, u32[]{:S(2)}, u32[]{:S(2)}) collective-permute-start(f32[4,4,8,512]{3,2,1,0:T(8,128)S(1)} %stack_blocks.1.own_ref), channel_id=1, source_target_pairs={{0,1},{1,0},{2,3},{3,2},{4,5},{5,4},{6,7},{7,6},{8,9},{9,8},{10,11... | collective-permute-start | bytes 786440 | tf_op jit(solution)/shard_map/ppermute | solution.py:283

commit v19 on v14

--- a/solution.py
+++ b/solution.py
@@ -131,13 +131,12 @@
 WIDTH = 256
 BIAS_TERMS = 3
 GELU_TERMS = (
-    0.7978849411010742,
-    0.03633308410644531,
-    -3.259492223151028e-05,
-    -5.530622001970187e-05,
-    3.964749794249656e-06,
-    -1.3226382122866198e-07,
-    1.7561855303327434e-09,
+    1.5957645177841187,
+    0.29075613617897034,
+    -0.0014313592109829187,
+    -0.006452994421124458,
+    0.0015898864949122071,
+    -0.0001365363277727738,
 )
 
 
@@ -166,8 +165,7 @@
 
 
 def turns(layers):
-    half = layers // 2
-    return list(range(half, layers)) + list(range(half - 1, -1, -1))
+    return list(range(1, layers)) + [0]
 
 
 def forward_x_table(cells_x, peers, rows_ky):
@@ -230,7 +228,7 @@
     row = lax.broadcasted_iota(jnp.int32, (shape[0], 1), 0)
     block = row // (2 * rows_ky)
     place = block // 2 % layers
-    turn = jnp.where(place < layers // 2, place + layers // 2, layers - 1 - place)
+    turn = (place + 1) % layers
     side = y ^ (1 - block // peers)
     owner = (side ^ (block % 2)) * peers + (z ^ turn) * 2 + (x ^ side)
     index = owner * rows_ky + row // 2 % rows_ky
@@ -442,13 +440,12 @@
     )(modes, *inverse_tables)
 
 
-def gelu(values):
-    square = jnp.minimum(values * values, 31.36)
+def gelu(half):
+    square = jnp.minimum(half * half, 6.25)
     inner = jnp.full_like(square, GELU_TERMS[-1])
     for term in GELU_TERMS[-2::-1]:
         inner = inner * square + term
-    half = 0.5 * values
-    return half + half * jnp.tanh(values * inner)
+    return half + half * jnp.tanh(half * inner)
 
 
 def output_kernel(layers, flow_ref, table_ref, local_ref, bias_ref, *refs):
@@ -460,8 +457,8 @@
     wide_ref[...] = jnp.zeros_like(wide_ref)
     for start in range(0, WIDTH, channels):
         span = slice(start, start + channels)
-        wide_ref[span, span] = local_ref[...]
-        level_ref[:, span] = bias_ref[...].reshape(1, channels)
+        wide_ref[span, span] = local_ref[...] * 0.5
+        level_ref[:, span] = bias_ref[...].reshape(1, channels) * 0.5
     level = level_ref[...]
     levels = []
     for _ in range(BIAS_TERMS):
@@ -533,7 +530,7 @@
     mixed, keep = keep_rows(modes, inverse_tables, send)
     own = along_columns(join_blocks(keep, arrived, cells_x), peers)
     parts = own + [flip_core(block) for block in own]
-    table = output_table(inverse_y_table(cells_y, groups_y, peers, rows_ky) * inverse_scale)
+    table = output_table(inverse_y_table(cells_y, groups_y, peers, rows_ky) * (0.5 * inverse_scale))
     return make_output(flow_field, parts, table, local_weight, bias_terms), mixed
 
 

time: 34.2 us -> 35.1 us (1.026)
  starting transfers between devices: 16.5 us -> 20.2 us
  waiting for transfers between devices: 10.5 us -> 7.92 us
    ppermute x10, starting transfers between devices: 5.42 us -> 8.83 us  [flip_core(): return lax.ppermute(block, 'gy', [(0, 1), (1, 0)])]
    ppermute x8, waiting for transfers between devices: 7.22 us -> 4.78 us  [along_columns(): arrived.append(lax.ppermute(block, ('gx', 'gy'), pairs))]
  transfers between devices with their start and end apart: 18 -> 18, of which waited for: 13 -> 10; matrix products, arithmetic and copies ran while one was open for 0% -> 0% of each run, Pallas kernels for 2% -> 2%
where the time goes in v19:
time: 35.1 us; the launch traced here: 34.9 us
  starting transfers between devices  20.2 us (58%)
  waiting for transfers between devices  7.92 us (23%)
  Pallas kernels  5.96 us (17%)
  between operations  0.77 us (2%)
    ppermute x8, starting transfers between devices, along_columns(): arrived.append(lax.ppermute(block, ('gx', 'gy'), pairs))  11.4 us
    ppermute x10, starting transfers between devices, flip_core(): return lax.ppermute(block, 'gy', [(0, 1), (1, 0)])  8.83 us
    ppermute x8, waiting for transfers between devices, along_columns(): arrived.append(lax.ppermute(block, ('gx', 'gy'), pairs))  4.78 us
    ppermute x10, waiting for transfers between devices, flip_core(): return lax.ppermute(block, 'gy', [(0, 1), (1, 0)])  3.15 us
    pallas_call x1, Pallas kernels, make_output(): pl.pallas_call(functools.partial(output_kernel, layers), out_specs=pl.Blo...  2.29 us
    pallas_call x1, Pallas kernels, forward_y(): pl.pallas_call(functools.partial(forward_y_kernel, extent, rows_ky), in_s...  1.75 us
    pallas_call x1, Pallas kernels, mix(): pl.pallas_call(functools.partial(mix_kernel, layers), out_shape=[jax.Shap...  1.06 us
    pallas_call x1, Pallas kernels, keep_rows(): pl.pallas_call(keep_kernel, out_shape=[jax.ShapeDtypeStruct((1, rows // 2...  0.79 us
  transfers between devices with their start and end apart: 18, of which 10 were waited for; matrix products, arithmetic and copies ran while one was open for 0% of the time, Pallas kernels for 2%

profile of v19, /device:TPU:0, one launch (start us, length us, event | category | flops | bytes accessed | tf_op | source)
XLA Modules:
  0.0 34.9 jit_solution(8659065554158278664)
XLA Ops:
  0.6 1.7 %forward_y.1 = (f32[4,2,16,512]{3,2,1,0:T(8,128)S(1)}, f32[4,2,16,512]{3,2,1,0:T(8,128)S(1)}) custom-call(bf16[4,256,512]{2,1,0:T(8,128)(2,1)} %flow_ref.1), custom_call_target="tpu_custom_call" | custom-call | tf_op jit(solution)/shard_map/forward_y/pallas_call | solution.py:262
  2.4 0.5 %collective-permute-start = (f32[4,2,16,512]{3,2,1,0:T(8,128)S(1)}, f32[4,2,16,512]{3,2,1,0:T(8,128)S(1)}, u32[]{:S(2)}, u32[]{:S(2)}) collective-permute-start(f32[4,2,16,512]{3,2,1,0:T(8,128)S(1)} %get-tuple-element.17), channel_id=1, source_target_pairs={{0,1},{1,0},{2,3},{3,2},{4,5},{5,4},{6,7},{7,6},{8,9},{9,8},{10,11... | collective-permute-start | bytes 786440 | tf_op jit(solution)/shard_map/ppermute | solution.py:276
  2.9 1.2 %collective-permute-done.arrived_ref = f32[4,2,16,512]{3,2,1,0:T(8,128)S(1)} collective-permute-done((f32[4,2,16,512]{3,2,1,0:T(8,128)S(1)}, f32[4,2,16,512]{3,2,1,0:T(8,128)S(1)}, u32[]{:S(2)}, u32[]{:S(2)}) %collective-permute-start) | collective-permute-done | bytes 262176 | tf_op jit(solution)/shard_map/ppermute | solution.py:276
  4.1 3.0 %collective-permute-start.1 = (f32[2,16,512]{2,1,0:T(8,128)S(1)}, f32[2,16,512]{2,1,0:T(8,128)S(1)}, u32[]{:S(2)}, u32[]{:S(2)}) collective-permute-start(f32[2,16,512]{2,1,0:T(8,128)S(1)} %get-tuple-element.18), channel_id=1, source_target_pairs={{0,4},{1,7},{2,6},{3,5},{4,0},{5,3},{6,2},{7,1},{8,12},{9,15},{10,... | collective-permute-start | bytes 196616 | tf_op jit(solution)/shard_map/ppermute | solution.py:287
  7.1 2.6 %collective-permute-start.2 = (f32[2,16,512]{2,1,0:T(8,128)S(1)}, f32[2,16,512]{2,1,0:T(8,128)S(1)}, u32[]{:S(2)}, u32[]{:S(2)}) collective-permute-start(f32[2,16,512]{2,1,0:T(8,128)S(1)} %get-tuple-element.19), channel_id=1, source_target_pairs={{0,8},{1,11},{2,10},{3,9},{4,12},{5,15},{6,14},{7,13},{8,0},{9,3},... | collective-permute-start | bytes 196616 | tf_op jit(solution)/shard_map/ppermute | solution.py:287
  9.7 0.7 %collective-permute-start.4 = (f32[2,16,512]{2,1,0:T(8,128)S(1)}, f32[2,16,512]{2,1,0:T(8,128)S(1)}, u32[]{:S(2)}, u32[]{:S(2)}) collective-permute-start(f32[2,16,512]{2,1,0:T(8,128)S(1)} %get-tuple-element.21), channel_id=1, source_target_pairs={{0,0},{1,3},{2,2},{3,1},{4,4},{5,7},{6,6},{7,5},{8,8},{9,11},{10,1... | collective-permute-start | bytes 196616 | tf_op jit(solution)/shard_map/ppermute | solution.py:287
  10.4 3.0 %collective-permute-start.5 = (f32[16,512]{1,0:T(8,128)S(1)}, f32[16,512]{1,0:T(8,128)S(1)}, u32[]{:S(2)}, u32[]{:S(2)}) collective-permute-start(f32[16,512]{1,0:T(8,128)S(1)} %second_half.4), channel_id=1, source_target_pairs={{0,1},{1,0},{2,3},{3,2},{4,5},{5,4},{6,7},{7,6},{8,9},{9,8},{10,11... | collective-permute-start | bytes 98312 | tf_op jit(solution)/shard_map/ppermute | solution.py:276
  13.4 0.8 %collective-permute-done.2.block_ref.refs_1_ = f32[2,16,512]{2,1,0:T(8,128)S(1)} collective-permute-done((f32[2,16,512]{2,1,0:T(8,128)S(1)}, f32[2,16,512]{2,1,0:T(8,128)S(1)}, u32[]{:S(2)}, u32[]{:S(2)}) %collective-permute-start.2) | collective-permute-done | bytes 65568 | tf_op jit(solution)/shard_map/ppermute | solution.py:287
  14.2 0.5 %collective-permute-start.6 = (f32[16,512]{1,0:T(8,128)S(1)}, f32[16,512]{1,0:T(8,128)S(1)}, u32[]{:S(2)}, u32[]{:S(2)}) collective-permute-start(f32[16,512]{1,0:T(8,128)S(1)} %second_half.5), channel_id=1, source_target_pairs={{0,1},{1,0},{2,3},{3,2},{4,5},{5,4},{6,7},{7,6},{8,9},{9,8},{10,11... | collective-permute-start | bytes 98312 | tf_op jit(solution)/shard_map/ppermute | solution.py:276
  14.8 1.5 %collective-permute-done.3.block_ref.refs_2_ = f32[2,16,512]{2,1,0:T(8,128)S(1)} collective-permute-done((f32[2,16,512]{2,1,0:T(8,128)S(1)}, f32[2,16,512]{2,1,0:T(8,128)S(1)}, u32[]{:S(2)}, u32[]{:S(2)}) %collective-permute-start.3) | collective-permute-done | bytes 65568 | tf_op jit(solution)/shard_map/ppermute | solution.py:287
  16.5 0.4 %collective-permute-start.8 = (f32[16,512]{1,0:T(8,128)S(1)}, f32[16,512]{1,0:T(8,128)S(1)}, u32[]{:S(2)}, u32[]{:S(2)}) collective-permute-start(f32[16,512]{1,0:T(8,128)S(1)} %second_half.7), channel_id=1, source_target_pairs={{0,1},{1,0},{2,3},{3,2},{4,5},{5,4},{6,7},{7,6},{8,9},{9,8},{10,11... | collective-permute-start | bytes 98312 | tf_op jit(solution)/shard_map/ppermute | solution.py:276
  16.9 0.6 %collective-permute-done.7.refs_6_ = f32[16,512]{1,0:T(8,128)S(1)} collective-permute-done((f32[16,512]{1,0:T(8,128)S(1)}, f32[16,512]{1,0:T(8,128)S(1)}, u32[]{:S(2)}, u32[]{:S(2)}) %collective-permute-start.7) | collective-permute-done | bytes 32800 | tf_op jit(solution)/shard_map/ppermute | solution.py:276
  17.8 1.1 %mix.1 = (f32[128,512]{1,0:T(8,128)S(1)}, f32[4,16,512]{2,1,0:T(8,128)S(1)}) custom-call(f32[2,16,512]{2,1,0:T(8,128)S(1)} %collective-permute-done.1.block_ref.refs_0_, f32[2,16,512]{2,1,0:T(8,128)S(1)} %collective-permute-done.2.block_ref.refs_1_, f32[2,16,512]{2,1,0:T(8,128)S(1)} %collective-permute-done.3.block_ref.refs_2_, ...), custom_call_target="tpu_custom_call" | custom-call | tf_op jit(solution)/shard_map/mix/pallas_call | solution.py:404
  18.9 0.4 %collective-permute-start.9 = (f32[4,16,512]{2,1,0:T(8,128)S(1)}, f32[4,16,512]{2,1,0:T(8,128)S(1)}, u32[]{:S(2)}, u32[]{:S(2)}) collective-permute-start(f32[4,16,512]{2,1,0:T(8,128)S(1)} %get-tuple-element.24), channel_id=1, source_target_pairs={{0,1},{1,0},{2,3},{3,2},{4,5},{5,4},{6,7},{7,6},{8,9},{9,8},{10,11... | collective-permute-start | bytes 393224 | tf_op jit(solution)/shard_map/ppermute | solution.py:276
  19.3 0.8 %keep_rows.1 = (f32[1,64,1024]{2,1,0:T(8,128)}, f32[4,16,512]{2,1,0:T(8,128)S(1)}) custom-call(f32[128,512]{1,0:T(8,128)S(1)} %get-tuple-element.22.modes_ref, bf16[2,64,128]{2,1,0:T(8,128)(2,1)S(1)} %copy-done.4, bf16[2,64,128]{2,1,0:T(8,128)(2,1)S(1)} %copy-done.3), custom_call_target="tpu_custom_call" | custom-call | tf_op jit(solution)/shard_map/keep_rows/pallas_call | solution.py:431
  20.3 1.8 %collective-permute-start.10 = (f32[4,8,512]{2,1,0:T(8,128)S(1)}, f32[4,8,512]{2,1,0:T(8,128)S(1)}, u32[]{:S(2)}, u32[]{:S(2)}) collective-permute-start(f32[4,8,512]{2,1,0:T(8,128)S(1)} %get-tuple-element.25), channel_id=1, source_target_pairs={{0,4},{1,7},{2,6},{3,5},{4,0},{5,3},{6,2},{7,1},{8,12},{9,15},{10,... | collective-permute-start | bytes 196616 | tf_op jit(solution)/shard_map/ppermute | solution.py:287
  22.1 1.6 %collective-permute-start.11 = (f32[4,8,512]{2,1,0:T(8,128)S(1)}, f32[4,8,512]{2,1,0:T(8,128)S(1)}, u32[]{:S(2)}, u32[]{:S(2)}) collective-permute-start(f32[4,8,512]{2,1,0:T(8,128)S(1)} %get-tuple-element.26), channel_id=1, source_target_pairs={{0,8},{1,11},{2,10},{3,9},{4,12},{5,15},{6,14},{7,13},{8,0},{9,3},... | collective-permute-start | bytes 196616 | tf_op jit(solution)/shard_map/ppermute | solution.py:287
  23.7 1.1 %collective-permute-start.12 = (f32[4,8,512]{2,1,0:T(8,128)S(1)}, f32[4,8,512]{2,1,0:T(8,128)S(1)}, u32[]{:S(2)}, u32[]{:S(2)}) collective-permute-start(f32[4,8,512]{2,1,0:T(8,128)S(1)} %get-tuple-element.27), channel_id=1, source_target_pairs={{0,12},{1,15},{2,14},{3,13},{4,8},{5,11},{6,10},{7,9},{8,4},{9,7},... | collective-permute-start | bytes 196616 | tf_op jit(solution)/shard_map/ppermute | solution.py:287
  24.8 0.7 %collective-permute-start.13 = (f32[4,8,512]{2,1,0:T(8,128)S(1)}, f32[4,8,512]{2,1,0:T(8,128)S(1)}, u32[]{:S(2)}, u32[]{:S(2)}) collective-permute-start(f32[4,8,512]{2,1,0:T(8,128)S(1)} %get-tuple-element.28), channel_id=1, source_target_pairs={{0,0},{1,3},{2,2},{3,1},{4,4},{5,7},{6,6},{7,5},{8,8},{9,11},{10,1... | collective-permute-start | bytes 196616 | tf_op jit(solution)/shard_map/ppermute | solution.py:287
  25.5 2.9 %collective-permute-start.14 = (f32[4,8,512]{2,1,0:T(8,128)S(1)}, f32[4,8,512]{2,1,0:T(8,128)S(1)}, u32[]{:S(2)}, u32[]{:S(2)}) collective-permute-start(f32[4,8,512]{2,1,0:T(8,128)S(1)} %collective-permute-done.10.refs_0_), channel_id=1, source_target_pairs={{0,1},{1,0},{2,3},{3,2},{4,5},{5,4},{6,7},{7,6},{8,9},{9,8},{10,11... | collective-permute-start | bytes 196616 | tf_op jit(solution)/shard_map/ppermute | solution.py:276
  28.4 2.4 %collective-permute-done.11.refs_1_ = f32[4,8,512]{2,1,0:T(8,128)S(1)} collective-permute-done((f32[4,8,512]{2,1,0:T(8,128)S(1)}, f32[4,8,512]{2,1,0:T(8,128)S(1)}, u32[]{:S(2)}, u32[]{:S(2)}) %collective-permute-start.11) | collective-permute-done | bytes 65568 | tf_op jit(solution)/shard_map/ppermute | solution.py:287
  31.7 0.4 %collective-permute-done.15.refs_5_ = f32[4,8,512]{2,1,0:T(8,128)S(1)} collective-permute-done((f32[4,8,512]{2,1,0:T(8,128)S(1)}, f32[4,8,512]{2,1,0:T(8,128)S(1)}, u32[]{:S(2)}, u32[]{:S(2)}) %collective-permute-start.15) | collective-permute-done | bytes 65568 | tf_op jit(solution)/shard_map/ppermute | solution.py:276
  32.1 0.3 collective-permute-done.16.refs_6_
  32.6 2.3 %make_output.1 = bf16[4,256,512]{2,1,0:T(8,128)(2,1)} custom-call(bf16[4,256,512]{2,1,0:T(8,128)(2,1)S(1)} %copy-done, bf16[2,2,256,256]{3,2,1,0:T(8,128)(2,1)S(1)} %copy-done.2, bf16[64,64]{1,0:T(8,128)(2,1)S(1)} %copy-done.7, f32[64]{0:T(128)S(1)} %copy-done.8, f32[4,8,512]{2,1,0:T(8,128)S(1)} %collective-permute-done.10.refs_0_, ...), custom_call_target="tpu_custom_call" | custom-call | tf_op jit(solution)/shard_map/make_output/pallas_call | solution.py:495
  (40 shorter events, 1.8 us)
Async XLA Ops:
  0.6 17.2 %copy-start.1 = (bf16[1,64,64,128]{3,2,1,0:T(8,128)(2,1)S(1)}, bf16[1,64,64,128]{3,2,1,0:T(8,128)(2,1)}, u32[]{:S(2)}) copy-start(bf16[1,64,64,128]{3,2,1,0:T(8,128)(2,1)} %refs_8_.1) | copy-start | bytes 3145732
  2.4 1.7 %collective-permute-start = (f32[4,2,16,512]{3,2,1,0:T(8,128)S(1)}, f32[4,2,16,512]{3,2,1,0:T(8,128)S(1)}, u32[]{:S(2)}, u32[]{:S(2)}) collective-permute-start(f32[4,2,16,512]{3,2,1,0:T(8,128)S(1)} %get-tuple-element.17), channel_id=1, source_target_pairs={{0,1},{1,0},{2,3},{3,2},{4,5},{5,4},{6,7},{7,6},{8,9},{9,8},{10,11... | collective-permute-start | bytes 786440 | tf_op jit(solution)/shard_map/ppermute | solution.py:276
  4.1 6.3 %collective-permute-start.1 = (f32[2,16,512]{2,1,0:T(8,128)S(1)}, f32[2,16,512]{2,1,0:T(8,128)S(1)}, u32[]{:S(2)}, u32[]{:S(2)}) collective-permute-start(f32[2,16,512]{2,1,0:T(8,128)S(1)} %get-tuple-element.18), channel_id=1, source_target_pairs={{0,4},{1,7},{2,6},{3,5},{4,0},{5,3},{6,2},{7,1},{8,12},{9,15},{10,... | collective-permute-start | bytes 196616 | tf_op jit(solution)/shard_map/ppermute | solution.py:287
  7.1 7.1 %collective-permute-start.2 = (f32[2,16,512]{2,1,0:T(8,128)S(1)}, f32[2,16,512]{2,1,0:T(8,128)S(1)}, u32[]{:S(2)}, u32[]{:S(2)}) collective-permute-start(f32[2,16,512]{2,1,0:T(8,128)S(1)} %get-tuple-element.19), channel_id=1, source_target_pairs={{0,8},{1,11},{2,10},{3,9},{4,12},{5,15},{6,14},{7,13},{8,0},{9,3},... | collective-permute-start | bytes 196616 | tf_op jit(solution)/shard_map/ppermute | solution.py:287
  9.7 6.5 %collective-permute-start.3 = (f32[2,16,512]{2,1,0:T(8,128)S(1)}, f32[2,16,512]{2,1,0:T(8,128)S(1)}, u32[]{:S(2)}, u32[]{:S(2)}) collective-permute-start(f32[2,16,512]{2,1,0:T(8,128)S(1)} %get-tuple-element.20), channel_id=1, source_target_pairs={{0,12},{1,15},{2,14},{3,13},{4,8},{5,11},{6,10},{7,9},{8,4},{9,7},... | collective-permute-start | bytes 196616 | tf_op jit(solution)/shard_map/ppermute | solution.py:287
  9.7 6.7 %collective-permute-start.4 = (f32[2,16,512]{2,1,0:T(8,128)S(1)}, f32[2,16,512]{2,1,0:T(8,128)S(1)}, u32[]{:S(2)}, u32[]{:S(2)}) collective-permute-start(f32[2,16,512]{2,1,0:T(8,128)S(1)} %get-tuple-element.21), channel_id=1, source_target_pairs={{0,0},{1,3},{2,2},{3,1},{4,4},{5,7},{6,6},{7,5},{8,8},{9,11},{10,1... | collective-permute-start | bytes 196616 | tf_op jit(solution)/shard_map/ppermute | solution.py:287
  10.4 6.5 %collective-permute-start.5 = (f32[16,512]{1,0:T(8,128)S(1)}, f32[16,512]{1,0:T(8,128)S(1)}, u32[]{:S(2)}, u32[]{:S(2)}) collective-permute-start(f32[16,512]{1,0:T(8,128)S(1)} %second_half.4), channel_id=1, source_target_pairs={{0,1},{1,0},{2,3},{3,2},{4,5},{5,4},{6,7},{7,6},{8,9},{9,8},{10,11... | collective-permute-start | bytes 98312 | tf_op jit(solution)/shard_map/ppermute | solution.py:276
  14.2 2.7 %collective-permute-start.6 = (f32[16,512]{1,0:T(8,128)S(1)}, f32[16,512]{1,0:T(8,128)S(1)}, u32[]{:S(2)}, u32[]{:S(2)}) collective-permute-start(f32[16,512]{1,0:T(8,128)S(1)} %second_half.5), channel_id=1, source_target_pairs={{0,1},{1,0},{2,3},{3,2},{4,5},{5,4},{6,7},{7,6},{8,9},{9,8},{10,11... | collective-permute-start | bytes 98312 | tf_op jit(solution)/shard_map/ppermute | solution.py:276
  16.2 1.6 %copy-start.6 = (bf16[128,128]{1,0:T(8,128)(2,1)S(1)}, bf16[128,128]{1,0:T(8,128)(2,1)}, u32[]{:S(2)}) copy-start(bf16[128,128]{1,0:T(8,128)(2,1)} %constant.10.clone.refs_9_) | copy-start | bytes 98308
  16.3 1.3 %collective-permute-start.7 = (f32[16,512]{1,0:T(8,128)S(1)}, f32[16,512]{1,0:T(8,128)S(1)}, u32[]{:S(2)}, u32[]{:S(2)}) collective-permute-start(f32[16,512]{1,0:T(8,128)S(1)} %second_half.6), channel_id=1, source_target_pairs={{0,1},{1,0},{2,3},{3,2},{4,5},{5,4},{6,7},{7,6},{8,9},{9,8},{10,11... | collective-permute-start | bytes 98312 | tf_op jit(solution)/shard_map/ppermute | solution.py:276
  16.5 16.1 %copy-start = (bf16[4,256,512]{2,1,0:T(8,128)(2,1)S(1)}, bf16[4,256,512]{2,1,0:T(8,128)(2,1)}, u32[]{:S(2)}) copy-start(bf16[4,256,512]{2,1,0:T(8,128)(2,1)} %flow_ref.1) | copy-start | bytes 3145732
  16.5 1.3 %collective-permute-start.8 = (f32[16,512]{1,0:T(8,128)S(1)}, f32[16,512]{1,0:T(8,128)S(1)}, u32[]{:S(2)}, u32[]{:S(2)}) collective-permute-start(f32[16,512]{1,0:T(8,128)S(1)} %second_half.7), channel_id=1, source_target_pairs={{0,1},{1,0},{2,3},{3,2},{4,5},{5,4},{6,7},{7,6},{8,9},{9,8},{10,11... | collective-permute-start | bytes 98312 | tf_op jit(solution)/shard_map/ppermute | solution.py:276
  18.9 13.7 %copy-start.2 = (bf16[2,2,256,256]{3,2,1,0:T(8,128)(2,1)S(1)}, bf16[2,2,256,256]{3,2,1,0:T(8,128)(2,1)}, u32[]{:S(2)}) copy-start(bf16[2,2,256,256]{3,2,1,0:T(8,128)(2,1)} %constant.14.clone.table_ref) | copy-start | bytes 1572868
  18.9 1.4 %collective-permute-start.9 = (f32[4,16,512]{2,1,0:T(8,128)S(1)}, f32[4,16,512]{2,1,0:T(8,128)S(1)}, u32[]{:S(2)}, u32[]{:S(2)}) collective-permute-start(f32[4,16,512]{2,1,0:T(8,128)S(1)} %get-tuple-element.24), channel_id=1, source_target_pairs={{0,1},{1,0},{2,3},{3,2},{4,5},{5,4},{6,7},{7,6},{8,9},{9,8},{10,11... | collective-permute-start | bytes 393224 | tf_op jit(solution)/shard_map/ppermute | solution.py:276
  20.3 12.3 %copy-start.7 = (bf16[64,64]{1,0:T(8,128)(2,1)S(1)}, bf16[64,64]{1,0:T(8,128)(2,1)}, u32[]{:S(2)}) copy-start(bf16[64,64]{1,0:T(8,128)(2,1)} %local_ref.1) | copy-start | bytes 24580
  20.3 5.1 %collective-permute-start.10 = (f32[4,8,512]{2,1,0:T(8,128)S(1)}, f32[4,8,512]{2,1,0:T(8,128)S(1)}, u32[]{:S(2)}, u32[]{:S(2)}) collective-permute-start(f32[4,8,512]{2,1,0:T(8,128)S(1)} %get-tuple-element.25), channel_id=1, source_target_pairs={{0,4},{1,7},{2,6},{3,5},{4,0},{5,3},{6,2},{7,1},{8,12},{9,15},{10,... | collective-permute-start | bytes 196616 | tf_op jit(solution)/shard_map/ppermute | solution.py:287
  22.1 8.7 %collective-permute-start.11 = (f32[4,8,512]{2,1,0:T(8,128)S(1)}, f32[4,8,512]{2,1,0:T(8,128)S(1)}, u32[]{:S(2)}, u32[]{:S(2)}) collective-permute-start(f32[4,8,512]{2,1,0:T(8,128)S(1)} %get-tuple-element.26), channel_id=1, source_target_pairs={{0,8},{1,11},{2,10},{3,9},{4,12},{5,15},{6,14},{7,13},{8,0},{9,3},... | collective-permute-start | bytes 196616 | tf_op jit(solution)/shard_map/ppermute | solution.py:287
  23.7 8.9 %copy-start.8 = (f32[64]{0:T(128)S(1)}, f32[64]{0:T(128)}, u32[]{:S(2)}) copy-start(f32[64]{0:T(128)} %bias_ref.1) | copy-start | bytes 772
  23.7 7.4 %collective-permute-start.12 = (f32[4,8,512]{2,1,0:T(8,128)S(1)}, f32[4,8,512]{2,1,0:T(8,128)S(1)}, u32[]{:S(2)}, u32[]{:S(2)}) collective-permute-start(f32[4,8,512]{2,1,0:T(8,128)S(1)} %get-tuple-element.27), channel_id=1, source_target_pairs={{0,12},{1,15},{2,14},{3,13},{4,8},{5,11},{6,10},{7,9},{8,4},{9,7},... | collective-permute-start | bytes 196616 | tf_op jit(solution)/shard_map/ppermute | solution.py:287
  24.8 6.5 %collective-permute-start.13 = (f32[4,8,512]{2,1,0:T(8,128)S(1)}, f32[4,8,512]{2,1,0:T(8,128)S(1)}, u32[]{:S(2)}, u32[]{:S(2)}) collective-permute-start(f32[4,8,512]{2,1,0:T(8,128)S(1)} %get-tuple-element.28), channel_id=1, source_target_pairs={{0,0},{1,3},{2,2},{3,1},{4,4},{5,7},{6,6},{7,5},{8,8},{9,11},{10,1... | collective-permute-start | bytes 196616 | tf_op jit(solution)/shard_map/ppermute | solution.py:287
  25.5 6.2 %collective-permute-start.14 = (f32[4,8,512]{2,1,0:T(8,128)S(1)}, f32[4,8,512]{2,1,0:T(8,128)S(1)}, u32[]{:S(2)}, u32[]{:S(2)}) collective-permute-start(f32[4,8,512]{2,1,0:T(8,128)S(1)} %collective-permute-done.10.refs_0_), channel_id=1, source_target_pairs={{0,1},{1,0},{2,3},{3,2},{4,5},{5,4},{6,7},{7,6},{8,9},{9,8},{10,11... | collective-permute-start | bytes 196616 | tf_op jit(solution)/shard_map/ppermute | solution.py:276
  30.8 1.3 %collective-permute-start.15 = (f32[4,8,512]{2,1,0:T(8,128)S(1)}, f32[4,8,512]{2,1,0:T(8,128)S(1)}, u32[]{:S(2)}, u32[]{:S(2)}) collective-permute-start(f32[4,8,512]{2,1,0:T(8,128)S(1)} %collective-permute-done.11.refs_1_), channel_id=1, source_target_pairs={{0,1},{1,0},{2,3},{3,2},{4,5},{5,4},{6,7},{7,6},{8,9},{9,8},{10,11... | collective-permute-start | bytes 196616 | tf_op jit(solution)/shard_map/ppermute | solution.py:276
  31.1 1.3 %collective-permute-start.16 = (f32[4,8,512]{2,1,0:T(8,128)S(1)}, f32[4,8,512]{2,1,0:T(8,128)S(1)}, u32[]{:S(2)}, u32[]{:S(2)}) collective-permute-start(f32[4,8,512]{2,1,0:T(8,128)S(1)} %collective-permute-done.12.refs_2_), channel_id=1, source_target_pairs={{0,1},{1,0},{2,3},{3,2},{4,5},{5,4},{6,7},{7,6},{8,9},{9,8},{10,11... | collective-permute-start | bytes 196616 | tf_op jit(solution)/shard_map/ppermute | solution.py:276
  31.3 1.3 %collective-permute-start.17 = (f32[4,8,512]{2,1,0:T(8,128)S(1)}, f32[4,8,512]{2,1,0:T(8,128)S(1)}, u32[]{:S(2)}, u32[]{:S(2)}) collective-permute-start(f32[4,8,512]{2,1,0:T(8,128)S(1)} %collective-permute-done.13.refs_3_), channel_id=1, source_target_pairs={{0,1},{1,0},{2,3},{3,2},{4,5},{5,4},{6,7},{7,6},{8,9},{9,8},{10,11... | collective-permute-start | bytes 196616 | tf_op jit(solution)/shard_map/ppermute | solution.py:276
  (3 other events, 4.6 us)

commit v20 on v19

--- a/solution.py
+++ b/solution.py
@@ -165,7 +165,7 @@
 
 
 def turns(layers):
-    return list(range(1, layers)) + [0]
+    return list(range(layers - 1, -1, -1))
 
 
 def forward_x_table(cells_x, peers, rows_ky):
@@ -228,7 +228,7 @@
     row = lax.broadcasted_iota(jnp.int32, (shape[0], 1), 0)
     block = row // (2 * rows_ky)
     place = block // 2 % layers
-    turn = (place + 1) % layers
+    turn = layers - 1 - place
     side = y ^ (1 - block // peers)
     owner = (side ^ (block % 2)) * peers + (z ^ turn) * 2 + (x ^ side)
     index = owner * rows_ky + row // 2 % rows_ky

time: 35.1 us -> 33.9 us (0.966)
  starting transfers between devices: 20.2 us -> 17 us
  waiting for transfers between devices: 7.92 us -> 9.99 us
    ppermute x10, starting transfers between devices: 8.83 us -> 5.59 us  [flip_core(): return lax.ppermute(block, 'gy', [(0, 1), (1, 0)])]
    ppermute x8, waiting for transfers between devices: 4.78 us -> 6.86 us  [along_columns(): arrived.append(lax.ppermute(block, ('gx', 'gy'), pairs))]
  transfers between devices with their start and end apart: 18 -> 18, of which waited for: 10 -> 12; matrix products, arithmetic and copies ran while one was open for 0% -> 0% of each run, Pallas kernels for 2% -> 2%
where the time goes in v20:
time: 33.9 us; the launch traced here: 33.8 us
  starting transfers between devices  17 us (50%)
  waiting for transfers between devices  9.99 us (29%)
  Pallas kernels  5.96 us (18%)
  between operations  0.76 us (2%)
    ppermute x8, starting transfers between devices, along_columns(): arrived.append(lax.ppermute(block, ('gx', 'gy'), pairs))  11.4 us
    ppermute x8, waiting for transfers between devices, along_columns(): arrived.append(lax.ppermute(block, ('gx', 'gy'), pairs))  6.86 us
    ppermute x10, starting transfers between devices, flip_core(): return lax.ppermute(block, 'gy', [(0, 1), (1, 0)])  5.59 us
    ppermute x10, waiting for transfers between devices, flip_core(): return lax.ppermute(block, 'gy', [(0, 1), (1, 0)])  3.13 us
    pallas_call x1, Pallas kernels, make_output(): pl.pallas_call(functools.partial(output_kernel, layers), out_specs=pl.Blo...  2.29 us
    pallas_call x1, Pallas kernels, forward_y(): pl.pallas_call(functools.partial(forward_y_kernel, extent, rows_ky), in_s...  1.75 us
    pallas_call x1, Pallas kernels, mix(): pl.pallas_call(functools.partial(mix_kernel, layers), out_shape=[jax.Shap...  1.06 us
    pallas_call x1, Pallas kernels, keep_rows(): pl.pallas_call(keep_kernel, out_shape=[jax.ShapeDtypeStruct((1, rows // 2...  0.79 us
  transfers between devices with their start and end apart: 18, of which 12 were waited for; matrix products, arithmetic and copies ran while one was open for 0% of the time, Pallas kernels for 2%

profile of v20, /device:TPU:0, one launch (start us, length us, event | category | flops | bytes accessed | tf_op | source)
XLA Modules:
  0.0 33.8 jit_solution(950316426813928502)
XLA Ops:
  0.6 1.7 %forward_y.1 = (f32[4,2,16,512]{3,2,1,0:T(8,128)S(1)}, f32[4,2,16,512]{3,2,1,0:T(8,128)S(1)}) custom-call(bf16[4,256,512]{2,1,0:T(8,128)(2,1)} %flow_ref.1), custom_call_target="tpu_custom_call" | custom-call | tf_op jit(solution)/shard_map/forward_y/pallas_call | solution.py:262
  2.4 0.5 %collective-permute-start = (f32[4,2,16,512]{3,2,1,0:T(8,128)S(1)}, f32[4,2,16,512]{3,2,1,0:T(8,128)S(1)}, u32[]{:S(2)}, u32[]{:S(2)}) collective-permute-start(f32[4,2,16,512]{3,2,1,0:T(8,128)S(1)} %get-tuple-element.17), channel_id=1, source_target_pairs={{0,1},{1,0},{2,3},{3,2},{4,5},{5,4},{6,7},{7,6},{8,9},{9,8},{10,11... | collective-permute-start | bytes 786440 | tf_op jit(solution)/shard_map/ppermute | solution.py:276
  2.9 1.2 %collective-permute-done.arrived_ref = f32[4,2,16,512]{3,2,1,0:T(8,128)S(1)} collective-permute-done((f32[4,2,16,512]{3,2,1,0:T(8,128)S(1)}, f32[4,2,16,512]{3,2,1,0:T(8,128)S(1)}, u32[]{:S(2)}, u32[]{:S(2)}) %collective-permute-start) | collective-permute-done | bytes 262176 | tf_op jit(solution)/shard_map/ppermute | solution.py:276
  4.1 5.0 %collective-permute-start.1 = (f32[2,16,512]{2,1,0:T(8,128)S(1)}, f32[2,16,512]{2,1,0:T(8,128)S(1)}, u32[]{:S(2)}, u32[]{:S(2)}) collective-permute-start(f32[2,16,512]{2,1,0:T(8,128)S(1)} %get-tuple-element.18), channel_id=1, source_target_pairs={{0,12},{1,15},{2,14},{3,13},{4,8},{5,11},{6,10},{7,9},{8,4},{9,7},... | collective-permute-start | bytes 196616 | tf_op jit(solution)/shard_map/ppermute | solution.py:287
  9.2 0.6 %collective-permute-start.3 = (f32[2,16,512]{2,1,0:T(8,128)S(1)}, f32[2,16,512]{2,1,0:T(8,128)S(1)}, u32[]{:S(2)}, u32[]{:S(2)}) collective-permute-start(f32[2,16,512]{2,1,0:T(8,128)S(1)} %get-tuple-element.20), channel_id=1, source_target_pairs={{0,4},{1,7},{2,6},{3,5},{4,0},{5,3},{6,2},{7,1},{8,12},{9,15},{10,... | collective-permute-start | bytes 196616 | tf_op jit(solution)/shard_map/ppermute | solution.py:287
  9.8 0.7 %collective-permute-start.4 = (f32[2,16,512]{2,1,0:T(8,128)S(1)}, f32[2,16,512]{2,1,0:T(8,128)S(1)}, u32[]{:S(2)}, u32[]{:S(2)}) collective-permute-start(f32[2,16,512]{2,1,0:T(8,128)S(1)} %get-tuple-element.21), channel_id=1, source_target_pairs={{0,0},{1,3},{2,2},{3,1},{4,4},{5,7},{6,6},{7,5},{8,8},{9,11},{10,1... | collective-permute-start | bytes 196616 | tf_op jit(solution)/shard_map/ppermute | solution.py:287
  10.4 1.4 %collective-permute-done.1.block_ref.refs_0_ = f32[2,16,512]{2,1,0:T(8,128)S(1)} collective-permute-done((f32[2,16,512]{2,1,0:T(8,128)S(1)}, f32[2,16,512]{2,1,0:T(8,128)S(1)}, u32[]{:S(2)}, u32[]{:S(2)}) %collective-permute-start.1) | collective-permute-done | bytes 65568 | tf_op jit(solution)/shard_map/ppermute | solution.py:287
  11.9 1.6 %collective-permute-start.5 = (f32[16,512]{1,0:T(8,128)S(1)}, f32[16,512]{1,0:T(8,128)S(1)}, u32[]{:S(2)}, u32[]{:S(2)}) collective-permute-start(f32[16,512]{1,0:T(8,128)S(1)} %second_half.4), channel_id=1, source_target_pairs={{0,1},{1,0},{2,3},{3,2},{4,5},{5,4},{6,7},{7,6},{8,9},{9,8},{10,11... | collective-permute-start | bytes 98312 | tf_op jit(solution)/shard_map/ppermute | solution.py:276
  13.5 2.2 %collective-permute-done.2.block_ref.refs_1_ = f32[2,16,512]{2,1,0:T(8,128)S(1)} collective-permute-done((f32[2,16,512]{2,1,0:T(8,128)S(1)}, f32[2,16,512]{2,1,0:T(8,128)S(1)}, u32[]{:S(2)}, u32[]{:S(2)}) %collective-permute-start.2) | collective-permute-done | bytes 65568 | tf_op jit(solution)/shard_map/ppermute | solution.py:287
  15.6 0.4 %collective-permute-start.6 = (f32[16,512]{1,0:T(8,128)S(1)}, f32[16,512]{1,0:T(8,128)S(1)}, u32[]{:S(2)}, u32[]{:S(2)}) collective-permute-start(f32[16,512]{1,0:T(8,128)S(1)} %second_half.5), channel_id=1, source_target_pairs={{0,1},{1,0},{2,3},{3,2},{4,5},{5,4},{6,7},{7,6},{8,9},{9,8},{10,11... | collective-permute-start | bytes 98312 | tf_op jit(solution)/shard_map/ppermute | solution.py:276
  16.3 0.4 %collective-permute-start.8 = (f32[16,512]{1,0:T(8,128)S(1)}, f32[16,512]{1,0:T(8,128)S(1)}, u32[]{:S(2)}, u32[]{:S(2)}) collective-permute-start(f32[16,512]{1,0:T(8,128)S(1)} %second_half.7), channel_id=1, source_target_pairs={{0,1},{1,0},{2,3},{3,2},{4,5},{5,4},{6,7},{7,6},{8,9},{9,8},{10,11... | collective-permute-start | bytes 98312 | tf_op jit(solution)/shard_map/ppermute | solution.py:276
  16.9 0.5 %collective-permute-done.7.refs_6_ = f32[16,512]{1,0:T(8,128)S(1)} collective-permute-done((f32[16,512]{1,0:T(8,128)S(1)}, f32[16,512]{1,0:T(8,128)S(1)}, u32[]{:S(2)}, u32[]{:S(2)}) %collective-permute-start.7) | collective-permute-done | bytes 32800 | tf_op jit(solution)/shard_map/ppermute | solution.py:276
  17.6 1.1 %mix.1 = (f32[128,512]{1,0:T(8,128)S(1)}, f32[4,16,512]{2,1,0:T(8,128)S(1)}) custom-call(f32[2,16,512]{2,1,0:T(8,128)S(1)} %collective-permute-done.1.block_ref.refs_0_, f32[2,16,512]{2,1,0:T(8,128)S(1)} %collective-permute-done.2.block_ref.refs_1_, f32[2,16,512]{2,1,0:T(8,128)S(1)} %collective-permute-done.3.block_ref.refs_2_, ...), custom_call_target="tpu_custom_call" | custom-call | tf_op jit(solution)/shard_map/mix/pallas_call | solution.py:404
  18.7 0.4 %collective-permute-start.9 = (f32[4,16,512]{2,1,0:T(8,128)S(1)}, f32[4,16,512]{2,1,0:T(8,128)S(1)}, u32[]{:S(2)}, u32[]{:S(2)}) collective-permute-start(f32[4,16,512]{2,1,0:T(8,128)S(1)} %get-tuple-element.24), channel_id=1, source_target_pairs={{0,1},{1,0},{2,3},{3,2},{4,5},{5,4},{6,7},{7,6},{8,9},{9,8},{10,11... | collective-permute-start | bytes 393224 | tf_op jit(solution)/shard_map/ppermute | solution.py:276
  19.1 0.8 %keep_rows.1 = (f32[1,64,1024]{2,1,0:T(8,128)}, f32[4,16,512]{2,1,0:T(8,128)S(1)}) custom-call(f32[128,512]{1,0:T(8,128)S(1)} %get-tuple-element.22.modes_ref, bf16[2,64,128]{2,1,0:T(8,128)(2,1)S(1)} %copy-done.4, bf16[2,64,128]{2,1,0:T(8,128)(2,1)S(1)} %copy-done.3), custom_call_target="tpu_custom_call" | custom-call | tf_op jit(solution)/shard_map/keep_rows/pallas_call | solution.py:431
  20.1 3.0 %collective-permute-start.10 = (f32[4,8,512]{2,1,0:T(8,128)S(1)}, f32[4,8,512]{2,1,0:T(8,128)S(1)}, u32[]{:S(2)}, u32[]{:S(2)}) collective-permute-start(f32[4,8,512]{2,1,0:T(8,128)S(1)} %get-tuple-element.25), channel_id=1, source_target_pairs={{0,12},{1,15},{2,14},{3,13},{4,8},{5,11},{6,10},{7,9},{8,4},{9,7},... | collective-permute-start | bytes 196616 | tf_op jit(solution)/shard_map/ppermute | solution.py:287
  23.1 1.5 %collective-permute-start.12 = (f32[4,8,512]{2,1,0:T(8,128)S(1)}, f32[4,8,512]{2,1,0:T(8,128)S(1)}, u32[]{:S(2)}, u32[]{:S(2)}) collective-permute-start(f32[4,8,512]{2,1,0:T(8,128)S(1)} %get-tuple-element.27), channel_id=1, source_target_pairs={{0,4},{1,7},{2,6},{3,5},{4,0},{5,3},{6,2},{7,1},{8,12},{9,15},{10,... | collective-permute-start | bytes 196616 | tf_op jit(solution)/shard_map/ppermute | solution.py:287
  24.6 0.7 %collective-permute-start.13 = (f32[4,8,512]{2,1,0:T(8,128)S(1)}, f32[4,8,512]{2,1,0:T(8,128)S(1)}, u32[]{:S(2)}, u32[]{:S(2)}) collective-permute-start(f32[4,8,512]{2,1,0:T(8,128)S(1)} %get-tuple-element.28), channel_id=1, source_target_pairs={{0,0},{1,3},{2,2},{3,1},{4,4},{5,7},{6,6},{7,5},{8,8},{9,11},{10,1... | collective-permute-start | bytes 196616 | tf_op jit(solution)/shard_map/ppermute | solution.py:287
  25.3 1.7 %collective-permute-done.10.refs_0_ = f32[4,8,512]{2,1,0:T(8,128)S(1)} collective-permute-done((f32[4,8,512]{2,1,0:T(8,128)S(1)}, f32[4,8,512]{2,1,0:T(8,128)S(1)}, u32[]{:S(2)}, u32[]{:S(2)}) %collective-permute-start.10) | collective-permute-done | bytes 65568 | tf_op jit(solution)/shard_map/ppermute | solution.py:287
  27.0 1.2 %collective-permute-start.14 = (f32[4,8,512]{2,1,0:T(8,128)S(1)}, f32[4,8,512]{2,1,0:T(8,128)S(1)}, u32[]{:S(2)}, u32[]{:S(2)}) collective-permute-start(f32[4,8,512]{2,1,0:T(8,128)S(1)} %collective-permute-done.10.refs_0_), channel_id=1, source_target_pairs={{0,1},{1,0},{2,3},{3,2},{4,5},{5,4},{6,7},{7,6},{8,9},{9,8},{10,11... | collective-permute-start | bytes 196616 | tf_op jit(solution)/shard_map/ppermute | solution.py:276
  28.2 1.5 %collective-permute-done.11.refs_1_ = f32[4,8,512]{2,1,0:T(8,128)S(1)} collective-permute-done((f32[4,8,512]{2,1,0:T(8,128)S(1)}, f32[4,8,512]{2,1,0:T(8,128)S(1)}, u32[]{:S(2)}, u32[]{:S(2)}) %collective-permute-start.11) | collective-permute-done | bytes 65568 | tf_op jit(solution)/shard_map/ppermute | solution.py:287
  30.2 0.3 %collective-permute-start.17 = (f32[4,8,512]{2,1,0:T(8,128)S(1)}, f32[4,8,512]{2,1,0:T(8,128)S(1)}, u32[]{:S(2)}, u32[]{:S(2)}) collective-permute-start(f32[4,8,512]{2,1,0:T(8,128)S(1)} %collective-permute-done.13.refs_3_), channel_id=1, source_target_pairs={{0,1},{1,0},{2,3},{3,2},{4,5},{5,4},{6,7},{7,6},{8,9},{9,8},{10,11... | collective-permute-start | bytes 196616 | tf_op jit(solution)/shard_map/ppermute | solution.py:276
  30.6 0.4 %collective-permute-done.15.refs_5_ = f32[4,8,512]{2,1,0:T(8,128)S(1)} collective-permute-done((f32[4,8,512]{2,1,0:T(8,128)S(1)}, f32[4,8,512]{2,1,0:T(8,128)S(1)}, u32[]{:S(2)}, u32[]{:S(2)}) %collective-permute-start.15) | collective-permute-done | bytes 65568 | tf_op jit(solution)/shard_map/ppermute | solution.py:276
  31.5 2.3 %make_output.1 = bf16[4,256,512]{2,1,0:T(8,128)(2,1)} custom-call(bf16[4,256,512]{2,1,0:T(8,128)(2,1)S(1)} %copy-done, bf16[2,2,256,256]{3,2,1,0:T(8,128)(2,1)S(1)} %copy-done.2, bf16[64,64]{1,0:T(8,128)(2,1)S(1)} %copy-done.7, f32[64]{0:T(128)S(1)} %copy-done.8, f32[4,8,512]{2,1,0:T(8,128)S(1)} %collective-permute-done.10.refs_0_, ...), custom_call_target="tpu_custom_call" | custom-call | tf_op jit(solution)/shard_map/make_output/pallas_call | solution.py:495
  (40 shorter events, 2.0 us)
Async XLA Ops:
  0.6 17.0 %copy-start.1 = (bf16[1,64,64,128]{3,2,1,0:T(8,128)(2,1)S(1)}, bf16[1,64,64,128]{3,2,1,0:T(8,128)(2,1)}, u32[]{:S(2)}) copy-start(bf16[1,64,64,128]{3,2,1,0:T(8,128)(2,1)} %refs_8_.1) | copy-start | bytes 3145732
  2.4 1.7 %collective-permute-start = (f32[4,2,16,512]{3,2,1,0:T(8,128)S(1)}, f32[4,2,16,512]{3,2,1,0:T(8,128)S(1)}, u32[]{:S(2)}, u32[]{:S(2)}) collective-permute-start(f32[4,2,16,512]{3,2,1,0:T(8,128)S(1)} %get-tuple-element.17), channel_id=1, source_target_pairs={{0,1},{1,0},{2,3},{3,2},{4,5},{5,4},{6,7},{7,6},{8,9},{9,8},{10,11... | collective-permute-start | bytes 786440 | tf_op jit(solution)/shard_map/ppermute | solution.py:276
  4.1 7.8 %collective-permute-start.1 = (f32[2,16,512]{2,1,0:T(8,128)S(1)}, f32[2,16,512]{2,1,0:T(8,128)S(1)}, u32[]{:S(2)}, u32[]{:S(2)}) collective-permute-start(f32[2,16,512]{2,1,0:T(8,128)S(1)} %get-tuple-element.18), channel_id=1, source_target_pairs={{0,12},{1,15},{2,14},{3,13},{4,8},{5,11},{6,10},{7,9},{8,4},{9,7},... | collective-permute-start | bytes 196616 | tf_op jit(solution)/shard_map/ppermute | solution.py:287
  9.1 6.5 %collective-permute-start.2 = (f32[2,16,512]{2,1,0:T(8,128)S(1)}, f32[2,16,512]{2,1,0:T(8,128)S(1)}, u32[]{:S(2)}, u32[]{:S(2)}) collective-permute-start(f32[2,16,512]{2,1,0:T(8,128)S(1)} %get-tuple-element.19), channel_id=1, source_target_pairs={{0,8},{1,11},{2,10},{3,9},{4,12},{5,15},{6,14},{7,13},{8,0},{9,3},... | collective-permute-start | bytes 196616 | tf_op jit(solution)/shard_map/ppermute | solution.py:287
  9.2 6.9 %collective-permute-start.3 = (f32[2,16,512]{2,1,0:T(8,128)S(1)}, f32[2,16,512]{2,1,0:T(8,128)S(1)}, u32[]{:S(2)}, u32[]{:S(2)}) collective-permute-start(f32[2,16,512]{2,1,0:T(8,128)S(1)} %get-tuple-element.20), channel_id=1, source_target_pairs={{0,4},{1,7},{2,6},{3,5},{4,0},{5,3},{6,2},{7,1},{8,12},{9,15},{10,... | collective-permute-start | bytes 196616 | tf_op jit(solution)/shard_map/ppermute | solution.py:287
  9.8 6.5 %collective-permute-start.4 = (f32[2,16,512]{2,1,0:T(8,128)S(1)}, f32[2,16,512]{2,1,0:T(8,128)S(1)}, u32[]{:S(2)}, u32[]{:S(2)}) collective-permute-start(f32[2,16,512]{2,1,0:T(8,128)S(1)} %get-tuple-element.21), channel_id=1, source_target_pairs={{0,0},{1,3},{2,2},{3,1},{4,4},{5,7},{6,6},{7,5},{8,8},{9,11},{10,1... | collective-permute-start | bytes 196616 | tf_op jit(solution)/shard_map/ppermute | solution.py:287
  11.9 4.8 %collective-permute-start.5 = (f32[16,512]{1,0:T(8,128)S(1)}, f32[16,512]{1,0:T(8,128)S(1)}, u32[]{:S(2)}, u32[]{:S(2)}) collective-permute-start(f32[16,512]{1,0:T(8,128)S(1)} %second_half.4), channel_id=1, source_target_pairs={{0,1},{1,0},{2,3},{3,2},{4,5},{5,4},{6,7},{7,6},{8,9},{9,8},{10,11... | collective-permute-start | bytes 98312 | tf_op jit(solution)/shard_map/ppermute | solution.py:276
  15.6 1.2 %collective-permute-start.6 = (f32[16,512]{1,0:T(8,128)S(1)}, f32[16,512]{1,0:T(8,128)S(1)}, u32[]{:S(2)}, u32[]{:S(2)}) collective-permute-start(f32[16,512]{1,0:T(8,128)S(1)} %second_half.5), channel_id=1, source_target_pairs={{0,1},{1,0},{2,3},{3,2},{4,5},{5,4},{6,7},{7,6},{8,9},{9,8},{10,11... | collective-permute-start | bytes 98312 | tf_op jit(solution)/shard_map/ppermute | solution.py:276
  16.0 1.6 %copy-start.6 = (bf16[128,128]{1,0:T(8,128)(2,1)S(1)}, bf16[128,128]{1,0:T(8,128)(2,1)}, u32[]{:S(2)}) copy-start(bf16[128,128]{1,0:T(8,128)(2,1)} %constant.10.clone.refs_9_) | copy-start | bytes 98308
  16.1 1.3 %collective-permute-start.7 = (f32[16,512]{1,0:T(8,128)S(1)}, f32[16,512]{1,0:T(8,128)S(1)}, u32[]{:S(2)}, u32[]{:S(2)}) collective-permute-start(f32[16,512]{1,0:T(8,128)S(1)} %second_half.6), channel_id=1, source_target_pairs={{0,1},{1,0},{2,3},{3,2},{4,5},{5,4},{6,7},{7,6},{8,9},{9,8},{10,11... | collective-permute-start | bytes 98312 | tf_op jit(solution)/shard_map/ppermute | solution.py:276
  16.3 15.2 %copy-start = (bf16[4,256,512]{2,1,0:T(8,128)(2,1)S(1)}, bf16[4,256,512]{2,1,0:T(8,128)(2,1)}, u32[]{:S(2)}) copy-start(bf16[4,256,512]{2,1,0:T(8,128)(2,1)} %flow_ref.1) | copy-start | bytes 3145732
  16.3 1.3 %collective-permute-start.8 = (f32[16,512]{1,0:T(8,128)S(1)}, f32[16,512]{1,0:T(8,128)S(1)}, u32[]{:S(2)}, u32[]{:S(2)}) collective-permute-start(f32[16,512]{1,0:T(8,128)S(1)} %second_half.7), channel_id=1, source_target_pairs={{0,1},{1,0},{2,3},{3,2},{4,5},{5,4},{6,7},{7,6},{8,9},{9,8},{10,11... | collective-permute-start | bytes 98312 | tf_op jit(solution)/shard_map/ppermute | solution.py:276
  18.7 12.8 %copy-start.2 = (bf16[2,2,256,256]{3,2,1,0:T(8,128)(2,1)S(1)}, bf16[2,2,256,256]{3,2,1,0:T(8,128)(2,1)}, u32[]{:S(2)}) copy-start(bf16[2,2,256,256]{3,2,1,0:T(8,128)(2,1)} %constant.14.clone.table_ref) | copy-start | bytes 1572868
  18.7 1.4 %collective-permute-start.9 = (f32[4,16,512]{2,1,0:T(8,128)S(1)}, f32[4,16,512]{2,1,0:T(8,128)S(1)}, u32[]{:S(2)}, u32[]{:S(2)}) collective-permute-start(f32[4,16,512]{2,1,0:T(8,128)S(1)} %get-tuple-element.24), channel_id=1, source_target_pairs={{0,1},{1,0},{2,3},{3,2},{4,5},{5,4},{6,7},{7,6},{8,9},{9,8},{10,11... | collective-permute-start | bytes 393224 | tf_op jit(solution)/shard_map/ppermute | solution.py:276
  20.1 11.4 %copy-start.7 = (bf16[64,64]{1,0:T(8,128)(2,1)S(1)}, bf16[64,64]{1,0:T(8,128)(2,1)}, u32[]{:S(2)}) copy-start(bf16[64,64]{1,0:T(8,128)(2,1)} %local_ref.1) | copy-start | bytes 24580
  20.1 6.8 %collective-permute-start.10 = (f32[4,8,512]{2,1,0:T(8,128)S(1)}, f32[4,8,512]{2,1,0:T(8,128)S(1)}, u32[]{:S(2)}, u32[]{:S(2)}) collective-permute-start(f32[4,8,512]{2,1,0:T(8,128)S(1)} %get-tuple-element.25), channel_id=1, source_target_pairs={{0,12},{1,15},{2,14},{3,13},{4,8},{5,11},{6,10},{7,9},{8,4},{9,7},... | collective-permute-start | bytes 196616 | tf_op jit(solution)/shard_map/ppermute | solution.py:287
  23.1 6.6 %collective-permute-start.11 = (f32[4,8,512]{2,1,0:T(8,128)S(1)}, f32[4,8,512]{2,1,0:T(8,128)S(1)}, u32[]{:S(2)}, u32[]{:S(2)}) collective-permute-start(f32[4,8,512]{2,1,0:T(8,128)S(1)} %get-tuple-element.26), channel_id=1, source_target_pairs={{0,8},{1,11},{2,10},{3,9},{4,12},{5,15},{6,14},{7,13},{8,0},{9,3},... | collective-permute-start | bytes 196616 | tf_op jit(solution)/shard_map/ppermute | solution.py:287
  23.1 8.3 %copy-start.8 = (f32[64]{0:T(128)S(1)}, f32[64]{0:T(128)}, u32[]{:S(2)}) copy-start(f32[64]{0:T(128)} %bias_ref.1) | copy-start | bytes 772
  23.1 6.7 %collective-permute-start.12 = (f32[4,8,512]{2,1,0:T(8,128)S(1)}, f32[4,8,512]{2,1,0:T(8,128)S(1)}, u32[]{:S(2)}, u32[]{:S(2)}) collective-permute-start(f32[4,8,512]{2,1,0:T(8,128)S(1)} %get-tuple-element.27), channel_id=1, source_target_pairs={{0,4},{1,7},{2,6},{3,5},{4,0},{5,3},{6,2},{7,1},{8,12},{9,15},{10,... | collective-permute-start | bytes 196616 | tf_op jit(solution)/shard_map/ppermute | solution.py:287
  24.6 5.6 %collective-permute-start.13 = (f32[4,8,512]{2,1,0:T(8,128)S(1)}, f32[4,8,512]{2,1,0:T(8,128)S(1)}, u32[]{:S(2)}, u32[]{:S(2)}) collective-permute-start(f32[4,8,512]{2,1,0:T(8,128)S(1)} %get-tuple-element.28), channel_id=1, source_target_pairs={{0,0},{1,3},{2,2},{3,1},{4,4},{5,7},{6,6},{7,5},{8,8},{9,11},{10,1... | collective-permute-start | bytes 196616 | tf_op jit(solution)/shard_map/ppermute | solution.py:287
  27.0 3.6 %collective-permute-start.14 = (f32[4,8,512]{2,1,0:T(8,128)S(1)}, f32[4,8,512]{2,1,0:T(8,128)S(1)}, u32[]{:S(2)}, u32[]{:S(2)}) collective-permute-start(f32[4,8,512]{2,1,0:T(8,128)S(1)} %collective-permute-done.10.refs_0_), channel_id=1, source_target_pairs={{0,1},{1,0},{2,3},{3,2},{4,5},{5,4},{6,7},{7,6},{8,9},{9,8},{10,11... | collective-permute-start | bytes 196616 | tf_op jit(solution)/shard_map/ppermute | solution.py:276
  29.7 1.3 %collective-permute-start.15 = (f32[4,8,512]{2,1,0:T(8,128)S(1)}, f32[4,8,512]{2,1,0:T(8,128)S(1)}, u32[]{:S(2)}, u32[]{:S(2)}) collective-permute-start(f32[4,8,512]{2,1,0:T(8,128)S(1)} %collective-permute-done.11.refs_1_), channel_id=1, source_target_pairs={{0,1},{1,0},{2,3},{3,2},{4,5},{5,4},{6,7},{7,6},{8,9},{9,8},{10,11... | collective-permute-start | bytes 196616 | tf_op jit(solution)/shard_map/ppermute | solution.py:276
  29.9 1.3 %collective-permute-start.16 = (f32[4,8,512]{2,1,0:T(8,128)S(1)}, f32[4,8,512]{2,1,0:T(8,128)S(1)}, u32[]{:S(2)}, u32[]{:S(2)}) collective-permute-start(f32[4,8,512]{2,1,0:T(8,128)S(1)} %collective-permute-done.12.refs_2_), channel_id=1, source_target_pairs={{0,1},{1,0},{2,3},{3,2},{4,5},{5,4},{6,7},{7,6},{8,9},{9,8},{10,11... | collective-permute-start | bytes 196616 | tf_op jit(solution)/shard_map/ppermute | solution.py:276
  30.2 1.3 %collective-permute-start.17 = (f32[4,8,512]{2,1,0:T(8,128)S(1)}, f32[4,8,512]{2,1,0:T(8,128)S(1)}, u32[]{:S(2)}, u32[]{:S(2)}) collective-permute-start(f32[4,8,512]{2,1,0:T(8,128)S(1)} %collective-permute-done.13.refs_3_), channel_id=1, source_target_pairs={{0,1},{1,0},{2,3},{3,2},{4,5},{5,4},{6,7},{7,6},{8,9},{9,8},{10,11... | collective-permute-start | bytes 196616 | tf_op jit(solution)/shard_map/ppermute | solution.py:276
  (3 other events, 4.6 us)

commit v21 on v20

--- a/solution.py
+++ b/solution.py
@@ -164,8 +164,11 @@
     return place // 2, place % 2, lax.axis_index("gy")
 
 
-def turns(layers):
-    return list(range(layers - 1, -1, -1))
+def turns(layers, inverse=False):
+    half = layers // 2
+    if inverse:
+        return list(range(layers - 1, -1, -1))
+    return list(range(half, layers)) + list(range(half - 1, -1, -1))
 
 
 def forward_x_table(cells_x, peers, rows_ky):
@@ -228,7 +231,7 @@
     row = lax.broadcasted_iota(jnp.int32, (shape[0], 1), 0)
     block = row // (2 * rows_ky)
     place = block // 2 % layers
-    turn = layers - 1 - place
+    turn = jnp.where(place < layers // 2, place + layers // 2, layers - 1 - place)
     side = y ^ (1 - block // peers)
     owner = (side ^ (block % 2)) * peers + (z ^ turn) * 2 + (x ^ side)
     index = owner * rows_ky + row // 2 % rows_ky
@@ -276,9 +279,9 @@
     return lax.ppermute(block, "gy", [(0, 1), (1, 0)])
 
 
-def along_columns(blocks, peers):
+def along_columns(blocks, peers, inverse=False):
     arrived = []
-    for turn, block in zip(turns(len(blocks)), blocks):
+    for turn, block in zip(turns(len(blocks), inverse), blocks):
         pairs = [
             (2 * place + core, 2 * (place ^ (2 * turn + core)) + core)
             for place in range(peers)
@@ -335,7 +338,7 @@
 
 
 def store_turns(out_ref, order_ref, z):
-    for index, turn in enumerate(turns(out_ref.shape[0])):
+    for index, turn in enumerate(turns(out_ref.shape[0], True)):
         out_ref[index] = order_ref[z ^ turn]
 
 
@@ -469,7 +472,7 @@
     below = jnp.concatenate(levels + [filled], axis=0).astype(jnp.bfloat16)
     below = jnp.concatenate([below, wide_ref[...]], axis=0)
     for column, block_refs in ((x ^ y, own_refs), (x ^ y ^ 1, core_refs)):
-        for turn, block_ref in zip(turns(layers), block_refs):
+        for turn, block_ref in zip(turns(layers, True), block_refs):
             order_ref[:, (z ^ turn) * 2 + column] = block_ref[...]
     table = table_ref[y, x ^ y]
     copies = []
@@ -528,7 +531,7 @@
     )
     arrived = flip_core(send)
     mixed, keep = keep_rows(modes, inverse_tables, send)
-    own = along_columns(join_blocks(keep, arrived, cells_x), peers)
+    own = along_columns(join_blocks(keep, arrived, cells_x), peers, True)
     parts = own + [flip_core(block) for block in own]
     table = output_table(inverse_y_table(cells_y, groups_y, peers, rows_ky) * (0.5 * inverse_scale))
     return make_output(flow_field, parts, table, local_weight, bias_terms), mixed

time: 33.9 us -> 34.1 us (level)
  starting transfers between devices: 17 us -> 18.1 us
  waiting for transfers between devices: 9.99 us -> 9.15 us
    ppermute x10, starting transfers between devices: 5.59 us -> 6.69 us  [flip_core(): return lax.ppermute(block, 'gy', [(0, 1), (1, 0)])]
    ppermute x8, waiting for transfers between devices: 6.86 us -> 5.9 us  [along_columns(): arrived.append(lax.ppermute(block, ('gx', 'gy'), pairs))]
where the time goes in v21:
time: 34.1 us; the launch traced here: 34 us
  starting transfers between devices  18.1 us (53%)
  waiting for transfers between devices  9.15 us (27%)
  Pallas kernels  5.96 us (17%)
  between operations  0.75 us (2%)
    ppermute x8, starting transfers between devices, along_columns(): arrived.append(lax.ppermute(block, ('gx', 'gy'), pairs))  11.4 us
    ppermute x10, starting transfers between devices, flip_core(): return lax.ppermute(block, 'gy', [(0, 1), (1, 0)])  6.69 us
    ppermute x8, waiting for transfers between devices, along_columns(): arrived.append(lax.ppermute(block, ('gx', 'gy'), pairs))  5.9 us
    ppermute x10, waiting for transfers between devices, flip_core(): return lax.ppermute(block, 'gy', [(0, 1), (1, 0)])  3.25 us
    pallas_call x1, Pallas kernels, make_output(): pl.pallas_call(functools.partial(output_kernel, layers), out_specs=pl.Blo...  2.29 us
    pallas_call x1, Pallas kernels, forward_y(): pl.pallas_call(functools.partial(forward_y_kernel, extent, rows_ky), in_s...  1.75 us
    pallas_call x1, Pallas kernels, mix(): pl.pallas_call(functools.partial(mix_kernel, layers), out_shape=[jax.Shap...  1.06 us
    pallas_call x1, Pallas kernels, keep_rows(): pl.pallas_call(keep_kernel, out_shape=[jax.ShapeDtypeStruct((1, rows // 2...  0.79 us
  transfers between devices with their start and end apart: 18, of which 12 were waited for; matrix products, arithmetic and copies ran while one was open for 0% of the time, Pallas kernels for 2%

profile of v21, /device:TPU:0, one launch (start us, length us, event | category | flops | bytes accessed | tf_op | source)
XLA Modules:
  0.0 34.0 jit_solution(4612334484813850717)
XLA Ops:
  0.6 1.7 %forward_y.1 = (f32[4,2,16,512]{3,2,1,0:T(8,128)S(1)}, f32[4,2,16,512]{3,2,1,0:T(8,128)S(1)}) custom-call(bf16[4,256,512]{2,1,0:T(8,128)(2,1)} %flow_ref.1), custom_call_target="tpu_custom_call" | custom-call | tf_op jit(solution)/shard_map/forward_y/pallas_call | solution.py:265
  2.4 0.5 %collective-permute-start = (f32[4,2,16,512]{3,2,1,0:T(8,128)S(1)}, f32[4,2,16,512]{3,2,1,0:T(8,128)S(1)}, u32[]{:S(2)}, u32[]{:S(2)}) collective-permute-start(f32[4,2,16,512]{3,2,1,0:T(8,128)S(1)} %get-tuple-element.17), channel_id=1, source_target_pairs={{0,1},{1,0},{2,3},{3,2},{4,5},{5,4},{6,7},{7,6},{8,9},{9,8},{10,11... | collective-permute-start | bytes 786440 | tf_op jit(solution)/shard_map/ppermute | solution.py:279
  2.9 1.2 %collective-permute-done.arrived_ref = f32[4,2,16,512]{3,2,1,0:T(8,128)S(1)} collective-permute-done((f32[4,2,16,512]{3,2,1,0:T(8,128)S(1)}, f32[4,2,16,512]{3,2,1,0:T(8,128)S(1)}, u32[]{:S(2)}, u32[]{:S(2)}) %collective-permute-start) | collective-permute-done | bytes 262176 | tf_op jit(solution)/shard_map/ppermute | solution.py:279
  4.1 4.0 %collective-permute-start.1 = (f32[2,16,512]{2,1,0:T(8,128)S(1)}, f32[2,16,512]{2,1,0:T(8,128)S(1)}, u32[]{:S(2)}, u32[]{:S(2)}) collective-permute-start(f32[2,16,512]{2,1,0:T(8,128)S(1)} %get-tuple-element.18), channel_id=1, source_target_pairs={{0,8},{1,11},{2,10},{3,9},{4,12},{5,15},{6,14},{7,13},{8,0},{9,3},... | collective-permute-start | bytes 196616 | tf_op jit(solution)/shard_map/ppermute | solution.py:290
  8.1 1.3 %collective-permute-start.2 = (f32[2,16,512]{2,1,0:T(8,128)S(1)}, f32[2,16,512]{2,1,0:T(8,128)S(1)}, u32[]{:S(2)}, u32[]{:S(2)}) collective-permute-start(f32[2,16,512]{2,1,0:T(8,128)S(1)} %get-tuple-element.19), channel_id=1, source_target_pairs={{0,12},{1,15},{2,14},{3,13},{4,8},{5,11},{6,10},{7,9},{8,4},{9,7},... | collective-permute-start | bytes 196616 | tf_op jit(solution)/shard_map/ppermute | solution.py:290
  9.7 0.7 %collective-permute-start.4 = (f32[2,16,512]{2,1,0:T(8,128)S(1)}, f32[2,16,512]{2,1,0:T(8,128)S(1)}, u32[]{:S(2)}, u32[]{:S(2)}) collective-permute-start(f32[2,16,512]{2,1,0:T(8,128)S(1)} %get-tuple-element.21), channel_id=1, source_target_pairs={{0,0},{1,3},{2,2},{3,1},{4,4},{5,7},{6,6},{7,5},{8,8},{9,11},{10,1... | collective-permute-start | bytes 196616 | tf_op jit(solution)/shard_map/ppermute | solution.py:290
  10.4 0.4 %collective-permute-done.1.block_ref.refs_0_ = f32[2,16,512]{2,1,0:T(8,128)S(1)} collective-permute-done((f32[2,16,512]{2,1,0:T(8,128)S(1)}, f32[2,16,512]{2,1,0:T(8,128)S(1)}, u32[]{:S(2)}, u32[]{:S(2)}) %collective-permute-start.1) | collective-permute-done | bytes 65568 | tf_op jit(solution)/shard_map/ppermute | solution.py:290
  10.7 2.6 %collective-permute-start.5 = (f32[16,512]{1,0:T(8,128)S(1)}, f32[16,512]{1,0:T(8,128)S(1)}, u32[]{:S(2)}, u32[]{:S(2)}) collective-permute-start(f32[16,512]{1,0:T(8,128)S(1)} %second_half.4), channel_id=1, source_target_pairs={{0,1},{1,0},{2,3},{3,2},{4,5},{5,4},{6,7},{7,6},{8,9},{9,8},{10,11... | collective-permute-start | bytes 98312 | tf_op jit(solution)/shard_map/ppermute | solution.py:279
  13.4 1.4 %collective-permute-done.2.block_ref.refs_1_ = f32[2,16,512]{2,1,0:T(8,128)S(1)} collective-permute-done((f32[2,16,512]{2,1,0:T(8,128)S(1)}, f32[2,16,512]{2,1,0:T(8,128)S(1)}, u32[]{:S(2)}, u32[]{:S(2)}) %collective-permute-start.2) | collective-permute-done | bytes 65568 | tf_op jit(solution)/shard_map/ppermute | solution.py:290
  14.8 0.5 %collective-permute-start.6 = (f32[16,512]{1,0:T(8,128)S(1)}, f32[16,512]{1,0:T(8,128)S(1)}, u32[]{:S(2)}, u32[]{:S(2)}) collective-permute-start(f32[16,512]{1,0:T(8,128)S(1)} %second_half.5), channel_id=1, source_target_pairs={{0,1},{1,0},{2,3},{3,2},{4,5},{5,4},{6,7},{7,6},{8,9},{9,8},{10,11... | collective-permute-start | bytes 98312 | tf_op jit(solution)/shard_map/ppermute | solution.py:279
  16.2 0.6 %collective-permute-done.7.refs_6_ = f32[16,512]{1,0:T(8,128)S(1)} collective-permute-done((f32[16,512]{1,0:T(8,128)S(1)}, f32[16,512]{1,0:T(8,128)S(1)}, u32[]{:S(2)}, u32[]{:S(2)}) %collective-permute-start.7) | collective-permute-done | bytes 32800 | tf_op jit(solution)/shard_map/ppermute | solution.py:279
  17.2 1.1 %mix.1 = (f32[128,512]{1,0:T(8,128)S(1)}, f32[4,16,512]{2,1,0:T(8,128)S(1)}) custom-call(f32[2,16,512]{2,1,0:T(8,128)S(1)} %collective-permute-done.1.block_ref.refs_0_, f32[2,16,512]{2,1,0:T(8,128)S(1)} %collective-permute-done.2.block_ref.refs_1_, f32[2,16,512]{2,1,0:T(8,128)S(1)} %collective-permute-done.3.block_ref.refs_2_, ...), custom_call_target="tpu_custom_call" | custom-call | tf_op jit(solution)/shard_map/mix/pallas_call | solution.py:407
  18.2 0.4 %collective-permute-start.9 = (f32[4,16,512]{2,1,0:T(8,128)S(1)}, f32[4,16,512]{2,1,0:T(8,128)S(1)}, u32[]{:S(2)}, u32[]{:S(2)}) collective-permute-start(f32[4,16,512]{2,1,0:T(8,128)S(1)} %get-tuple-element.24), channel_id=1, source_target_pairs={{0,1},{1,0},{2,3},{3,2},{4,5},{5,4},{6,7},{7,6},{8,9},{9,8},{10,11... | collective-permute-start | bytes 393224 | tf_op jit(solution)/shard_map/ppermute | solution.py:279
  18.6 0.8 %keep_rows.1 = (f32[1,64,1024]{2,1,0:T(8,128)}, f32[4,16,512]{2,1,0:T(8,128)S(1)}) custom-call(f32[128,512]{1,0:T(8,128)S(1)} %get-tuple-element.22.modes_ref, bf16[2,64,128]{2,1,0:T(8,128)(2,1)S(1)} %copy-done.4, bf16[2,64,128]{2,1,0:T(8,128)(2,1)S(1)} %copy-done.3), custom_call_target="tpu_custom_call" | custom-call | tf_op jit(solution)/shard_map/keep_rows/pallas_call | solution.py:434
  19.7 3.6 %collective-permute-start.10 = (f32[4,8,512]{2,1,0:T(8,128)S(1)}, f32[4,8,512]{2,1,0:T(8,128)S(1)}, u32[]{:S(2)}, u32[]{:S(2)}) collective-permute-start(f32[4,8,512]{2,1,0:T(8,128)S(1)} %get-tuple-element.25), channel_id=1, source_target_pairs={{0,12},{1,15},{2,14},{3,13},{4,8},{5,11},{6,10},{7,9},{8,4},{9,7},... | collective-permute-start | bytes 196616 | tf_op jit(solution)/shard_map/ppermute | solution.py:290
  23.2 0.9 %collective-permute-start.12 = (f32[4,8,512]{2,1,0:T(8,128)S(1)}, f32[4,8,512]{2,1,0:T(8,128)S(1)}, u32[]{:S(2)}, u32[]{:S(2)}) collective-permute-start(f32[4,8,512]{2,1,0:T(8,128)S(1)} %get-tuple-element.27), channel_id=1, source_target_pairs={{0,4},{1,7},{2,6},{3,5},{4,0},{5,3},{6,2},{7,1},{8,12},{9,15},{10,... | collective-permute-start | bytes 196616 | tf_op jit(solution)/shard_map/ppermute | solution.py:290
  24.1 0.7 %collective-permute-start.13 = (f32[4,8,512]{2,1,0:T(8,128)S(1)}, f32[4,8,512]{2,1,0:T(8,128)S(1)}, u32[]{:S(2)}, u32[]{:S(2)}) collective-permute-start(f32[4,8,512]{2,1,0:T(8,128)S(1)} %get-tuple-element.28), channel_id=1, source_target_pairs={{0,0},{1,3},{2,2},{3,1},{4,4},{5,7},{6,6},{7,5},{8,8},{9,11},{10,1... | collective-permute-start | bytes 196616 | tf_op jit(solution)/shard_map/ppermute | solution.py:290
  24.8 1.7 %collective-permute-done.10.refs_0_ = f32[4,8,512]{2,1,0:T(8,128)S(1)} collective-permute-done((f32[4,8,512]{2,1,0:T(8,128)S(1)}, f32[4,8,512]{2,1,0:T(8,128)S(1)}, u32[]{:S(2)}, u32[]{:S(2)}) %collective-permute-start.10) | collective-permute-done | bytes 65568 | tf_op jit(solution)/shard_map/ppermute | solution.py:290
  26.5 1.2 %collective-permute-start.14 = (f32[4,8,512]{2,1,0:T(8,128)S(1)}, f32[4,8,512]{2,1,0:T(8,128)S(1)}, u32[]{:S(2)}, u32[]{:S(2)}) collective-permute-start(f32[4,8,512]{2,1,0:T(8,128)S(1)} %collective-permute-done.10.refs_0_), channel_id=1, source_target_pairs={{0,1},{1,0},{2,3},{3,2},{4,5},{5,4},{6,7},{7,6},{8,9},{9,8},{10,11... | collective-permute-start | bytes 196616 | tf_op jit(solution)/shard_map/ppermute | solution.py:279
  27.7 2.2 %collective-permute-done.11.refs_1_ = f32[4,8,512]{2,1,0:T(8,128)S(1)} collective-permute-done((f32[4,8,512]{2,1,0:T(8,128)S(1)}, f32[4,8,512]{2,1,0:T(8,128)S(1)}, u32[]{:S(2)}, u32[]{:S(2)}) %collective-permute-start.11) | collective-permute-done | bytes 65568 | tf_op jit(solution)/shard_map/ppermute | solution.py:290
  29.9 0.4 %collective-permute-start.15 = (f32[4,8,512]{2,1,0:T(8,128)S(1)}, f32[4,8,512]{2,1,0:T(8,128)S(1)}, u32[]{:S(2)}, u32[]{:S(2)}) collective-permute-start(f32[4,8,512]{2,1,0:T(8,128)S(1)} %collective-permute-done.11.refs_1_), channel_id=1, source_target_pairs={{0,1},{1,0},{2,3},{3,2},{4,5},{5,4},{6,7},{7,6},{8,9},{9,8},{10,11... | collective-permute-start | bytes 196616 | tf_op jit(solution)/shard_map/ppermute | solution.py:279
  30.4 0.4 %collective-permute-start.17 = (f32[4,8,512]{2,1,0:T(8,128)S(1)}, f32[4,8,512]{2,1,0:T(8,128)S(1)}, u32[]{:S(2)}, u32[]{:S(2)}) collective-permute-start(f32[4,8,512]{2,1,0:T(8,128)S(1)} %collective-permute-done.13.refs_3_), channel_id=1, source_target_pairs={{0,1},{1,0},{2,3},{3,2},{4,5},{5,4},{6,7},{7,6},{8,9},{9,8},{10,11... | collective-permute-start | bytes 196616 | tf_op jit(solution)/shard_map/ppermute | solution.py:279
  30.8 0.4 %collective-permute-done.15.refs_5_ = f32[4,8,512]{2,1,0:T(8,128)S(1)} collective-permute-done((f32[4,8,512]{2,1,0:T(8,128)S(1)}, f32[4,8,512]{2,1,0:T(8,128)S(1)}, u32[]{:S(2)}, u32[]{:S(2)}) %collective-permute-start.15) | collective-permute-done | bytes 65568 | tf_op jit(solution)/shard_map/ppermute | solution.py:279
  31.7 2.3 %make_output.1 = bf16[4,256,512]{2,1,0:T(8,128)(2,1)} custom-call(bf16[4,256,512]{2,1,0:T(8,128)(2,1)S(1)} %copy-done, bf16[2,2,256,256]{3,2,1,0:T(8,128)(2,1)S(1)} %copy-done.2, bf16[64,64]{1,0:T(8,128)(2,1)S(1)} %copy-done.7, f32[64]{0:T(128)S(1)} %copy-done.8, f32[4,8,512]{2,1,0:T(8,128)S(1)} %collective-permute-done.10.refs_0_, ...), custom_call_target="tpu_custom_call" | custom-call | tf_op jit(solution)/shard_map/make_output/pallas_call | solution.py:498
  (40 shorter events, 2.4 us)
Async XLA Ops:
  0.6 16.5 %copy-start.1 = (bf16[1,64,64,128]{3,2,1,0:T(8,128)(2,1)S(1)}, bf16[1,64,64,128]{3,2,1,0:T(8,128)(2,1)}, u32[]{:S(2)}) copy-start(bf16[1,64,64,128]{3,2,1,0:T(8,128)(2,1)} %refs_8_.1) | copy-start | bytes 3145732
  2.4 1.7 %collective-permute-start = (f32[4,2,16,512]{3,2,1,0:T(8,128)S(1)}, f32[4,2,16,512]{3,2,1,0:T(8,128)S(1)}, u32[]{:S(2)}, u32[]{:S(2)}) collective-permute-start(f32[4,2,16,512]{3,2,1,0:T(8,128)S(1)} %get-tuple-element.17), channel_id=1, source_target_pairs={{0,1},{1,0},{2,3},{3,2},{4,5},{5,4},{6,7},{7,6},{8,9},{9,8},{10,11... | collective-permute-start | bytes 786440 | tf_op jit(solution)/shard_map/ppermute | solution.py:279
  4.1 6.6 %collective-permute-start.1 = (f32[2,16,512]{2,1,0:T(8,128)S(1)}, f32[2,16,512]{2,1,0:T(8,128)S(1)}, u32[]{:S(2)}, u32[]{:S(2)}) collective-permute-start(f32[2,16,512]{2,1,0:T(8,128)S(1)} %get-tuple-element.18), channel_id=1, source_target_pairs={{0,8},{1,11},{2,10},{3,9},{4,12},{5,15},{6,14},{7,13},{8,0},{9,3},... | collective-permute-start | bytes 196616 | tf_op jit(solution)/shard_map/ppermute | solution.py:290
  8.1 6.7 %collective-permute-start.2 = (f32[2,16,512]{2,1,0:T(8,128)S(1)}, f32[2,16,512]{2,1,0:T(8,128)S(1)}, u32[]{:S(2)}, u32[]{:S(2)}) collective-permute-start(f32[2,16,512]{2,1,0:T(8,128)S(1)} %get-tuple-element.19), channel_id=1, source_target_pairs={{0,12},{1,15},{2,14},{3,13},{4,8},{5,11},{6,10},{7,9},{8,4},{9,7},... | collective-permute-start | bytes 196616 | tf_op jit(solution)/shard_map/ppermute | solution.py:290
  9.5 6.0 %collective-permute-start.3 = (f32[2,16,512]{2,1,0:T(8,128)S(1)}, f32[2,16,512]{2,1,0:T(8,128)S(1)}, u32[]{:S(2)}, u32[]{:S(2)}) collective-permute-start(f32[2,16,512]{2,1,0:T(8,128)S(1)} %get-tuple-element.20), channel_id=1, source_target_pairs={{0,4},{1,7},{2,6},{3,5},{4,0},{5,3},{6,2},{7,1},{8,12},{9,15},{10,... | collective-permute-start | bytes 196616 | tf_op jit(solution)/shard_map/ppermute | solution.py:290
  9.7 6.1 %collective-permute-start.4 = (f32[2,16,512]{2,1,0:T(8,128)S(1)}, f32[2,16,512]{2,1,0:T(8,128)S(1)}, u32[]{:S(2)}, u32[]{:S(2)}) collective-permute-start(f32[2,16,512]{2,1,0:T(8,128)S(1)} %get-tuple-element.21), channel_id=1, source_target_pairs={{0,0},{1,3},{2,2},{3,1},{4,4},{5,7},{6,6},{7,5},{8,8},{9,11},{10,1... | collective-permute-start | bytes 196616 | tf_op jit(solution)/shard_map/ppermute | solution.py:290
  10.7 5.5 %collective-permute-start.5 = (f32[16,512]{1,0:T(8,128)S(1)}, f32[16,512]{1,0:T(8,128)S(1)}, u32[]{:S(2)}, u32[]{:S(2)}) collective-permute-start(f32[16,512]{1,0:T(8,128)S(1)} %second_half.4), channel_id=1, source_target_pairs={{0,1},{1,0},{2,3},{3,2},{4,5},{5,4},{6,7},{7,6},{8,9},{9,8},{10,11... | collective-permute-start | bytes 98312 | tf_op jit(solution)/shard_map/ppermute | solution.py:279
  14.8 1.4 %collective-permute-start.6 = (f32[16,512]{1,0:T(8,128)S(1)}, f32[16,512]{1,0:T(8,128)S(1)}, u32[]{:S(2)}, u32[]{:S(2)}) collective-permute-start(f32[16,512]{1,0:T(8,128)S(1)} %second_half.5), channel_id=1, source_target_pairs={{0,1},{1,0},{2,3},{3,2},{4,5},{5,4},{6,7},{7,6},{8,9},{9,8},{10,11... | collective-permute-start | bytes 98312 | tf_op jit(solution)/shard_map/ppermute | solution.py:279
  15.5 1.6 %copy-start.6 = (bf16[128,128]{1,0:T(8,128)(2,1)S(1)}, bf16[128,128]{1,0:T(8,128)(2,1)}, u32[]{:S(2)}) copy-start(bf16[128,128]{1,0:T(8,128)(2,1)} %constant.10.clone.refs_9_) | copy-start | bytes 98308
  15.6 1.3 %collective-permute-start.7 = (f32[16,512]{1,0:T(8,128)S(1)}, f32[16,512]{1,0:T(8,128)S(1)}, u32[]{:S(2)}, u32[]{:S(2)}) collective-permute-start(f32[16,512]{1,0:T(8,128)S(1)} %second_half.6), channel_id=1, source_target_pairs={{0,1},{1,0},{2,3},{3,2},{4,5},{5,4},{6,7},{7,6},{8,9},{9,8},{10,11... | collective-permute-start | bytes 98312 | tf_op jit(solution)/shard_map/ppermute | solution.py:279
  15.8 15.8 %copy-start = (bf16[4,256,512]{2,1,0:T(8,128)(2,1)S(1)}, bf16[4,256,512]{2,1,0:T(8,128)(2,1)}, u32[]{:S(2)}) copy-start(bf16[4,256,512]{2,1,0:T(8,128)(2,1)} %flow_ref.1) | copy-start | bytes 3145732
  15.8 1.3 %collective-permute-start.8 = (f32[16,512]{1,0:T(8,128)S(1)}, f32[16,512]{1,0:T(8,128)S(1)}, u32[]{:S(2)}, u32[]{:S(2)}) collective-permute-start(f32[16,512]{1,0:T(8,128)S(1)} %second_half.7), channel_id=1, source_target_pairs={{0,1},{1,0},{2,3},{3,2},{4,5},{5,4},{6,7},{7,6},{8,9},{9,8},{10,11... | collective-permute-start | bytes 98312 | tf_op jit(solution)/shard_map/ppermute | solution.py:279
  18.2 13.4 %copy-start.2 = (bf16[2,2,256,256]{3,2,1,0:T(8,128)(2,1)S(1)}, bf16[2,2,256,256]{3,2,1,0:T(8,128)(2,1)}, u32[]{:S(2)}) copy-start(bf16[2,2,256,256]{3,2,1,0:T(8,128)(2,1)} %constant.14.clone.table_ref) | copy-start | bytes 1572868
  18.2 1.4 %collective-permute-start.9 = (f32[4,16,512]{2,1,0:T(8,128)S(1)}, f32[4,16,512]{2,1,0:T(8,128)S(1)}, u32[]{:S(2)}, u32[]{:S(2)}) collective-permute-start(f32[4,16,512]{2,1,0:T(8,128)S(1)} %get-tuple-element.24), channel_id=1, source_target_pairs={{0,1},{1,0},{2,3},{3,2},{4,5},{5,4},{6,7},{7,6},{8,9},{9,8},{10,11... | collective-permute-start | bytes 393224 | tf_op jit(solution)/shard_map/ppermute | solution.py:279
  19.6 12.0 %copy-start.7 = (bf16[64,64]{1,0:T(8,128)(2,1)S(1)}, bf16[64,64]{1,0:T(8,128)(2,1)}, u32[]{:S(2)}) copy-start(bf16[64,64]{1,0:T(8,128)(2,1)} %local_ref.1) | copy-start | bytes 24580
  19.7 6.8 %collective-permute-start.10 = (f32[4,8,512]{2,1,0:T(8,128)S(1)}, f32[4,8,512]{2,1,0:T(8,128)S(1)}, u32[]{:S(2)}, u32[]{:S(2)}) collective-permute-start(f32[4,8,512]{2,1,0:T(8,128)S(1)} %get-tuple-element.25), channel_id=1, source_target_pairs={{0,12},{1,15},{2,14},{3,13},{4,8},{5,11},{6,10},{7,9},{8,4},{9,7},... | collective-permute-start | bytes 196616 | tf_op jit(solution)/shard_map/ppermute | solution.py:290
  23.2 6.6 %collective-permute-start.11 = (f32[4,8,512]{2,1,0:T(8,128)S(1)}, f32[4,8,512]{2,1,0:T(8,128)S(1)}, u32[]{:S(2)}, u32[]{:S(2)}) collective-permute-start(f32[4,8,512]{2,1,0:T(8,128)S(1)} %get-tuple-element.26), channel_id=1, source_target_pairs={{0,8},{1,11},{2,10},{3,9},{4,12},{5,15},{6,14},{7,13},{8,0},{9,3},... | collective-permute-start | bytes 196616 | tf_op jit(solution)/shard_map/ppermute | solution.py:290
  23.2 8.4 %copy-start.8 = (f32[64]{0:T(128)S(1)}, f32[64]{0:T(128)}, u32[]{:S(2)}) copy-start(f32[64]{0:T(128)} %bias_ref.1) | copy-start | bytes 772
  23.2 7.0 %collective-permute-start.12 = (f32[4,8,512]{2,1,0:T(8,128)S(1)}, f32[4,8,512]{2,1,0:T(8,128)S(1)}, u32[]{:S(2)}, u32[]{:S(2)}) collective-permute-start(f32[4,8,512]{2,1,0:T(8,128)S(1)} %get-tuple-element.27), channel_id=1, source_target_pairs={{0,4},{1,7},{2,6},{3,5},{4,0},{5,3},{6,2},{7,1},{8,12},{9,15},{10,... | collective-permute-start | bytes 196616 | tf_op jit(solution)/shard_map/ppermute | solution.py:290
  24.1 6.2 %collective-permute-start.13 = (f32[4,8,512]{2,1,0:T(8,128)S(1)}, f32[4,8,512]{2,1,0:T(8,128)S(1)}, u32[]{:S(2)}, u32[]{:S(2)}) collective-permute-start(f32[4,8,512]{2,1,0:T(8,128)S(1)} %get-tuple-element.28), channel_id=1, source_target_pairs={{0,0},{1,3},{2,2},{3,1},{4,4},{5,7},{6,6},{7,5},{8,8},{9,11},{10,1... | collective-permute-start | bytes 196616 | tf_op jit(solution)/shard_map/ppermute | solution.py:290
  26.5 4.3 %collective-permute-start.14 = (f32[4,8,512]{2,1,0:T(8,128)S(1)}, f32[4,8,512]{2,1,0:T(8,128)S(1)}, u32[]{:S(2)}, u32[]{:S(2)}) collective-permute-start(f32[4,8,512]{2,1,0:T(8,128)S(1)} %collective-permute-done.10.refs_0_), channel_id=1, source_target_pairs={{0,1},{1,0},{2,3},{3,2},{4,5},{5,4},{6,7},{7,6},{8,9},{9,8},{10,11... | collective-permute-start | bytes 196616 | tf_op jit(solution)/shard_map/ppermute | solution.py:279
  29.9 1.3 %collective-permute-start.15 = (f32[4,8,512]{2,1,0:T(8,128)S(1)}, f32[4,8,512]{2,1,0:T(8,128)S(1)}, u32[]{:S(2)}, u32[]{:S(2)}) collective-permute-start(f32[4,8,512]{2,1,0:T(8,128)S(1)} %collective-permute-done.11.refs_1_), channel_id=1, source_target_pairs={{0,1},{1,0},{2,3},{3,2},{4,5},{5,4},{6,7},{7,6},{8,9},{9,8},{10,11... | collective-permute-start | bytes 196616 | tf_op jit(solution)/shard_map/ppermute | solution.py:279
  30.2 1.3 %collective-permute-start.16 = (f32[4,8,512]{2,1,0:T(8,128)S(1)}, f32[4,8,512]{2,1,0:T(8,128)S(1)}, u32[]{:S(2)}, u32[]{:S(2)}) collective-permute-start(f32[4,8,512]{2,1,0:T(8,128)S(1)} %collective-permute-done.12.refs_2_), channel_id=1, source_target_pairs={{0,1},{1,0},{2,3},{3,2},{4,5},{5,4},{6,7},{7,6},{8,9},{9,8},{10,11... | collective-permute-start | bytes 196616 | tf_op jit(solution)/shard_map/ppermute | solution.py:279
  30.4 1.3 %collective-permute-start.17 = (f32[4,8,512]{2,1,0:T(8,128)S(1)}, f32[4,8,512]{2,1,0:T(8,128)S(1)}, u32[]{:S(2)}, u32[]{:S(2)}) collective-permute-start(f32[4,8,512]{2,1,0:T(8,128)S(1)} %collective-permute-done.13.refs_3_), channel_id=1, source_target_pairs={{0,1},{1,0},{2,3},{3,2},{4,5},{5,4},{6,7},{7,6},{8,9},{9,8},{10,11... | collective-permute-start | bytes 196616 | tf_op jit(solution)/shard_map/ppermute | solution.py:279
  (3 other events, 4.8 us)

commit v22 on v20

--- a/solution.py
+++ b/solution.py
@@ -165,7 +165,8 @@
 
 
 def turns(layers):
-    return list(range(layers - 1, -1, -1))
+    half = layers // 2
+    return list(range(half, layers)) + list(range(half - 1, -1, -1))
 
 
 def forward_x_table(cells_x, peers, rows_ky):
@@ -228,7 +229,7 @@
     row = lax.broadcasted_iota(jnp.int32, (shape[0], 1), 0)
     block = row // (2 * rows_ky)
     place = block // 2 % layers
-    turn = layers - 1 - place
+    turn = jnp.where(place < layers // 2, place + layers // 2, layers - 1 - place)
     side = y ^ (1 - block // peers)
     owner = (side ^ (block % 2)) * peers + (z ^ turn) * 2 + (x ^ side)
     index = owner * rows_ky + row // 2 % rows_ky

time: 33.9 us -> 33.9 us (level)
  waiting for transfers between devices: 9.99 us -> 10.5 us
  starting transfers between devices: 17 us -> 16.5 us
    ppermute x8, starting transfers between devices: 11.4 us -> 11 us  [along_columns(): arrived.append(lax.ppermute(block, ('gx', 'gy'), pairs))]
    ppermute x8, waiting for transfers between devices: 6.86 us -> 7.22 us  [along_columns(): arrived.append(lax.ppermute(block, ('gx', 'gy'), pairs))]
  transfers between devices with their start and end apart: 18 -> 18, of which waited for: 12 -> 13; matrix products, arithmetic and copies ran while one was open for 0% -> 0% of each run, Pallas kernels for 2% -> 2%
where the time goes in v22:
time: 33.9 us; the launch traced here: 33.8 us
  starting transfers between devices  16.5 us (49%)
  waiting for transfers between devices  10.5 us (31%)
  Pallas kernels  5.97 us (18%)
  between operations  0.76 us (2%)
    ppermute x8, starting transfers between devices, along_columns(): arrived.append(lax.ppermute(block, ('gx', 'gy'), pairs))  11 us
    ppermute x8, waiting for transfers between devices, along_columns(): arrived.append(lax.ppermute(block, ('gx', 'gy'), pairs))  7.22 us
    ppermute x10, starting transfers between devices, flip_core(): return lax.ppermute(block, 'gy', [(0, 1), (1, 0)])  5.42 us
    ppermute x10, waiting for transfers between devices, flip_core(): return lax.ppermute(block, 'gy', [(0, 1), (1, 0)])  3.32 us
    pallas_call x1, Pallas kernels, make_output(): pl.pallas_call(functools.partial(output_kernel, layers), out_specs=pl.Blo...  2.3 us
    pallas_call x1, Pallas kernels, forward_y(): pl.pallas_call(functools.partial(forward_y_kernel, extent, rows_ky), in_s...  1.75 us
    pallas_call x1, Pallas kernels, mix(): pl.pallas_call(functools.partial(mix_kernel, layers), out_shape=[jax.Shap...  1.05 us
    pallas_call x1, Pallas kernels, keep_rows(): pl.pallas_call(keep_kernel, out_shape=[jax.ShapeDtypeStruct((1, rows // 2...  0.79 us
  transfers between devices with their start and end apart: 18, of which 13 were waited for; matrix products, arithmetic and copies ran while one was open for 0% of the time, Pallas kernels for 2%

profile of v22, /device:TPU:0, one launch (start us, length us, event | category | flops | bytes accessed | tf_op | source)
XLA Modules:
  0.0 33.8 jit_solution(9904499502177000886)
XLA Ops:
  0.6 1.7 %forward_y.1 = (f32[4,2,16,512]{3,2,1,0:T(8,128)S(1)}, f32[4,2,16,512]{3,2,1,0:T(8,128)S(1)}) custom-call(bf16[4,256,512]{2,1,0:T(8,128)(2,1)} %flow_ref.1), custom_call_target="tpu_custom_call" | custom-call | tf_op jit(solution)/shard_map/forward_y/pallas_call | solution.py:263
  2.4 0.5 %collective-permute-start = (f32[4,2,16,512]{3,2,1,0:T(8,128)S(1)}, f32[4,2,16,512]{3,2,1,0:T(8,128)S(1)}, u32[]{:S(2)}, u32[]{:S(2)}) collective-permute-start(f32[4,2,16,512]{3,2,1,0:T(8,128)S(1)} %get-tuple-element.17), channel_id=1, source_target_pairs={{0,1},{1,0},{2,3},{3,2},{4,5},{5,4},{6,7},{7,6},{8,9},{9,8},{10,11... | collective-permute-start | bytes 786440 | tf_op jit(solution)/shard_map/ppermute | solution.py:277
  2.9 1.2 %collective-permute-done.arrived_ref = f32[4,2,16,512]{3,2,1,0:T(8,128)S(1)} collective-permute-done((f32[4,2,16,512]{3,2,1,0:T(8,128)S(1)}, f32[4,2,16,512]{3,2,1,0:T(8,128)S(1)}, u32[]{:S(2)}, u32[]{:S(2)}) %collective-permute-start) | collective-permute-done | bytes 262176 | tf_op jit(solution)/shard_map/ppermute | solution.py:277
  4.1 4.0 %collective-permute-start.1 = (f32[2,16,512]{2,1,0:T(8,128)S(1)}, f32[2,16,512]{2,1,0:T(8,128)S(1)}, u32[]{:S(2)}, u32[]{:S(2)}) collective-permute-start(f32[2,16,512]{2,1,0:T(8,128)S(1)} %get-tuple-element.18), channel_id=1, source_target_pairs={{0,8},{1,11},{2,10},{3,9},{4,12},{5,15},{6,14},{7,13},{8,0},{9,3},... | collective-permute-start | bytes 196616 | tf_op jit(solution)/shard_map/ppermute | solution.py:288
  8.1 1.3 %collective-permute-start.2 = (f32[2,16,512]{2,1,0:T(8,128)S(1)}, f32[2,16,512]{2,1,0:T(8,128)S(1)}, u32[]{:S(2)}, u32[]{:S(2)}) collective-permute-start(f32[2,16,512]{2,1,0:T(8,128)S(1)} %get-tuple-element.19), channel_id=1, source_target_pairs={{0,12},{1,15},{2,14},{3,13},{4,8},{5,11},{6,10},{7,9},{8,4},{9,7},... | collective-permute-start | bytes 196616 | tf_op jit(solution)/shard_map/ppermute | solution.py:288
  9.7 0.7 %collective-permute-start.4 = (f32[2,16,512]{2,1,0:T(8,128)S(1)}, f32[2,16,512]{2,1,0:T(8,128)S(1)}, u32[]{:S(2)}, u32[]{:S(2)}) collective-permute-start(f32[2,16,512]{2,1,0:T(8,128)S(1)} %get-tuple-element.21), channel_id=1, source_target_pairs={{0,0},{1,3},{2,2},{3,1},{4,4},{5,7},{6,6},{7,5},{8,8},{9,11},{10,1... | collective-permute-start | bytes 196616 | tf_op jit(solution)/shard_map/ppermute | solution.py:288
  10.4 0.4 %collective-permute-done.1.block_ref.refs_0_ = f32[2,16,512]{2,1,0:T(8,128)S(1)} collective-permute-done((f32[2,16,512]{2,1,0:T(8,128)S(1)}, f32[2,16,512]{2,1,0:T(8,128)S(1)}, u32[]{:S(2)}, u32[]{:S(2)}) %collective-permute-start.1) | collective-permute-done | bytes 65568 | tf_op jit(solution)/shard_map/ppermute | solution.py:288
  10.7 2.6 %collective-permute-start.5 = (f32[16,512]{1,0:T(8,128)S(1)}, f32[16,512]{1,0:T(8,128)S(1)}, u32[]{:S(2)}, u32[]{:S(2)}) collective-permute-start(f32[16,512]{1,0:T(8,128)S(1)} %second_half.4), channel_id=1, source_target_pairs={{0,1},{1,0},{2,3},{3,2},{4,5},{5,4},{6,7},{7,6},{8,9},{9,8},{10,11... | collective-permute-start | bytes 98312 | tf_op jit(solution)/shard_map/ppermute | solution.py:277
  13.4 1.4 %collective-permute-done.2.block_ref.refs_1_ = f32[2,16,512]{2,1,0:T(8,128)S(1)} collective-permute-done((f32[2,16,512]{2,1,0:T(8,128)S(1)}, f32[2,16,512]{2,1,0:T(8,128)S(1)}, u32[]{:S(2)}, u32[]{:S(2)}) %collective-permute-start.2) | collective-permute-done | bytes 65568 | tf_op jit(solution)/shard_map/ppermute | solution.py:288
  14.8 0.5 %collective-permute-start.6 = (f32[16,512]{1,0:T(8,128)S(1)}, f32[16,512]{1,0:T(8,128)S(1)}, u32[]{:S(2)}, u32[]{:S(2)}) collective-permute-start(f32[16,512]{1,0:T(8,128)S(1)} %second_half.5), channel_id=1, source_target_pairs={{0,1},{1,0},{2,3},{3,2},{4,5},{5,4},{6,7},{7,6},{8,9},{9,8},{10,11... | collective-permute-start | bytes 98312 | tf_op jit(solution)/shard_map/ppermute | solution.py:277
  15.8 0.4 %collective-permute-start.8 = (f32[16,512]{1,0:T(8,128)S(1)}, f32[16,512]{1,0:T(8,128)S(1)}, u32[]{:S(2)}, u32[]{:S(2)}) collective-permute-start(f32[16,512]{1,0:T(8,128)S(1)} %second_half.7), channel_id=1, source_target_pairs={{0,1},{1,0},{2,3},{3,2},{4,5},{5,4},{6,7},{7,6},{8,9},{9,8},{10,11... | collective-permute-start | bytes 98312 | tf_op jit(solution)/shard_map/ppermute | solution.py:277
  16.2 0.6 %collective-permute-done.7.refs_6_ = f32[16,512]{1,0:T(8,128)S(1)} collective-permute-done((f32[16,512]{1,0:T(8,128)S(1)}, f32[16,512]{1,0:T(8,128)S(1)}, u32[]{:S(2)}, u32[]{:S(2)}) %collective-permute-start.7) | collective-permute-done | bytes 32800 | tf_op jit(solution)/shard_map/ppermute | solution.py:277
  17.2 1.1 %mix.1 = (f32[128,512]{1,0:T(8,128)S(1)}, f32[4,16,512]{2,1,0:T(8,128)S(1)}) custom-call(f32[2,16,512]{2,1,0:T(8,128)S(1)} %collective-permute-done.1.block_ref.refs_0_, f32[2,16,512]{2,1,0:T(8,128)S(1)} %collective-permute-done.2.block_ref.refs_1_, f32[2,16,512]{2,1,0:T(8,128)S(1)} %collective-permute-done.3.block_ref.refs_2_, ...), custom_call_target="tpu_custom_call" | custom-call | tf_op jit(solution)/shard_map/mix/pallas_call | solution.py:405
  18.2 0.4 %collective-permute-start.9 = (f32[4,16,512]{2,1,0:T(8,128)S(1)}, f32[4,16,512]{2,1,0:T(8,128)S(1)}, u32[]{:S(2)}, u32[]{:S(2)}) collective-permute-start(f32[4,16,512]{2,1,0:T(8,128)S(1)} %get-tuple-element.24), channel_id=1, source_target_pairs={{0,1},{1,0},{2,3},{3,2},{4,5},{5,4},{6,7},{7,6},{8,9},{9,8},{10,11... | collective-permute-start | bytes 393224 | tf_op jit(solution)/shard_map/ppermute | solution.py:277
  18.6 0.8 %keep_rows.1 = (f32[1,64,1024]{2,1,0:T(8,128)}, f32[4,16,512]{2,1,0:T(8,128)S(1)}) custom-call(f32[128,512]{1,0:T(8,128)S(1)} %get-tuple-element.22.modes_ref, bf16[2,64,128]{2,1,0:T(8,128)(2,1)S(1)} %copy-done.4, bf16[2,64,128]{2,1,0:T(8,128)(2,1)S(1)} %copy-done.3), custom_call_target="tpu_custom_call" | custom-call | tf_op jit(solution)/shard_map/keep_rows/pallas_call | solution.py:432
  19.7 3.1 %collective-permute-start.10 = (f32[4,8,512]{2,1,0:T(8,128)S(1)}, f32[4,8,512]{2,1,0:T(8,128)S(1)}, u32[]{:S(2)}, u32[]{:S(2)}) collective-permute-start(f32[4,8,512]{2,1,0:T(8,128)S(1)} %get-tuple-element.25), channel_id=1, source_target_pairs={{0,8},{1,11},{2,10},{3,9},{4,12},{5,15},{6,14},{7,13},{8,0},{9,3},... | collective-permute-start | bytes 196616 | tf_op jit(solution)/shard_map/ppermute | solution.py:288
  22.8 0.7 %collective-permute-start.11 = (f32[4,8,512]{2,1,0:T(8,128)S(1)}, f32[4,8,512]{2,1,0:T(8,128)S(1)}, u32[]{:S(2)}, u32[]{:S(2)}) collective-permute-start(f32[4,8,512]{2,1,0:T(8,128)S(1)} %get-tuple-element.26), channel_id=1, source_target_pairs={{0,12},{1,15},{2,14},{3,13},{4,8},{5,11},{6,10},{7,9},{8,4},{9,7},... | collective-permute-start | bytes 196616 | tf_op jit(solution)/shard_map/ppermute | solution.py:288
  23.5 0.3 collective-permute-start.12
  23.8 0.7 %collective-permute-start.13 = (f32[4,8,512]{2,1,0:T(8,128)S(1)}, f32[4,8,512]{2,1,0:T(8,128)S(1)}, u32[]{:S(2)}, u32[]{:S(2)}) collective-permute-start(f32[4,8,512]{2,1,0:T(8,128)S(1)} %get-tuple-element.28), channel_id=1, source_target_pairs={{0,0},{1,3},{2,2},{3,1},{4,4},{5,7},{6,6},{7,5},{8,8},{9,11},{10,1... | collective-permute-start | bytes 196616 | tf_op jit(solution)/shard_map/ppermute | solution.py:288
  24.5 2.7 %collective-permute-done.10.refs_0_ = f32[4,8,512]{2,1,0:T(8,128)S(1)} collective-permute-done((f32[4,8,512]{2,1,0:T(8,128)S(1)}, f32[4,8,512]{2,1,0:T(8,128)S(1)}, u32[]{:S(2)}, u32[]{:S(2)}) %collective-permute-start.10) | collective-permute-done | bytes 65568 | tf_op jit(solution)/shard_map/ppermute | solution.py:288
  27.2 2.4 %collective-permute-done.11.refs_1_ = f32[4,8,512]{2,1,0:T(8,128)S(1)} collective-permute-done((f32[4,8,512]{2,1,0:T(8,128)S(1)}, f32[4,8,512]{2,1,0:T(8,128)S(1)}, u32[]{:S(2)}, u32[]{:S(2)}) %collective-permute-start.11) | collective-permute-done | bytes 65568 | tf_op jit(solution)/shard_map/ppermute | solution.py:288
  30.5 0.4 %collective-permute-done.15.refs_5_ = f32[4,8,512]{2,1,0:T(8,128)S(1)} collective-permute-done((f32[4,8,512]{2,1,0:T(8,128)S(1)}, f32[4,8,512]{2,1,0:T(8,128)S(1)}, u32[]{:S(2)}, u32[]{:S(2)}) %collective-permute-start.15) | collective-permute-done | bytes 65568 | tf_op jit(solution)/shard_map/ppermute | solution.py:277
  30.9 0.4 %collective-permute-done.16.refs_6_ = f32[4,8,512]{2,1,0:T(8,128)S(1)} collective-permute-done((f32[4,8,512]{2,1,0:T(8,128)S(1)}, f32[4,8,512]{2,1,0:T(8,128)S(1)}, u32[]{:S(2)}, u32[]{:S(2)}) %collective-permute-start.16) | collective-permute-done | bytes 65568 | tf_op jit(solution)/shard_map/ppermute | solution.py:277
  31.5 2.3 %make_output.1 = bf16[4,256,512]{2,1,0:T(8,128)(2,1)} custom-call(bf16[4,256,512]{2,1,0:T(8,128)(2,1)S(1)} %copy-done, bf16[2,2,256,256]{3,2,1,0:T(8,128)(2,1)S(1)} %copy-done.2, bf16[64,64]{1,0:T(8,128)(2,1)S(1)} %copy-done.7, f32[64]{0:T(128)S(1)} %copy-done.8, f32[4,8,512]{2,1,0:T(8,128)S(1)} %collective-permute-done.10.refs_0_, ...), custom_call_target="tpu_custom_call" | custom-call | tf_op jit(solution)/shard_map/make_output/pallas_call | solution.py:496
  (40 shorter events, 2.5 us)
Async XLA Ops:
  0.6 16.5 %copy-start.1 = (bf16[1,64,64,128]{3,2,1,0:T(8,128)(2,1)S(1)}, bf16[1,64,64,128]{3,2,1,0:T(8,128)(2,1)}, u32[]{:S(2)}) copy-start(bf16[1,64,64,128]{3,2,1,0:T(8,128)(2,1)} %refs_8_.1) | copy-start | bytes 3145732
  2.4 1.7 %collective-permute-start = (f32[4,2,16,512]{3,2,1,0:T(8,128)S(1)}, f32[4,2,16,512]{3,2,1,0:T(8,128)S(1)}, u32[]{:S(2)}, u32[]{:S(2)}) collective-permute-start(f32[4,2,16,512]{3,2,1,0:T(8,128)S(1)} %get-tuple-element.17), channel_id=1, source_target_pairs={{0,1},{1,0},{2,3},{3,2},{4,5},{5,4},{6,7},{7,6},{8,9},{9,8},{10,11... | collective-permute-start | bytes 786440 | tf_op jit(solution)/shard_map/ppermute | solution.py:277
  4.1 6.6 %collective-permute-start.1 = (f32[2,16,512]{2,1,0:T(8,128)S(1)}, f32[2,16,512]{2,1,0:T(8,128)S(1)}, u32[]{:S(2)}, u32[]{:S(2)}) collective-permute-start(f32[2,16,512]{2,1,0:T(8,128)S(1)} %get-tuple-element.18), channel_id=1, source_target_pairs={{0,8},{1,11},{2,10},{3,9},{4,12},{5,15},{6,14},{7,13},{8,0},{9,3},... | collective-permute-start | bytes 196616 | tf_op jit(solution)/shard_map/ppermute | solution.py:288
  8.1 6.7 %collective-permute-start.2 = (f32[2,16,512]{2,1,0:T(8,128)S(1)}, f32[2,16,512]{2,1,0:T(8,128)S(1)}, u32[]{:S(2)}, u32[]{:S(2)}) collective-permute-start(f32[2,16,512]{2,1,0:T(8,128)S(1)} %get-tuple-element.19), channel_id=1, source_target_pairs={{0,12},{1,15},{2,14},{3,13},{4,8},{5,11},{6,10},{7,9},{8,4},{9,7},... | collective-permute-start | bytes 196616 | tf_op jit(solution)/shard_map/ppermute | solution.py:288
  9.5 6.0 %collective-permute-start.3 = (f32[2,16,512]{2,1,0:T(8,128)S(1)}, f32[2,16,512]{2,1,0:T(8,128)S(1)}, u32[]{:S(2)}, u32[]{:S(2)}) collective-permute-start(f32[2,16,512]{2,1,0:T(8,128)S(1)} %get-tuple-element.20), channel_id=1, source_target_pairs={{0,4},{1,7},{2,6},{3,5},{4,0},{5,3},{6,2},{7,1},{8,12},{9,15},{10,... | collective-permute-start | bytes 196616 | tf_op jit(solution)/shard_map/ppermute | solution.py:288
  9.7 6.1 %collective-permute-start.4 = (f32[2,16,512]{2,1,0:T(8,128)S(1)}, f32[2,16,512]{2,1,0:T(8,128)S(1)}, u32[]{:S(2)}, u32[]{:S(2)}) collective-permute-start(f32[2,16,512]{2,1,0:T(8,128)S(1)} %get-tuple-element.21), channel_id=1, source_target_pairs={{0,0},{1,3},{2,2},{3,1},{4,4},{5,7},{6,6},{7,5},{8,8},{9,11},{10,1... | collective-permute-start | bytes 196616 | tf_op jit(solution)/shard_map/ppermute | solution.py:288
  10.7 5.5 %collective-permute-start.5 = (f32[16,512]{1,0:T(8,128)S(1)}, f32[16,512]{1,0:T(8,128)S(1)}, u32[]{:S(2)}, u32[]{:S(2)}) collective-permute-start(f32[16,512]{1,0:T(8,128)S(1)} %second_half.4), channel_id=1, source_target_pairs={{0,1},{1,0},{2,3},{3,2},{4,5},{5,4},{6,7},{7,6},{8,9},{9,8},{10,11... | collective-permute-start | bytes 98312 | tf_op jit(solution)/shard_map/ppermute | solution.py:277
  14.8 1.4 %collective-permute-start.6 = (f32[16,512]{1,0:T(8,128)S(1)}, f32[16,512]{1,0:T(8,128)S(1)}, u32[]{:S(2)}, u32[]{:S(2)}) collective-permute-start(f32[16,512]{1,0:T(8,128)S(1)} %second_half.5), channel_id=1, source_target_pairs={{0,1},{1,0},{2,3},{3,2},{4,5},{5,4},{6,7},{7,6},{8,9},{9,8},{10,11... | collective-permute-start | bytes 98312 | tf_op jit(solution)/shard_map/ppermute | solution.py:277
  15.5 1.6 %copy-start.6 = (bf16[128,128]{1,0:T(8,128)(2,1)S(1)}, bf16[128,128]{1,0:T(8,128)(2,1)}, u32[]{:S(2)}) copy-start(bf16[128,128]{1,0:T(8,128)(2,1)} %constant.10.clone.refs_9_) | copy-start | bytes 98308
  15.6 1.3 %collective-permute-start.7 = (f32[16,512]{1,0:T(8,128)S(1)}, f32[16,512]{1,0:T(8,128)S(1)}, u32[]{:S(2)}, u32[]{:S(2)}) collective-permute-start(f32[16,512]{1,0:T(8,128)S(1)} %second_half.6), channel_id=1, source_target_pairs={{0,1},{1,0},{2,3},{3,2},{4,5},{5,4},{6,7},{7,6},{8,9},{9,8},{10,11... | collective-permute-start | bytes 98312 | tf_op jit(solution)/shard_map/ppermute | solution.py:277
  15.8 15.6 %copy-start = (bf16[4,256,512]{2,1,0:T(8,128)(2,1)S(1)}, bf16[4,256,512]{2,1,0:T(8,128)(2,1)}, u32[]{:S(2)}) copy-start(bf16[4,256,512]{2,1,0:T(8,128)(2,1)} %flow_ref.1) | copy-start | bytes 3145732
  15.8 1.3 %collective-permute-start.8 = (f32[16,512]{1,0:T(8,128)S(1)}, f32[16,512]{1,0:T(8,128)S(1)}, u32[]{:S(2)}, u32[]{:S(2)}) collective-permute-start(f32[16,512]{1,0:T(8,128)S(1)} %second_half.7), channel_id=1, source_target_pairs={{0,1},{1,0},{2,3},{3,2},{4,5},{5,4},{6,7},{7,6},{8,9},{9,8},{10,11... | collective-permute-start | bytes 98312 | tf_op jit(solution)/shard_map/ppermute | solution.py:277
  18.2 13.2 %copy-start.2 = (bf16[2,2,256,256]{3,2,1,0:T(8,128)(2,1)S(1)}, bf16[2,2,256,256]{3,2,1,0:T(8,128)(2,1)}, u32[]{:S(2)}) copy-start(bf16[2,2,256,256]{3,2,1,0:T(8,128)(2,1)} %constant.14.clone.table_ref) | copy-start | bytes 1572868
  18.2 1.4 %collective-permute-start.9 = (f32[4,16,512]{2,1,0:T(8,128)S(1)}, f32[4,16,512]{2,1,0:T(8,128)S(1)}, u32[]{:S(2)}, u32[]{:S(2)}) collective-permute-start(f32[4,16,512]{2,1,0:T(8,128)S(1)} %get-tuple-element.24), channel_id=1, source_target_pairs={{0,1},{1,0},{2,3},{3,2},{4,5},{5,4},{6,7},{7,6},{8,9},{9,8},{10,11... | collective-permute-start | bytes 393224 | tf_op jit(solution)/shard_map/ppermute | solution.py:277
  19.6 11.8 %copy-start.7 = (bf16[64,64]{1,0:T(8,128)(2,1)S(1)}, bf16[64,64]{1,0:T(8,128)(2,1)}, u32[]{:S(2)}) copy-start(bf16[64,64]{1,0:T(8,128)(2,1)} %local_ref.1) | copy-start | bytes 24580
  19.7 7.5 %collective-permute-start.10 = (f32[4,8,512]{2,1,0:T(8,128)S(1)}, f32[4,8,512]{2,1,0:T(8,128)S(1)}, u32[]{:S(2)}, u32[]{:S(2)}) collective-permute-start(f32[4,8,512]{2,1,0:T(8,128)S(1)} %get-tuple-element.25), channel_id=1, source_target_pairs={{0,8},{1,11},{2,10},{3,9},{4,12},{5,15},{6,14},{7,13},{8,0},{9,3},... | collective-permute-start | bytes 196616 | tf_op jit(solution)/shard_map/ppermute | solution.py:288
  22.8 6.8 %collective-permute-start.11 = (f32[4,8,512]{2,1,0:T(8,128)S(1)}, f32[4,8,512]{2,1,0:T(8,128)S(1)}, u32[]{:S(2)}, u32[]{:S(2)}) collective-permute-start(f32[4,8,512]{2,1,0:T(8,128)S(1)} %get-tuple-element.26), channel_id=1, source_target_pairs={{0,12},{1,15},{2,14},{3,13},{4,8},{5,11},{6,10},{7,9},{8,4},{9,7},... | collective-permute-start | bytes 196616 | tf_op jit(solution)/shard_map/ppermute | solution.py:288
  23.5 8.0 %copy-start.8 = (f32[64]{0:T(128)S(1)}, f32[64]{0:T(128)}, u32[]{:S(2)}) copy-start(f32[64]{0:T(128)} %bias_ref.1) | copy-start | bytes 772
  23.5 6.5 %collective-permute-start.12 = (f32[4,8,512]{2,1,0:T(8,128)S(1)}, f32[4,8,512]{2,1,0:T(8,128)S(1)}, u32[]{:S(2)}, u32[]{:S(2)}) collective-permute-start(f32[4,8,512]{2,1,0:T(8,128)S(1)} %get-tuple-element.27), channel_id=1, source_target_pairs={{0,4},{1,7},{2,6},{3,5},{4,0},{5,3},{6,2},{7,1},{8,12},{9,15},{10,... | collective-permute-start | bytes 196616 | tf_op jit(solution)/shard_map/ppermute | solution.py:288
  23.8 6.4 %collective-permute-start.13 = (f32[4,8,512]{2,1,0:T(8,128)S(1)}, f32[4,8,512]{2,1,0:T(8,128)S(1)}, u32[]{:S(2)}, u32[]{:S(2)}) collective-permute-start(f32[4,8,512]{2,1,0:T(8,128)S(1)} %get-tuple-element.28), channel_id=1, source_target_pairs={{0,0},{1,3},{2,2},{3,1},{4,4},{5,7},{6,6},{7,5},{8,8},{9,11},{10,1... | collective-permute-start | bytes 196616 | tf_op jit(solution)/shard_map/ppermute | solution.py:288
  27.2 3.3 %collective-permute-start.14 = (f32[4,8,512]{2,1,0:T(8,128)S(1)}, f32[4,8,512]{2,1,0:T(8,128)S(1)}, u32[]{:S(2)}, u32[]{:S(2)}) collective-permute-start(f32[4,8,512]{2,1,0:T(8,128)S(1)} %collective-permute-done.10.refs_0_), channel_id=1, source_target_pairs={{0,1},{1,0},{2,3},{3,2},{4,5},{5,4},{6,7},{7,6},{8,9},{9,8},{10,11... | collective-permute-start | bytes 196616 | tf_op jit(solution)/shard_map/ppermute | solution.py:277
  29.6 1.3 %collective-permute-start.15 = (f32[4,8,512]{2,1,0:T(8,128)S(1)}, f32[4,8,512]{2,1,0:T(8,128)S(1)}, u32[]{:S(2)}, u32[]{:S(2)}) collective-permute-start(f32[4,8,512]{2,1,0:T(8,128)S(1)} %collective-permute-done.11.refs_1_), channel_id=1, source_target_pairs={{0,1},{1,0},{2,3},{3,2},{4,5},{5,4},{6,7},{7,6},{8,9},{9,8},{10,11... | collective-permute-start | bytes 196616 | tf_op jit(solution)/shard_map/ppermute | solution.py:277
  30.0 1.3 %collective-permute-start.16 = (f32[4,8,512]{2,1,0:T(8,128)S(1)}, f32[4,8,512]{2,1,0:T(8,128)S(1)}, u32[]{:S(2)}, u32[]{:S(2)}) collective-permute-start(f32[4,8,512]{2,1,0:T(8,128)S(1)} %collective-permute-done.12.refs_2_), channel_id=1, source_target_pairs={{0,1},{1,0},{2,3},{3,2},{4,5},{5,4},{6,7},{7,6},{8,9},{9,8},{10,11... | collective-permute-start | bytes 196616 | tf_op jit(solution)/shard_map/ppermute | solution.py:277
  30.2 1.3 %collective-permute-start.17 = (f32[4,8,512]{2,1,0:T(8,128)S(1)}, f32[4,8,512]{2,1,0:T(8,128)S(1)}, u32[]{:S(2)}, u32[]{:S(2)}) collective-permute-start(f32[4,8,512]{2,1,0:T(8,128)S(1)} %collective-permute-done.13.refs_3_), channel_id=1, source_target_pairs={{0,1},{1,0},{2,3},{3,2},{4,5},{5,4},{6,7},{7,6},{8,9},{9,8},{10,11... | collective-permute-start | bytes 196616 | tf_op jit(solution)/shard_map/ppermute | solution.py:277
  (3 other events, 4.8 us)

commit v23 on v21

--- a/solution.py
+++ b/solution.py
@@ -167,8 +167,8 @@
 def turns(layers, inverse=False):
     half = layers // 2
     if inverse:
-        return list(range(layers - 1, -1, -1))
-    return list(range(half, layers)) + list(range(half - 1, -1, -1))
+        return list(range(half, layers)) + list(range(half - 1, -1, -1))
+    return list(range(layers - 1, -1, -1))
 
 
 def forward_x_table(cells_x, peers, rows_ky):
@@ -231,7 +231,7 @@
     row = lax.broadcasted_iota(jnp.int32, (shape[0], 1), 0)
     block = row // (2 * rows_ky)
     place = block // 2 % layers
-    turn = jnp.where(place < layers // 2, place + layers // 2, layers - 1 - place)
+    turn = layers - 1 - place
     side = y ^ (1 - block // peers)
     owner = (side ^ (block % 2)) * peers + (z ^ turn) * 2 + (x ^ side)
     index = owner * rows_ky + row // 2 % rows_ky

time: 34.1 us -> 34.1 us (level)
  starting transfers between devices: 18.1 us -> 15.1 us
  waiting for transfers between devices: 9.15 us -> 12.1 us
    ppermute x8, waiting for transfers between devices: 5.9 us -> 8.93 us  [along_columns(): arrived.append(lax.ppermute(block, ('gx', 'gy'), pairs))]
    ppermute x10, starting transfers between devices: 6.69 us -> 4.55 us  [flip_core(): return lax.ppermute(block, 'gy', [(0, 1), (1, 0)])]
    ppermute x8, starting transfers between devices: 11.4 us -> 10.5 us  [along_columns(): arrived.append(lax.ppermute(block, ('gx', 'gy'), pairs))]
  transfers between devices with their start and end apart: 18 -> 18, of which waited for: 12 -> 11; matrix products, arithmetic and copies ran while one was open for 0% -> 0% of each run, Pallas kernels for 2% -> 2%
where the time goes in v23:
time: 34.1 us; the launch traced here: 34 us
  starting transfers between devices  15.1 us (44%)
  waiting for transfers between devices  12.1 us (35%)
  Pallas kernels  5.96 us (17%)
  between operations  0.76 us (2%)
    ppermute x8, starting transfers between devices, along_columns(): arrived.append(lax.ppermute(block, ('gx', 'gy'), pairs))  10.5 us
    ppermute x8, waiting for transfers between devices, along_columns(): arrived.append(lax.ppermute(block, ('gx', 'gy'), pairs))  8.93 us
    ppermute x10, starting transfers between devices, flip_core(): return lax.ppermute(block, 'gy', [(0, 1), (1, 0)])  4.55 us
    ppermute x10, waiting for transfers between devices, flip_core(): return lax.ppermute(block, 'gy', [(0, 1), (1, 0)])  3.16 us
    pallas_call x1, Pallas kernels, make_output(): pl.pallas_call(functools.partial(output_kernel, layers), out_specs=pl.Blo...  2.29 us
    pallas_call x1, Pallas kernels, forward_y(): pl.pallas_call(functools.partial(forward_y_kernel, extent, rows_ky), in_s...  1.75 us
    pallas_call x1, Pallas kernels, mix(): pl.pallas_call(functools.partial(mix_kernel, layers), out_shape=[jax.Shap...  1.06 us
    pallas_call x1, Pallas kernels, keep_rows(): pl.pallas_call(keep_kernel, out_shape=[jax.ShapeDtypeStruct((1, rows // 2...  0.79 us
  transfers between devices with their start and end apart: 18, of which 11 were waited for; matrix products, arithmetic and copies ran while one was open for 0% of the time, Pallas kernels for 2%

profile of v23, /device:TPU:0, one launch (start us, length us, event | category | flops | bytes accessed | tf_op | source)
XLA Modules:
  0.0 34.0 jit_solution(7122202619180583179)
XLA Ops:
  0.6 1.7 %forward_y.1 = (f32[4,2,16,512]{3,2,1,0:T(8,128)S(1)}, f32[4,2,16,512]{3,2,1,0:T(8,128)S(1)}) custom-call(bf16[4,256,512]{2,1,0:T(8,128)(2,1)} %flow_ref.1), custom_call_target="tpu_custom_call" | custom-call | tf_op jit(solution)/shard_map/forward_y/pallas_call | solution.py:265
  2.4 0.5 %collective-permute-start = (f32[4,2,16,512]{3,2,1,0:T(8,128)S(1)}, f32[4,2,16,512]{3,2,1,0:T(8,128)S(1)}, u32[]{:S(2)}, u32[]{:S(2)}) collective-permute-start(f32[4,2,16,512]{3,2,1,0:T(8,128)S(1)} %get-tuple-element.17), channel_id=1, source_target_pairs={{0,1},{1,0},{2,3},{3,2},{4,5},{5,4},{6,7},{7,6},{8,9},{9,8},{10,11... | collective-permute-start | bytes 786440 | tf_op jit(solution)/shard_map/ppermute | solution.py:279
  2.9 1.2 %collective-permute-done.arrived_ref = f32[4,2,16,512]{3,2,1,0:T(8,128)S(1)} collective-permute-done((f32[4,2,16,512]{3,2,1,0:T(8,128)S(1)}, f32[4,2,16,512]{3,2,1,0:T(8,128)S(1)}, u32[]{:S(2)}, u32[]{:S(2)}) %collective-permute-start) | collective-permute-done | bytes 262176 | tf_op jit(solution)/shard_map/ppermute | solution.py:279
  4.1 5.0 %collective-permute-start.1 = (f32[2,16,512]{2,1,0:T(8,128)S(1)}, f32[2,16,512]{2,1,0:T(8,128)S(1)}, u32[]{:S(2)}, u32[]{:S(2)}) collective-permute-start(f32[2,16,512]{2,1,0:T(8,128)S(1)} %get-tuple-element.18), channel_id=1, source_target_pairs={{0,12},{1,15},{2,14},{3,13},{4,8},{5,11},{6,10},{7,9},{8,4},{9,7},... | collective-permute-start | bytes 196616 | tf_op jit(solution)/shard_map/ppermute | solution.py:290
  9.2 0.6 %collective-permute-start.3 = (f32[2,16,512]{2,1,0:T(8,128)S(1)}, f32[2,16,512]{2,1,0:T(8,128)S(1)}, u32[]{:S(2)}, u32[]{:S(2)}) collective-permute-start(f32[2,16,512]{2,1,0:T(8,128)S(1)} %get-tuple-element.20), channel_id=1, source_target_pairs={{0,4},{1,7},{2,6},{3,5},{4,0},{5,3},{6,2},{7,1},{8,12},{9,15},{10,... | collective-permute-start | bytes 196616 | tf_op jit(solution)/shard_map/ppermute | solution.py:290
  9.8 0.7 %collective-permute-start.4 = (f32[2,16,512]{2,1,0:T(8,128)S(1)}, f32[2,16,512]{2,1,0:T(8,128)S(1)}, u32[]{:S(2)}, u32[]{:S(2)}) collective-permute-start(f32[2,16,512]{2,1,0:T(8,128)S(1)} %get-tuple-element.21), channel_id=1, source_target_pairs={{0,0},{1,3},{2,2},{3,1},{4,4},{5,7},{6,6},{7,5},{8,8},{9,11},{10,1... | collective-permute-start | bytes 196616 | tf_op jit(solution)/shard_map/ppermute | solution.py:290
  10.4 1.4 %collective-permute-done.1.block_ref.refs_0_ = f32[2,16,512]{2,1,0:T(8,128)S(1)} collective-permute-done((f32[2,16,512]{2,1,0:T(8,128)S(1)}, f32[2,16,512]{2,1,0:T(8,128)S(1)}, u32[]{:S(2)}, u32[]{:S(2)}) %collective-permute-start.1) | collective-permute-done | bytes 65568 | tf_op jit(solution)/shard_map/ppermute | solution.py:290
  11.9 1.6 %collective-permute-start.5 = (f32[16,512]{1,0:T(8,128)S(1)}, f32[16,512]{1,0:T(8,128)S(1)}, u32[]{:S(2)}, u32[]{:S(2)}) collective-permute-start(f32[16,512]{1,0:T(8,128)S(1)} %second_half.4), channel_id=1, source_target_pairs={{0,1},{1,0},{2,3},{3,2},{4,5},{5,4},{6,7},{7,6},{8,9},{9,8},{10,11... | collective-permute-start | bytes 98312 | tf_op jit(solution)/shard_map/ppermute | solution.py:279
  13.5 2.2 %collective-permute-done.2.block_ref.refs_1_ = f32[2,16,512]{2,1,0:T(8,128)S(1)} collective-permute-done((f32[2,16,512]{2,1,0:T(8,128)S(1)}, f32[2,16,512]{2,1,0:T(8,128)S(1)}, u32[]{:S(2)}, u32[]{:S(2)}) %collective-permute-start.2) | collective-permute-done | bytes 65568 | tf_op jit(solution)/shard_map/ppermute | solution.py:290
  15.6 0.4 %collective-permute-start.6 = (f32[16,512]{1,0:T(8,128)S(1)}, f32[16,512]{1,0:T(8,128)S(1)}, u32[]{:S(2)}, u32[]{:S(2)}) collective-permute-start(f32[16,512]{1,0:T(8,128)S(1)} %second_half.5), channel_id=1, source_target_pairs={{0,1},{1,0},{2,3},{3,2},{4,5},{5,4},{6,7},{7,6},{8,9},{9,8},{10,11... | collective-permute-start | bytes 98312 | tf_op jit(solution)/shard_map/ppermute | solution.py:279
  16.3 0.4 %collective-permute-start.8 = (f32[16,512]{1,0:T(8,128)S(1)}, f32[16,512]{1,0:T(8,128)S(1)}, u32[]{:S(2)}, u32[]{:S(2)}) collective-permute-start(f32[16,512]{1,0:T(8,128)S(1)} %second_half.7), channel_id=1, source_target_pairs={{0,1},{1,0},{2,3},{3,2},{4,5},{5,4},{6,7},{7,6},{8,9},{9,8},{10,11... | collective-permute-start | bytes 98312 | tf_op jit(solution)/shard_map/ppermute | solution.py:279
  16.9 0.5 %collective-permute-done.7.refs_6_ = f32[16,512]{1,0:T(8,128)S(1)} collective-permute-done((f32[16,512]{1,0:T(8,128)S(1)}, f32[16,512]{1,0:T(8,128)S(1)}, u32[]{:S(2)}, u32[]{:S(2)}) %collective-permute-start.7) | collective-permute-done | bytes 32800 | tf_op jit(solution)/shard_map/ppermute | solution.py:279
  17.6 1.1 %mix.1 = (f32[128,512]{1,0:T(8,128)S(1)}, f32[4,16,512]{2,1,0:T(8,128)S(1)}) custom-call(f32[2,16,512]{2,1,0:T(8,128)S(1)} %collective-permute-done.1.block_ref.refs_0_, f32[2,16,512]{2,1,0:T(8,128)S(1)} %collective-permute-done.2.block_ref.refs_1_, f32[2,16,512]{2,1,0:T(8,128)S(1)} %collective-permute-done.3.block_ref.refs_2_, ...), custom_call_target="tpu_custom_call" | custom-call | tf_op jit(solution)/shard_map/mix/pallas_call | solution.py:407
  18.7 0.4 %collective-permute-start.9 = (f32[4,16,512]{2,1,0:T(8,128)S(1)}, f32[4,16,512]{2,1,0:T(8,128)S(1)}, u32[]{:S(2)}, u32[]{:S(2)}) collective-permute-start(f32[4,16,512]{2,1,0:T(8,128)S(1)} %get-tuple-element.24), channel_id=1, source_target_pairs={{0,1},{1,0},{2,3},{3,2},{4,5},{5,4},{6,7},{7,6},{8,9},{9,8},{10,11... | collective-permute-start | bytes 393224 | tf_op jit(solution)/shard_map/ppermute | solution.py:279
  19.1 0.8 %keep_rows.1 = (f32[1,64,1024]{2,1,0:T(8,128)}, f32[4,16,512]{2,1,0:T(8,128)S(1)}) custom-call(f32[128,512]{1,0:T(8,128)S(1)} %get-tuple-element.22.modes_ref, bf16[2,64,128]{2,1,0:T(8,128)(2,1)S(1)} %copy-done.4, bf16[2,64,128]{2,1,0:T(8,128)(2,1)S(1)} %copy-done.3), custom_call_target="tpu_custom_call" | custom-call | tf_op jit(solution)/shard_map/keep_rows/pallas_call | solution.py:434
  20.1 1.1 %collective-permute-start.10 = (f32[4,8,512]{2,1,0:T(8,128)S(1)}, f32[4,8,512]{2,1,0:T(8,128)S(1)}, u32[]{:S(2)}, u32[]{:S(2)}) collective-permute-start(f32[4,8,512]{2,1,0:T(8,128)S(1)} %get-tuple-element.25), channel_id=1, source_target_pairs={{0,8},{1,11},{2,10},{3,9},{4,12},{5,15},{6,14},{7,13},{8,0},{9,3},... | collective-permute-start | bytes 196616 | tf_op jit(solution)/shard_map/ppermute | solution.py:290
  21.2 2.2 %collective-permute-start.11 = (f32[4,8,512]{2,1,0:T(8,128)S(1)}, f32[4,8,512]{2,1,0:T(8,128)S(1)}, u32[]{:S(2)}, u32[]{:S(2)}) collective-permute-start(f32[4,8,512]{2,1,0:T(8,128)S(1)} %get-tuple-element.26), channel_id=1, source_target_pairs={{0,12},{1,15},{2,14},{3,13},{4,8},{5,11},{6,10},{7,9},{8,4},{9,7},... | collective-permute-start | bytes 196616 | tf_op jit(solution)/shard_map/ppermute | solution.py:290
  23.7 0.7 %collective-permute-start.13 = (f32[4,8,512]{2,1,0:T(8,128)S(1)}, f32[4,8,512]{2,1,0:T(8,128)S(1)}, u32[]{:S(2)}, u32[]{:S(2)}) collective-permute-start(f32[4,8,512]{2,1,0:T(8,128)S(1)} %get-tuple-element.28), channel_id=1, source_target_pairs={{0,0},{1,3},{2,2},{3,1},{4,4},{5,7},{6,6},{7,5},{8,8},{9,11},{10,1... | collective-permute-start | bytes 196616 | tf_op jit(solution)/shard_map/ppermute | solution.py:290
  24.4 4.5 %collective-permute-done.10.refs_0_ = f32[4,8,512]{2,1,0:T(8,128)S(1)} collective-permute-done((f32[4,8,512]{2,1,0:T(8,128)S(1)}, f32[4,8,512]{2,1,0:T(8,128)S(1)}, u32[]{:S(2)}, u32[]{:S(2)}) %collective-permute-start.10) | collective-permute-done | bytes 65568 | tf_op jit(solution)/shard_map/ppermute | solution.py:290
  28.9 0.5 %collective-permute-start.15 = (f32[4,8,512]{2,1,0:T(8,128)S(1)}, f32[4,8,512]{2,1,0:T(8,128)S(1)}, u32[]{:S(2)}, u32[]{:S(2)}) collective-permute-start(f32[4,8,512]{2,1,0:T(8,128)S(1)} %collective-permute-done.11.refs_1_), channel_id=1, source_target_pairs={{0,1},{1,0},{2,3},{3,2},{4,5},{5,4},{6,7},{7,6},{8,9},{9,8},{10,11... | collective-permute-start | bytes 196616 | tf_op jit(solution)/shard_map/ppermute | solution.py:279
  29.4 0.8 %collective-permute-done.12.refs_2_ = f32[4,8,512]{2,1,0:T(8,128)S(1)} collective-permute-done((f32[4,8,512]{2,1,0:T(8,128)S(1)}, f32[4,8,512]{2,1,0:T(8,128)S(1)}, u32[]{:S(2)}, u32[]{:S(2)}) %collective-permute-start.12) | collective-permute-done | bytes 65568 | tf_op jit(solution)/shard_map/ppermute | solution.py:290
  30.4 0.3 collective-permute-start.17
  30.7 0.7 %collective-permute-done.16.refs_6_ = f32[4,8,512]{2,1,0:T(8,128)S(1)} collective-permute-done((f32[4,8,512]{2,1,0:T(8,128)S(1)}, f32[4,8,512]{2,1,0:T(8,128)S(1)}, u32[]{:S(2)}, u32[]{:S(2)}) %collective-permute-start.16) | collective-permute-done | bytes 65568 | tf_op jit(solution)/shard_map/ppermute | solution.py:279
  31.7 2.3 %make_output.1 = bf16[4,256,512]{2,1,0:T(8,128)(2,1)} custom-call(bf16[4,256,512]{2,1,0:T(8,128)(2,1)S(1)} %copy-done, bf16[2,2,256,256]{3,2,1,0:T(8,128)(2,1)S(1)} %copy-done.2, bf16[64,64]{1,0:T(8,128)(2,1)S(1)} %copy-done.7, f32[64]{0:T(128)S(1)} %copy-done.8, f32[4,8,512]{2,1,0:T(8,128)S(1)} %collective-permute-done.10.refs_0_, ...), custom_call_target="tpu_custom_call" | custom-call | tf_op jit(solution)/shard_map/make_output/pallas_call | solution.py:498
  (40 shorter events, 1.6 us)
Async XLA Ops:
  0.6 17.0 %copy-start.1 = (bf16[1,64,64,128]{3,2,1,0:T(8,128)(2,1)S(1)}, bf16[1,64,64,128]{3,2,1,0:T(8,128)(2,1)}, u32[]{:S(2)}) copy-start(bf16[1,64,64,128]{3,2,1,0:T(8,128)(2,1)} %refs_8_.1) | copy-start | bytes 3145732
  2.4 1.7 %collective-permute-start = (f32[4,2,16,512]{3,2,1,0:T(8,128)S(1)}, f32[4,2,16,512]{3,2,1,0:T(8,128)S(1)}, u32[]{:S(2)}, u32[]{:S(2)}) collective-permute-start(f32[4,2,16,512]{3,2,1,0:T(8,128)S(1)} %get-tuple-element.17), channel_id=1, source_target_pairs={{0,1},{1,0},{2,3},{3,2},{4,5},{5,4},{6,7},{7,6},{8,9},{9,8},{10,11... | collective-permute-start | bytes 786440 | tf_op jit(solution)/shard_map/ppermute | solution.py:279
  4.1 7.8 %collective-permute-start.1 = (f32[2,16,512]{2,1,0:T(8,128)S(1)}, f32[2,16,512]{2,1,0:T(8,128)S(1)}, u32[]{:S(2)}, u32[]{:S(2)}) collective-permute-start(f32[2,16,512]{2,1,0:T(8,128)S(1)} %get-tuple-element.18), channel_id=1, source_target_pairs={{0,12},{1,15},{2,14},{3,13},{4,8},{5,11},{6,10},{7,9},{8,4},{9,7},... | collective-permute-start | bytes 196616 | tf_op jit(solution)/shard_map/ppermute | solution.py:290
  9.1 6.5 %collective-permute-start.2 = (f32[2,16,512]{2,1,0:T(8,128)S(1)}, f32[2,16,512]{2,1,0:T(8,128)S(1)}, u32[]{:S(2)}, u32[]{:S(2)}) collective-permute-start(f32[2,16,512]{2,1,0:T(8,128)S(1)} %get-tuple-element.19), channel_id=1, source_target_pairs={{0,8},{1,11},{2,10},{3,9},{4,12},{5,15},{6,14},{7,13},{8,0},{9,3},... | collective-permute-start | bytes 196616 | tf_op jit(solution)/shard_map/ppermute | solution.py:290
  9.2 6.9 %collective-permute-start.3 = (f32[2,16,512]{2,1,0:T(8,128)S(1)}, f32[2,16,512]{2,1,0:T(8,128)S(1)}, u32[]{:S(2)}, u32[]{:S(2)}) collective-permute-start(f32[2,16,512]{2,1,0:T(8,128)S(1)} %get-tuple-element.20), channel_id=1, source_target_pairs={{0,4},{1,7},{2,6},{3,5},{4,0},{5,3},{6,2},{7,1},{8,12},{9,15},{10,... | collective-permute-start | bytes 196616 | tf_op jit(solution)/shard_map/ppermute | solution.py:290
  9.8 6.5 %collective-permute-start.4 = (f32[2,16,512]{2,1,0:T(8,128)S(1)}, f32[2,16,512]{2,1,0:T(8,128)S(1)}, u32[]{:S(2)}, u32[]{:S(2)}) collective-permute-start(f32[2,16,512]{2,1,0:T(8,128)S(1)} %get-tuple-element.21), channel_id=1, source_target_pairs={{0,0},{1,3},{2,2},{3,1},{4,4},{5,7},{6,6},{7,5},{8,8},{9,11},{10,1... | collective-permute-start | bytes 196616 | tf_op jit(solution)/shard_map/ppermute | solution.py:290
  11.9 4.8 %collective-permute-start.5 = (f32[16,512]{1,0:T(8,128)S(1)}, f32[16,512]{1,0:T(8,128)S(1)}, u32[]{:S(2)}, u32[]{:S(2)}) collective-permute-start(f32[16,512]{1,0:T(8,128)S(1)} %second_half.4), channel_id=1, source_target_pairs={{0,1},{1,0},{2,3},{3,2},{4,5},{5,4},{6,7},{7,6},{8,9},{9,8},{10,11... | collective-permute-start | bytes 98312 | tf_op jit(solution)/shard_map/ppermute | solution.py:279
  15.6 1.2 %collective-permute-start.6 = (f32[16,512]{1,0:T(8,128)S(1)}, f32[16,512]{1,0:T(8,128)S(1)}, u32[]{:S(2)}, u32[]{:S(2)}) collective-permute-start(f32[16,512]{1,0:T(8,128)S(1)} %second_half.5), channel_id=1, source_target_pairs={{0,1},{1,0},{2,3},{3,2},{4,5},{5,4},{6,7},{7,6},{8,9},{9,8},{10,11... | collective-permute-start | bytes 98312 | tf_op jit(solution)/shard_map/ppermute | solution.py:279
  16.0 1.6 %copy-start.6 = (bf16[128,128]{1,0:T(8,128)(2,1)S(1)}, bf16[128,128]{1,0:T(8,128)(2,1)}, u32[]{:S(2)}) copy-start(bf16[128,128]{1,0:T(8,128)(2,1)} %constant.10.clone.refs_9_) | copy-start | bytes 98308
  16.1 1.3 %collective-permute-start.7 = (f32[16,512]{1,0:T(8,128)S(1)}, f32[16,512]{1,0:T(8,128)S(1)}, u32[]{:S(2)}, u32[]{:S(2)}) collective-permute-start(f32[16,512]{1,0:T(8,128)S(1)} %second_half.6), channel_id=1, source_target_pairs={{0,1},{1,0},{2,3},{3,2},{4,5},{5,4},{6,7},{7,6},{8,9},{9,8},{10,11... | collective-permute-start | bytes 98312 | tf_op jit(solution)/shard_map/ppermute | solution.py:279
  16.3 15.4 %copy-start = (bf16[4,256,512]{2,1,0:T(8,128)(2,1)S(1)}, bf16[4,256,512]{2,1,0:T(8,128)(2,1)}, u32[]{:S(2)}) copy-start(bf16[4,256,512]{2,1,0:T(8,128)(2,1)} %flow_ref.1) | copy-start | bytes 3145732
  16.3 1.3 %collective-permute-start.8 = (f32[16,512]{1,0:T(8,128)S(1)}, f32[16,512]{1,0:T(8,128)S(1)}, u32[]{:S(2)}, u32[]{:S(2)}) collective-permute-start(f32[16,512]{1,0:T(8,128)S(1)} %second_half.7), channel_id=1, source_target_pairs={{0,1},{1,0},{2,3},{3,2},{4,5},{5,4},{6,7},{7,6},{8,9},{9,8},{10,11... | collective-permute-start | bytes 98312 | tf_op jit(solution)/shard_map/ppermute | solution.py:279
  18.7 13.0 %copy-start.2 = (bf16[2,2,256,256]{3,2,1,0:T(8,128)(2,1)S(1)}, bf16[2,2,256,256]{3,2,1,0:T(8,128)(2,1)}, u32[]{:S(2)}) copy-start(bf16[2,2,256,256]{3,2,1,0:T(8,128)(2,1)} %constant.14.clone.table_ref) | copy-start | bytes 1572868
  18.7 1.4 %collective-permute-start.9 = (f32[4,16,512]{2,1,0:T(8,128)S(1)}, f32[4,16,512]{2,1,0:T(8,128)S(1)}, u32[]{:S(2)}, u32[]{:S(2)}) collective-permute-start(f32[4,16,512]{2,1,0:T(8,128)S(1)} %get-tuple-element.24), channel_id=1, source_target_pairs={{0,1},{1,0},{2,3},{3,2},{4,5},{5,4},{6,7},{7,6},{8,9},{9,8},{10,11... | collective-permute-start | bytes 393224 | tf_op jit(solution)/shard_map/ppermute | solution.py:279
  20.1 11.6 %copy-start.7 = (bf16[64,64]{1,0:T(8,128)(2,1)S(1)}, bf16[64,64]{1,0:T(8,128)(2,1)}, u32[]{:S(2)}) copy-start(bf16[64,64]{1,0:T(8,128)(2,1)} %local_ref.1) | copy-start | bytes 24580
  20.1 8.8 %collective-permute-start.10 = (f32[4,8,512]{2,1,0:T(8,128)S(1)}, f32[4,8,512]{2,1,0:T(8,128)S(1)}, u32[]{:S(2)}, u32[]{:S(2)}) collective-permute-start(f32[4,8,512]{2,1,0:T(8,128)S(1)} %get-tuple-element.25), channel_id=1, source_target_pairs={{0,8},{1,11},{2,10},{3,9},{4,12},{5,15},{6,14},{7,13},{8,0},{9,3},... | collective-permute-start | bytes 196616 | tf_op jit(solution)/shard_map/ppermute | solution.py:290
  21.2 7.7 %collective-permute-start.11 = (f32[4,8,512]{2,1,0:T(8,128)S(1)}, f32[4,8,512]{2,1,0:T(8,128)S(1)}, u32[]{:S(2)}, u32[]{:S(2)}) collective-permute-start(f32[4,8,512]{2,1,0:T(8,128)S(1)} %get-tuple-element.26), channel_id=1, source_target_pairs={{0,12},{1,15},{2,14},{3,13},{4,8},{5,11},{6,10},{7,9},{8,4},{9,7},... | collective-permute-start | bytes 196616 | tf_op jit(solution)/shard_map/ppermute | solution.py:290
  23.4 8.2 %copy-start.8 = (f32[64]{0:T(128)S(1)}, f32[64]{0:T(128)}, u32[]{:S(2)}) copy-start(f32[64]{0:T(128)} %bias_ref.1) | copy-start | bytes 772
  23.4 6.8 %collective-permute-start.12 = (f32[4,8,512]{2,1,0:T(8,128)S(1)}, f32[4,8,512]{2,1,0:T(8,128)S(1)}, u32[]{:S(2)}, u32[]{:S(2)}) collective-permute-start(f32[4,8,512]{2,1,0:T(8,128)S(1)} %get-tuple-element.27), channel_id=1, source_target_pairs={{0,4},{1,7},{2,6},{3,5},{4,0},{5,3},{6,2},{7,1},{8,12},{9,15},{10,... | collective-permute-start | bytes 196616 | tf_op jit(solution)/shard_map/ppermute | solution.py:290
  23.7 6.7 %collective-permute-start.13 = (f32[4,8,512]{2,1,0:T(8,128)S(1)}, f32[4,8,512]{2,1,0:T(8,128)S(1)}, u32[]{:S(2)}, u32[]{:S(2)}) collective-permute-start(f32[4,8,512]{2,1,0:T(8,128)S(1)} %get-tuple-element.28), channel_id=1, source_target_pairs={{0,0},{1,3},{2,2},{3,1},{4,4},{5,7},{6,6},{7,5},{8,8},{9,11},{10,1... | collective-permute-start | bytes 196616 | tf_op jit(solution)/shard_map/ppermute | solution.py:290
  28.9 1.8 %collective-permute-start.14 = (f32[4,8,512]{2,1,0:T(8,128)S(1)}, f32[4,8,512]{2,1,0:T(8,128)S(1)}, u32[]{:S(2)}, u32[]{:S(2)}) collective-permute-start(f32[4,8,512]{2,1,0:T(8,128)S(1)} %collective-permute-done.10.refs_0_), channel_id=1, source_target_pairs={{0,1},{1,0},{2,3},{3,2},{4,5},{5,4},{6,7},{7,6},{8,9},{9,8},{10,11... | collective-permute-start | bytes 196616 | tf_op jit(solution)/shard_map/ppermute | solution.py:279
  28.9 1.8 %collective-permute-start.15 = (f32[4,8,512]{2,1,0:T(8,128)S(1)}, f32[4,8,512]{2,1,0:T(8,128)S(1)}, u32[]{:S(2)}, u32[]{:S(2)}) collective-permute-start(f32[4,8,512]{2,1,0:T(8,128)S(1)} %collective-permute-done.11.refs_1_), channel_id=1, source_target_pairs={{0,1},{1,0},{2,3},{3,2},{4,5},{5,4},{6,7},{7,6},{8,9},{9,8},{10,11... | collective-permute-start | bytes 196616 | tf_op jit(solution)/shard_map/ppermute | solution.py:279
  30.2 1.3 %collective-permute-start.16 = (f32[4,8,512]{2,1,0:T(8,128)S(1)}, f32[4,8,512]{2,1,0:T(8,128)S(1)}, u32[]{:S(2)}, u32[]{:S(2)}) collective-permute-start(f32[4,8,512]{2,1,0:T(8,128)S(1)} %collective-permute-done.12.refs_2_), channel_id=1, source_target_pairs={{0,1},{1,0},{2,3},{3,2},{4,5},{5,4},{6,7},{7,6},{8,9},{9,8},{10,11... | collective-permute-start | bytes 196616 | tf_op jit(solution)/shard_map/ppermute | solution.py:279
  30.4 1.3 %collective-permute-start.17 = (f32[4,8,512]{2,1,0:T(8,128)S(1)}, f32[4,8,512]{2,1,0:T(8,128)S(1)}, u32[]{:S(2)}, u32[]{:S(2)}) collective-permute-start(f32[4,8,512]{2,1,0:T(8,128)S(1)} %collective-permute-done.13.refs_3_), channel_id=1, source_target_pairs={{0,1},{1,0},{2,3},{3,2},{4,5},{5,4},{6,7},{7,6},{8,9},{9,8},{10,11... | collective-permute-start | bytes 196616 | tf_op jit(solution)/shard_map/ppermute | solution.py:279
  (3 other events, 4.6 us)

commit v24 on v22

--- a/solution.py
+++ b/solution.py
@@ -166,7 +166,7 @@
 
 def turns(layers):
     half = layers // 2
-    return list(range(half, layers)) + list(range(half - 1, -1, -1))
+    return list(range(half, 0, -1)) + list(range(half + 1, layers)) + [0]
 
 
 def forward_x_table(cells_x, peers, rows_ky):
@@ -229,7 +229,7 @@
     row = lax.broadcasted_iota(jnp.int32, (shape[0], 1), 0)
     block = row // (2 * rows_ky)
     place = block // 2 % layers
-    turn = jnp.where(place < layers // 2, place + layers // 2, layers - 1 - place)
+    turn = jnp.where(place < layers // 2, layers // 2 - place, (place + 1) % layers)
     side = y ^ (1 - block // peers)
     owner = (side ^ (block % 2)) * peers + (z ^ turn) * 2 + (x ^ side)
     index = owner * rows_ky + row // 2 % rows_ky

time: 33.9 us -> 34.4 us (1.015)
  starting transfers between devices: 16.5 us -> 18 us
  waiting for transfers between devices: 10.5 us -> 9.57 us
    ppermute x10, starting transfers between devices: 5.42 us -> 6.6 us  [flip_core(): return lax.ppermute(block, 'gy', [(0, 1), (1, 0)])]
    ppermute x8, waiting for transfers between devices: 7.22 us -> 6.44 us  [along_columns(): arrived.append(lax.ppermute(block, ('gx', 'gy'), pairs))]
  transfers between devices with their start and end apart: 18 -> 18, of which waited for: 13 -> 11; matrix products, arithmetic and copies ran while one was open for 0% -> 0% of each run, Pallas kernels for 2% -> 2%
where the time goes in v24:
time: 34.4 us; the launch traced here: 34.3 us
  starting transfers between devices  18 us (52%)
  waiting for transfers between devices  9.57 us (28%)
  Pallas kernels  5.97 us (17%)
  between operations  0.75 us (2%)
    ppermute x8, starting transfers between devices, along_columns(): arrived.append(lax.ppermute(block, ('gx', 'gy'), pairs))  11.4 us
    ppermute x10, starting transfers between devices, flip_core(): return lax.ppermute(block, 'gy', [(0, 1), (1, 0)])  6.6 us
    ppermute x8, waiting for transfers between devices, along_columns(): arrived.append(lax.ppermute(block, ('gx', 'gy'), pairs))  6.44 us
    ppermute x10, waiting for transfers between devices, flip_core(): return lax.ppermute(block, 'gy', [(0, 1), (1, 0)])  3.12 us
    pallas_call x1, Pallas kernels, make_output(): pl.pallas_call(functools.partial(output_kernel, layers), out_specs=pl.Blo...  2.3 us
    pallas_call x1, Pallas kernels, forward_y(): pl.pallas_call(functools.partial(forward_y_kernel, extent, rows_ky), in_s...  1.75 us
    pallas_call x1, Pallas kernels, mix(): pl.pallas_call(functools.partial(mix_kernel, layers), out_shape=[jax.Shap...  1.05 us
    pallas_call x1, Pallas kernels, keep_rows(): pl.pallas_call(keep_kernel, out_shape=[jax.ShapeDtypeStruct((1, rows // 2...  0.79 us
  transfers between devices with their start and end apart: 18, of which 11 were waited for; matrix products, arithmetic and copies ran while one was open for 0% of the time, Pallas kernels for 2%

profile of v24, /device:TPU:0, one launch (start us, length us, event | category | flops | bytes accessed | tf_op | source)
XLA Modules:
  0.0 34.3 jit_solution(16158740222634250549)
XLA Ops:
  0.6 1.7 %forward_y.1 = (f32[4,2,16,512]{3,2,1,0:T(8,128)S(1)}, f32[4,2,16,512]{3,2,1,0:T(8,128)S(1)}) custom-call(bf16[4,256,512]{2,1,0:T(8,128)(2,1)} %flow_ref.1), custom_call_target="tpu_custom_call" | custom-call | tf_op jit(solution)/shard_map/forward_y/pallas_call | solution.py:263
  2.4 0.5 %collective-permute-start = (f32[4,2,16,512]{3,2,1,0:T(8,128)S(1)}, f32[4,2,16,512]{3,2,1,0:T(8,128)S(1)}, u32[]{:S(2)}, u32[]{:S(2)}) collective-permute-start(f32[4,2,16,512]{3,2,1,0:T(8,128)S(1)} %get-tuple-element.17), channel_id=1, source_target_pairs={{0,1},{1,0},{2,3},{3,2},{4,5},{5,4},{6,7},{7,6},{8,9},{9,8},{10,11... | collective-permute-start | bytes 786440 | tf_op jit(solution)/shard_map/ppermute | solution.py:277
  2.9 1.2 %collective-permute-done.arrived_ref = f32[4,2,16,512]{3,2,1,0:T(8,128)S(1)} collective-permute-done((f32[4,2,16,512]{3,2,1,0:T(8,128)S(1)}, f32[4,2,16,512]{3,2,1,0:T(8,128)S(1)}, u32[]{:S(2)}, u32[]{:S(2)}) %collective-permute-start) | collective-permute-done | bytes 262176 | tf_op jit(solution)/shard_map/ppermute | solution.py:277
  4.1 4.0 %collective-permute-start.1 = (f32[2,16,512]{2,1,0:T(8,128)S(1)}, f32[2,16,512]{2,1,0:T(8,128)S(1)}, u32[]{:S(2)}, u32[]{:S(2)}) collective-permute-start(f32[2,16,512]{2,1,0:T(8,128)S(1)} %get-tuple-element.18), channel_id=1, source_target_pairs={{0,8},{1,11},{2,10},{3,9},{4,12},{5,15},{6,14},{7,13},{8,0},{9,3},... | collective-permute-start | bytes 196616 | tf_op jit(solution)/shard_map/ppermute | solution.py:288
  8.1 1.6 %collective-permute-start.2 = (f32[2,16,512]{2,1,0:T(8,128)S(1)}, f32[2,16,512]{2,1,0:T(8,128)S(1)}, u32[]{:S(2)}, u32[]{:S(2)}) collective-permute-start(f32[2,16,512]{2,1,0:T(8,128)S(1)} %get-tuple-element.19), channel_id=1, source_target_pairs={{0,4},{1,7},{2,6},{3,5},{4,0},{5,3},{6,2},{7,1},{8,12},{9,15},{10,... | collective-permute-start | bytes 196616 | tf_op jit(solution)/shard_map/ppermute | solution.py:288
  9.7 0.7 %collective-permute-start.4 = (f32[2,16,512]{2,1,0:T(8,128)S(1)}, f32[2,16,512]{2,1,0:T(8,128)S(1)}, u32[]{:S(2)}, u32[]{:S(2)}) collective-permute-start(f32[2,16,512]{2,1,0:T(8,128)S(1)} %get-tuple-element.21), channel_id=1, source_target_pairs={{0,0},{1,3},{2,2},{3,1},{4,4},{5,7},{6,6},{7,5},{8,8},{9,11},{10,1... | collective-permute-start | bytes 196616 | tf_op jit(solution)/shard_map/ppermute | solution.py:288
  10.7 2.6 %collective-permute-start.5 = (f32[16,512]{1,0:T(8,128)S(1)}, f32[16,512]{1,0:T(8,128)S(1)}, u32[]{:S(2)}, u32[]{:S(2)}) collective-permute-start(f32[16,512]{1,0:T(8,128)S(1)} %second_half.4), channel_id=1, source_target_pairs={{0,1},{1,0},{2,3},{3,2},{4,5},{5,4},{6,7},{7,6},{8,9},{9,8},{10,11... | collective-permute-start | bytes 98312 | tf_op jit(solution)/shard_map/ppermute | solution.py:277
  13.4 0.4 %collective-permute-start.6 = (f32[16,512]{1,0:T(8,128)S(1)}, f32[16,512]{1,0:T(8,128)S(1)}, u32[]{:S(2)}, u32[]{:S(2)}) collective-permute-start(f32[16,512]{1,0:T(8,128)S(1)} %second_half.5), channel_id=1, source_target_pairs={{0,1},{1,0},{2,3},{3,2},{4,5},{5,4},{6,7},{7,6},{8,9},{9,8},{10,11... | collective-permute-start | bytes 98312 | tf_op jit(solution)/shard_map/ppermute | solution.py:277
  13.8 2.3 %collective-permute-done.3.block_ref.refs_2_ = f32[2,16,512]{2,1,0:T(8,128)S(1)} collective-permute-done((f32[2,16,512]{2,1,0:T(8,128)S(1)}, f32[2,16,512]{2,1,0:T(8,128)S(1)}, u32[]{:S(2)}, u32[]{:S(2)}) %collective-permute-start.3) | collective-permute-done | bytes 65568 | tf_op jit(solution)/shard_map/ppermute | solution.py:288
  16.4 0.4 %collective-permute-start.8 = (f32[16,512]{1,0:T(8,128)S(1)}, f32[16,512]{1,0:T(8,128)S(1)}, u32[]{:S(2)}, u32[]{:S(2)}) collective-permute-start(f32[16,512]{1,0:T(8,128)S(1)} %second_half.7), channel_id=1, source_target_pairs={{0,1},{1,0},{2,3},{3,2},{4,5},{5,4},{6,7},{7,6},{8,9},{9,8},{10,11... | collective-permute-start | bytes 98312 | tf_op jit(solution)/shard_map/ppermute | solution.py:277
  16.8 0.6 %collective-permute-done.7.refs_6_ = f32[16,512]{1,0:T(8,128)S(1)} collective-permute-done((f32[16,512]{1,0:T(8,128)S(1)}, f32[16,512]{1,0:T(8,128)S(1)}, u32[]{:S(2)}, u32[]{:S(2)}) %collective-permute-start.7) | collective-permute-done | bytes 32800 | tf_op jit(solution)/shard_map/ppermute | solution.py:277
  17.7 1.1 %mix.1 = (f32[128,512]{1,0:T(8,128)S(1)}, f32[4,16,512]{2,1,0:T(8,128)S(1)}) custom-call(f32[2,16,512]{2,1,0:T(8,128)S(1)} %collective-permute-done.1.block_ref.refs_0_, f32[2,16,512]{2,1,0:T(8,128)S(1)} %collective-permute-done.2.block_ref.refs_1_, f32[2,16,512]{2,1,0:T(8,128)S(1)} %collective-permute-done.3.block_ref.refs_2_, ...), custom_call_target="tpu_custom_call" | custom-call | tf_op jit(solution)/shard_map/mix/pallas_call | solution.py:405
  18.8 0.4 %collective-permute-start.9 = (f32[4,16,512]{2,1,0:T(8,128)S(1)}, f32[4,16,512]{2,1,0:T(8,128)S(1)}, u32[]{:S(2)}, u32[]{:S(2)}) collective-permute-start(f32[4,16,512]{2,1,0:T(8,128)S(1)} %get-tuple-element.24), channel_id=1, source_target_pairs={{0,1},{1,0},{2,3},{3,2},{4,5},{5,4},{6,7},{7,6},{8,9},{9,8},{10,11... | collective-permute-start | bytes 393224 | tf_op jit(solution)/shard_map/ppermute | solution.py:277
  19.2 0.8 %keep_rows.1 = (f32[1,64,1024]{2,1,0:T(8,128)}, f32[4,16,512]{2,1,0:T(8,128)S(1)}) custom-call(f32[128,512]{1,0:T(8,128)S(1)} %get-tuple-element.22.modes_ref, bf16[2,64,128]{2,1,0:T(8,128)(2,1)S(1)} %copy-done.4, bf16[2,64,128]{2,1,0:T(8,128)(2,1)S(1)} %copy-done.3), custom_call_target="tpu_custom_call" | custom-call | tf_op jit(solution)/shard_map/keep_rows/pallas_call | solution.py:432
  20.2 2.1 %collective-permute-start.10 = (f32[4,8,512]{2,1,0:T(8,128)S(1)}, f32[4,8,512]{2,1,0:T(8,128)S(1)}, u32[]{:S(2)}, u32[]{:S(2)}) collective-permute-start(f32[4,8,512]{2,1,0:T(8,128)S(1)} %get-tuple-element.25), channel_id=1, source_target_pairs={{0,8},{1,11},{2,10},{3,9},{4,12},{5,15},{6,14},{7,13},{8,0},{9,3},... | collective-permute-start | bytes 196616 | tf_op jit(solution)/shard_map/ppermute | solution.py:288
  22.4 1.3 %collective-permute-start.11 = (f32[4,8,512]{2,1,0:T(8,128)S(1)}, f32[4,8,512]{2,1,0:T(8,128)S(1)}, u32[]{:S(2)}, u32[]{:S(2)}) collective-permute-start(f32[4,8,512]{2,1,0:T(8,128)S(1)} %get-tuple-element.26), channel_id=1, source_target_pairs={{0,4},{1,7},{2,6},{3,5},{4,0},{5,3},{6,2},{7,1},{8,12},{9,15},{10,... | collective-permute-start | bytes 196616 | tf_op jit(solution)/shard_map/ppermute | solution.py:288
  23.7 1.0 %collective-permute-start.12 = (f32[4,8,512]{2,1,0:T(8,128)S(1)}, f32[4,8,512]{2,1,0:T(8,128)S(1)}, u32[]{:S(2)}, u32[]{:S(2)}) collective-permute-start(f32[4,8,512]{2,1,0:T(8,128)S(1)} %get-tuple-element.27), channel_id=1, source_target_pairs={{0,12},{1,15},{2,14},{3,13},{4,8},{5,11},{6,10},{7,9},{8,4},{9,7},... | collective-permute-start | bytes 196616 | tf_op jit(solution)/shard_map/ppermute | solution.py:288
  24.7 0.7 %collective-permute-start.13 = (f32[4,8,512]{2,1,0:T(8,128)S(1)}, f32[4,8,512]{2,1,0:T(8,128)S(1)}, u32[]{:S(2)}, u32[]{:S(2)}) collective-permute-start(f32[4,8,512]{2,1,0:T(8,128)S(1)} %get-tuple-element.28), channel_id=1, source_target_pairs={{0,0},{1,3},{2,2},{3,1},{4,4},{5,7},{6,6},{7,5},{8,8},{9,11},{10,1... | collective-permute-start | bytes 196616 | tf_op jit(solution)/shard_map/ppermute | solution.py:288
  25.3 1.9 %collective-permute-done.10.refs_0_ = f32[4,8,512]{2,1,0:T(8,128)S(1)} collective-permute-done((f32[4,8,512]{2,1,0:T(8,128)S(1)}, f32[4,8,512]{2,1,0:T(8,128)S(1)}, u32[]{:S(2)}, u32[]{:S(2)}) %collective-permute-start.10) | collective-permute-done | bytes 65568 | tf_op jit(solution)/shard_map/ppermute | solution.py:288
  27.2 1.0 %collective-permute-start.14 = (f32[4,8,512]{2,1,0:T(8,128)S(1)}, f32[4,8,512]{2,1,0:T(8,128)S(1)}, u32[]{:S(2)}, u32[]{:S(2)}) collective-permute-start(f32[4,8,512]{2,1,0:T(8,128)S(1)} %collective-permute-done.10.refs_0_), channel_id=1, source_target_pairs={{0,1},{1,0},{2,3},{3,2},{4,5},{5,4},{6,7},{7,6},{8,9},{9,8},{10,11... | collective-permute-start | bytes 196616 | tf_op jit(solution)/shard_map/ppermute | solution.py:277
  28.7 1.6 %collective-permute-done.12.refs_2_ = f32[4,8,512]{2,1,0:T(8,128)S(1)} collective-permute-done((f32[4,8,512]{2,1,0:T(8,128)S(1)}, f32[4,8,512]{2,1,0:T(8,128)S(1)}, u32[]{:S(2)}, u32[]{:S(2)}) %collective-permute-start.12) | collective-permute-done | bytes 65568 | tf_op jit(solution)/shard_map/ppermute | solution.py:288
  30.4 0.7 %collective-permute-start.17 = (f32[4,8,512]{2,1,0:T(8,128)S(1)}, f32[4,8,512]{2,1,0:T(8,128)S(1)}, u32[]{:S(2)}, u32[]{:S(2)}) collective-permute-start(f32[4,8,512]{2,1,0:T(8,128)S(1)} %collective-permute-done.13.refs_3_), channel_id=1, source_target_pairs={{0,1},{1,0},{2,3},{3,2},{4,5},{5,4},{6,7},{7,6},{8,9},{9,8},{10,11... | collective-permute-start | bytes 196616 | tf_op jit(solution)/shard_map/ppermute | solution.py:277
  31.5 0.5 %collective-permute-done.17.refs_7_ = f32[4,8,512]{2,1,0:T(8,128)S(1)} collective-permute-done((f32[4,8,512]{2,1,0:T(8,128)S(1)}, f32[4,8,512]{2,1,0:T(8,128)S(1)}, u32[]{:S(2)}, u32[]{:S(2)}) %collective-permute-start.17) | collective-permute-done | bytes 65568 | tf_op jit(solution)/shard_map/ppermute | solution.py:277
  32.0 2.3 %make_output.1 = bf16[4,256,512]{2,1,0:T(8,128)(2,1)} custom-call(bf16[4,256,512]{2,1,0:T(8,128)(2,1)S(1)} %copy-done, bf16[2,2,256,256]{3,2,1,0:T(8,128)(2,1)S(1)} %copy-done.2, bf16[64,64]{1,0:T(8,128)(2,1)S(1)} %copy-done.7, f32[64]{0:T(128)S(1)} %copy-done.8, f32[4,8,512]{2,1,0:T(8,128)S(1)} %collective-permute-done.10.refs_0_, ...), custom_call_target="tpu_custom_call" | custom-call | tf_op jit(solution)/shard_map/make_output/pallas_call | solution.py:496
  (40 shorter events, 2.1 us)
Async XLA Ops:
  0.6 17.0 %copy-start.1 = (bf16[1,64,64,128]{3,2,1,0:T(8,128)(2,1)S(1)}, bf16[1,64,64,128]{3,2,1,0:T(8,128)(2,1)}, u32[]{:S(2)}) copy-start(bf16[1,64,64,128]{3,2,1,0:T(8,128)(2,1)} %refs_8_.1) | copy-start | bytes 3145732
  2.4 1.7 %collective-permute-start = (f32[4,2,16,512]{3,2,1,0:T(8,128)S(1)}, f32[4,2,16,512]{3,2,1,0:T(8,128)S(1)}, u32[]{:S(2)}, u32[]{:S(2)}) collective-permute-start(f32[4,2,16,512]{3,2,1,0:T(8,128)S(1)} %get-tuple-element.17), channel_id=1, source_target_pairs={{0,1},{1,0},{2,3},{3,2},{4,5},{5,4},{6,7},{7,6},{8,9},{9,8},{10,11... | collective-permute-start | bytes 786440 | tf_op jit(solution)/shard_map/ppermute | solution.py:277
  4.1 6.6 %collective-permute-start.1 = (f32[2,16,512]{2,1,0:T(8,128)S(1)}, f32[2,16,512]{2,1,0:T(8,128)S(1)}, u32[]{:S(2)}, u32[]{:S(2)}) collective-permute-start(f32[2,16,512]{2,1,0:T(8,128)S(1)} %get-tuple-element.18), channel_id=1, source_target_pairs={{0,8},{1,11},{2,10},{3,9},{4,12},{5,15},{6,14},{7,13},{8,0},{9,3},... | collective-permute-start | bytes 196616 | tf_op jit(solution)/shard_map/ppermute | solution.py:288
  8.1 5.3 %collective-permute-start.2 = (f32[2,16,512]{2,1,0:T(8,128)S(1)}, f32[2,16,512]{2,1,0:T(8,128)S(1)}, u32[]{:S(2)}, u32[]{:S(2)}) collective-permute-start(f32[2,16,512]{2,1,0:T(8,128)S(1)} %get-tuple-element.19), channel_id=1, source_target_pairs={{0,4},{1,7},{2,6},{3,5},{4,0},{5,3},{6,2},{7,1},{8,12},{9,15},{10,... | collective-permute-start | bytes 196616 | tf_op jit(solution)/shard_map/ppermute | solution.py:288
  9.7 6.4 %collective-permute-start.3 = (f32[2,16,512]{2,1,0:T(8,128)S(1)}, f32[2,16,512]{2,1,0:T(8,128)S(1)}, u32[]{:S(2)}, u32[]{:S(2)}) collective-permute-start(f32[2,16,512]{2,1,0:T(8,128)S(1)} %get-tuple-element.20), channel_id=1, source_target_pairs={{0,12},{1,15},{2,14},{3,13},{4,8},{5,11},{6,10},{7,9},{8,4},{9,7},... | collective-permute-start | bytes 196616 | tf_op jit(solution)/shard_map/ppermute | solution.py:288
  9.7 6.6 %collective-permute-start.4 = (f32[2,16,512]{2,1,0:T(8,128)S(1)}, f32[2,16,512]{2,1,0:T(8,128)S(1)}, u32[]{:S(2)}, u32[]{:S(2)}) collective-permute-start(f32[2,16,512]{2,1,0:T(8,128)S(1)} %get-tuple-element.21), channel_id=1, source_target_pairs={{0,0},{1,3},{2,2},{3,1},{4,4},{5,7},{6,6},{7,5},{8,8},{9,11},{10,1... | collective-permute-start | bytes 196616 | tf_op jit(solution)/shard_map/ppermute | solution.py:288
  10.7 6.1 %collective-permute-start.5 = (f32[16,512]{1,0:T(8,128)S(1)}, f32[16,512]{1,0:T(8,128)S(1)}, u32[]{:S(2)}, u32[]{:S(2)}) collective-permute-start(f32[16,512]{1,0:T(8,128)S(1)} %second_half.4), channel_id=1, source_target_pairs={{0,1},{1,0},{2,3},{3,2},{4,5},{5,4},{6,7},{7,6},{8,9},{9,8},{10,11... | collective-permute-start | bytes 98312 | tf_op jit(solution)/shard_map/ppermute | solution.py:277
  13.4 3.4 %collective-permute-start.6 = (f32[16,512]{1,0:T(8,128)S(1)}, f32[16,512]{1,0:T(8,128)S(1)}, u32[]{:S(2)}, u32[]{:S(2)}) collective-permute-start(f32[16,512]{1,0:T(8,128)S(1)} %second_half.5), channel_id=1, source_target_pairs={{0,1},{1,0},{2,3},{3,2},{4,5},{5,4},{6,7},{7,6},{8,9},{9,8},{10,11... | collective-permute-start | bytes 98312 | tf_op jit(solution)/shard_map/ppermute | solution.py:277
  16.1 1.6 %copy-start.6 = (bf16[128,128]{1,0:T(8,128)(2,1)S(1)}, bf16[128,128]{1,0:T(8,128)(2,1)}, u32[]{:S(2)}) copy-start(bf16[128,128]{1,0:T(8,128)(2,1)} %constant.10.clone.refs_9_) | copy-start | bytes 98308
  16.2 1.3 %collective-permute-start.7 = (f32[16,512]{1,0:T(8,128)S(1)}, f32[16,512]{1,0:T(8,128)S(1)}, u32[]{:S(2)}, u32[]{:S(2)}) collective-permute-start(f32[16,512]{1,0:T(8,128)S(1)} %second_half.6), channel_id=1, source_target_pairs={{0,1},{1,0},{2,3},{3,2},{4,5},{5,4},{6,7},{7,6},{8,9},{9,8},{10,11... | collective-permute-start | bytes 98312 | tf_op jit(solution)/shard_map/ppermute | solution.py:277
  16.4 15.6 %copy-start = (bf16[4,256,512]{2,1,0:T(8,128)(2,1)S(1)}, bf16[4,256,512]{2,1,0:T(8,128)(2,1)}, u32[]{:S(2)}) copy-start(bf16[4,256,512]{2,1,0:T(8,128)(2,1)} %flow_ref.1) | copy-start | bytes 3145732
  16.4 1.3 %collective-permute-start.8 = (f32[16,512]{1,0:T(8,128)S(1)}, f32[16,512]{1,0:T(8,128)S(1)}, u32[]{:S(2)}, u32[]{:S(2)}) collective-permute-start(f32[16,512]{1,0:T(8,128)S(1)} %second_half.7), channel_id=1, source_target_pairs={{0,1},{1,0},{2,3},{3,2},{4,5},{5,4},{6,7},{7,6},{8,9},{9,8},{10,11... | collective-permute-start | bytes 98312 | tf_op jit(solution)/shard_map/ppermute | solution.py:277
  18.8 13.2 %copy-start.2 = (bf16[2,2,256,256]{3,2,1,0:T(8,128)(2,1)S(1)}, bf16[2,2,256,256]{3,2,1,0:T(8,128)(2,1)}, u32[]{:S(2)}) copy-start(bf16[2,2,256,256]{3,2,1,0:T(8,128)(2,1)} %constant.14.clone.table_ref) | copy-start | bytes 1572868
  18.8 1.4 %collective-permute-start.9 = (f32[4,16,512]{2,1,0:T(8,128)S(1)}, f32[4,16,512]{2,1,0:T(8,128)S(1)}, u32[]{:S(2)}, u32[]{:S(2)}) collective-permute-start(f32[4,16,512]{2,1,0:T(8,128)S(1)} %get-tuple-element.24), channel_id=1, source_target_pairs={{0,1},{1,0},{2,3},{3,2},{4,5},{5,4},{6,7},{7,6},{8,9},{9,8},{10,11... | collective-permute-start | bytes 393224 | tf_op jit(solution)/shard_map/ppermute | solution.py:277
  20.2 11.8 %copy-start.7 = (bf16[64,64]{1,0:T(8,128)(2,1)S(1)}, bf16[64,64]{1,0:T(8,128)(2,1)}, u32[]{:S(2)}) copy-start(bf16[64,64]{1,0:T(8,128)(2,1)} %local_ref.1) | copy-start | bytes 24580
  20.2 7.0 %collective-permute-start.10 = (f32[4,8,512]{2,1,0:T(8,128)S(1)}, f32[4,8,512]{2,1,0:T(8,128)S(1)}, u32[]{:S(2)}, u32[]{:S(2)}) collective-permute-start(f32[4,8,512]{2,1,0:T(8,128)S(1)} %get-tuple-element.25), channel_id=1, source_target_pairs={{0,8},{1,11},{2,10},{3,9},{4,12},{5,15},{6,14},{7,13},{8,0},{9,3},... | collective-permute-start | bytes 196616 | tf_op jit(solution)/shard_map/ppermute | solution.py:288
  22.4 6.2 %collective-permute-start.11 = (f32[4,8,512]{2,1,0:T(8,128)S(1)}, f32[4,8,512]{2,1,0:T(8,128)S(1)}, u32[]{:S(2)}, u32[]{:S(2)}) collective-permute-start(f32[4,8,512]{2,1,0:T(8,128)S(1)} %get-tuple-element.26), channel_id=1, source_target_pairs={{0,4},{1,7},{2,6},{3,5},{4,0},{5,3},{6,2},{7,1},{8,12},{9,15},{10,... | collective-permute-start | bytes 196616 | tf_op jit(solution)/shard_map/ppermute | solution.py:288
  23.7 8.3 %copy-start.8 = (f32[64]{0:T(128)S(1)}, f32[64]{0:T(128)}, u32[]{:S(2)}) copy-start(f32[64]{0:T(128)} %bias_ref.1) | copy-start | bytes 772
  23.7 6.5 %collective-permute-start.12 = (f32[4,8,512]{2,1,0:T(8,128)S(1)}, f32[4,8,512]{2,1,0:T(8,128)S(1)}, u32[]{:S(2)}, u32[]{:S(2)}) collective-permute-start(f32[4,8,512]{2,1,0:T(8,128)S(1)} %get-tuple-element.27), channel_id=1, source_target_pairs={{0,12},{1,15},{2,14},{3,13},{4,8},{5,11},{6,10},{7,9},{8,4},{9,7},... | collective-permute-start | bytes 196616 | tf_op jit(solution)/shard_map/ppermute | solution.py:288
  24.7 5.7 %collective-permute-start.13 = (f32[4,8,512]{2,1,0:T(8,128)S(1)}, f32[4,8,512]{2,1,0:T(8,128)S(1)}, u32[]{:S(2)}, u32[]{:S(2)}) collective-permute-start(f32[4,8,512]{2,1,0:T(8,128)S(1)} %get-tuple-element.28), channel_id=1, source_target_pairs={{0,0},{1,3},{2,2},{3,1},{4,4},{5,7},{6,6},{7,5},{8,8},{9,11},{10,1... | collective-permute-start | bytes 196616 | tf_op jit(solution)/shard_map/ppermute | solution.py:288
  27.2 3.8 %collective-permute-start.14 = (f32[4,8,512]{2,1,0:T(8,128)S(1)}, f32[4,8,512]{2,1,0:T(8,128)S(1)}, u32[]{:S(2)}, u32[]{:S(2)}) collective-permute-start(f32[4,8,512]{2,1,0:T(8,128)S(1)} %collective-permute-done.10.refs_0_), channel_id=1, source_target_pairs={{0,1},{1,0},{2,3},{3,2},{4,5},{5,4},{6,7},{7,6},{8,9},{9,8},{10,11... | collective-permute-start | bytes 196616 | tf_op jit(solution)/shard_map/ppermute | solution.py:277
  28.6 2.5 %collective-permute-start.15 = (f32[4,8,512]{2,1,0:T(8,128)S(1)}, f32[4,8,512]{2,1,0:T(8,128)S(1)}, u32[]{:S(2)}, u32[]{:S(2)}) collective-permute-start(f32[4,8,512]{2,1,0:T(8,128)S(1)} %collective-permute-done.11.refs_1_), channel_id=1, source_target_pairs={{0,1},{1,0},{2,3},{3,2},{4,5},{5,4},{6,7},{7,6},{8,9},{9,8},{10,11... | collective-permute-start | bytes 196616 | tf_op jit(solution)/shard_map/ppermute | solution.py:277
  30.2 1.3 %collective-permute-start.16 = (f32[4,8,512]{2,1,0:T(8,128)S(1)}, f32[4,8,512]{2,1,0:T(8,128)S(1)}, u32[]{:S(2)}, u32[]{:S(2)}) collective-permute-start(f32[4,8,512]{2,1,0:T(8,128)S(1)} %collective-permute-done.12.refs_2_), channel_id=1, source_target_pairs={{0,1},{1,0},{2,3},{3,2},{4,5},{5,4},{6,7},{7,6},{8,9},{9,8},{10,11... | collective-permute-start | bytes 196616 | tf_op jit(solution)/shard_map/ppermute | solution.py:277
  30.4 1.6 %collective-permute-start.17 = (f32[4,8,512]{2,1,0:T(8,128)S(1)}, f32[4,8,512]{2,1,0:T(8,128)S(1)}, u32[]{:S(2)}, u32[]{:S(2)}) collective-permute-start(f32[4,8,512]{2,1,0:T(8,128)S(1)} %collective-permute-done.13.refs_3_), channel_id=1, source_target_pairs={{0,1},{1,0},{2,3},{3,2},{4,5},{5,4},{6,7},{7,6},{8,9},{9,8},{10,11... | collective-permute-start | bytes 196616 | tf_op jit(solution)/shard_map/ppermute | solution.py:277
  (3 other events, 4.6 us)

commit v25 on v18

--- a/solution.py
+++ b/solution.py
@@ -224,8 +224,8 @@
     return jnp.dot(left, right, preferred_element_type=jnp.float32)
 
 
-def column_of(turn, x, y):
-    return x ^ y ^ (1 if turn == 0 else 0)
+def column_of(x, y):
+    return x ^ y
 
 
 def forward_y_table(shape, extent, layers, rows_ky):
@@ -236,8 +236,7 @@
     place = block // 2 % layers
     turn = jnp.where(place < layers // 2, place + layers // 2, layers - 1 - place)
     side = y ^ (1 - block // peers)
-    column = x ^ side ^ jnp.where(turn == 0, 1, 0)
-    owner = (side ^ (block % 2)) * peers + (z ^ turn) * 2 + column
+    owner = (side ^ (block % 2)) * peers + (z ^ turn) * 2 + column_of(x, side)
     index = owner * rows_ky + row // 2 % rows_ky
     y_places = lax.broadcasted_iota(jnp.int32, (1, shape[1]), 1) + y * shape[1]
     steps = (wave_number(index, MY) * y_places) & (extent - 1)
@@ -287,7 +286,7 @@
     arrived = []
     for turn, block in zip(turns(len(blocks)), blocks):
         pairs = [
-            (2 * place + core, 2 * (place ^ (2 * turn + column_of(turn, 0, core))) + core)
+            (2 * place + core, 2 * (place ^ (2 * turn + column_of(0, core))) + core)
             for place in range(peers)
             for core in range(2)
         ]
@@ -348,7 +347,7 @@
 
 def back_rows(inverse_high, inverse_low, modes, shape, other):
     z, x, y = quad()
-    places = [(column_of(turn, x, y) ^ other, z ^ turn) for turn in turns(shape[0])]
+    places = [(column_of(x, y) ^ other, z ^ turn) for turn in turns(shape[0])]
     table_high, table_low = [
         jnp.concatenate([ref[column, place] for column, place in places], axis=0)
         for ref in (inverse_high, inverse_low)
@@ -366,7 +365,7 @@
     modes_ref, send_ref, order_ref, spread_ref, result_ref = refs[layers + 6 :]
     z, x, y = quad()
     for index, turn in enumerate(turns(layers)):
-        column = column_of(turn, x, y)
+        column = column_of(x, y)
         order_ref[(z ^ turn) * 2 + column] = block_refs[index][0]
         order_ref[(z ^ turn) * 2 + (column ^ 1)] = arrived_ref[index]
     feat_count = order_ref.shape[-1]
@@ -483,13 +482,9 @@
     below = jnp.concatenate(levels + [filled], axis=0).astype(jnp.bfloat16)
     below = jnp.concatenate([below, wide_ref[...]], axis=0)
     for index, turn in enumerate(turns(own_ref.shape[0])):
-        column = column_of(turn, x, y)
+        column = column_of(x, y)
         for peer, ref in ((column, own_ref), (column ^ 1, core_ref)):
-            block = ref[index]
-            if turn == 0:
-                rows = block.shape[1] // 2
-                block = jnp.concatenate([block[:, rows:], block[:, :rows]], axis=1)
-            order_ref[:, (z ^ turn) * 2 + peer] = block
+            order_ref[:, (z ^ turn) * 2 + peer] = ref[index]
     table = table_ref[y, x ^ y]
     copies = []
     for cell in range(cells_x):

time: 35 us -> 34.2 us (0.977)
  starting transfers between devices: 17.5 us -> 13.2 us
  waiting for transfers between devices: 10.4 us -> 14 us
    ppermute x8, starting transfers between devices: 16.7 us -> 11.5 us  [along_columns(): arrived.append(lax.ppermute(block, ('gx', 'gy'), pairs))]
    ppermute x8, waiting for transfers between devices: 5.97 us -> 10.3 us  [along_columns(): arrived.append(lax.ppermute(block, ('gx', 'gy'), pairs))]
    ppermute x4, starting transfers between devices: 0.86 us -> 1.73 us  [flip_core(): return lax.ppermute(block, 'gy', [(0, 1), (1, 0)])]
    ppermute x4, waiting for transfers between devices: 4.45 us -> 3.71 us  [flip_core(): return lax.ppermute(block, 'gy', [(0, 1), (1, 0)])]
where the time goes in v25:
time: 34.2 us; the launch traced here: 34 us
  waiting for transfers between devices  14 us (41%)
  starting transfers between devices  13.2 us (39%)
  Pallas kernels  5.92 us (17%)
  between operations  0.74 us (2%)
    ppermute x8, starting transfers between devices, along_columns(): arrived.append(lax.ppermute(block, ('gx', 'gy'), pairs))  11.5 us
    ppermute x8, waiting for transfers between devices, along_columns(): arrived.append(lax.ppermute(block, ('gx', 'gy'), pairs))  10.3 us
    ppermute x4, waiting for transfers between devices, flip_core(): return lax.ppermute(block, 'gy', [(0, 1), (1, 0)])  3.71 us
    pallas_call x1, Pallas kernels, make_output(): pl.pallas_call(output_kernel, out_specs=pl.BlockSpec(memory_space=pl.ANY)...  2.26 us
    pallas_call x1, Pallas kernels, forward_y(): pl.pallas_call(functools.partial(forward_y_kernel, extent, rows_ky), in_s...  1.75 us
    ppermute x4, starting transfers between devices, flip_core(): return lax.ppermute(block, 'gy', [(0, 1), (1, 0)])  1.73 us
    pallas_call x1, Pallas kernels, mix(): pl.pallas_call(functools.partial(mix_kernel, layers), out_shape=[jax.Shap...  1.04 us
    pallas_call x1, Pallas kernels, keep_rows(): pl.pallas_call(keep_kernel, out_shape=[jax.ShapeDtypeStruct((1, rows // 2...  0.78 us
  transfers between devices with their start and end apart: 12, of which 10 were waited for; matrix products, arithmetic and copies ran while one was open for 0% of the time, Pallas kernels for 2%

profile of v25, /device:TPU:0, one launch (start us, length us, event | category | flops | bytes accessed | tf_op | source)
XLA Modules:
  0.0 34.0 jit_solution(7667758409773445498)
XLA Ops:
  0.6 1.7 %forward_y.1 = (f32[4,2,16,512]{3,2,1,0:T(8,128)S(1)}, f32[4,2,16,512]{3,2,1,0:T(8,128)S(1)}) custom-call(bf16[4,256,512]{2,1,0:T(8,128)(2,1)} %flow_ref.1), custom_call_target="tpu_custom_call" | custom-call | tf_op jit(solution)/shard_map/forward_y/pallas_call | solution.py:268
  2.4 0.5 %collective-permute-start = (f32[4,2,16,512]{3,2,1,0:T(8,128)S(1)}, f32[4,2,16,512]{3,2,1,0:T(8,128)S(1)}, u32[]{:S(2)}, u32[]{:S(2)}) collective-permute-start(f32[4,2,16,512]{3,2,1,0:T(8,128)S(1)} %get-tuple-element.17), channel_id=1, source_target_pairs={{0,1},{1,0},{2,3},{3,2},{4,5},{5,4},{6,7},{7,6},{8,9},{9,8},{10,11... | collective-permute-start | bytes 786440 | tf_op jit(solution)/shard_map/ppermute | solution.py:282
  2.9 1.2 %collective-permute-done.arrived_ref = f32[4,2,16,512]{3,2,1,0:T(8,128)S(1)} collective-permute-done((f32[4,2,16,512]{3,2,1,0:T(8,128)S(1)}, f32[4,2,16,512]{3,2,1,0:T(8,128)S(1)}, u32[]{:S(2)}, u32[]{:S(2)}) %collective-permute-start) | collective-permute-done | bytes 262176 | tf_op jit(solution)/shard_map/ppermute | solution.py:282
  4.1 4.0 %collective-permute-start.1 = (f32[2,16,512]{2,1,0:T(8,128)S(1)}, f32[2,16,512]{2,1,0:T(8,128)S(1)}, u32[]{:S(2)}, u32[]{:S(2)}) collective-permute-start(f32[2,16,512]{2,1,0:T(8,128)S(1)} %get-tuple-element.18), channel_id=1, source_target_pairs={{0,8},{1,11},{2,10},{3,9},{4,12},{5,15},{6,14},{7,13},{8,0},{9,3},... | collective-permute-start | bytes 196616 | tf_op jit(solution)/shard_map/ppermute | solution.py:293
  8.1 1.3 %collective-permute-start.2 = (f32[2,16,512]{2,1,0:T(8,128)S(1)}, f32[2,16,512]{2,1,0:T(8,128)S(1)}, u32[]{:S(2)}, u32[]{:S(2)}) collective-permute-start(f32[2,16,512]{2,1,0:T(8,128)S(1)} %get-tuple-element.19), channel_id=1, source_target_pairs={{0,12},{1,15},{2,14},{3,13},{4,8},{5,11},{6,10},{7,9},{8,4},{9,7},... | collective-permute-start | bytes 196616 | tf_op jit(solution)/shard_map/ppermute | solution.py:293
  9.5 0.2 collective-permute-start.3
  9.7 0.8 %collective-permute-start.4 = (f32[2,16,512]{2,1,0:T(8,128)S(1)}, f32[2,16,512]{2,1,0:T(8,128)S(1)}, u32[]{:S(2)}, u32[]{:S(2)}) collective-permute-start(f32[2,16,512]{2,1,0:T(8,128)S(1)} %get-tuple-element.21), channel_id=1, source_target_pairs={{0,0},{1,3},{2,2},{3,1},{4,4},{5,7},{6,6},{7,5},{8,8},{9,11},{10,1... | collective-permute-start | bytes 196616 | tf_op jit(solution)/shard_map/ppermute | solution.py:293
  10.7 4.1 %collective-permute-done.2.refs_1_ = f32[2,16,512]{2,1,0:T(8,128)S(1)} collective-permute-done((f32[2,16,512]{2,1,0:T(8,128)S(1)}, f32[2,16,512]{2,1,0:T(8,128)S(1)}, u32[]{:S(2)}, u32[]{:S(2)}) %collective-permute-start.2) | collective-permute-done | bytes 65568 | tf_op jit(solution)/shard_map/ppermute | solution.py:293
  14.8 0.7 %collective-permute-done.3.refs_2_ = f32[2,16,512]{2,1,0:T(8,128)S(1)} collective-permute-done((f32[2,16,512]{2,1,0:T(8,128)S(1)}, f32[2,16,512]{2,1,0:T(8,128)S(1)}, u32[]{:S(2)}, u32[]{:S(2)}) %collective-permute-start.3) | collective-permute-done | bytes 65568 | tf_op jit(solution)/shard_map/ppermute | solution.py:293
  15.5 0.3 collective-permute-start.5
  15.9 1.1 %collective-permute-done.5.refs_4_ = f32[4,16,512]{2,1,0:T(8,128)S(1)} collective-permute-done((f32[4,16,512]{2,1,0:T(8,128)S(1)}, f32[4,16,512]{2,1,0:T(8,128)S(1)}, u32[]{:S(2)}, u32[]{:S(2)}) %collective-permute-start.5) | collective-permute-done | bytes 131104 | tf_op jit(solution)/shard_map/ppermute | solution.py:282
  17.0 1.0 %mix.1 = (f32[128,512]{1,0:T(8,128)S(1)}, f32[4,16,512]{2,1,0:T(8,128)S(1)}) custom-call(f32[2,16,512]{2,1,0:T(8,128)S(1)} %collective-permute-done.1.refs_0_, f32[2,16,512]{2,1,0:T(8,128)S(1)} %collective-permute-done.2.refs_1_, f32[2,16,512]{2,1,0:T(8,128)S(1)} %collective-permute-done.3.refs_2_, f32[2,16,512]{2,1,0:T(8,128)S(1)} %collective-permute-done.4.refs_3_, ...), custom_call_target="tpu_custom_call" | custom-call | tf_op jit(solution)/shard_map/mix/pallas_call | solution.py:420
  18.0 0.3 collective-permute-start.6
  18.4 0.8 %keep_rows.1 = (f32[1,64,1024]{2,1,0:T(8,128)}, f32[4,16,512]{2,1,0:T(8,128)S(1)}) custom-call(f32[128,512]{1,0:T(8,128)S(1)} %get-tuple-element.22.modes_ref, bf16[2,4,16,128]{3,2,1,0:T(8,128)(2,1)S(1)} %copy-done.4, bf16[2,4,16,128]{3,2,1,0:T(8,128)(2,1)S(1)} %copy-done.3), custom_call_target="tpu_custom_call" | custom-call | tf_op jit(solution)/shard_map/keep_rows/pallas_call | solution.py:444
  19.2 0.3 collective-permute-done.6.arrived_ref
  19.5 3.0 %collective-permute-start.7 = (f32[4,8,512]{2,1,0:T(8,128)S(1)}, f32[4,8,512]{2,1,0:T(8,128)S(1)}, u32[]{:S(2)}, u32[]{:S(2)}) collective-permute-start(f32[4,8,512]{2,1,0:T(8,128)S(1)} %get-tuple-element.25), channel_id=1, source_target_pairs={{0,8},{1,11},{2,10},{3,9},{4,12},{5,15},{6,14},{7,13},{8,0},{9,3},... | collective-permute-start | bytes 196616 | tf_op jit(solution)/shard_map/ppermute | solution.py:293
  22.5 1.3 %collective-permute-start.8 = (f32[4,8,512]{2,1,0:T(8,128)S(1)}, f32[4,8,512]{2,1,0:T(8,128)S(1)}, u32[]{:S(2)}, u32[]{:S(2)}) collective-permute-start(f32[4,8,512]{2,1,0:T(8,128)S(1)} %get-tuple-element.26), channel_id=1, source_target_pairs={{0,12},{1,15},{2,14},{3,13},{4,8},{5,11},{6,10},{7,9},{8,4},{9,7},... | collective-permute-start | bytes 196616 | tf_op jit(solution)/shard_map/ppermute | solution.py:293
  23.8 0.8 %collective-permute-start.10 = (f32[4,8,512]{2,1,0:T(8,128)S(1)}, f32[4,8,512]{2,1,0:T(8,128)S(1)}, u32[]{:S(2)}, u32[]{:S(2)}) collective-permute-start(f32[4,8,512]{2,1,0:T(8,128)S(1)} %get-tuple-element.28), channel_id=1, source_target_pairs={{0,0},{1,3},{2,2},{3,1},{4,4},{5,7},{6,6},{7,5},{8,8},{9,11},{10,1... | collective-permute-start | bytes 196616 | tf_op jit(solution)/shard_map/ppermute | solution.py:293
  24.6 1.8 %collective-permute-done.7.refs_0_ = f32[4,8,512]{2,1,0:T(8,128)S(1)} collective-permute-done((f32[4,8,512]{2,1,0:T(8,128)S(1)}, f32[4,8,512]{2,1,0:T(8,128)S(1)}, u32[]{:S(2)}, u32[]{:S(2)}) %collective-permute-start.7) | collective-permute-done | bytes 65568 | tf_op jit(solution)/shard_map/ppermute | solution.py:293
  26.5 2.9 %collective-permute-done.8.refs_1_ = f32[4,8,512]{2,1,0:T(8,128)S(1)} collective-permute-done((f32[4,8,512]{2,1,0:T(8,128)S(1)}, f32[4,8,512]{2,1,0:T(8,128)S(1)}, u32[]{:S(2)}, u32[]{:S(2)}) %collective-permute-start.8) | collective-permute-done | bytes 65568 | tf_op jit(solution)/shard_map/ppermute | solution.py:293
  29.3 0.6 %collective-permute-done.9.refs_2_ = f32[4,8,512]{2,1,0:T(8,128)S(1)} collective-permute-done((f32[4,8,512]{2,1,0:T(8,128)S(1)}, f32[4,8,512]{2,1,0:T(8,128)S(1)}, u32[]{:S(2)}, u32[]{:S(2)}) %collective-permute-start.9) | collective-permute-done | bytes 65568 | tf_op jit(solution)/shard_map/ppermute | solution.py:293
  30.0 0.5 %collective-permute-start.11 = (f32[4,4,8,512]{3,2,1,0:T(8,128)S(1)}, f32[4,4,8,512]{3,2,1,0:T(8,128)S(1)}, u32[]{:S(2)}, u32[]{:S(2)}) collective-permute-start(f32[4,4,8,512]{3,2,1,0:T(8,128)S(1)} %stack_blocks.1.own_ref), channel_id=1, source_target_pairs={{0,1},{1,0},{2,3},{3,2},{4,5},{5,4},{6,7},{7,6},{8,9},{9,8},{10,11... | collective-permute-start | bytes 786440 | tf_op jit(solution)/shard_map/ppermute | solution.py:282
  30.5 1.2 %collective-permute-done.11.core_ref = f32[4,4,8,512]{3,2,1,0:T(8,128)S(1)} collective-permute-done((f32[4,4,8,512]{3,2,1,0:T(8,128)S(1)}, f32[4,4,8,512]{3,2,1,0:T(8,128)S(1)}, u32[]{:S(2)}, u32[]{:S(2)}) %collective-permute-start.11) | collective-permute-done | bytes 262176 | tf_op jit(solution)/shard_map/ppermute | solution.py:282
  31.7 2.3 %make_output.1 = bf16[4,256,512]{2,1,0:T(8,128)(2,1)} custom-call(bf16[4,256,512]{2,1,0:T(8,128)(2,1)S(1)} %copy-done, bf16[2,2,256,256]{3,2,1,0:T(8,128)(2,1)S(1)} %copy-done.2, bf16[64,64]{1,0:T(8,128)(2,1)S(1)} %copy-done.7, f32[64]{0:T(128)S(1)} %copy-done.8, f32[4,4,8,512]{3,2,1,0:T(8,128)S(1)} %stack_blocks.1.own_ref, ...), custom_call_target="tpu_custom_call" | custom-call | tf_op jit(solution)/shard_map/make_output/pallas_call | solution.py:515
  (26 shorter events, 0.4 us)
Async XLA Ops:
  0.6 16.3 %copy-start.1 = (bf16[1,64,64,128]{3,2,1,0:T(8,128)(2,1)S(1)}, bf16[1,64,64,128]{3,2,1,0:T(8,128)(2,1)}, u32[]{:S(2)}) copy-start(bf16[1,64,64,128]{3,2,1,0:T(8,128)(2,1)} %refs_5_.1) | copy-start | bytes 3145732
  2.4 1.7 %collective-permute-start = (f32[4,2,16,512]{3,2,1,0:T(8,128)S(1)}, f32[4,2,16,512]{3,2,1,0:T(8,128)S(1)}, u32[]{:S(2)}, u32[]{:S(2)}) collective-permute-start(f32[4,2,16,512]{3,2,1,0:T(8,128)S(1)} %get-tuple-element.17), channel_id=1, source_target_pairs={{0,1},{1,0},{2,3},{3,2},{4,5},{5,4},{6,7},{7,6},{8,9},{9,8},{10,11... | collective-permute-start | bytes 786440 | tf_op jit(solution)/shard_map/ppermute | solution.py:282
  4.1 6.6 %collective-permute-start.1 = (f32[2,16,512]{2,1,0:T(8,128)S(1)}, f32[2,16,512]{2,1,0:T(8,128)S(1)}, u32[]{:S(2)}, u32[]{:S(2)}) collective-permute-start(f32[2,16,512]{2,1,0:T(8,128)S(1)} %get-tuple-element.18), channel_id=1, source_target_pairs={{0,8},{1,11},{2,10},{3,9},{4,12},{5,15},{6,14},{7,13},{8,0},{9,3},... | collective-permute-start | bytes 196616 | tf_op jit(solution)/shard_map/ppermute | solution.py:293
  8.1 6.7 %collective-permute-start.2 = (f32[2,16,512]{2,1,0:T(8,128)S(1)}, f32[2,16,512]{2,1,0:T(8,128)S(1)}, u32[]{:S(2)}, u32[]{:S(2)}) collective-permute-start(f32[2,16,512]{2,1,0:T(8,128)S(1)} %get-tuple-element.19), channel_id=1, source_target_pairs={{0,12},{1,15},{2,14},{3,13},{4,8},{5,11},{6,10},{7,9},{8,4},{9,7},... | collective-permute-start | bytes 196616 | tf_op jit(solution)/shard_map/ppermute | solution.py:293
  9.5 6.0 %collective-permute-start.3 = (f32[2,16,512]{2,1,0:T(8,128)S(1)}, f32[2,16,512]{2,1,0:T(8,128)S(1)}, u32[]{:S(2)}, u32[]{:S(2)}) collective-permute-start(f32[2,16,512]{2,1,0:T(8,128)S(1)} %get-tuple-element.20), channel_id=1, source_target_pairs={{0,4},{1,7},{2,6},{3,5},{4,0},{5,3},{6,2},{7,1},{8,12},{9,15},{10,... | collective-permute-start | bytes 196616 | tf_op jit(solution)/shard_map/ppermute | solution.py:293
  9.7 7.2 %copy-start.3 = (bf16[2,4,16,128]{3,2,1,0:T(8,128)(2,1)S(1)}, bf16[2,4,16,128]{3,2,1,0:T(8,128)(2,1)}, u32[]{:S(2)}) copy-start(bf16[2,4,16,128]{3,2,1,0:T(8,128)(2,1)} %constant.13.clone.refs_9_.inverse_low) | copy-start | bytes 98308
  9.7 7.2 %copy-start.4 = (bf16[2,4,16,128]{3,2,1,0:T(8,128)(2,1)S(1)}, bf16[2,4,16,128]{3,2,1,0:T(8,128)(2,1)}, u32[]{:S(2)}) copy-start(bf16[2,4,16,128]{3,2,1,0:T(8,128)(2,1)} %constant.12.clone.refs_8_.inverse_high) | copy-start | bytes 98308
  9.7 7.3 %copy-start.5 = (bf16[128,128]{1,0:T(8,128)(2,1)S(1)}, bf16[128,128]{1,0:T(8,128)(2,1)}, u32[]{:S(2)}) copy-start(bf16[128,128]{1,0:T(8,128)(2,1)} %constant.11.clone.refs_7_) | copy-start | bytes 98308
  9.7 7.3 %copy-start.6 = (bf16[128,128]{1,0:T(8,128)(2,1)S(1)}, bf16[128,128]{1,0:T(8,128)(2,1)}, u32[]{:S(2)}) copy-start(bf16[128,128]{1,0:T(8,128)(2,1)} %constant.10.clone.refs_6_) | copy-start | bytes 98308
  9.7 5.8 %collective-permute-start.4 = (f32[2,16,512]{2,1,0:T(8,128)S(1)}, f32[2,16,512]{2,1,0:T(8,128)S(1)}, u32[]{:S(2)}, u32[]{:S(2)}) collective-permute-start(f32[2,16,512]{2,1,0:T(8,128)S(1)} %get-tuple-element.21), channel_id=1, source_target_pairs={{0,0},{1,3},{2,2},{3,1},{4,4},{5,7},{6,6},{7,5},{8,8},{9,11},{10,1... | collective-permute-start | bytes 196616 | tf_op jit(solution)/shard_map/ppermute | solution.py:293
  15.5 16.2 %copy-start = (bf16[4,256,512]{2,1,0:T(8,128)(2,1)S(1)}, bf16[4,256,512]{2,1,0:T(8,128)(2,1)}, u32[]{:S(2)}) copy-start(bf16[4,256,512]{2,1,0:T(8,128)(2,1)} %flow_ref.1) | copy-start | bytes 3145732
  15.5 1.4 %collective-permute-start.5 = (f32[4,16,512]{2,1,0:T(8,128)S(1)}, f32[4,16,512]{2,1,0:T(8,128)S(1)}, u32[]{:S(2)}, u32[]{:S(2)}) collective-permute-start(f32[4,16,512]{2,1,0:T(8,128)S(1)} %second_halves.1), channel_id=1, source_target_pairs={{0,1},{1,0},{2,3},{3,2},{4,5},{5,4},{6,7},{7,6},{8,9},{9,8},{10,11... | collective-permute-start | bytes 393224 | tf_op jit(solution)/shard_map/ppermute | solution.py:282
  18.0 1.4 %collective-permute-start.6 = (f32[4,16,512]{2,1,0:T(8,128)S(1)}, f32[4,16,512]{2,1,0:T(8,128)S(1)}, u32[]{:S(2)}, u32[]{:S(2)}) collective-permute-start(f32[4,16,512]{2,1,0:T(8,128)S(1)} %get-tuple-element.24), channel_id=1, source_target_pairs={{0,1},{1,0},{2,3},{3,2},{4,5},{5,4},{6,7},{7,6},{8,9},{9,8},{10,11... | collective-permute-start | bytes 393224 | tf_op jit(solution)/shard_map/ppermute | solution.py:282
  18.4 13.3 %copy-start.2 = (bf16[2,2,256,256]{3,2,1,0:T(8,128)(2,1)S(1)}, bf16[2,2,256,256]{3,2,1,0:T(8,128)(2,1)}, u32[]{:S(2)}) copy-start(bf16[2,2,256,256]{3,2,1,0:T(8,128)(2,1)} %constant.14.clone.table_ref) | copy-start | bytes 1572868
  19.5 7.0 %collective-permute-start.7 = (f32[4,8,512]{2,1,0:T(8,128)S(1)}, f32[4,8,512]{2,1,0:T(8,128)S(1)}, u32[]{:S(2)}, u32[]{:S(2)}) collective-permute-start(f32[4,8,512]{2,1,0:T(8,128)S(1)} %get-tuple-element.25), channel_id=1, source_target_pairs={{0,8},{1,11},{2,10},{3,9},{4,12},{5,15},{6,14},{7,13},{8,0},{9,3},... | collective-permute-start | bytes 196616 | tf_op jit(solution)/shard_map/ppermute | solution.py:293
  22.5 6.8 %collective-permute-start.8 = (f32[4,8,512]{2,1,0:T(8,128)S(1)}, f32[4,8,512]{2,1,0:T(8,128)S(1)}, u32[]{:S(2)}, u32[]{:S(2)}) collective-permute-start(f32[4,8,512]{2,1,0:T(8,128)S(1)} %get-tuple-element.26), channel_id=1, source_target_pairs={{0,12},{1,15},{2,14},{3,13},{4,8},{5,11},{6,10},{7,9},{8,4},{9,7},... | collective-permute-start | bytes 196616 | tf_op jit(solution)/shard_map/ppermute | solution.py:293
  23.8 6.1 %collective-permute-start.9 = (f32[4,8,512]{2,1,0:T(8,128)S(1)}, f32[4,8,512]{2,1,0:T(8,128)S(1)}, u32[]{:S(2)}, u32[]{:S(2)}) collective-permute-start(f32[4,8,512]{2,1,0:T(8,128)S(1)} %get-tuple-element.27), channel_id=1, source_target_pairs={{0,4},{1,7},{2,6},{3,5},{4,0},{5,3},{6,2},{7,1},{8,12},{9,15},{10,... | collective-permute-start | bytes 196616 | tf_op jit(solution)/shard_map/ppermute | solution.py:293
  23.8 7.9 %copy-start.7 = (bf16[64,64]{1,0:T(8,128)(2,1)S(1)}, bf16[64,64]{1,0:T(8,128)(2,1)}, u32[]{:S(2)}) copy-start(bf16[64,64]{1,0:T(8,128)(2,1)} %local_ref.1) | copy-start | bytes 24580
  23.8 7.9 %copy-start.8 = (f32[64]{0:T(128)S(1)}, f32[64]{0:T(128)}, u32[]{:S(2)}) copy-start(f32[64]{0:T(128)} %bias_ref.1) | copy-start | bytes 772
  23.8 6.1 %collective-permute-start.10 = (f32[4,8,512]{2,1,0:T(8,128)S(1)}, f32[4,8,512]{2,1,0:T(8,128)S(1)}, u32[]{:S(2)}, u32[]{:S(2)}) collective-permute-start(f32[4,8,512]{2,1,0:T(8,128)S(1)} %get-tuple-element.28), channel_id=1, source_target_pairs={{0,0},{1,3},{2,2},{3,1},{4,4},{5,7},{6,6},{7,5},{8,8},{9,11},{10,1... | collective-permute-start | bytes 196616 | tf_op jit(solution)/shard_map/ppermute | solution.py:293
  30.0 1.7 %collective-permute-start.11 = (f32[4,4,8,512]{3,2,1,0:T(8,128)S(1)}, f32[4,4,8,512]{3,2,1,0:T(8,128)S(1)}, u32[]{:S(2)}, u32[]{:S(2)}) collective-permute-start(f32[4,4,8,512]{3,2,1,0:T(8,128)S(1)} %stack_blocks.1.own_ref), channel_id=1, source_target_pairs={{0,1},{1,0},{2,3},{3,2},{4,5},{5,4},{6,7},{7,6},{8,9},{9,8},{10,11... | collective-permute-start | bytes 786440 | tf_op jit(solution)/shard_map/ppermute | solution.py:282

commit v26 on v25

--- a/solution.py
+++ b/solution.py
@@ -306,16 +306,6 @@
 def second_halves(blocks):
     shape = jax.ShapeDtypeStruct((len(blocks),) + blocks[0].shape[1:], blocks[0].dtype)
     return small_call(second_kernel, shape, "second_halves")(*blocks)
-
-
-def stack_kernel(*refs):
-    for index, block_ref in enumerate(refs[:-1]):
-        refs[-1][index] = block_ref[...]
-
-
-def stack_blocks(blocks):
-    shape = jax.ShapeDtypeStruct((len(blocks),) + blocks[0].shape, blocks[0].dtype)
-    return small_call(stack_kernel, shape, "stack_blocks")(*blocks)
 
 
 def add_kernel(keep_ref, arrived_ref, *out_refs):
@@ -392,10 +382,7 @@
         for start in range(0, 8, group):
             span = slice(start, start + group)
             left = jnp.concatenate([block[span], turned[span]], axis=0)[:, :channels]
-            left_high, left_low = split_terms(left)
-            left = jnp.concatenate([left_high, left_low], axis=0)
-            product = dot(left, weight_ref[0, (base + start) // group])
-            product = product[: 2 * group] + product[2 * group :]
+            product = dot(left.astype(jnp.bfloat16), weight_ref[0, (base + start) // group])
             firsts.append(product[:group])
             seconds.append(product[group:])
         first = jnp.concatenate(firsts, axis=0)
@@ -460,11 +447,10 @@
     return half + half * jnp.tanh(half * inner)
 
 
-def output_kernel(
-    flow_ref, table_ref, local_ref, bias_ref, own_ref, core_ref,
-    out_hbm, order_ref, wide_ref, level_ref, done_ref, sent,
-):
-    cells_x, cells_y, feat_count = flow_ref.shape
+def output_kernel(layers, flow_ref, table_ref, local_ref, bias_ref, *refs):
+    own_refs, core_refs = refs[:layers], refs[layers : 2 * layers]
+    out_hbm, order_ref, wide_ref, level_ref, done_ref, sent = refs[2 * layers :]
+    cells_x, _, feat_count = flow_ref.shape
     channels = local_ref.shape[0]
     z, x, y = quad()
     wide_ref[...] = jnp.zeros_like(wide_ref)
@@ -481,51 +467,44 @@
     filled = jnp.zeros((table_ref.shape[-1] - terms - BIAS_TERMS, WIDTH), jnp.float32)
     below = jnp.concatenate(levels + [filled], axis=0).astype(jnp.bfloat16)
     below = jnp.concatenate([below, wide_ref[...]], axis=0)
-    for index, turn in enumerate(turns(own_ref.shape[0])):
-        column = column_of(x, y)
-        for peer, ref in ((column, own_ref), (column ^ 1, core_ref)):
-            order_ref[:, (z ^ turn) * 2 + peer] = ref[index]
+    for column, block_refs in ((x ^ y, own_refs), (x ^ y ^ 1, core_refs)):
+        for turn, block_ref in zip(turns(layers), block_refs):
+            order_ref[:, (z ^ turn) * 2 + column] = block_ref[...]
     table = table_ref[y, x ^ y]
     copies = []
     for cell in range(cells_x):
         high, low = split_terms(order_ref[cell].reshape(-1, feat_count))
         stack = jnp.concatenate([high, low, high], axis=0)
-        bounds = [0, FIRST, cells_y] if cell == 0 else [0, cells_y]
-        for begin, end in zip(bounds[:-1], bounds[1:]):
-            rows = slice(begin, end)
-            for start in range(0, feat_count, WIDTH):
-                columns = slice(start, start + WIDTH)
-                total = dot(
-                    jnp.concatenate([table[rows], flow_ref[cell, rows, columns]], axis=1),
-                    jnp.concatenate([stack[:, columns], below], axis=0),
-                )
-                done_ref[cell, rows, columns] = gelu(total).astype(done_ref.dtype)
-            copies.append(
-                pltpu.make_async_copy(
-                    done_ref.at[cell, rows], out_hbm.at[cell, rows], sent.at[len(copies)]
-                )
+        for start in range(0, feat_count, WIDTH):
+            columns = slice(start, start + WIDTH)
+            total = dot(
+                jnp.concatenate([table, flow_ref[cell, :, columns]], axis=1),
+                jnp.concatenate([stack[:, columns], below], axis=0),
             )
-            copies[-1].start()
+            done_ref[cell, :, columns] = gelu(total).astype(done_ref.dtype)
+        copies.append(pltpu.make_async_copy(done_ref.at[cell], out_hbm.at[cell], sent.at[cell]))
+        copies[-1].start()
     for copy in copies:
         copy.wait()
 
 
-def make_output(flow_field, own, core, table, local, bias):
+def make_output(flow_field, parts, table, local, bias):
     cells_x, _, feat_count = flow_field.shape
+    layers = len(parts) // 2
     return pl.pallas_call(
-        output_kernel,
+        functools.partial(output_kernel, layers),
         out_specs=pl.BlockSpec(memory_space=pl.ANY),
         scratch_shapes=[
-            pltpu.VMEM((cells_x, 2 * own.shape[0]) + own.shape[2:], jnp.float32),
+            pltpu.VMEM((cells_x, 2 * layers) + parts[0].shape[1:], jnp.float32),
             pltpu.VMEM((WIDTH, WIDTH), jnp.bfloat16),
             pltpu.VMEM((1, WIDTH), jnp.float32),
             pltpu.VMEM(flow_field.shape, jnp.bfloat16),
-            pltpu.SemaphoreType.DMA((cells_x + 1,)),
+            pltpu.SemaphoreType.DMA((cells_x,)),
         ],
         out_shape=jax.ShapeDtypeStruct(flow_field.shape, jnp.bfloat16),
         compiler_params=SMALL,
         name="make_output",
-    )(flow_field, table, local, bias, own, core)
+    )(flow_field, table, local, bias, *parts)
 
 
 def row_body(flow_field, spectral_weight, local_weight, bias_terms):
@@ -549,9 +528,9 @@
     arrived = flip_core(send)
     mixed, keep = keep_rows(modes, inverse_tables, send)
     own = along_columns(join_blocks(keep, arrived, cells_x), peers)
-    own = stack_blocks(own)
+    parts = own + [flip_core(block) for block in own]
     table = output_table(inverse_y_table(cells_y, groups_y, peers, rows_ky) * (0.5 * inverse_scale))
-    return make_output(flow_field, own, flip_core(own), table, local_weight, bias_terms), mixed
+    return make_output(flow_field, parts, table, local_weight, bias_terms), mixed
 
 
 def body(flow_field, spectral_weight, local_weight, bias_terms):

time: 34.2 us -> 33.9 us (level)
  waiting for transfers between devices: 14 us -> 12.8 us
  starting transfers between devices: 13.2 us -> 14.2 us
    ppermute x8, waiting for transfers between devices: 10.3 us -> 9.35 us  [along_columns(): arrived.append(lax.ppermute(block, ('gx', 'gy'), pairs))]
    ppermute x4 -> x7, starting transfers between devices: 1.73 us -> 2.66 us  [flip_core(): return lax.ppermute(block, 'gy', [(0, 1), (1, 0)])]
    ppermute x4 -> x7, waiting for transfers between devices: 3.71 us -> 3.49 us  [flip_core(): return lax.ppermute(block, 'gy', [(0, 1), (1, 0)])]
    pallas_call x2 -> x1, Pallas kernels: 2.28 us -> 2.29 us  [make_output(): pl.pallas_call(functools.partial(output_kernel, layers), out_specs=pl.Blo...]
  transfers between devices with their start and end apart: 12 -> 15, of which waited for: 10 -> 12; matrix products, arithmetic and copies ran while one was open for 0% -> 0% of each run, Pallas kernels for 2% -> 2%
where the time goes in v26:
time: 33.9 us; the launch traced here: 33.7 us
  starting transfers between devices  14.2 us (42%)
  waiting for transfers between devices  12.8 us (38%)
  Pallas kernels  5.93 us (17%)
  between operations  0.75 us (2%)
    ppermute x8, starting transfers between devices, along_columns(): arrived.append(lax.ppermute(block, ('gx', 'gy'), pairs))  11.5 us
    ppermute x8, waiting for transfers between devices, along_columns(): arrived.append(lax.ppermute(block, ('gx', 'gy'), pairs))  9.35 us
    ppermute x7, waiting for transfers between devices, flip_core(): return lax.ppermute(block, 'gy', [(0, 1), (1, 0)])  3.49 us
    ppermute x7, starting transfers between devices, flip_core(): return lax.ppermute(block, 'gy', [(0, 1), (1, 0)])  2.66 us
    pallas_call x1, Pallas kernels, make_output(): pl.pallas_call(functools.partial(output_kernel, layers), out_specs=pl.Blo...  2.29 us
    pallas_call x1, Pallas kernels, forward_y(): pl.pallas_call(functools.partial(forward_y_kernel, extent, rows_ky), in_s...  1.75 us
    pallas_call x1, Pallas kernels, mix(): pl.pallas_call(functools.partial(mix_kernel, layers), out_shape=[jax.Shap...  1.03 us
    pallas_call x1, Pallas kernels, keep_rows(): pl.pallas_call(keep_kernel, out_shape=[jax.ShapeDtypeStruct((1, rows // 2...  0.78 us
  transfers between devices with their start and end apart: 15, of which 12 were waited for; matrix products, arithmetic and copies ran while one was open for 0% of the time, Pallas kernels for 2%

profile of v26, /device:TPU:0, one launch (start us, length us, event | category | flops | bytes accessed | tf_op | source)
XLA Modules:
  0.0 33.7 jit_solution(15598308089129188973)
XLA Ops:
  0.6 1.7 %forward_y.1 = (f32[4,2,16,512]{3,2,1,0:T(8,128)S(1)}, f32[4,2,16,512]{3,2,1,0:T(8,128)S(1)}) custom-call(bf16[4,256,512]{2,1,0:T(8,128)(2,1)} %flow_ref.1), custom_call_target="tpu_custom_call" | custom-call | tf_op jit(solution)/shard_map/forward_y/pallas_call | solution.py:268
  2.4 0.5 %collective-permute-start = (f32[4,2,16,512]{3,2,1,0:T(8,128)S(1)}, f32[4,2,16,512]{3,2,1,0:T(8,128)S(1)}, u32[]{:S(2)}, u32[]{:S(2)}) collective-permute-start(f32[4,2,16,512]{3,2,1,0:T(8,128)S(1)} %get-tuple-element.17), channel_id=1, source_target_pairs={{0,1},{1,0},{2,3},{3,2},{4,5},{5,4},{6,7},{7,6},{8,9},{9,8},{10,11... | collective-permute-start | bytes 786440 | tf_op jit(solution)/shard_map/ppermute | solution.py:282
  2.9 1.2 %collective-permute-done.arrived_ref = f32[4,2,16,512]{3,2,1,0:T(8,128)S(1)} collective-permute-done((f32[4,2,16,512]{3,2,1,0:T(8,128)S(1)}, f32[4,2,16,512]{3,2,1,0:T(8,128)S(1)}, u32[]{:S(2)}, u32[]{:S(2)}) %collective-permute-start) | collective-permute-done | bytes 262176 | tf_op jit(solution)/shard_map/ppermute | solution.py:282
  4.1 4.0 %collective-permute-start.1 = (f32[2,16,512]{2,1,0:T(8,128)S(1)}, f32[2,16,512]{2,1,0:T(8,128)S(1)}, u32[]{:S(2)}, u32[]{:S(2)}) collective-permute-start(f32[2,16,512]{2,1,0:T(8,128)S(1)} %get-tuple-element.18), channel_id=1, source_target_pairs={{0,8},{1,11},{2,10},{3,9},{4,12},{5,15},{6,14},{7,13},{8,0},{9,3},... | collective-permute-start | bytes 196616 | tf_op jit(solution)/shard_map/ppermute | solution.py:293
  8.1 1.3 %collective-permute-start.2 = (f32[2,16,512]{2,1,0:T(8,128)S(1)}, f32[2,16,512]{2,1,0:T(8,128)S(1)}, u32[]{:S(2)}, u32[]{:S(2)}) collective-permute-start(f32[2,16,512]{2,1,0:T(8,128)S(1)} %get-tuple-element.19), channel_id=1, source_target_pairs={{0,12},{1,15},{2,14},{3,13},{4,8},{5,11},{6,10},{7,9},{8,4},{9,7},... | collective-permute-start | bytes 196616 | tf_op jit(solution)/shard_map/ppermute | solution.py:293
  9.7 0.8 %collective-permute-start.4 = (f32[2,16,512]{2,1,0:T(8,128)S(1)}, f32[2,16,512]{2,1,0:T(8,128)S(1)}, u32[]{:S(2)}, u32[]{:S(2)}) collective-permute-start(f32[2,16,512]{2,1,0:T(8,128)S(1)} %get-tuple-element.21), channel_id=1, source_target_pairs={{0,0},{1,3},{2,2},{3,1},{4,4},{5,7},{6,6},{7,5},{8,8},{9,11},{10,1... | collective-permute-start | bytes 196616 | tf_op jit(solution)/shard_map/ppermute | solution.py:293
  10.7 4.1 %collective-permute-done.2.refs_1_ = f32[2,16,512]{2,1,0:T(8,128)S(1)} collective-permute-done((f32[2,16,512]{2,1,0:T(8,128)S(1)}, f32[2,16,512]{2,1,0:T(8,128)S(1)}, u32[]{:S(2)}, u32[]{:S(2)}) %collective-permute-start.2) | collective-permute-done | bytes 65568 | tf_op jit(solution)/shard_map/ppermute | solution.py:293
  14.8 0.7 %collective-permute-done.3.refs_2_ = f32[2,16,512]{2,1,0:T(8,128)S(1)} collective-permute-done((f32[2,16,512]{2,1,0:T(8,128)S(1)}, f32[2,16,512]{2,1,0:T(8,128)S(1)}, u32[]{:S(2)}, u32[]{:S(2)}) %collective-permute-start.3) | collective-permute-done | bytes 65568 | tf_op jit(solution)/shard_map/ppermute | solution.py:293
  15.5 0.3 collective-permute-start.5
  15.9 1.1 %collective-permute-done.5.refs_4_ = f32[4,16,512]{2,1,0:T(8,128)S(1)} collective-permute-done((f32[4,16,512]{2,1,0:T(8,128)S(1)}, f32[4,16,512]{2,1,0:T(8,128)S(1)}, u32[]{:S(2)}, u32[]{:S(2)}) %collective-permute-start.5) | collective-permute-done | bytes 131104 | tf_op jit(solution)/shard_map/ppermute | solution.py:282
  17.0 1.0 %mix.1 = (f32[128,512]{1,0:T(8,128)S(1)}, f32[4,16,512]{2,1,0:T(8,128)S(1)}) custom-call(f32[2,16,512]{2,1,0:T(8,128)S(1)} %collective-permute-done.1.refs_0_, f32[2,16,512]{2,1,0:T(8,128)S(1)} %collective-permute-done.2.refs_1_, f32[2,16,512]{2,1,0:T(8,128)S(1)} %collective-permute-done.3.refs_2_, f32[2,16,512]{2,1,0:T(8,128)S(1)} %collective-permute-done.4.refs_3_, ...), custom_call_target="tpu_custom_call" | custom-call | tf_op jit(solution)/shard_map/mix/pallas_call | solution.py:407
  18.0 0.3 collective-permute-start.6
  18.4 0.8 %keep_rows.1 = (f32[1,64,1024]{2,1,0:T(8,128)}, f32[4,16,512]{2,1,0:T(8,128)S(1)}) custom-call(f32[128,512]{1,0:T(8,128)S(1)} %get-tuple-element.22.modes_ref, bf16[2,4,16,128]{3,2,1,0:T(8,128)(2,1)S(1)} %copy-done.4, bf16[2,4,16,128]{3,2,1,0:T(8,128)(2,1)S(1)} %copy-done.3), custom_call_target="tpu_custom_call" | custom-call | tf_op jit(solution)/shard_map/keep_rows/pallas_call | solution.py:431
  19.2 0.3 collective-permute-done.6.arrived_ref
  19.5 3.0 %collective-permute-start.7 = (f32[4,8,512]{2,1,0:T(8,128)S(1)}, f32[4,8,512]{2,1,0:T(8,128)S(1)}, u32[]{:S(2)}, u32[]{:S(2)}) collective-permute-start(f32[4,8,512]{2,1,0:T(8,128)S(1)} %get-tuple-element.25), channel_id=1, source_target_pairs={{0,8},{1,11},{2,10},{3,9},{4,12},{5,15},{6,14},{7,13},{8,0},{9,3},... | collective-permute-start | bytes 196616 | tf_op jit(solution)/shard_map/ppermute | solution.py:293
  22.5 1.3 %collective-permute-start.8 = (f32[4,8,512]{2,1,0:T(8,128)S(1)}, f32[4,8,512]{2,1,0:T(8,128)S(1)}, u32[]{:S(2)}, u32[]{:S(2)}) collective-permute-start(f32[4,8,512]{2,1,0:T(8,128)S(1)} %get-tuple-element.26), channel_id=1, source_target_pairs={{0,12},{1,15},{2,14},{3,13},{4,8},{5,11},{6,10},{7,9},{8,4},{9,7},... | collective-permute-start | bytes 196616 | tf_op jit(solution)/shard_map/ppermute | solution.py:293
  23.8 0.8 %collective-permute-start.10 = (f32[4,8,512]{2,1,0:T(8,128)S(1)}, f32[4,8,512]{2,1,0:T(8,128)S(1)}, u32[]{:S(2)}, u32[]{:S(2)}) collective-permute-start(f32[4,8,512]{2,1,0:T(8,128)S(1)} %get-tuple-element.28), channel_id=1, source_target_pairs={{0,0},{1,3},{2,2},{3,1},{4,4},{5,7},{6,6},{7,5},{8,8},{9,11},{10,1... | collective-permute-start | bytes 196616 | tf_op jit(solution)/shard_map/ppermute | solution.py:293
  24.6 1.8 %collective-permute-done.7.refs_0_ = f32[4,8,512]{2,1,0:T(8,128)S(1)} collective-permute-done((f32[4,8,512]{2,1,0:T(8,128)S(1)}, f32[4,8,512]{2,1,0:T(8,128)S(1)}, u32[]{:S(2)}, u32[]{:S(2)}) %collective-permute-start.7) | collective-permute-done | bytes 65568 | tf_op jit(solution)/shard_map/ppermute | solution.py:293
  26.5 0.6 %collective-permute-start.11 = (f32[4,8,512]{2,1,0:T(8,128)S(1)}, f32[4,8,512]{2,1,0:T(8,128)S(1)}, u32[]{:S(2)}, u32[]{:S(2)}) collective-permute-start(f32[4,8,512]{2,1,0:T(8,128)S(1)} %collective-permute-done.7.refs_0_), channel_id=1, source_target_pairs={{0,1},{1,0},{2,3},{3,2},{4,5},{5,4},{6,7},{7,6},{8,9},{9,8},{10,11... | collective-permute-start | bytes 196616 | tf_op jit(solution)/shard_map/ppermute | solution.py:282
  27.1 2.3 %collective-permute-done.8.refs_1_ = f32[4,8,512]{2,1,0:T(8,128)S(1)} collective-permute-done((f32[4,8,512]{2,1,0:T(8,128)S(1)}, f32[4,8,512]{2,1,0:T(8,128)S(1)}, u32[]{:S(2)}, u32[]{:S(2)}) %collective-permute-start.8) | collective-permute-done | bytes 65568 | tf_op jit(solution)/shard_map/ppermute | solution.py:293
  29.3 0.4 %collective-permute-start.12 = (f32[4,8,512]{2,1,0:T(8,128)S(1)}, f32[4,8,512]{2,1,0:T(8,128)S(1)}, u32[]{:S(2)}, u32[]{:S(2)}) collective-permute-start(f32[4,8,512]{2,1,0:T(8,128)S(1)} %collective-permute-done.8.refs_1_), channel_id=1, source_target_pairs={{0,1},{1,0},{2,3},{3,2},{4,5},{5,4},{6,7},{7,6},{8,9},{9,8},{10,11... | collective-permute-start | bytes 196616 | tf_op jit(solution)/shard_map/ppermute | solution.py:282
  30.2 0.3 collective-permute-start.14
  30.6 0.6 %collective-permute-done.13.refs_6_ = f32[4,8,512]{2,1,0:T(8,128)S(1)} collective-permute-done((f32[4,8,512]{2,1,0:T(8,128)S(1)}, f32[4,8,512]{2,1,0:T(8,128)S(1)}, u32[]{:S(2)}, u32[]{:S(2)}) %collective-permute-start.13) | collective-permute-done | bytes 65568 | tf_op jit(solution)/shard_map/ppermute | solution.py:282
  31.4 2.3 %make_output.1 = bf16[4,256,512]{2,1,0:T(8,128)(2,1)} custom-call(bf16[4,256,512]{2,1,0:T(8,128)(2,1)S(1)} %copy-done, bf16[2,2,256,256]{3,2,1,0:T(8,128)(2,1)S(1)} %copy-done.2, bf16[64,64]{1,0:T(8,128)(2,1)S(1)} %copy-done.7, f32[64]{0:T(128)S(1)} %copy-done.8, f32[4,8,512]{2,1,0:T(8,128)S(1)} %collective-permute-done.7.refs_0_, ...), custom_call_target="tpu_custom_call" | custom-call | tf_op jit(solution)/shard_map/make_output/pallas_call | solution.py:494
  (31 shorter events, 1.4 us)
Async XLA Ops:
  0.6 16.3 %copy-start.1 = (bf16[1,64,64,128]{3,2,1,0:T(8,128)(2,1)S(1)}, bf16[1,64,64,128]{3,2,1,0:T(8,128)(2,1)}, u32[]{:S(2)}) copy-start(bf16[1,64,64,128]{3,2,1,0:T(8,128)(2,1)} %refs_5_.1) | copy-start | bytes 3145732
  2.4 1.7 %collective-permute-start = (f32[4,2,16,512]{3,2,1,0:T(8,128)S(1)}, f32[4,2,16,512]{3,2,1,0:T(8,128)S(1)}, u32[]{:S(2)}, u32[]{:S(2)}) collective-permute-start(f32[4,2,16,512]{3,2,1,0:T(8,128)S(1)} %get-tuple-element.17), channel_id=1, source_target_pairs={{0,1},{1,0},{2,3},{3,2},{4,5},{5,4},{6,7},{7,6},{8,9},{9,8},{10,11... | collective-permute-start | bytes 786440 | tf_op jit(solution)/shard_map/ppermute | solution.py:282
  4.1 6.6 %collective-permute-start.1 = (f32[2,16,512]{2,1,0:T(8,128)S(1)}, f32[2,16,512]{2,1,0:T(8,128)S(1)}, u32[]{:S(2)}, u32[]{:S(2)}) collective-permute-start(f32[2,16,512]{2,1,0:T(8,128)S(1)} %get-tuple-element.18), channel_id=1, source_target_pairs={{0,8},{1,11},{2,10},{3,9},{4,12},{5,15},{6,14},{7,13},{8,0},{9,3},... | collective-permute-start | bytes 196616 | tf_op jit(solution)/shard_map/ppermute | solution.py:293
  8.1 6.7 %collective-permute-start.2 = (f32[2,16,512]{2,1,0:T(8,128)S(1)}, f32[2,16,512]{2,1,0:T(8,128)S(1)}, u32[]{:S(2)}, u32[]{:S(2)}) collective-permute-start(f32[2,16,512]{2,1,0:T(8,128)S(1)} %get-tuple-element.19), channel_id=1, source_target_pairs={{0,12},{1,15},{2,14},{3,13},{4,8},{5,11},{6,10},{7,9},{8,4},{9,7},... | collective-permute-start | bytes 196616 | tf_op jit(solution)/shard_map/ppermute | solution.py:293
  9.5 6.0 %collective-permute-start.3 = (f32[2,16,512]{2,1,0:T(8,128)S(1)}, f32[2,16,512]{2,1,0:T(8,128)S(1)}, u32[]{:S(2)}, u32[]{:S(2)}) collective-permute-start(f32[2,16,512]{2,1,0:T(8,128)S(1)} %get-tuple-element.20), channel_id=1, source_target_pairs={{0,4},{1,7},{2,6},{3,5},{4,0},{5,3},{6,2},{7,1},{8,12},{9,15},{10,... | collective-permute-start | bytes 196616 | tf_op jit(solution)/shard_map/ppermute | solution.py:293
  9.7 7.2 %copy-start.3 = (bf16[2,4,16,128]{3,2,1,0:T(8,128)(2,1)S(1)}, bf16[2,4,16,128]{3,2,1,0:T(8,128)(2,1)}, u32[]{:S(2)}) copy-start(bf16[2,4,16,128]{3,2,1,0:T(8,128)(2,1)} %constant.13.clone.refs_9_.inverse_low) | copy-start | bytes 98308
  9.7 7.2 %copy-start.4 = (bf16[2,4,16,128]{3,2,1,0:T(8,128)(2,1)S(1)}, bf16[2,4,16,128]{3,2,1,0:T(8,128)(2,1)}, u32[]{:S(2)}) copy-start(bf16[2,4,16,128]{3,2,1,0:T(8,128)(2,1)} %constant.12.clone.refs_8_.inverse_high) | copy-start | bytes 98308
  9.7 7.3 %copy-start.5 = (bf16[128,128]{1,0:T(8,128)(2,1)S(1)}, bf16[128,128]{1,0:T(8,128)(2,1)}, u32[]{:S(2)}) copy-start(bf16[128,128]{1,0:T(8,128)(2,1)} %constant.11.clone.refs_7_) | copy-start | bytes 98308
  9.7 7.3 %copy-start.6 = (bf16[128,128]{1,0:T(8,128)(2,1)S(1)}, bf16[128,128]{1,0:T(8,128)(2,1)}, u32[]{:S(2)}) copy-start(bf16[128,128]{1,0:T(8,128)(2,1)} %constant.10.clone.refs_6_) | copy-start | bytes 98308
  9.7 5.8 %collective-permute-start.4 = (f32[2,16,512]{2,1,0:T(8,128)S(1)}, f32[2,16,512]{2,1,0:T(8,128)S(1)}, u32[]{:S(2)}, u32[]{:S(2)}) collective-permute-start(f32[2,16,512]{2,1,0:T(8,128)S(1)} %get-tuple-element.21), channel_id=1, source_target_pairs={{0,0},{1,3},{2,2},{3,1},{4,4},{5,7},{6,6},{7,5},{8,8},{9,11},{10,1... | collective-permute-start | bytes 196616 | tf_op jit(solution)/shard_map/ppermute | solution.py:293
  15.5 15.9 %copy-start = (bf16[4,256,512]{2,1,0:T(8,128)(2,1)S(1)}, bf16[4,256,512]{2,1,0:T(8,128)(2,1)}, u32[]{:S(2)}) copy-start(bf16[4,256,512]{2,1,0:T(8,128)(2,1)} %flow_ref.1) | copy-start | bytes 3145732
  15.5 1.4 %collective-permute-start.5 = (f32[4,16,512]{2,1,0:T(8,128)S(1)}, f32[4,16,512]{2,1,0:T(8,128)S(1)}, u32[]{:S(2)}, u32[]{:S(2)}) collective-permute-start(f32[4,16,512]{2,1,0:T(8,128)S(1)} %second_halves.1), channel_id=1, source_target_pairs={{0,1},{1,0},{2,3},{3,2},{4,5},{5,4},{6,7},{7,6},{8,9},{9,8},{10,11... | collective-permute-start | bytes 393224 | tf_op jit(solution)/shard_map/ppermute | solution.py:282
  18.0 13.4 %copy-start.2 = (bf16[2,2,256,256]{3,2,1,0:T(8,128)(2,1)S(1)}, bf16[2,2,256,256]{3,2,1,0:T(8,128)(2,1)}, u32[]{:S(2)}) copy-start(bf16[2,2,256,256]{3,2,1,0:T(8,128)(2,1)} %constant.14.clone.table_ref) | copy-start | bytes 1572868
  18.0 1.4 %collective-permute-start.6 = (f32[4,16,512]{2,1,0:T(8,128)S(1)}, f32[4,16,512]{2,1,0:T(8,128)S(1)}, u32[]{:S(2)}, u32[]{:S(2)}) collective-permute-start(f32[4,16,512]{2,1,0:T(8,128)S(1)} %get-tuple-element.24), channel_id=1, source_target_pairs={{0,1},{1,0},{2,3},{3,2},{4,5},{5,4},{6,7},{7,6},{8,9},{9,8},{10,11... | collective-permute-start | bytes 393224 | tf_op jit(solution)/shard_map/ppermute | solution.py:282
  19.5 12.0 %copy-start.7 = (bf16[64,64]{1,0:T(8,128)(2,1)S(1)}, bf16[64,64]{1,0:T(8,128)(2,1)}, u32[]{:S(2)}) copy-start(bf16[64,64]{1,0:T(8,128)(2,1)} %local_ref.1) | copy-start | bytes 24580
  19.5 7.0 %collective-permute-start.7 = (f32[4,8,512]{2,1,0:T(8,128)S(1)}, f32[4,8,512]{2,1,0:T(8,128)S(1)}, u32[]{:S(2)}, u32[]{:S(2)}) collective-permute-start(f32[4,8,512]{2,1,0:T(8,128)S(1)} %get-tuple-element.25), channel_id=1, source_target_pairs={{0,8},{1,11},{2,10},{3,9},{4,12},{5,15},{6,14},{7,13},{8,0},{9,3},... | collective-permute-start | bytes 196616 | tf_op jit(solution)/shard_map/ppermute | solution.py:293
  22.5 6.8 %collective-permute-start.8 = (f32[4,8,512]{2,1,0:T(8,128)S(1)}, f32[4,8,512]{2,1,0:T(8,128)S(1)}, u32[]{:S(2)}, u32[]{:S(2)}) collective-permute-start(f32[4,8,512]{2,1,0:T(8,128)S(1)} %get-tuple-element.26), channel_id=1, source_target_pairs={{0,12},{1,15},{2,14},{3,13},{4,8},{5,11},{6,10},{7,9},{8,4},{9,7},... | collective-permute-start | bytes 196616 | tf_op jit(solution)/shard_map/ppermute | solution.py:293
  23.8 7.6 %copy-start.8 = (f32[64]{0:T(128)S(1)}, f32[64]{0:T(128)}, u32[]{:S(2)}) copy-start(f32[64]{0:T(128)} %bias_ref.1) | copy-start | bytes 772
  23.8 6.1 %collective-permute-start.9 = (f32[4,8,512]{2,1,0:T(8,128)S(1)}, f32[4,8,512]{2,1,0:T(8,128)S(1)}, u32[]{:S(2)}, u32[]{:S(2)}) collective-permute-start(f32[4,8,512]{2,1,0:T(8,128)S(1)} %get-tuple-element.27), channel_id=1, source_target_pairs={{0,4},{1,7},{2,6},{3,5},{4,0},{5,3},{6,2},{7,1},{8,12},{9,15},{10,... | collective-permute-start | bytes 196616 | tf_op jit(solution)/shard_map/ppermute | solution.py:293
  23.8 6.3 %collective-permute-start.10 = (f32[4,8,512]{2,1,0:T(8,128)S(1)}, f32[4,8,512]{2,1,0:T(8,128)S(1)}, u32[]{:S(2)}, u32[]{:S(2)}) collective-permute-start(f32[4,8,512]{2,1,0:T(8,128)S(1)} %get-tuple-element.28), channel_id=1, source_target_pairs={{0,0},{1,3},{2,2},{3,1},{4,4},{5,7},{6,6},{7,5},{8,8},{9,11},{10,1... | collective-permute-start | bytes 196616 | tf_op jit(solution)/shard_map/ppermute | solution.py:293
  26.5 4.0 %collective-permute-start.11 = (f32[4,8,512]{2,1,0:T(8,128)S(1)}, f32[4,8,512]{2,1,0:T(8,128)S(1)}, u32[]{:S(2)}, u32[]{:S(2)}) collective-permute-start(f32[4,8,512]{2,1,0:T(8,128)S(1)} %collective-permute-done.7.refs_0_), channel_id=1, source_target_pairs={{0,1},{1,0},{2,3},{3,2},{4,5},{5,4},{6,7},{7,6},{8,9},{9,8},{10,11... | collective-permute-start | bytes 196616 | tf_op jit(solution)/shard_map/ppermute | solution.py:282
  29.3 1.3 %collective-permute-start.12 = (f32[4,8,512]{2,1,0:T(8,128)S(1)}, f32[4,8,512]{2,1,0:T(8,128)S(1)}, u32[]{:S(2)}, u32[]{:S(2)}) collective-permute-start(f32[4,8,512]{2,1,0:T(8,128)S(1)} %collective-permute-done.8.refs_1_), channel_id=1, source_target_pairs={{0,1},{1,0},{2,3},{3,2},{4,5},{5,4},{6,7},{7,6},{8,9},{9,8},{10,11... | collective-permute-start | bytes 196616 | tf_op jit(solution)/shard_map/ppermute | solution.py:282
  30.0 1.3 %collective-permute-start.13 = (f32[4,8,512]{2,1,0:T(8,128)S(1)}, f32[4,8,512]{2,1,0:T(8,128)S(1)}, u32[]{:S(2)}, u32[]{:S(2)}) collective-permute-start(f32[4,8,512]{2,1,0:T(8,128)S(1)} %collective-permute-done.9.refs_2_), channel_id=1, source_target_pairs={{0,1},{1,0},{2,3},{3,2},{4,5},{5,4},{6,7},{7,6},{8,9},{9,8},{10,11... | collective-permute-start | bytes 196616 | tf_op jit(solution)/shard_map/ppermute | solution.py:282
  30.2 1.3 %collective-permute-start.14 = (f32[4,8,512]{2,1,0:T(8,128)S(1)}, f32[4,8,512]{2,1,0:T(8,128)S(1)}, u32[]{:S(2)}, u32[]{:S(2)}) collective-permute-start(f32[4,8,512]{2,1,0:T(8,128)S(1)} %collective-permute-done.10.refs_3_), channel_id=1, source_target_pairs={{0,1},{1,0},{2,3},{3,2},{4,5},{5,4},{6,7},{7,6},{8,9},{9,8},{10,11... | collective-permute-start | bytes 196616 | tf_op jit(solution)/shard_map/ppermute | solution.py:282

commit v27 on v26

--- a/solution.py
+++ b/solution.py
@@ -306,6 +306,16 @@
 def second_halves(blocks):
     shape = jax.ShapeDtypeStruct((len(blocks),) + blocks[0].shape[1:], blocks[0].dtype)
     return small_call(second_kernel, shape, "second_halves")(*blocks)
+
+
+def stack_kernel(*refs):
+    for index, block_ref in enumerate(refs[:-1]):
+        refs[-1][index] = block_ref[...]
+
+
+def stack_blocks(blocks):
+    shape = jax.ShapeDtypeStruct((len(blocks),) + blocks[0].shape, blocks[0].dtype)
+    return small_call(stack_kernel, shape, "stack_blocks")(*blocks)
 
 
 def add_kernel(keep_ref, arrived_ref, *out_refs):
@@ -382,7 +392,10 @@
         for start in range(0, 8, group):
             span = slice(start, start + group)
             left = jnp.concatenate([block[span], turned[span]], axis=0)[:, :channels]
-            product = dot(left.astype(jnp.bfloat16), weight_ref[0, (base + start) // group])
+            left_high, left_low = split_terms(left)
+            left = jnp.concatenate([left_high, left_low], axis=0)
+            product = dot(left, weight_ref[0, (base + start) // group])
+            product = product[: 2 * group] + product[2 * group :]
             firsts.append(product[:group])
             seconds.append(product[group:])
         first = jnp.concatenate(firsts, axis=0)
@@ -448,8 +461,9 @@
 
 
 def output_kernel(layers, flow_ref, table_ref, local_ref, bias_ref, *refs):
-    own_refs, core_refs = refs[:layers], refs[layers : 2 * layers]
-    out_hbm, order_ref, wide_ref, level_ref, done_ref, sent = refs[2 * layers :]
+    own_refs = refs[:layers]
+    core_refs = [ref.at[index] for ref in refs[layers : layers + 2] for index in range(layers // 2)]
+    out_hbm, order_ref, wide_ref, level_ref, done_ref, sent = refs[layers + 2 :]
     cells_x, _, feat_count = flow_ref.shape
     channels = local_ref.shape[0]
     z, x, y = quad()
@@ -490,7 +504,7 @@
 
 def make_output(flow_field, parts, table, local, bias):
     cells_x, _, feat_count = flow_field.shape
-    layers = len(parts) // 2
+    layers = len(parts) - 2
     return pl.pallas_call(
         functools.partial(output_kernel, layers),
         out_specs=pl.BlockSpec(memory_space=pl.ANY),
@@ -528,7 +542,8 @@
     arrived = flip_core(send)
     mixed, keep = keep_rows(modes, inverse_tables, send)
     own = along_columns(join_blocks(keep, arrived, cells_x), peers)
-    parts = own + [flip_core(block) for block in own]
+    middle = len(own) // 2
+    parts = own + [flip_core(stack_blocks(half)) for half in (own[:middle], own[middle:])]
     table = output_table(inverse_y_table(cells_y, groups_y, peers, rows_ky) * (0.5 * inverse_scale))
     return make_output(flow_field, parts, table, local_weight, bias_terms), mixed
 

time: 33.9 us -> 33.9 us (level)
  starting transfers between devices: 14.2 us -> 13.5 us
  waiting for transfers between devices: 12.8 us -> 13.5 us
    ppermute x8, waiting for transfers between devices: 9.35 us -> 9.97 us  [along_columns(): arrived.append(lax.ppermute(block, ('gx', 'gy'), pairs))]
    ppermute x7 -> x5, starting transfers between devices: 2.66 us -> 2.1 us  [flip_core(): return lax.ppermute(block, 'gy', [(0, 1), (1, 0)])]
    ppermute x7 -> x5, waiting for transfers between devices: 3.49 us -> 3.53 us  [flip_core(): return lax.ppermute(block, 'gy', [(0, 1), (1, 0)])]
  transfers between devices with their start and end apart: 15 -> 13, of which waited for: 12 -> 11; matrix products, arithmetic and copies ran while one was open for 0% -> 0% of each run, Pallas kernels for 2% -> 2%
where the time goes in v27:
time: 33.9 us; the launch traced here: 33.7 us
  starting transfers between devices  13.5 us (40%)
  waiting for transfers between devices  13.5 us (40%)
  Pallas kernels  5.95 us (18%)
  between operations  0.76 us (2%)
    ppermute x8, starting transfers between devices, along_columns(): arrived.append(lax.ppermute(block, ('gx', 'gy'), pairs))  11.4 us
    ppermute x8, waiting for transfers between devices, along_columns(): arrived.append(lax.ppermute(block, ('gx', 'gy'), pairs))  9.97 us
    ppermute x5, waiting for transfers between devices, flip_core(): return lax.ppermute(block, 'gy', [(0, 1), (1, 0)])  3.53 us
    pallas_call x1, Pallas kernels, make_output(): pl.pallas_call(functools.partial(output_kernel, layers), out_specs=pl.Blo...  2.29 us
    ppermute x5, starting transfers between devices, flip_core(): return lax.ppermute(block, 'gy', [(0, 1), (1, 0)])  2.1 us
    pallas_call x1, Pallas kernels, forward_y(): pl.pallas_call(functools.partial(forward_y_kernel, extent, rows_ky), in_s...  1.75 us
    pallas_call x1, Pallas kernels, mix(): pl.pallas_call(functools.partial(mix_kernel, layers), out_shape=[jax.Shap...  1.04 us
    pallas_call x1, Pallas kernels, keep_rows(): pl.pallas_call(keep_kernel, out_shape=[jax.ShapeDtypeStruct((1, rows // 2...  0.78 us
  transfers between devices with their start and end apart: 13, of which 11 were waited for; matrix products, arithmetic and copies ran while one was open for 0% of the time, Pallas kernels for 2%

profile of v27, /device:TPU:0, one launch (start us, length us, event | category | flops | bytes accessed | tf_op | source)
XLA Modules:
  0.0 33.7 jit_solution(10194213595745687399)
XLA Ops:
  0.6 1.7 %forward_y.1 = (f32[4,2,16,512]{3,2,1,0:T(8,128)S(1)}, f32[4,2,16,512]{3,2,1,0:T(8,128)S(1)}) custom-call(bf16[4,256,512]{2,1,0:T(8,128)(2,1)} %flow_ref.1), custom_call_target="tpu_custom_call" | custom-call | tf_op jit(solution)/shard_map/forward_y/pallas_call | solution.py:268
  2.4 0.5 %collective-permute-start = (f32[4,2,16,512]{3,2,1,0:T(8,128)S(1)}, f32[4,2,16,512]{3,2,1,0:T(8,128)S(1)}, u32[]{:S(2)}, u32[]{:S(2)}) collective-permute-start(f32[4,2,16,512]{3,2,1,0:T(8,128)S(1)} %get-tuple-element.17), channel_id=1, source_target_pairs={{0,1},{1,0},{2,3},{3,2},{4,5},{5,4},{6,7},{7,6},{8,9},{9,8},{10,11... | collective-permute-start | bytes 786440 | tf_op jit(solution)/shard_map/ppermute | solution.py:282
  2.9 1.2 %collective-permute-done.arrived_ref = f32[4,2,16,512]{3,2,1,0:T(8,128)S(1)} collective-permute-done((f32[4,2,16,512]{3,2,1,0:T(8,128)S(1)}, f32[4,2,16,512]{3,2,1,0:T(8,128)S(1)}, u32[]{:S(2)}, u32[]{:S(2)}) %collective-permute-start) | collective-permute-done | bytes 262176 | tf_op jit(solution)/shard_map/ppermute | solution.py:282
  4.1 4.0 %collective-permute-start.1 = (f32[2,16,512]{2,1,0:T(8,128)S(1)}, f32[2,16,512]{2,1,0:T(8,128)S(1)}, u32[]{:S(2)}, u32[]{:S(2)}) collective-permute-start(f32[2,16,512]{2,1,0:T(8,128)S(1)} %get-tuple-element.18), channel_id=1, source_target_pairs={{0,8},{1,11},{2,10},{3,9},{4,12},{5,15},{6,14},{7,13},{8,0},{9,3},... | collective-permute-start | bytes 196616 | tf_op jit(solution)/shard_map/ppermute | solution.py:293
  8.1 1.3 %collective-permute-start.2 = (f32[2,16,512]{2,1,0:T(8,128)S(1)}, f32[2,16,512]{2,1,0:T(8,128)S(1)}, u32[]{:S(2)}, u32[]{:S(2)}) collective-permute-start(f32[2,16,512]{2,1,0:T(8,128)S(1)} %get-tuple-element.19), channel_id=1, source_target_pairs={{0,12},{1,15},{2,14},{3,13},{4,8},{5,11},{6,10},{7,9},{8,4},{9,7},... | collective-permute-start | bytes 196616 | tf_op jit(solution)/shard_map/ppermute | solution.py:293
  9.7 0.8 %collective-permute-start.4 = (f32[2,16,512]{2,1,0:T(8,128)S(1)}, f32[2,16,512]{2,1,0:T(8,128)S(1)}, u32[]{:S(2)}, u32[]{:S(2)}) collective-permute-start(f32[2,16,512]{2,1,0:T(8,128)S(1)} %get-tuple-element.21), channel_id=1, source_target_pairs={{0,0},{1,3},{2,2},{3,1},{4,4},{5,7},{6,6},{7,5},{8,8},{9,11},{10,1... | collective-permute-start | bytes 196616 | tf_op jit(solution)/shard_map/ppermute | solution.py:293
  10.7 4.1 %collective-permute-done.2.refs_1_ = f32[2,16,512]{2,1,0:T(8,128)S(1)} collective-permute-done((f32[2,16,512]{2,1,0:T(8,128)S(1)}, f32[2,16,512]{2,1,0:T(8,128)S(1)}, u32[]{:S(2)}, u32[]{:S(2)}) %collective-permute-start.2) | collective-permute-done | bytes 65568 | tf_op jit(solution)/shard_map/ppermute | solution.py:293
  14.8 0.7 %collective-permute-done.3.refs_2_ = f32[2,16,512]{2,1,0:T(8,128)S(1)} collective-permute-done((f32[2,16,512]{2,1,0:T(8,128)S(1)}, f32[2,16,512]{2,1,0:T(8,128)S(1)}, u32[]{:S(2)}, u32[]{:S(2)}) %collective-permute-start.3) | collective-permute-done | bytes 65568 | tf_op jit(solution)/shard_map/ppermute | solution.py:293
  15.5 0.3 collective-permute-start.5
  15.9 1.1 %collective-permute-done.5.refs_4_ = f32[4,16,512]{2,1,0:T(8,128)S(1)} collective-permute-done((f32[4,16,512]{2,1,0:T(8,128)S(1)}, f32[4,16,512]{2,1,0:T(8,128)S(1)}, u32[]{:S(2)}, u32[]{:S(2)}) %collective-permute-start.5) | collective-permute-done | bytes 131104 | tf_op jit(solution)/shard_map/ppermute | solution.py:282
  17.0 1.0 %mix.1 = (f32[128,512]{1,0:T(8,128)S(1)}, f32[4,16,512]{2,1,0:T(8,128)S(1)}) custom-call(f32[2,16,512]{2,1,0:T(8,128)S(1)} %collective-permute-done.1.refs_0_, f32[2,16,512]{2,1,0:T(8,128)S(1)} %collective-permute-done.2.refs_1_, f32[2,16,512]{2,1,0:T(8,128)S(1)} %collective-permute-done.3.refs_2_, f32[2,16,512]{2,1,0:T(8,128)S(1)} %collective-permute-done.4.refs_3_, ...), custom_call_target="tpu_custom_call" | custom-call | tf_op jit(solution)/shard_map/mix/pallas_call | solution.py:420
  18.0 0.3 collective-permute-start.6
  18.4 0.8 %keep_rows.1 = (f32[1,64,1024]{2,1,0:T(8,128)}, f32[4,16,512]{2,1,0:T(8,128)S(1)}) custom-call(f32[128,512]{1,0:T(8,128)S(1)} %get-tuple-element.22.modes_ref, bf16[2,4,16,128]{3,2,1,0:T(8,128)(2,1)S(1)} %copy-done.4, bf16[2,4,16,128]{3,2,1,0:T(8,128)(2,1)S(1)} %copy-done.3), custom_call_target="tpu_custom_call" | custom-call | tf_op jit(solution)/shard_map/keep_rows/pallas_call | solution.py:444
  19.2 0.3 collective-permute-done.6.arrived_ref
  19.5 3.0 %collective-permute-start.7 = (f32[4,8,512]{2,1,0:T(8,128)S(1)}, f32[4,8,512]{2,1,0:T(8,128)S(1)}, u32[]{:S(2)}, u32[]{:S(2)}) collective-permute-start(f32[4,8,512]{2,1,0:T(8,128)S(1)} %get-tuple-element.25), channel_id=1, source_target_pairs={{0,8},{1,11},{2,10},{3,9},{4,12},{5,15},{6,14},{7,13},{8,0},{9,3},... | collective-permute-start | bytes 196616 | tf_op jit(solution)/shard_map/ppermute | solution.py:293
  22.5 1.3 %collective-permute-start.8 = (f32[4,8,512]{2,1,0:T(8,128)S(1)}, f32[4,8,512]{2,1,0:T(8,128)S(1)}, u32[]{:S(2)}, u32[]{:S(2)}) collective-permute-start(f32[4,8,512]{2,1,0:T(8,128)S(1)} %get-tuple-element.26), channel_id=1, source_target_pairs={{0,12},{1,15},{2,14},{3,13},{4,8},{5,11},{6,10},{7,9},{8,4},{9,7},... | collective-permute-start | bytes 196616 | tf_op jit(solution)/shard_map/ppermute | solution.py:293
  23.8 0.7 %collective-permute-start.10 = (f32[4,8,512]{2,1,0:T(8,128)S(1)}, f32[4,8,512]{2,1,0:T(8,128)S(1)}, u32[]{:S(2)}, u32[]{:S(2)}) collective-permute-start(f32[4,8,512]{2,1,0:T(8,128)S(1)} %get-tuple-element.28), channel_id=1, source_target_pairs={{0,0},{1,3},{2,2},{3,1},{4,4},{5,7},{6,6},{7,5},{8,8},{9,11},{10,1... | collective-permute-start | bytes 196616 | tf_op jit(solution)/shard_map/ppermute | solution.py:293
  24.5 2.0 %collective-permute-done.7.refs_0_ = f32[4,8,512]{2,1,0:T(8,128)S(1)} collective-permute-done((f32[4,8,512]{2,1,0:T(8,128)S(1)}, f32[4,8,512]{2,1,0:T(8,128)S(1)}, u32[]{:S(2)}, u32[]{:S(2)}) %collective-permute-start.7) | collective-permute-done | bytes 65568 | tf_op jit(solution)/shard_map/ppermute | solution.py:293
  26.5 2.9 %collective-permute-done.8.refs_1_ = f32[4,8,512]{2,1,0:T(8,128)S(1)} collective-permute-done((f32[4,8,512]{2,1,0:T(8,128)S(1)}, f32[4,8,512]{2,1,0:T(8,128)S(1)}, u32[]{:S(2)}, u32[]{:S(2)}) %collective-permute-start.8) | collective-permute-done | bytes 65568 | tf_op jit(solution)/shard_map/ppermute | solution.py:293
  29.4 0.4 %collective-permute-start.11 = (f32[2,4,8,512]{3,2,1,0:T(8,128)S(1)}, f32[2,4,8,512]{3,2,1,0:T(8,128)S(1)}, u32[]{:S(2)}, u32[]{:S(2)}) collective-permute-start(f32[2,4,8,512]{3,2,1,0:T(8,128)S(1)} %stack_blocks.2), channel_id=1, source_target_pairs={{0,1},{1,0},{2,3},{3,2},{4,5},{5,4},{6,7},{7,6},{8,9},{9,8},{10,11... | collective-permute-start | bytes 393224 | tf_op jit(solution)/shard_map/ppermute | solution.py:282
  30.0 0.5 %collective-permute-start.12 = (f32[2,4,8,512]{3,2,1,0:T(8,128)S(1)}, f32[2,4,8,512]{3,2,1,0:T(8,128)S(1)}, u32[]{:S(2)}, u32[]{:S(2)}) collective-permute-start(f32[2,4,8,512]{3,2,1,0:T(8,128)S(1)} %stack_blocks.3), channel_id=1, source_target_pairs={{0,1},{1,0},{2,3},{3,2},{4,5},{5,4},{6,7},{7,6},{8,9},{9,8},{10,11... | collective-permute-start | bytes 393224 | tf_op jit(solution)/shard_map/ppermute | solution.py:282
  30.4 0.3 %collective-permute-done.11.refs_4_ = f32[2,4,8,512]{3,2,1,0:T(8,128)S(1)} collective-permute-done((f32[2,4,8,512]{3,2,1,0:T(8,128)S(1)}, f32[2,4,8,512]{3,2,1,0:T(8,128)S(1)}, u32[]{:S(2)}, u32[]{:S(2)}) %collective-permute-start.11) | collective-permute-done | bytes 131104 | tf_op jit(solution)/shard_map/ppermute | solution.py:282
  30.8 0.6 %collective-permute-done.12.refs_5_ = f32[2,4,8,512]{3,2,1,0:T(8,128)S(1)} collective-permute-done((f32[2,4,8,512]{3,2,1,0:T(8,128)S(1)}, f32[2,4,8,512]{3,2,1,0:T(8,128)S(1)}, u32[]{:S(2)}, u32[]{:S(2)}) %collective-permute-start.12) | collective-permute-done | bytes 131104 | tf_op jit(solution)/shard_map/ppermute | solution.py:282
  31.4 2.3 %make_output.1 = bf16[4,256,512]{2,1,0:T(8,128)(2,1)} custom-call(bf16[4,256,512]{2,1,0:T(8,128)(2,1)S(1)} %copy-done, bf16[2,2,256,256]{3,2,1,0:T(8,128)(2,1)S(1)} %copy-done.2, bf16[64,64]{1,0:T(8,128)(2,1)S(1)} %copy-done.7, f32[64]{0:T(128)S(1)} %copy-done.8, f32[4,8,512]{2,1,0:T(8,128)S(1)} %collective-permute-done.7.refs_0_, ...), custom_call_target="tpu_custom_call" | custom-call | tf_op jit(solution)/shard_map/make_output/pallas_call | solution.py:508
  (29 shorter events, 0.7 us)
Async XLA Ops:
  0.6 16.3 %copy-start.1 = (bf16[1,64,64,128]{3,2,1,0:T(8,128)(2,1)S(1)}, bf16[1,64,64,128]{3,2,1,0:T(8,128)(2,1)}, u32[]{:S(2)}) copy-start(bf16[1,64,64,128]{3,2,1,0:T(8,128)(2,1)} %refs_5_.1) | copy-start | bytes 3145732
  2.4 1.7 %collective-permute-start = (f32[4,2,16,512]{3,2,1,0:T(8,128)S(1)}, f32[4,2,16,512]{3,2,1,0:T(8,128)S(1)}, u32[]{:S(2)}, u32[]{:S(2)}) collective-permute-start(f32[4,2,16,512]{3,2,1,0:T(8,128)S(1)} %get-tuple-element.17), channel_id=1, source_target_pairs={{0,1},{1,0},{2,3},{3,2},{4,5},{5,4},{6,7},{7,6},{8,9},{9,8},{10,11... | collective-permute-start | bytes 786440 | tf_op jit(solution)/shard_map/ppermute | solution.py:282
  4.1 6.6 %collective-permute-start.1 = (f32[2,16,512]{2,1,0:T(8,128)S(1)}, f32[2,16,512]{2,1,0:T(8,128)S(1)}, u32[]{:S(2)}, u32[]{:S(2)}) collective-permute-start(f32[2,16,512]{2,1,0:T(8,128)S(1)} %get-tuple-element.18), channel_id=1, source_target_pairs={{0,8},{1,11},{2,10},{3,9},{4,12},{5,15},{6,14},{7,13},{8,0},{9,3},... | collective-permute-start | bytes 196616 | tf_op jit(solution)/shard_map/ppermute | solution.py:293
  8.1 6.7 %collective-permute-start.2 = (f32[2,16,512]{2,1,0:T(8,128)S(1)}, f32[2,16,512]{2,1,0:T(8,128)S(1)}, u32[]{:S(2)}, u32[]{:S(2)}) collective-permute-start(f32[2,16,512]{2,1,0:T(8,128)S(1)} %get-tuple-element.19), channel_id=1, source_target_pairs={{0,12},{1,15},{2,14},{3,13},{4,8},{5,11},{6,10},{7,9},{8,4},{9,7},... | collective-permute-start | bytes 196616 | tf_op jit(solution)/shard_map/ppermute | solution.py:293
  9.5 6.0 %collective-permute-start.3 = (f32[2,16,512]{2,1,0:T(8,128)S(1)}, f32[2,16,512]{2,1,0:T(8,128)S(1)}, u32[]{:S(2)}, u32[]{:S(2)}) collective-permute-start(f32[2,16,512]{2,1,0:T(8,128)S(1)} %get-tuple-element.20), channel_id=1, source_target_pairs={{0,4},{1,7},{2,6},{3,5},{4,0},{5,3},{6,2},{7,1},{8,12},{9,15},{10,... | collective-permute-start | bytes 196616 | tf_op jit(solution)/shard_map/ppermute | solution.py:293
  9.7 7.2 %copy-start.3 = (bf16[2,4,16,128]{3,2,1,0:T(8,128)(2,1)S(1)}, bf16[2,4,16,128]{3,2,1,0:T(8,128)(2,1)}, u32[]{:S(2)}) copy-start(bf16[2,4,16,128]{3,2,1,0:T(8,128)(2,1)} %constant.13.clone.refs_9_.inverse_low) | copy-start | bytes 98308
  9.7 7.2 %copy-start.4 = (bf16[2,4,16,128]{3,2,1,0:T(8,128)(2,1)S(1)}, bf16[2,4,16,128]{3,2,1,0:T(8,128)(2,1)}, u32[]{:S(2)}) copy-start(bf16[2,4,16,128]{3,2,1,0:T(8,128)(2,1)} %constant.12.clone.refs_8_.inverse_high) | copy-start | bytes 98308
  9.7 7.3 %copy-start.5 = (bf16[128,128]{1,0:T(8,128)(2,1)S(1)}, bf16[128,128]{1,0:T(8,128)(2,1)}, u32[]{:S(2)}) copy-start(bf16[128,128]{1,0:T(8,128)(2,1)} %constant.11.clone.refs_7_) | copy-start | bytes 98308
  9.7 7.3 %copy-start.6 = (bf16[128,128]{1,0:T(8,128)(2,1)S(1)}, bf16[128,128]{1,0:T(8,128)(2,1)}, u32[]{:S(2)}) copy-start(bf16[128,128]{1,0:T(8,128)(2,1)} %constant.10.clone.refs_6_) | copy-start | bytes 98308
  9.7 5.8 %collective-permute-start.4 = (f32[2,16,512]{2,1,0:T(8,128)S(1)}, f32[2,16,512]{2,1,0:T(8,128)S(1)}, u32[]{:S(2)}, u32[]{:S(2)}) collective-permute-start(f32[2,16,512]{2,1,0:T(8,128)S(1)} %get-tuple-element.21), channel_id=1, source_target_pairs={{0,0},{1,3},{2,2},{3,1},{4,4},{5,7},{6,6},{7,5},{8,8},{9,11},{10,1... | collective-permute-start | bytes 196616 | tf_op jit(solution)/shard_map/ppermute | solution.py:293
  15.5 15.9 %copy-start = (bf16[4,256,512]{2,1,0:T(8,128)(2,1)S(1)}, bf16[4,256,512]{2,1,0:T(8,128)(2,1)}, u32[]{:S(2)}) copy-start(bf16[4,256,512]{2,1,0:T(8,128)(2,1)} %flow_ref.1) | copy-start | bytes 3145732
  15.5 1.4 %collective-permute-start.5 = (f32[4,16,512]{2,1,0:T(8,128)S(1)}, f32[4,16,512]{2,1,0:T(8,128)S(1)}, u32[]{:S(2)}, u32[]{:S(2)}) collective-permute-start(f32[4,16,512]{2,1,0:T(8,128)S(1)} %second_halves.1), channel_id=1, source_target_pairs={{0,1},{1,0},{2,3},{3,2},{4,5},{5,4},{6,7},{7,6},{8,9},{9,8},{10,11... | collective-permute-start | bytes 393224 | tf_op jit(solution)/shard_map/ppermute | solution.py:282
  18.0 1.4 %collective-permute-start.6 = (f32[4,16,512]{2,1,0:T(8,128)S(1)}, f32[4,16,512]{2,1,0:T(8,128)S(1)}, u32[]{:S(2)}, u32[]{:S(2)}) collective-permute-start(f32[4,16,512]{2,1,0:T(8,128)S(1)} %get-tuple-element.24), channel_id=1, source_target_pairs={{0,1},{1,0},{2,3},{3,2},{4,5},{5,4},{6,7},{7,6},{8,9},{9,8},{10,11... | collective-permute-start | bytes 393224 | tf_op jit(solution)/shard_map/ppermute | solution.py:282
  18.4 13.1 %copy-start.2 = (bf16[2,2,256,256]{3,2,1,0:T(8,128)(2,1)S(1)}, bf16[2,2,256,256]{3,2,1,0:T(8,128)(2,1)}, u32[]{:S(2)}) copy-start(bf16[2,2,256,256]{3,2,1,0:T(8,128)(2,1)} %constant.14.clone.table_ref) | copy-start | bytes 1572868
  19.5 7.0 %collective-permute-start.7 = (f32[4,8,512]{2,1,0:T(8,128)S(1)}, f32[4,8,512]{2,1,0:T(8,128)S(1)}, u32[]{:S(2)}, u32[]{:S(2)}) collective-permute-start(f32[4,8,512]{2,1,0:T(8,128)S(1)} %get-tuple-element.25), channel_id=1, source_target_pairs={{0,8},{1,11},{2,10},{3,9},{4,12},{5,15},{6,14},{7,13},{8,0},{9,3},... | collective-permute-start | bytes 196616 | tf_op jit(solution)/shard_map/ppermute | solution.py:293
  22.5 6.8 %collective-permute-start.8 = (f32[4,8,512]{2,1,0:T(8,128)S(1)}, f32[4,8,512]{2,1,0:T(8,128)S(1)}, u32[]{:S(2)}, u32[]{:S(2)}) collective-permute-start(f32[4,8,512]{2,1,0:T(8,128)S(1)} %get-tuple-element.26), channel_id=1, source_target_pairs={{0,12},{1,15},{2,14},{3,13},{4,8},{5,11},{6,10},{7,9},{8,4},{9,7},... | collective-permute-start | bytes 196616 | tf_op jit(solution)/shard_map/ppermute | solution.py:293
  23.8 6.1 %collective-permute-start.9 = (f32[4,8,512]{2,1,0:T(8,128)S(1)}, f32[4,8,512]{2,1,0:T(8,128)S(1)}, u32[]{:S(2)}, u32[]{:S(2)}) collective-permute-start(f32[4,8,512]{2,1,0:T(8,128)S(1)} %get-tuple-element.27), channel_id=1, source_target_pairs={{0,4},{1,7},{2,6},{3,5},{4,0},{5,3},{6,2},{7,1},{8,12},{9,15},{10,... | collective-permute-start | bytes 196616 | tf_op jit(solution)/shard_map/ppermute | solution.py:293
  23.8 6.1 %collective-permute-start.10 = (f32[4,8,512]{2,1,0:T(8,128)S(1)}, f32[4,8,512]{2,1,0:T(8,128)S(1)}, u32[]{:S(2)}, u32[]{:S(2)}) collective-permute-start(f32[4,8,512]{2,1,0:T(8,128)S(1)} %get-tuple-element.28), channel_id=1, source_target_pairs={{0,0},{1,3},{2,2},{3,1},{4,4},{5,7},{6,6},{7,5},{8,8},{9,11},{10,1... | collective-permute-start | bytes 196616 | tf_op jit(solution)/shard_map/ppermute | solution.py:293
  29.3 2.1 %copy-start.7 = (bf16[64,64]{1,0:T(8,128)(2,1)S(1)}, bf16[64,64]{1,0:T(8,128)(2,1)}, u32[]{:S(2)}) copy-start(bf16[64,64]{1,0:T(8,128)(2,1)} %local_ref.1) | copy-start | bytes 24580
  29.3 2.1 %copy-start.8 = (f32[64]{0:T(128)S(1)}, f32[64]{0:T(128)}, u32[]{:S(2)}) copy-start(f32[64]{0:T(128)} %bias_ref.1) | copy-start | bytes 772
  29.4 1.4 %collective-permute-start.11 = (f32[2,4,8,512]{3,2,1,0:T(8,128)S(1)}, f32[2,4,8,512]{3,2,1,0:T(8,128)S(1)}, u32[]{:S(2)}, u32[]{:S(2)}) collective-permute-start(f32[2,4,8,512]{3,2,1,0:T(8,128)S(1)} %stack_blocks.2), channel_id=1, source_target_pairs={{0,1},{1,0},{2,3},{3,2},{4,5},{5,4},{6,7},{7,6},{8,9},{9,8},{10,11... | collective-permute-start | bytes 393224 | tf_op jit(solution)/shard_map/ppermute | solution.py:282
  30.0 1.5 %collective-permute-start.12 = (f32[2,4,8,512]{3,2,1,0:T(8,128)S(1)}, f32[2,4,8,512]{3,2,1,0:T(8,128)S(1)}, u32[]{:S(2)}, u32[]{:S(2)}) collective-permute-start(f32[2,4,8,512]{3,2,1,0:T(8,128)S(1)} %stack_blocks.3), channel_id=1, source_target_pairs={{0,1},{1,0},{2,3},{3,2},{4,5},{5,4},{6,7},{7,6},{8,9},{9,8},{10,11... | collective-permute-start | bytes 393224 | tf_op jit(solution)/shard_map/ppermute | solution.py:282

commit v28 on v27

--- a/solution.py
+++ b/solution.py
@@ -165,9 +165,15 @@
     return place // 2, place % 2, lax.axis_index("gy")
 
 
-def turns(layers):
-    half = layers // 2
-    return list(range(half, layers)) + list(range(half - 1, -1, -1))
+def partner(index, layers, y):
+    turn = index // 2
+    return layers // 2 - 1 - turn + y * (2 * turn + 1), index % 2
+
+
+def peer_of(index, layers, y):
+    z, x, _ = quad()
+    turn, flip = partner(index, layers, y)
+    return (z ^ turn) * 2 + (x ^ flip)
 
 
 def forward_x_table(cells_x, peers, rows_ky):
@@ -204,11 +210,12 @@
     full = full.reshape(groups_y, peers, rows_ky, 2, groups_y, cells_y)
     out = np.zeros((groups_y, 2, cells_y, peers, 2, rows_ky, 2))
     for y in range(groups_y):
-        for column in range(2):
+        for near in range(2):
             for peer in range(peers):
+                far = peer // (peers // 2) ^ near
                 for place in range(2):
-                    half = y ^ place ^ column ^ (peer % 2)
-                    out[y, column, :, peer, place] = np.moveaxis(full[half, peer, :, :, y], -1, 0)
+                    block = full[place ^ far, peer, :, :, y]
+                    out[y, near, :, peer, place] = np.moveaxis(block, -1, 0)
     return out.reshape(groups_y, 2, cells_y, 4 * peers * rows_ky)
 
 
@@ -224,19 +231,14 @@
     return jnp.dot(left, right, preferred_element_type=jnp.float32)
 
 
-def column_of(x, y):
-    return x ^ y
-
-
 def forward_y_table(shape, extent, layers, rows_ky):
     z, x, y = quad()
     peers = 2 * layers
     row = lax.broadcasted_iota(jnp.int32, (shape[0], 1), 0)
     block = row // (2 * rows_ky)
-    place = block // 2 % layers
-    turn = jnp.where(place < layers // 2, place + layers // 2, layers - 1 - place)
     side = y ^ (1 - block // peers)
-    owner = (side ^ (block % 2)) * peers + (z ^ turn) * 2 + column_of(x, side)
+    turn, flip = partner(block // 2 % layers, layers, side)
+    owner = (side ^ (block % 2)) * peers + (z ^ turn) * 2 + (x ^ flip)
     index = owner * rows_ky + row // 2 % rows_ky
     y_places = lax.broadcasted_iota(jnp.int32, (1, shape[1]), 1) + y * shape[1]
     steps = (wave_number(index, MY) * y_places) & (extent - 1)
@@ -282,14 +284,15 @@
     return lax.ppermute(block, "gy", [(0, 1), (1, 0)])
 
 
-def along_columns(blocks, peers):
+def along_chips(blocks, peers):
     arrived = []
-    for turn, block in zip(turns(len(blocks)), blocks):
-        pairs = [
-            (2 * place + core, 2 * (place ^ (2 * turn + column_of(0, core))) + core)
-            for place in range(peers)
-            for core in range(2)
-        ]
+    for index, block in enumerate(blocks):
+        pairs = []
+        for core in range(2):
+            turn, flip = partner(index, len(blocks), core)
+            pairs += [
+                (2 * place + core, 2 * (place ^ (2 * turn + flip)) + core) for place in range(peers)
+            ]
         arrived.append(lax.ppermute(block, ("gx", "gy"), pairs))
     return arrived
 
@@ -347,7 +350,10 @@
 
 def back_rows(inverse_high, inverse_low, modes, shape, other):
     z, x, y = quad()
-    places = [(column_of(x, y) ^ other, z ^ turn) for turn in turns(shape[0])]
+    places = []
+    for index in range(shape[0]):
+        turn, flip = partner(index, shape[0], y ^ other)
+        places.append((x ^ flip, z ^ turn))
     table_high, table_low = [
         jnp.concatenate([ref[column, place] for column, place in places], axis=0)
         for ref in (inverse_high, inverse_low)
@@ -363,11 +369,10 @@
         layers + 1 : layers + 6
     ]
     modes_ref, send_ref, order_ref, spread_ref, result_ref = refs[layers + 6 :]
-    z, x, y = quad()
-    for index, turn in enumerate(turns(layers)):
-        column = column_of(x, y)
-        order_ref[(z ^ turn) * 2 + column] = block_refs[index][0]
-        order_ref[(z ^ turn) * 2 + (column ^ 1)] = arrived_ref[index]
+    _, _, y = quad()
+    for index in range(layers):
+        order_ref[peer_of(index, layers, y)] = block_refs[index][0]
+        order_ref[peer_of(index, layers, 1 - y)] = arrived_ref[index]
     feat_count = order_ref.shape[-1]
     count = weight_ref.shape[1]
     channels = weight_ref.shape[2]
@@ -481,10 +486,10 @@
     filled = jnp.zeros((table_ref.shape[-1] - terms - BIAS_TERMS, WIDTH), jnp.float32)
     below = jnp.concatenate(levels + [filled], axis=0).astype(jnp.bfloat16)
     below = jnp.concatenate([below, wide_ref[...]], axis=0)
-    for column, block_refs in ((x ^ y, own_refs), (x ^ y ^ 1, core_refs)):
-        for turn, block_ref in zip(turns(layers), block_refs):
-            order_ref[:, (z ^ turn) * 2 + column] = block_ref[...]
-    table = table_ref[y, x ^ y]
+    for core, block_refs in ((y, own_refs), (1 - y, core_refs)):
+        for index, block_ref in enumerate(block_refs):
+            order_ref[:, peer_of(index, layers, core)] = block_ref[...]
+    table = table_ref[y, z // (layers // 2)]
     copies = []
     for cell in range(cells_x):
         high, low = split_terms(order_ref[cell].reshape(-1, feat_count))
@@ -530,7 +535,7 @@
     inverse_scale = 1.0 / math.sqrt(MX * MY)
 
     send, keep = forward_y(flow_field, cells_y * groups_y, peers // 2, rows_ky)
-    blocks = along_columns(add_blocks(keep, flip_core(send)), peers)
+    blocks = along_chips(add_blocks(keep, flip_core(send)), peers)
     inverse_tables = split_table(inverse_x_table(cells_x, peers, rows_ky))
     modes, send = mix(
         blocks,
@@ -541,7 +546,7 @@
     )
     arrived = flip_core(send)
     mixed, keep = keep_rows(modes, inverse_tables, send)
-    own = along_columns(join_blocks(keep, arrived, cells_x), peers)
+    own = along_chips(join_blocks(keep, arrived, cells_x), peers)
     middle = len(own) // 2
     parts = own + [flip_core(stack_blocks(half)) for half in (own[:middle], own[middle:])]
     table = output_table(inverse_y_table(cells_y, groups_y, peers, rows_ky) * (0.5 * inverse_scale))

time: 33.9 us -> 38.5 us (1.14)
  starting transfers between devices: 13.5 us -> 21.7 us
  waiting for transfers between devices: 13.5 us -> 9.82 us
    ppermute x5, starting transfers between devices: 2.1 us -> 12.2 us  [flip_core(): return lax.ppermute(block, 'gy', [(0, 1), (1, 0)])]
    ppermute x8, waiting for transfers between devices: 9.97 us -> 6.48 us  [along_chips(): arrived.append(lax.ppermute(block, ('gx', 'gy'), pairs))]
    ppermute x8, starting transfers between devices: 11.4 us -> 9.54 us  [along_chips(): arrived.append(lax.ppermute(block, ('gx', 'gy'), pairs))]
  transfers between devices with their start and end apart: 13 -> 13, of which waited for: 11 -> 9; matrix products, arithmetic and copies ran while one was open for 0% -> 0% of each run, Pallas kernels for 2% -> 2%
where the time goes in v28:
time: 38.5 us; the launch traced here: 38.3 us
  starting transfers between devices  21.7 us (56%)
  waiting for transfers between devices  9.82 us (26%)
  Pallas kernels  5.95 us (15%)
  between operations  0.78 us (2%)
    ppermute x5, starting transfers between devices, flip_core(): return lax.ppermute(block, 'gy', [(0, 1), (1, 0)])  12.2 us
    ppermute x8, starting transfers between devices, along_chips(): arrived.append(lax.ppermute(block, ('gx', 'gy'), pairs))  9.54 us
    ppermute x8, waiting for transfers between devices, along_chips(): arrived.append(lax.ppermute(block, ('gx', 'gy'), pairs))  6.48 us
    ppermute x5, waiting for transfers between devices, flip_core(): return lax.ppermute(block, 'gy', [(0, 1), (1, 0)])  3.34 us
    pallas_call x1, Pallas kernels, make_output(): pl.pallas_call(functools.partial(output_kernel, layers), out_specs=pl.Blo...  2.28 us
    pallas_call x1, Pallas kernels, forward_y(): pl.pallas_call(functools.partial(forward_y_kernel, extent, rows_ky), in_s...  1.75 us
    pallas_call x1, Pallas kernels, mix(): pl.pallas_call(functools.partial(mix_kernel, layers), out_shape=[jax.Shap...  1.04 us
    pallas_call x1, Pallas kernels, keep_rows(): pl.pallas_call(keep_kernel, out_shape=[jax.ShapeDtypeStruct((1, rows // 2...  0.78 us
  transfers between devices with their start and end apart: 13, of which 9 were waited for; matrix products, arithmetic and copies ran while one was open for 0% of the time, Pallas kernels for 2%

profile of v28, /device:TPU:0, one launch (start us, length us, event | category | flops | bytes accessed | tf_op | source)
XLA Modules:
  0.0 38.3 jit_solution(17577901162236244155)
XLA Ops:
  0.6 1.7 %forward_y.1 = (f32[4,2,16,512]{3,2,1,0:T(8,128)S(1)}, f32[4,2,16,512]{3,2,1,0:T(8,128)S(1)}) custom-call(bf16[4,256,512]{2,1,0:T(8,128)(2,1)} %flow_ref.1), custom_call_target="tpu_custom_call" | custom-call | tf_op jit(solution)/shard_map/forward_y/pallas_call | solution.py:270
  2.4 0.5 %collective-permute-start = (f32[4,2,16,512]{3,2,1,0:T(8,128)S(1)}, f32[4,2,16,512]{3,2,1,0:T(8,128)S(1)}, u32[]{:S(2)}, u32[]{:S(2)}) collective-permute-start(f32[4,2,16,512]{3,2,1,0:T(8,128)S(1)} %get-tuple-element.17), channel_id=1, source_target_pairs={{0,1},{1,0},{2,3},{3,2},{4,5},{5,4},{6,7},{7,6},{8,9},{9,8},{10,11... | collective-permute-start | bytes 786440 | tf_op jit(solution)/shard_map/ppermute | solution.py:284
  2.9 1.2 %collective-permute-done.arrived_ref = f32[4,2,16,512]{3,2,1,0:T(8,128)S(1)} collective-permute-done((f32[4,2,16,512]{3,2,1,0:T(8,128)S(1)}, f32[4,2,16,512]{3,2,1,0:T(8,128)S(1)}, u32[]{:S(2)}, u32[]{:S(2)}) %collective-permute-start) | collective-permute-done | bytes 262176 | tf_op jit(solution)/shard_map/ppermute | solution.py:284
  4.1 3.0 %collective-permute-start.1 = (f32[2,16,512]{2,1,0:T(8,128)S(1)}, f32[2,16,512]{2,1,0:T(8,128)S(1)}, u32[]{:S(2)}, u32[]{:S(2)}) collective-permute-start(f32[2,16,512]{2,1,0:T(8,128)S(1)} %get-tuple-element.18), channel_id=1, source_target_pairs={{0,4},{2,6},{4,0},{6,2},{8,12},{10,14},{12,8},{14,10},{1,9},{3,11}... | collective-permute-start | bytes 196616 | tf_op jit(solution)/shard_map/ppermute | solution.py:296
  7.1 1.4 %collective-permute-start.2 = (f32[2,16,512]{2,1,0:T(8,128)S(1)}, f32[2,16,512]{2,1,0:T(8,128)S(1)}, u32[]{:S(2)}, u32[]{:S(2)}) collective-permute-start(f32[2,16,512]{2,1,0:T(8,128)S(1)} %get-tuple-element.19), channel_id=1, source_target_pairs={{0,6},{2,4},{4,2},{6,0},{8,14},{10,12},{12,10},{14,8},{1,11},{3,9}... | collective-permute-start | bytes 196616 | tf_op jit(solution)/shard_map/ppermute | solution.py:296
  8.5 0.7 %collective-permute-start.3 = (f32[2,16,512]{2,1,0:T(8,128)S(1)}, f32[2,16,512]{2,1,0:T(8,128)S(1)}, u32[]{:S(2)}, u32[]{:S(2)}) collective-permute-start(f32[2,16,512]{2,1,0:T(8,128)S(1)} %get-tuple-element.20), channel_id=1, source_target_pairs={{0,0},{2,2},{4,4},{6,6},{8,8},{10,10},{12,12},{14,14},{1,13},{3,15... | collective-permute-start | bytes 196616 | tf_op jit(solution)/shard_map/ppermute | solution.py:296
  9.2 0.2 collective-permute-start.4
  9.4 0.6 %collective-permute-done.1.refs_0_ = f32[2,16,512]{2,1,0:T(8,128)S(1)} collective-permute-done((f32[2,16,512]{2,1,0:T(8,128)S(1)}, f32[2,16,512]{2,1,0:T(8,128)S(1)}, u32[]{:S(2)}, u32[]{:S(2)}) %collective-permute-start.1) | collective-permute-done | bytes 65568 | tf_op jit(solution)/shard_map/ppermute | solution.py:296
  10.1 2.2 %collective-permute-done.2.refs_1_ = f32[2,16,512]{2,1,0:T(8,128)S(1)} collective-permute-done((f32[2,16,512]{2,1,0:T(8,128)S(1)}, f32[2,16,512]{2,1,0:T(8,128)S(1)}, u32[]{:S(2)}, u32[]{:S(2)}) %collective-permute-start.2) | collective-permute-done | bytes 65568 | tf_op jit(solution)/shard_map/ppermute | solution.py:296
  12.3 1.5 %collective-permute-done.4.refs_3_ = f32[2,16,512]{2,1,0:T(8,128)S(1)} collective-permute-done((f32[2,16,512]{2,1,0:T(8,128)S(1)}, f32[2,16,512]{2,1,0:T(8,128)S(1)}, u32[]{:S(2)}, u32[]{:S(2)}) %collective-permute-start.4) | collective-permute-done | bytes 65568 | tf_op jit(solution)/shard_map/ppermute | solution.py:296
  13.8 6.4 %collective-permute-start.5 = (f32[4,16,512]{2,1,0:T(8,128)S(1)}, f32[4,16,512]{2,1,0:T(8,128)S(1)}, u32[]{:S(2)}, u32[]{:S(2)}) collective-permute-start(f32[4,16,512]{2,1,0:T(8,128)S(1)} %second_halves.1), channel_id=1, source_target_pairs={{0,1},{1,0},{2,3},{3,2},{4,5},{5,4},{6,7},{7,6},{8,9},{9,8},{10,11... | collective-permute-start | bytes 393224 | tf_op jit(solution)/shard_map/ppermute | solution.py:284
  20.2 1.0 %collective-permute-done.5.refs_4_ = f32[4,16,512]{2,1,0:T(8,128)S(1)} collective-permute-done((f32[4,16,512]{2,1,0:T(8,128)S(1)}, f32[4,16,512]{2,1,0:T(8,128)S(1)}, u32[]{:S(2)}, u32[]{:S(2)}) %collective-permute-start.5) | collective-permute-done | bytes 131104 | tf_op jit(solution)/shard_map/ppermute | solution.py:284
  21.2 1.0 %mix.1 = (f32[128,512]{1,0:T(8,128)S(1)}, f32[4,16,512]{2,1,0:T(8,128)S(1)}) custom-call(f32[2,16,512]{2,1,0:T(8,128)S(1)} %collective-permute-done.1.refs_0_, f32[2,16,512]{2,1,0:T(8,128)S(1)} %collective-permute-done.2.refs_1_, f32[2,16,512]{2,1,0:T(8,128)S(1)} %collective-permute-done.3.refs_2_, f32[2,16,512]{2,1,0:T(8,128)S(1)} %collective-permute-done.4.refs_3_, ...), custom_call_target="tpu_custom_call" | custom-call | tf_op jit(solution)/shard_map/mix/pallas_call | solution.py:425
  22.3 0.4 %collective-permute-start.6 = (f32[4,16,512]{2,1,0:T(8,128)S(1)}, f32[4,16,512]{2,1,0:T(8,128)S(1)}, u32[]{:S(2)}, u32[]{:S(2)}) collective-permute-start(f32[4,16,512]{2,1,0:T(8,128)S(1)} %get-tuple-element.24), channel_id=1, source_target_pairs={{0,1},{1,0},{2,3},{3,2},{4,5},{5,4},{6,7},{7,6},{8,9},{9,8},{10,11... | collective-permute-start | bytes 393224 | tf_op jit(solution)/shard_map/ppermute | solution.py:284
  22.7 0.8 %keep_rows.1 = (f32[1,64,1024]{2,1,0:T(8,128)}, f32[4,16,512]{2,1,0:T(8,128)S(1)}) custom-call(f32[128,512]{1,0:T(8,128)S(1)} %get-tuple-element.22.modes_ref, bf16[2,4,16,128]{3,2,1,0:T(8,128)(2,1)S(1)} %copy-done.4, bf16[2,4,16,128]{3,2,1,0:T(8,128)(2,1)S(1)} %copy-done.3), custom_call_target="tpu_custom_call" | custom-call | tf_op jit(solution)/shard_map/keep_rows/pallas_call | solution.py:449
  23.8 2.0 %collective-permute-start.8 = (f32[4,8,512]{2,1,0:T(8,128)S(1)}, f32[4,8,512]{2,1,0:T(8,128)S(1)}, u32[]{:S(2)}, u32[]{:S(2)}) collective-permute-start(f32[4,8,512]{2,1,0:T(8,128)S(1)} %get-tuple-element.26), channel_id=1, source_target_pairs={{0,6},{2,4},{4,2},{6,0},{8,14},{10,12},{12,10},{14,8},{1,11},{3,9}... | collective-permute-start | bytes 196616 | tf_op jit(solution)/shard_map/ppermute | solution.py:296
  25.8 0.7 %collective-permute-start.9 = (f32[4,8,512]{2,1,0:T(8,128)S(1)}, f32[4,8,512]{2,1,0:T(8,128)S(1)}, u32[]{:S(2)}, u32[]{:S(2)}) collective-permute-start(f32[4,8,512]{2,1,0:T(8,128)S(1)} %get-tuple-element.27), channel_id=1, source_target_pairs={{0,0},{2,2},{4,4},{6,6},{8,8},{10,10},{12,12},{14,14},{1,13},{3,15... | collective-permute-start | bytes 196616 | tf_op jit(solution)/shard_map/ppermute | solution.py:296
  26.5 1.6 %collective-permute-start.10 = (f32[4,8,512]{2,1,0:T(8,128)S(1)}, f32[4,8,512]{2,1,0:T(8,128)S(1)}, u32[]{:S(2)}, u32[]{:S(2)}) collective-permute-start(f32[4,8,512]{2,1,0:T(8,128)S(1)} %get-tuple-element.28), channel_id=1, source_target_pairs={{0,2},{2,0},{4,6},{6,4},{8,10},{10,8},{12,14},{14,12},{1,15},{3,13... | collective-permute-start | bytes 196616 | tf_op jit(solution)/shard_map/ppermute | solution.py:296
  28.0 1.0 %collective-permute-done.7.refs_0_ = f32[4,8,512]{2,1,0:T(8,128)S(1)} collective-permute-done((f32[4,8,512]{2,1,0:T(8,128)S(1)}, f32[4,8,512]{2,1,0:T(8,128)S(1)}, u32[]{:S(2)}, u32[]{:S(2)}) %collective-permute-start.7) | collective-permute-done | bytes 65568 | tf_op jit(solution)/shard_map/ppermute | solution.py:296
  29.0 1.1 %collective-permute-done.8.refs_1_ = f32[4,8,512]{2,1,0:T(8,128)S(1)} collective-permute-done((f32[4,8,512]{2,1,0:T(8,128)S(1)}, f32[4,8,512]{2,1,0:T(8,128)S(1)}, u32[]{:S(2)}, u32[]{:S(2)}) %collective-permute-start.8) | collective-permute-done | bytes 65568 | tf_op jit(solution)/shard_map/ppermute | solution.py:296
  30.2 2.6 %collective-permute-start.11 = (f32[2,4,8,512]{3,2,1,0:T(8,128)S(1)}, f32[2,4,8,512]{3,2,1,0:T(8,128)S(1)}, u32[]{:S(2)}, u32[]{:S(2)}) collective-permute-start(f32[2,4,8,512]{3,2,1,0:T(8,128)S(1)} %stack_blocks.2), channel_id=1, source_target_pairs={{0,1},{1,0},{2,3},{3,2},{4,5},{5,4},{6,7},{7,6},{8,9},{9,8},{10,11... | collective-permute-start | bytes 393224 | tf_op jit(solution)/shard_map/ppermute | solution.py:284
  32.8 2.2 %collective-permute-start.12 = (f32[2,4,8,512]{3,2,1,0:T(8,128)S(1)}, f32[2,4,8,512]{3,2,1,0:T(8,128)S(1)}, u32[]{:S(2)}, u32[]{:S(2)}) collective-permute-start(f32[2,4,8,512]{3,2,1,0:T(8,128)S(1)} %stack_blocks.3), channel_id=1, source_target_pairs={{0,1},{1,0},{2,3},{3,2},{4,5},{5,4},{6,7},{7,6},{8,9},{9,8},{10,11... | collective-permute-start | bytes 393224 | tf_op jit(solution)/shard_map/ppermute | solution.py:284
  35.0 1.0 %collective-permute-done.12.refs_5_ = f32[2,4,8,512]{3,2,1,0:T(8,128)S(1)} collective-permute-done((f32[2,4,8,512]{3,2,1,0:T(8,128)S(1)}, f32[2,4,8,512]{3,2,1,0:T(8,128)S(1)}, u32[]{:S(2)}, u32[]{:S(2)}) %collective-permute-start.12) | collective-permute-done | bytes 131104 | tf_op jit(solution)/shard_map/ppermute | solution.py:284
  36.0 2.3 %make_output.1 = bf16[4,256,512]{2,1,0:T(8,128)(2,1)} custom-call(bf16[4,256,512]{2,1,0:T(8,128)(2,1)S(1)} %copy-done, bf16[2,2,256,256]{3,2,1,0:T(8,128)(2,1)S(1)} %copy-done.2, bf16[64,64]{1,0:T(8,128)(2,1)S(1)} %copy-done.7, f32[64]{0:T(128)S(1)} %copy-done.8, f32[4,8,512]{2,1,0:T(8,128)S(1)} %collective-permute-done.7.refs_0_, ...), custom_call_target="tpu_custom_call" | custom-call | tf_op jit(solution)/shard_map/make_output/pallas_call | solution.py:513
  (29 shorter events, 0.4 us)
Async XLA Ops:
  0.6 20.6 %copy-start.1 = (bf16[1,64,64,128]{3,2,1,0:T(8,128)(2,1)S(1)}, bf16[1,64,64,128]{3,2,1,0:T(8,128)(2,1)}, u32[]{:S(2)}) copy-start(bf16[1,64,64,128]{3,2,1,0:T(8,128)(2,1)} %refs_5_.1) | copy-start | bytes 3145732
  2.4 1.7 %collective-permute-start = (f32[4,2,16,512]{3,2,1,0:T(8,128)S(1)}, f32[4,2,16,512]{3,2,1,0:T(8,128)S(1)}, u32[]{:S(2)}, u32[]{:S(2)}) collective-permute-start(f32[4,2,16,512]{3,2,1,0:T(8,128)S(1)} %get-tuple-element.17), channel_id=1, source_target_pairs={{0,1},{1,0},{2,3},{3,2},{4,5},{5,4},{6,7},{7,6},{8,9},{9,8},{10,11... | collective-permute-start | bytes 786440 | tf_op jit(solution)/shard_map/ppermute | solution.py:284
  4.1 6.0 %collective-permute-start.1 = (f32[2,16,512]{2,1,0:T(8,128)S(1)}, f32[2,16,512]{2,1,0:T(8,128)S(1)}, u32[]{:S(2)}, u32[]{:S(2)}) collective-permute-start(f32[2,16,512]{2,1,0:T(8,128)S(1)} %get-tuple-element.18), channel_id=1, source_target_pairs={{0,4},{2,6},{4,0},{6,2},{8,12},{10,14},{12,8},{14,10},{1,9},{3,11}... | collective-permute-start | bytes 196616 | tf_op jit(solution)/shard_map/ppermute | solution.py:296
  7.1 5.2 %collective-permute-start.2 = (f32[2,16,512]{2,1,0:T(8,128)S(1)}, f32[2,16,512]{2,1,0:T(8,128)S(1)}, u32[]{:S(2)}, u32[]{:S(2)}) collective-permute-start(f32[2,16,512]{2,1,0:T(8,128)S(1)} %get-tuple-element.19), channel_id=1, source_target_pairs={{0,6},{2,4},{4,2},{6,0},{8,14},{10,12},{12,10},{14,8},{1,11},{3,9}... | collective-permute-start | bytes 196616 | tf_op jit(solution)/shard_map/ppermute | solution.py:296
  8.5 3.8 %collective-permute-start.3 = (f32[2,16,512]{2,1,0:T(8,128)S(1)}, f32[2,16,512]{2,1,0:T(8,128)S(1)}, u32[]{:S(2)}, u32[]{:S(2)}) collective-permute-start(f32[2,16,512]{2,1,0:T(8,128)S(1)} %get-tuple-element.20), channel_id=1, source_target_pairs={{0,0},{2,2},{4,4},{6,6},{8,8},{10,10},{12,12},{14,14},{1,13},{3,15... | collective-permute-start | bytes 196616 | tf_op jit(solution)/shard_map/ppermute | solution.py:296
  9.2 12.1 %copy-start.3 = (bf16[2,4,16,128]{3,2,1,0:T(8,128)(2,1)S(1)}, bf16[2,4,16,128]{3,2,1,0:T(8,128)(2,1)}, u32[]{:S(2)}) copy-start(bf16[2,4,16,128]{3,2,1,0:T(8,128)(2,1)} %constant.13.clone.refs_9_.inverse_low) | copy-start | bytes 98308
  9.2 12.0 %copy-start.4 = (bf16[2,4,16,128]{3,2,1,0:T(8,128)(2,1)S(1)}, bf16[2,4,16,128]{3,2,1,0:T(8,128)(2,1)}, u32[]{:S(2)}) copy-start(bf16[2,4,16,128]{3,2,1,0:T(8,128)(2,1)} %constant.12.clone.refs_8_.inverse_high) | copy-start | bytes 98308
  9.2 12.0 %copy-start.5 = (bf16[128,128]{1,0:T(8,128)(2,1)S(1)}, bf16[128,128]{1,0:T(8,128)(2,1)}, u32[]{:S(2)}) copy-start(bf16[128,128]{1,0:T(8,128)(2,1)} %constant.11.clone.refs_7_) | copy-start | bytes 98308
  9.2 12.0 %copy-start.6 = (bf16[128,128]{1,0:T(8,128)(2,1)S(1)}, bf16[128,128]{1,0:T(8,128)(2,1)}, u32[]{:S(2)}) copy-start(bf16[128,128]{1,0:T(8,128)(2,1)} %constant.10.clone.refs_6_) | copy-start | bytes 98308
  9.2 4.6 %collective-permute-start.4 = (f32[2,16,512]{2,1,0:T(8,128)S(1)}, f32[2,16,512]{2,1,0:T(8,128)S(1)}, u32[]{:S(2)}, u32[]{:S(2)}) collective-permute-start(f32[2,16,512]{2,1,0:T(8,128)S(1)} %get-tuple-element.21), channel_id=1, source_target_pairs={{0,2},{2,0},{4,6},{6,4},{8,10},{10,8},{12,14},{14,12},{1,15},{3,13... | collective-permute-start | bytes 196616 | tf_op jit(solution)/shard_map/ppermute | solution.py:296
  13.8 22.2 %copy-start = (bf16[4,256,512]{2,1,0:T(8,128)(2,1)S(1)}, bf16[4,256,512]{2,1,0:T(8,128)(2,1)}, u32[]{:S(2)}) copy-start(bf16[4,256,512]{2,1,0:T(8,128)(2,1)} %flow_ref.1) | copy-start | bytes 3145732
  13.8 7.4 %collective-permute-start.5 = (f32[4,16,512]{2,1,0:T(8,128)S(1)}, f32[4,16,512]{2,1,0:T(8,128)S(1)}, u32[]{:S(2)}, u32[]{:S(2)}) collective-permute-start(f32[4,16,512]{2,1,0:T(8,128)S(1)} %second_halves.1), channel_id=1, source_target_pairs={{0,1},{1,0},{2,3},{3,2},{4,5},{5,4},{6,7},{7,6},{8,9},{9,8},{10,11... | collective-permute-start | bytes 393224 | tf_op jit(solution)/shard_map/ppermute | solution.py:284
  22.3 1.4 %collective-permute-start.6 = (f32[4,16,512]{2,1,0:T(8,128)S(1)}, f32[4,16,512]{2,1,0:T(8,128)S(1)}, u32[]{:S(2)}, u32[]{:S(2)}) collective-permute-start(f32[4,16,512]{2,1,0:T(8,128)S(1)} %get-tuple-element.24), channel_id=1, source_target_pairs={{0,1},{1,0},{2,3},{3,2},{4,5},{5,4},{6,7},{7,6},{8,9},{9,8},{10,11... | collective-permute-start | bytes 393224 | tf_op jit(solution)/shard_map/ppermute | solution.py:284
  22.7 13.3 %copy-start.2 = (bf16[2,2,256,256]{3,2,1,0:T(8,128)(2,1)S(1)}, bf16[2,2,256,256]{3,2,1,0:T(8,128)(2,1)}, u32[]{:S(2)}) copy-start(bf16[2,2,256,256]{3,2,1,0:T(8,128)(2,1)} %constant.14.clone.table_ref) | copy-start | bytes 1572868
  23.7 5.3 %collective-permute-start.7 = (f32[4,8,512]{2,1,0:T(8,128)S(1)}, f32[4,8,512]{2,1,0:T(8,128)S(1)}, u32[]{:S(2)}, u32[]{:S(2)}) collective-permute-start(f32[4,8,512]{2,1,0:T(8,128)S(1)} %get-tuple-element.25), channel_id=1, source_target_pairs={{0,4},{2,6},{4,0},{6,2},{8,12},{10,14},{12,8},{14,10},{1,9},{3,11}... | collective-permute-start | bytes 196616 | tf_op jit(solution)/shard_map/ppermute | solution.py:296
  23.8 6.3 %collective-permute-start.8 = (f32[4,8,512]{2,1,0:T(8,128)S(1)}, f32[4,8,512]{2,1,0:T(8,128)S(1)}, u32[]{:S(2)}, u32[]{:S(2)}) collective-permute-start(f32[4,8,512]{2,1,0:T(8,128)S(1)} %get-tuple-element.26), channel_id=1, source_target_pairs={{0,6},{2,4},{4,2},{6,0},{8,14},{10,12},{12,10},{14,8},{1,11},{3,9}... | collective-permute-start | bytes 196616 | tf_op jit(solution)/shard_map/ppermute | solution.py:296
  25.8 7.0 %collective-permute-start.9 = (f32[4,8,512]{2,1,0:T(8,128)S(1)}, f32[4,8,512]{2,1,0:T(8,128)S(1)}, u32[]{:S(2)}, u32[]{:S(2)}) collective-permute-start(f32[4,8,512]{2,1,0:T(8,128)S(1)} %get-tuple-element.27), channel_id=1, source_target_pairs={{0,0},{2,2},{4,4},{6,6},{8,8},{10,10},{12,12},{14,14},{1,13},{3,15... | collective-permute-start | bytes 196616 | tf_op jit(solution)/shard_map/ppermute | solution.py:296
  26.5 6.3 %collective-permute-start.10 = (f32[4,8,512]{2,1,0:T(8,128)S(1)}, f32[4,8,512]{2,1,0:T(8,128)S(1)}, u32[]{:S(2)}, u32[]{:S(2)}) collective-permute-start(f32[4,8,512]{2,1,0:T(8,128)S(1)} %get-tuple-element.28), channel_id=1, source_target_pairs={{0,2},{2,0},{4,6},{6,4},{8,10},{10,8},{12,14},{14,12},{1,15},{3,13... | collective-permute-start | bytes 196616 | tf_op jit(solution)/shard_map/ppermute | solution.py:296
  30.2 5.8 %copy-start.7 = (bf16[64,64]{1,0:T(8,128)(2,1)S(1)}, bf16[64,64]{1,0:T(8,128)(2,1)}, u32[]{:S(2)}) copy-start(bf16[64,64]{1,0:T(8,128)(2,1)} %local_ref.1) | copy-start | bytes 24580
  30.2 5.8 %copy-start.8 = (f32[64]{0:T(128)S(1)}, f32[64]{0:T(128)}, u32[]{:S(2)}) copy-start(f32[64]{0:T(128)} %bias_ref.1) | copy-start | bytes 772
  30.2 4.8 %collective-permute-start.11 = (f32[2,4,8,512]{3,2,1,0:T(8,128)S(1)}, f32[2,4,8,512]{3,2,1,0:T(8,128)S(1)}, u32[]{:S(2)}, u32[]{:S(2)}) collective-permute-start(f32[2,4,8,512]{3,2,1,0:T(8,128)S(1)} %stack_blocks.2), channel_id=1, source_target_pairs={{0,1},{1,0},{2,3},{3,2},{4,5},{5,4},{6,7},{7,6},{8,9},{9,8},{10,11... | collective-permute-start | bytes 393224 | tf_op jit(solution)/shard_map/ppermute | solution.py:284
  32.8 3.2 %collective-permute-start.12 = (f32[2,4,8,512]{3,2,1,0:T(8,128)S(1)}, f32[2,4,8,512]{3,2,1,0:T(8,128)S(1)}, u32[]{:S(2)}, u32[]{:S(2)}) collective-permute-start(f32[2,4,8,512]{3,2,1,0:T(8,128)S(1)} %stack_blocks.3), channel_id=1, source_target_pairs={{0,1},{1,0},{2,3},{3,2},{4,5},{5,4},{6,7},{7,6},{8,9},{9,8},{10,11... | collective-permute-start | bytes 393224 | tf_op jit(solution)/shard_map/ppermute | solution.py:284

commit v29 on v27

--- a/solution.py
+++ b/solution.py
@@ -282,9 +282,9 @@
     return lax.ppermute(block, "gy", [(0, 1), (1, 0)])
 
 
-def along_columns(blocks, peers):
+def along_columns(blocks, peers, order):
     arrived = []
-    for turn, block in zip(turns(len(blocks)), blocks):
+    for turn, block in zip(order, blocks):
         pairs = [
             (2 * place + core, 2 * (place ^ (2 * turn + column_of(0, core))) + core)
             for place in range(peers)
@@ -362,7 +362,7 @@
     weight_ref, forward_high, forward_low, inverse_high, inverse_low = refs[
         layers + 1 : layers + 6
     ]
-    modes_ref, send_ref, order_ref, spread_ref, result_ref = refs[layers + 6 :]
+    modes_ref, far_ref, near_ref, order_ref, spread_ref, result_ref = refs[layers + 6 :]
     z, x, y = quad()
     for index, turn in enumerate(turns(layers)):
         column = column_of(x, y)
@@ -409,7 +409,10 @@
             modes_ref[part * count : (part + 1) * count, tile * 128 : (tile + 1) * 128] = (
                 result_ref[pl.ds(part * tiles + tile, count, stride=group), :]
             )
-    send_ref[...] = back_rows(inverse_high, inverse_low, modes_ref[...], send_ref.shape, 1)
+    shape = (layers,) + far_ref.shape[1:]
+    send = back_rows(inverse_high, inverse_low, modes_ref[...], shape, 1)
+    far_ref[...] = send[: layers // 2]
+    near_ref[...] = send[layers // 2 :]
 
 
 def mix(blocks, arrived, weights, forward_table, inverse_tables):
@@ -421,7 +424,8 @@
         functools.partial(mix_kernel, layers),
         out_shape=[
             jax.ShapeDtypeStruct((2 * count, feat_count), jnp.float32),
-            jax.ShapeDtypeStruct((layers, rows, feat_count), jnp.float32),
+            jax.ShapeDtypeStruct((layers // 2, rows, feat_count), jnp.float32),
+            jax.ShapeDtypeStruct((layers // 2, rows, feat_count), jnp.float32),
         ],
         scratch_shapes=[pltpu.VMEM((2 * layers, rows, feat_count), jnp.float32), scratch, scratch],
         compiler_params=SMALL,
@@ -429,24 +433,18 @@
     )(*blocks, arrived, weights, *split_table(forward_table), *inverse_tables)
 
 
-def keep_kernel(modes_ref, inverse_high, inverse_low, mixed_ref, keep_ref):
-    count = mixed_ref.shape[1]
-    feat_count = modes_ref.shape[1]
-    for part in range(2):
-        mixed_ref[0, :, part * feat_count : (part + 1) * feat_count] = modes_ref[
-            part * count : (part + 1) * count
-        ]
-    keep_ref[...] = back_rows(inverse_high, inverse_low, modes_ref[...], keep_ref.shape, 0)
+def keep_kernel(modes_ref, inverse_high, inverse_low, far_ref, near_ref):
+    half = far_ref.shape[0]
+    shape = (2 * half,) + far_ref.shape[1:]
+    keep = back_rows(inverse_high, inverse_low, modes_ref[...], shape, 0)
+    far_ref[...] = keep[:half]
+    near_ref[...] = keep[half:]
 
 
 def keep_rows(modes, inverse_tables, like):
-    rows, feat_count = modes.shape
     return pl.pallas_call(
         keep_kernel,
-        out_shape=[
-            jax.ShapeDtypeStruct((1, rows // 2, 2 * feat_count), jnp.float32),
-            jax.ShapeDtypeStruct(like.shape, jnp.float32),
-        ],
+        out_shape=[jax.ShapeDtypeStruct(like.shape, jnp.float32)] * 2,
         compiler_params=SMALL,
         name="keep_rows",
     )(modes, *inverse_tables)
@@ -460,10 +458,11 @@
     return half + half * jnp.tanh(half * inner)
 
 
-def output_kernel(layers, flow_ref, table_ref, local_ref, bias_ref, *refs):
-    own_refs = refs[:layers]
-    core_refs = [ref.at[index] for ref in refs[layers : layers + 2] for index in range(layers // 2)]
-    out_hbm, order_ref, wide_ref, level_ref, done_ref, sent = refs[layers + 2 :]
+def output_kernel(layers, flow_ref, table_ref, local_ref, bias_ref, modes_ref, *refs):
+    own_refs = refs[layers // 2 : layers] + refs[: layers // 2]
+    near_ref, far_ref = refs[layers : layers + 2]
+    core_refs = [ref.at[index] for ref in (far_ref, near_ref) for index in range(layers // 2)]
+    out_hbm, mixed_hbm, order_ref, wide_ref, level_ref, done_ref, sent = refs[layers + 2 :]
     cells_x, _, feat_count = flow_ref.shape
     channels = local_ref.shape[0]
     z, x, y = quad()
@@ -485,7 +484,17 @@
         for turn, block_ref in zip(turns(layers), block_refs):
             order_ref[:, (z ^ turn) * 2 + column] = block_ref[...]
     table = table_ref[y, x ^ y]
+    count = modes_ref.shape[0] // 2
     copies = []
+    for part in range(2):
+        copies.append(
+            pltpu.make_async_copy(
+                modes_ref.at[pl.ds(part * count, count)],
+                mixed_hbm.at[0, :, pl.ds(part * feat_count, feat_count)],
+                sent.at[cells_x + part],
+            )
+        )
+        copies[-1].start()
     for cell in range(cells_x):
         high, low = split_terms(order_ref[cell].reshape(-1, feat_count))
         stack = jnp.concatenate([high, low, high], axis=0)
@@ -502,23 +511,27 @@
         copy.wait()
 
 
-def make_output(flow_field, parts, table, local, bias):
+def make_output(flow_field, parts, table, local, bias, modes):
     cells_x, _, feat_count = flow_field.shape
     layers = len(parts) - 2
+    rows, _ = modes.shape
     return pl.pallas_call(
         functools.partial(output_kernel, layers),
-        out_specs=pl.BlockSpec(memory_space=pl.ANY),
+        out_specs=[pl.BlockSpec(memory_space=pl.ANY)] * 2,
         scratch_shapes=[
             pltpu.VMEM((cells_x, 2 * layers) + parts[0].shape[1:], jnp.float32),
             pltpu.VMEM((WIDTH, WIDTH), jnp.bfloat16),
             pltpu.VMEM((1, WIDTH), jnp.float32),
             pltpu.VMEM(flow_field.shape, jnp.bfloat16),
-            pltpu.SemaphoreType.DMA((cells_x,)),
+            pltpu.SemaphoreType.DMA((cells_x + 2,)),
         ],
-        out_shape=jax.ShapeDtypeStruct(flow_field.shape, jnp.bfloat16),
+        out_shape=[
+            jax.ShapeDtypeStruct(flow_field.shape, jnp.bfloat16),
+            jax.ShapeDtypeStruct((1, rows // 2, 2 * feat_count), jnp.float32),
+        ],
         compiler_params=SMALL,
         name="make_output",
-    )(flow_field, table, local, bias, *parts)
+    )(flow_field, table, local, bias, modes, *parts)
 
 
 def row_body(flow_field, spectral_weight, local_weight, bias_terms):
@@ -530,22 +543,25 @@
     inverse_scale = 1.0 / math.sqrt(MX * MY)
 
     send, keep = forward_y(flow_field, cells_y * groups_y, peers // 2, rows_ky)
-    blocks = along_columns(add_blocks(keep, flip_core(send)), peers)
+    order = turns(peers // 2)
+    blocks = along_columns(add_blocks(keep, flip_core(send)), peers, order)
     inverse_tables = split_table(inverse_x_table(cells_x, peers, rows_ky))
-    modes, send = mix(
+    modes, far, near = mix(
         blocks,
         flip_core(second_halves(blocks)),
         spectral_weight,
         forward_x_table(cells_x, peers, rows_ky) * forward_scale,
         inverse_tables,
     )
-    arrived = flip_core(send)
-    mixed, keep = keep_rows(modes, inverse_tables, send)
-    own = along_columns(join_blocks(keep, arrived, cells_x), peers)
-    middle = len(own) // 2
-    parts = own + [flip_core(stack_blocks(half)) for half in (own[:middle], own[middle:])]
+    middle = peers // 4
+    arrived_near, arrived_far = flip_core(near), flip_core(far)
+    keep_far, keep_near = keep_rows(modes, inverse_tables, far)
+    own_near = along_columns(join_blocks(keep_near, arrived_near, cells_x), peers, order[middle:])
+    own_far = along_columns(join_blocks(keep_far, arrived_far, cells_x), peers, order[:middle])
+    flipped = [flip_core(stack_blocks(own)) for own in (own_near, own_far)]
+    parts = own_near + own_far + flipped
     table = output_table(inverse_y_table(cells_y, groups_y, peers, rows_ky) * (0.5 * inverse_scale))
-    return make_output(flow_field, parts, table, local_weight, bias_terms), mixed
+    return tuple(make_output(flow_field, parts, table, local_weight, bias_terms, modes))
 
 
 def body(flow_field, spectral_weight, local_weight, bias_terms):

time: 33.9 us -> 34 us (level)
  Pallas kernels: 5.95 us -> 5.4 us
    pallas_call x2, Pallas kernels: 3.06 us -> 2.51 us  [the longest x1 2.31 us: make_output(): pl.pallas_call(functools.partial(output_kernel, layers), out_specs=[pl.Bl...]
    ppermute x5 -> x6, waiting for transfers between devices: 3.53 us -> 3.76 us  [flip_core(): return lax.ppermute(block, 'gy', [(0, 1), (1, 0)])]
    ppermute x5 -> x6, starting transfers between devices: 2.1 us -> 2.28 us  [flip_core(): return lax.ppermute(block, 'gy', [(0, 1), (1, 0)])]
  transfers between devices with their start and end apart: 13 -> 14, of which waited for: 11 -> 11; matrix products, arithmetic and copies ran while one was open for 0% -> 0% of each run, Pallas kernels for 2% -> 1%
where the time goes in v29:
time: 34 us; the launch traced here: 33.8 us
  waiting for transfers between devices  13.8 us (41%)
  starting transfers between devices  13.7 us (40%)
  Pallas kernels  5.4 us (16%)
  between operations  0.78 us (2%)
    ppermute x8, starting transfers between devices, along_columns(): arrived.append(lax.ppermute(block, ('gx', 'gy'), pairs))  11.5 us
    ppermute x8, waiting for transfers between devices, along_columns(): arrived.append(lax.ppermute(block, ('gx', 'gy'), pairs))  10.1 us
    ppermute x6, waiting for transfers between devices, flip_core(): return lax.ppermute(block, 'gy', [(0, 1), (1, 0)])  3.76 us
    pallas_call x1, Pallas kernels, make_output(): pl.pallas_call(functools.partial(output_kernel, layers), out_specs=[pl.Bl...  2.31 us
    ppermute x6, starting transfers between devices, flip_core(): return lax.ppermute(block, 'gy', [(0, 1), (1, 0)])  2.28 us
    pallas_call x1, Pallas kernels, forward_y(): pl.pallas_call(functools.partial(forward_y_kernel, extent, rows_ky), in_s...  1.75 us
    pallas_call x1, Pallas kernels, mix(): pl.pallas_call(functools.partial(mix_kernel, layers), out_shape=[jax.Shap...  1.05 us
  transfers between devices with their start and end apart: 14, of which 11 were waited for; matrix products, arithmetic and copies ran while one was open for 0% of the time, Pallas kernels for 1%

profile of v29, /device:TPU:0, one launch (start us, length us, event | category | flops | bytes accessed | tf_op | source)
XLA Modules:
  0.0 33.8 jit_solution(14723115919590665809)
XLA Ops:
  0.6 1.7 %forward_y.1 = (f32[4,2,16,512]{3,2,1,0:T(8,128)S(1)}, f32[4,2,16,512]{3,2,1,0:T(8,128)S(1)}) custom-call(bf16[4,256,512]{2,1,0:T(8,128)(2,1)} %flow_ref.1), custom_call_target="tpu_custom_call" | custom-call | tf_op jit(solution)/shard_map/forward_y/pallas_call | solution.py:268
  2.4 0.5 %collective-permute-start = (f32[4,2,16,512]{3,2,1,0:T(8,128)S(1)}, f32[4,2,16,512]{3,2,1,0:T(8,128)S(1)}, u32[]{:S(2)}, u32[]{:S(2)}) collective-permute-start(f32[4,2,16,512]{3,2,1,0:T(8,128)S(1)} %get-tuple-element.18), channel_id=1, source_target_pairs={{0,1},{1,0},{2,3},{3,2},{4,5},{5,4},{6,7},{7,6},{8,9},{9,8},{10,11... | collective-permute-start | bytes 786440 | tf_op jit(solution)/shard_map/ppermute | solution.py:282
  2.9 1.2 %collective-permute-done.arrived_ref = f32[4,2,16,512]{3,2,1,0:T(8,128)S(1)} collective-permute-done((f32[4,2,16,512]{3,2,1,0:T(8,128)S(1)}, f32[4,2,16,512]{3,2,1,0:T(8,128)S(1)}, u32[]{:S(2)}, u32[]{:S(2)}) %collective-permute-start) | collective-permute-done | bytes 262176 | tf_op jit(solution)/shard_map/ppermute | solution.py:282
  4.1 4.0 %collective-permute-start.1 = (f32[2,16,512]{2,1,0:T(8,128)S(1)}, f32[2,16,512]{2,1,0:T(8,128)S(1)}, u32[]{:S(2)}, u32[]{:S(2)}) collective-permute-start(f32[2,16,512]{2,1,0:T(8,128)S(1)} %get-tuple-element.19), channel_id=1, source_target_pairs={{0,8},{1,11},{2,10},{3,9},{4,12},{5,15},{6,14},{7,13},{8,0},{9,3},... | collective-permute-start | bytes 196616 | tf_op jit(solution)/shard_map/ppermute | solution.py:293
  8.1 1.3 %collective-permute-start.2 = (f32[2,16,512]{2,1,0:T(8,128)S(1)}, f32[2,16,512]{2,1,0:T(8,128)S(1)}, u32[]{:S(2)}, u32[]{:S(2)}) collective-permute-start(f32[2,16,512]{2,1,0:T(8,128)S(1)} %get-tuple-element.20), channel_id=1, source_target_pairs={{0,12},{1,15},{2,14},{3,13},{4,8},{5,11},{6,10},{7,9},{8,4},{9,7},... | collective-permute-start | bytes 196616 | tf_op jit(solution)/shard_map/ppermute | solution.py:293
  9.7 0.8 %collective-permute-start.4 = (f32[2,16,512]{2,1,0:T(8,128)S(1)}, f32[2,16,512]{2,1,0:T(8,128)S(1)}, u32[]{:S(2)}, u32[]{:S(2)}) collective-permute-start(f32[2,16,512]{2,1,0:T(8,128)S(1)} %get-tuple-element.22), channel_id=1, source_target_pairs={{0,0},{1,3},{2,2},{3,1},{4,4},{5,7},{6,6},{7,5},{8,8},{9,11},{10,1... | collective-permute-start | bytes 196616 | tf_op jit(solution)/shard_map/ppermute | solution.py:293
  10.7 4.1 %collective-permute-done.2.refs_1_ = f32[2,16,512]{2,1,0:T(8,128)S(1)} collective-permute-done((f32[2,16,512]{2,1,0:T(8,128)S(1)}, f32[2,16,512]{2,1,0:T(8,128)S(1)}, u32[]{:S(2)}, u32[]{:S(2)}) %collective-permute-start.2) | collective-permute-done | bytes 65568 | tf_op jit(solution)/shard_map/ppermute | solution.py:293
  14.8 0.7 %collective-permute-done.3.refs_2_ = f32[2,16,512]{2,1,0:T(8,128)S(1)} collective-permute-done((f32[2,16,512]{2,1,0:T(8,128)S(1)}, f32[2,16,512]{2,1,0:T(8,128)S(1)}, u32[]{:S(2)}, u32[]{:S(2)}) %collective-permute-start.3) | collective-permute-done | bytes 65568 | tf_op jit(solution)/shard_map/ppermute | solution.py:293
  15.5 0.3 collective-permute-start.5
  15.9 1.1 %collective-permute-done.5.refs_4_ = f32[4,16,512]{2,1,0:T(8,128)S(1)} collective-permute-done((f32[4,16,512]{2,1,0:T(8,128)S(1)}, f32[4,16,512]{2,1,0:T(8,128)S(1)}, u32[]{:S(2)}, u32[]{:S(2)}) %collective-permute-start.5) | collective-permute-done | bytes 131104 | tf_op jit(solution)/shard_map/ppermute | solution.py:282
  17.0 1.0 %mix.1 = (f32[128,512]{1,0:T(8,128)S(1)}, f32[2,16,512]{2,1,0:T(8,128)S(1)}, f32[2,16,512]{2,1,0:T(8,128)S(1)}) custom-call(f32[2,16,512]{2,1,0:T(8,128)S(1)} %collective-permute-done.1.refs_0_, f32[2,16,512]{2,1,0:T(8,128)S(1)} %collective-permute-done.2.refs_1_, f32[2,16,512]{2,1,0:T(8,128)S(1)} %collective-permute-done.3.refs_2_, ...), custom_call_target="tpu_custom_call" | custom-call | tf_op jit(solution)/shard_map/mix/pallas_call | solution.py:423
  18.0 0.3 collective-permute-start.9
  18.4 0.2 collective-permute-start.6
  18.8 0.5 %collective-permute-done.9.arrived_ref = f32[2,16,512]{2,1,0:T(8,128)S(1)} collective-permute-done((f32[2,16,512]{2,1,0:T(8,128)S(1)}, f32[2,16,512]{2,1,0:T(8,128)S(1)}, u32[]{:S(2)}, u32[]{:S(2)}) %collective-permute-start.9) | collective-permute-done | bytes 65568 | tf_op jit(solution)/shard_map/ppermute | solution.py:282
  19.4 3.0 %collective-permute-start.10 = (f32[4,8,512]{2,1,0:T(8,128)S(1)}, f32[4,8,512]{2,1,0:T(8,128)S(1)}, u32[]{:S(2)}, u32[]{:S(2)}) collective-permute-start(f32[4,8,512]{2,1,0:T(8,128)S(1)} %get-tuple-element.30), channel_id=1, source_target_pairs={{0,8},{1,11},{2,10},{3,9},{4,12},{5,15},{6,14},{7,13},{8,0},{9,3},... | collective-permute-start | bytes 196616 | tf_op jit(solution)/shard_map/ppermute | solution.py:293
  22.4 1.3 %collective-permute-start.11 = (f32[4,8,512]{2,1,0:T(8,128)S(1)}, f32[4,8,512]{2,1,0:T(8,128)S(1)}, u32[]{:S(2)}, u32[]{:S(2)}) collective-permute-start(f32[4,8,512]{2,1,0:T(8,128)S(1)} %get-tuple-element.31), channel_id=1, source_target_pairs={{0,12},{1,15},{2,14},{3,13},{4,8},{5,11},{6,10},{7,9},{8,4},{9,7},... | collective-permute-start | bytes 196616 | tf_op jit(solution)/shard_map/ppermute | solution.py:293
  23.8 0.7 %collective-permute-start.8 = (f32[4,8,512]{2,1,0:T(8,128)S(1)}, f32[4,8,512]{2,1,0:T(8,128)S(1)}, u32[]{:S(2)}, u32[]{:S(2)}) collective-permute-start(f32[4,8,512]{2,1,0:T(8,128)S(1)} %get-tuple-element.27), channel_id=1, source_target_pairs={{0,0},{1,3},{2,2},{3,1},{4,4},{5,7},{6,6},{7,5},{8,8},{9,11},{10,1... | collective-permute-start | bytes 196616 | tf_op jit(solution)/shard_map/ppermute | solution.py:293
  24.5 1.8 %collective-permute-done.10.refs_0_.refs_2_ = f32[4,8,512]{2,1,0:T(8,128)S(1)} collective-permute-done((f32[4,8,512]{2,1,0:T(8,128)S(1)}, f32[4,8,512]{2,1,0:T(8,128)S(1)}, u32[]{:S(2)}, u32[]{:S(2)}) %collective-permute-start.10) | collective-permute-done | bytes 65568 | tf_op jit(solution)/shard_map/ppermute | solution.py:293
  26.3 2.9 %collective-permute-done.11.refs_1_.refs_3_ = f32[4,8,512]{2,1,0:T(8,128)S(1)} collective-permute-done((f32[4,8,512]{2,1,0:T(8,128)S(1)}, f32[4,8,512]{2,1,0:T(8,128)S(1)}, u32[]{:S(2)}, u32[]{:S(2)}) %collective-permute-start.11) | collective-permute-done | bytes 65568 | tf_op jit(solution)/shard_map/ppermute | solution.py:293
  29.3 0.3 collective-permute-start.13
  29.6 0.3 collective-permute-done.7.refs_0_
  29.9 0.5 %collective-permute-start.12 = (f32[2,4,8,512]{3,2,1,0:T(8,128)S(1)}, f32[2,4,8,512]{3,2,1,0:T(8,128)S(1)}, u32[]{:S(2)}, u32[]{:S(2)}) collective-permute-start(f32[2,4,8,512]{3,2,1,0:T(8,128)S(1)} %stack_blocks.2), channel_id=1, source_target_pairs={{0,1},{1,0},{2,3},{3,2},{4,5},{5,4},{6,7},{7,6},{8,9},{9,8},{10,11... | collective-permute-start | bytes 393224 | tf_op jit(solution)/shard_map/ppermute | solution.py:282
  30.7 0.8 %collective-permute-done.12.refs_4_ = f32[2,4,8,512]{3,2,1,0:T(8,128)S(1)} collective-permute-done((f32[2,4,8,512]{3,2,1,0:T(8,128)S(1)}, f32[2,4,8,512]{3,2,1,0:T(8,128)S(1)}, u32[]{:S(2)}, u32[]{:S(2)}) %collective-permute-start.12) | collective-permute-done | bytes 131104 | tf_op jit(solution)/shard_map/ppermute | solution.py:282
  31.5 2.3 %make_output.1 = (bf16[4,256,512]{2,1,0:T(8,128)(2,1)}, f32[1,64,1024]{2,1,0:T(8,128)}) custom-call(bf16[4,256,512]{2,1,0:T(8,128)(2,1)S(1)} %copy-done, bf16[2,2,256,256]{3,2,1,0:T(8,128)(2,1)S(1)} %copy-done.2, bf16[64,64]{1,0:T(8,128)(2,1)S(1)} %copy-done.7, f32[64]{0:T(128)S(1)} %copy-done.8, f32[128,512]{1,0:T(8,128)S(1)} %get-tuple-element.23.modes_ref, ...), custom_call_target="tpu_custom_call" | custom-call | tf_op jit(solution)/shard_map/make_output/pallas_call | solution.py:518
  (32 shorter events, 1.1 us)
Async XLA Ops:
  0.6 16.3 %copy-start.1 = (bf16[1,64,64,128]{3,2,1,0:T(8,128)(2,1)S(1)}, bf16[1,64,64,128]{3,2,1,0:T(8,128)(2,1)}, u32[]{:S(2)}) copy-start(bf16[1,64,64,128]{3,2,1,0:T(8,128)(2,1)} %refs_5_.1) | copy-start | bytes 3145732
  2.4 1.7 %collective-permute-start = (f32[4,2,16,512]{3,2,1,0:T(8,128)S(1)}, f32[4,2,16,512]{3,2,1,0:T(8,128)S(1)}, u32[]{:S(2)}, u32[]{:S(2)}) collective-permute-start(f32[4,2,16,512]{3,2,1,0:T(8,128)S(1)} %get-tuple-element.18), channel_id=1, source_target_pairs={{0,1},{1,0},{2,3},{3,2},{4,5},{5,4},{6,7},{7,6},{8,9},{9,8},{10,11... | collective-permute-start | bytes 786440 | tf_op jit(solution)/shard_map/ppermute | solution.py:282
  4.1 6.6 %collective-permute-start.1 = (f32[2,16,512]{2,1,0:T(8,128)S(1)}, f32[2,16,512]{2,1,0:T(8,128)S(1)}, u32[]{:S(2)}, u32[]{:S(2)}) collective-permute-start(f32[2,16,512]{2,1,0:T(8,128)S(1)} %get-tuple-element.19), channel_id=1, source_target_pairs={{0,8},{1,11},{2,10},{3,9},{4,12},{5,15},{6,14},{7,13},{8,0},{9,3},... | collective-permute-start | bytes 196616 | tf_op jit(solution)/shard_map/ppermute | solution.py:293
  8.1 6.7 %collective-permute-start.2 = (f32[2,16,512]{2,1,0:T(8,128)S(1)}, f32[2,16,512]{2,1,0:T(8,128)S(1)}, u32[]{:S(2)}, u32[]{:S(2)}) collective-permute-start(f32[2,16,512]{2,1,0:T(8,128)S(1)} %get-tuple-element.20), channel_id=1, source_target_pairs={{0,12},{1,15},{2,14},{3,13},{4,8},{5,11},{6,10},{7,9},{8,4},{9,7},... | collective-permute-start | bytes 196616 | tf_op jit(solution)/shard_map/ppermute | solution.py:293
  9.5 6.0 %collective-permute-start.3 = (f32[2,16,512]{2,1,0:T(8,128)S(1)}, f32[2,16,512]{2,1,0:T(8,128)S(1)}, u32[]{:S(2)}, u32[]{:S(2)}) collective-permute-start(f32[2,16,512]{2,1,0:T(8,128)S(1)} %get-tuple-element.21), channel_id=1, source_target_pairs={{0,4},{1,7},{2,6},{3,5},{4,0},{5,3},{6,2},{7,1},{8,12},{9,15},{10,... | collective-permute-start | bytes 196616 | tf_op jit(solution)/shard_map/ppermute | solution.py:293
  9.7 7.2 %copy-start.3 = (bf16[2,4,16,128]{3,2,1,0:T(8,128)(2,1)S(1)}, bf16[2,4,16,128]{3,2,1,0:T(8,128)(2,1)}, u32[]{:S(2)}) copy-start(bf16[2,4,16,128]{3,2,1,0:T(8,128)(2,1)} %constant.13.clone.refs_9_.inverse_low) | copy-start | bytes 98308
  9.7 7.2 %copy-start.4 = (bf16[2,4,16,128]{3,2,1,0:T(8,128)(2,1)S(1)}, bf16[2,4,16,128]{3,2,1,0:T(8,128)(2,1)}, u32[]{:S(2)}) copy-start(bf16[2,4,16,128]{3,2,1,0:T(8,128)(2,1)} %constant.12.clone.refs_8_.inverse_high) | copy-start | bytes 98308
  9.7 7.3 %copy-start.5 = (bf16[128,128]{1,0:T(8,128)(2,1)S(1)}, bf16[128,128]{1,0:T(8,128)(2,1)}, u32[]{:S(2)}) copy-start(bf16[128,128]{1,0:T(8,128)(2,1)} %constant.11.clone.refs_7_) | copy-start | bytes 98308
  9.7 7.3 %copy-start.6 = (bf16[128,128]{1,0:T(8,128)(2,1)S(1)}, bf16[128,128]{1,0:T(8,128)(2,1)}, u32[]{:S(2)}) copy-start(bf16[128,128]{1,0:T(8,128)(2,1)} %constant.10.clone.refs_6_) | copy-start | bytes 98308
  9.7 5.8 %collective-permute-start.4 = (f32[2,16,512]{2,1,0:T(8,128)S(1)}, f32[2,16,512]{2,1,0:T(8,128)S(1)}, u32[]{:S(2)}, u32[]{:S(2)}) collective-permute-start(f32[2,16,512]{2,1,0:T(8,128)S(1)} %get-tuple-element.22), channel_id=1, source_target_pairs={{0,0},{1,3},{2,2},{3,1},{4,4},{5,7},{6,6},{7,5},{8,8},{9,11},{10,1... | collective-permute-start | bytes 196616 | tf_op jit(solution)/shard_map/ppermute | solution.py:293
  15.5 15.9 %copy-start = (bf16[4,256,512]{2,1,0:T(8,128)(2,1)S(1)}, bf16[4,256,512]{2,1,0:T(8,128)(2,1)}, u32[]{:S(2)}) copy-start(bf16[4,256,512]{2,1,0:T(8,128)(2,1)} %flow_ref.1) | copy-start | bytes 3145732
  15.5 1.4 %collective-permute-start.5 = (f32[4,16,512]{2,1,0:T(8,128)S(1)}, f32[4,16,512]{2,1,0:T(8,128)S(1)}, u32[]{:S(2)}, u32[]{:S(2)}) collective-permute-start(f32[4,16,512]{2,1,0:T(8,128)S(1)} %second_halves.1), channel_id=1, source_target_pairs={{0,1},{1,0},{2,3},{3,2},{4,5},{5,4},{6,7},{7,6},{8,9},{9,8},{10,11... | collective-permute-start | bytes 393224 | tf_op jit(solution)/shard_map/ppermute | solution.py:282
  18.0 1.3 %collective-permute-start.9 = (f32[2,16,512]{2,1,0:T(8,128)S(1)}, f32[2,16,512]{2,1,0:T(8,128)S(1)}, u32[]{:S(2)}, u32[]{:S(2)}) collective-permute-start(f32[2,16,512]{2,1,0:T(8,128)S(1)} %get-tuple-element.29), channel_id=1, source_target_pairs={{0,1},{1,0},{2,3},{3,2},{4,5},{5,4},{6,7},{7,6},{8,9},{9,8},{10,11... | collective-permute-start | bytes 196616 | tf_op jit(solution)/shard_map/ppermute | solution.py:282
  18.4 5.3 %collective-permute-start.6 = (f32[2,16,512]{2,1,0:T(8,128)S(1)}, f32[2,16,512]{2,1,0:T(8,128)S(1)}, u32[]{:S(2)}, u32[]{:S(2)}) collective-permute-start(f32[2,16,512]{2,1,0:T(8,128)S(1)} %get-tuple-element.25), channel_id=1, source_target_pairs={{0,1},{1,0},{2,3},{3,2},{4,5},{5,4},{6,7},{7,6},{8,9},{9,8},{10,11... | collective-permute-start | bytes 196616 | tf_op jit(solution)/shard_map/ppermute | solution.py:282
  18.6 12.9 %copy-start.2 = (bf16[2,2,256,256]{3,2,1,0:T(8,128)(2,1)S(1)}, bf16[2,2,256,256]{3,2,1,0:T(8,128)(2,1)}, u32[]{:S(2)}) copy-start(bf16[2,2,256,256]{3,2,1,0:T(8,128)(2,1)} %constant.14.clone.table_ref) | copy-start | bytes 1572868
  19.4 7.0 %collective-permute-start.10 = (f32[4,8,512]{2,1,0:T(8,128)S(1)}, f32[4,8,512]{2,1,0:T(8,128)S(1)}, u32[]{:S(2)}, u32[]{:S(2)}) collective-permute-start(f32[4,8,512]{2,1,0:T(8,128)S(1)} %get-tuple-element.30), channel_id=1, source_target_pairs={{0,8},{1,11},{2,10},{3,9},{4,12},{5,15},{6,14},{7,13},{8,0},{9,3},... | collective-permute-start | bytes 196616 | tf_op jit(solution)/shard_map/ppermute | solution.py:293
  22.4 6.9 %collective-permute-start.11 = (f32[4,8,512]{2,1,0:T(8,128)S(1)}, f32[4,8,512]{2,1,0:T(8,128)S(1)}, u32[]{:S(2)}, u32[]{:S(2)}) collective-permute-start(f32[4,8,512]{2,1,0:T(8,128)S(1)} %get-tuple-element.31), channel_id=1, source_target_pairs={{0,12},{1,15},{2,14},{3,13},{4,8},{5,11},{6,10},{7,9},{8,4},{9,7},... | collective-permute-start | bytes 196616 | tf_op jit(solution)/shard_map/ppermute | solution.py:293
  23.7 6.2 %collective-permute-start.7 = (f32[4,8,512]{2,1,0:T(8,128)S(1)}, f32[4,8,512]{2,1,0:T(8,128)S(1)}, u32[]{:S(2)}, u32[]{:S(2)}) collective-permute-start(f32[4,8,512]{2,1,0:T(8,128)S(1)} %get-tuple-element.26), channel_id=1, source_target_pairs={{0,4},{1,7},{2,6},{3,5},{4,0},{5,3},{6,2},{7,1},{8,12},{9,15},{10,... | collective-permute-start | bytes 196616 | tf_op jit(solution)/shard_map/ppermute | solution.py:293
  23.8 6.1 %collective-permute-start.8 = (f32[4,8,512]{2,1,0:T(8,128)S(1)}, f32[4,8,512]{2,1,0:T(8,128)S(1)}, u32[]{:S(2)}, u32[]{:S(2)}) collective-permute-start(f32[4,8,512]{2,1,0:T(8,128)S(1)} %get-tuple-element.27), channel_id=1, source_target_pairs={{0,0},{1,3},{2,2},{3,1},{4,4},{5,7},{6,6},{7,5},{8,8},{9,11},{10,1... | collective-permute-start | bytes 196616 | tf_op jit(solution)/shard_map/ppermute | solution.py:293
  29.3 2.2 %copy-start.7 = (bf16[64,64]{1,0:T(8,128)(2,1)S(1)}, bf16[64,64]{1,0:T(8,128)(2,1)}, u32[]{:S(2)}) copy-start(bf16[64,64]{1,0:T(8,128)(2,1)} %local_ref.1) | copy-start | bytes 24580
  29.3 2.2 %copy-start.8 = (f32[64]{0:T(128)S(1)}, f32[64]{0:T(128)}, u32[]{:S(2)}) copy-start(f32[64]{0:T(128)} %bias_ref.1) | copy-start | bytes 772
  29.3 1.4 %collective-permute-start.13 = (f32[2,4,8,512]{3,2,1,0:T(8,128)S(1)}, f32[2,4,8,512]{3,2,1,0:T(8,128)S(1)}, u32[]{:S(2)}, u32[]{:S(2)}) collective-permute-start(f32[2,4,8,512]{3,2,1,0:T(8,128)S(1)} %stack_blocks.3), channel_id=1, source_target_pairs={{0,1},{1,0},{2,3},{3,2},{4,5},{5,4},{6,7},{7,6},{8,9},{9,8},{10,11... | collective-permute-start | bytes 393224 | tf_op jit(solution)/shard_map/ppermute | solution.py:282
  29.9 1.5 %collective-permute-start.12 = (f32[2,4,8,512]{3,2,1,0:T(8,128)S(1)}, f32[2,4,8,512]{3,2,1,0:T(8,128)S(1)}, u32[]{:S(2)}, u32[]{:S(2)}) collective-permute-start(f32[2,4,8,512]{3,2,1,0:T(8,128)S(1)} %stack_blocks.2), channel_id=1, source_target_pairs={{0,1},{1,0},{2,3},{3,2},{4,5},{5,4},{6,7},{7,6},{8,9},{9,8},{10,11... | collective-permute-start | bytes 393224 | tf_op jit(solution)/shard_map/ppermute | solution.py:282

commit v30 on v29

--- a/solution.py
+++ b/solution.py
@@ -244,8 +244,10 @@
     return jnp.where(row % 2 == 0, jnp.cos(angle), -jnp.sin(angle)).astype(jnp.bfloat16)
 
 
-def forward_y_kernel(extent, rows_ky, flow_hbm, send_ref, keep_ref, flow_ref, arrived):
-    layers, _, rows, feat_count = send_ref.shape
+def forward_y_kernel(extent, rows_ky, flow_hbm, *refs):
+    out_refs, (flow_ref, arrived) = refs[:4], refs[4:]
+    half, _, rows, feat_count = out_refs[0].shape
+    layers = 2 * half
     cells_x, cells_y, _ = flow_ref.shape
     rows = rows // cells_x
     copies = [
@@ -257,18 +259,18 @@
     table = forward_y_table((2 * MY, cells_y), extent, layers, rows_ky)
     for x in range(cells_x):
         copies[x].wait()
-        result = dot(table, flow_ref[x]).reshape(2, layers, 2, rows, feat_count)
-        send_ref[:, :, x * rows : (x + 1) * rows, :] = result[0]
-        keep_ref[:, :, x * rows : (x + 1) * rows, :] = result[1]
+        result = dot(table, flow_ref[x]).reshape(4, half, 2, rows, feat_count)
+        for index, out_ref in enumerate(out_refs):
+            out_ref[:, :, x * rows : (x + 1) * rows, :] = result[index]
 
 
 def forward_y(flow_field, extent, layers, rows_ky):
     cells_x, _, feat_count = flow_field.shape
-    shape = jax.ShapeDtypeStruct((layers, 2, cells_x * 2 * rows_ky, feat_count), jnp.float32)
+    shape = jax.ShapeDtypeStruct((layers // 2, 2, cells_x * 2 * rows_ky, feat_count), jnp.float32)
     return pl.pallas_call(
         functools.partial(forward_y_kernel, extent, rows_ky),
         in_specs=[pl.BlockSpec(memory_space=pltpu.HBM)],
-        out_shape=[shape] * 2,
+        out_shape=[shape] * 4,
         scratch_shapes=[
             pltpu.VMEM(flow_field.shape, flow_field.dtype),
             pltpu.SemaphoreType.DMA((cells_x,)),
@@ -542,9 +544,14 @@
     forward_scale = 1.0 / math.sqrt(cells_x * peers * cells_y * groups_y)
     inverse_scale = 1.0 / math.sqrt(MX * MY)
 
-    send, keep = forward_y(flow_field, cells_y * groups_y, peers // 2, rows_ky)
+    send_far, send_near, keep_far, keep_near = forward_y(
+        flow_field, cells_y * groups_y, peers // 2, rows_ky
+    )
     order = turns(peers // 2)
-    blocks = along_columns(add_blocks(keep, flip_core(send)), peers, order)
+    middle = peers // 4
+    near = along_columns(add_blocks(keep_near, flip_core(send_near)), peers, order[middle:])
+    far = along_columns(add_blocks(keep_far, flip_core(send_far)), peers, order[:middle])
+    blocks = far + near
     inverse_tables = split_table(inverse_x_table(cells_x, peers, rows_ky))
     modes, far, near = mix(
         blocks,
@@ -553,7 +560,6 @@
         forward_x_table(cells_x, peers, rows_ky) * forward_scale,
         inverse_tables,
     )
-    middle = peers // 4
     arrived_near, arrived_far = flip_core(near), flip_core(far)
     keep_far, keep_near = keep_rows(modes, inverse_tables, far)
     own_near = along_columns(join_blocks(keep_near, arrived_near, cells_x), peers, order[middle:])

time: 34 us -> 33.9 us (level)
    ppermute x6 -> x7, waiting for transfers between devices: 3.76 us -> 3.55 us  [flip_core(): return lax.ppermute(block, 'gy', [(0, 1), (1, 0)])]
    ppermute x6 -> x7, starting transfers between devices: 2.28 us -> 2.26 us  [flip_core(): return lax.ppermute(block, 'gy', [(0, 1), (1, 0)])]
  transfers between devices with their start and end apart: 14 -> 15, of which waited for: 11 -> 11; matrix products, arithmetic and copies ran while one was open for 0% -> 0% of each run, Pallas kernels for 1% -> 1%
where the time goes in v30:
time: 33.9 us; the launch traced here: 33.7 us
  starting transfers between devices  13.7 us (40%)
  waiting for transfers between devices  13.7 us (40%)
  Pallas kernels  5.4 us (16%)
  between operations  0.78 us (2%)
    ppermute x8, starting transfers between devices, along_columns(): arrived.append(lax.ppermute(block, ('gx', 'gy'), pairs))  11.5 us
    ppermute x8, waiting for transfers between devices, along_columns(): arrived.append(lax.ppermute(block, ('gx', 'gy'), pairs))  10.2 us
    ppermute x7, waiting for transfers between devices, flip_core(): return lax.ppermute(block, 'gy', [(0, 1), (1, 0)])  3.55 us
    pallas_call x1, Pallas kernels, make_output(): pl.pallas_call(functools.partial(output_kernel, layers), out_specs=[pl.Bl...  2.3 us
    ppermute x7, starting transfers between devices, flip_core(): return lax.ppermute(block, 'gy', [(0, 1), (1, 0)])  2.26 us
    pallas_call x1, Pallas kernels, forward_y(): pl.pallas_call(functools.partial(forward_y_kernel, extent, rows_ky), in_s...  1.75 us
    pallas_call x1, Pallas kernels, mix(): pl.pallas_call(functools.partial(mix_kernel, layers), out_shape=[jax.Shap...  1.04 us
  transfers between devices with their start and end apart: 15, of which 11 were waited for; matrix products, arithmetic and copies ran while one was open for 0% of the time, Pallas kernels for 1%

profile of v30, /device:TPU:0, one launch (start us, length us, event | category | flops | bytes accessed | tf_op | source)
XLA Modules:
  0.0 33.7 jit_solution(6693272525060370637)
XLA Ops:
  0.6 1.7 %forward_y.1 = (f32[2,2,16,512]{3,2,1,0:T(8,128)S(1)}, f32[2,2,16,512]{3,2,1,0:T(8,128)S(1)}, f32[2,2,16,512]{3,2,1,0:T(8,128)S(1)}, f32[2,2,16,512]{3,2,1,0:T(8,128)S(1)}) custom-call(bf16[4,256,512]{2,1,0:T(8,128)(2,1)} %flow_ref.1), custom_call_target="tpu_custom_call" | custom-call | tf_op jit(solution)/shard_map/forward_y/pallas_call | solution.py:270
  2.4 0.5 %collective-permute-start = (f32[2,2,16,512]{3,2,1,0:T(8,128)S(1)}, f32[2,2,16,512]{3,2,1,0:T(8,128)S(1)}, u32[]{:S(2)}, u32[]{:S(2)}) collective-permute-start(f32[2,2,16,512]{3,2,1,0:T(8,128)S(1)} %get-tuple-element.20), channel_id=1, source_target_pairs={{0,1},{1,0},{2,3},{3,2},{4,5},{5,4},{6,7},{7,6},{8,9},{9,8},{10,11... | collective-permute-start | bytes 393224 | tf_op jit(solution)/shard_map/ppermute | solution.py:284
  3.0 0.9 %collective-permute-done.arrived_ref = f32[2,2,16,512]{3,2,1,0:T(8,128)S(1)} collective-permute-done((f32[2,2,16,512]{3,2,1,0:T(8,128)S(1)}, f32[2,2,16,512]{3,2,1,0:T(8,128)S(1)}, u32[]{:S(2)}, u32[]{:S(2)}) %collective-permute-start) | collective-permute-done | bytes 131104 | tf_op jit(solution)/shard_map/ppermute | solution.py:284
  3.9 4.0 %collective-permute-start.1 = (f32[2,16,512]{2,1,0:T(8,128)S(1)}, f32[2,16,512]{2,1,0:T(8,128)S(1)}, u32[]{:S(2)}, u32[]{:S(2)}) collective-permute-start(f32[2,16,512]{2,1,0:T(8,128)S(1)} %get-tuple-element.21), channel_id=1, source_target_pairs={{0,8},{1,11},{2,10},{3,9},{4,12},{5,15},{6,14},{7,13},{8,0},{9,3},... | collective-permute-start | bytes 196616 | tf_op jit(solution)/shard_map/ppermute | solution.py:295
  7.9 1.3 %collective-permute-start.2 = (f32[2,16,512]{2,1,0:T(8,128)S(1)}, f32[2,16,512]{2,1,0:T(8,128)S(1)}, u32[]{:S(2)}, u32[]{:S(2)}) collective-permute-start(f32[2,16,512]{2,1,0:T(8,128)S(1)} %get-tuple-element.22), channel_id=1, source_target_pairs={{0,12},{1,15},{2,14},{3,13},{4,8},{5,11},{6,10},{7,9},{8,4},{9,7},... | collective-permute-start | bytes 196616 | tf_op jit(solution)/shard_map/ppermute | solution.py:295
  9.3 0.3 collective-permute-start.4
  9.6 0.8 %collective-permute-start.5 = (f32[2,16,512]{2,1,0:T(8,128)S(1)}, f32[2,16,512]{2,1,0:T(8,128)S(1)}, u32[]{:S(2)}, u32[]{:S(2)}) collective-permute-start(f32[2,16,512]{2,1,0:T(8,128)S(1)} %get-tuple-element.26), channel_id=1, source_target_pairs={{0,0},{1,3},{2,2},{3,1},{4,4},{5,7},{6,6},{7,5},{8,8},{9,11},{10,1... | collective-permute-start | bytes 196616 | tf_op jit(solution)/shard_map/ppermute | solution.py:295
  10.5 4.1 %collective-permute-done.2.refs_1_ = f32[2,16,512]{2,1,0:T(8,128)S(1)} collective-permute-done((f32[2,16,512]{2,1,0:T(8,128)S(1)}, f32[2,16,512]{2,1,0:T(8,128)S(1)}, u32[]{:S(2)}, u32[]{:S(2)}) %collective-permute-start.2) | collective-permute-done | bytes 65568 | tf_op jit(solution)/shard_map/ppermute | solution.py:295
  14.6 0.8 %collective-permute-done.4.refs_2_ = f32[2,16,512]{2,1,0:T(8,128)S(1)} collective-permute-done((f32[2,16,512]{2,1,0:T(8,128)S(1)}, f32[2,16,512]{2,1,0:T(8,128)S(1)}, u32[]{:S(2)}, u32[]{:S(2)}) %collective-permute-start.4) | collective-permute-done | bytes 65568 | tf_op jit(solution)/shard_map/ppermute | solution.py:295
  15.5 0.3 collective-permute-start.6
  15.8 1.1 %collective-permute-done.6.refs_4_ = f32[4,16,512]{2,1,0:T(8,128)S(1)} collective-permute-done((f32[4,16,512]{2,1,0:T(8,128)S(1)}, f32[4,16,512]{2,1,0:T(8,128)S(1)}, u32[]{:S(2)}, u32[]{:S(2)}) %collective-permute-start.6) | collective-permute-done | bytes 131104 | tf_op jit(solution)/shard_map/ppermute | solution.py:284
  16.9 1.0 %mix.1 = (f32[128,512]{1,0:T(8,128)S(1)}, f32[2,16,512]{2,1,0:T(8,128)S(1)}, f32[2,16,512]{2,1,0:T(8,128)S(1)}) custom-call(f32[2,16,512]{2,1,0:T(8,128)S(1)} %collective-permute-done.1.refs_0_, f32[2,16,512]{2,1,0:T(8,128)S(1)} %collective-permute-done.2.refs_1_, f32[2,16,512]{2,1,0:T(8,128)S(1)} %collective-permute-done.4.refs_2_, ...), custom_call_target="tpu_custom_call" | custom-call | tf_op jit(solution)/shard_map/mix/pallas_call | solution.py:425
  18.0 0.3 collective-permute-start.10
  18.3 0.3 collective-permute-start.7
  18.8 0.5 %collective-permute-done.10.arrived_ref = f32[2,16,512]{2,1,0:T(8,128)S(1)} collective-permute-done((f32[2,16,512]{2,1,0:T(8,128)S(1)}, f32[2,16,512]{2,1,0:T(8,128)S(1)}, u32[]{:S(2)}, u32[]{:S(2)}) %collective-permute-start.10) | collective-permute-done | bytes 65568 | tf_op jit(solution)/shard_map/ppermute | solution.py:284
  19.3 2.9 %collective-permute-start.11 = (f32[4,8,512]{2,1,0:T(8,128)S(1)}, f32[4,8,512]{2,1,0:T(8,128)S(1)}, u32[]{:S(2)}, u32[]{:S(2)}) collective-permute-start(f32[4,8,512]{2,1,0:T(8,128)S(1)} %get-tuple-element.34), channel_id=1, source_target_pairs={{0,8},{1,11},{2,10},{3,9},{4,12},{5,15},{6,14},{7,13},{8,0},{9,3},... | collective-permute-start | bytes 196616 | tf_op jit(solution)/shard_map/ppermute | solution.py:295
  22.3 1.3 %collective-permute-start.12 = (f32[4,8,512]{2,1,0:T(8,128)S(1)}, f32[4,8,512]{2,1,0:T(8,128)S(1)}, u32[]{:S(2)}, u32[]{:S(2)}) collective-permute-start(f32[4,8,512]{2,1,0:T(8,128)S(1)} %get-tuple-element.35), channel_id=1, source_target_pairs={{0,12},{1,15},{2,14},{3,13},{4,8},{5,11},{6,10},{7,9},{8,4},{9,7},... | collective-permute-start | bytes 196616 | tf_op jit(solution)/shard_map/ppermute | solution.py:295
  23.7 0.7 %collective-permute-start.9 = (f32[4,8,512]{2,1,0:T(8,128)S(1)}, f32[4,8,512]{2,1,0:T(8,128)S(1)}, u32[]{:S(2)}, u32[]{:S(2)}) collective-permute-start(f32[4,8,512]{2,1,0:T(8,128)S(1)} %get-tuple-element.31), channel_id=1, source_target_pairs={{0,0},{1,3},{2,2},{3,1},{4,4},{5,7},{6,6},{7,5},{8,8},{9,11},{10,1... | collective-permute-start | bytes 196616 | tf_op jit(solution)/shard_map/ppermute | solution.py:295
  24.4 2.0 %collective-permute-done.11.refs_0_.refs_2_ = f32[4,8,512]{2,1,0:T(8,128)S(1)} collective-permute-done((f32[4,8,512]{2,1,0:T(8,128)S(1)}, f32[4,8,512]{2,1,0:T(8,128)S(1)}, u32[]{:S(2)}, u32[]{:S(2)}) %collective-permute-start.11) | collective-permute-done | bytes 65568 | tf_op jit(solution)/shard_map/ppermute | solution.py:295
  26.4 2.8 %collective-permute-done.12.refs_1_.refs_3_ = f32[4,8,512]{2,1,0:T(8,128)S(1)} collective-permute-done((f32[4,8,512]{2,1,0:T(8,128)S(1)}, f32[4,8,512]{2,1,0:T(8,128)S(1)}, u32[]{:S(2)}, u32[]{:S(2)}) %collective-permute-start.12) | collective-permute-done | bytes 65568 | tf_op jit(solution)/shard_map/ppermute | solution.py:295
  29.4 0.4 %collective-permute-done.8.refs_0_ = f32[4,8,512]{2,1,0:T(8,128)S(1)} collective-permute-done((f32[4,8,512]{2,1,0:T(8,128)S(1)}, f32[4,8,512]{2,1,0:T(8,128)S(1)}, u32[]{:S(2)}, u32[]{:S(2)}) %collective-permute-start.8) | collective-permute-done | bytes 65568 | tf_op jit(solution)/shard_map/ppermute | solution.py:295
  29.8 0.5 %collective-permute-start.13 = (f32[2,4,8,512]{3,2,1,0:T(8,128)S(1)}, f32[2,4,8,512]{3,2,1,0:T(8,128)S(1)}, u32[]{:S(2)}, u32[]{:S(2)}) collective-permute-start(f32[2,4,8,512]{3,2,1,0:T(8,128)S(1)} %stack_blocks.2), channel_id=1, source_target_pairs={{0,1},{1,0},{2,3},{3,2},{4,5},{5,4},{6,7},{7,6},{8,9},{9,8},{10,11... | collective-permute-start | bytes 393224 | tf_op jit(solution)/shard_map/ppermute | solution.py:284
  30.6 0.8 %collective-permute-done.13.refs_4_ = f32[2,4,8,512]{3,2,1,0:T(8,128)S(1)} collective-permute-done((f32[2,4,8,512]{3,2,1,0:T(8,128)S(1)}, f32[2,4,8,512]{3,2,1,0:T(8,128)S(1)}, u32[]{:S(2)}, u32[]{:S(2)}) %collective-permute-start.13) | collective-permute-done | bytes 131104 | tf_op jit(solution)/shard_map/ppermute | solution.py:284
  31.4 2.3 %make_output.1 = (bf16[4,256,512]{2,1,0:T(8,128)(2,1)}, f32[1,64,1024]{2,1,0:T(8,128)}) custom-call(bf16[4,256,512]{2,1,0:T(8,128)(2,1)S(1)} %copy-done, bf16[2,2,256,256]{3,2,1,0:T(8,128)(2,1)S(1)} %copy-done.2, bf16[64,64]{1,0:T(8,128)(2,1)S(1)} %copy-done.7, f32[64]{0:T(128)S(1)} %copy-done.8, f32[128,512]{1,0:T(8,128)S(1)} %get-tuple-element.27.modes_ref, ...), custom_call_target="tpu_custom_call" | custom-call | tf_op jit(solution)/shard_map/make_output/pallas_call | solution.py:520
  (35 shorter events, 1.1 us)
Async XLA Ops:
  0.6 16.3 %copy-start.1 = (bf16[1,64,64,128]{3,2,1,0:T(8,128)(2,1)S(1)}, bf16[1,64,64,128]{3,2,1,0:T(8,128)(2,1)}, u32[]{:S(2)}) copy-start(bf16[1,64,64,128]{3,2,1,0:T(8,128)(2,1)} %refs_5_.1) | copy-start | bytes 3145732
  2.4 1.5 %collective-permute-start = (f32[2,2,16,512]{3,2,1,0:T(8,128)S(1)}, f32[2,2,16,512]{3,2,1,0:T(8,128)S(1)}, u32[]{:S(2)}, u32[]{:S(2)}) collective-permute-start(f32[2,2,16,512]{3,2,1,0:T(8,128)S(1)} %get-tuple-element.20), channel_id=1, source_target_pairs={{0,1},{1,0},{2,3},{3,2},{4,5},{5,4},{6,7},{7,6},{8,9},{9,8},{10,11... | collective-permute-start | bytes 393224 | tf_op jit(solution)/shard_map/ppermute | solution.py:284
  2.9 6.4 %collective-permute-start.3 = (f32[2,2,16,512]{3,2,1,0:T(8,128)S(1)}, f32[2,2,16,512]{3,2,1,0:T(8,128)S(1)}, u32[]{:S(2)}, u32[]{:S(2)}) collective-permute-start(f32[2,2,16,512]{3,2,1,0:T(8,128)S(1)} %get-tuple-element.24), channel_id=1, source_target_pairs={{0,1},{1,0},{2,3},{3,2},{4,5},{5,4},{6,7},{7,6},{8,9},{9,8},{10,11... | collective-permute-start | bytes 393224 | tf_op jit(solution)/shard_map/ppermute | solution.py:284
  3.9 6.6 %collective-permute-start.1 = (f32[2,16,512]{2,1,0:T(8,128)S(1)}, f32[2,16,512]{2,1,0:T(8,128)S(1)}, u32[]{:S(2)}, u32[]{:S(2)}) collective-permute-start(f32[2,16,512]{2,1,0:T(8,128)S(1)} %get-tuple-element.21), channel_id=1, source_target_pairs={{0,8},{1,11},{2,10},{3,9},{4,12},{5,15},{6,14},{7,13},{8,0},{9,3},... | collective-permute-start | bytes 196616 | tf_op jit(solution)/shard_map/ppermute | solution.py:295
  7.9 6.7 %collective-permute-start.2 = (f32[2,16,512]{2,1,0:T(8,128)S(1)}, f32[2,16,512]{2,1,0:T(8,128)S(1)}, u32[]{:S(2)}, u32[]{:S(2)}) collective-permute-start(f32[2,16,512]{2,1,0:T(8,128)S(1)} %get-tuple-element.22), channel_id=1, source_target_pairs={{0,12},{1,15},{2,14},{3,13},{4,8},{5,11},{6,10},{7,9},{8,4},{9,7},... | collective-permute-start | bytes 196616 | tf_op jit(solution)/shard_map/ppermute | solution.py:295
  9.3 6.2 %collective-permute-start.4 = (f32[2,16,512]{2,1,0:T(8,128)S(1)}, f32[2,16,512]{2,1,0:T(8,128)S(1)}, u32[]{:S(2)}, u32[]{:S(2)}) collective-permute-start(f32[2,16,512]{2,1,0:T(8,128)S(1)} %get-tuple-element.25), channel_id=1, source_target_pairs={{0,4},{1,7},{2,6},{3,5},{4,0},{5,3},{6,2},{7,1},{8,12},{9,15},{10,... | collective-permute-start | bytes 196616 | tf_op jit(solution)/shard_map/ppermute | solution.py:295
  9.6 7.3 %copy-start.3 = (bf16[2,4,16,128]{3,2,1,0:T(8,128)(2,1)S(1)}, bf16[2,4,16,128]{3,2,1,0:T(8,128)(2,1)}, u32[]{:S(2)}) copy-start(bf16[2,4,16,128]{3,2,1,0:T(8,128)(2,1)} %constant.13.clone.refs_9_.inverse_low) | copy-start | bytes 98308
  9.6 7.3 %copy-start.4 = (bf16[2,4,16,128]{3,2,1,0:T(8,128)(2,1)S(1)}, bf16[2,4,16,128]{3,2,1,0:T(8,128)(2,1)}, u32[]{:S(2)}) copy-start(bf16[2,4,16,128]{3,2,1,0:T(8,128)(2,1)} %constant.12.clone.refs_8_.inverse_high) | copy-start | bytes 98308
  9.6 7.3 %copy-start.5 = (bf16[128,128]{1,0:T(8,128)(2,1)S(1)}, bf16[128,128]{1,0:T(8,128)(2,1)}, u32[]{:S(2)}) copy-start(bf16[128,128]{1,0:T(8,128)(2,1)} %constant.11.clone.refs_7_) | copy-start | bytes 98308
  9.6 7.3 %copy-start.6 = (bf16[128,128]{1,0:T(8,128)(2,1)S(1)}, bf16[128,128]{1,0:T(8,128)(2,1)}, u32[]{:S(2)}) copy-start(bf16[128,128]{1,0:T(8,128)(2,1)} %constant.10.clone.refs_6_) | copy-start | bytes 98308
  9.6 5.9 %collective-permute-start.5 = (f32[2,16,512]{2,1,0:T(8,128)S(1)}, f32[2,16,512]{2,1,0:T(8,128)S(1)}, u32[]{:S(2)}, u32[]{:S(2)}) collective-permute-start(f32[2,16,512]{2,1,0:T(8,128)S(1)} %get-tuple-element.26), channel_id=1, source_target_pairs={{0,0},{1,3},{2,2},{3,1},{4,4},{5,7},{6,6},{7,5},{8,8},{9,11},{10,1... | collective-permute-start | bytes 196616 | tf_op jit(solution)/shard_map/ppermute | solution.py:295
  15.5 15.9 %copy-start = (bf16[4,256,512]{2,1,0:T(8,128)(2,1)S(1)}, bf16[4,256,512]{2,1,0:T(8,128)(2,1)}, u32[]{:S(2)}) copy-start(bf16[4,256,512]{2,1,0:T(8,128)(2,1)} %flow_ref.1) | copy-start | bytes 3145732
  15.5 1.4 %collective-permute-start.6 = (f32[4,16,512]{2,1,0:T(8,128)S(1)}, f32[4,16,512]{2,1,0:T(8,128)S(1)}, u32[]{:S(2)}, u32[]{:S(2)}) collective-permute-start(f32[4,16,512]{2,1,0:T(8,128)S(1)} %second_halves.1), channel_id=1, source_target_pairs={{0,1},{1,0},{2,3},{3,2},{4,5},{5,4},{6,7},{7,6},{8,9},{9,8},{10,11... | collective-permute-start | bytes 393224 | tf_op jit(solution)/shard_map/ppermute | solution.py:284
  18.0 1.3 %collective-permute-start.10 = (f32[2,16,512]{2,1,0:T(8,128)S(1)}, f32[2,16,512]{2,1,0:T(8,128)S(1)}, u32[]{:S(2)}, u32[]{:S(2)}) collective-permute-start(f32[2,16,512]{2,1,0:T(8,128)S(1)} %get-tuple-element.33), channel_id=1, source_target_pairs={{0,1},{1,0},{2,3},{3,2},{4,5},{5,4},{6,7},{7,6},{8,9},{9,8},{10,11... | collective-permute-start | bytes 196616 | tf_op jit(solution)/shard_map/ppermute | solution.py:284
  18.3 5.3 %collective-permute-start.7 = (f32[2,16,512]{2,1,0:T(8,128)S(1)}, f32[2,16,512]{2,1,0:T(8,128)S(1)}, u32[]{:S(2)}, u32[]{:S(2)}) collective-permute-start(f32[2,16,512]{2,1,0:T(8,128)S(1)} %get-tuple-element.29), channel_id=1, source_target_pairs={{0,1},{1,0},{2,3},{3,2},{4,5},{5,4},{6,7},{7,6},{8,9},{9,8},{10,11... | collective-permute-start | bytes 196616 | tf_op jit(solution)/shard_map/ppermute | solution.py:284
  18.6 12.8 %copy-start.2 = (bf16[2,2,256,256]{3,2,1,0:T(8,128)(2,1)S(1)}, bf16[2,2,256,256]{3,2,1,0:T(8,128)(2,1)}, u32[]{:S(2)}) copy-start(bf16[2,2,256,256]{3,2,1,0:T(8,128)(2,1)} %constant.14.clone.table_ref) | copy-start | bytes 1572868
  19.3 7.0 %collective-permute-start.11 = (f32[4,8,512]{2,1,0:T(8,128)S(1)}, f32[4,8,512]{2,1,0:T(8,128)S(1)}, u32[]{:S(2)}, u32[]{:S(2)}) collective-permute-start(f32[4,8,512]{2,1,0:T(8,128)S(1)} %get-tuple-element.34), channel_id=1, source_target_pairs={{0,8},{1,11},{2,10},{3,9},{4,12},{5,15},{6,14},{7,13},{8,0},{9,3},... | collective-permute-start | bytes 196616 | tf_op jit(solution)/shard_map/ppermute | solution.py:295
  22.3 6.9 %collective-permute-start.12 = (f32[4,8,512]{2,1,0:T(8,128)S(1)}, f32[4,8,512]{2,1,0:T(8,128)S(1)}, u32[]{:S(2)}, u32[]{:S(2)}) collective-permute-start(f32[4,8,512]{2,1,0:T(8,128)S(1)} %get-tuple-element.35), channel_id=1, source_target_pairs={{0,12},{1,15},{2,14},{3,13},{4,8},{5,11},{6,10},{7,9},{8,4},{9,7},... | collective-permute-start | bytes 196616 | tf_op jit(solution)/shard_map/ppermute | solution.py:295
  23.6 6.2 %collective-permute-start.8 = (f32[4,8,512]{2,1,0:T(8,128)S(1)}, f32[4,8,512]{2,1,0:T(8,128)S(1)}, u32[]{:S(2)}, u32[]{:S(2)}) collective-permute-start(f32[4,8,512]{2,1,0:T(8,128)S(1)} %get-tuple-element.30), channel_id=1, source_target_pairs={{0,4},{1,7},{2,6},{3,5},{4,0},{5,3},{6,2},{7,1},{8,12},{9,15},{10,... | collective-permute-start | bytes 196616 | tf_op jit(solution)/shard_map/ppermute | solution.py:295
  23.7 6.1 %collective-permute-start.9 = (f32[4,8,512]{2,1,0:T(8,128)S(1)}, f32[4,8,512]{2,1,0:T(8,128)S(1)}, u32[]{:S(2)}, u32[]{:S(2)}) collective-permute-start(f32[4,8,512]{2,1,0:T(8,128)S(1)} %get-tuple-element.31), channel_id=1, source_target_pairs={{0,0},{1,3},{2,2},{3,1},{4,4},{5,7},{6,6},{7,5},{8,8},{9,11},{10,1... | collective-permute-start | bytes 196616 | tf_op jit(solution)/shard_map/ppermute | solution.py:295
  29.1 2.2 %copy-start.7 = (bf16[64,64]{1,0:T(8,128)(2,1)S(1)}, bf16[64,64]{1,0:T(8,128)(2,1)}, u32[]{:S(2)}) copy-start(bf16[64,64]{1,0:T(8,128)(2,1)} %local_ref.1) | copy-start | bytes 24580
  29.2 2.2 %copy-start.8 = (f32[64]{0:T(128)S(1)}, f32[64]{0:T(128)}, u32[]{:S(2)}) copy-start(f32[64]{0:T(128)} %bias_ref.1) | copy-start | bytes 772
  29.2 1.4 %collective-permute-start.14 = (f32[2,4,8,512]{3,2,1,0:T(8,128)S(1)}, f32[2,4,8,512]{3,2,1,0:T(8,128)S(1)}, u32[]{:S(2)}, u32[]{:S(2)}) collective-permute-start(f32[2,4,8,512]{3,2,1,0:T(8,128)S(1)} %stack_blocks.3), channel_id=1, source_target_pairs={{0,1},{1,0},{2,3},{3,2},{4,5},{5,4},{6,7},{7,6},{8,9},{9,8},{10,11... | collective-permute-start | bytes 393224 | tf_op jit(solution)/shard_map/ppermute | solution.py:284
  29.8 1.5 %collective-permute-start.13 = (f32[2,4,8,512]{3,2,1,0:T(8,128)S(1)}, f32[2,4,8,512]{3,2,1,0:T(8,128)S(1)}, u32[]{:S(2)}, u32[]{:S(2)}) collective-permute-start(f32[2,4,8,512]{3,2,1,0:T(8,128)S(1)} %stack_blocks.2), channel_id=1, source_target_pairs={{0,1},{1,0},{2,3},{3,2},{4,5},{5,4},{6,7},{7,6},{8,9},{9,8},{10,11... | collective-permute-start | bytes 393224 | tf_op jit(solution)/shard_map/ppermute | solution.py:284

commit v31 on v30

--- a/solution.py
+++ b/solution.py
@@ -360,16 +360,19 @@
 
 
 def mix_kernel(layers, *refs):
-    block_refs, arrived_ref = refs[:layers], refs[layers]
+    half = layers // 2
+    block_refs = refs[:layers]
+    far_arrived, near_arrived = refs[layers : layers + 2]
     weight_ref, forward_high, forward_low, inverse_high, inverse_low = refs[
-        layers + 1 : layers + 6
+        layers + 2 : layers + 7
     ]
-    modes_ref, far_ref, near_ref, order_ref, spread_ref, result_ref = refs[layers + 6 :]
+    modes_ref, far_ref, near_ref, order_ref, spread_ref, result_ref = refs[layers + 7 :]
     z, x, y = quad()
+    column = column_of(x, y)
     for index, turn in enumerate(turns(layers)):
-        column = column_of(x, y)
+        arrived_ref = near_arrived if index >= half else far_arrived
         order_ref[(z ^ turn) * 2 + column] = block_refs[index][0]
-        order_ref[(z ^ turn) * 2 + (column ^ 1)] = arrived_ref[index]
+        order_ref[(z ^ turn) * 2 + (column ^ 1)] = arrived_ref[index % half]
     feat_count = order_ref.shape[-1]
     count = weight_ref.shape[1]
     channels = weight_ref.shape[2]
@@ -432,7 +435,7 @@
         scratch_shapes=[pltpu.VMEM((2 * layers, rows, feat_count), jnp.float32), scratch, scratch],
         compiler_params=SMALL,
         name="mix",
-    )(*blocks, arrived, weights, *split_table(forward_table), *inverse_tables)
+    )(*blocks, *arrived, weights, *split_table(forward_table), *inverse_tables)
 
 
 def keep_kernel(modes_ref, inverse_high, inverse_low, far_ref, near_ref):
@@ -553,15 +556,15 @@
     far = along_columns(add_blocks(keep_far, flip_core(send_far)), peers, order[:middle])
     blocks = far + near
     inverse_tables = split_table(inverse_x_table(cells_x, peers, rows_ky))
-    modes, far, near = mix(
+    modes, send_far, send_near = mix(
         blocks,
-        flip_core(second_halves(blocks)),
+        [flip_core(second_halves(far)), flip_core(second_halves(near))],
         spectral_weight,
         forward_x_table(cells_x, peers, rows_ky) * forward_scale,
         inverse_tables,
     )
-    arrived_near, arrived_far = flip_core(near), flip_core(far)
-    keep_far, keep_near = keep_rows(modes, inverse_tables, far)
+    arrived_near, arrived_far = flip_core(send_near), flip_core(send_far)
+    keep_far, keep_near = keep_rows(modes, inverse_tables, send_far)
     own_near = along_columns(join_blocks(keep_near, arrived_near, cells_x), peers, order[middle:])
     own_far = along_columns(join_blocks(keep_far, arrived_far, cells_x), peers, order[:middle])
     flipped = [flip_core(stack_blocks(own)) for own in (own_near, own_far)]

time: 33.9 us -> 33.5 us (0.988)
    ppermute x7 -> x8, starting transfers between devices: 2.26 us -> 2.43 us  [flip_core(): return lax.ppermute(block, 'gy', [(0, 1), (1, 0)])]
    ppermute x7 -> x8, waiting for transfers between devices: 3.55 us -> 3.58 us  [flip_core(): return lax.ppermute(block, 'gy', [(0, 1), (1, 0)])]
  transfers between devices with their start and end apart: 15 -> 16, of which waited for: 11 -> 12; matrix products, arithmetic and copies ran while one was open for 0% -> 0% of each run, Pallas kernels for 1% -> 1%
where the time goes in v31:
time: 33.5 us; the launch traced here: 33.4 us
  starting transfers between devices  13.6 us (41%)
  waiting for transfers between devices  13.5 us (40%)
  Pallas kernels  5.4 us (16%)
  between operations  0.81 us (2%)
    ppermute x8, starting transfers between devices, along_columns(): arrived.append(lax.ppermute(block, ('gx', 'gy'), pairs))  11.2 us
    ppermute x8, waiting for transfers between devices, along_columns(): arrived.append(lax.ppermute(block, ('gx', 'gy'), pairs))  9.92 us
    ppermute x8, waiting for transfers between devices, flip_core(): return lax.ppermute(block, 'gy', [(0, 1), (1, 0)])  3.58 us
    ppermute x8, starting transfers between devices, flip_core(): return lax.ppermute(block, 'gy', [(0, 1), (1, 0)])  2.43 us
    pallas_call x1, Pallas kernels, make_output(): pl.pallas_call(functools.partial(output_kernel, layers), out_specs=[pl.Bl...  2.31 us
    pallas_call x1, Pallas kernels, forward_y(): pl.pallas_call(functools.partial(forward_y_kernel, extent, rows_ky), in_s...  1.75 us
    pallas_call x1, Pallas kernels, mix(): pl.pallas_call(functools.partial(mix_kernel, layers), out_shape=[jax.Shap...  1.04 us
  transfers between devices with their start and end apart: 16, of which 12 were waited for; matrix products, arithmetic and copies ran while one was open for 0% of the time, Pallas kernels for 1%

profile of v31, /device:TPU:0, one launch (start us, length us, event | category | flops | bytes accessed | tf_op | source)
XLA Modules:
  0.0 33.4 jit_solution(11576393937129794290)
XLA Ops:
  0.6 1.7 %forward_y.1 = (f32[2,2,16,512]{3,2,1,0:T(8,128)S(1)}, f32[2,2,16,512]{3,2,1,0:T(8,128)S(1)}, f32[2,2,16,512]{3,2,1,0:T(8,128)S(1)}, f32[2,2,16,512]{3,2,1,0:T(8,128)S(1)}) custom-call(bf16[4,256,512]{2,1,0:T(8,128)(2,1)} %flow_ref.1), custom_call_target="tpu_custom_call" | custom-call | tf_op jit(solution)/shard_map/forward_y/pallas_call | solution.py:270
  2.4 0.5 %collective-permute-start = (f32[2,2,16,512]{3,2,1,0:T(8,128)S(1)}, f32[2,2,16,512]{3,2,1,0:T(8,128)S(1)}, u32[]{:S(2)}, u32[]{:S(2)}) collective-permute-start(f32[2,2,16,512]{3,2,1,0:T(8,128)S(1)} %get-tuple-element.20), channel_id=1, source_target_pairs={{0,1},{1,0},{2,3},{3,2},{4,5},{5,4},{6,7},{7,6},{8,9},{9,8},{10,11... | collective-permute-start | bytes 393224 | tf_op jit(solution)/shard_map/ppermute | solution.py:284
  3.0 0.9 %collective-permute-done.arrived_ref = f32[2,2,16,512]{3,2,1,0:T(8,128)S(1)} collective-permute-done((f32[2,2,16,512]{3,2,1,0:T(8,128)S(1)}, f32[2,2,16,512]{3,2,1,0:T(8,128)S(1)}, u32[]{:S(2)}, u32[]{:S(2)}) %collective-permute-start) | collective-permute-done | bytes 131104 | tf_op jit(solution)/shard_map/ppermute | solution.py:284
  3.9 4.0 %collective-permute-start.1 = (f32[2,16,512]{2,1,0:T(8,128)S(1)}, f32[2,16,512]{2,1,0:T(8,128)S(1)}, u32[]{:S(2)}, u32[]{:S(2)}) collective-permute-start(f32[2,16,512]{2,1,0:T(8,128)S(1)} %get-tuple-element.21), channel_id=1, source_target_pairs={{0,8},{1,11},{2,10},{3,9},{4,12},{5,15},{6,14},{7,13},{8,0},{9,3},... | collective-permute-start | bytes 196616 | tf_op jit(solution)/shard_map/ppermute | solution.py:295
  7.9 1.3 %collective-permute-start.2 = (f32[2,16,512]{2,1,0:T(8,128)S(1)}, f32[2,16,512]{2,1,0:T(8,128)S(1)}, u32[]{:S(2)}, u32[]{:S(2)}) collective-permute-start(f32[2,16,512]{2,1,0:T(8,128)S(1)} %get-tuple-element.22), channel_id=1, source_target_pairs={{0,12},{1,15},{2,14},{3,13},{4,8},{5,11},{6,10},{7,9},{8,4},{9,7},... | collective-permute-start | bytes 196616 | tf_op jit(solution)/shard_map/ppermute | solution.py:295
  9.3 0.3 collective-permute-start.4
  9.6 0.7 %collective-permute-start.5 = (f32[2,16,512]{2,1,0:T(8,128)S(1)}, f32[2,16,512]{2,1,0:T(8,128)S(1)}, u32[]{:S(2)}, u32[]{:S(2)}) collective-permute-start(f32[2,16,512]{2,1,0:T(8,128)S(1)} %get-tuple-element.26), channel_id=1, source_target_pairs={{0,0},{1,3},{2,2},{3,1},{4,4},{5,7},{6,6},{7,5},{8,8},{9,11},{10,1... | collective-permute-start | bytes 196616 | tf_op jit(solution)/shard_map/ppermute | solution.py:295
  10.5 4.1 %collective-permute-done.2.refs_1_ = f32[2,16,512]{2,1,0:T(8,128)S(1)} collective-permute-done((f32[2,16,512]{2,1,0:T(8,128)S(1)}, f32[2,16,512]{2,1,0:T(8,128)S(1)}, u32[]{:S(2)}, u32[]{:S(2)}) %collective-permute-start.2) | collective-permute-done | bytes 65568 | tf_op jit(solution)/shard_map/ppermute | solution.py:295
  14.7 0.6 %collective-permute-start.6 = (f32[2,16,512]{2,1,0:T(8,128)S(1)}, f32[2,16,512]{2,1,0:T(8,128)S(1)}, u32[]{:S(2)}, u32[]{:S(2)}) collective-permute-start(f32[2,16,512]{2,1,0:T(8,128)S(1)} %second_halves.2), channel_id=1, source_target_pairs={{0,1},{1,0},{2,3},{3,2},{4,5},{5,4},{6,7},{7,6},{8,9},{9,8},{10,11... | collective-permute-start | bytes 196616 | tf_op jit(solution)/shard_map/ppermute | solution.py:284
  15.7 0.4 %collective-permute-done.6.refs_4_ = f32[2,16,512]{2,1,0:T(8,128)S(1)} collective-permute-done((f32[2,16,512]{2,1,0:T(8,128)S(1)}, f32[2,16,512]{2,1,0:T(8,128)S(1)}, u32[]{:S(2)}, u32[]{:S(2)}) %collective-permute-start.6) | collective-permute-done | bytes 65568 | tf_op jit(solution)/shard_map/ppermute | solution.py:284
  16.2 0.6 %collective-permute-done.7.refs_5_ = f32[2,16,512]{2,1,0:T(8,128)S(1)} collective-permute-done((f32[2,16,512]{2,1,0:T(8,128)S(1)}, f32[2,16,512]{2,1,0:T(8,128)S(1)}, u32[]{:S(2)}, u32[]{:S(2)}) %collective-permute-start.7) | collective-permute-done | bytes 65568 | tf_op jit(solution)/shard_map/ppermute | solution.py:284
  16.8 1.0 %mix.1 = (f32[128,512]{1,0:T(8,128)S(1)}, f32[2,16,512]{2,1,0:T(8,128)S(1)}, f32[2,16,512]{2,1,0:T(8,128)S(1)}) custom-call(f32[2,16,512]{2,1,0:T(8,128)S(1)} %collective-permute-done.1.refs_0_, f32[2,16,512]{2,1,0:T(8,128)S(1)} %collective-permute-done.2.refs_1_, f32[2,16,512]{2,1,0:T(8,128)S(1)} %collective-permute-done.4.refs_0_.refs_2_, ...), custom_call_target="tpu_custom_call" | custom-call | tf_op jit(solution)/shard_map/mix/pallas_call | solution.py:428
  18.1 0.3 collective-permute-start.8
  18.7 0.5 %collective-permute-done.11.arrived_ref = f32[2,16,512]{2,1,0:T(8,128)S(1)} collective-permute-done((f32[2,16,512]{2,1,0:T(8,128)S(1)}, f32[2,16,512]{2,1,0:T(8,128)S(1)}, u32[]{:S(2)}, u32[]{:S(2)}) %collective-permute-start.11) | collective-permute-done | bytes 65568 | tf_op jit(solution)/shard_map/ppermute | solution.py:284
  19.2 2.9 %collective-permute-start.12 = (f32[4,8,512]{2,1,0:T(8,128)S(1)}, f32[4,8,512]{2,1,0:T(8,128)S(1)}, u32[]{:S(2)}, u32[]{:S(2)}) collective-permute-start(f32[4,8,512]{2,1,0:T(8,128)S(1)} %get-tuple-element.34), channel_id=1, source_target_pairs={{0,8},{1,11},{2,10},{3,9},{4,12},{5,15},{6,14},{7,13},{8,0},{9,3},... | collective-permute-start | bytes 196616 | tf_op jit(solution)/shard_map/ppermute | solution.py:295
  22.2 1.2 %collective-permute-start.13 = (f32[4,8,512]{2,1,0:T(8,128)S(1)}, f32[4,8,512]{2,1,0:T(8,128)S(1)}, u32[]{:S(2)}, u32[]{:S(2)}) collective-permute-start(f32[4,8,512]{2,1,0:T(8,128)S(1)} %get-tuple-element.35), channel_id=1, source_target_pairs={{0,12},{1,15},{2,14},{3,13},{4,8},{5,11},{6,10},{7,9},{8,4},{9,7},... | collective-permute-start | bytes 196616 | tf_op jit(solution)/shard_map/ppermute | solution.py:295
  23.5 0.7 %collective-permute-start.10 = (f32[4,8,512]{2,1,0:T(8,128)S(1)}, f32[4,8,512]{2,1,0:T(8,128)S(1)}, u32[]{:S(2)}, u32[]{:S(2)}) collective-permute-start(f32[4,8,512]{2,1,0:T(8,128)S(1)} %get-tuple-element.31), channel_id=1, source_target_pairs={{0,0},{1,3},{2,2},{3,1},{4,4},{5,7},{6,6},{7,5},{8,8},{9,11},{10,1... | collective-permute-start | bytes 196616 | tf_op jit(solution)/shard_map/ppermute | solution.py:295
  24.1 2.2 %collective-permute-done.12.refs_0_.refs_2_ = f32[4,8,512]{2,1,0:T(8,128)S(1)} collective-permute-done((f32[4,8,512]{2,1,0:T(8,128)S(1)}, f32[4,8,512]{2,1,0:T(8,128)S(1)}, u32[]{:S(2)}, u32[]{:S(2)}) %collective-permute-start.12) | collective-permute-done | bytes 65568 | tf_op jit(solution)/shard_map/ppermute | solution.py:295
  26.3 2.7 %collective-permute-done.13.refs_1_.refs_3_ = f32[4,8,512]{2,1,0:T(8,128)S(1)} collective-permute-done((f32[4,8,512]{2,1,0:T(8,128)S(1)}, f32[4,8,512]{2,1,0:T(8,128)S(1)}, u32[]{:S(2)}, u32[]{:S(2)}) %collective-permute-start.13) | collective-permute-done | bytes 65568 | tf_op jit(solution)/shard_map/ppermute | solution.py:295
  29.1 0.5 %collective-permute-done.9.refs_0_ = f32[4,8,512]{2,1,0:T(8,128)S(1)} collective-permute-done((f32[4,8,512]{2,1,0:T(8,128)S(1)}, f32[4,8,512]{2,1,0:T(8,128)S(1)}, u32[]{:S(2)}, u32[]{:S(2)}) %collective-permute-start.9) | collective-permute-done | bytes 65568 | tf_op jit(solution)/shard_map/ppermute | solution.py:295
  29.6 0.3 %collective-permute-start.14 = (f32[2,4,8,512]{3,2,1,0:T(8,128)S(1)}, f32[2,4,8,512]{3,2,1,0:T(8,128)S(1)}, u32[]{:S(2)}, u32[]{:S(2)}) collective-permute-start(f32[2,4,8,512]{3,2,1,0:T(8,128)S(1)} %stack_blocks.2), channel_id=1, source_target_pairs={{0,1},{1,0},{2,3},{3,2},{4,5},{5,4},{6,7},{7,6},{8,9},{9,8},{10,11... | collective-permute-start | bytes 393224 | tf_op jit(solution)/shard_map/ppermute | solution.py:284
  30.0 0.5 %collective-permute-done.15.refs_5_ = f32[2,4,8,512]{3,2,1,0:T(8,128)S(1)} collective-permute-done((f32[2,4,8,512]{3,2,1,0:T(8,128)S(1)}, f32[2,4,8,512]{3,2,1,0:T(8,128)S(1)}, u32[]{:S(2)}, u32[]{:S(2)}) %collective-permute-start.15) | collective-permute-done | bytes 131104 | tf_op jit(solution)/shard_map/ppermute | solution.py:284
  30.5 0.6 %collective-permute-done.14.refs_4_ = f32[2,4,8,512]{3,2,1,0:T(8,128)S(1)} collective-permute-done((f32[2,4,8,512]{3,2,1,0:T(8,128)S(1)}, f32[2,4,8,512]{3,2,1,0:T(8,128)S(1)}, u32[]{:S(2)}, u32[]{:S(2)}) %collective-permute-start.14) | collective-permute-done | bytes 131104 | tf_op jit(solution)/shard_map/ppermute | solution.py:284
  31.1 2.3 %make_output.1 = (bf16[4,256,512]{2,1,0:T(8,128)(2,1)}, f32[1,64,1024]{2,1,0:T(8,128)}) custom-call(bf16[4,256,512]{2,1,0:T(8,128)(2,1)S(1)} %copy-done, bf16[2,2,256,256]{3,2,1,0:T(8,128)(2,1)S(1)} %copy-done.2, bf16[64,64]{1,0:T(8,128)(2,1)S(1)} %copy-done.7, f32[64]{0:T(128)S(1)} %copy-done.8, f32[128,512]{1,0:T(8,128)S(1)} %get-tuple-element.27.modes_ref, ...), custom_call_target="tpu_custom_call" | custom-call | tf_op jit(solution)/shard_map/make_output/pallas_call | solution.py:523
  (38 shorter events, 1.6 us)
Async XLA Ops:
  0.6 16.2 %copy-start.1 = (bf16[1,64,64,128]{3,2,1,0:T(8,128)(2,1)S(1)}, bf16[1,64,64,128]{3,2,1,0:T(8,128)(2,1)}, u32[]{:S(2)}) copy-start(bf16[1,64,64,128]{3,2,1,0:T(8,128)(2,1)} %refs_6_.1) | copy-start | bytes 3145732
  2.4 1.5 %collective-permute-start = (f32[2,2,16,512]{3,2,1,0:T(8,128)S(1)}, f32[2,2,16,512]{3,2,1,0:T(8,128)S(1)}, u32[]{:S(2)}, u32[]{:S(2)}) collective-permute-start(f32[2,2,16,512]{3,2,1,0:T(8,128)S(1)} %get-tuple-element.20), channel_id=1, source_target_pairs={{0,1},{1,0},{2,3},{3,2},{4,5},{5,4},{6,7},{7,6},{8,9},{9,8},{10,11... | collective-permute-start | bytes 393224 | tf_op jit(solution)/shard_map/ppermute | solution.py:284
  2.9 6.4 %collective-permute-start.3 = (f32[2,2,16,512]{3,2,1,0:T(8,128)S(1)}, f32[2,2,16,512]{3,2,1,0:T(8,128)S(1)}, u32[]{:S(2)}, u32[]{:S(2)}) collective-permute-start(f32[2,2,16,512]{3,2,1,0:T(8,128)S(1)} %get-tuple-element.24), channel_id=1, source_target_pairs={{0,1},{1,0},{2,3},{3,2},{4,5},{5,4},{6,7},{7,6},{8,9},{9,8},{10,11... | collective-permute-start | bytes 393224 | tf_op jit(solution)/shard_map/ppermute | solution.py:284
  3.9 6.6 %collective-permute-start.1 = (f32[2,16,512]{2,1,0:T(8,128)S(1)}, f32[2,16,512]{2,1,0:T(8,128)S(1)}, u32[]{:S(2)}, u32[]{:S(2)}) collective-permute-start(f32[2,16,512]{2,1,0:T(8,128)S(1)} %get-tuple-element.21), channel_id=1, source_target_pairs={{0,8},{1,11},{2,10},{3,9},{4,12},{5,15},{6,14},{7,13},{8,0},{9,3},... | collective-permute-start | bytes 196616 | tf_op jit(solution)/shard_map/ppermute | solution.py:295
  7.9 6.7 %collective-permute-start.2 = (f32[2,16,512]{2,1,0:T(8,128)S(1)}, f32[2,16,512]{2,1,0:T(8,128)S(1)}, u32[]{:S(2)}, u32[]{:S(2)}) collective-permute-start(f32[2,16,512]{2,1,0:T(8,128)S(1)} %get-tuple-element.22), channel_id=1, source_target_pairs={{0,12},{1,15},{2,14},{3,13},{4,8},{5,11},{6,10},{7,9},{8,4},{9,7},... | collective-permute-start | bytes 196616 | tf_op jit(solution)/shard_map/ppermute | solution.py:295
  9.3 6.2 %collective-permute-start.4 = (f32[2,16,512]{2,1,0:T(8,128)S(1)}, f32[2,16,512]{2,1,0:T(8,128)S(1)}, u32[]{:S(2)}, u32[]{:S(2)}) collective-permute-start(f32[2,16,512]{2,1,0:T(8,128)S(1)} %get-tuple-element.25), channel_id=1, source_target_pairs={{0,4},{1,7},{2,6},{3,5},{4,0},{5,3},{6,2},{7,1},{8,12},{9,15},{10,... | collective-permute-start | bytes 196616 | tf_op jit(solution)/shard_map/ppermute | solution.py:295
  9.6 5.9 %collective-permute-start.5 = (f32[2,16,512]{2,1,0:T(8,128)S(1)}, f32[2,16,512]{2,1,0:T(8,128)S(1)}, u32[]{:S(2)}, u32[]{:S(2)}) collective-permute-start(f32[2,16,512]{2,1,0:T(8,128)S(1)} %get-tuple-element.26), channel_id=1, source_target_pairs={{0,0},{1,3},{2,2},{3,1},{4,4},{5,7},{6,6},{7,5},{8,8},{9,11},{10,1... | collective-permute-start | bytes 196616 | tf_op jit(solution)/shard_map/ppermute | solution.py:295
  14.6 2.2 %copy-start.3 = (bf16[2,4,16,128]{3,2,1,0:T(8,128)(2,1)S(1)}, bf16[2,4,16,128]{3,2,1,0:T(8,128)(2,1)}, u32[]{:S(2)}) copy-start(bf16[2,4,16,128]{3,2,1,0:T(8,128)(2,1)} %constant.13.clone.refs_10_.inverse_low) | copy-start | bytes 98308
  14.6 2.2 %copy-start.4 = (bf16[2,4,16,128]{3,2,1,0:T(8,128)(2,1)S(1)}, bf16[2,4,16,128]{3,2,1,0:T(8,128)(2,1)}, u32[]{:S(2)}) copy-start(bf16[2,4,16,128]{3,2,1,0:T(8,128)(2,1)} %constant.12.clone.refs_9_.inverse_high) | copy-start | bytes 98308
  14.6 2.2 %copy-start.5 = (bf16[128,128]{1,0:T(8,128)(2,1)S(1)}, bf16[128,128]{1,0:T(8,128)(2,1)}, u32[]{:S(2)}) copy-start(bf16[128,128]{1,0:T(8,128)(2,1)} %constant.11.clone.refs_8_) | copy-start | bytes 98308
  14.7 2.2 %copy-start.6 = (bf16[128,128]{1,0:T(8,128)(2,1)S(1)}, bf16[128,128]{1,0:T(8,128)(2,1)}, u32[]{:S(2)}) copy-start(bf16[128,128]{1,0:T(8,128)(2,1)} %constant.10.clone.refs_7_) | copy-start | bytes 98308
  14.7 1.5 %collective-permute-start.6 = (f32[2,16,512]{2,1,0:T(8,128)S(1)}, f32[2,16,512]{2,1,0:T(8,128)S(1)}, u32[]{:S(2)}, u32[]{:S(2)}) collective-permute-start(f32[2,16,512]{2,1,0:T(8,128)S(1)} %second_halves.2), channel_id=1, source_target_pairs={{0,1},{1,0},{2,3},{3,2},{4,5},{5,4},{6,7},{7,6},{8,9},{9,8},{10,11... | collective-permute-start | bytes 196616 | tf_op jit(solution)/shard_map/ppermute | solution.py:284
  15.5 15.6 %copy-start = (bf16[4,256,512]{2,1,0:T(8,128)(2,1)S(1)}, bf16[4,256,512]{2,1,0:T(8,128)(2,1)}, u32[]{:S(2)}) copy-start(bf16[4,256,512]{2,1,0:T(8,128)(2,1)} %flow_ref.1) | copy-start | bytes 3145732
  15.5 1.3 %collective-permute-start.7 = (f32[2,16,512]{2,1,0:T(8,128)S(1)}, f32[2,16,512]{2,1,0:T(8,128)S(1)}, u32[]{:S(2)}, u32[]{:S(2)}) collective-permute-start(f32[2,16,512]{2,1,0:T(8,128)S(1)} %second_halves.3), channel_id=1, source_target_pairs={{0,1},{1,0},{2,3},{3,2},{4,5},{5,4},{6,7},{7,6},{8,9},{9,8},{10,11... | collective-permute-start | bytes 196616 | tf_op jit(solution)/shard_map/ppermute | solution.py:284
  17.9 1.3 %collective-permute-start.11 = (f32[2,16,512]{2,1,0:T(8,128)S(1)}, f32[2,16,512]{2,1,0:T(8,128)S(1)}, u32[]{:S(2)}, u32[]{:S(2)}) collective-permute-start(f32[2,16,512]{2,1,0:T(8,128)S(1)} %get-tuple-element.33), channel_id=1, source_target_pairs={{0,1},{1,0},{2,3},{3,2},{4,5},{5,4},{6,7},{7,6},{8,9},{9,8},{10,11... | collective-permute-start | bytes 196616 | tf_op jit(solution)/shard_map/ppermute | solution.py:284
  18.1 5.2 %collective-permute-start.8 = (f32[2,16,512]{2,1,0:T(8,128)S(1)}, f32[2,16,512]{2,1,0:T(8,128)S(1)}, u32[]{:S(2)}, u32[]{:S(2)}) collective-permute-start(f32[2,16,512]{2,1,0:T(8,128)S(1)} %get-tuple-element.29), channel_id=1, source_target_pairs={{0,1},{1,0},{2,3},{3,2},{4,5},{5,4},{6,7},{7,6},{8,9},{9,8},{10,11... | collective-permute-start | bytes 196616 | tf_op jit(solution)/shard_map/ppermute | solution.py:284
  18.5 12.6 %copy-start.2 = (bf16[2,2,256,256]{3,2,1,0:T(8,128)(2,1)S(1)}, bf16[2,2,256,256]{3,2,1,0:T(8,128)(2,1)}, u32[]{:S(2)}) copy-start(bf16[2,2,256,256]{3,2,1,0:T(8,128)(2,1)} %constant.14.clone.table_ref) | copy-start | bytes 1572868
  19.2 7.1 %collective-permute-start.12 = (f32[4,8,512]{2,1,0:T(8,128)S(1)}, f32[4,8,512]{2,1,0:T(8,128)S(1)}, u32[]{:S(2)}, u32[]{:S(2)}) collective-permute-start(f32[4,8,512]{2,1,0:T(8,128)S(1)} %get-tuple-element.34), channel_id=1, source_target_pairs={{0,8},{1,11},{2,10},{3,9},{4,12},{5,15},{6,14},{7,13},{8,0},{9,3},... | collective-permute-start | bytes 196616 | tf_op jit(solution)/shard_map/ppermute | solution.py:295
  22.2 6.9 %collective-permute-start.13 = (f32[4,8,512]{2,1,0:T(8,128)S(1)}, f32[4,8,512]{2,1,0:T(8,128)S(1)}, u32[]{:S(2)}, u32[]{:S(2)}) collective-permute-start(f32[4,8,512]{2,1,0:T(8,128)S(1)} %get-tuple-element.35), channel_id=1, source_target_pairs={{0,12},{1,15},{2,14},{3,13},{4,8},{5,11},{6,10},{7,9},{8,4},{9,7},... | collective-permute-start | bytes 196616 | tf_op jit(solution)/shard_map/ppermute | solution.py:295
  23.4 6.2 %collective-permute-start.9 = (f32[4,8,512]{2,1,0:T(8,128)S(1)}, f32[4,8,512]{2,1,0:T(8,128)S(1)}, u32[]{:S(2)}, u32[]{:S(2)}) collective-permute-start(f32[4,8,512]{2,1,0:T(8,128)S(1)} %get-tuple-element.30), channel_id=1, source_target_pairs={{0,4},{1,7},{2,6},{3,5},{4,0},{5,3},{6,2},{7,1},{8,12},{9,15},{10,... | collective-permute-start | bytes 196616 | tf_op jit(solution)/shard_map/ppermute | solution.py:295
  23.5 6.1 %collective-permute-start.10 = (f32[4,8,512]{2,1,0:T(8,128)S(1)}, f32[4,8,512]{2,1,0:T(8,128)S(1)}, u32[]{:S(2)}, u32[]{:S(2)}) collective-permute-start(f32[4,8,512]{2,1,0:T(8,128)S(1)} %get-tuple-element.31), channel_id=1, source_target_pairs={{0,0},{1,3},{2,2},{3,1},{4,4},{5,7},{6,6},{7,5},{8,8},{9,11},{10,1... | collective-permute-start | bytes 196616 | tf_op jit(solution)/shard_map/ppermute | solution.py:295
  29.0 2.0 %copy-start.7 = (bf16[64,64]{1,0:T(8,128)(2,1)S(1)}, bf16[64,64]{1,0:T(8,128)(2,1)}, u32[]{:S(2)}) copy-start(bf16[64,64]{1,0:T(8,128)(2,1)} %local_ref.1) | copy-start | bytes 24580
  29.1 1.4 %collective-permute-start.15 = (f32[2,4,8,512]{3,2,1,0:T(8,128)S(1)}, f32[2,4,8,512]{3,2,1,0:T(8,128)S(1)}, u32[]{:S(2)}, u32[]{:S(2)}) collective-permute-start(f32[2,4,8,512]{3,2,1,0:T(8,128)S(1)} %stack_blocks.3), channel_id=1, source_target_pairs={{0,1},{1,0},{2,3},{3,2},{4,5},{5,4},{6,7},{7,6},{8,9},{9,8},{10,11... | collective-permute-start | bytes 393224 | tf_op jit(solution)/shard_map/ppermute | solution.py:284
  29.6 1.4 %collective-permute-start.14 = (f32[2,4,8,512]{3,2,1,0:T(8,128)S(1)}, f32[2,4,8,512]{3,2,1,0:T(8,128)S(1)}, u32[]{:S(2)}, u32[]{:S(2)}) collective-permute-start(f32[2,4,8,512]{3,2,1,0:T(8,128)S(1)} %stack_blocks.2), channel_id=1, source_target_pairs={{0,1},{1,0},{2,3},{3,2},{4,5},{5,4},{6,7},{7,6},{8,9},{9,8},{10,11... | collective-permute-start | bytes 393224 | tf_op jit(solution)/shard_map/ppermute | solution.py:284
  (1 other events, 2.0 us)

commit v32 on v31

--- a/solution.py
+++ b/solution.py
@@ -165,9 +165,11 @@
     return place // 2, place % 2, lax.axis_index("gy")
 
 
-def turns(layers):
+def turns(layers, inverse=False):
     half = layers // 2
-    return list(range(half, layers)) + list(range(half - 1, -1, -1))
+    if inverse:
+        return list(range(half, layers)) + list(range(half - 1, -1, -1))
+    return list(range(layers - 1, -1, -1))
 
 
 def forward_x_table(cells_x, peers, rows_ky):
@@ -234,7 +236,7 @@
     row = lax.broadcasted_iota(jnp.int32, (shape[0], 1), 0)
     block = row // (2 * rows_ky)
     place = block // 2 % layers
-    turn = jnp.where(place < layers // 2, place + layers // 2, layers - 1 - place)
+    turn = layers - 1 - place
     side = y ^ (1 - block // peers)
     owner = (side ^ (block % 2)) * peers + (z ^ turn) * 2 + column_of(x, side)
     index = owner * rows_ky + row // 2 % rows_ky
@@ -349,7 +351,7 @@
 
 def back_rows(inverse_high, inverse_low, modes, shape, other):
     z, x, y = quad()
-    places = [(column_of(x, y) ^ other, z ^ turn) for turn in turns(shape[0])]
+    places = [(column_of(x, y) ^ other, z ^ turn) for turn in turns(shape[0], True)]
     table_high, table_low = [
         jnp.concatenate([ref[column, place] for column, place in places], axis=0)
         for ref in (inverse_high, inverse_low)
@@ -486,7 +488,7 @@
     below = jnp.concatenate(levels + [filled], axis=0).astype(jnp.bfloat16)
     below = jnp.concatenate([below, wide_ref[...]], axis=0)
     for column, block_refs in ((x ^ y, own_refs), (x ^ y ^ 1, core_refs)):
-        for turn, block_ref in zip(turns(layers), block_refs):
+        for turn, block_ref in zip(turns(layers, True), block_refs):
             order_ref[:, (z ^ turn) * 2 + column] = block_ref[...]
     table = table_ref[y, x ^ y]
     count = modes_ref.shape[0] // 2
@@ -565,6 +567,7 @@
     )
     arrived_near, arrived_far = flip_core(send_near), flip_core(send_far)
     keep_far, keep_near = keep_rows(modes, inverse_tables, send_far)
+    order = turns(peers // 2, True)
     own_near = along_columns(join_blocks(keep_near, arrived_near, cells_x), peers, order[middle:])
     own_far = along_columns(join_blocks(keep_far, arrived_far, cells_x), peers, order[:middle])
     flipped = [flip_core(stack_blocks(own)) for own in (own_near, own_far)]

time: 33.5 us -> 33.5 us (level)
  transfers between devices with their start and end apart: 16 -> 16, of which waited for: 12 -> 9; matrix products, arithmetic and copies ran while one was open for 0% -> 0% of each run, Pallas kernels for 1% -> 1%
where the time goes in v32:
time: 33.5 us; the launch traced here: 33.3 us
  starting transfers between devices  13.5 us (40%)
  waiting for transfers between devices  13.5 us (40%)
  Pallas kernels  5.4 us (16%)
  between operations  0.8 us (2%)
    ppermute x8, starting transfers between devices, along_columns(): arrived.append(lax.ppermute(block, ('gx', 'gy'), pairs))  11 us
    ppermute x8, waiting for transfers between devices, along_columns(): arrived.append(lax.ppermute(block, ('gx', 'gy'), pairs))  10.1 us
    ppermute x8, waiting for transfers between devices, flip_core(): return lax.ppermute(block, 'gy', [(0, 1), (1, 0)])  3.4 us
    ppermute x8, starting transfers between devices, flip_core(): return lax.ppermute(block, 'gy', [(0, 1), (1, 0)])  2.56 us
    pallas_call x1, Pallas kernels, make_output(): pl.pallas_call(functools.partial(output_kernel, layers), out_specs=[pl.Bl...  2.3 us
    pallas_call x1, Pallas kernels, forward_y(): pl.pallas_call(functools.partial(forward_y_kernel, extent, rows_ky), in_s...  1.75 us
    pallas_call x1, Pallas kernels, mix(): pl.pallas_call(functools.partial(mix_kernel, layers), out_shape=[jax.Shap...  1.04 us
  transfers between devices with their start and end apart: 16, of which 9 were waited for; matrix products, arithmetic and copies ran while one was open for 0% of the time, Pallas kernels for 1%

profile of v32, /device:TPU:0, one launch (start us, length us, event | category | flops | bytes accessed | tf_op | source)
XLA Modules:
  0.0 33.3 jit_solution(4253838337883516384)
XLA Ops:
  0.6 1.7 %forward_y.1 = (f32[2,2,16,512]{3,2,1,0:T(8,128)S(1)}, f32[2,2,16,512]{3,2,1,0:T(8,128)S(1)}, f32[2,2,16,512]{3,2,1,0:T(8,128)S(1)}, f32[2,2,16,512]{3,2,1,0:T(8,128)S(1)}) custom-call(bf16[4,256,512]{2,1,0:T(8,128)(2,1)} %flow_ref.1), custom_call_target="tpu_custom_call" | custom-call | tf_op jit(solution)/shard_map/forward_y/pallas_call | solution.py:272
  2.4 0.5 %collective-permute-start = (f32[2,2,16,512]{3,2,1,0:T(8,128)S(1)}, f32[2,2,16,512]{3,2,1,0:T(8,128)S(1)}, u32[]{:S(2)}, u32[]{:S(2)}) collective-permute-start(f32[2,2,16,512]{3,2,1,0:T(8,128)S(1)} %get-tuple-element.20), channel_id=1, source_target_pairs={{0,1},{1,0},{2,3},{3,2},{4,5},{5,4},{6,7},{7,6},{8,9},{9,8},{10,11... | collective-permute-start | bytes 393224 | tf_op jit(solution)/shard_map/ppermute | solution.py:286
  3.0 0.9 %collective-permute-done.arrived_ref = f32[2,2,16,512]{3,2,1,0:T(8,128)S(1)} collective-permute-done((f32[2,2,16,512]{3,2,1,0:T(8,128)S(1)}, f32[2,2,16,512]{3,2,1,0:T(8,128)S(1)}, u32[]{:S(2)}, u32[]{:S(2)}) %collective-permute-start) | collective-permute-done | bytes 131104 | tf_op jit(solution)/shard_map/ppermute | solution.py:286
  3.9 5.0 %collective-permute-start.1 = (f32[2,16,512]{2,1,0:T(8,128)S(1)}, f32[2,16,512]{2,1,0:T(8,128)S(1)}, u32[]{:S(2)}, u32[]{:S(2)}) collective-permute-start(f32[2,16,512]{2,1,0:T(8,128)S(1)} %get-tuple-element.21), channel_id=1, source_target_pairs={{0,12},{1,15},{2,14},{3,13},{4,8},{5,11},{6,10},{7,9},{8,4},{9,7},... | collective-permute-start | bytes 196616 | tf_op jit(solution)/shard_map/ppermute | solution.py:297
  9.0 0.7 %collective-permute-start.4 = (f32[2,16,512]{2,1,0:T(8,128)S(1)}, f32[2,16,512]{2,1,0:T(8,128)S(1)}, u32[]{:S(2)}, u32[]{:S(2)}) collective-permute-start(f32[2,16,512]{2,1,0:T(8,128)S(1)} %get-tuple-element.25), channel_id=1, source_target_pairs={{0,4},{1,7},{2,6},{3,5},{4,0},{5,3},{6,2},{7,1},{8,12},{9,15},{10,... | collective-permute-start | bytes 196616 | tf_op jit(solution)/shard_map/ppermute | solution.py:297
  9.7 0.7 %collective-permute-start.5 = (f32[2,16,512]{2,1,0:T(8,128)S(1)}, f32[2,16,512]{2,1,0:T(8,128)S(1)}, u32[]{:S(2)}, u32[]{:S(2)}) collective-permute-start(f32[2,16,512]{2,1,0:T(8,128)S(1)} %get-tuple-element.26), channel_id=1, source_target_pairs={{0,0},{1,3},{2,2},{3,1},{4,4},{5,7},{6,6},{7,5},{8,8},{9,11},{10,1... | collective-permute-start | bytes 196616 | tf_op jit(solution)/shard_map/ppermute | solution.py:297
  10.3 1.3 %collective-permute-done.1.refs_0_ = f32[2,16,512]{2,1,0:T(8,128)S(1)} collective-permute-done((f32[2,16,512]{2,1,0:T(8,128)S(1)}, f32[2,16,512]{2,1,0:T(8,128)S(1)}, u32[]{:S(2)}, u32[]{:S(2)}) %collective-permute-start.1) | collective-permute-done | bytes 65568 | tf_op jit(solution)/shard_map/ppermute | solution.py:297
  11.7 3.8 %collective-permute-done.2.refs_1_ = f32[2,16,512]{2,1,0:T(8,128)S(1)} collective-permute-done((f32[2,16,512]{2,1,0:T(8,128)S(1)}, f32[2,16,512]{2,1,0:T(8,128)S(1)}, u32[]{:S(2)}, u32[]{:S(2)}) %collective-permute-start.2) | collective-permute-done | bytes 65568 | tf_op jit(solution)/shard_map/ppermute | solution.py:297
  15.5 0.5 %collective-permute-start.6 = (f32[2,16,512]{2,1,0:T(8,128)S(1)}, f32[2,16,512]{2,1,0:T(8,128)S(1)}, u32[]{:S(2)}, u32[]{:S(2)}) collective-permute-start(f32[2,16,512]{2,1,0:T(8,128)S(1)} %second_halves.2), channel_id=1, source_target_pairs={{0,1},{1,0},{2,3},{3,2},{4,5},{5,4},{6,7},{7,6},{8,9},{9,8},{10,11... | collective-permute-start | bytes 196616 | tf_op jit(solution)/shard_map/ppermute | solution.py:286
  16.0 0.3 %collective-permute-start.7 = (f32[2,16,512]{2,1,0:T(8,128)S(1)}, f32[2,16,512]{2,1,0:T(8,128)S(1)}, u32[]{:S(2)}, u32[]{:S(2)}) collective-permute-start(f32[2,16,512]{2,1,0:T(8,128)S(1)} %second_halves.3), channel_id=1, source_target_pairs={{0,1},{1,0},{2,3},{3,2},{4,5},{5,4},{6,7},{7,6},{8,9},{9,8},{10,11... | collective-permute-start | bytes 196616 | tf_op jit(solution)/shard_map/ppermute | solution.py:286
  16.3 0.5 %collective-permute-done.6.refs_4_ = f32[2,16,512]{2,1,0:T(8,128)S(1)} collective-permute-done((f32[2,16,512]{2,1,0:T(8,128)S(1)}, f32[2,16,512]{2,1,0:T(8,128)S(1)}, u32[]{:S(2)}, u32[]{:S(2)}) %collective-permute-start.6) | collective-permute-done | bytes 65568 | tf_op jit(solution)/shard_map/ppermute | solution.py:286
  16.8 0.4 %collective-permute-done.7.refs_5_ = f32[2,16,512]{2,1,0:T(8,128)S(1)} collective-permute-done((f32[2,16,512]{2,1,0:T(8,128)S(1)}, f32[2,16,512]{2,1,0:T(8,128)S(1)}, u32[]{:S(2)}, u32[]{:S(2)}) %collective-permute-start.7) | collective-permute-done | bytes 65568 | tf_op jit(solution)/shard_map/ppermute | solution.py:286
  17.3 1.0 %mix.1 = (f32[128,512]{1,0:T(8,128)S(1)}, f32[2,16,512]{2,1,0:T(8,128)S(1)}, f32[2,16,512]{2,1,0:T(8,128)S(1)}) custom-call(f32[2,16,512]{2,1,0:T(8,128)S(1)} %collective-permute-done.1.refs_0_, f32[2,16,512]{2,1,0:T(8,128)S(1)} %collective-permute-done.2.refs_1_, f32[2,16,512]{2,1,0:T(8,128)S(1)} %collective-permute-done.4.refs_0_.refs_2_, ...), custom_call_target="tpu_custom_call" | custom-call | tf_op jit(solution)/shard_map/mix/pallas_call | solution.py:430
  18.4 0.3 %collective-permute-start.11 = (f32[2,16,512]{2,1,0:T(8,128)S(1)}, f32[2,16,512]{2,1,0:T(8,128)S(1)}, u32[]{:S(2)}, u32[]{:S(2)}) collective-permute-start(f32[2,16,512]{2,1,0:T(8,128)S(1)} %get-tuple-element.33), channel_id=1, source_target_pairs={{0,1},{1,0},{2,3},{3,2},{4,5},{5,4},{6,7},{7,6},{8,9},{9,8},{10,11... | collective-permute-start | bytes 196616 | tf_op jit(solution)/shard_map/ppermute | solution.py:286
  19.2 0.5 %collective-permute-done.11.arrived_ref = f32[2,16,512]{2,1,0:T(8,128)S(1)} collective-permute-done((f32[2,16,512]{2,1,0:T(8,128)S(1)}, f32[2,16,512]{2,1,0:T(8,128)S(1)}, u32[]{:S(2)}, u32[]{:S(2)}) %collective-permute-start.11) | collective-permute-done | bytes 65568 | tf_op jit(solution)/shard_map/ppermute | solution.py:286
  19.7 1.4 %collective-permute-start.12 = (f32[4,8,512]{2,1,0:T(8,128)S(1)}, f32[4,8,512]{2,1,0:T(8,128)S(1)}, u32[]{:S(2)}, u32[]{:S(2)}) collective-permute-start(f32[4,8,512]{2,1,0:T(8,128)S(1)} %get-tuple-element.34), channel_id=1, source_target_pairs={{0,8},{1,11},{2,10},{3,9},{4,12},{5,15},{6,14},{7,13},{8,0},{9,3},... | collective-permute-start | bytes 196616 | tf_op jit(solution)/shard_map/ppermute | solution.py:297
  21.1 2.0 %collective-permute-start.13 = (f32[4,8,512]{2,1,0:T(8,128)S(1)}, f32[4,8,512]{2,1,0:T(8,128)S(1)}, u32[]{:S(2)}, u32[]{:S(2)}) collective-permute-start(f32[4,8,512]{2,1,0:T(8,128)S(1)} %get-tuple-element.35), channel_id=1, source_target_pairs={{0,12},{1,15},{2,14},{3,13},{4,8},{5,11},{6,10},{7,9},{8,4},{9,7},... | collective-permute-start | bytes 196616 | tf_op jit(solution)/shard_map/ppermute | solution.py:297
  23.1 0.6 %collective-permute-start.9 = (f32[4,8,512]{2,1,0:T(8,128)S(1)}, f32[4,8,512]{2,1,0:T(8,128)S(1)}, u32[]{:S(2)}, u32[]{:S(2)}) collective-permute-start(f32[4,8,512]{2,1,0:T(8,128)S(1)} %get-tuple-element.30), channel_id=1, source_target_pairs={{0,4},{1,7},{2,6},{3,5},{4,0},{5,3},{6,2},{7,1},{8,12},{9,15},{10,... | collective-permute-start | bytes 196616 | tf_op jit(solution)/shard_map/ppermute | solution.py:297
  23.7 0.7 %collective-permute-start.10 = (f32[4,8,512]{2,1,0:T(8,128)S(1)}, f32[4,8,512]{2,1,0:T(8,128)S(1)}, u32[]{:S(2)}, u32[]{:S(2)}) collective-permute-start(f32[4,8,512]{2,1,0:T(8,128)S(1)} %get-tuple-element.31), channel_id=1, source_target_pairs={{0,0},{1,3},{2,2},{3,1},{4,4},{5,7},{6,6},{7,5},{8,8},{9,11},{10,1... | collective-permute-start | bytes 196616 | tf_op jit(solution)/shard_map/ppermute | solution.py:297
  24.3 4.1 %collective-permute-done.12.refs_0_.refs_2_ = f32[4,8,512]{2,1,0:T(8,128)S(1)} collective-permute-done((f32[4,8,512]{2,1,0:T(8,128)S(1)}, f32[4,8,512]{2,1,0:T(8,128)S(1)}, u32[]{:S(2)}, u32[]{:S(2)}) %collective-permute-start.12) | collective-permute-done | bytes 65568 | tf_op jit(solution)/shard_map/ppermute | solution.py:297
  28.7 0.9 %collective-permute-done.9.refs_0_ = f32[4,8,512]{2,1,0:T(8,128)S(1)} collective-permute-done((f32[4,8,512]{2,1,0:T(8,128)S(1)}, f32[4,8,512]{2,1,0:T(8,128)S(1)}, u32[]{:S(2)}, u32[]{:S(2)}) %collective-permute-start.9) | collective-permute-done | bytes 65568 | tf_op jit(solution)/shard_map/ppermute | solution.py:297
  29.6 0.4 %collective-permute-start.14 = (f32[2,4,8,512]{3,2,1,0:T(8,128)S(1)}, f32[2,4,8,512]{3,2,1,0:T(8,128)S(1)}, u32[]{:S(2)}, u32[]{:S(2)}) collective-permute-start(f32[2,4,8,512]{3,2,1,0:T(8,128)S(1)} %stack_blocks.2), channel_id=1, source_target_pairs={{0,1},{1,0},{2,3},{3,2},{4,5},{5,4},{6,7},{7,6},{8,9},{9,8},{10,11... | collective-permute-start | bytes 393224 | tf_op jit(solution)/shard_map/ppermute | solution.py:286
  30.0 1.0 %collective-permute-done.14.refs_4_ = f32[2,4,8,512]{3,2,1,0:T(8,128)S(1)} collective-permute-done((f32[2,4,8,512]{3,2,1,0:T(8,128)S(1)}, f32[2,4,8,512]{3,2,1,0:T(8,128)S(1)}, u32[]{:S(2)}, u32[]{:S(2)}) %collective-permute-start.14) | collective-permute-done | bytes 131104 | tf_op jit(solution)/shard_map/ppermute | solution.py:286
  31.0 2.3 %make_output.1 = (bf16[4,256,512]{2,1,0:T(8,128)(2,1)}, f32[1,64,1024]{2,1,0:T(8,128)}) custom-call(bf16[4,256,512]{2,1,0:T(8,128)(2,1)S(1)} %copy-done, bf16[2,2,256,256]{3,2,1,0:T(8,128)(2,1)S(1)} %copy-done.2, bf16[64,64]{1,0:T(8,128)(2,1)S(1)} %copy-done.7, f32[64]{0:T(128)S(1)} %copy-done.8, f32[128,512]{1,0:T(8,128)S(1)} %get-tuple-element.27.modes_ref, ...), custom_call_target="tpu_custom_call" | custom-call | tf_op jit(solution)/shard_map/make_output/pallas_call | solution.py:525
  (38 shorter events, 0.8 us)
Async XLA Ops:
  0.6 16.7 %copy-start.1 = (bf16[1,64,64,128]{3,2,1,0:T(8,128)(2,1)S(1)}, bf16[1,64,64,128]{3,2,1,0:T(8,128)(2,1)}, u32[]{:S(2)}) copy-start(bf16[1,64,64,128]{3,2,1,0:T(8,128)(2,1)} %refs_6_.1) | copy-start | bytes 3145732
  2.4 1.5 %collective-permute-start = (f32[2,2,16,512]{3,2,1,0:T(8,128)S(1)}, f32[2,2,16,512]{3,2,1,0:T(8,128)S(1)}, u32[]{:S(2)}, u32[]{:S(2)}) collective-permute-start(f32[2,2,16,512]{3,2,1,0:T(8,128)S(1)} %get-tuple-element.20), channel_id=1, source_target_pairs={{0,1},{1,0},{2,3},{3,2},{4,5},{5,4},{6,7},{7,6},{8,9},{9,8},{10,11... | collective-permute-start | bytes 393224 | tf_op jit(solution)/shard_map/ppermute | solution.py:286
  2.9 6.0 %collective-permute-start.3 = (f32[2,2,16,512]{3,2,1,0:T(8,128)S(1)}, f32[2,2,16,512]{3,2,1,0:T(8,128)S(1)}, u32[]{:S(2)}, u32[]{:S(2)}) collective-permute-start(f32[2,2,16,512]{3,2,1,0:T(8,128)S(1)} %get-tuple-element.24), channel_id=1, source_target_pairs={{0,1},{1,0},{2,3},{3,2},{4,5},{5,4},{6,7},{7,6},{8,9},{9,8},{10,11... | collective-permute-start | bytes 393224 | tf_op jit(solution)/shard_map/ppermute | solution.py:286
  3.9 7.8 %collective-permute-start.1 = (f32[2,16,512]{2,1,0:T(8,128)S(1)}, f32[2,16,512]{2,1,0:T(8,128)S(1)}, u32[]{:S(2)}, u32[]{:S(2)}) collective-permute-start(f32[2,16,512]{2,1,0:T(8,128)S(1)} %get-tuple-element.21), channel_id=1, source_target_pairs={{0,12},{1,15},{2,14},{3,13},{4,8},{5,11},{6,10},{7,9},{8,4},{9,7},... | collective-permute-start | bytes 196616 | tf_op jit(solution)/shard_map/ppermute | solution.py:297
  8.9 6.5 %collective-permute-start.2 = (f32[2,16,512]{2,1,0:T(8,128)S(1)}, f32[2,16,512]{2,1,0:T(8,128)S(1)}, u32[]{:S(2)}, u32[]{:S(2)}) collective-permute-start(f32[2,16,512]{2,1,0:T(8,128)S(1)} %get-tuple-element.22), channel_id=1, source_target_pairs={{0,8},{1,11},{2,10},{3,9},{4,12},{5,15},{6,14},{7,13},{8,0},{9,3},... | collective-permute-start | bytes 196616 | tf_op jit(solution)/shard_map/ppermute | solution.py:297
  9.0 7.0 %collective-permute-start.4 = (f32[2,16,512]{2,1,0:T(8,128)S(1)}, f32[2,16,512]{2,1,0:T(8,128)S(1)}, u32[]{:S(2)}, u32[]{:S(2)}) collective-permute-start(f32[2,16,512]{2,1,0:T(8,128)S(1)} %get-tuple-element.25), channel_id=1, source_target_pairs={{0,4},{1,7},{2,6},{3,5},{4,0},{5,3},{6,2},{7,1},{8,12},{9,15},{10,... | collective-permute-start | bytes 196616 | tf_op jit(solution)/shard_map/ppermute | solution.py:297
  9.7 6.3 %collective-permute-start.5 = (f32[2,16,512]{2,1,0:T(8,128)S(1)}, f32[2,16,512]{2,1,0:T(8,128)S(1)}, u32[]{:S(2)}, u32[]{:S(2)}) collective-permute-start(f32[2,16,512]{2,1,0:T(8,128)S(1)} %get-tuple-element.26), channel_id=1, source_target_pairs={{0,0},{1,3},{2,2},{3,1},{4,4},{5,7},{6,6},{7,5},{8,8},{9,11},{10,1... | collective-permute-start | bytes 196616 | tf_op jit(solution)/shard_map/ppermute | solution.py:297
  15.4 1.9 %copy-start.3 = (bf16[2,4,16,128]{3,2,1,0:T(8,128)(2,1)S(1)}, bf16[2,4,16,128]{3,2,1,0:T(8,128)(2,1)}, u32[]{:S(2)}) copy-start(bf16[2,4,16,128]{3,2,1,0:T(8,128)(2,1)} %constant.13.clone.refs_10_.inverse_low) | copy-start | bytes 98308
  15.4 1.9 %copy-start.4 = (bf16[2,4,16,128]{3,2,1,0:T(8,128)(2,1)S(1)}, bf16[2,4,16,128]{3,2,1,0:T(8,128)(2,1)}, u32[]{:S(2)}) copy-start(bf16[2,4,16,128]{3,2,1,0:T(8,128)(2,1)} %constant.12.clone.refs_9_.inverse_high) | copy-start | bytes 98308
  15.5 1.9 %copy-start.5 = (bf16[128,128]{1,0:T(8,128)(2,1)S(1)}, bf16[128,128]{1,0:T(8,128)(2,1)}, u32[]{:S(2)}) copy-start(bf16[128,128]{1,0:T(8,128)(2,1)} %constant.11.clone.refs_8_) | copy-start | bytes 98308
  15.5 1.4 %collective-permute-start.6 = (f32[2,16,512]{2,1,0:T(8,128)S(1)}, f32[2,16,512]{2,1,0:T(8,128)S(1)}, u32[]{:S(2)}, u32[]{:S(2)}) collective-permute-start(f32[2,16,512]{2,1,0:T(8,128)S(1)} %second_halves.2), channel_id=1, source_target_pairs={{0,1},{1,0},{2,3},{3,2},{4,5},{5,4},{6,7},{7,6},{8,9},{9,8},{10,11... | collective-permute-start | bytes 196616 | tf_op jit(solution)/shard_map/ppermute | solution.py:286
  16.0 15.0 %copy-start = (bf16[4,256,512]{2,1,0:T(8,128)(2,1)S(1)}, bf16[4,256,512]{2,1,0:T(8,128)(2,1)}, u32[]{:S(2)}) copy-start(bf16[4,256,512]{2,1,0:T(8,128)(2,1)} %flow_ref.1) | copy-start | bytes 3145732
  16.0 1.3 %collective-permute-start.7 = (f32[2,16,512]{2,1,0:T(8,128)S(1)}, f32[2,16,512]{2,1,0:T(8,128)S(1)}, u32[]{:S(2)}, u32[]{:S(2)}) collective-permute-start(f32[2,16,512]{2,1,0:T(8,128)S(1)} %second_halves.3), channel_id=1, source_target_pairs={{0,1},{1,0},{2,3},{3,2},{4,5},{5,4},{6,7},{7,6},{8,9},{9,8},{10,11... | collective-permute-start | bytes 196616 | tf_op jit(solution)/shard_map/ppermute | solution.py:286
  18.4 1.3 %collective-permute-start.11 = (f32[2,16,512]{2,1,0:T(8,128)S(1)}, f32[2,16,512]{2,1,0:T(8,128)S(1)}, u32[]{:S(2)}, u32[]{:S(2)}) collective-permute-start(f32[2,16,512]{2,1,0:T(8,128)S(1)} %get-tuple-element.33), channel_id=1, source_target_pairs={{0,1},{1,0},{2,3},{3,2},{4,5},{5,4},{6,7},{7,6},{8,9},{9,8},{10,11... | collective-permute-start | bytes 196616 | tf_op jit(solution)/shard_map/ppermute | solution.py:286
  18.7 4.4 %collective-permute-start.8 = (f32[2,16,512]{2,1,0:T(8,128)S(1)}, f32[2,16,512]{2,1,0:T(8,128)S(1)}, u32[]{:S(2)}, u32[]{:S(2)}) collective-permute-start(f32[2,16,512]{2,1,0:T(8,128)S(1)} %get-tuple-element.29), channel_id=1, source_target_pairs={{0,1},{1,0},{2,3},{3,2},{4,5},{5,4},{6,7},{7,6},{8,9},{9,8},{10,11... | collective-permute-start | bytes 196616 | tf_op jit(solution)/shard_map/ppermute | solution.py:286
  19.0 12.1 %copy-start.2 = (bf16[2,2,256,256]{3,2,1,0:T(8,128)(2,1)S(1)}, bf16[2,2,256,256]{3,2,1,0:T(8,128)(2,1)}, u32[]{:S(2)}) copy-start(bf16[2,2,256,256]{3,2,1,0:T(8,128)(2,1)} %constant.14.clone.table_ref) | copy-start | bytes 1572868
  19.7 8.7 %collective-permute-start.12 = (f32[4,8,512]{2,1,0:T(8,128)S(1)}, f32[4,8,512]{2,1,0:T(8,128)S(1)}, u32[]{:S(2)}, u32[]{:S(2)}) collective-permute-start(f32[4,8,512]{2,1,0:T(8,128)S(1)} %get-tuple-element.34), channel_id=1, source_target_pairs={{0,8},{1,11},{2,10},{3,9},{4,12},{5,15},{6,14},{7,13},{8,0},{9,3},... | collective-permute-start | bytes 196616 | tf_op jit(solution)/shard_map/ppermute | solution.py:297
  21.1 7.4 %collective-permute-start.13 = (f32[4,8,512]{2,1,0:T(8,128)S(1)}, f32[4,8,512]{2,1,0:T(8,128)S(1)}, u32[]{:S(2)}, u32[]{:S(2)}) collective-permute-start(f32[4,8,512]{2,1,0:T(8,128)S(1)} %get-tuple-element.35), channel_id=1, source_target_pairs={{0,12},{1,15},{2,14},{3,13},{4,8},{5,11},{6,10},{7,9},{8,4},{9,7},... | collective-permute-start | bytes 196616 | tf_op jit(solution)/shard_map/ppermute | solution.py:297
  23.1 6.4 %collective-permute-start.9 = (f32[4,8,512]{2,1,0:T(8,128)S(1)}, f32[4,8,512]{2,1,0:T(8,128)S(1)}, u32[]{:S(2)}, u32[]{:S(2)}) collective-permute-start(f32[4,8,512]{2,1,0:T(8,128)S(1)} %get-tuple-element.30), channel_id=1, source_target_pairs={{0,4},{1,7},{2,6},{3,5},{4,0},{5,3},{6,2},{7,1},{8,12},{9,15},{10,... | collective-permute-start | bytes 196616 | tf_op jit(solution)/shard_map/ppermute | solution.py:297
  23.7 5.9 %collective-permute-start.10 = (f32[4,8,512]{2,1,0:T(8,128)S(1)}, f32[4,8,512]{2,1,0:T(8,128)S(1)}, u32[]{:S(2)}, u32[]{:S(2)}) collective-permute-start(f32[4,8,512]{2,1,0:T(8,128)S(1)} %get-tuple-element.31), channel_id=1, source_target_pairs={{0,0},{1,3},{2,2},{3,1},{4,4},{5,7},{6,6},{7,5},{8,8},{9,11},{10,1... | collective-permute-start | bytes 196616 | tf_op jit(solution)/shard_map/ppermute | solution.py:297
  28.5 2.5 %copy-start.7 = (bf16[64,64]{1,0:T(8,128)(2,1)S(1)}, bf16[64,64]{1,0:T(8,128)(2,1)}, u32[]{:S(2)}) copy-start(bf16[64,64]{1,0:T(8,128)(2,1)} %local_ref.1) | copy-start | bytes 24580
  28.5 2.5 %copy-start.8 = (f32[64]{0:T(128)S(1)}, f32[64]{0:T(128)}, u32[]{:S(2)}) copy-start(f32[64]{0:T(128)} %bias_ref.1) | copy-start | bytes 772
  28.5 1.5 %collective-permute-start.15 = (f32[2,4,8,512]{3,2,1,0:T(8,128)S(1)}, f32[2,4,8,512]{3,2,1,0:T(8,128)S(1)}, u32[]{:S(2)}, u32[]{:S(2)}) collective-permute-start(f32[2,4,8,512]{3,2,1,0:T(8,128)S(1)} %stack_blocks.3), channel_id=1, source_target_pairs={{0,1},{1,0},{2,3},{3,2},{4,5},{5,4},{6,7},{7,6},{8,9},{9,8},{10,11... | collective-permute-start | bytes 393224 | tf_op jit(solution)/shard_map/ppermute | solution.py:286
  29.6 1.4 %collective-permute-start.14 = (f32[2,4,8,512]{3,2,1,0:T(8,128)S(1)}, f32[2,4,8,512]{3,2,1,0:T(8,128)S(1)}, u32[]{:S(2)}, u32[]{:S(2)}) collective-permute-start(f32[2,4,8,512]{3,2,1,0:T(8,128)S(1)} %stack_blocks.2), channel_id=1, source_target_pairs={{0,1},{1,0},{2,3},{3,2},{4,5},{5,4},{6,7},{7,6},{8,9},{9,8},{10,11... | collective-permute-start | bytes 393224 | tf_op jit(solution)/shard_map/ppermute | solution.py:286
  (1 other events, 1.8 us)

commit v33 on v32

--- a/solution.py
+++ b/solution.py
@@ -130,6 +130,7 @@
 LARGE = pltpu.CompilerParams(vmem_limit_bytes=53 * 1024 * 1024)
 WIDTH = 256
 BIAS_TERMS = 3
+LAST = 64
 FIRST = 64
 GELU_TERMS = (
     1.5957645177841187,
@@ -470,7 +471,7 @@
     near_ref, far_ref = refs[layers : layers + 2]
     core_refs = [ref.at[index] for ref in (far_ref, near_ref) for index in range(layers // 2)]
     out_hbm, mixed_hbm, order_ref, wide_ref, level_ref, done_ref, sent = refs[layers + 2 :]
-    cells_x, _, feat_count = flow_ref.shape
+    cells_x, cells_y, feat_count = flow_ref.shape
     channels = local_ref.shape[0]
     z, x, y = quad()
     wide_ref[...] = jnp.zeros_like(wide_ref)
@@ -498,22 +499,29 @@
             pltpu.make_async_copy(
                 modes_ref.at[pl.ds(part * count, count)],
                 mixed_hbm.at[0, :, pl.ds(part * feat_count, feat_count)],
-                sent.at[cells_x + part],
+                sent.at[part],
             )
         )
         copies[-1].start()
     for cell in range(cells_x):
         high, low = split_terms(order_ref[cell].reshape(-1, feat_count))
         stack = jnp.concatenate([high, low, high], axis=0)
-        for start in range(0, feat_count, WIDTH):
-            columns = slice(start, start + WIDTH)
-            total = dot(
-                jnp.concatenate([table, flow_ref[cell, :, columns]], axis=1),
-                jnp.concatenate([stack[:, columns], below], axis=0),
+        bounds = [0, cells_y - LAST, cells_y] if cell == cells_x - 1 else [0, cells_y]
+        for begin, end in zip(bounds[:-1], bounds[1:]):
+            rows = slice(begin, end)
+            for start in range(0, feat_count, WIDTH):
+                columns = slice(start, start + WIDTH)
+                total = dot(
+                    jnp.concatenate([table[rows], flow_ref[cell, rows, columns]], axis=1),
+                    jnp.concatenate([stack[:, columns], below], axis=0),
+                )
+                done_ref[cell, rows, columns] = gelu(total).astype(done_ref.dtype)
+            copies.append(
+                pltpu.make_async_copy(
+                    done_ref.at[cell, rows], out_hbm.at[cell, rows], sent.at[len(copies)]
+                )
             )
-            done_ref[cell, :, columns] = gelu(total).astype(done_ref.dtype)
-        copies.append(pltpu.make_async_copy(done_ref.at[cell], out_hbm.at[cell], sent.at[cell]))
-        copies[-1].start()
+            copies[-1].start()
     for copy in copies:
         copy.wait()
 
@@ -530,7 +538,7 @@
             pltpu.VMEM((WIDTH, WIDTH), jnp.bfloat16),
             pltpu.VMEM((1, WIDTH), jnp.float32),
             pltpu.VMEM(flow_field.shape, jnp.bfloat16),
-            pltpu.SemaphoreType.DMA((cells_x + 2,)),
+            pltpu.SemaphoreType.DMA((cells_x + 3,)),
         ],
         out_shape=[
             jax.ShapeDtypeStruct(flow_field.shape, jnp.bfloat16),

time: 33.5 us -> 33.4 us (level)
  no operation moved by 1% of the time
where the time goes in v33:
time: 33.4 us; the launch traced here: 33.3 us
  starting transfers between devices  13.5 us (40%)
  waiting for transfers between devices  13.5 us (40%)
  Pallas kernels  5.35 us (16%)
  between operations  0.8 us (2%)
    ppermute x8, starting transfers between devices, along_columns(): arrived.append(lax.ppermute(block, ('gx', 'gy'), pairs))  11 us
    ppermute x8, waiting for transfers between devices, along_columns(): arrived.append(lax.ppermute(block, ('gx', 'gy'), pairs))  10.1 us
    ppermute x8, waiting for transfers between devices, flip_core(): return lax.ppermute(block, 'gy', [(0, 1), (1, 0)])  3.4 us
    ppermute x8, starting transfers between devices, flip_core(): return lax.ppermute(block, 'gy', [(0, 1), (1, 0)])  2.56 us
    pallas_call x1, Pallas kernels, make_output(): pl.pallas_call(functools.partial(output_kernel, layers), out_specs=[pl.Bl...  2.25 us
    pallas_call x1, Pallas kernels, forward_y(): pl.pallas_call(functools.partial(forward_y_kernel, extent, rows_ky), in_s...  1.75 us
    pallas_call x1, Pallas kernels, mix(): pl.pallas_call(functools.partial(mix_kernel, layers), out_shape=[jax.Shap...  1.04 us
  transfers between devices with their start and end apart: 16, of which 9 were waited for; matrix products, arithmetic and copies ran while one was open for 0% of the time, Pallas kernels for 1%

profile of v33, /device:TPU:0, one launch (start us, length us, event | category | flops | bytes accessed | tf_op | source)
XLA Modules:
  0.0 33.3 jit_solution(11709176128337525008)
XLA Ops:
  0.6 1.7 %forward_y.1 = (f32[2,2,16,512]{3,2,1,0:T(8,128)S(1)}, f32[2,2,16,512]{3,2,1,0:T(8,128)S(1)}, f32[2,2,16,512]{3,2,1,0:T(8,128)S(1)}, f32[2,2,16,512]{3,2,1,0:T(8,128)S(1)}) custom-call(bf16[4,256,512]{2,1,0:T(8,128)(2,1)} %flow_ref.1), custom_call_target="tpu_custom_call" | custom-call | tf_op jit(solution)/shard_map/forward_y/pallas_call | solution.py:273
  2.4 0.5 %collective-permute-start = (f32[2,2,16,512]{3,2,1,0:T(8,128)S(1)}, f32[2,2,16,512]{3,2,1,0:T(8,128)S(1)}, u32[]{:S(2)}, u32[]{:S(2)}) collective-permute-start(f32[2,2,16,512]{3,2,1,0:T(8,128)S(1)} %get-tuple-element.20), channel_id=1, source_target_pairs={{0,1},{1,0},{2,3},{3,2},{4,5},{5,4},{6,7},{7,6},{8,9},{9,8},{10,11... | collective-permute-start | bytes 393224 | tf_op jit(solution)/shard_map/ppermute | solution.py:287
  3.0 0.9 %collective-permute-done.arrived_ref = f32[2,2,16,512]{3,2,1,0:T(8,128)S(1)} collective-permute-done((f32[2,2,16,512]{3,2,1,0:T(8,128)S(1)}, f32[2,2,16,512]{3,2,1,0:T(8,128)S(1)}, u32[]{:S(2)}, u32[]{:S(2)}) %collective-permute-start) | collective-permute-done | bytes 131104 | tf_op jit(solution)/shard_map/ppermute | solution.py:287
  3.9 5.0 %collective-permute-start.1 = (f32[2,16,512]{2,1,0:T(8,128)S(1)}, f32[2,16,512]{2,1,0:T(8,128)S(1)}, u32[]{:S(2)}, u32[]{:S(2)}) collective-permute-start(f32[2,16,512]{2,1,0:T(8,128)S(1)} %get-tuple-element.21), channel_id=1, source_target_pairs={{0,12},{1,15},{2,14},{3,13},{4,8},{5,11},{6,10},{7,9},{8,4},{9,7},... | collective-permute-start | bytes 196616 | tf_op jit(solution)/shard_map/ppermute | solution.py:298
  9.0 0.7 %collective-permute-start.4 = (f32[2,16,512]{2,1,0:T(8,128)S(1)}, f32[2,16,512]{2,1,0:T(8,128)S(1)}, u32[]{:S(2)}, u32[]{:S(2)}) collective-permute-start(f32[2,16,512]{2,1,0:T(8,128)S(1)} %get-tuple-element.25), channel_id=1, source_target_pairs={{0,4},{1,7},{2,6},{3,5},{4,0},{5,3},{6,2},{7,1},{8,12},{9,15},{10,... | collective-permute-start | bytes 196616 | tf_op jit(solution)/shard_map/ppermute | solution.py:298
  9.7 0.7 %collective-permute-start.5 = (f32[2,16,512]{2,1,0:T(8,128)S(1)}, f32[2,16,512]{2,1,0:T(8,128)S(1)}, u32[]{:S(2)}, u32[]{:S(2)}) collective-permute-start(f32[2,16,512]{2,1,0:T(8,128)S(1)} %get-tuple-element.26), channel_id=1, source_target_pairs={{0,0},{1,3},{2,2},{3,1},{4,4},{5,7},{6,6},{7,5},{8,8},{9,11},{10,1... | collective-permute-start | bytes 196616 | tf_op jit(solution)/shard_map/ppermute | solution.py:298
  10.3 1.3 %collective-permute-done.1.refs_0_ = f32[2,16,512]{2,1,0:T(8,128)S(1)} collective-permute-done((f32[2,16,512]{2,1,0:T(8,128)S(1)}, f32[2,16,512]{2,1,0:T(8,128)S(1)}, u32[]{:S(2)}, u32[]{:S(2)}) %collective-permute-start.1) | collective-permute-done | bytes 65568 | tf_op jit(solution)/shard_map/ppermute | solution.py:298
  11.7 3.8 %collective-permute-done.2.refs_1_ = f32[2,16,512]{2,1,0:T(8,128)S(1)} collective-permute-done((f32[2,16,512]{2,1,0:T(8,128)S(1)}, f32[2,16,512]{2,1,0:T(8,128)S(1)}, u32[]{:S(2)}, u32[]{:S(2)}) %collective-permute-start.2) | collective-permute-done | bytes 65568 | tf_op jit(solution)/shard_map/ppermute | solution.py:298
  15.5 0.5 %collective-permute-start.6 = (f32[2,16,512]{2,1,0:T(8,128)S(1)}, f32[2,16,512]{2,1,0:T(8,128)S(1)}, u32[]{:S(2)}, u32[]{:S(2)}) collective-permute-start(f32[2,16,512]{2,1,0:T(8,128)S(1)} %second_halves.2), channel_id=1, source_target_pairs={{0,1},{1,0},{2,3},{3,2},{4,5},{5,4},{6,7},{7,6},{8,9},{9,8},{10,11... | collective-permute-start | bytes 196616 | tf_op jit(solution)/shard_map/ppermute | solution.py:287
  16.0 0.3 %collective-permute-start.7 = (f32[2,16,512]{2,1,0:T(8,128)S(1)}, f32[2,16,512]{2,1,0:T(8,128)S(1)}, u32[]{:S(2)}, u32[]{:S(2)}) collective-permute-start(f32[2,16,512]{2,1,0:T(8,128)S(1)} %second_halves.3), channel_id=1, source_target_pairs={{0,1},{1,0},{2,3},{3,2},{4,5},{5,4},{6,7},{7,6},{8,9},{9,8},{10,11... | collective-permute-start | bytes 196616 | tf_op jit(solution)/shard_map/ppermute | solution.py:287
  16.3 0.5 %collective-permute-done.6.refs_4_ = f32[2,16,512]{2,1,0:T(8,128)S(1)} collective-permute-done((f32[2,16,512]{2,1,0:T(8,128)S(1)}, f32[2,16,512]{2,1,0:T(8,128)S(1)}, u32[]{:S(2)}, u32[]{:S(2)}) %collective-permute-start.6) | collective-permute-done | bytes 65568 | tf_op jit(solution)/shard_map/ppermute | solution.py:287
  16.8 0.4 %collective-permute-done.7.refs_5_ = f32[2,16,512]{2,1,0:T(8,128)S(1)} collective-permute-done((f32[2,16,512]{2,1,0:T(8,128)S(1)}, f32[2,16,512]{2,1,0:T(8,128)S(1)}, u32[]{:S(2)}, u32[]{:S(2)}) %collective-permute-start.7) | collective-permute-done | bytes 65568 | tf_op jit(solution)/shard_map/ppermute | solution.py:287
  17.3 1.0 %mix.1 = (f32[128,512]{1,0:T(8,128)S(1)}, f32[2,16,512]{2,1,0:T(8,128)S(1)}, f32[2,16,512]{2,1,0:T(8,128)S(1)}) custom-call(f32[2,16,512]{2,1,0:T(8,128)S(1)} %collective-permute-done.1.refs_0_, f32[2,16,512]{2,1,0:T(8,128)S(1)} %collective-permute-done.2.refs_1_, f32[2,16,512]{2,1,0:T(8,128)S(1)} %collective-permute-done.4.refs_0_.refs_2_, ...), custom_call_target="tpu_custom_call" | custom-call | tf_op jit(solution)/shard_map/mix/pallas_call | solution.py:431
  18.4 0.3 %collective-permute-start.11 = (f32[2,16,512]{2,1,0:T(8,128)S(1)}, f32[2,16,512]{2,1,0:T(8,128)S(1)}, u32[]{:S(2)}, u32[]{:S(2)}) collective-permute-start(f32[2,16,512]{2,1,0:T(8,128)S(1)} %get-tuple-element.33), channel_id=1, source_target_pairs={{0,1},{1,0},{2,3},{3,2},{4,5},{5,4},{6,7},{7,6},{8,9},{9,8},{10,11... | collective-permute-start | bytes 196616 | tf_op jit(solution)/shard_map/ppermute | solution.py:287
  19.2 0.5 %collective-permute-done.11.arrived_ref = f32[2,16,512]{2,1,0:T(8,128)S(1)} collective-permute-done((f32[2,16,512]{2,1,0:T(8,128)S(1)}, f32[2,16,512]{2,1,0:T(8,128)S(1)}, u32[]{:S(2)}, u32[]{:S(2)}) %collective-permute-start.11) | collective-permute-done | bytes 65568 | tf_op jit(solution)/shard_map/ppermute | solution.py:287
  19.7 1.4 %collective-permute-start.12 = (f32[4,8,512]{2,1,0:T(8,128)S(1)}, f32[4,8,512]{2,1,0:T(8,128)S(1)}, u32[]{:S(2)}, u32[]{:S(2)}) collective-permute-start(f32[4,8,512]{2,1,0:T(8,128)S(1)} %get-tuple-element.34), channel_id=1, source_target_pairs={{0,8},{1,11},{2,10},{3,9},{4,12},{5,15},{6,14},{7,13},{8,0},{9,3},... | collective-permute-start | bytes 196616 | tf_op jit(solution)/shard_map/ppermute | solution.py:298
  21.1 2.0 %collective-permute-start.13 = (f32[4,8,512]{2,1,0:T(8,128)S(1)}, f32[4,8,512]{2,1,0:T(8,128)S(1)}, u32[]{:S(2)}, u32[]{:S(2)}) collective-permute-start(f32[4,8,512]{2,1,0:T(8,128)S(1)} %get-tuple-element.35), channel_id=1, source_target_pairs={{0,12},{1,15},{2,14},{3,13},{4,8},{5,11},{6,10},{7,9},{8,4},{9,7},... | collective-permute-start | bytes 196616 | tf_op jit(solution)/shard_map/ppermute | solution.py:298
  23.1 0.6 %collective-permute-start.9 = (f32[4,8,512]{2,1,0:T(8,128)S(1)}, f32[4,8,512]{2,1,0:T(8,128)S(1)}, u32[]{:S(2)}, u32[]{:S(2)}) collective-permute-start(f32[4,8,512]{2,1,0:T(8,128)S(1)} %get-tuple-element.30), channel_id=1, source_target_pairs={{0,4},{1,7},{2,6},{3,5},{4,0},{5,3},{6,2},{7,1},{8,12},{9,15},{10,... | collective-permute-start | bytes 196616 | tf_op jit(solution)/shard_map/ppermute | solution.py:298
  23.7 0.7 %collective-permute-start.10 = (f32[4,8,512]{2,1,0:T(8,128)S(1)}, f32[4,8,512]{2,1,0:T(8,128)S(1)}, u32[]{:S(2)}, u32[]{:S(2)}) collective-permute-start(f32[4,8,512]{2,1,0:T(8,128)S(1)} %get-tuple-element.31), channel_id=1, source_target_pairs={{0,0},{1,3},{2,2},{3,1},{4,4},{5,7},{6,6},{7,5},{8,8},{9,11},{10,1... | collective-permute-start | bytes 196616 | tf_op jit(solution)/shard_map/ppermute | solution.py:298
  24.3 4.1 %collective-permute-done.12.refs_0_.refs_2_ = f32[4,8,512]{2,1,0:T(8,128)S(1)} collective-permute-done((f32[4,8,512]{2,1,0:T(8,128)S(1)}, f32[4,8,512]{2,1,0:T(8,128)S(1)}, u32[]{:S(2)}, u32[]{:S(2)}) %collective-permute-start.12) | collective-permute-done | bytes 65568 | tf_op jit(solution)/shard_map/ppermute | solution.py:298
  28.7 0.9 %collective-permute-done.9.refs_0_ = f32[4,8,512]{2,1,0:T(8,128)S(1)} collective-permute-done((f32[4,8,512]{2,1,0:T(8,128)S(1)}, f32[4,8,512]{2,1,0:T(8,128)S(1)}, u32[]{:S(2)}, u32[]{:S(2)}) %collective-permute-start.9) | collective-permute-done | bytes 65568 | tf_op jit(solution)/shard_map/ppermute | solution.py:298
  29.6 0.4 %collective-permute-start.14 = (f32[2,4,8,512]{3,2,1,0:T(8,128)S(1)}, f32[2,4,8,512]{3,2,1,0:T(8,128)S(1)}, u32[]{:S(2)}, u32[]{:S(2)}) collective-permute-start(f32[2,4,8,512]{3,2,1,0:T(8,128)S(1)} %stack_blocks.2), channel_id=1, source_target_pairs={{0,1},{1,0},{2,3},{3,2},{4,5},{5,4},{6,7},{7,6},{8,9},{9,8},{10,11... | collective-permute-start | bytes 393224 | tf_op jit(solution)/shard_map/ppermute | solution.py:287
  30.0 1.0 %collective-permute-done.14.refs_4_ = f32[2,4,8,512]{3,2,1,0:T(8,128)S(1)} collective-permute-done((f32[2,4,8,512]{3,2,1,0:T(8,128)S(1)}, f32[2,4,8,512]{3,2,1,0:T(8,128)S(1)}, u32[]{:S(2)}, u32[]{:S(2)}) %collective-permute-start.14) | collective-permute-done | bytes 131104 | tf_op jit(solution)/shard_map/ppermute | solution.py:287
  31.0 2.2 %make_output.1 = (bf16[4,256,512]{2,1,0:T(8,128)(2,1)}, f32[1,64,1024]{2,1,0:T(8,128)}) custom-call(bf16[4,256,512]{2,1,0:T(8,128)(2,1)S(1)} %copy-done, bf16[2,2,256,256]{3,2,1,0:T(8,128)(2,1)S(1)} %copy-done.2, bf16[64,64]{1,0:T(8,128)(2,1)S(1)} %copy-done.7, f32[64]{0:T(128)S(1)} %copy-done.8, f32[128,512]{1,0:T(8,128)S(1)} %get-tuple-element.27.modes_ref, ...), custom_call_target="tpu_custom_call" | custom-call | tf_op jit(solution)/shard_map/make_output/pallas_call | solution.py:533
  (38 shorter events, 0.8 us)
Async XLA Ops:
  0.6 16.7 %copy-start.1 = (bf16[1,64,64,128]{3,2,1,0:T(8,128)(2,1)S(1)}, bf16[1,64,64,128]{3,2,1,0:T(8,128)(2,1)}, u32[]{:S(2)}) copy-start(bf16[1,64,64,128]{3,2,1,0:T(8,128)(2,1)} %refs_6_.1) | copy-start | bytes 3145732
  2.4 1.5 %collective-permute-start = (f32[2,2,16,512]{3,2,1,0:T(8,128)S(1)}, f32[2,2,16,512]{3,2,1,0:T(8,128)S(1)}, u32[]{:S(2)}, u32[]{:S(2)}) collective-permute-start(f32[2,2,16,512]{3,2,1,0:T(8,128)S(1)} %get-tuple-element.20), channel_id=1, source_target_pairs={{0,1},{1,0},{2,3},{3,2},{4,5},{5,4},{6,7},{7,6},{8,9},{9,8},{10,11... | collective-permute-start | bytes 393224 | tf_op jit(solution)/shard_map/ppermute | solution.py:287
  2.9 6.0 %collective-permute-start.3 = (f32[2,2,16,512]{3,2,1,0:T(8,128)S(1)}, f32[2,2,16,512]{3,2,1,0:T(8,128)S(1)}, u32[]{:S(2)}, u32[]{:S(2)}) collective-permute-start(f32[2,2,16,512]{3,2,1,0:T(8,128)S(1)} %get-tuple-element.24), channel_id=1, source_target_pairs={{0,1},{1,0},{2,3},{3,2},{4,5},{5,4},{6,7},{7,6},{8,9},{9,8},{10,11... | collective-permute-start | bytes 393224 | tf_op jit(solution)/shard_map/ppermute | solution.py:287
  3.9 7.8 %collective-permute-start.1 = (f32[2,16,512]{2,1,0:T(8,128)S(1)}, f32[2,16,512]{2,1,0:T(8,128)S(1)}, u32[]{:S(2)}, u32[]{:S(2)}) collective-permute-start(f32[2,16,512]{2,1,0:T(8,128)S(1)} %get-tuple-element.21), channel_id=1, source_target_pairs={{0,12},{1,15},{2,14},{3,13},{4,8},{5,11},{6,10},{7,9},{8,4},{9,7},... | collective-permute-start | bytes 196616 | tf_op jit(solution)/shard_map/ppermute | solution.py:298
  8.9 6.5 %collective-permute-start.2 = (f32[2,16,512]{2,1,0:T(8,128)S(1)}, f32[2,16,512]{2,1,0:T(8,128)S(1)}, u32[]{:S(2)}, u32[]{:S(2)}) collective-permute-start(f32[2,16,512]{2,1,0:T(8,128)S(1)} %get-tuple-element.22), channel_id=1, source_target_pairs={{0,8},{1,11},{2,10},{3,9},{4,12},{5,15},{6,14},{7,13},{8,0},{9,3},... | collective-permute-start | bytes 196616 | tf_op jit(solution)/shard_map/ppermute | solution.py:298
  9.0 7.0 %collective-permute-start.4 = (f32[2,16,512]{2,1,0:T(8,128)S(1)}, f32[2,16,512]{2,1,0:T(8,128)S(1)}, u32[]{:S(2)}, u32[]{:S(2)}) collective-permute-start(f32[2,16,512]{2,1,0:T(8,128)S(1)} %get-tuple-element.25), channel_id=1, source_target_pairs={{0,4},{1,7},{2,6},{3,5},{4,0},{5,3},{6,2},{7,1},{8,12},{9,15},{10,... | collective-permute-start | bytes 196616 | tf_op jit(solution)/shard_map/ppermute | solution.py:298
  9.7 6.3 %collective-permute-start.5 = (f32[2,16,512]{2,1,0:T(8,128)S(1)}, f32[2,16,512]{2,1,0:T(8,128)S(1)}, u32[]{:S(2)}, u32[]{:S(2)}) collective-permute-start(f32[2,16,512]{2,1,0:T(8,128)S(1)} %get-tuple-element.26), channel_id=1, source_target_pairs={{0,0},{1,3},{2,2},{3,1},{4,4},{5,7},{6,6},{7,5},{8,8},{9,11},{10,1... | collective-permute-start | bytes 196616 | tf_op jit(solution)/shard_map/ppermute | solution.py:298
  15.4 1.9 %copy-start.3 = (bf16[2,4,16,128]{3,2,1,0:T(8,128)(2,1)S(1)}, bf16[2,4,16,128]{3,2,1,0:T(8,128)(2,1)}, u32[]{:S(2)}) copy-start(bf16[2,4,16,128]{3,2,1,0:T(8,128)(2,1)} %constant.13.clone.refs_10_.inverse_low) | copy-start | bytes 98308
  15.4 1.9 %copy-start.4 = (bf16[2,4,16,128]{3,2,1,0:T(8,128)(2,1)S(1)}, bf16[2,4,16,128]{3,2,1,0:T(8,128)(2,1)}, u32[]{:S(2)}) copy-start(bf16[2,4,16,128]{3,2,1,0:T(8,128)(2,1)} %constant.12.clone.refs_9_.inverse_high) | copy-start | bytes 98308
  15.5 1.9 %copy-start.5 = (bf16[128,128]{1,0:T(8,128)(2,1)S(1)}, bf16[128,128]{1,0:T(8,128)(2,1)}, u32[]{:S(2)}) copy-start(bf16[128,128]{1,0:T(8,128)(2,1)} %constant.11.clone.refs_8_) | copy-start | bytes 98308
  15.5 1.4 %collective-permute-start.6 = (f32[2,16,512]{2,1,0:T(8,128)S(1)}, f32[2,16,512]{2,1,0:T(8,128)S(1)}, u32[]{:S(2)}, u32[]{:S(2)}) collective-permute-start(f32[2,16,512]{2,1,0:T(8,128)S(1)} %second_halves.2), channel_id=1, source_target_pairs={{0,1},{1,0},{2,3},{3,2},{4,5},{5,4},{6,7},{7,6},{8,9},{9,8},{10,11... | collective-permute-start | bytes 196616 | tf_op jit(solution)/shard_map/ppermute | solution.py:287
  16.0 15.0 %copy-start = (bf16[4,256,512]{2,1,0:T(8,128)(2,1)S(1)}, bf16[4,256,512]{2,1,0:T(8,128)(2,1)}, u32[]{:S(2)}) copy-start(bf16[4,256,512]{2,1,0:T(8,128)(2,1)} %flow_ref.1) | copy-start | bytes 3145732
  16.0 1.3 %collective-permute-start.7 = (f32[2,16,512]{2,1,0:T(8,128)S(1)}, f32[2,16,512]{2,1,0:T(8,128)S(1)}, u32[]{:S(2)}, u32[]{:S(2)}) collective-permute-start(f32[2,16,512]{2,1,0:T(8,128)S(1)} %second_halves.3), channel_id=1, source_target_pairs={{0,1},{1,0},{2,3},{3,2},{4,5},{5,4},{6,7},{7,6},{8,9},{9,8},{10,11... | collective-permute-start | bytes 196616 | tf_op jit(solution)/shard_map/ppermute | solution.py:287
  18.4 1.3 %collective-permute-start.11 = (f32[2,16,512]{2,1,0:T(8,128)S(1)}, f32[2,16,512]{2,1,0:T(8,128)S(1)}, u32[]{:S(2)}, u32[]{:S(2)}) collective-permute-start(f32[2,16,512]{2,1,0:T(8,128)S(1)} %get-tuple-element.33), channel_id=1, source_target_pairs={{0,1},{1,0},{2,3},{3,2},{4,5},{5,4},{6,7},{7,6},{8,9},{9,8},{10,11... | collective-permute-start | bytes 196616 | tf_op jit(solution)/shard_map/ppermute | solution.py:287
  18.7 4.4 %collective-permute-start.8 = (f32[2,16,512]{2,1,0:T(8,128)S(1)}, f32[2,16,512]{2,1,0:T(8,128)S(1)}, u32[]{:S(2)}, u32[]{:S(2)}) collective-permute-start(f32[2,16,512]{2,1,0:T(8,128)S(1)} %get-tuple-element.29), channel_id=1, source_target_pairs={{0,1},{1,0},{2,3},{3,2},{4,5},{5,4},{6,7},{7,6},{8,9},{9,8},{10,11... | collective-permute-start | bytes 196616 | tf_op jit(solution)/shard_map/ppermute | solution.py:287
  19.0 12.1 %copy-start.2 = (bf16[2,2,256,256]{3,2,1,0:T(8,128)(2,1)S(1)}, bf16[2,2,256,256]{3,2,1,0:T(8,128)(2,1)}, u32[]{:S(2)}) copy-start(bf16[2,2,256,256]{3,2,1,0:T(8,128)(2,1)} %constant.14.clone.table_ref) | copy-start | bytes 1572868
  19.7 8.7 %collective-permute-start.12 = (f32[4,8,512]{2,1,0:T(8,128)S(1)}, f32[4,8,512]{2,1,0:T(8,128)S(1)}, u32[]{:S(2)}, u32[]{:S(2)}) collective-permute-start(f32[4,8,512]{2,1,0:T(8,128)S(1)} %get-tuple-element.34), channel_id=1, source_target_pairs={{0,8},{1,11},{2,10},{3,9},{4,12},{5,15},{6,14},{7,13},{8,0},{9,3},... | collective-permute-start | bytes 196616 | tf_op jit(solution)/shard_map/ppermute | solution.py:298
  21.1 7.4 %collective-permute-start.13 = (f32[4,8,512]{2,1,0:T(8,128)S(1)}, f32[4,8,512]{2,1,0:T(8,128)S(1)}, u32[]{:S(2)}, u32[]{:S(2)}) collective-permute-start(f32[4,8,512]{2,1,0:T(8,128)S(1)} %get-tuple-element.35), channel_id=1, source_target_pairs={{0,12},{1,15},{2,14},{3,13},{4,8},{5,11},{6,10},{7,9},{8,4},{9,7},... | collective-permute-start | bytes 196616 | tf_op jit(solution)/shard_map/ppermute | solution.py:298
  23.1 6.4 %collective-permute-start.9 = (f32[4,8,512]{2,1,0:T(8,128)S(1)}, f32[4,8,512]{2,1,0:T(8,128)S(1)}, u32[]{:S(2)}, u32[]{:S(2)}) collective-permute-start(f32[4,8,512]{2,1,0:T(8,128)S(1)} %get-tuple-element.30), channel_id=1, source_target_pairs={{0,4},{1,7},{2,6},{3,5},{4,0},{5,3},{6,2},{7,1},{8,12},{9,15},{10,... | collective-permute-start | bytes 196616 | tf_op jit(solution)/shard_map/ppermute | solution.py:298
  23.7 5.9 %collective-permute-start.10 = (f32[4,8,512]{2,1,0:T(8,128)S(1)}, f32[4,8,512]{2,1,0:T(8,128)S(1)}, u32[]{:S(2)}, u32[]{:S(2)}) collective-permute-start(f32[4,8,512]{2,1,0:T(8,128)S(1)} %get-tuple-element.31), channel_id=1, source_target_pairs={{0,0},{1,3},{2,2},{3,1},{4,4},{5,7},{6,6},{7,5},{8,8},{9,11},{10,1... | collective-permute-start | bytes 196616 | tf_op jit(solution)/shard_map/ppermute | solution.py:298
  28.5 2.5 %copy-start.7 = (bf16[64,64]{1,0:T(8,128)(2,1)S(1)}, bf16[64,64]{1,0:T(8,128)(2,1)}, u32[]{:S(2)}) copy-start(bf16[64,64]{1,0:T(8,128)(2,1)} %local_ref.1) | copy-start | bytes 24580
  28.5 2.5 %copy-start.8 = (f32[64]{0:T(128)S(1)}, f32[64]{0:T(128)}, u32[]{:S(2)}) copy-start(f32[64]{0:T(128)} %bias_ref.1) | copy-start | bytes 772
  28.5 1.5 %collective-permute-start.15 = (f32[2,4,8,512]{3,2,1,0:T(8,128)S(1)}, f32[2,4,8,512]{3,2,1,0:T(8,128)S(1)}, u32[]{:S(2)}, u32[]{:S(2)}) collective-permute-start(f32[2,4,8,512]{3,2,1,0:T(8,128)S(1)} %stack_blocks.3), channel_id=1, source_target_pairs={{0,1},{1,0},{2,3},{3,2},{4,5},{5,4},{6,7},{7,6},{8,9},{9,8},{10,11... | collective-permute-start | bytes 393224 | tf_op jit(solution)/shard_map/ppermute | solution.py:287
  29.6 1.4 %collective-permute-start.14 = (f32[2,4,8,512]{3,2,1,0:T(8,128)S(1)}, f32[2,4,8,512]{3,2,1,0:T(8,128)S(1)}, u32[]{:S(2)}, u32[]{:S(2)}) collective-permute-start(f32[2,4,8,512]{3,2,1,0:T(8,128)S(1)} %stack_blocks.2), channel_id=1, source_target_pairs={{0,1},{1,0},{2,3},{3,2},{4,5},{5,4},{6,7},{7,6},{8,9},{9,8},{10,11... | collective-permute-start | bytes 393224 | tf_op jit(solution)/shard_map/ppermute | solution.py:287
  (1 other events, 1.8 us)

commit v34 on v33

--- a/solution.py
+++ b/solution.py
@@ -131,7 +131,6 @@
 WIDTH = 256
 BIAS_TERMS = 3
 LAST = 64
-FIRST = 64
 GELU_TERMS = (
     1.5957645177841187,
     0.29075613617897034,
@@ -213,6 +212,16 @@
                     half = y ^ place ^ column ^ (peer % 2)
                     out[y, column, :, peer, place] = np.moveaxis(full[half, peer, :, :, y], -1, 0)
     return out.reshape(groups_y, 2, cells_y, 4 * peers * rows_ky)
+
+
+def joined_table(table):
+    high, low = split_table(table)
+    return np.concatenate([high, high, low], axis=-1)
+
+
+def joined_terms(values):
+    high, low = split_terms(values)
+    return jnp.concatenate([high, low, high], axis=0)
 
 
 def output_table(table):
@@ -350,15 +359,11 @@
     return small_call(join_kernel, [shape] * layers, "join_blocks")(keep, arrived)
 
 
-def back_rows(inverse_high, inverse_low, modes, shape, other):
+def back_rows(inverse_table, modes, shape, other):
     z, x, y = quad()
     places = [(column_of(x, y) ^ other, z ^ turn) for turn in turns(shape[0], True)]
-    table_high, table_low = [
-        jnp.concatenate([ref[column, place] for column, place in places], axis=0)
-        for ref in (inverse_high, inverse_low)
-    ]
-    high, low = split_terms(modes)
-    back = dot(table_high, high) + dot(table_high, low) + dot(table_low, high)
+    table = jnp.concatenate([inverse_table[column, place] for column, place in places], axis=0)
+    back = dot(table, joined_terms(modes))
     return back.reshape(shape)
 
 
@@ -366,10 +371,8 @@
     half = layers // 2
     block_refs = refs[:layers]
     far_arrived, near_arrived = refs[layers : layers + 2]
-    weight_ref, forward_high, forward_low, inverse_high, inverse_low = refs[
-        layers + 2 : layers + 7
-    ]
-    modes_ref, far_ref, near_ref, order_ref, spread_ref, result_ref = refs[layers + 7 :]
+    weight_ref, forward_table, inverse_table = refs[layers + 2 : layers + 5]
+    modes_ref, far_ref, near_ref, order_ref, spread_ref, result_ref = refs[layers + 5 :]
     z, x, y = quad()
     column = column_of(x, y)
     for index, turn in enumerate(turns(layers)):
@@ -381,10 +384,7 @@
     channels = weight_ref.shape[2]
     tiles = feat_count // 128
     group = 2 * tiles
-    high, low = split_terms(order_ref[...].reshape(-1, feat_count))
-    spectrum = (
-        dot(forward_high[...], high) + dot(forward_high[...], low) + dot(forward_low[...], high)
-    )
+    spectrum = dot(forward_table[...], joined_terms(order_ref[...].reshape(-1, feat_count)))
     for part in range(2):
         for tile in range(tiles):
             spread_ref[pl.ds(part * tiles + tile, count, stride=group), :] = spectrum[
@@ -418,12 +418,12 @@
                 result_ref[pl.ds(part * tiles + tile, count, stride=group), :]
             )
     shape = (layers,) + far_ref.shape[1:]
-    send = back_rows(inverse_high, inverse_low, modes_ref[...], shape, 1)
+    send = back_rows(inverse_table, modes_ref[...], shape, 1)
     far_ref[...] = send[: layers // 2]
     near_ref[...] = send[layers // 2 :]
 
 
-def mix(blocks, arrived, weights, forward_table, inverse_tables):
+def mix(blocks, arrived, weights, forward_table, inverse_table):
     layers = len(blocks)
     _, rows, feat_count = blocks[0].shape
     count = weights.shape[1]
@@ -438,24 +438,24 @@
         scratch_shapes=[pltpu.VMEM((2 * layers, rows, feat_count), jnp.float32), scratch, scratch],
         compiler_params=SMALL,
         name="mix",
-    )(*blocks, *arrived, weights, *split_table(forward_table), *inverse_tables)
-
-
-def keep_kernel(modes_ref, inverse_high, inverse_low, far_ref, near_ref):
+    )(*blocks, *arrived, weights, joined_table(forward_table), inverse_table)
+
+
+def keep_kernel(modes_ref, inverse_table, far_ref, near_ref):
     half = far_ref.shape[0]
     shape = (2 * half,) + far_ref.shape[1:]
-    keep = back_rows(inverse_high, inverse_low, modes_ref[...], shape, 0)
+    keep = back_rows(inverse_table, modes_ref[...], shape, 0)
     far_ref[...] = keep[:half]
     near_ref[...] = keep[half:]
 
 
-def keep_rows(modes, inverse_tables, like):
+def keep_rows(modes, inverse_table, like):
     return pl.pallas_call(
         keep_kernel,
         out_shape=[jax.ShapeDtypeStruct(like.shape, jnp.float32)] * 2,
         compiler_params=SMALL,
         name="keep_rows",
-    )(modes, *inverse_tables)
+    )(modes, inverse_table)
 
 
 def gelu(half):
@@ -565,16 +565,16 @@
     near = along_columns(add_blocks(keep_near, flip_core(send_near)), peers, order[middle:])
     far = along_columns(add_blocks(keep_far, flip_core(send_far)), peers, order[:middle])
     blocks = far + near
-    inverse_tables = split_table(inverse_x_table(cells_x, peers, rows_ky))
+    inverse_table = joined_table(inverse_x_table(cells_x, peers, rows_ky))
     modes, send_far, send_near = mix(
         blocks,
         [flip_core(second_halves(far)), flip_core(second_halves(near))],
         spectral_weight,
         forward_x_table(cells_x, peers, rows_ky) * forward_scale,
-        inverse_tables,
+        inverse_table,
     )
     arrived_near, arrived_far = flip_core(send_near), flip_core(send_far)
-    keep_far, keep_near = keep_rows(modes, inverse_tables, send_far)
+    keep_far, keep_near = keep_rows(modes, inverse_table, send_far)
     order = turns(peers // 2, True)
     own_near = along_columns(join_blocks(keep_near, arrived_near, cells_x), peers, order[middle:])
     own_far = along_columns(join_blocks(keep_far, arrived_far, cells_x), peers, order[:middle])

time: 33.4 us -> 33.4 us (level)
  no operation moved by 1% of the time
where the time goes in v34:
time: 33.4 us; the launch traced here: 33.2 us
  starting transfers between devices  13.6 us (41%)
  waiting for transfers between devices  13.5 us (40%)
  Pallas kernels  5.3 us (16%)
  between operations  0.77 us (2%)
    ppermute x8, starting transfers between devices, along_columns(): arrived.append(lax.ppermute(block, ('gx', 'gy'), pairs))  11 us
    ppermute x8, waiting for transfers between devices, along_columns(): arrived.append(lax.ppermute(block, ('gx', 'gy'), pairs))  10.1 us
    ppermute x8, waiting for transfers between devices, flip_core(): return lax.ppermute(block, 'gy', [(0, 1), (1, 0)])  3.39 us
    ppermute x8, starting transfers between devices, flip_core(): return lax.ppermute(block, 'gy', [(0, 1), (1, 0)])  2.64 us
    pallas_call x1, Pallas kernels, make_output(): pl.pallas_call(functools.partial(output_kernel, layers), out_specs=[pl.Bl...  2.26 us
    pallas_call x1, Pallas kernels, forward_y(): pl.pallas_call(functools.partial(forward_y_kernel, extent, rows_ky), in_s...  1.75 us
    pallas_call x1, Pallas kernels, mix(): pl.pallas_call(functools.partial(mix_kernel, layers), out_shape=[jax.Shap...  1 us
  transfers between devices with their start and end apart: 16, of which 9 were waited for; matrix products, arithmetic and copies ran while one was open for 0% of the time, Pallas kernels for 1%

profile of v34, /device:TPU:0, one launch (start us, length us, event | category | flops | bytes accessed | tf_op | source)
XLA Modules:
  0.0 33.2 jit_solution(4292010292296198026)
XLA Ops:
  0.6 1.7 %forward_y.1 = (f32[2,2,16,512]{3,2,1,0:T(8,128)S(1)}, f32[2,2,16,512]{3,2,1,0:T(8,128)S(1)}, f32[2,2,16,512]{3,2,1,0:T(8,128)S(1)}, f32[2,2,16,512]{3,2,1,0:T(8,128)S(1)}) custom-call(bf16[4,256,512]{2,1,0:T(8,128)(2,1)} %flow_ref.1), custom_call_target="tpu_custom_call" | custom-call | tf_op jit(solution)/shard_map/forward_y/pallas_call | solution.py:282
  2.4 0.5 %collective-permute-start = (f32[2,2,16,512]{3,2,1,0:T(8,128)S(1)}, f32[2,2,16,512]{3,2,1,0:T(8,128)S(1)}, u32[]{:S(2)}, u32[]{:S(2)}) collective-permute-start(f32[2,2,16,512]{3,2,1,0:T(8,128)S(1)} %get-tuple-element.20), channel_id=1, source_target_pairs={{0,1},{1,0},{2,3},{3,2},{4,5},{5,4},{6,7},{7,6},{8,9},{9,8},{10,11... | collective-permute-start | bytes 393224 | tf_op jit(solution)/shard_map/ppermute | solution.py:296
  3.0 0.9 %collective-permute-done.arrived_ref = f32[2,2,16,512]{3,2,1,0:T(8,128)S(1)} collective-permute-done((f32[2,2,16,512]{3,2,1,0:T(8,128)S(1)}, f32[2,2,16,512]{3,2,1,0:T(8,128)S(1)}, u32[]{:S(2)}, u32[]{:S(2)}) %collective-permute-start) | collective-permute-done | bytes 131104 | tf_op jit(solution)/shard_map/ppermute | solution.py:296
  3.9 5.0 %collective-permute-start.1 = (f32[2,16,512]{2,1,0:T(8,128)S(1)}, f32[2,16,512]{2,1,0:T(8,128)S(1)}, u32[]{:S(2)}, u32[]{:S(2)}) collective-permute-start(f32[2,16,512]{2,1,0:T(8,128)S(1)} %get-tuple-element.21), channel_id=1, source_target_pairs={{0,12},{1,15},{2,14},{3,13},{4,8},{5,11},{6,10},{7,9},{8,4},{9,7},... | collective-permute-start | bytes 196616 | tf_op jit(solution)/shard_map/ppermute | solution.py:307
  9.0 0.7 %collective-permute-start.4 = (f32[2,16,512]{2,1,0:T(8,128)S(1)}, f32[2,16,512]{2,1,0:T(8,128)S(1)}, u32[]{:S(2)}, u32[]{:S(2)}) collective-permute-start(f32[2,16,512]{2,1,0:T(8,128)S(1)} %get-tuple-element.25), channel_id=1, source_target_pairs={{0,4},{1,7},{2,6},{3,5},{4,0},{5,3},{6,2},{7,1},{8,12},{9,15},{10,... | collective-permute-start | bytes 196616 | tf_op jit(solution)/shard_map/ppermute | solution.py:307
  9.7 0.7 %collective-permute-start.5 = (f32[2,16,512]{2,1,0:T(8,128)S(1)}, f32[2,16,512]{2,1,0:T(8,128)S(1)}, u32[]{:S(2)}, u32[]{:S(2)}) collective-permute-start(f32[2,16,512]{2,1,0:T(8,128)S(1)} %get-tuple-element.26), channel_id=1, source_target_pairs={{0,0},{1,3},{2,2},{3,1},{4,4},{5,7},{6,6},{7,5},{8,8},{9,11},{10,1... | collective-permute-start | bytes 196616 | tf_op jit(solution)/shard_map/ppermute | solution.py:307
  10.3 1.3 %collective-permute-done.1.refs_0_ = f32[2,16,512]{2,1,0:T(8,128)S(1)} collective-permute-done((f32[2,16,512]{2,1,0:T(8,128)S(1)}, f32[2,16,512]{2,1,0:T(8,128)S(1)}, u32[]{:S(2)}, u32[]{:S(2)}) %collective-permute-start.1) | collective-permute-done | bytes 65568 | tf_op jit(solution)/shard_map/ppermute | solution.py:307
  11.7 3.8 %collective-permute-done.2.refs_1_ = f32[2,16,512]{2,1,0:T(8,128)S(1)} collective-permute-done((f32[2,16,512]{2,1,0:T(8,128)S(1)}, f32[2,16,512]{2,1,0:T(8,128)S(1)}, u32[]{:S(2)}, u32[]{:S(2)}) %collective-permute-start.2) | collective-permute-done | bytes 65568 | tf_op jit(solution)/shard_map/ppermute | solution.py:307
  15.5 0.5 %collective-permute-start.6 = (f32[2,16,512]{2,1,0:T(8,128)S(1)}, f32[2,16,512]{2,1,0:T(8,128)S(1)}, u32[]{:S(2)}, u32[]{:S(2)}) collective-permute-start(f32[2,16,512]{2,1,0:T(8,128)S(1)} %second_halves.2), channel_id=1, source_target_pairs={{0,1},{1,0},{2,3},{3,2},{4,5},{5,4},{6,7},{7,6},{8,9},{9,8},{10,11... | collective-permute-start | bytes 196616 | tf_op jit(solution)/shard_map/ppermute | solution.py:296
  15.9 0.4 %collective-permute-start.7 = (f32[2,16,512]{2,1,0:T(8,128)S(1)}, f32[2,16,512]{2,1,0:T(8,128)S(1)}, u32[]{:S(2)}, u32[]{:S(2)}) collective-permute-start(f32[2,16,512]{2,1,0:T(8,128)S(1)} %second_halves.3), channel_id=1, source_target_pairs={{0,1},{1,0},{2,3},{3,2},{4,5},{5,4},{6,7},{7,6},{8,9},{9,8},{10,11... | collective-permute-start | bytes 196616 | tf_op jit(solution)/shard_map/ppermute | solution.py:296
  16.3 0.5 %collective-permute-done.6.refs_4_ = f32[2,16,512]{2,1,0:T(8,128)S(1)} collective-permute-done((f32[2,16,512]{2,1,0:T(8,128)S(1)}, f32[2,16,512]{2,1,0:T(8,128)S(1)}, u32[]{:S(2)}, u32[]{:S(2)}) %collective-permute-start.6) | collective-permute-done | bytes 65568 | tf_op jit(solution)/shard_map/ppermute | solution.py:296
  16.8 0.4 %collective-permute-done.7.refs_5_ = f32[2,16,512]{2,1,0:T(8,128)S(1)} collective-permute-done((f32[2,16,512]{2,1,0:T(8,128)S(1)}, f32[2,16,512]{2,1,0:T(8,128)S(1)}, u32[]{:S(2)}, u32[]{:S(2)}) %collective-permute-start.7) | collective-permute-done | bytes 65568 | tf_op jit(solution)/shard_map/ppermute | solution.py:296
  17.3 1.0 %mix.1 = (f32[128,512]{1,0:T(8,128)S(1)}, f32[2,16,512]{2,1,0:T(8,128)S(1)}, f32[2,16,512]{2,1,0:T(8,128)S(1)}) custom-call(f32[2,16,512]{2,1,0:T(8,128)S(1)} %collective-permute-done.1.refs_0_, f32[2,16,512]{2,1,0:T(8,128)S(1)} %collective-permute-done.2.refs_1_, f32[2,16,512]{2,1,0:T(8,128)S(1)} %collective-permute-done.4.refs_0_.refs_2_, ...), custom_call_target="tpu_custom_call" | custom-call | tf_op jit(solution)/shard_map/mix/pallas_call | solution.py:431
  18.3 0.4 %collective-permute-start.11 = (f32[2,16,512]{2,1,0:T(8,128)S(1)}, f32[2,16,512]{2,1,0:T(8,128)S(1)}, u32[]{:S(2)}, u32[]{:S(2)}) collective-permute-start(f32[2,16,512]{2,1,0:T(8,128)S(1)} %get-tuple-element.33), channel_id=1, source_target_pairs={{0,1},{1,0},{2,3},{3,2},{4,5},{5,4},{6,7},{7,6},{8,9},{9,8},{10,11... | collective-permute-start | bytes 196616 | tf_op jit(solution)/shard_map/ppermute | solution.py:296
  19.1 0.5 %collective-permute-done.11.arrived_ref = f32[2,16,512]{2,1,0:T(8,128)S(1)} collective-permute-done((f32[2,16,512]{2,1,0:T(8,128)S(1)}, f32[2,16,512]{2,1,0:T(8,128)S(1)}, u32[]{:S(2)}, u32[]{:S(2)}) %collective-permute-start.11) | collective-permute-done | bytes 65568 | tf_op jit(solution)/shard_map/ppermute | solution.py:296
  19.6 1.4 %collective-permute-start.12 = (f32[4,8,512]{2,1,0:T(8,128)S(1)}, f32[4,8,512]{2,1,0:T(8,128)S(1)}, u32[]{:S(2)}, u32[]{:S(2)}) collective-permute-start(f32[4,8,512]{2,1,0:T(8,128)S(1)} %get-tuple-element.34), channel_id=1, source_target_pairs={{0,8},{1,11},{2,10},{3,9},{4,12},{5,15},{6,14},{7,13},{8,0},{9,3},... | collective-permute-start | bytes 196616 | tf_op jit(solution)/shard_map/ppermute | solution.py:307
  21.0 2.0 %collective-permute-start.13 = (f32[4,8,512]{2,1,0:T(8,128)S(1)}, f32[4,8,512]{2,1,0:T(8,128)S(1)}, u32[]{:S(2)}, u32[]{:S(2)}) collective-permute-start(f32[4,8,512]{2,1,0:T(8,128)S(1)} %get-tuple-element.35), channel_id=1, source_target_pairs={{0,12},{1,15},{2,14},{3,13},{4,8},{5,11},{6,10},{7,9},{8,4},{9,7},... | collective-permute-start | bytes 196616 | tf_op jit(solution)/shard_map/ppermute | solution.py:307
  23.1 0.6 %collective-permute-start.9 = (f32[4,8,512]{2,1,0:T(8,128)S(1)}, f32[4,8,512]{2,1,0:T(8,128)S(1)}, u32[]{:S(2)}, u32[]{:S(2)}) collective-permute-start(f32[4,8,512]{2,1,0:T(8,128)S(1)} %get-tuple-element.30), channel_id=1, source_target_pairs={{0,4},{1,7},{2,6},{3,5},{4,0},{5,3},{6,2},{7,1},{8,12},{9,15},{10,... | collective-permute-start | bytes 196616 | tf_op jit(solution)/shard_map/ppermute | solution.py:307
  23.6 0.7 %collective-permute-start.10 = (f32[4,8,512]{2,1,0:T(8,128)S(1)}, f32[4,8,512]{2,1,0:T(8,128)S(1)}, u32[]{:S(2)}, u32[]{:S(2)}) collective-permute-start(f32[4,8,512]{2,1,0:T(8,128)S(1)} %get-tuple-element.31), channel_id=1, source_target_pairs={{0,0},{1,3},{2,2},{3,1},{4,4},{5,7},{6,6},{7,5},{8,8},{9,11},{10,1... | collective-permute-start | bytes 196616 | tf_op jit(solution)/shard_map/ppermute | solution.py:307
  24.3 4.1 %collective-permute-done.12.refs_0_.refs_2_ = f32[4,8,512]{2,1,0:T(8,128)S(1)} collective-permute-done((f32[4,8,512]{2,1,0:T(8,128)S(1)}, f32[4,8,512]{2,1,0:T(8,128)S(1)}, u32[]{:S(2)}, u32[]{:S(2)}) %collective-permute-start.12) | collective-permute-done | bytes 65568 | tf_op jit(solution)/shard_map/ppermute | solution.py:307
  28.6 0.9 %collective-permute-done.9.refs_0_ = f32[4,8,512]{2,1,0:T(8,128)S(1)} collective-permute-done((f32[4,8,512]{2,1,0:T(8,128)S(1)}, f32[4,8,512]{2,1,0:T(8,128)S(1)}, u32[]{:S(2)}, u32[]{:S(2)}) %collective-permute-start.9) | collective-permute-done | bytes 65568 | tf_op jit(solution)/shard_map/ppermute | solution.py:307
  29.5 0.5 %collective-permute-start.14 = (f32[2,4,8,512]{3,2,1,0:T(8,128)S(1)}, f32[2,4,8,512]{3,2,1,0:T(8,128)S(1)}, u32[]{:S(2)}, u32[]{:S(2)}) collective-permute-start(f32[2,4,8,512]{3,2,1,0:T(8,128)S(1)} %stack_blocks.2), channel_id=1, source_target_pairs={{0,1},{1,0},{2,3},{3,2},{4,5},{5,4},{6,7},{7,6},{8,9},{9,8},{10,11... | collective-permute-start | bytes 393224 | tf_op jit(solution)/shard_map/ppermute | solution.py:296
  30.0 1.0 %collective-permute-done.14.refs_4_ = f32[2,4,8,512]{3,2,1,0:T(8,128)S(1)} collective-permute-done((f32[2,4,8,512]{3,2,1,0:T(8,128)S(1)}, f32[2,4,8,512]{3,2,1,0:T(8,128)S(1)}, u32[]{:S(2)}, u32[]{:S(2)}) %collective-permute-start.14) | collective-permute-done | bytes 131104 | tf_op jit(solution)/shard_map/ppermute | solution.py:296
  31.0 2.3 %make_output.1 = (bf16[4,256,512]{2,1,0:T(8,128)(2,1)}, f32[1,64,1024]{2,1,0:T(8,128)}) custom-call(bf16[4,256,512]{2,1,0:T(8,128)(2,1)S(1)} %copy-done, bf16[2,2,256,256]{3,2,1,0:T(8,128)(2,1)S(1)} %copy-done.2, bf16[64,64]{1,0:T(8,128)(2,1)S(1)} %copy-done.5, f32[64]{0:T(128)S(1)} %copy-done.6, f32[128,512]{1,0:T(8,128)S(1)} %get-tuple-element.27.modes_ref, ...), custom_call_target="tpu_custom_call" | custom-call | tf_op jit(solution)/shard_map/make_output/pallas_call | solution.py:533
  (34 shorter events, 0.8 us)
Async XLA Ops:
  0.6 16.6 %copy-start.1 = (bf16[1,64,64,128]{3,2,1,0:T(8,128)(2,1)S(1)}, bf16[1,64,64,128]{3,2,1,0:T(8,128)(2,1)}, u32[]{:S(2)}) copy-start(bf16[1,64,64,128]{3,2,1,0:T(8,128)(2,1)} %refs_6_.1) | copy-start | bytes 3145732
  2.4 1.5 %collective-permute-start = (f32[2,2,16,512]{3,2,1,0:T(8,128)S(1)}, f32[2,2,16,512]{3,2,1,0:T(8,128)S(1)}, u32[]{:S(2)}, u32[]{:S(2)}) collective-permute-start(f32[2,2,16,512]{3,2,1,0:T(8,128)S(1)} %get-tuple-element.20), channel_id=1, source_target_pairs={{0,1},{1,0},{2,3},{3,2},{4,5},{5,4},{6,7},{7,6},{8,9},{9,8},{10,11... | collective-permute-start | bytes 393224 | tf_op jit(solution)/shard_map/ppermute | solution.py:296
  2.9 6.0 %collective-permute-start.3 = (f32[2,2,16,512]{3,2,1,0:T(8,128)S(1)}, f32[2,2,16,512]{3,2,1,0:T(8,128)S(1)}, u32[]{:S(2)}, u32[]{:S(2)}) collective-permute-start(f32[2,2,16,512]{3,2,1,0:T(8,128)S(1)} %get-tuple-element.24), channel_id=1, source_target_pairs={{0,1},{1,0},{2,3},{3,2},{4,5},{5,4},{6,7},{7,6},{8,9},{9,8},{10,11... | collective-permute-start | bytes 393224 | tf_op jit(solution)/shard_map/ppermute | solution.py:296
  3.9 7.8 %collective-permute-start.1 = (f32[2,16,512]{2,1,0:T(8,128)S(1)}, f32[2,16,512]{2,1,0:T(8,128)S(1)}, u32[]{:S(2)}, u32[]{:S(2)}) collective-permute-start(f32[2,16,512]{2,1,0:T(8,128)S(1)} %get-tuple-element.21), channel_id=1, source_target_pairs={{0,12},{1,15},{2,14},{3,13},{4,8},{5,11},{6,10},{7,9},{8,4},{9,7},... | collective-permute-start | bytes 196616 | tf_op jit(solution)/shard_map/ppermute | solution.py:307
  8.9 6.5 %collective-permute-start.2 = (f32[2,16,512]{2,1,0:T(8,128)S(1)}, f32[2,16,512]{2,1,0:T(8,128)S(1)}, u32[]{:S(2)}, u32[]{:S(2)}) collective-permute-start(f32[2,16,512]{2,1,0:T(8,128)S(1)} %get-tuple-element.22), channel_id=1, source_target_pairs={{0,8},{1,11},{2,10},{3,9},{4,12},{5,15},{6,14},{7,13},{8,0},{9,3},... | collective-permute-start | bytes 196616 | tf_op jit(solution)/shard_map/ppermute | solution.py:307
  9.0 7.0 %collective-permute-start.4 = (f32[2,16,512]{2,1,0:T(8,128)S(1)}, f32[2,16,512]{2,1,0:T(8,128)S(1)}, u32[]{:S(2)}, u32[]{:S(2)}) collective-permute-start(f32[2,16,512]{2,1,0:T(8,128)S(1)} %get-tuple-element.25), channel_id=1, source_target_pairs={{0,4},{1,7},{2,6},{3,5},{4,0},{5,3},{6,2},{7,1},{8,12},{9,15},{10,... | collective-permute-start | bytes 196616 | tf_op jit(solution)/shard_map/ppermute | solution.py:307
  9.7 6.3 %collective-permute-start.5 = (f32[2,16,512]{2,1,0:T(8,128)S(1)}, f32[2,16,512]{2,1,0:T(8,128)S(1)}, u32[]{:S(2)}, u32[]{:S(2)}) collective-permute-start(f32[2,16,512]{2,1,0:T(8,128)S(1)} %get-tuple-element.26), channel_id=1, source_target_pairs={{0,0},{1,3},{2,2},{3,1},{4,4},{5,7},{6,6},{7,5},{8,8},{9,11},{10,1... | collective-permute-start | bytes 196616 | tf_op jit(solution)/shard_map/ppermute | solution.py:307
  15.4 1.8 %copy-start.3 = (bf16[2,4,16,384]{3,2,1,0:T(8,128)(2,1)S(1)}, bf16[2,4,16,384]{3,2,1,0:T(8,128)(2,1)}, u32[]{:S(2)}) copy-start(bf16[2,4,16,384]{3,2,1,0:T(8,128)(2,1)} %constant.7.clone.refs_8_.inverse_table) | copy-start | bytes 294916
  15.4 1.8 %copy-start.4 = (bf16[128,384]{1,0:T(8,128)(2,1)S(1)}, bf16[128,384]{1,0:T(8,128)(2,1)}, u32[]{:S(2)}) copy-start(bf16[128,384]{1,0:T(8,128)(2,1)} %constant.6.clone.refs_7_) | copy-start | bytes 294916
  15.5 1.4 %collective-permute-start.6 = (f32[2,16,512]{2,1,0:T(8,128)S(1)}, f32[2,16,512]{2,1,0:T(8,128)S(1)}, u32[]{:S(2)}, u32[]{:S(2)}) collective-permute-start(f32[2,16,512]{2,1,0:T(8,128)S(1)} %second_halves.2), channel_id=1, source_target_pairs={{0,1},{1,0},{2,3},{3,2},{4,5},{5,4},{6,7},{7,6},{8,9},{9,8},{10,11... | collective-permute-start | bytes 196616 | tf_op jit(solution)/shard_map/ppermute | solution.py:296
  15.9 15.0 %copy-start = (bf16[4,256,512]{2,1,0:T(8,128)(2,1)S(1)}, bf16[4,256,512]{2,1,0:T(8,128)(2,1)}, u32[]{:S(2)}) copy-start(bf16[4,256,512]{2,1,0:T(8,128)(2,1)} %flow_ref.1) | copy-start | bytes 3145732
  15.9 1.3 %collective-permute-start.7 = (f32[2,16,512]{2,1,0:T(8,128)S(1)}, f32[2,16,512]{2,1,0:T(8,128)S(1)}, u32[]{:S(2)}, u32[]{:S(2)}) collective-permute-start(f32[2,16,512]{2,1,0:T(8,128)S(1)} %second_halves.3), channel_id=1, source_target_pairs={{0,1},{1,0},{2,3},{3,2},{4,5},{5,4},{6,7},{7,6},{8,9},{9,8},{10,11... | collective-permute-start | bytes 196616 | tf_op jit(solution)/shard_map/ppermute | solution.py:296
  18.3 1.3 %collective-permute-start.11 = (f32[2,16,512]{2,1,0:T(8,128)S(1)}, f32[2,16,512]{2,1,0:T(8,128)S(1)}, u32[]{:S(2)}, u32[]{:S(2)}) collective-permute-start(f32[2,16,512]{2,1,0:T(8,128)S(1)} %get-tuple-element.33), channel_id=1, source_target_pairs={{0,1},{1,0},{2,3},{3,2},{4,5},{5,4},{6,7},{7,6},{8,9},{9,8},{10,11... | collective-permute-start | bytes 196616 | tf_op jit(solution)/shard_map/ppermute | solution.py:296
  18.7 4.4 %collective-permute-start.8 = (f32[2,16,512]{2,1,0:T(8,128)S(1)}, f32[2,16,512]{2,1,0:T(8,128)S(1)}, u32[]{:S(2)}, u32[]{:S(2)}) collective-permute-start(f32[2,16,512]{2,1,0:T(8,128)S(1)} %get-tuple-element.29), channel_id=1, source_target_pairs={{0,1},{1,0},{2,3},{3,2},{4,5},{5,4},{6,7},{7,6},{8,9},{9,8},{10,11... | collective-permute-start | bytes 196616 | tf_op jit(solution)/shard_map/ppermute | solution.py:296
  18.9 12.1 %copy-start.2 = (bf16[2,2,256,256]{3,2,1,0:T(8,128)(2,1)S(1)}, bf16[2,2,256,256]{3,2,1,0:T(8,128)(2,1)}, u32[]{:S(2)}) copy-start(bf16[2,2,256,256]{3,2,1,0:T(8,128)(2,1)} %constant.8.clone.table_ref) | copy-start | bytes 1572868
  19.6 8.7 %collective-permute-start.12 = (f32[4,8,512]{2,1,0:T(8,128)S(1)}, f32[4,8,512]{2,1,0:T(8,128)S(1)}, u32[]{:S(2)}, u32[]{:S(2)}) collective-permute-start(f32[4,8,512]{2,1,0:T(8,128)S(1)} %get-tuple-element.34), channel_id=1, source_target_pairs={{0,8},{1,11},{2,10},{3,9},{4,12},{5,15},{6,14},{7,13},{8,0},{9,3},... | collective-permute-start | bytes 196616 | tf_op jit(solution)/shard_map/ppermute | solution.py:307
  21.0 7.3 %collective-permute-start.13 = (f32[4,8,512]{2,1,0:T(8,128)S(1)}, f32[4,8,512]{2,1,0:T(8,128)S(1)}, u32[]{:S(2)}, u32[]{:S(2)}) collective-permute-start(f32[4,8,512]{2,1,0:T(8,128)S(1)} %get-tuple-element.35), channel_id=1, source_target_pairs={{0,12},{1,15},{2,14},{3,13},{4,8},{5,11},{6,10},{7,9},{8,4},{9,7},... | collective-permute-start | bytes 196616 | tf_op jit(solution)/shard_map/ppermute | solution.py:307
  23.1 6.4 %collective-permute-start.9 = (f32[4,8,512]{2,1,0:T(8,128)S(1)}, f32[4,8,512]{2,1,0:T(8,128)S(1)}, u32[]{:S(2)}, u32[]{:S(2)}) collective-permute-start(f32[4,8,512]{2,1,0:T(8,128)S(1)} %get-tuple-element.30), channel_id=1, source_target_pairs={{0,4},{1,7},{2,6},{3,5},{4,0},{5,3},{6,2},{7,1},{8,12},{9,15},{10,... | collective-permute-start | bytes 196616 | tf_op jit(solution)/shard_map/ppermute | solution.py:307
  23.6 5.9 %collective-permute-start.10 = (f32[4,8,512]{2,1,0:T(8,128)S(1)}, f32[4,8,512]{2,1,0:T(8,128)S(1)}, u32[]{:S(2)}, u32[]{:S(2)}) collective-permute-start(f32[4,8,512]{2,1,0:T(8,128)S(1)} %get-tuple-element.31), channel_id=1, source_target_pairs={{0,0},{1,3},{2,2},{3,1},{4,4},{5,7},{6,6},{7,5},{8,8},{9,11},{10,1... | collective-permute-start | bytes 196616 | tf_op jit(solution)/shard_map/ppermute | solution.py:307
  28.4 2.6 %copy-start.5 = (bf16[64,64]{1,0:T(8,128)(2,1)S(1)}, bf16[64,64]{1,0:T(8,128)(2,1)}, u32[]{:S(2)}) copy-start(bf16[64,64]{1,0:T(8,128)(2,1)} %local_ref.1) | copy-start | bytes 24580
  28.4 2.6 %copy-start.6 = (f32[64]{0:T(128)S(1)}, f32[64]{0:T(128)}, u32[]{:S(2)}) copy-start(f32[64]{0:T(128)} %bias_ref.1) | copy-start | bytes 772
  28.4 1.5 %collective-permute-start.15 = (f32[2,4,8,512]{3,2,1,0:T(8,128)S(1)}, f32[2,4,8,512]{3,2,1,0:T(8,128)S(1)}, u32[]{:S(2)}, u32[]{:S(2)}) collective-permute-start(f32[2,4,8,512]{3,2,1,0:T(8,128)S(1)} %stack_blocks.3), channel_id=1, source_target_pairs={{0,1},{1,0},{2,3},{3,2},{4,5},{5,4},{6,7},{7,6},{8,9},{9,8},{10,11... | collective-permute-start | bytes 393224 | tf_op jit(solution)/shard_map/ppermute | solution.py:296
  29.5 1.4 %collective-permute-start.14 = (f32[2,4,8,512]{3,2,1,0:T(8,128)S(1)}, f32[2,4,8,512]{3,2,1,0:T(8,128)S(1)}, u32[]{:S(2)}, u32[]{:S(2)}) collective-permute-start(f32[2,4,8,512]{3,2,1,0:T(8,128)S(1)} %stack_blocks.2), channel_id=1, source_target_pairs={{0,1},{1,0},{2,3},{3,2},{4,5},{5,4},{6,7},{7,6},{8,9},{9,8},{10,11... | collective-permute-start | bytes 393224 | tf_op jit(solution)/shard_map/ppermute | solution.py:296

commit v35 on v33

--- a/solution.py
+++ b/solution.py
@@ -131,7 +131,6 @@
 WIDTH = 256
 BIAS_TERMS = 3
 LAST = 64
-FIRST = 64
 GELU_TERMS = (
     1.5957645177841187,
     0.29075613617897034,
@@ -350,9 +349,9 @@
     return small_call(join_kernel, [shape] * layers, "join_blocks")(keep, arrived)
 
 
-def back_rows(inverse_high, inverse_low, modes, shape, other):
+def back_rows(inverse_high, inverse_low, modes, chosen, shape, other):
     z, x, y = quad()
-    places = [(column_of(x, y) ^ other, z ^ turn) for turn in turns(shape[0], True)]
+    places = [(column_of(x, y) ^ other, z ^ turn) for turn in chosen]
     table_high, table_low = [
         jnp.concatenate([ref[column, place] for column, place in places], axis=0)
         for ref in (inverse_high, inverse_low)
@@ -369,7 +368,7 @@
     weight_ref, forward_high, forward_low, inverse_high, inverse_low = refs[
         layers + 2 : layers + 7
     ]
-    modes_ref, far_ref, near_ref, order_ref, spread_ref, result_ref = refs[layers + 7 :]
+    modes_ref, far_ref, order_ref, spread_ref, result_ref = refs[layers + 7 :]
     z, x, y = quad()
     column = column_of(x, y)
     for index, turn in enumerate(turns(layers)):
@@ -417,10 +416,10 @@
             modes_ref[part * count : (part + 1) * count, tile * 128 : (tile + 1) * 128] = (
                 result_ref[pl.ds(part * tiles + tile, count, stride=group), :]
             )
-    shape = (layers,) + far_ref.shape[1:]
-    send = back_rows(inverse_high, inverse_low, modes_ref[...], shape, 1)
-    far_ref[...] = send[: layers // 2]
-    near_ref[...] = send[layers // 2 :]
+    chosen = turns(layers, True)[:half]
+    far_ref[...] = back_rows(
+        inverse_high, inverse_low, modes_ref[...], chosen, far_ref.shape, 1
+    )
 
 
 def mix(blocks, arrived, weights, forward_table, inverse_tables):
@@ -433,7 +432,6 @@
         out_shape=[
             jax.ShapeDtypeStruct((2 * count, feat_count), jnp.float32),
             jax.ShapeDtypeStruct((layers // 2, rows, feat_count), jnp.float32),
-            jax.ShapeDtypeStruct((layers // 2, rows, feat_count), jnp.float32),
         ],
         scratch_shapes=[pltpu.VMEM((2 * layers, rows, feat_count), jnp.float32), scratch, scratch],
         compiler_params=SMALL,
@@ -441,10 +439,13 @@
     )(*blocks, *arrived, weights, *split_table(forward_table), *inverse_tables)
 
 
-def keep_kernel(modes_ref, inverse_high, inverse_low, far_ref, near_ref):
+def keep_kernel(modes_ref, inverse_high, inverse_low, far_ref, near_ref, send_ref):
     half = far_ref.shape[0]
+    order = turns(2 * half, True)
+    modes = modes_ref[...]
     shape = (2 * half,) + far_ref.shape[1:]
-    keep = back_rows(inverse_high, inverse_low, modes_ref[...], shape, 0)
+    send_ref[...] = back_rows(inverse_high, inverse_low, modes, order[half:], send_ref.shape, 1)
+    keep = back_rows(inverse_high, inverse_low, modes, order, shape, 0)
     far_ref[...] = keep[:half]
     near_ref[...] = keep[half:]
 
@@ -452,7 +453,7 @@
 def keep_rows(modes, inverse_tables, like):
     return pl.pallas_call(
         keep_kernel,
-        out_shape=[jax.ShapeDtypeStruct(like.shape, jnp.float32)] * 2,
+        out_shape=[jax.ShapeDtypeStruct(like.shape, jnp.float32)] * 3,
         compiler_params=SMALL,
         name="keep_rows",
     )(modes, *inverse_tables)
@@ -566,15 +567,15 @@
     far = along_columns(add_blocks(keep_far, flip_core(send_far)), peers, order[:middle])
     blocks = far + near
     inverse_tables = split_table(inverse_x_table(cells_x, peers, rows_ky))
-    modes, send_far, send_near = mix(
+    modes, send_far = mix(
         blocks,
         [flip_core(second_halves(far)), flip_core(second_halves(near))],
         spectral_weight,
         forward_x_table(cells_x, peers, rows_ky) * forward_scale,
         inverse_tables,
     )
+    keep_far, keep_near, send_near = keep_rows(modes, inverse_tables, send_far)
     arrived_near, arrived_far = flip_core(send_near), flip_core(send_far)
-    keep_far, keep_near = keep_rows(modes, inverse_tables, send_far)
     order = turns(peers // 2, True)
     own_near = along_columns(join_blocks(keep_near, arrived_near, cells_x), peers, order[middle:])
     own_far = along_columns(join_blocks(keep_far, arrived_far, cells_x), peers, order[:middle])

time: 33.4 us -> 33.4 us (level)
  no operation moved by 1% of the time
where the time goes in v35:
time: 33.4 us; the launch traced here: 33.2 us
  starting transfers between devices  13.5 us (40%)
  waiting for transfers between devices  13.4 us (40%)
  Pallas kernels  5.39 us (16%)
  between operations  0.8 us (2%)
    ppermute x8, starting transfers between devices, along_columns(): arrived.append(lax.ppermute(block, ('gx', 'gy'), pairs))  11 us
    ppermute x8, waiting for transfers between devices, along_columns(): arrived.append(lax.ppermute(block, ('gx', 'gy'), pairs))  10.1 us
    ppermute x8, waiting for transfers between devices, flip_core(): return lax.ppermute(block, 'gy', [(0, 1), (1, 0)])  3.28 us
    ppermute x8, starting transfers between devices, flip_core(): return lax.ppermute(block, 'gy', [(0, 1), (1, 0)])  2.58 us
    pallas_call x1, Pallas kernels, make_output(): pl.pallas_call(functools.partial(output_kernel, layers), out_specs=[pl.Bl...  2.26 us
    pallas_call x1, Pallas kernels, forward_y(): pl.pallas_call(functools.partial(forward_y_kernel, extent, rows_ky), in_s...  1.75 us
    pallas_call x1, Pallas kernels, mix(): pl.pallas_call(functools.partial(mix_kernel, layers), out_shape=[jax.Shap...  1.02 us
  transfers between devices with their start and end apart: 16, of which 9 were waited for; matrix products, arithmetic and copies ran while one was open for 0% of the time, Pallas kernels for 1%

profile of v35, /device:TPU:0, one launch (start us, length us, event | category | flops | bytes accessed | tf_op | source)
XLA Modules:
  0.0 33.2 jit_solution(10250785988851478649)
XLA Ops:
  0.6 1.7 %forward_y.1 = (f32[2,2,16,512]{3,2,1,0:T(8,128)S(1)}, f32[2,2,16,512]{3,2,1,0:T(8,128)S(1)}, f32[2,2,16,512]{3,2,1,0:T(8,128)S(1)}, f32[2,2,16,512]{3,2,1,0:T(8,128)S(1)}) custom-call(bf16[4,256,512]{2,1,0:T(8,128)(2,1)} %flow_ref.1), custom_call_target="tpu_custom_call" | custom-call | tf_op jit(solution)/shard_map/forward_y/pallas_call | solution.py:272
  2.4 0.5 %collective-permute-start = (f32[2,2,16,512]{3,2,1,0:T(8,128)S(1)}, f32[2,2,16,512]{3,2,1,0:T(8,128)S(1)}, u32[]{:S(2)}, u32[]{:S(2)}) collective-permute-start(f32[2,2,16,512]{3,2,1,0:T(8,128)S(1)} %get-tuple-element.20), channel_id=1, source_target_pairs={{0,1},{1,0},{2,3},{3,2},{4,5},{5,4},{6,7},{7,6},{8,9},{9,8},{10,11... | collective-permute-start | bytes 393224 | tf_op jit(solution)/shard_map/ppermute | solution.py:286
  3.0 0.9 %collective-permute-done.arrived_ref = f32[2,2,16,512]{3,2,1,0:T(8,128)S(1)} collective-permute-done((f32[2,2,16,512]{3,2,1,0:T(8,128)S(1)}, f32[2,2,16,512]{3,2,1,0:T(8,128)S(1)}, u32[]{:S(2)}, u32[]{:S(2)}) %collective-permute-start) | collective-permute-done | bytes 131104 | tf_op jit(solution)/shard_map/ppermute | solution.py:286
  3.9 5.0 %collective-permute-start.1 = (f32[2,16,512]{2,1,0:T(8,128)S(1)}, f32[2,16,512]{2,1,0:T(8,128)S(1)}, u32[]{:S(2)}, u32[]{:S(2)}) collective-permute-start(f32[2,16,512]{2,1,0:T(8,128)S(1)} %get-tuple-element.21), channel_id=1, source_target_pairs={{0,12},{1,15},{2,14},{3,13},{4,8},{5,11},{6,10},{7,9},{8,4},{9,7},... | collective-permute-start | bytes 196616 | tf_op jit(solution)/shard_map/ppermute | solution.py:297
  9.0 0.7 %collective-permute-start.4 = (f32[2,16,512]{2,1,0:T(8,128)S(1)}, f32[2,16,512]{2,1,0:T(8,128)S(1)}, u32[]{:S(2)}, u32[]{:S(2)}) collective-permute-start(f32[2,16,512]{2,1,0:T(8,128)S(1)} %get-tuple-element.25), channel_id=1, source_target_pairs={{0,4},{1,7},{2,6},{3,5},{4,0},{5,3},{6,2},{7,1},{8,12},{9,15},{10,... | collective-permute-start | bytes 196616 | tf_op jit(solution)/shard_map/ppermute | solution.py:297
  9.7 0.7 %collective-permute-start.5 = (f32[2,16,512]{2,1,0:T(8,128)S(1)}, f32[2,16,512]{2,1,0:T(8,128)S(1)}, u32[]{:S(2)}, u32[]{:S(2)}) collective-permute-start(f32[2,16,512]{2,1,0:T(8,128)S(1)} %get-tuple-element.26), channel_id=1, source_target_pairs={{0,0},{1,3},{2,2},{3,1},{4,4},{5,7},{6,6},{7,5},{8,8},{9,11},{10,1... | collective-permute-start | bytes 196616 | tf_op jit(solution)/shard_map/ppermute | solution.py:297
  10.3 1.3 %collective-permute-done.1.refs_0_ = f32[2,16,512]{2,1,0:T(8,128)S(1)} collective-permute-done((f32[2,16,512]{2,1,0:T(8,128)S(1)}, f32[2,16,512]{2,1,0:T(8,128)S(1)}, u32[]{:S(2)}, u32[]{:S(2)}) %collective-permute-start.1) | collective-permute-done | bytes 65568 | tf_op jit(solution)/shard_map/ppermute | solution.py:297
  11.7 3.8 %collective-permute-done.2.refs_1_ = f32[2,16,512]{2,1,0:T(8,128)S(1)} collective-permute-done((f32[2,16,512]{2,1,0:T(8,128)S(1)}, f32[2,16,512]{2,1,0:T(8,128)S(1)}, u32[]{:S(2)}, u32[]{:S(2)}) %collective-permute-start.2) | collective-permute-done | bytes 65568 | tf_op jit(solution)/shard_map/ppermute | solution.py:297
  15.5 0.5 %collective-permute-start.6 = (f32[2,16,512]{2,1,0:T(8,128)S(1)}, f32[2,16,512]{2,1,0:T(8,128)S(1)}, u32[]{:S(2)}, u32[]{:S(2)}) collective-permute-start(f32[2,16,512]{2,1,0:T(8,128)S(1)} %second_halves.2), channel_id=1, source_target_pairs={{0,1},{1,0},{2,3},{3,2},{4,5},{5,4},{6,7},{7,6},{8,9},{9,8},{10,11... | collective-permute-start | bytes 196616 | tf_op jit(solution)/shard_map/ppermute | solution.py:286
  16.0 0.3 %collective-permute-start.7 = (f32[2,16,512]{2,1,0:T(8,128)S(1)}, f32[2,16,512]{2,1,0:T(8,128)S(1)}, u32[]{:S(2)}, u32[]{:S(2)}) collective-permute-start(f32[2,16,512]{2,1,0:T(8,128)S(1)} %second_halves.3), channel_id=1, source_target_pairs={{0,1},{1,0},{2,3},{3,2},{4,5},{5,4},{6,7},{7,6},{8,9},{9,8},{10,11... | collective-permute-start | bytes 196616 | tf_op jit(solution)/shard_map/ppermute | solution.py:286
  16.3 0.5 %collective-permute-done.6.refs_4_ = f32[2,16,512]{2,1,0:T(8,128)S(1)} collective-permute-done((f32[2,16,512]{2,1,0:T(8,128)S(1)}, f32[2,16,512]{2,1,0:T(8,128)S(1)}, u32[]{:S(2)}, u32[]{:S(2)}) %collective-permute-start.6) | collective-permute-done | bytes 65568 | tf_op jit(solution)/shard_map/ppermute | solution.py:286
  16.8 0.4 %collective-permute-done.7.refs_5_ = f32[2,16,512]{2,1,0:T(8,128)S(1)} collective-permute-done((f32[2,16,512]{2,1,0:T(8,128)S(1)}, f32[2,16,512]{2,1,0:T(8,128)S(1)}, u32[]{:S(2)}, u32[]{:S(2)}) %collective-permute-start.7) | collective-permute-done | bytes 65568 | tf_op jit(solution)/shard_map/ppermute | solution.py:286
  17.3 1.0 %mix.1 = (f32[128,512]{1,0:T(8,128)S(1)}, f32[2,16,512]{2,1,0:T(8,128)S(1)}) custom-call(f32[2,16,512]{2,1,0:T(8,128)S(1)} %collective-permute-done.1.refs_0_, f32[2,16,512]{2,1,0:T(8,128)S(1)} %collective-permute-done.2.refs_1_, f32[2,16,512]{2,1,0:T(8,128)S(1)} %collective-permute-done.4.refs_0_.refs_2_, ...), custom_call_target="tpu_custom_call" | custom-call | tf_op jit(solution)/shard_map/mix/pallas_call | solution.py:430
  18.3 0.3 collective-permute-start.11
  19.2 0.4 %collective-permute-done.11.arrived_ref = f32[2,16,512]{2,1,0:T(8,128)S(1)} collective-permute-done((f32[2,16,512]{2,1,0:T(8,128)S(1)}, f32[2,16,512]{2,1,0:T(8,128)S(1)}, u32[]{:S(2)}, u32[]{:S(2)}) %collective-permute-start.11) | collective-permute-done | bytes 65568 | tf_op jit(solution)/shard_map/ppermute | solution.py:286
  19.6 1.4 %collective-permute-start.12 = (f32[4,8,512]{2,1,0:T(8,128)S(1)}, f32[4,8,512]{2,1,0:T(8,128)S(1)}, u32[]{:S(2)}, u32[]{:S(2)}) collective-permute-start(f32[4,8,512]{2,1,0:T(8,128)S(1)} %get-tuple-element.34), channel_id=1, source_target_pairs={{0,8},{1,11},{2,10},{3,9},{4,12},{5,15},{6,14},{7,13},{8,0},{9,3},... | collective-permute-start | bytes 196616 | tf_op jit(solution)/shard_map/ppermute | solution.py:297
  21.0 2.0 %collective-permute-start.13 = (f32[4,8,512]{2,1,0:T(8,128)S(1)}, f32[4,8,512]{2,1,0:T(8,128)S(1)}, u32[]{:S(2)}, u32[]{:S(2)}) collective-permute-start(f32[4,8,512]{2,1,0:T(8,128)S(1)} %get-tuple-element.35), channel_id=1, source_target_pairs={{0,12},{1,15},{2,14},{3,13},{4,8},{5,11},{6,10},{7,9},{8,4},{9,7},... | collective-permute-start | bytes 196616 | tf_op jit(solution)/shard_map/ppermute | solution.py:297
  23.0 0.6 %collective-permute-start.9 = (f32[4,8,512]{2,1,0:T(8,128)S(1)}, f32[4,8,512]{2,1,0:T(8,128)S(1)}, u32[]{:S(2)}, u32[]{:S(2)}) collective-permute-start(f32[4,8,512]{2,1,0:T(8,128)S(1)} %get-tuple-element.30), channel_id=1, source_target_pairs={{0,4},{1,7},{2,6},{3,5},{4,0},{5,3},{6,2},{7,1},{8,12},{9,15},{10,... | collective-permute-start | bytes 196616 | tf_op jit(solution)/shard_map/ppermute | solution.py:297
  23.6 0.7 %collective-permute-start.10 = (f32[4,8,512]{2,1,0:T(8,128)S(1)}, f32[4,8,512]{2,1,0:T(8,128)S(1)}, u32[]{:S(2)}, u32[]{:S(2)}) collective-permute-start(f32[4,8,512]{2,1,0:T(8,128)S(1)} %get-tuple-element.31), channel_id=1, source_target_pairs={{0,0},{1,3},{2,2},{3,1},{4,4},{5,7},{6,6},{7,5},{8,8},{9,11},{10,1... | collective-permute-start | bytes 196616 | tf_op jit(solution)/shard_map/ppermute | solution.py:297
  24.3 4.1 %collective-permute-done.12.refs_0_.refs_2_ = f32[4,8,512]{2,1,0:T(8,128)S(1)} collective-permute-done((f32[4,8,512]{2,1,0:T(8,128)S(1)}, f32[4,8,512]{2,1,0:T(8,128)S(1)}, u32[]{:S(2)}, u32[]{:S(2)}) %collective-permute-start.12) | collective-permute-done | bytes 65568 | tf_op jit(solution)/shard_map/ppermute | solution.py:297
  28.6 0.9 %collective-permute-done.9.refs_0_ = f32[4,8,512]{2,1,0:T(8,128)S(1)} collective-permute-done((f32[4,8,512]{2,1,0:T(8,128)S(1)}, f32[4,8,512]{2,1,0:T(8,128)S(1)}, u32[]{:S(2)}, u32[]{:S(2)}) %collective-permute-start.9) | collective-permute-done | bytes 65568 | tf_op jit(solution)/shard_map/ppermute | solution.py:297
  29.5 0.4 %collective-permute-start.14 = (f32[2,4,8,512]{3,2,1,0:T(8,128)S(1)}, f32[2,4,8,512]{3,2,1,0:T(8,128)S(1)}, u32[]{:S(2)}, u32[]{:S(2)}) collective-permute-start(f32[2,4,8,512]{3,2,1,0:T(8,128)S(1)} %stack_blocks.2), channel_id=1, source_target_pairs={{0,1},{1,0},{2,3},{3,2},{4,5},{5,4},{6,7},{7,6},{8,9},{9,8},{10,11... | collective-permute-start | bytes 393224 | tf_op jit(solution)/shard_map/ppermute | solution.py:286
  29.9 1.0 %collective-permute-done.14.refs_4_ = f32[2,4,8,512]{3,2,1,0:T(8,128)S(1)} collective-permute-done((f32[2,4,8,512]{3,2,1,0:T(8,128)S(1)}, f32[2,4,8,512]{3,2,1,0:T(8,128)S(1)}, u32[]{:S(2)}, u32[]{:S(2)}) %collective-permute-start.14) | collective-permute-done | bytes 131104 | tf_op jit(solution)/shard_map/ppermute | solution.py:286
  30.9 2.3 %make_output.1 = (bf16[4,256,512]{2,1,0:T(8,128)(2,1)}, f32[1,64,1024]{2,1,0:T(8,128)}) custom-call(bf16[4,256,512]{2,1,0:T(8,128)(2,1)S(1)} %copy-done, bf16[2,2,256,256]{3,2,1,0:T(8,128)(2,1)S(1)} %copy-done.2, bf16[64,64]{1,0:T(8,128)(2,1)S(1)} %copy-done.7, f32[64]{0:T(128)S(1)} %copy-done.8, f32[128,512]{1,0:T(8,128)S(1)} %get-tuple-element.27.modes_ref, ...), custom_call_target="tpu_custom_call" | custom-call | tf_op jit(solution)/shard_map/make_output/pallas_call | solution.py:534
  (38 shorter events, 1.0 us)
Async XLA Ops:
  0.6 16.7 %copy-start.1 = (bf16[1,64,64,128]{3,2,1,0:T(8,128)(2,1)S(1)}, bf16[1,64,64,128]{3,2,1,0:T(8,128)(2,1)}, u32[]{:S(2)}) copy-start(bf16[1,64,64,128]{3,2,1,0:T(8,128)(2,1)} %refs_6_.1) | copy-start | bytes 3145732
  2.4 1.5 %collective-permute-start = (f32[2,2,16,512]{3,2,1,0:T(8,128)S(1)}, f32[2,2,16,512]{3,2,1,0:T(8,128)S(1)}, u32[]{:S(2)}, u32[]{:S(2)}) collective-permute-start(f32[2,2,16,512]{3,2,1,0:T(8,128)S(1)} %get-tuple-element.20), channel_id=1, source_target_pairs={{0,1},{1,0},{2,3},{3,2},{4,5},{5,4},{6,7},{7,6},{8,9},{9,8},{10,11... | collective-permute-start | bytes 393224 | tf_op jit(solution)/shard_map/ppermute | solution.py:286
  2.9 6.0 %collective-permute-start.3 = (f32[2,2,16,512]{3,2,1,0:T(8,128)S(1)}, f32[2,2,16,512]{3,2,1,0:T(8,128)S(1)}, u32[]{:S(2)}, u32[]{:S(2)}) collective-permute-start(f32[2,2,16,512]{3,2,1,0:T(8,128)S(1)} %get-tuple-element.24), channel_id=1, source_target_pairs={{0,1},{1,0},{2,3},{3,2},{4,5},{5,4},{6,7},{7,6},{8,9},{9,8},{10,11... | collective-permute-start | bytes 393224 | tf_op jit(solution)/shard_map/ppermute | solution.py:286
  3.9 7.8 %collective-permute-start.1 = (f32[2,16,512]{2,1,0:T(8,128)S(1)}, f32[2,16,512]{2,1,0:T(8,128)S(1)}, u32[]{:S(2)}, u32[]{:S(2)}) collective-permute-start(f32[2,16,512]{2,1,0:T(8,128)S(1)} %get-tuple-element.21), channel_id=1, source_target_pairs={{0,12},{1,15},{2,14},{3,13},{4,8},{5,11},{6,10},{7,9},{8,4},{9,7},... | collective-permute-start | bytes 196616 | tf_op jit(solution)/shard_map/ppermute | solution.py:297
  8.9 6.5 %collective-permute-start.2 = (f32[2,16,512]{2,1,0:T(8,128)S(1)}, f32[2,16,512]{2,1,0:T(8,128)S(1)}, u32[]{:S(2)}, u32[]{:S(2)}) collective-permute-start(f32[2,16,512]{2,1,0:T(8,128)S(1)} %get-tuple-element.22), channel_id=1, source_target_pairs={{0,8},{1,11},{2,10},{3,9},{4,12},{5,15},{6,14},{7,13},{8,0},{9,3},... | collective-permute-start | bytes 196616 | tf_op jit(solution)/shard_map/ppermute | solution.py:297
  9.0 7.0 %collective-permute-start.4 = (f32[2,16,512]{2,1,0:T(8,128)S(1)}, f32[2,16,512]{2,1,0:T(8,128)S(1)}, u32[]{:S(2)}, u32[]{:S(2)}) collective-permute-start(f32[2,16,512]{2,1,0:T(8,128)S(1)} %get-tuple-element.25), channel_id=1, source_target_pairs={{0,4},{1,7},{2,6},{3,5},{4,0},{5,3},{6,2},{7,1},{8,12},{9,15},{10,... | collective-permute-start | bytes 196616 | tf_op jit(solution)/shard_map/ppermute | solution.py:297
  9.7 6.3 %collective-permute-start.5 = (f32[2,16,512]{2,1,0:T(8,128)S(1)}, f32[2,16,512]{2,1,0:T(8,128)S(1)}, u32[]{:S(2)}, u32[]{:S(2)}) collective-permute-start(f32[2,16,512]{2,1,0:T(8,128)S(1)} %get-tuple-element.26), channel_id=1, source_target_pairs={{0,0},{1,3},{2,2},{3,1},{4,4},{5,7},{6,6},{7,5},{8,8},{9,11},{10,1... | collective-permute-start | bytes 196616 | tf_op jit(solution)/shard_map/ppermute | solution.py:297
  15.4 1.9 %copy-start.3 = (bf16[2,4,16,128]{3,2,1,0:T(8,128)(2,1)S(1)}, bf16[2,4,16,128]{3,2,1,0:T(8,128)(2,1)}, u32[]{:S(2)}) copy-start(bf16[2,4,16,128]{3,2,1,0:T(8,128)(2,1)} %constant.13.clone.refs_10_.inverse_low) | copy-start | bytes 98308
  15.4 1.9 %copy-start.4 = (bf16[2,4,16,128]{3,2,1,0:T(8,128)(2,1)S(1)}, bf16[2,4,16,128]{3,2,1,0:T(8,128)(2,1)}, u32[]{:S(2)}) copy-start(bf16[2,4,16,128]{3,2,1,0:T(8,128)(2,1)} %constant.12.clone.refs_9_.inverse_high) | copy-start | bytes 98308
  15.5 1.9 %copy-start.5 = (bf16[128,128]{1,0:T(8,128)(2,1)S(1)}, bf16[128,128]{1,0:T(8,128)(2,1)}, u32[]{:S(2)}) copy-start(bf16[128,128]{1,0:T(8,128)(2,1)} %constant.11.clone.refs_8_) | copy-start | bytes 98308
  15.5 1.4 %collective-permute-start.6 = (f32[2,16,512]{2,1,0:T(8,128)S(1)}, f32[2,16,512]{2,1,0:T(8,128)S(1)}, u32[]{:S(2)}, u32[]{:S(2)}) collective-permute-start(f32[2,16,512]{2,1,0:T(8,128)S(1)} %second_halves.2), channel_id=1, source_target_pairs={{0,1},{1,0},{2,3},{3,2},{4,5},{5,4},{6,7},{7,6},{8,9},{9,8},{10,11... | collective-permute-start | bytes 196616 | tf_op jit(solution)/shard_map/ppermute | solution.py:286
  16.0 15.0 %copy-start = (bf16[4,256,512]{2,1,0:T(8,128)(2,1)S(1)}, bf16[4,256,512]{2,1,0:T(8,128)(2,1)}, u32[]{:S(2)}) copy-start(bf16[4,256,512]{2,1,0:T(8,128)(2,1)} %flow_ref.1) | copy-start | bytes 3145732
  16.0 1.3 %collective-permute-start.7 = (f32[2,16,512]{2,1,0:T(8,128)S(1)}, f32[2,16,512]{2,1,0:T(8,128)S(1)}, u32[]{:S(2)}, u32[]{:S(2)}) collective-permute-start(f32[2,16,512]{2,1,0:T(8,128)S(1)} %second_halves.3), channel_id=1, source_target_pairs={{0,1},{1,0},{2,3},{3,2},{4,5},{5,4},{6,7},{7,6},{8,9},{9,8},{10,11... | collective-permute-start | bytes 196616 | tf_op jit(solution)/shard_map/ppermute | solution.py:286
  18.3 1.3 %collective-permute-start.11 = (f32[2,16,512]{2,1,0:T(8,128)S(1)}, f32[2,16,512]{2,1,0:T(8,128)S(1)}, u32[]{:S(2)}, u32[]{:S(2)}) collective-permute-start(f32[2,16,512]{2,1,0:T(8,128)S(1)} %get-tuple-element.33), channel_id=1, source_target_pairs={{0,1},{1,0},{2,3},{3,2},{4,5},{5,4},{6,7},{7,6},{8,9},{9,8},{10,11... | collective-permute-start | bytes 196616 | tf_op jit(solution)/shard_map/ppermute | solution.py:286
  18.6 12.3 %copy-start.2 = (bf16[2,2,256,256]{3,2,1,0:T(8,128)(2,1)S(1)}, bf16[2,2,256,256]{3,2,1,0:T(8,128)(2,1)}, u32[]{:S(2)}) copy-start(bf16[2,2,256,256]{3,2,1,0:T(8,128)(2,1)} %constant.14.clone.table_ref) | copy-start | bytes 1572868
  18.9 4.1 %collective-permute-start.8 = (f32[2,16,512]{2,1,0:T(8,128)S(1)}, f32[2,16,512]{2,1,0:T(8,128)S(1)}, u32[]{:S(2)}, u32[]{:S(2)}) collective-permute-start(f32[2,16,512]{2,1,0:T(8,128)S(1)} %get-tuple-element.29), channel_id=1, source_target_pairs={{0,1},{1,0},{2,3},{3,2},{4,5},{5,4},{6,7},{7,6},{8,9},{9,8},{10,11... | collective-permute-start | bytes 196616 | tf_op jit(solution)/shard_map/ppermute | solution.py:286
  19.6 8.7 %collective-permute-start.12 = (f32[4,8,512]{2,1,0:T(8,128)S(1)}, f32[4,8,512]{2,1,0:T(8,128)S(1)}, u32[]{:S(2)}, u32[]{:S(2)}) collective-permute-start(f32[4,8,512]{2,1,0:T(8,128)S(1)} %get-tuple-element.34), channel_id=1, source_target_pairs={{0,8},{1,11},{2,10},{3,9},{4,12},{5,15},{6,14},{7,13},{8,0},{9,3},... | collective-permute-start | bytes 196616 | tf_op jit(solution)/shard_map/ppermute | solution.py:297
  21.0 7.4 %collective-permute-start.13 = (f32[4,8,512]{2,1,0:T(8,128)S(1)}, f32[4,8,512]{2,1,0:T(8,128)S(1)}, u32[]{:S(2)}, u32[]{:S(2)}) collective-permute-start(f32[4,8,512]{2,1,0:T(8,128)S(1)} %get-tuple-element.35), channel_id=1, source_target_pairs={{0,12},{1,15},{2,14},{3,13},{4,8},{5,11},{6,10},{7,9},{8,4},{9,7},... | collective-permute-start | bytes 196616 | tf_op jit(solution)/shard_map/ppermute | solution.py:297
  23.0 6.5 %collective-permute-start.9 = (f32[4,8,512]{2,1,0:T(8,128)S(1)}, f32[4,8,512]{2,1,0:T(8,128)S(1)}, u32[]{:S(2)}, u32[]{:S(2)}) collective-permute-start(f32[4,8,512]{2,1,0:T(8,128)S(1)} %get-tuple-element.30), channel_id=1, source_target_pairs={{0,4},{1,7},{2,6},{3,5},{4,0},{5,3},{6,2},{7,1},{8,12},{9,15},{10,... | collective-permute-start | bytes 196616 | tf_op jit(solution)/shard_map/ppermute | solution.py:297
  23.6 5.9 %collective-permute-start.10 = (f32[4,8,512]{2,1,0:T(8,128)S(1)}, f32[4,8,512]{2,1,0:T(8,128)S(1)}, u32[]{:S(2)}, u32[]{:S(2)}) collective-permute-start(f32[4,8,512]{2,1,0:T(8,128)S(1)} %get-tuple-element.31), channel_id=1, source_target_pairs={{0,0},{1,3},{2,2},{3,1},{4,4},{5,7},{6,6},{7,5},{8,8},{9,11},{10,1... | collective-permute-start | bytes 196616 | tf_op jit(solution)/shard_map/ppermute | solution.py:297
  28.4 2.5 %copy-start.7 = (bf16[64,64]{1,0:T(8,128)(2,1)S(1)}, bf16[64,64]{1,0:T(8,128)(2,1)}, u32[]{:S(2)}) copy-start(bf16[64,64]{1,0:T(8,128)(2,1)} %local_ref.1) | copy-start | bytes 24580
  28.4 2.5 %copy-start.8 = (f32[64]{0:T(128)S(1)}, f32[64]{0:T(128)}, u32[]{:S(2)}) copy-start(f32[64]{0:T(128)} %bias_ref.1) | copy-start | bytes 772
  28.4 1.5 %collective-permute-start.15 = (f32[2,4,8,512]{3,2,1,0:T(8,128)S(1)}, f32[2,4,8,512]{3,2,1,0:T(8,128)S(1)}, u32[]{:S(2)}, u32[]{:S(2)}) collective-permute-start(f32[2,4,8,512]{3,2,1,0:T(8,128)S(1)} %stack_blocks.3), channel_id=1, source_target_pairs={{0,1},{1,0},{2,3},{3,2},{4,5},{5,4},{6,7},{7,6},{8,9},{9,8},{10,11... | collective-permute-start | bytes 393224 | tf_op jit(solution)/shard_map/ppermute | solution.py:286
  29.5 1.4 %collective-permute-start.14 = (f32[2,4,8,512]{3,2,1,0:T(8,128)S(1)}, f32[2,4,8,512]{3,2,1,0:T(8,128)S(1)}, u32[]{:S(2)}, u32[]{:S(2)}) collective-permute-start(f32[2,4,8,512]{3,2,1,0:T(8,128)S(1)} %stack_blocks.2), channel_id=1, source_target_pairs={{0,1},{1,0},{2,3},{3,2},{4,5},{5,4},{6,7},{7,6},{8,9},{9,8},{10,11... | collective-permute-start | bytes 393224 | tf_op jit(solution)/shard_map/ppermute | solution.py:286
  (1 other events, 1.8 us)

commit v36 on v33

--- a/solution.py
+++ b/solution.py
@@ -169,7 +169,7 @@
 def turns(layers, inverse=False):
     half = layers // 2
     if inverse:
-        return list(range(half, layers)) + list(range(half - 1, -1, -1))
+        return list(range(half, layers)) + list(range(half))
     return list(range(layers - 1, -1, -1))
 
 

time: 33.4 us -> 34.2 us (1.024)
  starting transfers between devices: 13.5 us -> 15.1 us
  waiting for transfers between devices: 13.5 us -> 12.8 us
    ppermute x8, starting transfers between devices: 2.56 us -> 4.08 us  [flip_core(): return lax.ppermute(block, 'gy', [(0, 1), (1, 0)])]
    ppermute x8, waiting for transfers between devices: 10.1 us -> 9.39 us  [along_columns(): arrived.append(lax.ppermute(block, ('gx', 'gy'), pairs))]
where the time goes in v36:
time: 34.2 us; the launch traced here: 34 us
  starting transfers between devices  15.1 us (44%)
  waiting for transfers between devices  12.8 us (37%)
  Pallas kernels  5.35 us (16%)
  between operations  0.8 us (2%)
    ppermute x8, starting transfers between devices, along_columns(): arrived.append(lax.ppermute(block, ('gx', 'gy'), pairs))  11 us
    ppermute x8, waiting for transfers between devices, along_columns(): arrived.append(lax.ppermute(block, ('gx', 'gy'), pairs))  9.39 us
    ppermute x8, starting transfers between devices, flip_core(): return lax.ppermute(block, 'gy', [(0, 1), (1, 0)])  4.08 us
    ppermute x8, waiting for transfers between devices, flip_core(): return lax.ppermute(block, 'gy', [(0, 1), (1, 0)])  3.4 us
    pallas_call x1, Pallas kernels, make_output(): pl.pallas_call(functools.partial(output_kernel, layers), out_specs=[pl.Bl...  2.25 us
    pallas_call x1, Pallas kernels, forward_y(): pl.pallas_call(functools.partial(forward_y_kernel, extent, rows_ky), in_s...  1.75 us
    pallas_call x1, Pallas kernels, mix(): pl.pallas_call(functools.partial(mix_kernel, layers), out_shape=[jax.Shap...  1.04 us
  transfers between devices with their start and end apart: 16, of which 9 were waited for; matrix products, arithmetic and copies ran while one was open for 0% of the time, Pallas kernels for 1%

profile of v36, /device:TPU:0, one launch (start us, length us, event | category | flops | bytes accessed | tf_op | source)
XLA Modules:
  0.0 34.0 jit_solution(11425568898507001357)
XLA Ops:
  0.6 1.7 %forward_y.1 = (f32[2,2,16,512]{3,2,1,0:T(8,128)S(1)}, f32[2,2,16,512]{3,2,1,0:T(8,128)S(1)}, f32[2,2,16,512]{3,2,1,0:T(8,128)S(1)}, f32[2,2,16,512]{3,2,1,0:T(8,128)S(1)}) custom-call(bf16[4,256,512]{2,1,0:T(8,128)(2,1)} %flow_ref.1), custom_call_target="tpu_custom_call" | custom-call | tf_op jit(solution)/shard_map/forward_y/pallas_call | solution.py:273
  2.4 0.5 %collective-permute-start = (f32[2,2,16,512]{3,2,1,0:T(8,128)S(1)}, f32[2,2,16,512]{3,2,1,0:T(8,128)S(1)}, u32[]{:S(2)}, u32[]{:S(2)}) collective-permute-start(f32[2,2,16,512]{3,2,1,0:T(8,128)S(1)} %get-tuple-element.20), channel_id=1, source_target_pairs={{0,1},{1,0},{2,3},{3,2},{4,5},{5,4},{6,7},{7,6},{8,9},{9,8},{10,11... | collective-permute-start | bytes 393224 | tf_op jit(solution)/shard_map/ppermute | solution.py:287
  3.0 0.9 %collective-permute-done.arrived_ref = f32[2,2,16,512]{3,2,1,0:T(8,128)S(1)} collective-permute-done((f32[2,2,16,512]{3,2,1,0:T(8,128)S(1)}, f32[2,2,16,512]{3,2,1,0:T(8,128)S(1)}, u32[]{:S(2)}, u32[]{:S(2)}) %collective-permute-start) | collective-permute-done | bytes 131104 | tf_op jit(solution)/shard_map/ppermute | solution.py:287
  3.9 5.0 %collective-permute-start.1 = (f32[2,16,512]{2,1,0:T(8,128)S(1)}, f32[2,16,512]{2,1,0:T(8,128)S(1)}, u32[]{:S(2)}, u32[]{:S(2)}) collective-permute-start(f32[2,16,512]{2,1,0:T(8,128)S(1)} %get-tuple-element.21), channel_id=1, source_target_pairs={{0,12},{1,15},{2,14},{3,13},{4,8},{5,11},{6,10},{7,9},{8,4},{9,7},... | collective-permute-start | bytes 196616 | tf_op jit(solution)/shard_map/ppermute | solution.py:298
  9.0 0.7 %collective-permute-start.4 = (f32[2,16,512]{2,1,0:T(8,128)S(1)}, f32[2,16,512]{2,1,0:T(8,128)S(1)}, u32[]{:S(2)}, u32[]{:S(2)}) collective-permute-start(f32[2,16,512]{2,1,0:T(8,128)S(1)} %get-tuple-element.25), channel_id=1, source_target_pairs={{0,4},{1,7},{2,6},{3,5},{4,0},{5,3},{6,2},{7,1},{8,12},{9,15},{10,... | collective-permute-start | bytes 196616 | tf_op jit(solution)/shard_map/ppermute | solution.py:298
  9.7 0.7 %collective-permute-start.5 = (f32[2,16,512]{2,1,0:T(8,128)S(1)}, f32[2,16,512]{2,1,0:T(8,128)S(1)}, u32[]{:S(2)}, u32[]{:S(2)}) collective-permute-start(f32[2,16,512]{2,1,0:T(8,128)S(1)} %get-tuple-element.26), channel_id=1, source_target_pairs={{0,0},{1,3},{2,2},{3,1},{4,4},{5,7},{6,6},{7,5},{8,8},{9,11},{10,1... | collective-permute-start | bytes 196616 | tf_op jit(solution)/shard_map/ppermute | solution.py:298
  10.3 1.3 %collective-permute-done.1.refs_0_ = f32[2,16,512]{2,1,0:T(8,128)S(1)} collective-permute-done((f32[2,16,512]{2,1,0:T(8,128)S(1)}, f32[2,16,512]{2,1,0:T(8,128)S(1)}, u32[]{:S(2)}, u32[]{:S(2)}) %collective-permute-start.1) | collective-permute-done | bytes 65568 | tf_op jit(solution)/shard_map/ppermute | solution.py:298
  11.7 3.8 %collective-permute-done.2.refs_1_ = f32[2,16,512]{2,1,0:T(8,128)S(1)} collective-permute-done((f32[2,16,512]{2,1,0:T(8,128)S(1)}, f32[2,16,512]{2,1,0:T(8,128)S(1)}, u32[]{:S(2)}, u32[]{:S(2)}) %collective-permute-start.2) | collective-permute-done | bytes 65568 | tf_op jit(solution)/shard_map/ppermute | solution.py:298
  15.5 0.5 %collective-permute-start.6 = (f32[2,16,512]{2,1,0:T(8,128)S(1)}, f32[2,16,512]{2,1,0:T(8,128)S(1)}, u32[]{:S(2)}, u32[]{:S(2)}) collective-permute-start(f32[2,16,512]{2,1,0:T(8,128)S(1)} %second_halves.2), channel_id=1, source_target_pairs={{0,1},{1,0},{2,3},{3,2},{4,5},{5,4},{6,7},{7,6},{8,9},{9,8},{10,11... | collective-permute-start | bytes 196616 | tf_op jit(solution)/shard_map/ppermute | solution.py:287
  16.0 0.3 %collective-permute-start.7 = (f32[2,16,512]{2,1,0:T(8,128)S(1)}, f32[2,16,512]{2,1,0:T(8,128)S(1)}, u32[]{:S(2)}, u32[]{:S(2)}) collective-permute-start(f32[2,16,512]{2,1,0:T(8,128)S(1)} %second_halves.3), channel_id=1, source_target_pairs={{0,1},{1,0},{2,3},{3,2},{4,5},{5,4},{6,7},{7,6},{8,9},{9,8},{10,11... | collective-permute-start | bytes 196616 | tf_op jit(solution)/shard_map/ppermute | solution.py:287
  16.3 0.5 %collective-permute-done.6.refs_4_ = f32[2,16,512]{2,1,0:T(8,128)S(1)} collective-permute-done((f32[2,16,512]{2,1,0:T(8,128)S(1)}, f32[2,16,512]{2,1,0:T(8,128)S(1)}, u32[]{:S(2)}, u32[]{:S(2)}) %collective-permute-start.6) | collective-permute-done | bytes 65568 | tf_op jit(solution)/shard_map/ppermute | solution.py:287
  16.8 0.4 %collective-permute-done.7.refs_5_ = f32[2,16,512]{2,1,0:T(8,128)S(1)} collective-permute-done((f32[2,16,512]{2,1,0:T(8,128)S(1)}, f32[2,16,512]{2,1,0:T(8,128)S(1)}, u32[]{:S(2)}, u32[]{:S(2)}) %collective-permute-start.7) | collective-permute-done | bytes 65568 | tf_op jit(solution)/shard_map/ppermute | solution.py:287
  17.3 1.0 %mix.1 = (f32[128,512]{1,0:T(8,128)S(1)}, f32[2,16,512]{2,1,0:T(8,128)S(1)}, f32[2,16,512]{2,1,0:T(8,128)S(1)}) custom-call(f32[2,16,512]{2,1,0:T(8,128)S(1)} %collective-permute-done.1.refs_0_, f32[2,16,512]{2,1,0:T(8,128)S(1)} %collective-permute-done.2.refs_1_, f32[2,16,512]{2,1,0:T(8,128)S(1)} %collective-permute-done.4.refs_0_.refs_2_, ...), custom_call_target="tpu_custom_call" | custom-call | tf_op jit(solution)/shard_map/mix/pallas_call | solution.py:431
  18.4 0.3 %collective-permute-start.11 = (f32[2,16,512]{2,1,0:T(8,128)S(1)}, f32[2,16,512]{2,1,0:T(8,128)S(1)}, u32[]{:S(2)}, u32[]{:S(2)}) collective-permute-start(f32[2,16,512]{2,1,0:T(8,128)S(1)} %get-tuple-element.33), channel_id=1, source_target_pairs={{0,1},{1,0},{2,3},{3,2},{4,5},{5,4},{6,7},{7,6},{8,9},{9,8},{10,11... | collective-permute-start | bytes 196616 | tf_op jit(solution)/shard_map/ppermute | solution.py:287
  18.7 0.2 collective-permute-start.8
  19.2 0.5 %collective-permute-done.11.arrived_ref = f32[2,16,512]{2,1,0:T(8,128)S(1)} collective-permute-done((f32[2,16,512]{2,1,0:T(8,128)S(1)}, f32[2,16,512]{2,1,0:T(8,128)S(1)}, u32[]{:S(2)}, u32[]{:S(2)}) %collective-permute-start.11) | collective-permute-done | bytes 65568 | tf_op jit(solution)/shard_map/ppermute | solution.py:287
  19.7 1.4 %collective-permute-start.12 = (f32[4,8,512]{2,1,0:T(8,128)S(1)}, f32[4,8,512]{2,1,0:T(8,128)S(1)}, u32[]{:S(2)}, u32[]{:S(2)}) collective-permute-start(f32[4,8,512]{2,1,0:T(8,128)S(1)} %get-tuple-element.34), channel_id=1, source_target_pairs={{0,8},{1,11},{2,10},{3,9},{4,12},{5,15},{6,14},{7,13},{8,0},{9,3},... | collective-permute-start | bytes 196616 | tf_op jit(solution)/shard_map/ppermute | solution.py:298
  21.1 2.0 %collective-permute-start.13 = (f32[4,8,512]{2,1,0:T(8,128)S(1)}, f32[4,8,512]{2,1,0:T(8,128)S(1)}, u32[]{:S(2)}, u32[]{:S(2)}) collective-permute-start(f32[4,8,512]{2,1,0:T(8,128)S(1)} %get-tuple-element.35), channel_id=1, source_target_pairs={{0,12},{1,15},{2,14},{3,13},{4,8},{5,11},{6,10},{7,9},{8,4},{9,7},... | collective-permute-start | bytes 196616 | tf_op jit(solution)/shard_map/ppermute | solution.py:298
  23.1 0.7 %collective-permute-start.9 = (f32[4,8,512]{2,1,0:T(8,128)S(1)}, f32[4,8,512]{2,1,0:T(8,128)S(1)}, u32[]{:S(2)}, u32[]{:S(2)}) collective-permute-start(f32[4,8,512]{2,1,0:T(8,128)S(1)} %get-tuple-element.30), channel_id=1, source_target_pairs={{0,0},{1,3},{2,2},{3,1},{4,4},{5,7},{6,6},{7,5},{8,8},{9,11},{10,1... | collective-permute-start | bytes 196616 | tf_op jit(solution)/shard_map/ppermute | solution.py:298
  23.8 0.6 %collective-permute-start.10 = (f32[4,8,512]{2,1,0:T(8,128)S(1)}, f32[4,8,512]{2,1,0:T(8,128)S(1)}, u32[]{:S(2)}, u32[]{:S(2)}) collective-permute-start(f32[4,8,512]{2,1,0:T(8,128)S(1)} %get-tuple-element.31), channel_id=1, source_target_pairs={{0,4},{1,7},{2,6},{3,5},{4,0},{5,3},{6,2},{7,1},{8,12},{9,15},{10,... | collective-permute-start | bytes 196616 | tf_op jit(solution)/shard_map/ppermute | solution.py:298
  24.4 4.1 %collective-permute-done.12.refs_0_.refs_2_ = f32[4,8,512]{2,1,0:T(8,128)S(1)} collective-permute-done((f32[4,8,512]{2,1,0:T(8,128)S(1)}, f32[4,8,512]{2,1,0:T(8,128)S(1)}, u32[]{:S(2)}, u32[]{:S(2)}) %collective-permute-start.12) | collective-permute-done | bytes 65568 | tf_op jit(solution)/shard_map/ppermute | solution.py:298
  28.9 1.9 %collective-permute-start.14 = (f32[2,4,8,512]{3,2,1,0:T(8,128)S(1)}, f32[2,4,8,512]{3,2,1,0:T(8,128)S(1)}, u32[]{:S(2)}, u32[]{:S(2)}) collective-permute-start(f32[2,4,8,512]{3,2,1,0:T(8,128)S(1)} %stack_blocks.2), channel_id=1, source_target_pairs={{0,1},{1,0},{2,3},{3,2},{4,5},{5,4},{6,7},{7,6},{8,9},{9,8},{10,11... | collective-permute-start | bytes 393224 | tf_op jit(solution)/shard_map/ppermute | solution.py:287
  30.8 1.0 %collective-permute-done.14.refs_4_ = f32[2,4,8,512]{3,2,1,0:T(8,128)S(1)} collective-permute-done((f32[2,4,8,512]{3,2,1,0:T(8,128)S(1)}, f32[2,4,8,512]{3,2,1,0:T(8,128)S(1)}, u32[]{:S(2)}, u32[]{:S(2)}) %collective-permute-start.14) | collective-permute-done | bytes 131104 | tf_op jit(solution)/shard_map/ppermute | solution.py:287
  31.8 2.3 %make_output.1 = (bf16[4,256,512]{2,1,0:T(8,128)(2,1)}, f32[1,64,1024]{2,1,0:T(8,128)}) custom-call(bf16[4,256,512]{2,1,0:T(8,128)(2,1)S(1)} %copy-done, bf16[2,2,256,256]{3,2,1,0:T(8,128)(2,1)S(1)} %copy-done.2, bf16[64,64]{1,0:T(8,128)(2,1)S(1)} %copy-done.7, f32[64]{0:T(128)S(1)} %copy-done.8, f32[128,512]{1,0:T(8,128)S(1)} %get-tuple-element.27.modes_ref, ...), custom_call_target="tpu_custom_call" | custom-call | tf_op jit(solution)/shard_map/make_output/pallas_call | solution.py:533
  (38 shorter events, 0.9 us)
Async XLA Ops:
  0.6 16.7 %copy-start.1 = (bf16[1,64,64,128]{3,2,1,0:T(8,128)(2,1)S(1)}, bf16[1,64,64,128]{3,2,1,0:T(8,128)(2,1)}, u32[]{:S(2)}) copy-start(bf16[1,64,64,128]{3,2,1,0:T(8,128)(2,1)} %refs_6_.1) | copy-start | bytes 3145732
  2.4 1.5 %collective-permute-start = (f32[2,2,16,512]{3,2,1,0:T(8,128)S(1)}, f32[2,2,16,512]{3,2,1,0:T(8,128)S(1)}, u32[]{:S(2)}, u32[]{:S(2)}) collective-permute-start(f32[2,2,16,512]{3,2,1,0:T(8,128)S(1)} %get-tuple-element.20), channel_id=1, source_target_pairs={{0,1},{1,0},{2,3},{3,2},{4,5},{5,4},{6,7},{7,6},{8,9},{9,8},{10,11... | collective-permute-start | bytes 393224 | tf_op jit(solution)/shard_map/ppermute | solution.py:287
  2.9 6.0 %collective-permute-start.3 = (f32[2,2,16,512]{3,2,1,0:T(8,128)S(1)}, f32[2,2,16,512]{3,2,1,0:T(8,128)S(1)}, u32[]{:S(2)}, u32[]{:S(2)}) collective-permute-start(f32[2,2,16,512]{3,2,1,0:T(8,128)S(1)} %get-tuple-element.24), channel_id=1, source_target_pairs={{0,1},{1,0},{2,3},{3,2},{4,5},{5,4},{6,7},{7,6},{8,9},{9,8},{10,11... | collective-permute-start | bytes 393224 | tf_op jit(solution)/shard_map/ppermute | solution.py:287
  3.9 7.8 %collective-permute-start.1 = (f32[2,16,512]{2,1,0:T(8,128)S(1)}, f32[2,16,512]{2,1,0:T(8,128)S(1)}, u32[]{:S(2)}, u32[]{:S(2)}) collective-permute-start(f32[2,16,512]{2,1,0:T(8,128)S(1)} %get-tuple-element.21), channel_id=1, source_target_pairs={{0,12},{1,15},{2,14},{3,13},{4,8},{5,11},{6,10},{7,9},{8,4},{9,7},... | collective-permute-start | bytes 196616 | tf_op jit(solution)/shard_map/ppermute | solution.py:298
  8.9 6.5 %collective-permute-start.2 = (f32[2,16,512]{2,1,0:T(8,128)S(1)}, f32[2,16,512]{2,1,0:T(8,128)S(1)}, u32[]{:S(2)}, u32[]{:S(2)}) collective-permute-start(f32[2,16,512]{2,1,0:T(8,128)S(1)} %get-tuple-element.22), channel_id=1, source_target_pairs={{0,8},{1,11},{2,10},{3,9},{4,12},{5,15},{6,14},{7,13},{8,0},{9,3},... | collective-permute-start | bytes 196616 | tf_op jit(solution)/shard_map/ppermute | solution.py:298
  9.0 7.0 %collective-permute-start.4 = (f32[2,16,512]{2,1,0:T(8,128)S(1)}, f32[2,16,512]{2,1,0:T(8,128)S(1)}, u32[]{:S(2)}, u32[]{:S(2)}) collective-permute-start(f32[2,16,512]{2,1,0:T(8,128)S(1)} %get-tuple-element.25), channel_id=1, source_target_pairs={{0,4},{1,7},{2,6},{3,5},{4,0},{5,3},{6,2},{7,1},{8,12},{9,15},{10,... | collective-permute-start | bytes 196616 | tf_op jit(solution)/shard_map/ppermute | solution.py:298
  9.7 6.3 %collective-permute-start.5 = (f32[2,16,512]{2,1,0:T(8,128)S(1)}, f32[2,16,512]{2,1,0:T(8,128)S(1)}, u32[]{:S(2)}, u32[]{:S(2)}) collective-permute-start(f32[2,16,512]{2,1,0:T(8,128)S(1)} %get-tuple-element.26), channel_id=1, source_target_pairs={{0,0},{1,3},{2,2},{3,1},{4,4},{5,7},{6,6},{7,5},{8,8},{9,11},{10,1... | collective-permute-start | bytes 196616 | tf_op jit(solution)/shard_map/ppermute | solution.py:298
  15.4 1.9 %copy-start.3 = (bf16[2,4,16,128]{3,2,1,0:T(8,128)(2,1)S(1)}, bf16[2,4,16,128]{3,2,1,0:T(8,128)(2,1)}, u32[]{:S(2)}) copy-start(bf16[2,4,16,128]{3,2,1,0:T(8,128)(2,1)} %constant.13.clone.refs_10_.inverse_low) | copy-start | bytes 98308
  15.4 1.9 %copy-start.4 = (bf16[2,4,16,128]{3,2,1,0:T(8,128)(2,1)S(1)}, bf16[2,4,16,128]{3,2,1,0:T(8,128)(2,1)}, u32[]{:S(2)}) copy-start(bf16[2,4,16,128]{3,2,1,0:T(8,128)(2,1)} %constant.12.clone.refs_9_.inverse_high) | copy-start | bytes 98308
  15.5 1.9 %copy-start.5 = (bf16[128,128]{1,0:T(8,128)(2,1)S(1)}, bf16[128,128]{1,0:T(8,128)(2,1)}, u32[]{:S(2)}) copy-start(bf16[128,128]{1,0:T(8,128)(2,1)} %constant.11.clone.refs_8_) | copy-start | bytes 98308
  15.5 1.4 %collective-permute-start.6 = (f32[2,16,512]{2,1,0:T(8,128)S(1)}, f32[2,16,512]{2,1,0:T(8,128)S(1)}, u32[]{:S(2)}, u32[]{:S(2)}) collective-permute-start(f32[2,16,512]{2,1,0:T(8,128)S(1)} %second_halves.2), channel_id=1, source_target_pairs={{0,1},{1,0},{2,3},{3,2},{4,5},{5,4},{6,7},{7,6},{8,9},{9,8},{10,11... | collective-permute-start | bytes 196616 | tf_op jit(solution)/shard_map/ppermute | solution.py:287
  16.0 15.8 %copy-start = (bf16[4,256,512]{2,1,0:T(8,128)(2,1)S(1)}, bf16[4,256,512]{2,1,0:T(8,128)(2,1)}, u32[]{:S(2)}) copy-start(bf16[4,256,512]{2,1,0:T(8,128)(2,1)} %flow_ref.1) | copy-start | bytes 3145732
  16.0 1.3 %collective-permute-start.7 = (f32[2,16,512]{2,1,0:T(8,128)S(1)}, f32[2,16,512]{2,1,0:T(8,128)S(1)}, u32[]{:S(2)}, u32[]{:S(2)}) collective-permute-start(f32[2,16,512]{2,1,0:T(8,128)S(1)} %second_halves.3), channel_id=1, source_target_pairs={{0,1},{1,0},{2,3},{3,2},{4,5},{5,4},{6,7},{7,6},{8,9},{9,8},{10,11... | collective-permute-start | bytes 196616 | tf_op jit(solution)/shard_map/ppermute | solution.py:287
  18.4 1.3 %collective-permute-start.11 = (f32[2,16,512]{2,1,0:T(8,128)S(1)}, f32[2,16,512]{2,1,0:T(8,128)S(1)}, u32[]{:S(2)}, u32[]{:S(2)}) collective-permute-start(f32[2,16,512]{2,1,0:T(8,128)S(1)} %get-tuple-element.33), channel_id=1, source_target_pairs={{0,1},{1,0},{2,3},{3,2},{4,5},{5,4},{6,7},{7,6},{8,9},{9,8},{10,11... | collective-permute-start | bytes 196616 | tf_op jit(solution)/shard_map/ppermute | solution.py:287
  18.7 4.4 %collective-permute-start.8 = (f32[2,16,512]{2,1,0:T(8,128)S(1)}, f32[2,16,512]{2,1,0:T(8,128)S(1)}, u32[]{:S(2)}, u32[]{:S(2)}) collective-permute-start(f32[2,16,512]{2,1,0:T(8,128)S(1)} %get-tuple-element.29), channel_id=1, source_target_pairs={{0,1},{1,0},{2,3},{3,2},{4,5},{5,4},{6,7},{7,6},{8,9},{9,8},{10,11... | collective-permute-start | bytes 196616 | tf_op jit(solution)/shard_map/ppermute | solution.py:287
  19.0 12.8 %copy-start.2 = (bf16[2,2,256,256]{3,2,1,0:T(8,128)(2,1)S(1)}, bf16[2,2,256,256]{3,2,1,0:T(8,128)(2,1)}, u32[]{:S(2)}) copy-start(bf16[2,2,256,256]{3,2,1,0:T(8,128)(2,1)} %constant.14.clone.table_ref) | copy-start | bytes 1572868
  19.7 8.7 %collective-permute-start.12 = (f32[4,8,512]{2,1,0:T(8,128)S(1)}, f32[4,8,512]{2,1,0:T(8,128)S(1)}, u32[]{:S(2)}, u32[]{:S(2)}) collective-permute-start(f32[4,8,512]{2,1,0:T(8,128)S(1)} %get-tuple-element.34), channel_id=1, source_target_pairs={{0,8},{1,11},{2,10},{3,9},{4,12},{5,15},{6,14},{7,13},{8,0},{9,3},... | collective-permute-start | bytes 196616 | tf_op jit(solution)/shard_map/ppermute | solution.py:298
  21.1 7.4 %collective-permute-start.13 = (f32[4,8,512]{2,1,0:T(8,128)S(1)}, f32[4,8,512]{2,1,0:T(8,128)S(1)}, u32[]{:S(2)}, u32[]{:S(2)}) collective-permute-start(f32[4,8,512]{2,1,0:T(8,128)S(1)} %get-tuple-element.35), channel_id=1, source_target_pairs={{0,12},{1,15},{2,14},{3,13},{4,8},{5,11},{6,10},{7,9},{8,4},{9,7},... | collective-permute-start | bytes 196616 | tf_op jit(solution)/shard_map/ppermute | solution.py:298
  23.1 5.6 %collective-permute-start.9 = (f32[4,8,512]{2,1,0:T(8,128)S(1)}, f32[4,8,512]{2,1,0:T(8,128)S(1)}, u32[]{:S(2)}, u32[]{:S(2)}) collective-permute-start(f32[4,8,512]{2,1,0:T(8,128)S(1)} %get-tuple-element.30), channel_id=1, source_target_pairs={{0,0},{1,3},{2,2},{3,1},{4,4},{5,7},{6,6},{7,5},{8,8},{9,11},{10,1... | collective-permute-start | bytes 196616 | tf_op jit(solution)/shard_map/ppermute | solution.py:298
  23.8 5.1 %collective-permute-start.10 = (f32[4,8,512]{2,1,0:T(8,128)S(1)}, f32[4,8,512]{2,1,0:T(8,128)S(1)}, u32[]{:S(2)}, u32[]{:S(2)}) collective-permute-start(f32[4,8,512]{2,1,0:T(8,128)S(1)} %get-tuple-element.31), channel_id=1, source_target_pairs={{0,4},{1,7},{2,6},{3,5},{4,0},{5,3},{6,2},{7,1},{8,12},{9,15},{10,... | collective-permute-start | bytes 196616 | tf_op jit(solution)/shard_map/ppermute | solution.py:298
  28.5 3.3 %copy-start.7 = (bf16[64,64]{1,0:T(8,128)(2,1)S(1)}, bf16[64,64]{1,0:T(8,128)(2,1)}, u32[]{:S(2)}) copy-start(bf16[64,64]{1,0:T(8,128)(2,1)} %local_ref.1) | copy-start | bytes 24580
  28.5 3.3 %copy-start.8 = (f32[64]{0:T(128)S(1)}, f32[64]{0:T(128)}, u32[]{:S(2)}) copy-start(f32[64]{0:T(128)} %bias_ref.1) | copy-start | bytes 772
  28.5 2.3 %collective-permute-start.15 = (f32[2,4,8,512]{3,2,1,0:T(8,128)S(1)}, f32[2,4,8,512]{3,2,1,0:T(8,128)S(1)}, u32[]{:S(2)}, u32[]{:S(2)}) collective-permute-start(f32[2,4,8,512]{3,2,1,0:T(8,128)S(1)} %stack_blocks.3), channel_id=1, source_target_pairs={{0,1},{1,0},{2,3},{3,2},{4,5},{5,4},{6,7},{7,6},{8,9},{9,8},{10,11... | collective-permute-start | bytes 393224 | tf_op jit(solution)/shard_map/ppermute | solution.py:287
  28.9 2.9 %collective-permute-start.14 = (f32[2,4,8,512]{3,2,1,0:T(8,128)S(1)}, f32[2,4,8,512]{3,2,1,0:T(8,128)S(1)}, u32[]{:S(2)}, u32[]{:S(2)}) collective-permute-start(f32[2,4,8,512]{3,2,1,0:T(8,128)S(1)} %stack_blocks.2), channel_id=1, source_target_pairs={{0,1},{1,0},{2,3},{3,2},{4,5},{5,4},{6,7},{7,6},{8,9},{9,8},{10,11... | collective-permute-start | bytes 393224 | tf_op jit(solution)/shard_map/ppermute | solution.py:287
  (1 other events, 1.8 us)
